TPU v7x, 32 devices: a whole 2x2x4 slice. The times are simulated.
32 devices in a mesh: outer: 4 (over y, x), inner: 8 (over z, core).
Axes of the slice: x: 2, y: 2, z: 4, core: 2. Of those that a mesh axis runs over, the one named last changes fastest.
Arguments:
- queries: bfloat16 [4096, 512], P(('outer', 'inner')), may hold values from -24 to 24
- keys: bfloat16 [4096, 512], P(('outer', 'inner')), may hold values from -24 to 24
- values: bfloat16 [4096, 512], P(('outer', 'inner')), may hold values from -6 to 6
- block_pos: int32 [32], P(('outer', 'inner')), may hold values from 0 to 31, each once
Outputs:
- attended: bfloat16 [4096, 512], P(('outer', 'inner'))
All inputs are finite; a program needn't handle non-finite values.
Results may differ from a plain program's by a relative error of at most 0.009.
Values may be sent and summed in bfloat16 or wider, within the bound.
No kernel may reach another device: no remote copies, remote signals or barrier semaphores. Data moves between devices by JAX's collectives and lax.ppermute only.
A program may use at most 192 MiB of HBM per device.

v0:
```python
import jax
import jax.numpy as jnp
from jax import lax
from jax.sharding import PartitionSpec as P

HEADS = 4


def token_positions(blockpos, tok):
    return (blockpos[:, None] * tok + jnp.arange(tok, dtype=jnp.int32)[None, :]).reshape(-1)


def absorb(carry, queries, qpos, keys_part, vals_part, kpos, heads):
    acc, top, total = carry
    rows = queries.shape[0]
    count = keys_part.shape[0]
    width = queries.shape[1]
    head_size = width // heads
    qh = queries.reshape(rows, heads, head_size)
    kh = keys_part.reshape(count, heads, head_size)
    vh = vals_part.reshape(count, heads, head_size)
    scores = jnp.einsum("qhd,khd->hqk", qh, kh, preferred_element_type=jnp.float32) * head_size ** (
        -0.5
    )
    allowed = kpos[None, :] <= qpos[:, None]
    scores = jnp.where(allowed[None], scores, -1e30)
    newtop = jnp.maximum(top, jnp.max(scores, axis=-1))
    weights = jnp.where(allowed[None], jnp.exp(scores - newtop[..., None]), 0.0).astype(
        jnp.bfloat16
    )
    factor = jnp.exp(top - newtop)
    total = jnp.sum(weights.astype(jnp.float32), axis=-1)
    update = jnp.einsum("hqk,khd->qhd", weights, vh, preferred_element_type=jnp.float32)
    acc = acc.reshape(rows, heads, head_size) * factor.T[:, :, None] + update
    return (acc.reshape(rows, width), newtop, total)


def visit(carry, queries, qpos, keys_part, vals_part, kpos, heads):
    return absorb(carry, queries, qpos, keys_part, vals_part, kpos, heads)


def shards(queries, keys, values, block_pos):
    tok = queries.shape[0]
    width = queries.shape[1]
    heads = HEADS
    head_size = width // heads
    q_group, qblocks = (
        lax.all_gather(queries, "outer", axis=0, tiled=True),
        lax.all_gather(block_pos, "outer", axis=0, tiled=True),
    )
    groups = qblocks.shape[0]
    rows = q_group.shape[0]
    qpos = token_positions(qblocks, tok)
    init = (
        jnp.zeros((rows, width), jnp.float32),
        jnp.full((heads, rows), -1e30, jnp.float32),
        jnp.zeros((heads, rows), jnp.float32),
    )
    keys_part = lax.all_gather(keys, "inner", axis=0, tiled=True)
    vals_part = lax.all_gather(values, "inner", axis=0, tiled=True)
    kblocks = lax.all_gather(block_pos, "inner", axis=0, tiled=True)
    kpos = token_positions(kblocks, tok)
    acc, top, total = visit(init, q_group, qpos, keys_part, vals_part, kpos, heads)
    acc_parts = acc.reshape(groups, tok, width)
    top_parts = top.reshape(heads, groups, tok).transpose(1, 0, 2)
    total_parts = total.reshape(heads, groups, tok).transpose(1, 0, 2)
    acc_parts, top_parts, total_parts = (
        lax.all_to_all(acc_parts, "outer", split_axis=0, concat_axis=0, tiled=True),
        lax.all_to_all(top_parts, "outer", split_axis=0, concat_axis=0, tiled=True),
        lax.all_to_all(total_parts, "outer", split_axis=0, concat_axis=0, tiled=True),
    )
    best = jnp.max(top_parts, axis=0)
    factor = jnp.exp(top_parts - best[None])
    denom = jnp.sum(total_parts * factor, axis=0)
    numer = jnp.sum(
        acc_parts.reshape(groups, tok, heads, head_size) * factor.transpose(0, 2, 1)[..., None],
        axis=0,
    )
    return (numer / denom.T[:, :, None]).reshape(tok, width).astype(jnp.bfloat16)


def solution(mesh):
    return jax.shard_map(
        shards,
        mesh=mesh,
        in_specs=(
            P(("outer", "inner"), None),
            P(("outer", "inner"), None),
            P(("outer", "inner"), None),
            P(("outer", "inner")),
        ),
        out_specs=P(("outer", "inner"), None),
        check_vma=False,
    )
```

profile of v0, /device:TPU:0, one launch (start us, length us, event | category | flops | bytes accessed | tf_op | source)
XLA Modules:
  0.0 93.7 jit_solution(365289014335287865)
XLA Ops:
  6.5 0.0 all-gather.3.cloned.1.call-start
  6.5 1.7 %copy.15 = bf16[128,512]{0,1:T(8,128)(2,1)} copy(bf16[128,512]{1,0:T(8,128)(2,1)} %param.5) | data formatting | bytes 262144 | tf_op args[1]
  8.2 0.0 all-gather.3.cloned.1.call-update
  8.2 0.0 all-gather.5.cloned.1.call-start
  8.3 1.7 %copy.18 = bf16[128,512]{0,1:T(8,128)(2,1)} copy(bf16[128,512]{1,0:T(8,128)(2,1)} %param.6) | data formatting | bytes 262144 | tf_op args[2]
  9.9 0.0 all-gather.5.cloned.1.call-update
  10.6 1.3 %dynamic-slice.1 = u32[1]{0:T(128)} dynamic-slice(u32[32]{0:T(128)} %constant.21, u32[]{:T(128)S(6)} %add.52), dynamic_slice_sizes={1} | dynamic-slice | bytes 12
  11.9 0.7 dynamic-update-slice.1
  12.6 1.3 %dynamic-slice = u32[1]{0:T(128)} dynamic-slice(u32[32]{0:T(128)} %constant.16, u32[]{:T(128)S(6)} %add.52), dynamic_slice_sizes={1} | dynamic-slice | bytes 12
  13.9 8.8 %all-reduce.1 = s32[4]{0:T(128)S(1)} all-reduce(s32[4]{0:T(128)S(1)} %dynamic-update-slice.1), channel_id=1, replica_groups=mesh['outer'=4,'inner'=8] {'outer'}, use_global_device_ids=true, to_apply=%add.1 | all-reduce | flops 4 | bytes 32
  22.8 0.7 dynamic-update-slice
  23.5 9.2 %all-reduce = s32[8]{0:T(128)S(1)} all-reduce(s32[8]{0:T(128)S(1)} %dynamic-update-slice), channel_id=1, replica_groups=mesh['outer'=4,'inner'=8] {'inner'}, use_global_device_ids=true, to_apply=%add | all-reduce | flops 8 | bytes 64
  32.7 0.1 add_bitcast_fusion
  32.8 0.1 add_bitcast_fusion.1
  32.8 1.0 %copy.14 = bf16[128,512]{0,1:T(8,128)(2,1)S(1)} copy(bf16[128,512]{1,0:T(8,128)(2,1)} %param.4) | data formatting | bytes 262144 | tf_op args[0]
  33.9 10.5 %all_gather.17 = bf16[512,512]{0,1:T(8,128)(2,1)S(1)} all-gather(bf16[128,512]{0,1:T(8,128)(2,1)S(1)} %copy.14), channel_id=1, replica_groups=mesh['outer'=4,'inner'=8] {'outer'}, dimensions={0}, use_global_device_ids=true | all-gather | bytes 655360 | tf_op jit(solution)/shard_map/all_gather | solution.py:48
  44.3 0.4 broadcast_compare_fusion
  44.7 0.0 all-gather.3.cloned.1.call-done
  44.7 3.1 %fusion = (f32[4,512]{1,0:T(4,128)S(1)}, f32[4,512,1024]{2,1,0:T(8,128)S(1)}) fusion(pred[512,1024]{1,0:T(8,128)(4,1)S(1)} %broadcast_compare_fusion, bf16[512,4,128]{0,2,1:T(8,128)(2,1)S(1)} %bitcast.33, bf16[1024,4,128]{0,2,1:T(8,128)(2,1)} %bitcast.34), kind=kOutput, calls=%fused_computation.3 | convolution fusion | flops 543160320 | bytes 10493952 | tf_op jit(solution)/shard_map/qhd,khd->hqk/dot_general | solution.py:22
  47.8 0.0 copy-start
  47.8 0.6 fusion.4
  48.5 2.6 %copy-done = f32[4,512,1024]{2,1,0:T(8,128)} copy-done((f32[4,512,1024]{2,1,0:T(8,128)}, f32[4,512,1024]{2,1,0:T(8,128)S(1)}, u32[]{:S(2)}) %copy-start) | copy-done | bytes 8388632
  51.1 3.0 %convert_reduce_fusion = f32[4,512]{1,0:T(4,128)S(1)} fusion(f32[4,512]{1,0:T(4,128)S(1)} %get-tuple-element.9, f32[4,512,1024]{2,1,0:T(8,128)S(1)} %get-tuple-element.11, pred[512,1024]{1,0:T(8,128)(4,1)S(1)} %broadcast_compare_fusion), kind=kLoop, calls=%fused_computation | loop fusion | flops 14678016 | bytes 8929280 | tf_op jit(solution)/shard_map/reduce_sum | solution.py:32
  54.1 7.2 %all_to_all.15 = f32[4,4,128]{2,1,0:T(4,128)S(1)} all-to-all(f32[4,4,128]{2,1,0:T(4,128)S(1)} %bitcast.36), channel_id=1, replica_groups=mesh['outer'=4,'inner'=8] {'outer'}, dimensions={0} | all-to-all | bytes 16384 | tf_op jit(solution)/shard_map/all_to_all | solution.py:70
  61.3 3.2 %all-to-all-start.1 = ((f32[4,4,128]{2,1,0:T(4,128)}), f32[4,4,128]{2,1,0:T(4,128)S(1)}, u32[]{:S(2)}, u32[]{:S(2)}) async-start(f32[4,4,128]{2,1,0:T(4,128)} %get-tuple-element.7), calls=%async_computation.1 | async-start | bytes 16384 | tf_op jit(solution)/shard_map/all_to_all | solution.py:69
  64.6 0.0 all-gather.5.cloned.1.call-done
  64.6 5.4 %fusion.1 = f32[512,4,128]{2,0,1:T(8,128)S(1)} fusion(bf16[1024,4,128]{0,2,1:T(8,128)(2,1)} %bitcast.38, f32[512,4]{0,1:T(4,128)S(1)} %get-tuple-element.8, f32[4,512,1024]{2,1,0:T(8,128)} %copy-done, f32[4,512]{1,0:T(4,128)S(1)} %get-tuple-element.9, pred[512,1024]{1,0:T(8,128)(4,1)S(1)} %broadcast_compare_fusion), kind=kOutput, calls=%fused_computation.5 | convolution fusion | flops 547618816 | bytes 11026432 | tf_op jit(solution)/shard_map/hqk,khd->qhd/dot_general | solution.py:33
  70.1 0.7 copy.20
  70.7 1.4 %reshape_reshape.3 = f32[4,128,512]{2,1,0:T(8,128)} reshape(f32[512,4,128]{2,1,0:T(4,128)S(1)} %copy.20) | data formatting | bytes 2097152 | tf_op jit(solution)/shard_map/reshape;reshape | solution.py:64
  72.1 0.0 all-to-all-done.1
  72.1 4.1 %all-to-all-start = ((f32[4,128,512]{2,1,0:T(8,128)}), f32[4,128,512]{2,1,0:T(8,128)S(1)}, u32[]{:S(2)}, u32[]{:S(2)}) async-start(f32[4,128,512]{2,1,0:T(8,128)} %reshape_reshape.3), calls=%async_computation | async-start | bytes 2097152 | tf_op jit(solution)/shard_map/all_to_all | solution.py:68
  76.3 0.1 copy.23
  76.4 0.1 copy.21
  76.6 0.6 mul.38
  77.2 0.4 mul.39
  77.6 8.1 %all-to-all-done = f32[4,128,512]{2,1,0:T(8,128)S(1)} async-done(((f32[4,128,512]{2,1,0:T(8,128)}), f32[4,128,512]{2,1,0:T(8,128)S(1)}, u32[]{:S(2)}, u32[]{:S(2)}) %all-to-all-start) | async-done | bytes 1048608 | tf_op jit(solution)/shard_map/all_to_all | solution.py:68
  85.7 0.2 multiply_reduce_fusion
  85.9 0.2 div.11
  86.1 0.7 fusion.2
  (6 shorter events, 0.0 us)
Async XLA Ops:
  6.5 38.2 %all-gather.3.cloned.1.call-start = ((), (), s32[]{:S(2)}) async-start(), calls=%async_computation.3 | async-start | bytes 1179648 | tf_op jit(solution)/shard_map/all_gather | solution.py:59
  8.2 56.4 %all-gather.5.cloned.1.call-start = ((), (), s32[]{:S(2)}) async-start(), calls=%async_computation.4 | async-start | bytes 1179648 | tf_op jit(solution)/shard_map/all_gather | solution.py:60
  47.8 3.2 %copy-start = (f32[4,512,1024]{2,1,0:T(8,128)}, f32[4,512,1024]{2,1,0:T(8,128)S(1)}, u32[]{:S(2)}) copy-start(f32[4,512,1024]{2,1,0:T(8,128)S(1)} %get-tuple-element.11) | copy-start | bytes 25165828
  61.3 10.8 %all-to-all-start.1 = ((f32[4,4,128]{2,1,0:T(4,128)}), f32[4,4,128]{2,1,0:T(4,128)S(1)}, u32[]{:S(2)}, u32[]{:S(2)}) async-start(f32[4,4,128]{2,1,0:T(4,128)} %get-tuple-element.7), calls=%async_computation.1 | async-start | bytes 16384 | tf_op jit(solution)/shard_map/all_to_all | solution.py:69
  72.1 13.6 %all-to-all-start = ((f32[4,128,512]{2,1,0:T(8,128)}), f32[4,128,512]{2,1,0:T(8,128)S(1)}, u32[]{:S(2)}, u32[]{:S(2)}) async-start(f32[4,128,512]{2,1,0:T(8,128)} %reshape_reshape.3), calls=%async_computation | async-start | bytes 2097152 | tf_op jit(solution)/shard_map/all_to_all | solution.py:68
Sparse Core Ops, SparseCore 0:
  8.9 26.7 all-gather.2
  37.3 22.5 all-gather.4
where the time goes:
time: 94.1 us; the launch traced here: 93.7 us
  blocking collectives  35.7 us (38%)
  local copies, waits for them, and re-layouts  14.6 us (16%)
  between operations  14.2 us (15%)
  matrix products  8.56 us (9%)
  waiting for transfers between devices  8.16 us (9%)
  starting transfers between devices  7.41 us (8%)
  other arithmetic  5.11 us (5%)
    unnamed x2, blocking collectives  18 us
    unnamed x11, local copies, waits for them, and re-layouts  11 us
    all_gather x1, blocking collectives, shards(): lax.all_gather(queries, 'outer', axis=0, tiled=True)  10.5 us
    all_to_all x1, waiting for transfers between devices, shards(): lax.all_to_all(acc_parts, 'outer', split_axis=0, concat_axis=0, tiled=True)  8.08 us
    all_to_all x1, blocking collectives, shards(): lax.all_to_all(total_parts, 'outer', split_axis=0, concat_axis=0, tiled=T...  7.24 us
    dot_general x1, matrix products, absorb(): jnp.einsum('hqk,khd->qhd', weights, vh, preferred_element_type=jnp.float32)  5.45 us
    all_to_all x1, starting transfers between devices, shards(): lax.all_to_all(acc_parts, 'outer', split_axis=0, concat_axis=0, tiled=True)  4.12 us
    all_to_all x1, starting transfers between devices, shards(): lax.all_to_all(top_parts, 'outer', split_axis=0, concat_axis=0, tiled=True)  3.25 us
  transfers between devices with their start and end apart: 4, of which 1 were waited for; matrix products, arithmetic and copies ran while one was open for 24% of the time, Pallas kernels for 0%

commit v1 on v0

v1 whole, which is shorter than its diff:
```python
import functools
import math

import jax
import jax.numpy as jnp
from jax import lax
from jax.experimental import pallas as pl
from jax.experimental.pallas import tpu as pltpu
from jax.sharding import PartitionSpec as P

HEADS = 4
CORES = 2
PAD = 16
LOW = -1e30
FLOOR = -1e29
BF16 = jnp.bfloat16
F32 = jnp.float32


def nt_dot(a, b):
    return lax.dot_general(a, b, (((1,), (1,)), ((), ())), preferred_element_type=F32)


def pack_kernel(pos_ref, q_ref, k_ref, v_ref, q_out, kv_out):
    tok = q_ref.shape[0]
    size = q_ref.shape[1] // HEADS
    per = HEADS // CORES
    pos = jnp.full((PAD, size), pos_ref[0].astype(F32), F32).astype(BF16)
    for c in range(CORES):
        parts_q, parts_kv = [], []
        for j in range(per):
            cols = slice((c * per + j) * size, (c * per + j + 1) * size)
            parts_q.append(q_ref[:, cols])
        for j in range(per):
            cols = slice((c * per + j) * size, (c * per + j + 1) * size)
            parts_kv.append(k_ref[:, cols])
        for j in range(per):
            cols = slice((c * per + j) * size, (c * per + j + 1) * size)
            parts_kv.append(v_ref[:, cols].astype(F32).T.astype(BF16))
        for d in range(q_out.shape[0] // CORES):
            for j, part in enumerate(parts_q):
                q_out[d * CORES + c, j * tok : (j + 1) * tok, :] = part
            q_out[d * CORES + c, per * tok :, :] = pos
        for d in range(kv_out.shape[0] // CORES):
            for j, part in enumerate(parts_kv):
                kv_out[d * CORES + c, j * tok : (j + 1) * tok, :] = part
            kv_out[d * CORES + c, 2 * per * tok :, :] = pos


def attend_kernel(q_ref, kv_ref, out_ref, k_all, v_all, kpos_all):
    nq, nk = q_ref.shape[0], kv_ref.shape[0]
    size = q_ref.shape[2]
    tok = size
    per = HEADS // CORES
    rate = size ** -0.5 * math.log2(math.e)
    for j in range(nk):
        for h in range(per):
            k_all[h, j * tok : (j + 1) * tok, :] = kv_ref[j, h * tok : (h + 1) * tok, :]
            v_all[h, 0:size, j * tok : (j + 1) * tok] = kv_ref[j, (per + h) * tok : (per + h + 1) * tok, :]
    for h in range(per):
        v_all[h, size:, :] = jnp.ones((PAD, nk * tok), BF16)
    two = 2 * tok
    for j in range(nk):
        base = kv_ref[j, 2 * per * tok : 2 * per * tok + 8, :].astype(F32)[0:1, :] * tok
        kpos_all[j] = jnp.concatenate([base, base], axis=1)
    rows = lax.broadcasted_iota(jnp.int32, (tok, two), 0).astype(F32)
    lanes = lax.broadcasted_iota(jnp.int32, (1, tok), 1).astype(F32)

    def body(i, _):
        q0, q1 = 2 * i, 2 * i + 1
        qp = [
            q_ref[q, per * tok : per * tok + 8, :].astype(F32)[0:1, :] * tok + lanes for q in (q0, q1)
        ]
        qpos = jnp.concatenate(qp, axis=1)
        stats = [[], []]
        for h in range(per):
            q = jnp.concatenate([q_ref[q0, h * tok : (h + 1) * tok, :], q_ref[q1, h * tok : (h + 1) * tok, :]], axis=0)
            s = nt_dot(k_all[h], q)
            parts = []
            for j in range(nk):
                keep = rows <= qpos - kpos_all[j]
                parts.append(jnp.where(keep, s[j * tok : (j + 1) * tok, :], LOW))
            s = jnp.concatenate(parts, axis=0)
            top = jnp.maximum(jnp.max(s, axis=0, keepdims=True), FLOOR).astype(BF16)
            p = jnp.exp2((s - top.astype(F32)) * rate).astype(BF16)
            o = jnp.dot(v_all[h], p, preferred_element_type=F32)
            total = o[size : size + 1, :]
            hi = total.astype(BF16)
            lo = (total - hi.astype(F32)).astype(BF16)
            for n, qi in enumerate((q0, q1)):
                cols = slice(n * tok, (n + 1) * tok)
                out_ref[qi, h * size : (h + 1) * size, :] = o[0:size, cols].astype(BF16)
                stats[n] += [top[:, cols].astype(F32), hi[:, cols].astype(F32), lo[:, cols].astype(F32)]
        for n, qi in enumerate((q0, q1)):
            rest = jnp.zeros((PAD - 3 * per, tok), F32)
            out_ref[qi, per * size :, :] = jnp.concatenate(stats[n] + [rest], axis=0).astype(BF16)
        return 0

    lax.fori_loop(0, nq // 2, body, 0, unroll=nq <= 8)


def combine_kernel(parts_ref, out_ref):
    n = parts_ref.shape[0]
    size = parts_ref.shape[2]
    per = HEADS // CORES
    rate = size ** -0.5 * math.log2(math.e)
    for c in range(CORES):
        stats = [parts_ref[w * CORES + c, per * size :, :].astype(F32) for w in range(n // CORES)]
        for h in range(per):
            tops = [s[3 * h : 3 * h + 1, :] for s in stats]
            best = functools.reduce(jnp.maximum, tops)
            factors = [jnp.exp2((t - best) * rate) for t in tops]
            denom = sum(f * (s[3 * h + 1 : 3 * h + 2, :] + s[3 * h + 2 : 3 * h + 3, :]) for f, s in zip(factors, stats))
            numer = sum(
                f * parts_ref[w * CORES + c, h * size : (h + 1) * size, :].astype(F32) for w, f in enumerate(factors)
            )
            col = (c * per + h) * size
            out_ref[:, col : col + size] = (numer / denom).T.astype(BF16)


def vmem(n=1):
    return [pl.BlockSpec(memory_space=pltpu.VMEM)] * n


def shards(n_out, n_in, queries, keys, values, block_pos):
    tok, width = queries.shape
    size = width // HEADS
    per = HEADS // CORES
    params = pltpu.CompilerParams(vmem_limit_bytes=40 * 1024 * 1024)
    with jax.named_scope("pack"):
        q_send, kv_send = pl.pallas_call(
            pack_kernel,
            out_shape=(
                jax.ShapeDtypeStruct((n_in, per * tok + PAD, size), BF16),
                jax.ShapeDtypeStruct((n_out * CORES, 2 * per * tok + PAD, size), BF16),
            ),
            in_specs=[pl.BlockSpec(memory_space=pltpu.SMEM)] + vmem(3),
            out_specs=tuple(vmem(2)),
            compiler_params=params,
            name="pack",
        )(block_pos, queries, keys, values)
    with jax.named_scope("exchange"):
        groups = [
            [o * n_in + w * CORES + c for o in range(n_out) for c in range(CORES)] for w in range(n_in // CORES)
        ]
        kv = lax.all_to_all(
            kv_send, ("outer", "inner"), split_axis=0, concat_axis=0, tiled=True, axis_index_groups=groups
        )
        q = lax.all_to_all(q_send, "inner", split_axis=0, concat_axis=0, tiled=True)
    nk = kv.shape[0]
    with jax.named_scope("attend"):
        parts = pl.pallas_call(
            attend_kernel,
            out_shape=jax.ShapeDtypeStruct((n_in, per * size + PAD, tok), BF16),
            in_specs=vmem(2),
            out_specs=vmem()[0],
            scratch_shapes=[
                pltpu.VMEM((per, nk * tok, size), BF16),
                pltpu.VMEM((per, size + PAD, nk * tok), BF16),
                pltpu.VMEM((nk, 1, 2 * tok), F32),
            ],
            compiler_params=params,
            name="attend",
        )(q, kv)
    with jax.named_scope("return"):
        parts = lax.all_to_all(parts, "inner", split_axis=0, concat_axis=0, tiled=True)
    with jax.named_scope("combine"):
        return pl.pallas_call(
            combine_kernel,
            out_shape=jax.ShapeDtypeStruct((tok, width), BF16),
            in_specs=vmem(),
            out_specs=vmem()[0],
            compiler_params=params,
            name="combine",
        )(parts)


def solution(mesh):
    n_out, n_in = mesh.shape["outer"], mesh.shape["inner"]
    return jax.shard_map(
        functools.partial(shards, n_out, n_in),
        mesh=mesh,
        in_specs=(
            P(("outer", "inner"), None),
            P(("outer", "inner"), None),
            P(("outer", "inner"), None),
            P(("outer", "inner")),
        ),
        out_specs=P(("outer", "inner"), None),
        check_vma=False,
    )
```

time: 94.1 us -> 69.9 us (0.74)
  blocking collectives: 35.7 us -> 59.8 us
  between operations: 14.2 us -> 0.68 us
  local copies, waits for them, and re-layouts: 14.6 us -> 2.7 us
  matrix products: 8.56 us -> 0 us
  waiting for transfers between devices: 8.16 us -> 0 us
  starting transfers between devices: 7.41 us -> 0 us
  Pallas kernels: 0 us -> 6.43 us
  other arithmetic: 5.11 us -> 0 us
    all_to_all x1 -> x3, blocking collectives: 7.24 us -> 59.8 us  [the longest x1 20.7 us: shards(): q = lax.all_to_all(q_send, 'inner', split_axis=0, concat_axis=0, tiled=True)]
    unnamed x2 -> x0, blocking collectives: 18 us -> none
    all_gather x1 -> x0, blocking collectives: 10.5 us -> none  [shards(): lax.all_gather(queries, 'outer', axis=0, tiled=True)]
    dot_general x2 -> x0, matrix products: 8.56 us -> none  [the longest x1 5.45 us: absorb(): jnp.einsum('hqk,khd->qhd', weights, vh, preferred_element_type=jnp.float32)]
    unnamed x11 -> x6, local copies, waits for them, and re-layouts: 11 us -> 2.7 us
    all_to_all x2 -> x0, waiting for transfers between devices: 8.08 us -> none  [the longest x1 8.08 us: shards(): lax.all_to_all(acc_parts, 'outer', split_axis=0, concat_axis=0, tiled=True)]
    all_to_all x2 -> x0, starting transfers between devices: 7.37 us -> none  [the longest x1 4.12 us: shards(): lax.all_to_all(acc_parts, 'outer', split_axis=0, concat_axis=0, tiled=True)]
    pallas_call x0 -> x3, Pallas kernels: none -> 6.43 us  [the longest x1 5.39 us: shards(): pl.pallas_call(attend_kernel, out_shape=jax.ShapeDtypeStruct((n_in, per *...]
  transfers between devices with their start and end apart: 4 -> 0, of which waited for: 1 -> 0; matrix products, arithmetic and copies ran while one was open for 24% -> 0% of each run, Pallas kernels for 0% -> 0%
where the time goes in v1:
time: 69.9 us; the launch traced here: 69.7 us
  blocking collectives  59.8 us (86%)
  Pallas kernels  6.43 us (9%)
  local copies, waits for them, and re-layouts  2.7 us (4%)
    all_to_all x1, blocking collectives, shards(): q = lax.all_to_all(q_send, 'inner', split_axis=0, concat_axis=0, tiled=True)  20.7 us
    all_to_all x1, blocking collectives, shards(): lax.all_to_all(kv_send, ('outer', 'inner'), split_axis=0, concat_axis=0,...  20.7 us
    all_to_all x1, blocking collectives, shards(): lax.all_to_all(parts, 'inner', split_axis=0, concat_axis=0, tiled=True)  18.4 us
    pallas_call x1, Pallas kernels, shards(): pl.pallas_call(attend_kernel, out_shape=jax.ShapeDtypeStruct((n_in, per *...  5.39 us
    unnamed x6, local copies, waits for them, and re-layouts  2.7 us

profile of v1, /device:TPU:0, one launch (start us, length us, event | category | flops | bytes accessed | tf_op | source)
XLA Modules:
  0.0 69.7 jit_solution(13416841947889064321)
XLA Ops:
  0.7 0.0 copy-start
  0.7 0.9 %copy-done = bf16[128,512]{1,0:T(8,128)(2,1)S(1)} copy-done((bf16[128,512]{1,0:T(8,128)(2,1)S(1)}, bf16[128,512]{1,0:T(8,128)(2,1)}, u32[]{:S(2)}) %copy-start) | copy-done | bytes 131096
  1.6 0.0 copy-start.1
  1.6 0.9 %copy-done.1 = bf16[128,512]{1,0:T(8,128)(2,1)S(1)} copy-done((bf16[128,512]{1,0:T(8,128)(2,1)S(1)}, bf16[128,512]{1,0:T(8,128)(2,1)}, u32[]{:S(2)}) %copy-start.1) | copy-done | bytes 131096
  2.5 0.0 copy-start.2
  2.5 0.9 %copy-done.2 = bf16[128,512]{1,0:T(8,128)(2,1)S(1)} copy-done((bf16[128,512]{1,0:T(8,128)(2,1)S(1)}, bf16[128,512]{1,0:T(8,128)(2,1)}, u32[]{:S(2)}) %copy-start.2) | copy-done | bytes 131096
  3.4 0.2 pack.1
  3.6 20.7 %all_to_all.15.kv_ref = bf16[8,528,128]{2,1,0:T(8,128)(2,1)S(1)} all-to-all(bf16[8,528,128]{2,1,0:T(8,128)(2,1)S(1)} %get-tuple-element.8), channel_id=1, replica_groups={{0,1,8,9,16,17,24,25},{2,3,10,11,18,19,26,27},{4,5,12,13,20,21,28,29},{..., dimensions={0} | all-to-all | bytes 2162688 | tf_op jit(solution)/shard_map/exchange/all_to_all | solution.py:146
  24.2 20.7 %all_to_all.16.q_ref = bf16[8,272,128]{2,1,0:T(8,128)(2,1)S(1)} all-to-all(bf16[8,272,128]{2,1,0:T(8,128)(2,1)S(1)} %get-tuple-element.7), channel_id=1, replica_groups=mesh['outer'=4,'inner'=8] {'inner'}, dimensions={0} | all-to-all | bytes 1114112 | tf_op jit(solution)/shard_map/exchange/all_to_all | solution.py:149
  45.0 5.4 %attend.1 = bf16[8,272,128]{2,1,0:T(8,128)(2,1)S(1)} custom-call(bf16[8,272,128]{2,1,0:T(8,128)(2,1)S(1)} %all_to_all.16.q_ref, bf16[8,528,128]{2,1,0:T(8,128)(2,1)S(1)} %all_to_all.15.kv_ref), custom_call_target="tpu_custom_call" | custom-call | tf_op jit(solution)/shard_map/attend/attend/pallas_call | solution.py:152
  50.4 18.4 %all_to_all.17.parts_ref = bf16[8,272,128]{2,1,0:T(8,128)(2,1)S(1)} all-to-all(bf16[8,272,128]{2,1,0:T(8,128)(2,1)S(1)} %attend.1), channel_id=1, replica_groups=mesh['outer'=4,'inner'=8] {'inner'}, dimensions={0} | all-to-all | bytes 1114112 | tf_op jit(solution)/shard_map/return/all_to_all | solution.py:166
  68.8 0.8 %combine.1 = bf16[128,512]{1,0:T(8,128)(2,1)} custom-call(bf16[8,272,128]{2,1,0:T(8,128)(2,1)S(1)} %all_to_all.17.parts_ref), custom_call_target="tpu_custom_call" | custom-call | tf_op jit(solution)/shard_map/combine/combine/pallas_call | solution.py:168
Async XLA Ops:
  0.7 0.9 %copy-start = (bf16[128,512]{1,0:T(8,128)(2,1)S(1)}, bf16[128,512]{1,0:T(8,128)(2,1)}, u32[]{:S(2)}) copy-start(bf16[128,512]{1,0:T(8,128)(2,1)} %q_ref.1) | copy-start | bytes 393220
  1.6 0.9 %copy-start.1 = (bf16[128,512]{1,0:T(8,128)(2,1)S(1)}, bf16[128,512]{1,0:T(8,128)(2,1)}, u32[]{:S(2)}) copy-start(bf16[128,512]{1,0:T(8,128)(2,1)} %k_ref.1) | copy-start | bytes 393220
  2.5 0.9 %copy-start.2 = (bf16[128,512]{1,0:T(8,128)(2,1)S(1)}, bf16[128,512]{1,0:T(8,128)(2,1)}, u32[]{:S(2)}) copy-start(bf16[128,512]{1,0:T(8,128)(2,1)} %v_ref.1) | copy-start | bytes 393220

commit v2 on v1

v2 whole, which is shorter than its diff:
```python
import functools
import math

import jax
import jax.numpy as jnp
from jax import lax
from jax.experimental import pallas as pl
from jax.experimental.pallas import tpu as pltpu
from jax.sharding import PartitionSpec as P

HEADS = 4
CORES = 2
PER = HEADS // CORES
PAD = 16
LOW = -1e30
FLOOR = -1e29
BF16 = jnp.bfloat16
F32 = jnp.float32


def nt_dot(a, b):
    return lax.dot_general(a, b, (((1,), (1,)), ((), ())), preferred_element_type=F32)


def pack_kernel(pos_ref, q_ref, k_ref, v_ref, q_same, kv_same, q_other, kv_other, v_buf, sems):
    tok = q_ref.shape[0]
    size = q_ref.shape[1] // HEADS
    core = lax.rem(lax.axis_index("inner"), CORES)
    copies = [pltpu.make_async_copy(v_ref, v_buf, sems.at[0])]
    for x, (q_out, kv_out) in enumerate(((q_same, kv_same), (q_other, kv_other))):
        pair = jnp.bitwise_xor(core, x)
        for j in range(PER):
            cols = pl.ds(pl.multiple_of((pair * PER + j) * size, size), size)
            rows = pl.ds(j * tok, tok)
            at = 1 + 2 * (x * PER + j)
            copies.append(pltpu.make_async_copy(q_ref.at[:, cols], q_out.at[rows, :], sems.at[at]))
            copies.append(pltpu.make_async_copy(k_ref.at[:, cols], kv_out.at[rows, :], sems.at[at + 1]))
    for copy in copies:
        copy.start()
    pos = jnp.full((PAD, size), pos_ref[0].astype(F32), F32).astype(BF16)
    for q_out, kv_out in ((q_same, kv_same), (q_other, kv_other)):
        q_out[PER * tok :, :] = pos
        kv_out[2 * PER * tok :, :] = pos
    copies[0].wait()
    for x, kv_out in enumerate((kv_same, kv_other)):
        pair = jnp.bitwise_xor(core, x)
        for j in range(PER):
            cols = pl.ds(pl.multiple_of((pair * PER + j) * size, size), size)
            kv_out[(PER + j) * tok : (PER + j + 1) * tok, :] = v_buf[:, cols].astype(F32).T.astype(BF16)
    for copy in copies[1:]:
        copy.wait()


def attend_kernel(nq, nk, *refs):
    q_refs, kv_refs, out_refs = refs[:nq], refs[nq : nq + nk], refs[nq + nk : nq + nk + nq]
    k_all, v_all, kpos_all = refs[nq + nk + nq :]
    size = q_refs[0].shape[1]
    tok = size
    rate = size ** -0.5 * math.log2(math.e)
    for j in range(nk):
        for h in range(PER):
            k_all[h, j * tok : (j + 1) * tok, :] = kv_refs[j][h * tok : (h + 1) * tok, :]
            v_all[h, 0:size, j * tok : (j + 1) * tok] = kv_refs[j][(PER + h) * tok : (PER + h + 1) * tok, :]
    for h in range(PER):
        v_all[h, size:, :] = jnp.ones((PAD, nk * tok), BF16)
    two = 2 * tok
    for j in range(nk):
        base = kv_refs[j][2 * PER * tok : 2 * PER * tok + 8, :].astype(F32)[0:1, :] * tok
        kpos_all[j] = jnp.concatenate([base, base], axis=1)
    rows = lax.broadcasted_iota(jnp.int32, (tok, two), 0).astype(F32)
    lanes = lax.broadcasted_iota(jnp.int32, (1, tok), 1).astype(F32)

    for i in range(nq // 2):
        pair = (2 * i, 2 * i + 1)
        qpos = jnp.concatenate(
            [q_refs[q][PER * tok : PER * tok + 8, :].astype(F32)[0:1, :] * tok + lanes for q in pair], axis=1
        )
        stats = [[], []]
        for h in range(PER):
            q = jnp.concatenate([q_refs[n][h * tok : (h + 1) * tok, :] for n in pair], axis=0)
            s = nt_dot(k_all[h], q)
            parts = []
            for j in range(nk):
                keep = rows <= qpos - kpos_all[j]
                parts.append(jnp.where(keep, s[j * tok : (j + 1) * tok, :], LOW))
            s = jnp.concatenate(parts, axis=0)
            top = jnp.maximum(jnp.max(s, axis=0, keepdims=True), FLOOR).astype(BF16)
            p = jnp.exp2((s - top.astype(F32)) * rate).astype(BF16)
            o = jnp.dot(v_all[h], p, preferred_element_type=F32)
            total = o[size : size + 1, :]
            hi = total.astype(BF16)
            lo = (total - hi.astype(F32)).astype(BF16)
            for n, at in enumerate(pair):
                cols = slice(n * tok, (n + 1) * tok)
                out_refs[at][h * size : (h + 1) * size, :] = o[0:size, cols].astype(BF16)
                stats[n] += [top[:, cols].astype(F32), hi[:, cols].astype(F32), lo[:, cols].astype(F32)]
        for n, at in enumerate(pair):
            rest = jnp.zeros((PAD - 3 * PER, tok), F32)
            out_refs[at][PER * size :, :] = jnp.concatenate(stats[n] + [rest], axis=0).astype(BF16)


def combine_kernel(n, *refs):
    parts, out_ref = refs[:n], refs[n]
    size = parts[0].shape[1]
    rate = size ** -0.5 * math.log2(math.e)
    core = lax.rem(lax.axis_index("inner"), CORES)
    for x in range(CORES):
        mine = parts[x::CORES]
        pair = jnp.bitwise_xor(core, x)
        stats = [part[PER * size :, :].astype(F32) for part in mine]
        for h in range(PER):
            tops = [s[3 * h : 3 * h + 1, :] for s in stats]
            best = functools.reduce(jnp.maximum, tops)
            factors = [jnp.exp2((t - best) * rate) for t in tops]
            denom = sum(f * (s[3 * h + 1 : 3 * h + 2, :] + s[3 * h + 2 : 3 * h + 3, :]) for f, s in zip(factors, stats))
            numer = sum(f * part[h * size : (h + 1) * size, :].astype(F32) for f, part in zip(factors, mine))
            cols = pl.ds(pl.multiple_of((pair * PER + h) * size, size), size)
            out_ref[:, cols] = (numer / denom).T.astype(BF16)


def vmem(n=1):
    return [pl.BlockSpec(memory_space=pltpu.VMEM)] * n


def shards(n_out, n_in, queries, keys, values, block_pos):
    tok, width = queries.shape
    size = width // HEADS
    chips = n_in // CORES
    params = pltpu.CompilerParams(vmem_limit_bytes=40 * 1024 * 1024)
    q_piece = jax.ShapeDtypeStruct((PER * tok + PAD, size), BF16)
    kv_piece = jax.ShapeDtypeStruct((2 * PER * tok + PAD, size), BF16)
    with jax.named_scope("pack"):
        q_same, kv_same, q_other, kv_other = pl.pallas_call(
            pack_kernel,
            out_shape=(q_piece, kv_piece, q_piece, kv_piece),
            in_specs=[pl.BlockSpec(memory_space=pltpu.SMEM)] + [pl.BlockSpec(memory_space=pltpu.HBM)] * 3,
            out_specs=tuple(vmem(4)),
            scratch_shapes=[pltpu.VMEM((tok, width), BF16), pltpu.SemaphoreType.DMA((1 + 4 * PER,))],
            compiler_params=params,
            name="pack",
        )(block_pos, queries, keys, values)

    def along_inner(r, x):
        return [(w * CORES + c, (w + r) % chips * CORES + (c ^ x)) for w in range(chips) for c in range(CORES)]

    def along_plane(r, x):
        return [
            (o * n_in + w * CORES + c, (o + r) % n_out * n_in + w * CORES + (c ^ x))
            for o in range(n_out)
            for w in range(chips)
            for c in range(CORES)
        ]

    with jax.named_scope("exchange"):
        q_parts, kv_parts = [], []
        for r in range(n_out):
            for x in range(CORES):
                piece = (kv_same, kv_other)[x]
                kv_parts.append(piece if r + x == 0 else lax.ppermute(piece, ("outer", "inner"), along_plane(r, x)))
        for r in range(chips):
            for x in range(CORES):
                piece = (q_same, q_other)[x]
                q_parts.append(piece if r + x == 0 else lax.ppermute(piece, "inner", along_inner(r, x)))
    nq, nk = len(q_parts), len(kv_parts)
    with jax.named_scope("attend"):
        parts = pl.pallas_call(
            functools.partial(attend_kernel, nq, nk),
            out_shape=(jax.ShapeDtypeStruct((PER * size + PAD, tok), BF16),) * nq,
            in_specs=vmem(nq + nk),
            out_specs=tuple(vmem(nq)),
            scratch_shapes=[
                pltpu.VMEM((PER, nk * tok, size), BF16),
                pltpu.VMEM((PER, size + PAD, nk * tok), BF16),
                pltpu.VMEM((nk, 1, 2 * tok), F32),
            ],
            compiler_params=params,
            name="attend",
        )(*q_parts, *kv_parts)
    with jax.named_scope("return"):
        back = []
        for i, part in enumerate(parts):
            r, x = i // CORES, i % CORES
            back.append(part if i == 0 else lax.ppermute(part, "inner", along_inner(-r, x)))
    with jax.named_scope("combine"):
        return pl.pallas_call(
            functools.partial(combine_kernel, nq),
            out_shape=jax.ShapeDtypeStruct((tok, width), BF16),
            in_specs=vmem(nq),
            out_specs=vmem()[0],
            compiler_params=params,
            name="combine",
        )(*back)


def solution(mesh):
    n_out, n_in = mesh.shape["outer"], mesh.shape["inner"]
    return jax.shard_map(
        functools.partial(shards, n_out, n_in),
        mesh=mesh,
        in_specs=(
            P(("outer", "inner"), None),
            P(("outer", "inner"), None),
            P(("outer", "inner"), None),
            P(("outer", "inner")),
        ),
        out_specs=P(("outer", "inner"), None),
        check_vma=False,
    )
```

time: 69.9 us -> 56.6 us (0.81)
  blocking collectives: 59.8 us -> 0 us
  starting transfers between devices: 0 us -> 23.3 us
  waiting for transfers between devices: 0 us -> 23 us
    all_to_all x3 -> x0, blocking collectives: 59.8 us -> none  [the longest x1 20.7 us: shards(): q = lax.all_to_all(q_send, 'inner', split_axis=0, concat_axis=0, tiled=True)]
    ppermute x0 -> x21, starting transfers between devices: none -> 23.3 us  [the longest x7 9.76 us: shards(): lax.ppermute(piece, 'inner', along_inner(r, x))]
    ppermute x0 -> x21, waiting for transfers between devices: none -> 23 us  [the longest x7 9.52 us: shards(): lax.ppermute(part, 'inner', along_inner(-r, x))]
  transfers between devices with their start and end apart: 0 -> 21, of which waited for: 0 -> 9; matrix products, arithmetic and copies ran while one was open for 0% -> 0% of each run, Pallas kernels for 0% -> 0%
where the time goes in v2:
time: 56.6 us; the launch traced here: 56.5 us
  starting transfers between devices  23.3 us (41%)
  waiting for transfers between devices  23 us (41%)
  Pallas kernels  6.69 us (12%)
  local copies, waits for them, and re-layouts  2.7 us (5%)
  between operations  0.7 us (1%)
    ppermute x7, starting transfers between devices, shards(): lax.ppermute(piece, 'inner', along_inner(r, x))  9.76 us
    ppermute x7, waiting for transfers between devices, shards(): lax.ppermute(part, 'inner', along_inner(-r, x))  9.52 us
    ppermute x7, starting transfers between devices, shards(): lax.ppermute(piece, ('outer', 'inner'), along_plane(r, x))  7.48 us
    ppermute x7, waiting for transfers between devices, shards(): lax.ppermute(piece, ('outer', 'inner'), along_plane(r, x))  6.89 us
    ppermute x7, waiting for transfers between devices, shards(): lax.ppermute(piece, 'inner', along_inner(r, x))  6.64 us
    ppermute x7, starting transfers between devices, shards(): lax.ppermute(part, 'inner', along_inner(-r, x))  6.08 us
    pallas_call x1, Pallas kernels, shards(): pl.pallas_call(functools.partial(attend_kernel, nq, nk), out_shape=(jax.S...  5.43 us
    unnamed x6, local copies, waits for them, and re-layouts  2.7 us
  transfers between devices with their start and end apart: 21, of which 9 were waited for; matrix products, arithmetic and copies ran while one was open for 0% of the time, Pallas kernels for 0%

profile of v2, /device:TPU:0, one launch (start us, length us, event | category | flops | bytes accessed | tf_op | source)
XLA Modules:
  0.0 56.5 jit_solution(513586899465872388)
XLA Ops:
  0.7 0.9 %copy-done = bf16[128,512]{1,0:T(8,128)(2,1)S(1)} copy-done((bf16[128,512]{1,0:T(8,128)(2,1)S(1)}, bf16[128,512]{1,0:T(8,128)(2,1)}, u32[]{:S(2)}) %copy-start) | copy-done | bytes 131096
  1.6 0.9 %copy-done.1 = bf16[128,512]{1,0:T(8,128)(2,1)S(1)} copy-done((bf16[128,512]{1,0:T(8,128)(2,1)S(1)}, bf16[128,512]{1,0:T(8,128)(2,1)}, u32[]{:S(2)}) %copy-start.1) | copy-done | bytes 131096
  2.5 0.9 %copy-done.2 = bf16[128,512]{1,0:T(8,128)(2,1)S(1)} copy-done((bf16[128,512]{1,0:T(8,128)(2,1)S(1)}, bf16[128,512]{1,0:T(8,128)(2,1)}, u32[]{:S(2)}) %copy-start.2) | copy-done | bytes 131096
  3.4 0.4 pack.1
  3.8 5.1 %collective-permute-start.5 = (bf16[272,128]{1,0:T(8,128)(2,1)S(1)}, bf16[272,128]{1,0:T(8,128)(2,1)S(1)}, u32[]{:S(2)}, u32[]{:S(2)}) collective-permute-start(bf16[272,128]{1,0:T(8,128)(2,1)S(1)} %get-tuple-element.17.refs_0_), channel_id=1, source_target_pairs={{0,6},{1,7},{2,0},{3,1},{4,2},{5,3},{6,4},{7,5},{8,14},{9,15},{10,... | collective-permute-start | bytes 208904 | tf_op jit(solution)/shard_map/exchange/ppermute | solution.py:163
  8.9 0.0 collective-permute-start.3
  8.9 1.0 %collective-permute-start.1 = (bf16[272,128]{1,0:T(8,128)(2,1)S(1)}, bf16[272,128]{1,0:T(8,128)(2,1)S(1)}, u32[]{:S(2)}, u32[]{:S(2)}) collective-permute-start(bf16[272,128]{1,0:T(8,128)(2,1)S(1)} %get-tuple-element.17.refs_0_), channel_id=1, source_target_pairs={{0,2},{1,3},{2,4},{3,5},{4,6},{5,7},{6,0},{7,1},{8,10},{9,11},{10,... | collective-permute-start | bytes 208904 | tf_op jit(solution)/shard_map/exchange/ppermute | solution.py:163
  9.9 1.7 %collective-permute-start.6 = (bf16[272,128]{1,0:T(8,128)(2,1)S(1)}, bf16[272,128]{1,0:T(8,128)(2,1)S(1)}, u32[]{:S(2)}, u32[]{:S(2)}) collective-permute-start(bf16[272,128]{1,0:T(8,128)(2,1)S(1)} %get-tuple-element.18), channel_id=1, source_target_pairs={{0,7},{1,6},{2,1},{3,0},{4,3},{5,2},{6,5},{7,4},{8,15},{9,14},{10,... | collective-permute-start | bytes 208904 | tf_op jit(solution)/shard_map/exchange/ppermute | solution.py:163
  11.6 2.4 %collective-permute-start.12 = (bf16[528,128]{1,0:T(8,128)(2,1)S(1)}, bf16[528,128]{1,0:T(8,128)(2,1)S(1)}, u32[]{:S(2)}, u32[]{:S(2)}) collective-permute-start(bf16[528,128]{1,0:T(8,128)(2,1)S(1)} %get-tuple-element.19.refs_8_), channel_id=1, source_target_pairs={{0,24},{1,25},{2,26},{3,27},{4,28},{5,29},{6,30},{7,31},{8,0},{9,1... | collective-permute-start | bytes 405512 | tf_op jit(solution)/shard_map/exchange/ppermute | solution.py:159
  14.0 0.0 collective-permute-done.5.refs_6_
  14.0 0.5 collective-permute-start.10
  14.5 1.3 %collective-permute-done.3.refs_4_ = bf16[272,128]{1,0:T(8,128)(2,1)S(1)} collective-permute-done((bf16[272,128]{1,0:T(8,128)(2,1)S(1)}, bf16[272,128]{1,0:T(8,128)(2,1)S(1)}, u32[]{:S(2)}, u32[]{:S(2)}) %collective-permute-start.3) | collective-permute-done | bytes 69664 | tf_op jit(solution)/shard_map/exchange/ppermute | solution.py:163
  15.9 0.1 collective-permute-start.4
  16.0 0.0 collective-permute-done.1.refs_2_
  16.0 1.8 %collective-permute-start.2 = (bf16[272,128]{1,0:T(8,128)(2,1)S(1)}, bf16[272,128]{1,0:T(8,128)(2,1)S(1)}, u32[]{:S(2)}, u32[]{:S(2)}) collective-permute-start(bf16[272,128]{1,0:T(8,128)(2,1)S(1)} %get-tuple-element.18), channel_id=1, source_target_pairs={{0,3},{1,2},{2,5},{3,4},{4,7},{5,6},{6,1},{7,0},{8,11},{9,10},{10,... | collective-permute-start | bytes 208904 | tf_op jit(solution)/shard_map/exchange/ppermute | solution.py:163
  17.8 0.0 collective-permute-done.6.refs_7_
  17.8 0.0 collective-permute-start
  17.8 5.3 %collective-permute-done.4.refs_5_ = bf16[272,128]{1,0:T(8,128)(2,1)S(1)} collective-permute-done((bf16[272,128]{1,0:T(8,128)(2,1)S(1)}, bf16[272,128]{1,0:T(8,128)(2,1)S(1)}, u32[]{:S(2)}, u32[]{:S(2)}) %collective-permute-start.4) | collective-permute-done | bytes 69664 | tf_op jit(solution)/shard_map/exchange/ppermute | solution.py:163
  23.1 1.2 %collective-permute-start.8 = (bf16[528,128]{1,0:T(8,128)(2,1)S(1)}, bf16[528,128]{1,0:T(8,128)(2,1)S(1)}, u32[]{:S(2)}, u32[]{:S(2)}) collective-permute-start(bf16[528,128]{1,0:T(8,128)(2,1)S(1)} %get-tuple-element.19.refs_8_), channel_id=1, source_target_pairs={{0,8},{1,9},{2,10},{3,11},{4,12},{5,13},{6,14},{7,15},{8,16},{9,17... | collective-permute-start | bytes 405512 | tf_op jit(solution)/shard_map/exchange/ppermute | solution.py:159
  24.3 0.0 collective-permute-done.2.refs_3_
  24.3 1.2 %collective-permute-start.13 = (bf16[528,128]{1,0:T(8,128)(2,1)S(1)}, bf16[528,128]{1,0:T(8,128)(2,1)S(1)}, u32[]{:S(2)}, u32[]{:S(2)}) collective-permute-start(bf16[528,128]{1,0:T(8,128)(2,1)S(1)} %get-tuple-element.20), channel_id=1, source_target_pairs={{0,25},{1,24},{2,27},{3,26},{4,29},{5,28},{6,31},{7,30},{8,1},{9,0... | collective-permute-start | bytes 405512 | tf_op jit(solution)/shard_map/exchange/ppermute | solution.py:159
  25.5 0.0 collective-permute-done.refs_1_
  25.5 1.8 %collective-permute-start.11 = (bf16[528,128]{1,0:T(8,128)(2,1)S(1)}, bf16[528,128]{1,0:T(8,128)(2,1)S(1)}, u32[]{:S(2)}, u32[]{:S(2)}) collective-permute-start(bf16[528,128]{1,0:T(8,128)(2,1)S(1)} %get-tuple-element.20), channel_id=1, source_target_pairs={{0,17},{1,16},{2,19},{3,18},{4,21},{5,20},{6,23},{7,22},{8,25},{9,... | collective-permute-start | bytes 405512 | tf_op jit(solution)/shard_map/exchange/ppermute | solution.py:159
  27.3 0.0 collective-permute-done.12.refs_14_
  27.3 0.0 collective-permute-start.9
  27.3 0.0 collective-permute-done.10.refs_12_
  27.3 0.4 collective-permute-start.7
  27.7 2.8 %collective-permute-done.8.refs_10_ = bf16[528,128]{1,0:T(8,128)(2,1)S(1)} collective-permute-done((bf16[528,128]{1,0:T(8,128)(2,1)S(1)}, bf16[528,128]{1,0:T(8,128)(2,1)S(1)}, u32[]{:S(2)}, u32[]{:S(2)}) %collective-permute-start.8) | collective-permute-done | bytes 135200 | tf_op jit(solution)/shard_map/exchange/ppermute | solution.py:159
  30.5 1.3 %collective-permute-done.13.refs_15_ = bf16[528,128]{1,0:T(8,128)(2,1)S(1)} collective-permute-done((bf16[528,128]{1,0:T(8,128)(2,1)S(1)}, bf16[528,128]{1,0:T(8,128)(2,1)S(1)}, u32[]{:S(2)}, u32[]{:S(2)}) %collective-permute-start.13) | collective-permute-done | bytes 135200 | tf_op jit(solution)/shard_map/exchange/ppermute | solution.py:159
  31.7 1.1 %collective-permute-done.11.refs_13_ = bf16[528,128]{1,0:T(8,128)(2,1)S(1)} collective-permute-done((bf16[528,128]{1,0:T(8,128)(2,1)S(1)}, bf16[528,128]{1,0:T(8,128)(2,1)S(1)}, u32[]{:S(2)}, u32[]{:S(2)}) %collective-permute-start.11) | collective-permute-done | bytes 135200 | tf_op jit(solution)/shard_map/exchange/ppermute | solution.py:159
  32.8 1.8 %collective-permute-done.9.refs_11_ = bf16[528,128]{1,0:T(8,128)(2,1)S(1)} collective-permute-done((bf16[528,128]{1,0:T(8,128)(2,1)S(1)}, bf16[528,128]{1,0:T(8,128)(2,1)S(1)}, u32[]{:S(2)}, u32[]{:S(2)}) %collective-permute-start.9) | collective-permute-done | bytes 135200 | tf_op jit(solution)/shard_map/exchange/ppermute | solution.py:159
  34.6 0.0 collective-permute-done.7.refs_9_
  34.6 5.4 %attend.1 = (bf16[272,128]{1,0:T(8,128)(2,1)S(1)}, bf16[272,128]{1,0:T(8,128)(2,1)S(1)}, bf16[272,128]{1,0:T(8,128)(2,1)S(1)}, bf16[272,128]{1,0:T(8,128)(2,1)S(...) custom-call(bf16[272,128]{1,0:T(8,128)(2,1)S(1)} %get-tuple-element., ...), custom_call_target="tpu_custom_call" | custom-call | tf_op jit(solution)/shard_map/attend/attend/pallas_call | solution.py:166
  40.0 0.7 %collective-permute-start.14 = (bf16[272,128]{1,0:T(8,128)(2,1)S(1)}, bf16[272,128]{1,0:T(8,128)(2,1)S(1)}, u32[]{:S(2)}, u32[]{:S(2)}) collective-permute-start(bf16[272,128]{1,0:T(8,128)(2,1)S(1)} %get-tuple-element.22), channel_id=1, source_target_pairs={{0,1},{1,0},{2,3},{3,2},{4,5},{5,4},{6,7},{7,6},{8,9},{9,8},{10,11... | collective-permute-start | bytes 208904 | tf_op jit(solution)/shard_map/return/ppermute | solution.py:183
  40.7 0.0 collective-permute-start.15
  40.7 0.5 collective-permute-start.16
  41.2 2.4 %collective-permute-start.17 = (bf16[272,128]{1,0:T(8,128)(2,1)S(1)}, bf16[272,128]{1,0:T(8,128)(2,1)S(1)}, u32[]{:S(2)}, u32[]{:S(2)}) collective-permute-start(bf16[272,128]{1,0:T(8,128)(2,1)S(1)} %get-tuple-element.25), channel_id=1, source_target_pairs={{0,4},{1,5},{2,6},{3,7},{4,0},{5,1},{6,2},{7,3},{8,12},{9,13},{10,... | collective-permute-start | bytes 208904 | tf_op jit(solution)/shard_map/return/ppermute | solution.py:183
  43.6 0.6 %collective-permute-start.18 = (bf16[272,128]{1,0:T(8,128)(2,1)S(1)}, bf16[272,128]{1,0:T(8,128)(2,1)S(1)}, u32[]{:S(2)}, u32[]{:S(2)}) collective-permute-start(bf16[272,128]{1,0:T(8,128)(2,1)S(1)} %get-tuple-element.26), channel_id=1, source_target_pairs={{0,5},{1,4},{2,7},{3,6},{4,1},{5,0},{6,3},{7,2},{8,13},{9,12},{10,... | collective-permute-start | bytes 208904 | tf_op jit(solution)/shard_map/return/ppermute | solution.py:183
  44.2 0.0 collective-permute-done.14.refs_1_
  44.2 1.0 %collective-permute-start.19 = (bf16[272,128]{1,0:T(8,128)(2,1)S(1)}, bf16[272,128]{1,0:T(8,128)(2,1)S(1)}, u32[]{:S(2)}, u32[]{:S(2)}) collective-permute-start(bf16[272,128]{1,0:T(8,128)(2,1)S(1)} %get-tuple-element.27), channel_id=1, source_target_pairs={{0,2},{1,3},{2,4},{3,5},{4,6},{5,7},{6,0},{7,1},{8,10},{9,11},{10,... | collective-permute-start | bytes 208904 | tf_op jit(solution)/shard_map/return/ppermute | solution.py:183
  45.2 0.5 collective-permute-done.15.refs_2_
  45.6 0.9 %collective-permute-start.20 = (bf16[272,128]{1,0:T(8,128)(2,1)S(1)}, bf16[272,128]{1,0:T(8,128)(2,1)S(1)}, u32[]{:S(2)}, u32[]{:S(2)}) collective-permute-start(bf16[272,128]{1,0:T(8,128)(2,1)S(1)} %get-tuple-element.28), channel_id=1, source_target_pairs={{0,3},{1,2},{2,5},{3,4},{4,7},{5,6},{6,1},{7,0},{8,11},{9,10},{10,... | collective-permute-start | bytes 208904 | tf_op jit(solution)/shard_map/return/ppermute | solution.py:183
  46.6 0.0 collective-permute-done.16.refs_3_
  46.6 7.5 %collective-permute-done.17.refs_4_ = bf16[272,128]{1,0:T(8,128)(2,1)S(1)} collective-permute-done((bf16[272,128]{1,0:T(8,128)(2,1)S(1)}, bf16[272,128]{1,0:T(8,128)(2,1)S(1)}, u32[]{:S(2)}, u32[]{:S(2)}) %collective-permute-start.17) | collective-permute-done | bytes 69664 | tf_op jit(solution)/shard_map/return/ppermute | solution.py:183
  54.1 1.5 %collective-permute-done.18.refs_5_ = bf16[272,128]{1,0:T(8,128)(2,1)S(1)} collective-permute-done((bf16[272,128]{1,0:T(8,128)(2,1)S(1)}, bf16[272,128]{1,0:T(8,128)(2,1)S(1)}, u32[]{:S(2)}, u32[]{:S(2)}) %collective-permute-start.18) | collective-permute-done | bytes 69664 | tf_op jit(solution)/shard_map/return/ppermute | solution.py:183
  55.6 0.0 collective-permute-done.19.refs_6_
  55.6 0.0 collective-permute-done.20.refs_7_
  55.6 0.9 %combine.1 = bf16[128,512]{1,0:T(8,128)(2,1)} custom-call(bf16[272,128]{1,0:T(8,128)(2,1)S(1)} %get-tuple-element.21.refs_0_, bf16[272,128]{1,0:T(8,128)(2,1)S(1)} %collective-permute-done.14.refs_1_, bf16[272,128]{1,0:T(8,128)(2,1)S(1)} %collective-permute-done.15.refs_2_, bf16[272,128]{1,0:T(8,128)(2,1)S(1)} %collective-permute-done.16.refs_3_, ...), custom_call_target="tpu_custom_call" | custom-call | tf_op jit(solution)/shard_map/combine/combine/pallas_call | solution.py:185
  (3 shorter events, 0.0 us)
Async XLA Ops:
  0.7 0.9 %copy-start = (bf16[128,512]{1,0:T(8,128)(2,1)S(1)}, bf16[128,512]{1,0:T(8,128)(2,1)}, u32[]{:S(2)}) copy-start(bf16[128,512]{1,0:T(8,128)(2,1)} %q_ref.1) | copy-start | bytes 393220
  1.6 0.9 %copy-start.1 = (bf16[128,512]{1,0:T(8,128)(2,1)S(1)}, bf16[128,512]{1,0:T(8,128)(2,1)}, u32[]{:S(2)}) copy-start(bf16[128,512]{1,0:T(8,128)(2,1)} %k_ref.1) | copy-start | bytes 393220
  2.5 0.9 %copy-start.2 = (bf16[128,512]{1,0:T(8,128)(2,1)S(1)}, bf16[128,512]{1,0:T(8,128)(2,1)}, u32[]{:S(2)}) copy-start(bf16[128,512]{1,0:T(8,128)(2,1)} %v_ref.1) | copy-start | bytes 393220
  3.8 10.3 %collective-permute-start.5 = (bf16[272,128]{1,0:T(8,128)(2,1)S(1)}, bf16[272,128]{1,0:T(8,128)(2,1)S(1)}, u32[]{:S(2)}, u32[]{:S(2)}) collective-permute-start(bf16[272,128]{1,0:T(8,128)(2,1)S(1)} %get-tuple-element.17.refs_0_), channel_id=1, source_target_pairs={{0,6},{1,7},{2,0},{3,1},{4,2},{5,3},{6,4},{7,5},{8,14},{9,15},{10,... | collective-permute-start | bytes 208904 | tf_op jit(solution)/shard_map/exchange/ppermute | solution.py:163
  8.9 7.0 %collective-permute-start.3 = (bf16[272,128]{1,0:T(8,128)(2,1)S(1)}, bf16[272,128]{1,0:T(8,128)(2,1)S(1)}, u32[]{:S(2)}, u32[]{:S(2)}) collective-permute-start(bf16[272,128]{1,0:T(8,128)(2,1)S(1)} %get-tuple-element.17.refs_0_), channel_id=1, source_target_pairs={{0,4},{1,5},{2,6},{3,7},{4,0},{5,1},{6,2},{7,3},{8,12},{9,13},{10,... | collective-permute-start | bytes 208904 | tf_op jit(solution)/shard_map/exchange/ppermute | solution.py:163
  8.9 7.1 %collective-permute-start.1 = (bf16[272,128]{1,0:T(8,128)(2,1)S(1)}, bf16[272,128]{1,0:T(8,128)(2,1)S(1)}, u32[]{:S(2)}, u32[]{:S(2)}) collective-permute-start(bf16[272,128]{1,0:T(8,128)(2,1)S(1)} %get-tuple-element.17.refs_0_), channel_id=1, source_target_pairs={{0,2},{1,3},{2,4},{3,5},{4,6},{5,7},{6,0},{7,1},{8,10},{9,11},{10,... | collective-permute-start | bytes 208904 | tf_op jit(solution)/shard_map/exchange/ppermute | solution.py:163
  9.9 7.9 %collective-permute-start.6 = (bf16[272,128]{1,0:T(8,128)(2,1)S(1)}, bf16[272,128]{1,0:T(8,128)(2,1)S(1)}, u32[]{:S(2)}, u32[]{:S(2)}) collective-permute-start(bf16[272,128]{1,0:T(8,128)(2,1)S(1)} %get-tuple-element.18), channel_id=1, source_target_pairs={{0,7},{1,6},{2,1},{3,0},{4,3},{5,2},{6,5},{7,4},{8,15},{9,14},{10,... | collective-permute-start | bytes 208904 | tf_op jit(solution)/shard_map/exchange/ppermute | solution.py:163
  11.6 15.7 %collective-permute-start.12 = (bf16[528,128]{1,0:T(8,128)(2,1)S(1)}, bf16[528,128]{1,0:T(8,128)(2,1)S(1)}, u32[]{:S(2)}, u32[]{:S(2)}) collective-permute-start(bf16[528,128]{1,0:T(8,128)(2,1)S(1)} %get-tuple-element.19.refs_8_), channel_id=1, source_target_pairs={{0,24},{1,25},{2,26},{3,27},{4,28},{5,29},{6,30},{7,31},{8,0},{9,1... | collective-permute-start | bytes 405512 | tf_op jit(solution)/shard_map/exchange/ppermute | solution.py:159
  14.0 13.3 %collective-permute-start.10 = (bf16[528,128]{1,0:T(8,128)(2,1)S(1)}, bf16[528,128]{1,0:T(8,128)(2,1)S(1)}, u32[]{:S(2)}, u32[]{:S(2)}) collective-permute-start(bf16[528,128]{1,0:T(8,128)(2,1)S(1)} %get-tuple-element.19.refs_8_), channel_id=1, source_target_pairs={{0,16},{1,17},{2,18},{3,19},{4,20},{5,21},{6,22},{7,23},{8,24},{9,... | collective-permute-start | bytes 405512 | tf_op jit(solution)/shard_map/exchange/ppermute | solution.py:159
  15.9 7.3 %collective-permute-start.4 = (bf16[272,128]{1,0:T(8,128)(2,1)S(1)}, bf16[272,128]{1,0:T(8,128)(2,1)S(1)}, u32[]{:S(2)}, u32[]{:S(2)}) collective-permute-start(bf16[272,128]{1,0:T(8,128)(2,1)S(1)} %get-tuple-element.18), channel_id=1, source_target_pairs={{0,5},{1,4},{2,7},{3,6},{4,1},{5,0},{6,3},{7,2},{8,13},{9,12},{10,... | collective-permute-start | bytes 208904 | tf_op jit(solution)/shard_map/exchange/ppermute | solution.py:163
  16.0 8.3 %collective-permute-start.2 = (bf16[272,128]{1,0:T(8,128)(2,1)S(1)}, bf16[272,128]{1,0:T(8,128)(2,1)S(1)}, u32[]{:S(2)}, u32[]{:S(2)}) collective-permute-start(bf16[272,128]{1,0:T(8,128)(2,1)S(1)} %get-tuple-element.18), channel_id=1, source_target_pairs={{0,3},{1,2},{2,5},{3,4},{4,7},{5,6},{6,1},{7,0},{8,11},{9,10},{10,... | collective-permute-start | bytes 208904 | tf_op jit(solution)/shard_map/exchange/ppermute | solution.py:163
  17.8 7.7 %collective-permute-start = (bf16[272,128]{1,0:T(8,128)(2,1)S(1)}, bf16[272,128]{1,0:T(8,128)(2,1)S(1)}, u32[]{:S(2)}, u32[]{:S(2)}) collective-permute-start(bf16[272,128]{1,0:T(8,128)(2,1)S(1)} %get-tuple-element.18), channel_id=1, source_target_pairs={{0,1},{1,0},{2,3},{3,2},{4,5},{5,4},{6,7},{7,6},{8,9},{9,8},{10,11... | collective-permute-start | bytes 208904 | tf_op jit(solution)/shard_map/exchange/ppermute | solution.py:163
  23.1 7.3 %collective-permute-start.8 = (bf16[528,128]{1,0:T(8,128)(2,1)S(1)}, bf16[528,128]{1,0:T(8,128)(2,1)S(1)}, u32[]{:S(2)}, u32[]{:S(2)}) collective-permute-start(bf16[528,128]{1,0:T(8,128)(2,1)S(1)} %get-tuple-element.19.refs_8_), channel_id=1, source_target_pairs={{0,8},{1,9},{2,10},{3,11},{4,12},{5,13},{6,14},{7,15},{8,16},{9,17... | collective-permute-start | bytes 405512 | tf_op jit(solution)/shard_map/exchange/ppermute | solution.py:159
  24.3 7.4 %collective-permute-start.13 = (bf16[528,128]{1,0:T(8,128)(2,1)S(1)}, bf16[528,128]{1,0:T(8,128)(2,1)S(1)}, u32[]{:S(2)}, u32[]{:S(2)}) collective-permute-start(bf16[528,128]{1,0:T(8,128)(2,1)S(1)} %get-tuple-element.20), channel_id=1, source_target_pairs={{0,25},{1,24},{2,27},{3,26},{4,29},{5,28},{6,31},{7,30},{8,1},{9,0... | collective-permute-start | bytes 405512 | tf_op jit(solution)/shard_map/exchange/ppermute | solution.py:159
  25.5 7.3 %collective-permute-start.11 = (bf16[528,128]{1,0:T(8,128)(2,1)S(1)}, bf16[528,128]{1,0:T(8,128)(2,1)S(1)}, u32[]{:S(2)}, u32[]{:S(2)}) collective-permute-start(bf16[528,128]{1,0:T(8,128)(2,1)S(1)} %get-tuple-element.20), channel_id=1, source_target_pairs={{0,17},{1,16},{2,19},{3,18},{4,21},{5,20},{6,23},{7,22},{8,25},{9,... | collective-permute-start | bytes 405512 | tf_op jit(solution)/shard_map/exchange/ppermute | solution.py:159
  27.3 7.3 %collective-permute-start.9 = (bf16[528,128]{1,0:T(8,128)(2,1)S(1)}, bf16[528,128]{1,0:T(8,128)(2,1)S(1)}, u32[]{:S(2)}, u32[]{:S(2)}) collective-permute-start(bf16[528,128]{1,0:T(8,128)(2,1)S(1)} %get-tuple-element.20), channel_id=1, source_target_pairs={{0,9},{1,8},{2,11},{3,10},{4,13},{5,12},{6,15},{7,14},{8,17},{9,16... | collective-permute-start | bytes 405512 | tf_op jit(solution)/shard_map/exchange/ppermute | solution.py:159
  27.3 7.2 %collective-permute-start.7 = (bf16[528,128]{1,0:T(8,128)(2,1)S(1)}, bf16[528,128]{1,0:T(8,128)(2,1)S(1)}, u32[]{:S(2)}, u32[]{:S(2)}) collective-permute-start(bf16[528,128]{1,0:T(8,128)(2,1)S(1)} %get-tuple-element.20), channel_id=1, source_target_pairs={{0,1},{1,0},{2,3},{3,2},{4,5},{5,4},{6,7},{7,6},{8,9},{9,8},{10,11... | collective-permute-start | bytes 405512 | tf_op jit(solution)/shard_map/exchange/ppermute | solution.py:159
  40.0 4.2 %collective-permute-start.14 = (bf16[272,128]{1,0:T(8,128)(2,1)S(1)}, bf16[272,128]{1,0:T(8,128)(2,1)S(1)}, u32[]{:S(2)}, u32[]{:S(2)}) collective-permute-start(bf16[272,128]{1,0:T(8,128)(2,1)S(1)} %get-tuple-element.22), channel_id=1, source_target_pairs={{0,1},{1,0},{2,3},{3,2},{4,5},{5,4},{6,7},{7,6},{8,9},{9,8},{10,11... | collective-permute-start | bytes 208904 | tf_op jit(solution)/shard_map/return/ppermute | solution.py:183
  40.7 4.9 %collective-permute-start.15 = (bf16[272,128]{1,0:T(8,128)(2,1)S(1)}, bf16[272,128]{1,0:T(8,128)(2,1)S(1)}, u32[]{:S(2)}, u32[]{:S(2)}) collective-permute-start(bf16[272,128]{1,0:T(8,128)(2,1)S(1)} %get-tuple-element.23), channel_id=1, source_target_pairs={{0,6},{1,7},{2,0},{3,1},{4,2},{5,3},{6,4},{7,5},{8,14},{9,15},{10,... | collective-permute-start | bytes 208904 | tf_op jit(solution)/shard_map/return/ppermute | solution.py:183
  40.7 5.8 %collective-permute-start.16 = (bf16[272,128]{1,0:T(8,128)(2,1)S(1)}, bf16[272,128]{1,0:T(8,128)(2,1)S(1)}, u32[]{:S(2)}, u32[]{:S(2)}) collective-permute-start(bf16[272,128]{1,0:T(8,128)(2,1)S(1)} %get-tuple-element.24), channel_id=1, source_target_pairs={{0,7},{1,6},{2,1},{3,0},{4,3},{5,2},{6,5},{7,4},{8,15},{9,14},{10,... | collective-permute-start | bytes 208904 | tf_op jit(solution)/shard_map/return/ppermute | solution.py:183
  41.2 12.9 %collective-permute-start.17 = (bf16[272,128]{1,0:T(8,128)(2,1)S(1)}, bf16[272,128]{1,0:T(8,128)(2,1)S(1)}, u32[]{:S(2)}, u32[]{:S(2)}) collective-permute-start(bf16[272,128]{1,0:T(8,128)(2,1)S(1)} %get-tuple-element.25), channel_id=1, source_target_pairs={{0,4},{1,5},{2,6},{3,7},{4,0},{5,1},{6,2},{7,3},{8,12},{9,13},{10,... | collective-permute-start | bytes 208904 | tf_op jit(solution)/shard_map/return/ppermute | solution.py:183
  43.6 12.0 %collective-permute-start.18 = (bf16[272,128]{1,0:T(8,128)(2,1)S(1)}, bf16[272,128]{1,0:T(8,128)(2,1)S(1)}, u32[]{:S(2)}, u32[]{:S(2)}) collective-permute-start(bf16[272,128]{1,0:T(8,128)(2,1)S(1)} %get-tuple-element.26), channel_id=1, source_target_pairs={{0,5},{1,4},{2,7},{3,6},{4,1},{5,0},{6,3},{7,2},{8,13},{9,12},{10,... | collective-permute-start | bytes 208904 | tf_op jit(solution)/shard_map/return/ppermute | solution.py:183
  44.2 11.4 %collective-permute-start.19 = (bf16[272,128]{1,0:T(8,128)(2,1)S(1)}, bf16[272,128]{1,0:T(8,128)(2,1)S(1)}, u32[]{:S(2)}, u32[]{:S(2)}) collective-permute-start(bf16[272,128]{1,0:T(8,128)(2,1)S(1)} %get-tuple-element.27), channel_id=1, source_target_pairs={{0,2},{1,3},{2,4},{3,5},{4,6},{5,7},{6,0},{7,1},{8,10},{9,11},{10,... | collective-permute-start | bytes 208904 | tf_op jit(solution)/shard_map/return/ppermute | solution.py:183
  45.6 10.0 %collective-permute-start.20 = (bf16[272,128]{1,0:T(8,128)(2,1)S(1)}, bf16[272,128]{1,0:T(8,128)(2,1)S(1)}, u32[]{:S(2)}, u32[]{:S(2)}) collective-permute-start(bf16[272,128]{1,0:T(8,128)(2,1)S(1)} %get-tuple-element.28), channel_id=1, source_target_pairs={{0,3},{1,2},{2,5},{3,4},{4,7},{5,6},{6,1},{7,0},{8,11},{9,10},{10,... | collective-permute-start | bytes 208904 | tf_op jit(solution)/shard_map/return/ppermute | solution.py:183

commit v3 on v2

v3 whole, which is shorter than its diff:
```python
import functools
import math

import jax
import jax.numpy as jnp
from jax import lax
from jax.experimental import pallas as pl
from jax.experimental.pallas import tpu as pltpu
from jax.sharding import PartitionSpec as P

HEADS = 4
CORES = 2
PER = HEADS // CORES
PAD = 16
LOW = -1e30
FLOOR = -1e29
BF16 = jnp.bfloat16
F32 = jnp.float32


def nt_dot(a, b):
    return lax.dot_general(a, b, (((1,), (1,)), ((), ())), preferred_element_type=F32)


def merge_kernel(p0, p1, q0, q1, k0, k1, v0, v1, q_out, kv_out):
    tok = q0.shape[0]
    size = q0.shape[1] // HEADS
    core = lax.rem(lax.axis_index("inner"), CORES)
    both = CORES * tok
    for b, (p, q, k, v) in enumerate(((p0, q0, k0, v0), (p1, q1, k1, v1))):
        for j in range(PER):
            cols = pl.ds(pl.multiple_of((core * PER + j) * size, size), size)
            q_out[j * both + b * tok : j * both + (b + 1) * tok, :] = q[:, cols]
            kv_out[j * both + b * tok : j * both + (b + 1) * tok, :] = k[:, cols]
            at = (PER + j) * both + b * tok
            kv_out[at : at + tok, :] = v[:, cols].astype(F32).T.astype(BF16)
    half = PAD // CORES
    pos = jnp.concatenate([jnp.full((half, size), p[0].astype(F32), F32) for p in (p0, p1)], axis=0).astype(BF16)
    q_out[PER * both :, :] = pos
    kv_out[2 * PER * both :, :] = pos


def attend_kernel(nk, q_ref, *refs):
    kv_refs, out_refs = refs[:nk], refs[nk:]
    size = q_ref.shape[1]
    tok = size
    both = CORES * tok
    half = PAD // CORES
    rate = size ** -0.5 * math.log2(math.e)
    rows = lax.broadcasted_iota(jnp.int32, (tok, both), 0).astype(F32)
    lanes = lax.broadcasted_iota(jnp.int32, (1, tok), 1).astype(F32)

    def start_of(ref, at):
        first = ref[at : at + PAD, :].astype(F32)
        return [first[b * half : b * half + 1, :] * tok for b in range(CORES)]

    qpos = jnp.concatenate([s + lanes for s in start_of(q_ref, PER * both)], axis=1)
    limits = []
    for ref in kv_refs:
        for s in start_of(ref, 2 * PER * both):
            limits.append(qpos - jnp.concatenate([s] * CORES, axis=1))
    stats = [[] for _ in range(CORES)]
    for h in range(PER):
        q = q_ref[h * both : (h + 1) * both, :]
        parts = []
        for j, ref in enumerate(kv_refs):
            s = nt_dot(ref[h * both : (h + 1) * both, :], q)
            for b in range(CORES):
                parts.append(jnp.where(rows <= limits[j * CORES + b], s[b * tok : (b + 1) * tok, :], LOW))
        s = jnp.concatenate(parts, axis=0)
        top = jnp.maximum(jnp.max(s, axis=0, keepdims=True), FLOOR).astype(BF16)
        p = jnp.exp2((s - top.astype(F32)) * rate).astype(BF16)
        at = (PER + h) * both
        vt = jnp.concatenate(
            [ref[at + b * tok : at + (b + 1) * tok, :] for ref in kv_refs for b in range(CORES)], axis=1
        )
        vt = jnp.concatenate([vt, jnp.ones((PAD, vt.shape[1]), BF16)], axis=0)
        o = jnp.dot(vt, p, preferred_element_type=F32)
        total = o[size : size + 1, :]
        hi = total.astype(BF16)
        lo = (total - hi.astype(F32)).astype(BF16)
        for b in range(CORES):
            cols = slice(b * tok, (b + 1) * tok)
            out_refs[b][h * size : (h + 1) * size, :] = o[0:size, cols].astype(BF16)
            stats[b] += [top[:, cols].astype(F32), hi[:, cols].astype(F32), lo[:, cols].astype(F32)]
    for b in range(CORES):
        rest = jnp.zeros((PAD - 3 * PER, tok), F32)
        out_refs[b][PER * size :, :] = jnp.concatenate(stats[b] + [rest], axis=0).astype(BF16)


def combine_kernel(n, *refs):
    parts, out_ref = refs[:n], refs[n]
    size = parts[0].shape[1]
    rate = size ** -0.5 * math.log2(math.e)
    core = lax.rem(lax.axis_index("inner"), CORES)
    for x in range(CORES):
        mine = parts[x::CORES]
        pair = jnp.bitwise_xor(core, x)
        stats = [part[PER * size :, :].astype(F32) for part in mine]
        for h in range(PER):
            tops = [s[3 * h : 3 * h + 1, :] for s in stats]
            best = functools.reduce(jnp.maximum, tops)
            factors = [jnp.exp2((t - best) * rate) for t in tops]
            denom = sum(f * (s[3 * h + 1 : 3 * h + 2, :] + s[3 * h + 2 : 3 * h + 3, :]) for f, s in zip(factors, stats))
            numer = sum(f * part[h * size : (h + 1) * size, :].astype(F32) for f, part in zip(factors, mine))
            cols = pl.ds(pl.multiple_of((pair * PER + h) * size, size), size)
            out_ref[:, cols] = (numer / denom).T.astype(BF16)


def vmem(n=1):
    return [pl.BlockSpec(memory_space=pltpu.VMEM)] * n


def shards(n_out, n_in, queries, keys, values, block_pos):
    tok, width = queries.shape
    size = width // HEADS
    chips = n_in // CORES
    both = CORES * tok
    params = pltpu.CompilerParams(vmem_limit_bytes=40 * 1024 * 1024)

    def along_inner(r, x):
        return [(w * CORES + c, (w ^ r) * CORES + (c ^ x)) for w in range(chips) for c in range(CORES)]

    with jax.named_scope("swap"):
        other = [lax.ppermute(a, "inner", along_inner(0, 1)) for a in (queries, keys, values, block_pos)]
    with jax.named_scope("merge"):
        smem = [pl.BlockSpec(memory_space=pltpu.SMEM)]
        q_piece, kv_piece = pl.pallas_call(
            merge_kernel,
            out_shape=(
                jax.ShapeDtypeStruct((PER * both + PAD, size), BF16),
                jax.ShapeDtypeStruct((2 * PER * both + PAD, size), BF16),
            ),
            in_specs=smem * 2 + vmem(6),
            out_specs=tuple(vmem(2)),
            compiler_params=params,
            name="merge",
        )(block_pos, other[3], queries, other[0], keys, other[1], values, other[2])
    with jax.named_scope("exchange"):
        kv = [kv_piece]
        for r in range(1, n_out):
            kv.append(lax.ppermute(kv_piece, "outer", [(o, o ^ r) for o in range(n_out)]))
        qs = [q_piece]
        for r in range(1, chips):
            qs.append(lax.ppermute(q_piece, "inner", along_inner(r, 0)))
    back = [None] * n_in
    work = 4 * PER * both * n_out * both * size
    for r in reversed(range(chips)):
        with jax.named_scope("attend"):
            parts = pl.pallas_call(
                functools.partial(attend_kernel, n_out),
                out_shape=(jax.ShapeDtypeStruct((PER * size + PAD, tok), BF16),) * CORES,
                in_specs=vmem(1 + n_out),
                out_specs=tuple(vmem(CORES)),
                compiler_params=params,
                cost_estimate=pl.CostEstimate(flops=work, bytes_accessed=2**20, transcendentals=work // (4 * size)),
                name="attend",
            )(qs[r], *kv)
        with jax.named_scope("return"):
            for x in range(CORES):
                part = parts[x]
                back[r * CORES + x] = part if r + x == 0 else lax.ppermute(part, "inner", along_inner(r, x))
    with jax.named_scope("combine"):
        return pl.pallas_call(
            functools.partial(combine_kernel, n_in),
            out_shape=jax.ShapeDtypeStruct((tok, width), BF16),
            in_specs=vmem(n_in),
            out_specs=vmem()[0],
            compiler_params=params,
            name="combine",
        )(*back)


def solution(mesh):
    n_out, n_in = mesh.shape["outer"], mesh.shape["inner"]
    return jax.shard_map(
        functools.partial(shards, n_out, n_in),
        mesh=mesh,
        in_specs=(
            P(("outer", "inner"), None),
            P(("outer", "inner"), None),
            P(("outer", "inner"), None),
            P(("outer", "inner")),
        ),
        out_specs=P(("outer", "inner"), None),
        check_vma=False,
    )
```

time: 56.6 us -> 42.7 us (0.75)
  waiting for transfers between devices: 23 us -> 9.86 us
    ppermute x21 -> x17, waiting for transfers between devices: 23 us -> 9.86 us  [the longest x7 4.64 us: shards(): lax.ppermute(part, 'inner', along_inner(r, x))]
    ppermute x21 -> x17, starting transfers between devices: 23.3 us -> 22.9 us  [the longest x3 9.27 us: shards(): qs.append(lax.ppermute(q_piece, 'inner', along_inner(r, 0)))]
    pallas_call x3 -> x6, Pallas kernels: 6.69 us -> 6.34 us  [the longest x4 4.71 us: shards(): pl.pallas_call(functools.partial(attend_kernel, n_out), out_shape=(jax.Sh...]
  transfers between devices with their start and end apart: 21 -> 17, of which waited for: 9 -> 6; matrix products, arithmetic and copies ran while one was open for 0% -> 0% of each run, Pallas kernels for 0% -> 11%
where the time goes in v3:
time: 42.7 us; the launch traced here: 42.5 us
  starting transfers between devices  22.9 us (54%)
  waiting for transfers between devices  9.86 us (23%)
  Pallas kernels  6.34 us (15%)
  local copies, waits for them, and re-layouts  2.7 us (6%)
  between operations  0.74 us (2%)
    ppermute x3, starting transfers between devices, shards(): qs.append(lax.ppermute(q_piece, 'inner', along_inner(r, 0)))  9.27 us
    ppermute x7, starting transfers between devices, shards(): lax.ppermute(part, 'inner', along_inner(r, x))  8.31 us
    pallas_call x4, Pallas kernels, shards(): pl.pallas_call(functools.partial(attend_kernel, n_out), out_shape=(jax.Sh...  4.71 us
    ppermute x7, waiting for transfers between devices, shards(): lax.ppermute(part, 'inner', along_inner(r, x))  4.64 us
    ppermute x3, waiting for transfers between devices, shards(): qs.append(lax.ppermute(q_piece, 'inner', along_inner(r, 0)))  4.52 us
    ppermute x3, starting transfers between devices, shards(): lax.ppermute(kv_piece, 'outer', [(o, o ^ r) for o in range(n_out)])  4.3 us
    unnamed x6, local copies, waits for them, and re-layouts  2.7 us
    ppermute x4, starting transfers between devices, shards(): lax.ppermute(a, 'inner', along_inner(0, 1))  1.02 us
  transfers between devices with their start and end apart: 17, of which 6 were waited for; matrix products, arithmetic and copies ran while one was open for 0% of the time, Pallas kernels for 11%

profile of v3, /device:TPU:0, one launch (start us, length us, event | category | flops | bytes accessed | tf_op | source)
XLA Modules:
  0.0 42.5 jit_solution(4772972218205940441)
XLA Ops:
  0.0 0.5 %collective-permute-start.1 = (bf16[128,512]{1,0:T(8,128)(2,1)}, bf16[128,512]{1,0:T(8,128)(2,1)S(1)}, u32[]{:S(2)}, u32[]{:S(2)}) collective-permute-start(bf16[128,512]{1,0:T(8,128)(2,1)} %q0.1), channel_id=1, source_target_pairs={{0,1},{1,0},{2,3},{3,2},{4,5},{5,4},{6,7},{7,6},{8,9},{9,8},{10,11... | collective-permute-start | bytes 393224 | tf_op jit(solution)/shard_map/swap/ppermute | solution.py:125
  0.5 0.1 collective-permute-start.2
  0.5 0.5 %collective-permute-start.3 = (bf16[128,512]{1,0:T(8,128)(2,1)}, bf16[128,512]{1,0:T(8,128)(2,1)S(1)}, u32[]{:S(2)}, u32[]{:S(2)}) collective-permute-start(bf16[128,512]{1,0:T(8,128)(2,1)} %v0.1), channel_id=1, source_target_pairs={{0,1},{1,0},{2,3},{3,2},{4,5},{5,4},{6,7},{7,6},{8,9},{9,8},{10,11... | collective-permute-start | bytes 393224 | tf_op jit(solution)/shard_map/swap/ppermute | solution.py:125
  1.0 0.1 collective-permute-start
  1.7 0.7 %collective-permute-done.p1 = s32[1]{0:T(128)} collective-permute-done((s32[1]{0:T(128)}, s32[1]{0:T(128)}, u32[]{:S(2)}, u32[]{:S(2)}) %collective-permute-start) | collective-permute-done | bytes 36 | tf_op jit(solution)/shard_map/swap/ppermute | solution.py:125
  2.4 0.0 collective-permute-done.1.q1
  2.4 0.0 collective-permute-done.2.k1
  2.4 0.0 collective-permute-done.3.v1
  2.4 0.0 copy-start
  2.4 0.9 %copy-done = bf16[128,512]{1,0:T(8,128)(2,1)S(1)} copy-done((bf16[128,512]{1,0:T(8,128)(2,1)S(1)}, bf16[128,512]{1,0:T(8,128)(2,1)}, u32[]{:S(2)}) %copy-start) | copy-done | bytes 131096
  3.3 0.0 copy-start.1
  3.3 0.9 %copy-done.1 = bf16[128,512]{1,0:T(8,128)(2,1)S(1)} copy-done((bf16[128,512]{1,0:T(8,128)(2,1)S(1)}, bf16[128,512]{1,0:T(8,128)(2,1)}, u32[]{:S(2)}) %copy-start.1) | copy-done | bytes 131096
  4.2 0.0 copy-start.2
  4.2 0.9 %copy-done.2 = bf16[128,512]{1,0:T(8,128)(2,1)S(1)} copy-done((bf16[128,512]{1,0:T(8,128)(2,1)S(1)}, bf16[128,512]{1,0:T(8,128)(2,1)}, u32[]{:S(2)}) %copy-start.2) | copy-done | bytes 131096
  5.1 0.8 %merge.1 = (bf16[528,128]{1,0:T(8,128)(2,1)S(1)}, bf16[1040,128]{1,0:T(8,128)(2,1)S(1)}) custom-call(s32[1]{0:T(128)S(6)} %copy.5.p0, s32[1]{0:T(128)} %collective-permute-done.p1, bf16[128,512]{1,0:T(8,128)(2,1)S(1)} %copy-done, bf16[128,512]{1,0:T(8,128)(2,1)S(1)} %collective-permute-done.1.q1, bf16[128,512]{1,0:T(8,128)(2,1)S(1)} %copy-done.1, ...), custom_call_target="tpu_custom_call" | custom-call | tf_op jit(solution)/shard_map/merge/merge/pallas_call | solution.py:128
  5.9 2.8 %collective-permute-start.4 = (bf16[1040,128]{1,0:T(8,128)(2,1)S(1)}, bf16[1040,128]{1,0:T(8,128)(2,1)S(1)}, u32[]{:S(2)}, u32[]{:S(2)}) collective-permute-start(bf16[1040,128]{1,0:T(8,128)(2,1)S(1)} %get-tuple-element.16.refs_0_), channel_id=1, source_target_pairs={{0,8},{8,0},{16,24},{24,16},{1,9},{9,1},{17,25},{25,17},{2,10},{10... | collective-permute-start | bytes 798728 | tf_op jit(solution)/shard_map/exchange/ppermute | solution.py:142
  8.6 1.5 %collective-permute-start.5 = (bf16[1040,128]{1,0:T(8,128)(2,1)S(1)}, bf16[1040,128]{1,0:T(8,128)(2,1)S(1)}, u32[]{:S(2)}, u32[]{:S(2)}) collective-permute-start(bf16[1040,128]{1,0:T(8,128)(2,1)S(1)} %get-tuple-element.16.refs_0_), channel_id=1, source_target_pairs={{0,16},{8,24},{16,0},{24,8},{1,17},{9,25},{17,1},{25,9},{2,18},{10... | collective-permute-start | bytes 798728 | tf_op jit(solution)/shard_map/exchange/ppermute | solution.py:142
  10.1 0.0 collective-permute-start.6
  10.2 4.1 %collective-permute-start.14 = (bf16[528,128]{1,0:T(8,128)(2,1)S(1)}, bf16[528,128]{1,0:T(8,128)(2,1)S(1)}, u32[]{:S(2)}, u32[]{:S(2)}) collective-permute-start(bf16[528,128]{1,0:T(8,128)(2,1)S(1)} %get-tuple-element.15.q_ref), channel_id=1, source_target_pairs={{0,6},{1,7},{2,4},{3,5},{4,2},{5,3},{6,0},{7,1},{8,14},{9,15},{10,... | collective-permute-start | bytes 405512 | tf_op jit(solution)/shard_map/exchange/ppermute | solution.py:145
  14.2 0.0 collective-permute-start.11
  14.2 4.5 %collective-permute-done.14.q_ref = bf16[528,128]{1,0:T(8,128)(2,1)S(1)} collective-permute-done((bf16[528,128]{1,0:T(8,128)(2,1)S(1)}, bf16[528,128]{1,0:T(8,128)(2,1)S(1)}, u32[]{:S(2)}, u32[]{:S(2)}) %collective-permute-start.14) | collective-permute-done | bytes 135200 | tf_op jit(solution)/shard_map/exchange/ppermute | solution.py:145
  18.7 5.2 %collective-permute-start.8 = (bf16[528,128]{1,0:T(8,128)(2,1)S(1)}, bf16[528,128]{1,0:T(8,128)(2,1)S(1)}, u32[]{:S(2)}, u32[]{:S(2)}) collective-permute-start(bf16[528,128]{1,0:T(8,128)(2,1)S(1)} %get-tuple-element.15.q_ref), channel_id=1, source_target_pairs={{0,2},{1,3},{2,0},{3,1},{4,6},{5,7},{6,4},{7,5},{8,10},{9,11},{10,... | collective-permute-start | bytes 405512 | tf_op jit(solution)/shard_map/exchange/ppermute | solution.py:145
  24.0 0.0 collective-permute-done.4.refs_1_
  24.0 0.0 collective-permute-done.5.refs_2_
  24.0 0.0 collective-permute-done.6.refs_3_
  24.0 1.2 %attend.7 = (bf16[272,128]{1,0:T(8,128)(2,1)S(1)}, bf16[272,128]{1,0:T(8,128)(2,1)S(1)}) custom-call(bf16[528,128]{1,0:T(8,128)(2,1)S(1)} %collective-permute-done.14.q_ref, bf16[1040,128]{1,0:T(8,128)(2,1)S(1)} %get-tuple-element.16.refs_0_, bf16[1040,128]{1,0:T(8,128)(2,1)S(1)} %collective-permute-done.4.refs_1_, ...), custom_call_target="tpu_custom_call" | custom-call | flops 268435456 | bytes 1048576 | tf_op jit(solution)/shard_map/attend/attend/pallas_call | solution.py:150
  25.2 3.0 %collective-permute-start.15 = (bf16[272,128]{1,0:T(8,128)(2,1)S(1)}, bf16[272,128]{1,0:T(8,128)(2,1)S(1)}, u32[]{:S(2)}, u32[]{:S(2)}) collective-permute-start(bf16[272,128]{1,0:T(8,128)(2,1)S(1)} %get-tuple-element.23), channel_id=1, source_target_pairs={{0,6},{1,7},{2,4},{3,5},{4,2},{5,3},{6,0},{7,1},{8,14},{9,15},{10,... | collective-permute-start | bytes 208904 | tf_op jit(solution)/shard_map/return/ppermute | solution.py:162
  28.1 0.0 collective-permute-start.16
  28.1 0.0 collective-permute-done.11.q_ref
  28.1 1.2 %attend.6 = (bf16[272,128]{1,0:T(8,128)(2,1)S(1)}, bf16[272,128]{1,0:T(8,128)(2,1)S(1)}) custom-call(bf16[528,128]{1,0:T(8,128)(2,1)S(1)} %collective-permute-done.11.q_ref, bf16[1040,128]{1,0:T(8,128)(2,1)S(1)} %get-tuple-element.16.refs_0_, bf16[1040,128]{1,0:T(8,128)(2,1)S(1)} %collective-permute-done.4.refs_1_, ...), custom_call_target="tpu_custom_call" | custom-call | flops 268435456 | bytes 1048576 | tf_op jit(solution)/shard_map/attend/attend/pallas_call | solution.py:150
  29.3 0.1 collective-permute-start.12
  29.4 3.3 %collective-permute-start.13 = (bf16[272,128]{1,0:T(8,128)(2,1)S(1)}, bf16[272,128]{1,0:T(8,128)(2,1)S(1)}, u32[]{:S(2)}, u32[]{:S(2)}) collective-permute-start(bf16[272,128]{1,0:T(8,128)(2,1)S(1)} %get-tuple-element.22), channel_id=1, source_target_pairs={{0,5},{1,4},{2,7},{3,6},{4,1},{5,0},{6,3},{7,2},{8,13},{9,12},{10,... | collective-permute-start | bytes 208904 | tf_op jit(solution)/shard_map/return/ppermute | solution.py:162
  32.7 0.0 collective-permute-done.8.q_ref
  32.7 1.2 %attend.5 = (bf16[272,128]{1,0:T(8,128)(2,1)S(1)}, bf16[272,128]{1,0:T(8,128)(2,1)S(1)}) custom-call(bf16[528,128]{1,0:T(8,128)(2,1)S(1)} %collective-permute-done.8.q_ref, bf16[1040,128]{1,0:T(8,128)(2,1)S(1)} %get-tuple-element.16.refs_0_, bf16[1040,128]{1,0:T(8,128)(2,1)S(1)} %collective-permute-done.4.refs_1_, ...), custom_call_target="tpu_custom_call" | custom-call | flops 268435456 | bytes 1048576 | tf_op jit(solution)/shard_map/attend/attend/pallas_call | solution.py:150
  33.9 0.6 %collective-permute-start.10 = (bf16[272,128]{1,0:T(8,128)(2,1)S(1)}, bf16[272,128]{1,0:T(8,128)(2,1)S(1)}, u32[]{:S(2)}, u32[]{:S(2)}) collective-permute-start(bf16[272,128]{1,0:T(8,128)(2,1)S(1)} %get-tuple-element.20), channel_id=1, source_target_pairs={{0,3},{1,2},{2,1},{3,0},{4,7},{5,6},{6,5},{7,4},{8,11},{9,10},{10,... | collective-permute-start | bytes 208904 | tf_op jit(solution)/shard_map/return/ppermute | solution.py:162
  34.5 1.2 %attend.4 = (bf16[272,128]{1,0:T(8,128)(2,1)S(1)}, bf16[272,128]{1,0:T(8,128)(2,1)S(1)}) custom-call(bf16[528,128]{1,0:T(8,128)(2,1)S(1)} %get-tuple-element.15.q_ref, bf16[1040,128]{1,0:T(8,128)(2,1)S(1)} %get-tuple-element.16.refs_0_, bf16[1040,128]{1,0:T(8,128)(2,1)S(1)} %collective-permute-done.4.refs_1_, ...), custom_call_target="tpu_custom_call" | custom-call | flops 268435456 | bytes 1048576 | tf_op jit(solution)/shard_map/attend/attend/pallas_call | solution.py:150
  35.7 0.0 collective-permute-done.15.refs_6_
  35.7 0.9 %collective-permute-start.9 = (bf16[272,128]{1,0:T(8,128)(2,1)S(1)}, bf16[272,128]{1,0:T(8,128)(2,1)S(1)}, u32[]{:S(2)}, u32[]{:S(2)}) collective-permute-start(bf16[272,128]{1,0:T(8,128)(2,1)S(1)} %get-tuple-element.19), channel_id=1, source_target_pairs={{0,2},{1,3},{2,0},{3,1},{4,6},{5,7},{6,4},{7,5},{8,10},{9,11},{10,... | collective-permute-start | bytes 208904 | tf_op jit(solution)/shard_map/return/ppermute | solution.py:162
  36.6 0.0 collective-permute-done.16.refs_7_
  36.6 0.5 %collective-permute-start.7 = (bf16[272,128]{1,0:T(8,128)(2,1)S(1)}, bf16[272,128]{1,0:T(8,128)(2,1)S(1)}, u32[]{:S(2)}, u32[]{:S(2)}) collective-permute-start(bf16[272,128]{1,0:T(8,128)(2,1)S(1)} %get-tuple-element.18), channel_id=1, source_target_pairs={{0,1},{1,0},{2,3},{3,2},{4,5},{5,4},{6,7},{7,6},{8,9},{9,8},{10,11... | collective-permute-start | bytes 208904 | tf_op jit(solution)/shard_map/return/ppermute | solution.py:162
  37.0 0.2 collective-permute-done.12.refs_4_
  37.2 2.3 %collective-permute-done.13.refs_5_ = bf16[272,128]{1,0:T(8,128)(2,1)S(1)} collective-permute-done((bf16[272,128]{1,0:T(8,128)(2,1)S(1)}, bf16[272,128]{1,0:T(8,128)(2,1)S(1)}, u32[]{:S(2)}, u32[]{:S(2)}) %collective-permute-start.13) | collective-permute-done | bytes 69664 | tf_op jit(solution)/shard_map/return/ppermute | solution.py:162
  39.5 0.7 %collective-permute-done.10.refs_3_ = bf16[272,128]{1,0:T(8,128)(2,1)S(1)} collective-permute-done((bf16[272,128]{1,0:T(8,128)(2,1)S(1)}, bf16[272,128]{1,0:T(8,128)(2,1)S(1)}, u32[]{:S(2)}, u32[]{:S(2)}) %collective-permute-start.10) | collective-permute-done | bytes 69664 | tf_op jit(solution)/shard_map/return/ppermute | solution.py:162
  40.2 1.5 %collective-permute-done.9.refs_2_ = bf16[272,128]{1,0:T(8,128)(2,1)S(1)} collective-permute-done((bf16[272,128]{1,0:T(8,128)(2,1)S(1)}, bf16[272,128]{1,0:T(8,128)(2,1)S(1)}, u32[]{:S(2)}, u32[]{:S(2)}) %collective-permute-start.9) | collective-permute-done | bytes 69664 | tf_op jit(solution)/shard_map/return/ppermute | solution.py:162
  41.7 0.0 collective-permute-done.7.refs_1_
  41.7 0.9 %combine.1 = bf16[128,512]{1,0:T(8,128)(2,1)} custom-call(bf16[272,128]{1,0:T(8,128)(2,1)S(1)} %get-tuple-element.17.refs_0_, bf16[272,128]{1,0:T(8,128)(2,1)S(1)} %collective-permute-done.7.refs_1_, bf16[272,128]{1,0:T(8,128)(2,1)S(1)} %collective-permute-done.9.refs_2_, bf16[272,128]{1,0:T(8,128)(2,1)S(1)} %collective-permute-done.10.refs_3_, ...), custom_call_target="tpu_custom_call" | custom-call | tf_op jit(solution)/shard_map/combine/combine/pallas_call | solution.py:164
Async XLA Ops:
  0.0 2.4 %collective-permute-start.1 = (bf16[128,512]{1,0:T(8,128)(2,1)}, bf16[128,512]{1,0:T(8,128)(2,1)S(1)}, u32[]{:S(2)}, u32[]{:S(2)}) collective-permute-start(bf16[128,512]{1,0:T(8,128)(2,1)} %q0.1), channel_id=1, source_target_pairs={{0,1},{1,0},{2,3},{3,2},{4,5},{5,4},{6,7},{7,6},{8,9},{9,8},{10,11... | collective-permute-start | bytes 393224 | tf_op jit(solution)/shard_map/swap/ppermute | solution.py:125
  0.5 1.9 %collective-permute-start.2 = (bf16[128,512]{1,0:T(8,128)(2,1)}, bf16[128,512]{1,0:T(8,128)(2,1)S(1)}, u32[]{:S(2)}, u32[]{:S(2)}) collective-permute-start(bf16[128,512]{1,0:T(8,128)(2,1)} %k0.1), channel_id=1, source_target_pairs={{0,1},{1,0},{2,3},{3,2},{4,5},{5,4},{6,7},{7,6},{8,9},{9,8},{10,11... | collective-permute-start | bytes 393224 | tf_op jit(solution)/shard_map/swap/ppermute | solution.py:125
  0.5 1.9 %collective-permute-start.3 = (bf16[128,512]{1,0:T(8,128)(2,1)}, bf16[128,512]{1,0:T(8,128)(2,1)S(1)}, u32[]{:S(2)}, u32[]{:S(2)}) collective-permute-start(bf16[128,512]{1,0:T(8,128)(2,1)} %v0.1), channel_id=1, source_target_pairs={{0,1},{1,0},{2,3},{3,2},{4,5},{5,4},{6,7},{7,6},{8,9},{9,8},{10,11... | collective-permute-start | bytes 393224 | tf_op jit(solution)/shard_map/swap/ppermute | solution.py:125
  1.0 1.4 %collective-permute-start = (s32[1]{0:T(128)}, s32[1]{0:T(128)}, u32[]{:S(2)}, u32[]{:S(2)}) collective-permute-start(s32[1]{0:T(128)} %param.7), channel_id=1, source_target_pairs={{0,1},{1,0},{2,3},{3,2},{4,5},{5,4},{6,7},{7,6},{8,9},{9,8},{10,11... | collective-permute-start | bytes 20 | tf_op jit(solution)/shard_map/swap/ppermute | solution.py:125
  2.4 0.9 %copy-start = (bf16[128,512]{1,0:T(8,128)(2,1)S(1)}, bf16[128,512]{1,0:T(8,128)(2,1)}, u32[]{:S(2)}) copy-start(bf16[128,512]{1,0:T(8,128)(2,1)} %q0.1) | copy-start | bytes 393220
  3.3 0.9 %copy-start.1 = (bf16[128,512]{1,0:T(8,128)(2,1)S(1)}, bf16[128,512]{1,0:T(8,128)(2,1)}, u32[]{:S(2)}) copy-start(bf16[128,512]{1,0:T(8,128)(2,1)} %k0.1) | copy-start | bytes 393220
  4.2 0.9 %copy-start.2 = (bf16[128,512]{1,0:T(8,128)(2,1)S(1)}, bf16[128,512]{1,0:T(8,128)(2,1)}, u32[]{:S(2)}) copy-start(bf16[128,512]{1,0:T(8,128)(2,1)} %v0.1) | copy-start | bytes 393220
  5.9 18.1 %collective-permute-start.4 = (bf16[1040,128]{1,0:T(8,128)(2,1)S(1)}, bf16[1040,128]{1,0:T(8,128)(2,1)S(1)}, u32[]{:S(2)}, u32[]{:S(2)}) collective-permute-start(bf16[1040,128]{1,0:T(8,128)(2,1)S(1)} %get-tuple-element.16.refs_0_), channel_id=1, source_target_pairs={{0,8},{8,0},{16,24},{24,16},{1,9},{9,1},{17,25},{25,17},{2,10},{10... | collective-permute-start | bytes 798728 | tf_op jit(solution)/shard_map/exchange/ppermute | solution.py:142
  8.6 15.3 %collective-permute-start.5 = (bf16[1040,128]{1,0:T(8,128)(2,1)S(1)}, bf16[1040,128]{1,0:T(8,128)(2,1)S(1)}, u32[]{:S(2)}, u32[]{:S(2)}) collective-permute-start(bf16[1040,128]{1,0:T(8,128)(2,1)S(1)} %get-tuple-element.16.refs_0_), channel_id=1, source_target_pairs={{0,16},{8,24},{16,0},{24,8},{1,17},{9,25},{17,1},{25,9},{2,18},{10... | collective-permute-start | bytes 798728 | tf_op jit(solution)/shard_map/exchange/ppermute | solution.py:142
  10.1 13.8 %collective-permute-start.6 = (bf16[1040,128]{1,0:T(8,128)(2,1)S(1)}, bf16[1040,128]{1,0:T(8,128)(2,1)S(1)}, u32[]{:S(2)}, u32[]{:S(2)}) collective-permute-start(bf16[1040,128]{1,0:T(8,128)(2,1)S(1)} %get-tuple-element.16.refs_0_), channel_id=1, source_target_pairs={{0,24},{8,16},{16,8},{24,0},{1,25},{9,17},{17,9},{25,1},{2,26},{10... | collective-permute-start | bytes 798728 | tf_op jit(solution)/shard_map/exchange/ppermute | solution.py:142
  10.2 8.6 %collective-permute-start.14 = (bf16[528,128]{1,0:T(8,128)(2,1)S(1)}, bf16[528,128]{1,0:T(8,128)(2,1)S(1)}, u32[]{:S(2)}, u32[]{:S(2)}) collective-permute-start(bf16[528,128]{1,0:T(8,128)(2,1)S(1)} %get-tuple-element.15.q_ref), channel_id=1, source_target_pairs={{0,6},{1,7},{2,4},{3,5},{4,2},{5,3},{6,0},{7,1},{8,14},{9,15},{10,... | collective-permute-start | bytes 405512 | tf_op jit(solution)/shard_map/exchange/ppermute | solution.py:145
  14.2 13.9 %collective-permute-start.11 = (bf16[528,128]{1,0:T(8,128)(2,1)S(1)}, bf16[528,128]{1,0:T(8,128)(2,1)S(1)}, u32[]{:S(2)}, u32[]{:S(2)}) collective-permute-start(bf16[528,128]{1,0:T(8,128)(2,1)S(1)} %get-tuple-element.15.q_ref), channel_id=1, source_target_pairs={{0,4},{1,5},{2,6},{3,7},{4,0},{5,1},{6,2},{7,3},{8,12},{9,13},{10,... | collective-permute-start | bytes 405512 | tf_op jit(solution)/shard_map/exchange/ppermute | solution.py:145
  18.7 13.9 %collective-permute-start.8 = (bf16[528,128]{1,0:T(8,128)(2,1)S(1)}, bf16[528,128]{1,0:T(8,128)(2,1)S(1)}, u32[]{:S(2)}, u32[]{:S(2)}) collective-permute-start(bf16[528,128]{1,0:T(8,128)(2,1)S(1)} %get-tuple-element.15.q_ref), channel_id=1, source_target_pairs={{0,2},{1,3},{2,0},{3,1},{4,6},{5,7},{6,4},{7,5},{8,10},{9,11},{10,... | collective-permute-start | bytes 405512 | tf_op jit(solution)/shard_map/exchange/ppermute | solution.py:145
  25.2 10.5 %collective-permute-start.15 = (bf16[272,128]{1,0:T(8,128)(2,1)S(1)}, bf16[272,128]{1,0:T(8,128)(2,1)S(1)}, u32[]{:S(2)}, u32[]{:S(2)}) collective-permute-start(bf16[272,128]{1,0:T(8,128)(2,1)S(1)} %get-tuple-element.23), channel_id=1, source_target_pairs={{0,6},{1,7},{2,4},{3,5},{4,2},{5,3},{6,0},{7,1},{8,14},{9,15},{10,... | collective-permute-start | bytes 208904 | tf_op jit(solution)/shard_map/return/ppermute | solution.py:162
  28.1 8.4 %collective-permute-start.16 = (bf16[272,128]{1,0:T(8,128)(2,1)S(1)}, bf16[272,128]{1,0:T(8,128)(2,1)S(1)}, u32[]{:S(2)}, u32[]{:S(2)}) collective-permute-start(bf16[272,128]{1,0:T(8,128)(2,1)S(1)} %get-tuple-element.24), channel_id=1, source_target_pairs={{0,7},{1,6},{2,5},{3,4},{4,3},{5,2},{6,1},{7,0},{8,15},{9,14},{10,... | collective-permute-start | bytes 208904 | tf_op jit(solution)/shard_map/return/ppermute | solution.py:162
  29.3 7.9 %collective-permute-start.12 = (bf16[272,128]{1,0:T(8,128)(2,1)S(1)}, bf16[272,128]{1,0:T(8,128)(2,1)S(1)}, u32[]{:S(2)}, u32[]{:S(2)}) collective-permute-start(bf16[272,128]{1,0:T(8,128)(2,1)S(1)} %get-tuple-element.21), channel_id=1, source_target_pairs={{0,4},{1,5},{2,6},{3,7},{4,0},{5,1},{6,2},{7,3},{8,12},{9,13},{10,... | collective-permute-start | bytes 208904 | tf_op jit(solution)/shard_map/return/ppermute | solution.py:162
  29.4 10.1 %collective-permute-start.13 = (bf16[272,128]{1,0:T(8,128)(2,1)S(1)}, bf16[272,128]{1,0:T(8,128)(2,1)S(1)}, u32[]{:S(2)}, u32[]{:S(2)}) collective-permute-start(bf16[272,128]{1,0:T(8,128)(2,1)S(1)} %get-tuple-element.22), channel_id=1, source_target_pairs={{0,5},{1,4},{2,7},{3,6},{4,1},{5,0},{6,3},{7,2},{8,13},{9,12},{10,... | collective-permute-start | bytes 208904 | tf_op jit(solution)/shard_map/return/ppermute | solution.py:162
  33.9 6.3 %collective-permute-start.10 = (bf16[272,128]{1,0:T(8,128)(2,1)S(1)}, bf16[272,128]{1,0:T(8,128)(2,1)S(1)}, u32[]{:S(2)}, u32[]{:S(2)}) collective-permute-start(bf16[272,128]{1,0:T(8,128)(2,1)S(1)} %get-tuple-element.20), channel_id=1, source_target_pairs={{0,3},{1,2},{2,1},{3,0},{4,7},{5,6},{6,5},{7,4},{8,11},{9,10},{10,... | collective-permute-start | bytes 208904 | tf_op jit(solution)/shard_map/return/ppermute | solution.py:162
  35.7 6.0 %collective-permute-start.9 = (bf16[272,128]{1,0:T(8,128)(2,1)S(1)}, bf16[272,128]{1,0:T(8,128)(2,1)S(1)}, u32[]{:S(2)}, u32[]{:S(2)}) collective-permute-start(bf16[272,128]{1,0:T(8,128)(2,1)S(1)} %get-tuple-element.19), channel_id=1, source_target_pairs={{0,2},{1,3},{2,0},{3,1},{4,6},{5,7},{6,4},{7,5},{8,10},{9,11},{10,... | collective-permute-start | bytes 208904 | tf_op jit(solution)/shard_map/return/ppermute | solution.py:162
  36.6 5.1 %collective-permute-start.7 = (bf16[272,128]{1,0:T(8,128)(2,1)S(1)}, bf16[272,128]{1,0:T(8,128)(2,1)S(1)}, u32[]{:S(2)}, u32[]{:S(2)}) collective-permute-start(bf16[272,128]{1,0:T(8,128)(2,1)S(1)} %get-tuple-element.18), channel_id=1, source_target_pairs={{0,1},{1,0},{2,3},{3,2},{4,5},{5,4},{6,7},{7,6},{8,9},{9,8},{10,11... | collective-permute-start | bytes 208904 | tf_op jit(solution)/shard_map/return/ppermute | solution.py:162

commit v4 on v3

--- a/solution.py
+++ b/solution.py
@@ -22,9 +22,10 @@
     return lax.dot_general(a, b, (((1,), (1,)), ((), ())), preferred_element_type=F32)
 
 
-def merge_kernel(p0, p1, q0, q1, k0, k1, v0, v1, q_out, kv_out):
-    tok = q0.shape[0]
-    size = q0.shape[1] // HEADS
+def merge_kernel(p0, p1, own, q1, k1, v1, q_out, kv_out):
+    tok = q1.shape[0]
+    size = q1.shape[1] // HEADS
+    q0, k0, v0 = (own.at[i * tok : (i + 1) * tok, :] for i in range(3))
     core = lax.rem(lax.axis_index("inner"), CORES)
     both = CORES * tok
     for b, (p, q, k, v) in enumerate(((p0, q0, k0, v0), (p1, q1, k1, v1))):
@@ -123,6 +124,7 @@
 
     with jax.named_scope("swap"):
         other = [lax.ppermute(a, "inner", along_inner(0, 1)) for a in (queries, keys, values, block_pos)]
+        own = jnp.concatenate([queries, keys, values], axis=0)
     with jax.named_scope("merge"):
         smem = [pl.BlockSpec(memory_space=pltpu.SMEM)]
         q_piece, kv_piece = pl.pallas_call(
@@ -131,18 +133,19 @@
                 jax.ShapeDtypeStruct((PER * both + PAD, size), BF16),
                 jax.ShapeDtypeStruct((2 * PER * both + PAD, size), BF16),
             ),
-            in_specs=smem * 2 + vmem(6),
+            in_specs=smem * 2 + vmem(4),
             out_specs=tuple(vmem(2)),
             compiler_params=params,
             name="merge",
-        )(block_pos, other[3], queries, other[0], keys, other[1], values, other[2])
+        )(block_pos, other[3], own, *other[:3])
     with jax.named_scope("exchange"):
         kv = [kv_piece]
         for r in range(1, n_out):
             kv.append(lax.ppermute(kv_piece, "outer", [(o, o ^ r) for o in range(n_out)]))
         qs = [q_piece]
         for r in range(1, chips):
-            qs.append(lax.ppermute(q_piece, "inner", along_inner(r, 0)))
+            piece = lax.optimization_barrier((q_piece, kv[1]))[0] if r == 1 else q_piece
+            qs.append(lax.ppermute(piece, "inner", along_inner(r, 0)))
     back = [None] * n_in
     work = 4 * PER * both * n_out * both * size
     for r in reversed(range(chips)):

time: 42.7 us -> 40.6 us (0.951)
  local copies, waits for them, and re-layouts: 2.7 us -> 0 us
  starting transfers between devices: 22.9 us -> 21.3 us
  waiting for transfers between devices: 9.86 us -> 11 us
  other arithmetic: 0 us -> 1.06 us
    ppermute x3, waiting for transfers between devices: 0.01 us -> 5.16 us  [shards(): lax.ppermute(kv_piece, 'outer', [(o, o ^ r) for o in range(n_out)])]
    ppermute x3, waiting for transfers between devices: 4.52 us -> 0.83 us  [shards(): qs.append(lax.ppermute(piece, 'inner', along_inner(r, 0)))]
    ppermute x3, starting transfers between devices: 9.27 us -> 6.2 us  [shards(): qs.append(lax.ppermute(piece, 'inner', along_inner(r, 0)))]
    unnamed x6 -> x0, local copies, waits for them, and re-layouts: 2.7 us -> none
    ppermute x7, starting transfers between devices: 8.31 us -> 9.56 us  [shards(): lax.ppermute(part, 'inner', along_inner(r, x))]
    concatenate x0 -> x1, other arithmetic: none -> 1.06 us  [shards(): own = jnp.concatenate([queries, keys, values], axis=0)]
    ppermute x4, waiting for transfers between devices: 0.69 us -> 0.01 us  [shards(): lax.ppermute(a, 'inner', along_inner(0, 1))]
  transfers between devices with their start and end apart: 17 -> 17, of which waited for: 6 -> 7; matrix products, arithmetic and copies ran while one was open for 0% -> 3% of each run, Pallas kernels for 11% -> 12%
where the time goes in v4:
time: 40.6 us; the launch traced here: 40.5 us
  starting transfers between devices  21.3 us (52%)
  waiting for transfers between devices  11 us (27%)
  Pallas kernels  6.35 us (16%)
  other arithmetic  1.06 us (3%)
  between operations  0.76 us (2%)
    ppermute x7, starting transfers between devices, shards(): lax.ppermute(part, 'inner', along_inner(r, x))  9.56 us
    ppermute x3, starting transfers between devices, shards(): qs.append(lax.ppermute(piece, 'inner', along_inner(r, 0)))  6.2 us
    ppermute x3, waiting for transfers between devices, shards(): lax.ppermute(kv_piece, 'outer', [(o, o ^ r) for o in range(n_out)])  5.16 us
    ppermute x7, waiting for transfers between devices, shards(): lax.ppermute(part, 'inner', along_inner(r, x))  4.98 us
    pallas_call x4, Pallas kernels, shards(): pl.pallas_call(functools.partial(attend_kernel, n_out), out_shape=(jax.Sh...  4.71 us
    ppermute x3, starting transfers between devices, shards(): lax.ppermute(kv_piece, 'outer', [(o, o ^ r) for o in range(n_out)])  4.54 us
    concatenate x1, other arithmetic, shards(): own = jnp.concatenate([queries, keys, values], axis=0)  1.06 us
    ppermute x4, starting transfers between devices, shards(): lax.ppermute(a, 'inner', along_inner(0, 1))  1.02 us
  transfers between devices with their start and end apart: 17, of which 7 were waited for; matrix products, arithmetic and copies ran while one was open for 3% of the time, Pallas kernels for 12%

profile of v4, /device:TPU:0, one launch (start us, length us, event | category | flops | bytes accessed | tf_op | source)
XLA Modules:
  0.0 40.5 jit_solution(12611422136626998512)
XLA Ops:
  0.0 0.5 %collective-permute-start.1 = (bf16[128,512]{1,0:T(8,128)(2,1)}, bf16[128,512]{1,0:T(8,128)(2,1)S(1)}, u32[]{:S(2)}, u32[]{:S(2)}) collective-permute-start(bf16[128,512]{1,0:T(8,128)(2,1)} %param.4), channel_id=1, source_target_pairs={{0,1},{1,0},{2,3},{3,2},{4,5},{5,4},{6,7},{7,6},{8,9},{9,8},{10,11... | collective-permute-start | bytes 393224 | tf_op jit(solution)/shard_map/swap/ppermute | solution.py:126
  0.5 0.1 collective-permute-start.2
  0.5 0.5 %collective-permute-start.3 = (bf16[128,512]{1,0:T(8,128)(2,1)}, bf16[128,512]{1,0:T(8,128)(2,1)S(1)}, u32[]{:S(2)}, u32[]{:S(2)}) collective-permute-start(bf16[128,512]{1,0:T(8,128)(2,1)} %param.6), channel_id=1, source_target_pairs={{0,1},{1,0},{2,3},{3,2},{4,5},{5,4},{6,7},{7,6},{8,9},{9,8},{10,11... | collective-permute-start | bytes 393224 | tf_op jit(solution)/shard_map/swap/ppermute | solution.py:126
  1.0 0.1 collective-permute-start
  1.7 1.1 %pad_maximum_fusion.own = bf16[384,512]{1,0:T(8,128)(2,1)S(1)} fusion(bf16[128,512]{1,0:T(8,128)(2,1)} %param.6, bf16[128,512]{1,0:T(8,128)(2,1)} %param.5, bf16[128,512]{1,0:T(8,128)(2,1)} %param.4), kind=kLoop, calls=%fused_computation | loop fusion | flops 1179648 | bytes 786432 | tf_op jit(solution)/shard_map/swap/concatenate | solution.py:127
  2.7 0.0 collective-permute-done.p1
  2.7 0.0 collective-permute-done.1.q1
  2.8 0.0 collective-permute-done.2.k1
  2.8 0.0 collective-permute-done.3.v1
  2.8 0.8 %merge.1 = (bf16[528,128]{1,0:T(8,128)(2,1)S(1)}, bf16[1040,128]{1,0:T(8,128)(2,1)S(1)}) custom-call(s32[1]{0:T(128)S(6)} %copy.5.p0, s32[1]{0:T(128)} %collective-permute-done.p1, bf16[384,512]{1,0:T(8,128)(2,1)S(1)} %pad_maximum_fusion.own, bf16[128,512]{1,0:T(8,128)(2,1)S(1)} %collective-permute-done.1.q1, ...), custom_call_target="tpu_custom_call" | custom-call | tf_op jit(solution)/shard_map/merge/merge/pallas_call | solution.py:130
  3.6 3.0 %collective-permute-start.4 = (bf16[1040,128]{1,0:T(8,128)(2,1)S(1)}, bf16[1040,128]{1,0:T(8,128)(2,1)S(1)}, u32[]{:S(2)}, u32[]{:S(2)}) collective-permute-start(bf16[1040,128]{1,0:T(8,128)(2,1)S(1)} %get-tuple-element.17.refs_0_), channel_id=1, source_target_pairs={{0,8},{8,0},{16,24},{24,16},{1,9},{9,1},{17,25},{25,17},{2,10},{10... | collective-permute-start | bytes 798728 | tf_op jit(solution)/shard_map/exchange/ppermute | solution.py:144
  6.6 1.5 %collective-permute-start.5 = (bf16[1040,128]{1,0:T(8,128)(2,1)S(1)}, bf16[1040,128]{1,0:T(8,128)(2,1)S(1)}, u32[]{:S(2)}, u32[]{:S(2)}) collective-permute-start(bf16[1040,128]{1,0:T(8,128)(2,1)S(1)} %get-tuple-element.17.refs_0_), channel_id=1, source_target_pairs={{0,16},{8,24},{16,0},{24,8},{1,17},{9,25},{17,1},{25,9},{2,18},{10... | collective-permute-start | bytes 798728 | tf_op jit(solution)/shard_map/exchange/ppermute | solution.py:144
  8.1 0.0 collective-permute-start.6
  8.1 4.1 %collective-permute-start.14 = (bf16[528,128]{1,0:T(8,128)(2,1)S(1)}, bf16[528,128]{1,0:T(8,128)(2,1)S(1)}, u32[]{:S(2)}, u32[]{:S(2)}) collective-permute-start(bf16[528,128]{1,0:T(8,128)(2,1)S(1)} %get-tuple-element.20.q_ref), channel_id=1, source_target_pairs={{0,6},{1,7},{2,4},{3,5},{4,2},{5,3},{6,0},{7,1},{8,14},{9,15},{10,... | collective-permute-start | bytes 405512 | tf_op jit(solution)/shard_map/exchange/ppermute | solution.py:148
  12.2 0.0 collective-permute-start.11
  12.2 1.6 %collective-permute-done.4.refs_1_ = bf16[1040,128]{1,0:T(8,128)(2,1)S(1)} collective-permute-done((bf16[1040,128]{1,0:T(8,128)(2,1)S(1)}, bf16[1040,128]{1,0:T(8,128)(2,1)S(1)}, u32[]{:S(2)}, u32[]{:S(2)}) %collective-permute-start.4) | collective-permute-done | bytes 266272 | tf_op jit(solution)/shard_map/exchange/ppermute | solution.py:144
  13.8 2.1 %collective-permute-start.8 = (bf16[528,128]{1,0:T(8,128)(2,1)S(1)}, bf16[528,128]{1,0:T(8,128)(2,1)S(1)}, u32[]{:S(2)}, u32[]{:S(2)}) collective-permute-start(bf16[528,128]{1,0:T(8,128)(2,1)S(1)} %get-tuple-element.20.q_ref), channel_id=1, source_target_pairs={{0,2},{1,3},{2,0},{3,1},{4,6},{5,7},{6,4},{7,5},{8,10},{9,11},{10,... | collective-permute-start | bytes 405512 | tf_op jit(solution)/shard_map/exchange/ppermute | solution.py:148
  15.9 0.8 %collective-permute-done.14.q_ref = bf16[528,128]{1,0:T(8,128)(2,1)S(1)} collective-permute-done((bf16[528,128]{1,0:T(8,128)(2,1)S(1)}, bf16[528,128]{1,0:T(8,128)(2,1)S(1)}, u32[]{:S(2)}, u32[]{:S(2)}) %collective-permute-start.14) | collective-permute-done | bytes 135200 | tf_op jit(solution)/shard_map/exchange/ppermute | solution.py:148
  16.7 3.6 %collective-permute-done.5.refs_2_ = bf16[1040,128]{1,0:T(8,128)(2,1)S(1)} collective-permute-done((bf16[1040,128]{1,0:T(8,128)(2,1)S(1)}, bf16[1040,128]{1,0:T(8,128)(2,1)S(1)}, u32[]{:S(2)}, u32[]{:S(2)}) %collective-permute-start.5) | collective-permute-done | bytes 266272 | tf_op jit(solution)/shard_map/exchange/ppermute | solution.py:144
  20.3 0.0 collective-permute-done.6.refs_3_
  20.3 1.2 %attend.7 = (bf16[272,128]{1,0:T(8,128)(2,1)S(1)}, bf16[272,128]{1,0:T(8,128)(2,1)S(1)}) custom-call(bf16[528,128]{1,0:T(8,128)(2,1)S(1)} %collective-permute-done.14.q_ref, bf16[1040,128]{1,0:T(8,128)(2,1)S(1)} %get-tuple-element.17.refs_0_, bf16[1040,128]{1,0:T(8,128)(2,1)S(1)} %collective-permute-done.4.refs_1_, ...), custom_call_target="tpu_custom_call" | custom-call | flops 268435456 | bytes 1048576 | tf_op jit(solution)/shard_map/attend/attend/pallas_call | solution.py:153
  21.5 3.7 %collective-permute-start.15 = (bf16[272,128]{1,0:T(8,128)(2,1)S(1)}, bf16[272,128]{1,0:T(8,128)(2,1)S(1)}, u32[]{:S(2)}, u32[]{:S(2)}) collective-permute-start(bf16[272,128]{1,0:T(8,128)(2,1)S(1)} %get-tuple-element.25), channel_id=1, source_target_pairs={{0,6},{1,7},{2,4},{3,5},{4,2},{5,3},{6,0},{7,1},{8,14},{9,15},{10,... | collective-permute-start | bytes 208904 | tf_op jit(solution)/shard_map/return/ppermute | solution.py:165
  25.2 0.0 collective-permute-start.16
  25.2 0.0 collective-permute-done.11.q_ref
  25.2 1.2 %attend.6 = (bf16[272,128]{1,0:T(8,128)(2,1)S(1)}, bf16[272,128]{1,0:T(8,128)(2,1)S(1)}) custom-call(bf16[528,128]{1,0:T(8,128)(2,1)S(1)} %collective-permute-done.11.q_ref, bf16[1040,128]{1,0:T(8,128)(2,1)S(1)} %get-tuple-element.17.refs_0_, bf16[1040,128]{1,0:T(8,128)(2,1)S(1)} %collective-permute-done.4.refs_1_, ...), custom_call_target="tpu_custom_call" | custom-call | flops 268435456 | bytes 1048576 | tf_op jit(solution)/shard_map/attend/attend/pallas_call | solution.py:153
  26.3 0.1 collective-permute-start.12
  26.4 2.6 %collective-permute-start.13 = (bf16[272,128]{1,0:T(8,128)(2,1)S(1)}, bf16[272,128]{1,0:T(8,128)(2,1)S(1)}, u32[]{:S(2)}, u32[]{:S(2)}) collective-permute-start(bf16[272,128]{1,0:T(8,128)(2,1)S(1)} %get-tuple-element.24), channel_id=1, source_target_pairs={{0,5},{1,4},{2,7},{3,6},{4,1},{5,0},{6,3},{7,2},{8,13},{9,12},{10,... | collective-permute-start | bytes 208904 | tf_op jit(solution)/shard_map/return/ppermute | solution.py:165
  29.0 1.2 %attend.4 = (bf16[272,128]{1,0:T(8,128)(2,1)S(1)}, bf16[272,128]{1,0:T(8,128)(2,1)S(1)}) custom-call(bf16[528,128]{1,0:T(8,128)(2,1)S(1)} %get-tuple-element.20.q_ref, bf16[1040,128]{1,0:T(8,128)(2,1)S(1)} %get-tuple-element.17.refs_0_, bf16[1040,128]{1,0:T(8,128)(2,1)S(1)} %collective-permute-done.4.refs_1_, ...), custom_call_target="tpu_custom_call" | custom-call | flops 268435456 | bytes 1048576 | tf_op jit(solution)/shard_map/attend/attend/pallas_call | solution.py:153
  30.2 0.0 collective-permute-done.8.q_ref
  30.2 0.5 %collective-permute-start.7 = (bf16[272,128]{1,0:T(8,128)(2,1)S(1)}, bf16[272,128]{1,0:T(8,128)(2,1)S(1)}, u32[]{:S(2)}, u32[]{:S(2)}) collective-permute-start(bf16[272,128]{1,0:T(8,128)(2,1)S(1)} %get-tuple-element.19), channel_id=1, source_target_pairs={{0,1},{1,0},{2,3},{3,2},{4,5},{5,4},{6,7},{7,6},{8,9},{9,8},{10,11... | collective-permute-start | bytes 208904 | tf_op jit(solution)/shard_map/return/ppermute | solution.py:165
  30.7 1.2 %attend.5 = (bf16[272,128]{1,0:T(8,128)(2,1)S(1)}, bf16[272,128]{1,0:T(8,128)(2,1)S(1)}) custom-call(bf16[528,128]{1,0:T(8,128)(2,1)S(1)} %collective-permute-done.8.q_ref, bf16[1040,128]{1,0:T(8,128)(2,1)S(1)} %get-tuple-element.17.refs_0_, bf16[1040,128]{1,0:T(8,128)(2,1)S(1)} %collective-permute-done.4.refs_1_, ...), custom_call_target="tpu_custom_call" | custom-call | flops 268435456 | bytes 1048576 | tf_op jit(solution)/shard_map/attend/attend/pallas_call | solution.py:153
  31.9 0.0 collective-permute-done.15.refs_6_
  31.9 1.3 %collective-permute-start.10 = (bf16[272,128]{1,0:T(8,128)(2,1)S(1)}, bf16[272,128]{1,0:T(8,128)(2,1)S(1)}, u32[]{:S(2)}, u32[]{:S(2)}) collective-permute-start(bf16[272,128]{1,0:T(8,128)(2,1)S(1)} %get-tuple-element.22), channel_id=1, source_target_pairs={{0,3},{1,2},{2,1},{3,0},{4,7},{5,6},{6,5},{7,4},{8,11},{9,10},{10,... | collective-permute-start | bytes 208904 | tf_op jit(solution)/shard_map/return/ppermute | solution.py:165
  33.2 0.0 collective-permute-done.16.refs_7_
  33.2 1.4 %collective-permute-start.9 = (bf16[272,128]{1,0:T(8,128)(2,1)S(1)}, bf16[272,128]{1,0:T(8,128)(2,1)S(1)}, u32[]{:S(2)}, u32[]{:S(2)}) collective-permute-start(bf16[272,128]{1,0:T(8,128)(2,1)S(1)} %get-tuple-element.21), channel_id=1, source_target_pairs={{0,2},{1,3},{2,0},{3,1},{4,6},{5,7},{6,4},{7,5},{8,10},{9,11},{10,... | collective-permute-start | bytes 208904 | tf_op jit(solution)/shard_map/return/ppermute | solution.py:165
  34.6 0.6 %collective-permute-done.12.refs_4_ = bf16[272,128]{1,0:T(8,128)(2,1)S(1)} collective-permute-done((bf16[272,128]{1,0:T(8,128)(2,1)S(1)}, bf16[272,128]{1,0:T(8,128)(2,1)S(1)}, u32[]{:S(2)}, u32[]{:S(2)}) %collective-permute-start.12) | collective-permute-done | bytes 69664 | tf_op jit(solution)/shard_map/return/ppermute | solution.py:165
  35.3 1.5 %collective-permute-done.13.refs_5_ = bf16[272,128]{1,0:T(8,128)(2,1)S(1)} collective-permute-done((bf16[272,128]{1,0:T(8,128)(2,1)S(1)}, bf16[272,128]{1,0:T(8,128)(2,1)S(1)}, u32[]{:S(2)}, u32[]{:S(2)}) %collective-permute-start.13) | collective-permute-done | bytes 69664 | tf_op jit(solution)/shard_map/return/ppermute | solution.py:165
  36.8 0.0 collective-permute-done.7.refs_1_
  36.8 1.2 %collective-permute-done.10.refs_3_ = bf16[272,128]{1,0:T(8,128)(2,1)S(1)} collective-permute-done((bf16[272,128]{1,0:T(8,128)(2,1)S(1)}, bf16[272,128]{1,0:T(8,128)(2,1)S(1)}, u32[]{:S(2)}, u32[]{:S(2)}) %collective-permute-start.10) | collective-permute-done | bytes 69664 | tf_op jit(solution)/shard_map/return/ppermute | solution.py:165
  38.0 1.6 %collective-permute-done.9.refs_2_ = bf16[272,128]{1,0:T(8,128)(2,1)S(1)} collective-permute-done((bf16[272,128]{1,0:T(8,128)(2,1)S(1)}, bf16[272,128]{1,0:T(8,128)(2,1)S(1)}, u32[]{:S(2)}, u32[]{:S(2)}) %collective-permute-start.9) | collective-permute-done | bytes 69664 | tf_op jit(solution)/shard_map/return/ppermute | solution.py:165
  39.6 0.9 %combine.1 = bf16[128,512]{1,0:T(8,128)(2,1)} custom-call(bf16[272,128]{1,0:T(8,128)(2,1)S(1)} %get-tuple-element.18.refs_0_, bf16[272,128]{1,0:T(8,128)(2,1)S(1)} %collective-permute-done.7.refs_1_, bf16[272,128]{1,0:T(8,128)(2,1)S(1)} %collective-permute-done.9.refs_2_, bf16[272,128]{1,0:T(8,128)(2,1)S(1)} %collective-permute-done.10.refs_3_, ...), custom_call_target="tpu_custom_call" | custom-call | tf_op jit(solution)/shard_map/combine/combine/pallas_call | solution.py:167
Async XLA Ops:
  0.0 2.7 %collective-permute-start.1 = (bf16[128,512]{1,0:T(8,128)(2,1)}, bf16[128,512]{1,0:T(8,128)(2,1)S(1)}, u32[]{:S(2)}, u32[]{:S(2)}) collective-permute-start(bf16[128,512]{1,0:T(8,128)(2,1)} %param.4), channel_id=1, source_target_pairs={{0,1},{1,0},{2,3},{3,2},{4,5},{5,4},{6,7},{7,6},{8,9},{9,8},{10,11... | collective-permute-start | bytes 393224 | tf_op jit(solution)/shard_map/swap/ppermute | solution.py:126
  0.5 2.3 %collective-permute-start.2 = (bf16[128,512]{1,0:T(8,128)(2,1)}, bf16[128,512]{1,0:T(8,128)(2,1)S(1)}, u32[]{:S(2)}, u32[]{:S(2)}) collective-permute-start(bf16[128,512]{1,0:T(8,128)(2,1)} %param.5), channel_id=1, source_target_pairs={{0,1},{1,0},{2,3},{3,2},{4,5},{5,4},{6,7},{7,6},{8,9},{9,8},{10,11... | collective-permute-start | bytes 393224 | tf_op jit(solution)/shard_map/swap/ppermute | solution.py:126
  0.5 2.3 %collective-permute-start.3 = (bf16[128,512]{1,0:T(8,128)(2,1)}, bf16[128,512]{1,0:T(8,128)(2,1)S(1)}, u32[]{:S(2)}, u32[]{:S(2)}) collective-permute-start(bf16[128,512]{1,0:T(8,128)(2,1)} %param.6), channel_id=1, source_target_pairs={{0,1},{1,0},{2,3},{3,2},{4,5},{5,4},{6,7},{7,6},{8,9},{9,8},{10,11... | collective-permute-start | bytes 393224 | tf_op jit(solution)/shard_map/swap/ppermute | solution.py:126
  1.0 1.8 %collective-permute-start = (s32[1]{0:T(128)}, s32[1]{0:T(128)}, u32[]{:S(2)}, u32[]{:S(2)}) collective-permute-start(s32[1]{0:T(128)} %param.7), channel_id=1, source_target_pairs={{0,1},{1,0},{2,3},{3,2},{4,5},{5,4},{6,7},{7,6},{8,9},{9,8},{10,11... | collective-permute-start | bytes 20 | tf_op jit(solution)/shard_map/swap/ppermute | solution.py:126
  3.6 10.2 %collective-permute-start.4 = (bf16[1040,128]{1,0:T(8,128)(2,1)S(1)}, bf16[1040,128]{1,0:T(8,128)(2,1)S(1)}, u32[]{:S(2)}, u32[]{:S(2)}) collective-permute-start(bf16[1040,128]{1,0:T(8,128)(2,1)S(1)} %get-tuple-element.17.refs_0_), channel_id=1, source_target_pairs={{0,8},{8,0},{16,24},{24,16},{1,9},{9,1},{17,25},{25,17},{2,10},{10... | collective-permute-start | bytes 798728 | tf_op jit(solution)/shard_map/exchange/ppermute | solution.py:144
  6.6 13.7 %collective-permute-start.5 = (bf16[1040,128]{1,0:T(8,128)(2,1)S(1)}, bf16[1040,128]{1,0:T(8,128)(2,1)S(1)}, u32[]{:S(2)}, u32[]{:S(2)}) collective-permute-start(bf16[1040,128]{1,0:T(8,128)(2,1)S(1)} %get-tuple-element.17.refs_0_), channel_id=1, source_target_pairs={{0,16},{8,24},{16,0},{24,8},{1,17},{9,25},{17,1},{25,9},{2,18},{10... | collective-permute-start | bytes 798728 | tf_op jit(solution)/shard_map/exchange/ppermute | solution.py:144
  8.1 12.2 %collective-permute-start.6 = (bf16[1040,128]{1,0:T(8,128)(2,1)S(1)}, bf16[1040,128]{1,0:T(8,128)(2,1)S(1)}, u32[]{:S(2)}, u32[]{:S(2)}) collective-permute-start(bf16[1040,128]{1,0:T(8,128)(2,1)S(1)} %get-tuple-element.17.refs_0_), channel_id=1, source_target_pairs={{0,24},{8,16},{16,8},{24,0},{1,25},{9,17},{17,9},{25,1},{2,26},{10... | collective-permute-start | bytes 798728 | tf_op jit(solution)/shard_map/exchange/ppermute | solution.py:144
  8.1 8.6 %collective-permute-start.14 = (bf16[528,128]{1,0:T(8,128)(2,1)S(1)}, bf16[528,128]{1,0:T(8,128)(2,1)S(1)}, u32[]{:S(2)}, u32[]{:S(2)}) collective-permute-start(bf16[528,128]{1,0:T(8,128)(2,1)S(1)} %get-tuple-element.20.q_ref), channel_id=1, source_target_pairs={{0,6},{1,7},{2,4},{3,5},{4,2},{5,3},{6,0},{7,1},{8,14},{9,15},{10,... | collective-permute-start | bytes 405512 | tf_op jit(solution)/shard_map/exchange/ppermute | solution.py:148
  12.2 13.0 %collective-permute-start.11 = (bf16[528,128]{1,0:T(8,128)(2,1)S(1)}, bf16[528,128]{1,0:T(8,128)(2,1)S(1)}, u32[]{:S(2)}, u32[]{:S(2)}) collective-permute-start(bf16[528,128]{1,0:T(8,128)(2,1)S(1)} %get-tuple-element.20.q_ref), channel_id=1, source_target_pairs={{0,4},{1,5},{2,6},{3,7},{4,0},{5,1},{6,2},{7,3},{8,12},{9,13},{10,... | collective-permute-start | bytes 405512 | tf_op jit(solution)/shard_map/exchange/ppermute | solution.py:148
  13.8 16.4 %collective-permute-start.8 = (bf16[528,128]{1,0:T(8,128)(2,1)S(1)}, bf16[528,128]{1,0:T(8,128)(2,1)S(1)}, u32[]{:S(2)}, u32[]{:S(2)}) collective-permute-start(bf16[528,128]{1,0:T(8,128)(2,1)S(1)} %get-tuple-element.20.q_ref), channel_id=1, source_target_pairs={{0,2},{1,3},{2,0},{3,1},{4,6},{5,7},{6,4},{7,5},{8,10},{9,11},{10,... | collective-permute-start | bytes 405512 | tf_op jit(solution)/shard_map/exchange/ppermute | solution.py:148
  21.5 10.4 %collective-permute-start.15 = (bf16[272,128]{1,0:T(8,128)(2,1)S(1)}, bf16[272,128]{1,0:T(8,128)(2,1)S(1)}, u32[]{:S(2)}, u32[]{:S(2)}) collective-permute-start(bf16[272,128]{1,0:T(8,128)(2,1)S(1)} %get-tuple-element.25), channel_id=1, source_target_pairs={{0,6},{1,7},{2,4},{3,5},{4,2},{5,3},{6,0},{7,1},{8,14},{9,15},{10,... | collective-permute-start | bytes 208904 | tf_op jit(solution)/shard_map/return/ppermute | solution.py:165
  25.2 8.1 %collective-permute-start.16 = (bf16[272,128]{1,0:T(8,128)(2,1)S(1)}, bf16[272,128]{1,0:T(8,128)(2,1)S(1)}, u32[]{:S(2)}, u32[]{:S(2)}) collective-permute-start(bf16[272,128]{1,0:T(8,128)(2,1)S(1)} %get-tuple-element.26), channel_id=1, source_target_pairs={{0,7},{1,6},{2,5},{3,4},{4,3},{5,2},{6,1},{7,0},{8,15},{9,14},{10,... | collective-permute-start | bytes 208904 | tf_op jit(solution)/shard_map/return/ppermute | solution.py:165
  26.3 8.9 %collective-permute-start.12 = (bf16[272,128]{1,0:T(8,128)(2,1)S(1)}, bf16[272,128]{1,0:T(8,128)(2,1)S(1)}, u32[]{:S(2)}, u32[]{:S(2)}) collective-permute-start(bf16[272,128]{1,0:T(8,128)(2,1)S(1)} %get-tuple-element.23), channel_id=1, source_target_pairs={{0,4},{1,5},{2,6},{3,7},{4,0},{5,1},{6,2},{7,3},{8,12},{9,13},{10,... | collective-permute-start | bytes 208904 | tf_op jit(solution)/shard_map/return/ppermute | solution.py:165
  26.4 10.3 %collective-permute-start.13 = (bf16[272,128]{1,0:T(8,128)(2,1)S(1)}, bf16[272,128]{1,0:T(8,128)(2,1)S(1)}, u32[]{:S(2)}, u32[]{:S(2)}) collective-permute-start(bf16[272,128]{1,0:T(8,128)(2,1)S(1)} %get-tuple-element.24), channel_id=1, source_target_pairs={{0,5},{1,4},{2,7},{3,6},{4,1},{5,0},{6,3},{7,2},{8,13},{9,12},{10,... | collective-permute-start | bytes 208904 | tf_op jit(solution)/shard_map/return/ppermute | solution.py:165
  30.2 6.6 %collective-permute-start.7 = (bf16[272,128]{1,0:T(8,128)(2,1)S(1)}, bf16[272,128]{1,0:T(8,128)(2,1)S(1)}, u32[]{:S(2)}, u32[]{:S(2)}) collective-permute-start(bf16[272,128]{1,0:T(8,128)(2,1)S(1)} %get-tuple-element.19), channel_id=1, source_target_pairs={{0,1},{1,0},{2,3},{3,2},{4,5},{5,4},{6,7},{7,6},{8,9},{9,8},{10,11... | collective-permute-start | bytes 208904 | tf_op jit(solution)/shard_map/return/ppermute | solution.py:165
  31.9 6.1 %collective-permute-start.10 = (bf16[272,128]{1,0:T(8,128)(2,1)S(1)}, bf16[272,128]{1,0:T(8,128)(2,1)S(1)}, u32[]{:S(2)}, u32[]{:S(2)}) collective-permute-start(bf16[272,128]{1,0:T(8,128)(2,1)S(1)} %get-tuple-element.22), channel_id=1, source_target_pairs={{0,3},{1,2},{2,1},{3,0},{4,7},{5,6},{6,5},{7,4},{8,11},{9,10},{10,... | collective-permute-start | bytes 208904 | tf_op jit(solution)/shard_map/return/ppermute | solution.py:165
  33.2 6.4 %collective-permute-start.9 = (bf16[272,128]{1,0:T(8,128)(2,1)S(1)}, bf16[272,128]{1,0:T(8,128)(2,1)S(1)}, u32[]{:S(2)}, u32[]{:S(2)}) collective-permute-start(bf16[272,128]{1,0:T(8,128)(2,1)S(1)} %get-tuple-element.21), channel_id=1, source_target_pairs={{0,2},{1,3},{2,0},{3,1},{4,6},{5,7},{6,4},{7,5},{8,10},{9,11},{10,... | collective-permute-start | bytes 208904 | tf_op jit(solution)/shard_map/return/ppermute | solution.py:165

commit v5 on v4

v5 whole, which is shorter than its diff:
```python
import functools
import math

import jax
import jax.numpy as jnp
from jax import lax
from jax.experimental import pallas as pl
from jax.experimental.pallas import tpu as pltpu
from jax.sharding import PartitionSpec as P

HEADS = 4
CORES = 2
PER = HEADS // CORES
PAD = 16
LOW = -1e30
FLOOR = -1e29
BF16 = jnp.bfloat16
F32 = jnp.float32


def nt_dot(a, b):
    return lax.dot_general(a, b, (((1,), (1,)), ((), ())), preferred_element_type=F32)


def merge_kernel(p0, p1, own, q1, k1, v1, q_out, kv_out):
    tok = q1.shape[0]
    size = q1.shape[1] // HEADS
    q0, k0, v0 = (own.at[i * tok : (i + 1) * tok, :] for i in range(3))
    core = lax.rem(lax.axis_index("inner"), CORES)
    both = CORES * tok
    for b, (q, k, v) in enumerate(((q0, k0, v0), (q1, k1, v1))):
        for j in range(PER):
            cols = pl.ds(pl.multiple_of((core * PER + j) * size, size), size)
            q_out[j * both + b * tok : j * both + (b + 1) * tok, :] = q[:, cols]
            kv_out[j * both + b * tok : j * both + (b + 1) * tok, :] = k[:, cols]
            at = PAD + (PER + j) * both + b * tok
            kv_out[at : at + tok, :] = v[:, cols].astype(F32).T.astype(BF16)
    half = PAD // CORES
    pos = jnp.concatenate([jnp.full((half, size), p[0].astype(F32), F32) for p in (p0, p1)], axis=0).astype(BF16)
    q_out[PER * both :, :] = pos
    kv_out[PER * both : PER * both + PAD, :] = pos


def attend_kernel(wide, where, q_ref, *refs):
    n = 1 + max(w[2] for w in where)
    kv_refs, out_refs = refs[:n], refs[n:]
    size = q_ref.shape[1]
    tok = size
    both = CORES * tok
    half = PAD // CORES
    block = PER * size + PAD
    rate = size ** -0.5 * math.log2(math.e)
    rows = lax.broadcasted_iota(jnp.int32, (tok, both), 0).astype(F32)
    lanes = lax.broadcasted_iota(jnp.int32, (1, tok), 1).astype(F32)

    def start_of(ref, at):
        first = ref[at : at + PAD, :].astype(F32)
        return [first[b * half : b * half + 1, :] * tok for b in range(CORES)]

    def store(b, at, value):
        if wide:
            out_refs[0][b * block + at : b * block + at + value.shape[0], :] = value
        else:
            out_refs[b][at : at + value.shape[0], :] = value

    qpos = jnp.concatenate([s + lanes for s in start_of(q_ref, PER * both)], axis=1)
    limits = []
    for k, k_at, _, _ in where:
        for s in start_of(kv_refs[k], k_at + PER * both):
            limits.append(qpos - jnp.concatenate([s] * CORES, axis=1))
    stats = [[] for _ in range(CORES)]
    for h in range(PER):
        q = q_ref[h * both : (h + 1) * both, :]
        parts, vals = [], []
        for j, (k, k_at, v, v_at) in enumerate(where):
            s = nt_dot(kv_refs[k][k_at + h * both : k_at + (h + 1) * both, :], q)
            for b in range(CORES):
                parts.append(jnp.where(rows <= limits[j * CORES + b], s[b * tok : (b + 1) * tok, :], LOW))
                at = v_at + h * both + b * tok
                vals.append(kv_refs[v][at : at + tok, :])
        s = jnp.concatenate(parts, axis=0)
        top = jnp.maximum(jnp.max(s, axis=0, keepdims=True), FLOOR).astype(BF16)
        p = jnp.exp2((s - top.astype(F32)) * rate).astype(BF16)
        vt = jnp.concatenate(vals, axis=1)
        vt = jnp.concatenate([vt, jnp.ones((PAD, vt.shape[1]), BF16)], axis=0)
        o = jnp.dot(vt, p, preferred_element_type=F32)
        total = o[size : size + 1, :]
        hi = total.astype(BF16)
        lo = (total - hi.astype(F32)).astype(BF16)
        for b in range(CORES):
            cols = slice(b * tok, (b + 1) * tok)
            store(b, h * size, o[0:size, cols].astype(BF16))
            stats[b] += [top[:, cols].astype(F32), hi[:, cols].astype(F32), lo[:, cols].astype(F32)]
    for b in range(CORES):
        rest = jnp.zeros((PAD - 3 * PER, tok), F32)
        store(b, PER * size, jnp.concatenate(stats[b] + [rest], axis=0).astype(BF16))


def joined(parts, stats, h, rate):
    size = parts[0].shape[0]
    tops = [s[3 * h : 3 * h + 1, :] for s in stats]
    best = functools.reduce(jnp.maximum, tops)
    factors = [jnp.exp2((t - best) * rate) for t in tops]
    total = sum(f * (s[3 * h + 1 : 3 * h + 2, :] + s[3 * h + 2 : 3 * h + 3, :]) for f, s in zip(factors, stats))
    numer = sum(f * part.astype(F32) for f, part in zip(factors, parts))
    return best, total, numer


def add_kernel(n, wide, *refs):
    size = refs[0].shape[1]
    block = PER * size + PAD
    rate = size ** -0.5 * math.log2(math.e)
    for b in range(CORES):
        base = b * block
        stats = [ref[base + PER * size : base + block, :].astype(F32) for ref in refs[:n]]
        out, at = (refs[n], base) if wide else (refs[n + b], 0)
        rows = []
        for h in range(PER):
            parts = [ref[base + h * size : base + (h + 1) * size, :] for ref in refs[:n]]
            best, total, numer = joined(parts, stats, h, rate)
            hi = total.astype(BF16).astype(F32)
            rows += [best, hi, total - hi]
            out[at + h * size : at + (h + 1) * size, :] = numer.astype(BF16)
        rest = jnp.zeros((PAD - 3 * PER, size), F32)
        out[at + PER * size : at + block, :] = jnp.concatenate(rows + [rest], axis=0).astype(BF16)


def combine_kernel(n, *refs):
    parts, out_ref = refs[:n], refs[n]
    size = parts[0].shape[1]
    rate = size ** -0.5 * math.log2(math.e)
    core = lax.rem(lax.axis_index("inner"), CORES)
    for x in range(CORES):
        mine = parts[x::CORES]
        pair = jnp.bitwise_xor(core, x)
        stats = [part[PER * size :, :].astype(F32) for part in mine]
        for h in range(PER):
            _, total, numer = joined([part[h * size : (h + 1) * size, :] for part in mine], stats, h, rate)
            cols = pl.ds(pl.multiple_of((pair * PER + h) * size, size), size)
            out_ref[:, cols] = (numer / total).T.astype(BF16)


def vmem(n=1):
    return [pl.BlockSpec(memory_space=pltpu.VMEM)] * n


def shards(n_out, n_in, queries, keys, values, block_pos):
    tok, width = queries.shape
    size = width // HEADS
    chips = n_in // CORES
    both = CORES * tok
    params = pltpu.CompilerParams(vmem_limit_bytes=40 * 1024 * 1024)

    def along_inner(r, x):
        return [(w * CORES + c, (w ^ r) * CORES + (c ^ x)) for w in range(chips) for c in range(CORES)]

    with jax.named_scope("swap"):
        other = [lax.ppermute(a, "inner", along_inner(0, 1)) for a in (queries, keys, values, block_pos)]
        own = jnp.concatenate([queries, keys, values], axis=0)
    with jax.named_scope("merge"):
        smem = [pl.BlockSpec(memory_space=pltpu.SMEM)]
        q_piece, kv_piece = pl.pallas_call(
            merge_kernel,
            out_shape=(
                jax.ShapeDtypeStruct((PER * both + PAD, size), BF16),
                jax.ShapeDtypeStruct((2 * PER * both + PAD, size), BF16),
            ),
            in_specs=smem * 2 + vmem(4),
            out_specs=tuple(vmem(2)),
            compiler_params=params,
            name="merge",
        )(block_pos, other[3], own, *other[:3])
    half = PER * both + PAD
    block = PER * size + PAD

    def low(r):
        return r & -r

    def high(r):
        return 1 << (r.bit_length() - 1)

    def single(r):
        return r == low(r)

    def over(a, r):
        return lax.ppermute(a, "outer", [(o, o ^ r) for o in range(n_out)])

    with jax.named_scope("exchange"):
        whole = {0: kv_piece}
        for r in range(1, n_out):
            if single(r):
                whole[r] = over(kv_piece, r)
        k_part = {r: a[:half, :] for r, a in whole.items() if r}
        v_part = {r: a[half:, :] for r, a in whole.items() if r}
        for r in range(1, n_out):
            if not single(r):
                k_part[r] = over(k_part[r - high(r)], high(r))
        for r in sorted(range(1, n_out), key=lambda r: r.bit_count()):
            if not single(r):
                v_part[r] = over(v_part[r - low(r)], low(r))
        q_by = {0: q_piece}
        bit = chips // 2
        while bit:
            for r in sorted(q_by):
                q_by[r | bit] = lax.ppermute(q_by[r], "inner", along_inner(bit, 0))
            bit //= 2
    kv, where = [], []
    for r in range(n_out):
        if r in whole:
            where.append((len(kv), 0, len(kv), half))
            kv.append(whole[r])
        else:
            where.append((len(kv), 0, len(kv) + 1, 0))
            kv += [k_part[r], v_part[r]]

    def shapes(wide):
        rows = CORES * block if wide else block
        return (jax.ShapeDtypeStruct((rows, tok), BF16),) * (1 if wide else CORES)

    def attend(r, wide):
        work = 4 * PER * both * n_out * both * size
        with jax.named_scope("attend"):
            return pl.pallas_call(
                functools.partial(attend_kernel, wide, tuple(where)),
                out_shape=shapes(wide),
                in_specs=vmem(1 + len(kv)),
                out_specs=tuple(vmem(len(shapes(wide)))),
                compiler_params=params,
                cost_estimate=pl.CostEstimate(flops=work, bytes_accessed=2**20, transcendentals=work // (4 * size)),
                name="attend",
            )(q_by[r], *kv)

    def add(arrays, wide):
        with jax.named_scope("add"):
            return pl.pallas_call(
                functools.partial(add_kernel, len(arrays), wide),
                out_shape=shapes(wide),
                in_specs=vmem(len(arrays)),
                out_specs=tuple(vmem(len(shapes(wide)))),
                compiler_params=params,
                name="add",
            )(*arrays)

    arrived = {r: [] for r in range(chips)}
    ends = []
    for r in sorted(range(1, chips), key=lambda r: (low(r), -r)):
        last = single(r)
        alone = not (low(r) > 1)
        parts = attend(r, not (last and alone))
        if not alone:
            parts = add([parts[0], *arrived[r]], not last)
        with jax.named_scope("return"):
            if last:
                ends += [lax.ppermute(parts[x], "inner", along_inner(r, x)) for x in range(CORES)]
            else:
                arrived[r - low(r)].append(lax.ppermute(parts[0], "inner", along_inner(low(r), 0)))
    own = attend(0, False)
    with jax.named_scope("return"):
        ends = [own[0], lax.ppermute(own[1], "inner", along_inner(0, 1))] + ends
    with jax.named_scope("combine"):
        return pl.pallas_call(
            functools.partial(combine_kernel, len(ends)),
            out_shape=jax.ShapeDtypeStruct((tok, width), BF16),
            in_specs=vmem(len(ends)),
            out_specs=vmem()[0],
            compiler_params=params,
            name="combine",
        )(*ends)


def solution(mesh):
    n_out, n_in = mesh.shape["outer"], mesh.shape["inner"]
    return jax.shard_map(
        functools.partial(shards, n_out, n_in),
        mesh=mesh,
        in_specs=(
            P(("outer", "inner"), None),
            P(("outer", "inner"), None),
            P(("outer", "inner"), None),
            P(("outer", "inner")),
        ),
        out_specs=P(("outer", "inner"), None),
        check_vma=False,
    )
```

time: 40.6 us -> 42.3 us (1.042)
  waiting for transfers between devices: 11 us -> 16.2 us
  starting transfers between devices: 21.3 us -> 17.8 us
    ppermute x13, waiting for transfers between devices: 11 us -> 16.2 us  [the longest x3 9.33 us: shards(): q_by[r | bit] = lax.ppermute(q_by[r], 'inner', along_inner(bit, 0))]
    ppermute x13, starting transfers between devices: 20.3 us -> 16.8 us  [the longest x4 5.69 us: over(): return lax.ppermute(a, 'outer', [(o, o ^ r) for o in range(n_out)])]
    pallas_call x5 -> x6, Pallas kernels: 5.57 us -> 5.63 us  [the longest x4 4.72 us: attend(): pl.pallas_call(functools.partial(attend_kernel, wide, tuple(where)), out_...]
  transfers between devices with their start and end apart: 17 -> 17, of which waited for: 7 -> 4; matrix products, arithmetic and copies ran while one was open for 3% -> 3% of each run, Pallas kernels for 12% -> 11%
where the time goes in v5:
time: 42.3 us; the launch traced here: 42.2 us
  starting transfers between devices  17.8 us (42%)
  waiting for transfers between devices  16.2 us (38%)
  Pallas kernels  6.34 us (15%)
  other arithmetic  1.06 us (3%)
  between operations  0.77 us (2%)
    ppermute x3, waiting for transfers between devices, shards(): q_by[r | bit] = lax.ppermute(q_by[r], 'inner', along_inner(bit, 0))  9.33 us
    ppermute x4, waiting for transfers between devices, shards(): lax.ppermute(parts[x], 'inner', along_inner(r, x))  6.82 us
    ppermute x4, starting transfers between devices, over(): return lax.ppermute(a, 'outer', [(o, o ^ r) for o in range(n_out)])  5.69 us
    pallas_call x4, Pallas kernels, attend(): pl.pallas_call(functools.partial(attend_kernel, wide, tuple(where)), out_...  4.72 us
    ppermute x3, starting transfers between devices, shards(): q_by[r | bit] = lax.ppermute(q_by[r], 'inner', along_inner(bit, 0))  4.56 us
    ppermute x4, starting transfers between devices, shards(): lax.ppermute(parts[x], 'inner', along_inner(r, x))  3.7 us
    ppermute x1, starting transfers between devices, shards(): ends = [own[0], lax.ppermute(own[1], 'inner', along_inner(0, 1))] + ends  1.48 us
    ppermute x1, starting transfers between devices, shards(): lax.ppermute(parts[0], 'inner', along_inner(low(r), 0))  1.36 us
  transfers between devices with their start and end apart: 17, of which 4 were waited for; matrix products, arithmetic and copies ran while one was open for 3% of the time, Pallas kernels for 11%

profile of v5, /device:TPU:0, one launch (start us, length us, event | category | flops | bytes accessed | tf_op | source)
XLA Modules:
  0.0 42.2 jit_solution(12148263135604350090)
XLA Ops:
  0.0 0.5 %collective-permute-start.1 = (bf16[128,512]{1,0:T(8,128)(2,1)}, bf16[128,512]{1,0:T(8,128)(2,1)S(1)}, u32[]{:S(2)}, u32[]{:S(2)}) collective-permute-start(bf16[128,512]{1,0:T(8,128)(2,1)} %param.4), channel_id=1, source_target_pairs={{0,1},{1,0},{2,3},{3,2},{4,5},{5,4},{6,7},{7,6},{8,9},{9,8},{10,11... | collective-permute-start | bytes 393224 | tf_op jit(solution)/shard_map/swap/ppermute | solution.py:158
  0.5 0.1 collective-permute-start.2
  0.5 0.5 %collective-permute-start.3 = (bf16[128,512]{1,0:T(8,128)(2,1)}, bf16[128,512]{1,0:T(8,128)(2,1)S(1)}, u32[]{:S(2)}, u32[]{:S(2)}) collective-permute-start(bf16[128,512]{1,0:T(8,128)(2,1)} %param.6), channel_id=1, source_target_pairs={{0,1},{1,0},{2,3},{3,2},{4,5},{5,4},{6,7},{7,6},{8,9},{9,8},{10,11... | collective-permute-start | bytes 393224 | tf_op jit(solution)/shard_map/swap/ppermute | solution.py:158
  1.0 0.1 collective-permute-start
  1.7 1.1 %pad_maximum_fusion.own = bf16[384,512]{1,0:T(8,128)(2,1)S(1)} fusion(bf16[128,512]{1,0:T(8,128)(2,1)} %param.6, bf16[128,512]{1,0:T(8,128)(2,1)} %param.5, bf16[128,512]{1,0:T(8,128)(2,1)} %param.4), kind=kLoop, calls=%fused_computation | loop fusion | flops 1179648 | bytes 786432 | tf_op jit(solution)/shard_map/swap/concatenate | solution.py:159
  2.7 0.0 collective-permute-done.p1
  2.7 0.0 collective-permute-done.1.q1
  2.8 0.0 collective-permute-done.2.k1
  2.8 0.0 collective-permute-done.3.v1
  2.8 0.7 %merge.1 = (bf16[528,128]{1,0:T(8,128)(2,1)S(1)}, bf16[1040,128]{1,0:T(8,128)(2,1)S(1)}) custom-call(s32[1]{0:T(128)S(6)} %copy.5.p0, s32[1]{0:T(128)} %collective-permute-done.p1, bf16[384,512]{1,0:T(8,128)(2,1)S(1)} %pad_maximum_fusion.own, bf16[128,512]{1,0:T(8,128)(2,1)S(1)} %collective-permute-done.1.q1, ...), custom_call_target="tpu_custom_call" | custom-call | tf_op jit(solution)/shard_map/merge/merge/pallas_call | solution.py:162
  3.5 3.0 %collective-permute-start.4 = (bf16[1040,128]{1,0:T(8,128)(2,1)S(1)}, bf16[1040,128]{1,0:T(8,128)(2,1)S(1)}, u32[]{:S(2)}, u32[]{:S(2)}) collective-permute-start(bf16[1040,128]{1,0:T(8,128)(2,1)S(1)} %get-tuple-element.14.refs_0_), channel_id=1, source_target_pairs={{0,8},{8,0},{16,24},{24,16},{1,9},{9,1},{17,25},{25,17},{2,10},{10... | collective-permute-start | bytes 798728 | tf_op jit(solution)/shard_map/exchange/ppermute | solution.py:186
  6.5 1.5 %collective-permute-start.5 = (bf16[1040,128]{1,0:T(8,128)(2,1)S(1)}, bf16[1040,128]{1,0:T(8,128)(2,1)S(1)}, u32[]{:S(2)}, u32[]{:S(2)}) collective-permute-start(bf16[1040,128]{1,0:T(8,128)(2,1)S(1)} %get-tuple-element.14.refs_0_), channel_id=1, source_target_pairs={{0,16},{8,24},{16,0},{24,8},{1,17},{9,25},{17,1},{25,9},{2,18},{10... | collective-permute-start | bytes 798728 | tf_op jit(solution)/shard_map/exchange/ppermute | solution.py:186
  8.0 2.6 %collective-permute-start.12 = (bf16[528,128]{1,0:T(8,128)(2,1)S(1)}, bf16[528,128]{1,0:T(8,128)(2,1)S(1)}, u32[]{:S(2)}, u32[]{:S(2)}) collective-permute-start(bf16[528,128]{1,0:T(8,128)(2,1)S(1)} %get-tuple-element.13.q_ref), channel_id=1, source_target_pairs={{0,4},{1,5},{2,6},{3,7},{4,0},{5,1},{6,2},{7,3},{8,12},{9,13},{10,... | collective-permute-start | bytes 405512 | tf_op jit(solution)/shard_map/exchange/ppermute | solution.py:205
  10.6 6.1 %collective-permute-done.12.q_ref = bf16[528,128]{1,0:T(8,128)(2,1)S(1)} collective-permute-done((bf16[528,128]{1,0:T(8,128)(2,1)S(1)}, bf16[528,128]{1,0:T(8,128)(2,1)S(1)}, u32[]{:S(2)}, u32[]{:S(2)}) %collective-permute-start.12) | collective-permute-done | bytes 135200 | tf_op jit(solution)/shard_map/exchange/ppermute | solution.py:205
  16.8 0.7 %collective-permute-start.13 = (bf16[528,128]{1,0:T(8,128)(2,1)S(1)}, bf16[528,128]{1,0:T(8,128)(2,1)S(1)}, u32[]{:S(2)}, u32[]{:S(2)}) collective-permute-start(bf16[528,128]{1,0:T(8,128)(2,1)S(1)} %collective-permute-done.12.q_ref), channel_id=1, source_target_pairs={{0,2},{1,3},{2,0},{3,1},{4,6},{5,7},{6,4},{7,5},{8,10},{9,11},{10,... | collective-permute-start | bytes 405512 | tf_op jit(solution)/shard_map/exchange/ppermute | solution.py:205
  17.4 0.0 collective-permute-done.4.refs_1_
  17.4 0.6 %collective-permute-start.6 = (bf16[528,128]{1,0:T(8,128)(2,1)S(1)}, bf16[528,128]{1,0:T(8,128)(2,1)S(1)}, u32[]{:S(2)}, u32[]{:S(2)}) collective-permute-start(bf16[528,128]{1,0:T(8,128)(2,1)S(1)} %slice.8), channel_id=1, source_target_pairs={{0,16},{8,24},{16,0},{24,8},{1,17},{9,25},{17,1},{25,9},{2,18},{10... | collective-permute-start | bytes 405512 | tf_op jit(solution)/shard_map/exchange/ppermute | solution.py:186
  18.0 0.0 collective-permute-done.5.refs_2_
  18.0 0.6 %collective-permute-start.7 = (bf16[512,128]{1,0:T(8,128)(2,1)S(1)}, bf16[512,128]{1,0:T(8,128)(2,1)S(1)}, u32[]{:S(2)}, u32[]{:S(2)}) collective-permute-start(bf16[512,128]{1,0:T(8,128)(2,1)S(1)} %slice.9), channel_id=1, source_target_pairs={{0,8},{8,0},{16,24},{24,16},{1,9},{9,1},{17,25},{25,17},{2,10},{10... | collective-permute-start | bytes 393224 | tf_op jit(solution)/shard_map/exchange/ppermute | solution.py:186
  18.6 1.3 %collective-permute-start.9 = (bf16[528,128]{1,0:T(8,128)(2,1)S(1)}, bf16[528,128]{1,0:T(8,128)(2,1)S(1)}, u32[]{:S(2)}, u32[]{:S(2)}) collective-permute-start(bf16[528,128]{1,0:T(8,128)(2,1)S(1)} %get-tuple-element.13.q_ref), channel_id=1, source_target_pairs={{0,2},{1,3},{2,0},{3,1},{4,6},{5,7},{6,4},{7,5},{8,10},{9,11},{10,... | collective-permute-start | bytes 405512 | tf_op jit(solution)/shard_map/exchange/ppermute | solution.py:205
  19.9 3.2 %collective-permute-done.13.q_ref = bf16[528,128]{1,0:T(8,128)(2,1)S(1)} collective-permute-done((bf16[528,128]{1,0:T(8,128)(2,1)S(1)}, bf16[528,128]{1,0:T(8,128)(2,1)S(1)}, u32[]{:S(2)}, u32[]{:S(2)}) %collective-permute-start.13) | collective-permute-done | bytes 135200 | tf_op jit(solution)/shard_map/exchange/ppermute | solution.py:205
  23.1 0.0 collective-permute-done.7.refs_4_
  23.1 0.0 collective-permute-done.6.refs_3_
  23.1 1.2 %attend.7 = bf16[544,128]{1,0:T(8,128)(2,1)S(1)} custom-call(bf16[528,128]{1,0:T(8,128)(2,1)S(1)} %collective-permute-done.13.q_ref, bf16[1040,128]{1,0:T(8,128)(2,1)S(1)} %get-tuple-element.14.refs_0_, bf16[1040,128]{1,0:T(8,128)(2,1)S(1)} %collective-permute-done.4.refs_1_, bf16[1040,128]{1,0:T(8,128)(2,1)S(1)} %collective-permute-done.5.refs_2_, ...), custom_call_target="tpu_custom_call" | custom-call | flops 268435456 | bytes 1048576 | tf_op jit(solution)/shard_map/attend/attend/pallas_call | solution.py:223
  24.3 1.4 %collective-permute-start.14 = (bf16[544,128]{1,0:T(8,128)(2,1)S(1)}, bf16[544,128]{1,0:T(8,128)(2,1)S(1)}, u32[]{:S(2)}, u32[]{:S(2)}) collective-permute-start(bf16[544,128]{1,0:T(8,128)(2,1)S(1)} %attend.7), channel_id=1, source_target_pairs={{0,2},{1,3},{2,0},{3,1},{4,6},{5,7},{6,4},{7,5},{8,10},{9,11},{10,... | collective-permute-start | bytes 417800 | tf_op jit(solution)/shard_map/return/ppermute | solution.py:256
  25.7 0.0 collective-permute-done.9.q_ref
  25.7 1.2 %attend.5 = (bf16[272,128]{1,0:T(8,128)(2,1)S(1)}, bf16[272,128]{1,0:T(8,128)(2,1)S(1)}) custom-call(bf16[528,128]{1,0:T(8,128)(2,1)S(1)} %collective-permute-done.9.q_ref, bf16[1040,128]{1,0:T(8,128)(2,1)S(1)} %get-tuple-element.14.refs_0_, bf16[1040,128]{1,0:T(8,128)(2,1)S(1)} %collective-permute-done.4.refs_1_, ...), custom_call_target="tpu_custom_call" | custom-call | flops 268435456 | bytes 1048576 | tf_op jit(solution)/shard_map/attend/attend/pallas_call | solution.py:223
  26.9 0.8 %collective-permute-start.10 = (bf16[272,128]{1,0:T(8,128)(2,1)S(1)}, bf16[272,128]{1,0:T(8,128)(2,1)S(1)}, u32[]{:S(2)}, u32[]{:S(2)}) collective-permute-start(bf16[272,128]{1,0:T(8,128)(2,1)S(1)} %get-tuple-element.17), channel_id=1, source_target_pairs={{0,2},{1,3},{2,0},{3,1},{4,6},{5,7},{6,4},{7,5},{8,10},{9,11},{10,... | collective-permute-start | bytes 208904 | tf_op jit(solution)/shard_map/return/ppermute | solution.py:254
  27.7 0.0 collective-permute-start.11
  27.7 1.2 %attend.4 = (bf16[272,128]{1,0:T(8,128)(2,1)S(1)}, bf16[272,128]{1,0:T(8,128)(2,1)S(1)}) custom-call(bf16[528,128]{1,0:T(8,128)(2,1)S(1)} %get-tuple-element.13.q_ref, bf16[1040,128]{1,0:T(8,128)(2,1)S(1)} %get-tuple-element.14.refs_0_, bf16[1040,128]{1,0:T(8,128)(2,1)S(1)} %collective-permute-done.4.refs_1_, ...), custom_call_target="tpu_custom_call" | custom-call | flops 268435456 | bytes 1048576 | tf_op jit(solution)/shard_map/attend/attend/pallas_call | solution.py:223
  28.8 1.5 %collective-permute-start.8 = (bf16[272,128]{1,0:T(8,128)(2,1)S(1)}, bf16[272,128]{1,0:T(8,128)(2,1)S(1)}, u32[]{:S(2)}, u32[]{:S(2)}) collective-permute-start(bf16[272,128]{1,0:T(8,128)(2,1)S(1)} %get-tuple-element.16), channel_id=1, source_target_pairs={{0,1},{1,0},{2,3},{3,2},{4,5},{5,4},{6,7},{7,6},{8,9},{9,8},{10,11... | collective-permute-start | bytes 208904 | tf_op jit(solution)/shard_map/return/ppermute | solution.py:259
  30.3 1.2 %attend.6.refs_0_ = bf16[544,128]{1,0:T(8,128)(2,1)S(1)} custom-call(bf16[528,128]{1,0:T(8,128)(2,1)S(1)} %collective-permute-done.12.q_ref, bf16[1040,128]{1,0:T(8,128)(2,1)S(1)} %get-tuple-element.14.refs_0_, bf16[1040,128]{1,0:T(8,128)(2,1)S(1)} %collective-permute-done.4.refs_1_, bf16[1040,128]{1,0:T(8,128)(2,1)S(1)} %collective-permute-done.5.refs_2_, ...), custom_call_target="tpu_custom_call" | custom-call | flops 268435456 | bytes 1048576 | tf_op jit(solution)/shard_map/attend/attend/pallas_call | solution.py:223
  31.5 0.0 collective-permute-done.14.refs_1_
  31.5 0.1 add.1
  31.6 2.9 %collective-permute-start.15 = (bf16[272,128]{1,0:T(8,128)(2,1)S(1)}, bf16[272,128]{1,0:T(8,128)(2,1)S(1)}, u32[]{:S(2)}, u32[]{:S(2)}) collective-permute-start(bf16[272,128]{1,0:T(8,128)(2,1)S(1)} %get-tuple-element.19), channel_id=1, source_target_pairs={{0,4},{1,5},{2,6},{3,7},{4,0},{5,1},{6,2},{7,3},{8,12},{9,13},{10,... | collective-permute-start | bytes 208904 | tf_op jit(solution)/shard_map/return/ppermute | solution.py:254
  34.5 0.0 collective-permute-start.16
  34.5 0.0 collective-permute-done.10.refs_2_
  34.5 0.0 collective-permute-done.11.refs_3_
  34.5 0.0 collective-permute-done.8.refs_1_
  34.5 3.8 %collective-permute-done.15.refs_4_ = bf16[272,128]{1,0:T(8,128)(2,1)S(1)} collective-permute-done((bf16[272,128]{1,0:T(8,128)(2,1)S(1)}, bf16[272,128]{1,0:T(8,128)(2,1)S(1)}, u32[]{:S(2)}, u32[]{:S(2)}) %collective-permute-start.15) | collective-permute-done | bytes 69664 | tf_op jit(solution)/shard_map/return/ppermute | solution.py:254
  38.4 3.0 %collective-permute-done.16.refs_5_ = bf16[272,128]{1,0:T(8,128)(2,1)S(1)} collective-permute-done((bf16[272,128]{1,0:T(8,128)(2,1)S(1)}, bf16[272,128]{1,0:T(8,128)(2,1)S(1)}, u32[]{:S(2)}, u32[]{:S(2)}) %collective-permute-start.16) | collective-permute-done | bytes 69664 | tf_op jit(solution)/shard_map/return/ppermute | solution.py:254
  41.3 0.8 %combine.1 = bf16[128,512]{1,0:T(8,128)(2,1)} custom-call(bf16[272,128]{1,0:T(8,128)(2,1)S(1)} %get-tuple-element.15.refs_0_, bf16[272,128]{1,0:T(8,128)(2,1)S(1)} %collective-permute-done.8.refs_1_, bf16[272,128]{1,0:T(8,128)(2,1)S(1)} %collective-permute-done.10.refs_2_, bf16[272,128]{1,0:T(8,128)(2,1)S(1)} %collective-permute-done.11.refs_3_, ...), custom_call_target="tpu_custom_call" | custom-call | tf_op jit(solution)/shard_map/combine/combine/pallas_call | solution.py:261
  (2 shorter events, 0.0 us)
Async XLA Ops:
  0.0 2.7 %collective-permute-start.1 = (bf16[128,512]{1,0:T(8,128)(2,1)}, bf16[128,512]{1,0:T(8,128)(2,1)S(1)}, u32[]{:S(2)}, u32[]{:S(2)}) collective-permute-start(bf16[128,512]{1,0:T(8,128)(2,1)} %param.4), channel_id=1, source_target_pairs={{0,1},{1,0},{2,3},{3,2},{4,5},{5,4},{6,7},{7,6},{8,9},{9,8},{10,11... | collective-permute-start | bytes 393224 | tf_op jit(solution)/shard_map/swap/ppermute | solution.py:158
  0.5 2.3 %collective-permute-start.2 = (bf16[128,512]{1,0:T(8,128)(2,1)}, bf16[128,512]{1,0:T(8,128)(2,1)S(1)}, u32[]{:S(2)}, u32[]{:S(2)}) collective-permute-start(bf16[128,512]{1,0:T(8,128)(2,1)} %param.5), channel_id=1, source_target_pairs={{0,1},{1,0},{2,3},{3,2},{4,5},{5,4},{6,7},{7,6},{8,9},{9,8},{10,11... | collective-permute-start | bytes 393224 | tf_op jit(solution)/shard_map/swap/ppermute | solution.py:158
  0.5 2.3 %collective-permute-start.3 = (bf16[128,512]{1,0:T(8,128)(2,1)}, bf16[128,512]{1,0:T(8,128)(2,1)S(1)}, u32[]{:S(2)}, u32[]{:S(2)}) collective-permute-start(bf16[128,512]{1,0:T(8,128)(2,1)} %param.6), channel_id=1, source_target_pairs={{0,1},{1,0},{2,3},{3,2},{4,5},{5,4},{6,7},{7,6},{8,9},{9,8},{10,11... | collective-permute-start | bytes 393224 | tf_op jit(solution)/shard_map/swap/ppermute | solution.py:158
  1.0 1.8 %collective-permute-start = (s32[1]{0:T(128)}, s32[1]{0:T(128)}, u32[]{:S(2)}, u32[]{:S(2)}) collective-permute-start(s32[1]{0:T(128)} %param.7), channel_id=1, source_target_pairs={{0,1},{1,0},{2,3},{3,2},{4,5},{5,4},{6,7},{7,6},{8,9},{9,8},{10,11... | collective-permute-start | bytes 20 | tf_op jit(solution)/shard_map/swap/ppermute | solution.py:158
  3.5 13.9 %collective-permute-start.4 = (bf16[1040,128]{1,0:T(8,128)(2,1)S(1)}, bf16[1040,128]{1,0:T(8,128)(2,1)S(1)}, u32[]{:S(2)}, u32[]{:S(2)}) collective-permute-start(bf16[1040,128]{1,0:T(8,128)(2,1)S(1)} %get-tuple-element.14.refs_0_), channel_id=1, source_target_pairs={{0,8},{8,0},{16,24},{24,16},{1,9},{9,1},{17,25},{25,17},{2,10},{10... | collective-permute-start | bytes 798728 | tf_op jit(solution)/shard_map/exchange/ppermute | solution.py:186
  6.5 11.5 %collective-permute-start.5 = (bf16[1040,128]{1,0:T(8,128)(2,1)S(1)}, bf16[1040,128]{1,0:T(8,128)(2,1)S(1)}, u32[]{:S(2)}, u32[]{:S(2)}) collective-permute-start(bf16[1040,128]{1,0:T(8,128)(2,1)S(1)} %get-tuple-element.14.refs_0_), channel_id=1, source_target_pairs={{0,16},{8,24},{16,0},{24,8},{1,17},{9,25},{17,1},{25,9},{2,18},{10... | collective-permute-start | bytes 798728 | tf_op jit(solution)/shard_map/exchange/ppermute | solution.py:186
  8.0 8.7 %collective-permute-start.12 = (bf16[528,128]{1,0:T(8,128)(2,1)S(1)}, bf16[528,128]{1,0:T(8,128)(2,1)S(1)}, u32[]{:S(2)}, u32[]{:S(2)}) collective-permute-start(bf16[528,128]{1,0:T(8,128)(2,1)S(1)} %get-tuple-element.13.q_ref), channel_id=1, source_target_pairs={{0,4},{1,5},{2,6},{3,7},{4,0},{5,1},{6,2},{7,3},{8,12},{9,13},{10,... | collective-permute-start | bytes 405512 | tf_op jit(solution)/shard_map/exchange/ppermute | solution.py:205
  16.8 6.4 %collective-permute-start.13 = (bf16[528,128]{1,0:T(8,128)(2,1)S(1)}, bf16[528,128]{1,0:T(8,128)(2,1)S(1)}, u32[]{:S(2)}, u32[]{:S(2)}) collective-permute-start(bf16[528,128]{1,0:T(8,128)(2,1)S(1)} %collective-permute-done.12.q_ref), channel_id=1, source_target_pairs={{0,2},{1,3},{2,0},{3,1},{4,6},{5,7},{6,4},{7,5},{8,10},{9,11},{10,... | collective-permute-start | bytes 405512 | tf_op jit(solution)/shard_map/exchange/ppermute | solution.py:205
  17.4 5.7 %collective-permute-start.6 = (bf16[528,128]{1,0:T(8,128)(2,1)S(1)}, bf16[528,128]{1,0:T(8,128)(2,1)S(1)}, u32[]{:S(2)}, u32[]{:S(2)}) collective-permute-start(bf16[528,128]{1,0:T(8,128)(2,1)S(1)} %slice.8), channel_id=1, source_target_pairs={{0,16},{8,24},{16,0},{24,8},{1,17},{9,25},{17,1},{25,9},{2,18},{10... | collective-permute-start | bytes 405512 | tf_op jit(solution)/shard_map/exchange/ppermute | solution.py:186
  18.0 5.1 %collective-permute-start.7 = (bf16[512,128]{1,0:T(8,128)(2,1)S(1)}, bf16[512,128]{1,0:T(8,128)(2,1)S(1)}, u32[]{:S(2)}, u32[]{:S(2)}) collective-permute-start(bf16[512,128]{1,0:T(8,128)(2,1)S(1)} %slice.9), channel_id=1, source_target_pairs={{0,8},{8,0},{16,24},{24,16},{1,9},{9,1},{17,25},{25,17},{2,10},{10... | collective-permute-start | bytes 393224 | tf_op jit(solution)/shard_map/exchange/ppermute | solution.py:186
  18.6 7.0 %collective-permute-start.9 = (bf16[528,128]{1,0:T(8,128)(2,1)S(1)}, bf16[528,128]{1,0:T(8,128)(2,1)S(1)}, u32[]{:S(2)}, u32[]{:S(2)}) collective-permute-start(bf16[528,128]{1,0:T(8,128)(2,1)S(1)} %get-tuple-element.13.q_ref), channel_id=1, source_target_pairs={{0,2},{1,3},{2,0},{3,1},{4,6},{5,7},{6,4},{7,5},{8,10},{9,11},{10,... | collective-permute-start | bytes 405512 | tf_op jit(solution)/shard_map/exchange/ppermute | solution.py:205
  24.3 7.2 %collective-permute-start.14 = (bf16[544,128]{1,0:T(8,128)(2,1)S(1)}, bf16[544,128]{1,0:T(8,128)(2,1)S(1)}, u32[]{:S(2)}, u32[]{:S(2)}) collective-permute-start(bf16[544,128]{1,0:T(8,128)(2,1)S(1)} %attend.7), channel_id=1, source_target_pairs={{0,2},{1,3},{2,0},{3,1},{4,6},{5,7},{6,4},{7,5},{8,10},{9,11},{10,... | collective-permute-start | bytes 417800 | tf_op jit(solution)/shard_map/return/ppermute | solution.py:256
  26.9 7.6 %collective-permute-start.10 = (bf16[272,128]{1,0:T(8,128)(2,1)S(1)}, bf16[272,128]{1,0:T(8,128)(2,1)S(1)}, u32[]{:S(2)}, u32[]{:S(2)}) collective-permute-start(bf16[272,128]{1,0:T(8,128)(2,1)S(1)} %get-tuple-element.17), channel_id=1, source_target_pairs={{0,2},{1,3},{2,0},{3,1},{4,6},{5,7},{6,4},{7,5},{8,10},{9,11},{10,... | collective-permute-start | bytes 208904 | tf_op jit(solution)/shard_map/return/ppermute | solution.py:254
  27.7 6.9 %collective-permute-start.11 = (bf16[272,128]{1,0:T(8,128)(2,1)S(1)}, bf16[272,128]{1,0:T(8,128)(2,1)S(1)}, u32[]{:S(2)}, u32[]{:S(2)}) collective-permute-start(bf16[272,128]{1,0:T(8,128)(2,1)S(1)} %get-tuple-element.18), channel_id=1, source_target_pairs={{0,3},{1,2},{2,1},{3,0},{4,7},{5,6},{6,5},{7,4},{8,11},{9,10},{10,... | collective-permute-start | bytes 208904 | tf_op jit(solution)/shard_map/return/ppermute | solution.py:254
  28.8 5.7 %collective-permute-start.8 = (bf16[272,128]{1,0:T(8,128)(2,1)S(1)}, bf16[272,128]{1,0:T(8,128)(2,1)S(1)}, u32[]{:S(2)}, u32[]{:S(2)}) collective-permute-start(bf16[272,128]{1,0:T(8,128)(2,1)S(1)} %get-tuple-element.16), channel_id=1, source_target_pairs={{0,1},{1,0},{2,3},{3,2},{4,5},{5,4},{6,7},{7,6},{8,9},{9,8},{10,11... | collective-permute-start | bytes 208904 | tf_op jit(solution)/shard_map/return/ppermute | solution.py:259
  31.6 6.8 %collective-permute-start.15 = (bf16[272,128]{1,0:T(8,128)(2,1)S(1)}, bf16[272,128]{1,0:T(8,128)(2,1)S(1)}, u32[]{:S(2)}, u32[]{:S(2)}) collective-permute-start(bf16[272,128]{1,0:T(8,128)(2,1)S(1)} %get-tuple-element.19), channel_id=1, source_target_pairs={{0,4},{1,5},{2,6},{3,7},{4,0},{5,1},{6,2},{7,3},{8,12},{9,13},{10,... | collective-permute-start | bytes 208904 | tf_op jit(solution)/shard_map/return/ppermute | solution.py:254
  34.5 6.8 %collective-permute-start.16 = (bf16[272,128]{1,0:T(8,128)(2,1)S(1)}, bf16[272,128]{1,0:T(8,128)(2,1)S(1)}, u32[]{:S(2)}, u32[]{:S(2)}) collective-permute-start(bf16[272,128]{1,0:T(8,128)(2,1)S(1)} %get-tuple-element.20), channel_id=1, source_target_pairs={{0,5},{1,4},{2,7},{3,6},{4,1},{5,0},{6,3},{7,2},{8,13},{9,12},{10,... | collective-permute-start | bytes 208904 | tf_op jit(solution)/shard_map/return/ppermute | solution.py:254

commit v6 on v5

--- a/solution.py
+++ b/solution.py
@@ -182,6 +182,9 @@
     def single(r):
         return r == low(r)
 
+    def after(a, b):
+        return lax.optimization_barrier((a, b))[0]
+
     def over(a, r):
         return lax.ppermute(a, "outer", [(o, o ^ r) for o in range(n_out)])
 
@@ -199,11 +202,9 @@
             if not single(r):
                 v_part[r] = over(v_part[r - low(r)], low(r))
         q_by = {0: q_piece}
-        bit = chips // 2
-        while bit:
-            for r in sorted(q_by):
-                q_by[r | bit] = lax.ppermute(q_by[r], "inner", along_inner(bit, 0))
-            bit //= 2
+        for r in reversed(range(1, chips)):
+            piece = after(q_piece, whole[1]) if r == 1 else q_piece
+            q_by[r] = lax.ppermute(piece, "inner", along_inner(r, 0))
     kv, where = [], []
     for r in range(n_out):
         if r in whole:
@@ -217,7 +218,8 @@
         rows = CORES * block if wide else block
         return (jax.ShapeDtypeStruct((rows, tok), BF16),) * (1 if wide else CORES)
 
-    def attend(r, wide):
+    def attend(r, wide, done=None):
+        q = q_by[r] if done is None else after(q_by[r], done)
         work = 4 * PER * both * n_out * both * size
         with jax.named_scope("attend"):
             return pl.pallas_call(
@@ -228,7 +230,7 @@
                 compiler_params=params,
                 cost_estimate=pl.CostEstimate(flops=work, bytes_accessed=2**20, transcendentals=work // (4 * size)),
                 name="attend",
-            )(q_by[r], *kv)
+            )(q, *kv)
 
     def add(arrays, wide):
         with jax.named_scope("add"):
@@ -243,20 +245,32 @@
 
     arrived = {r: [] for r in range(chips)}
     ends = []
-    for r in sorted(range(1, chips), key=lambda r: (low(r), -r)):
-        last = single(r)
-        alone = not (low(r) > 1)
-        parts = attend(r, not (last and alone))
-        if not alone:
-            parts = add([parts[0], *arrived[r]], not last)
+
+    def send(r, parts):
         with jax.named_scope("return"):
-            if last:
-                ends += [lax.ppermute(parts[x], "inner", along_inner(r, x)) for x in range(CORES)]
+            if single(r):
+                ends.extend(lax.ppermute(parts[x], "inner", along_inner(r, x)) for x in range(CORES))
             else:
                 arrived[r - low(r)].append(lax.ppermute(parts[0], "inner", along_inner(low(r), 0)))
-    own = attend(0, False)
+
+    done = q_by[2] if chips > 2 else None
+    partial = {}
+    for r in reversed(range(2, chips)):
+        partial[r] = attend(r, True, done)
+        done = partial[r][0]
+    own = attend(0, False, done)
+    for r in reversed(range(2, chips)):
+        parts = partial[r]
+        if arrived[r]:
+            parts = add([parts[0], *arrived[r]], not single(r))
+        done = parts[0]
+        send(r, parts)
     with jax.named_scope("return"):
-        ends = [own[0], lax.ppermute(own[1], "inner", along_inner(0, 1))] + ends
+        piece = own[1] if done is None else after(own[1], done)
+        across = lax.ppermute(piece, "inner", along_inner(0, 1))
+    if chips > 1:
+        send(1, attend(1, False, across))
+    ends = [own[0], across] + ends
     with jax.named_scope("combine"):
         return pl.pallas_call(
             functools.partial(combine_kernel, len(ends)),

time: 42.3 us -> 43 us (1.017)
  starting transfers between devices: 17.8 us -> 21.1 us
  waiting for transfers between devices: 16.2 us -> 13.4 us
    ppermute x9, waiting for transfers between devices: 16.2 us -> 12.3 us  [the longest x4 5.95 us: send(): lax.ppermute(parts[x], 'inner', along_inner(r, x))]
    ppermute x4, starting transfers between devices: 5.69 us -> 7.91 us  [over(): return lax.ppermute(a, 'outer', [(o, o ^ r) for o in range(n_out)])]
    ppermute x4, waiting for transfers between devices: 0.01 us -> 1.11 us  [over(): return lax.ppermute(a, 'outer', [(o, o ^ r) for o in range(n_out)])]
    ppermute x9, starting transfers between devices: 11.1 us -> 12.2 us  [the longest x4 5.66 us: send(): lax.ppermute(parts[x], 'inner', along_inner(r, x))]
  transfers between devices with their start and end apart: 17 -> 17, of which waited for: 4 -> 6; matrix products, arithmetic and copies ran while one was open for 3% -> 3% of each run, Pallas kernels for 11% -> 8%
where the time goes in v6:
time: 43 us; the launch traced here: 42.8 us
  starting transfers between devices  21.1 us (49%)
  waiting for transfers between devices  13.4 us (31%)
  Pallas kernels  6.35 us (15%)
  other arithmetic  1.06 us (2%)
  between operations  0.76 us (2%)
    ppermute x4, starting transfers between devices, over(): return lax.ppermute(a, 'outer', [(o, o ^ r) for o in range(n_out)])  7.91 us
    ppermute x4, waiting for transfers between devices, send(): lax.ppermute(parts[x], 'inner', along_inner(r, x))  5.95 us
    ppermute x4, starting transfers between devices, send(): lax.ppermute(parts[x], 'inner', along_inner(r, x))  5.66 us
    pallas_call x4, Pallas kernels, attend(): pl.pallas_call(functools.partial(attend_kernel, wide, tuple(where)), out_...  4.73 us
    ppermute x3, waiting for transfers between devices, shards(): q_by[r] = lax.ppermute(piece, 'inner', along_inner(r, 0))  4.34 us
    ppermute x3, starting transfers between devices, shards(): q_by[r] = lax.ppermute(piece, 'inner', along_inner(r, 0))  4.02 us
    ppermute x1, starting transfers between devices, send(): lax.ppermute(parts[0], 'inner', along_inner(low(r), 0))  2.45 us
    ppermute x1, waiting for transfers between devices, send(): lax.ppermute(parts[0], 'inner', along_inner(low(r), 0))  2.02 us
  transfers between devices with their start and end apart: 17, of which 6 were waited for; matrix products, arithmetic and copies ran while one was open for 3% of the time, Pallas kernels for 8%

profile of v6, /device:TPU:0, one launch (start us, length us, event | category | flops | bytes accessed | tf_op | source)
XLA Modules:
  0.0 42.8 jit_solution(2611477582609127634)
XLA Ops:
  0.0 0.5 %collective-permute-start.1 = (bf16[128,512]{1,0:T(8,128)(2,1)}, bf16[128,512]{1,0:T(8,128)(2,1)S(1)}, u32[]{:S(2)}, u32[]{:S(2)}) collective-permute-start(bf16[128,512]{1,0:T(8,128)(2,1)} %param.4), channel_id=1, source_target_pairs={{0,1},{1,0},{2,3},{3,2},{4,5},{5,4},{6,7},{7,6},{8,9},{9,8},{10,11... | collective-permute-start | bytes 393224 | tf_op jit(solution)/shard_map/swap/ppermute | solution.py:158
  0.5 0.1 collective-permute-start.2
  0.5 0.5 %collective-permute-start.3 = (bf16[128,512]{1,0:T(8,128)(2,1)}, bf16[128,512]{1,0:T(8,128)(2,1)S(1)}, u32[]{:S(2)}, u32[]{:S(2)}) collective-permute-start(bf16[128,512]{1,0:T(8,128)(2,1)} %param.6), channel_id=1, source_target_pairs={{0,1},{1,0},{2,3},{3,2},{4,5},{5,4},{6,7},{7,6},{8,9},{9,8},{10,11... | collective-permute-start | bytes 393224 | tf_op jit(solution)/shard_map/swap/ppermute | solution.py:158
  1.0 0.1 collective-permute-start
  1.7 1.1 %pad_maximum_fusion.own = bf16[384,512]{1,0:T(8,128)(2,1)S(1)} fusion(bf16[128,512]{1,0:T(8,128)(2,1)} %param.6, bf16[128,512]{1,0:T(8,128)(2,1)} %param.5, bf16[128,512]{1,0:T(8,128)(2,1)} %param.4), kind=kLoop, calls=%fused_computation | loop fusion | flops 1179648 | bytes 786432 | tf_op jit(solution)/shard_map/swap/concatenate | solution.py:159
  2.7 0.0 collective-permute-done.p1
  2.7 0.0 collective-permute-done.1.q1
  2.8 0.0 collective-permute-done.2.k1
  2.8 0.0 collective-permute-done.3.v1
  2.8 0.7 %merge.1 = (bf16[528,128]{1,0:T(8,128)(2,1)S(1)}, bf16[1040,128]{1,0:T(8,128)(2,1)S(1)}) custom-call(s32[1]{0:T(128)S(6)} %copy.5.p0, s32[1]{0:T(128)} %collective-permute-done.p1, bf16[384,512]{1,0:T(8,128)(2,1)S(1)} %pad_maximum_fusion.own, bf16[128,512]{1,0:T(8,128)(2,1)S(1)} %collective-permute-done.1.q1, ...), custom_call_target="tpu_custom_call" | custom-call | tf_op jit(solution)/shard_map/merge/merge/pallas_call | solution.py:162
  3.5 3.0 %collective-permute-start.6 = (bf16[1040,128]{1,0:T(8,128)(2,1)S(1)}, bf16[1040,128]{1,0:T(8,128)(2,1)S(1)}, u32[]{:S(2)}, u32[]{:S(2)}) collective-permute-start(bf16[1040,128]{1,0:T(8,128)(2,1)S(1)} %get-tuple-element.21.refs_0_), channel_id=1, source_target_pairs={{0,8},{8,0},{16,24},{24,16},{1,9},{9,1},{17,25},{25,17},{2,10},{10... | collective-permute-start | bytes 798728 | tf_op jit(solution)/shard_map/exchange/ppermute | solution.py:189
  6.5 1.5 %collective-permute-start.7 = (bf16[1040,128]{1,0:T(8,128)(2,1)S(1)}, bf16[1040,128]{1,0:T(8,128)(2,1)S(1)}, u32[]{:S(2)}, u32[]{:S(2)}) collective-permute-start(bf16[1040,128]{1,0:T(8,128)(2,1)S(1)} %get-tuple-element.21.refs_0_), channel_id=1, source_target_pairs={{0,16},{8,24},{16,0},{24,8},{1,17},{9,25},{17,1},{25,9},{2,18},{10... | collective-permute-start | bytes 798728 | tf_op jit(solution)/shard_map/exchange/ppermute | solution.py:189
  8.0 2.6 %collective-permute-start.4 = (bf16[528,128]{1,0:T(8,128)(2,1)S(1)}, bf16[528,128]{1,0:T(8,128)(2,1)S(1)}, u32[]{:S(2)}, u32[]{:S(2)}) collective-permute-start(bf16[528,128]{1,0:T(8,128)(2,1)S(1)} %get-tuple-element.29.q_ref), channel_id=1, source_target_pairs={{0,4},{1,5},{2,6},{3,7},{4,0},{5,1},{6,2},{7,3},{8,12},{9,13},{10,... | collective-permute-start | bytes 405512 | tf_op jit(solution)/shard_map/exchange/ppermute | solution.py:207
  10.6 1.3 %collective-permute-start.5 = (bf16[528,128]{1,0:T(8,128)(2,1)S(1)}, bf16[528,128]{1,0:T(8,128)(2,1)S(1)}, u32[]{:S(2)}, u32[]{:S(2)}) collective-permute-start(bf16[528,128]{1,0:T(8,128)(2,1)S(1)} %get-tuple-element.29.q_ref), channel_id=1, source_target_pairs={{0,6},{1,7},{2,4},{3,5},{4,2},{5,3},{6,0},{7,1},{8,14},{9,15},{10,... | collective-permute-start | bytes 405512 | tf_op jit(solution)/shard_map/exchange/ppermute | solution.py:207
  12.0 1.1 %collective-permute-done.6.refs_1_ = bf16[1040,128]{1,0:T(8,128)(2,1)S(1)} collective-permute-done((bf16[1040,128]{1,0:T(8,128)(2,1)S(1)}, bf16[1040,128]{1,0:T(8,128)(2,1)S(1)}, u32[]{:S(2)}, u32[]{:S(2)}) %collective-permute-start.6) | collective-permute-done | bytes 266272 | tf_op jit(solution)/shard_map/exchange/ppermute | solution.py:189
  13.1 1.8 %collective-permute-start.8 = (bf16[528,128]{1,0:T(8,128)(2,1)S(1)}, bf16[528,128]{1,0:T(8,128)(2,1)S(1)}, u32[]{:S(2)}, u32[]{:S(2)}) collective-permute-start(bf16[528,128]{1,0:T(8,128)(2,1)S(1)} %slice.8), channel_id=1, source_target_pairs={{0,16},{8,24},{16,0},{24,8},{1,17},{9,25},{17,1},{25,9},{2,18},{10... | collective-permute-start | bytes 405512 | tf_op jit(solution)/shard_map/exchange/ppermute | solution.py:189
  14.9 0.0 collective-permute-done.7.refs_2_
  14.9 1.6 %collective-permute-start.9 = (bf16[512,128]{1,0:T(8,128)(2,1)S(1)}, bf16[512,128]{1,0:T(8,128)(2,1)S(1)}, u32[]{:S(2)}, u32[]{:S(2)}) collective-permute-start(bf16[512,128]{1,0:T(8,128)(2,1)S(1)} %slice.9), channel_id=1, source_target_pairs={{0,8},{8,0},{16,24},{24,16},{1,9},{9,1},{17,25},{25,17},{2,10},{10... | collective-permute-start | bytes 393224 | tf_op jit(solution)/shard_map/exchange/ppermute | solution.py:189
  16.5 4.3 %collective-permute-done.4.q_ref = bf16[528,128]{1,0:T(8,128)(2,1)S(1)} collective-permute-done((bf16[528,128]{1,0:T(8,128)(2,1)S(1)}, bf16[528,128]{1,0:T(8,128)(2,1)S(1)}, u32[]{:S(2)}, u32[]{:S(2)}) %collective-permute-start.4) | collective-permute-done | bytes 135200 | tf_op jit(solution)/shard_map/exchange/ppermute | solution.py:207
  20.8 0.0 collective-permute-done.5.q_ref
  20.8 0.0 collective-permute-done.9.refs_4_
  20.8 0.0 collective-permute-done.8.refs_3_
  20.8 1.2 %attend.4 = bf16[544,128]{1,0:T(8,128)(2,1)S(1)} custom-call(bf16[528,128]{1,0:T(8,128)(2,1)S(1)} %collective-permute-done.5.q_ref, bf16[1040,128]{1,0:T(8,128)(2,1)S(1)} %get-tuple-element.21.refs_0_, bf16[1040,128]{1,0:T(8,128)(2,1)S(1)} %collective-permute-done.6.refs_1_, bf16[1040,128]{1,0:T(8,128)(2,1)S(1)} %collective-permute-done.7.refs_2_, ...), custom_call_target="tpu_custom_call" | custom-call | flops 268435456 | bytes 1048576 | tf_op jit(solution)/shard_map/attend/attend/pallas_call | solution.py:225
  22.0 2.5 %collective-permute-start.10 = (bf16[544,128]{1,0:T(8,128)(2,1)S(1)}, bf16[544,128]{1,0:T(8,128)(2,1)S(1)}, u32[]{:S(2)}, u32[]{:S(2)}) collective-permute-start(bf16[544,128]{1,0:T(8,128)(2,1)S(1)} %attend.4), channel_id=1, source_target_pairs={{0,2},{1,3},{2,0},{3,1},{4,6},{5,7},{6,4},{7,5},{8,10},{9,11},{10,... | collective-permute-start | bytes 417800 | tf_op jit(solution)/shard_map/return/ppermute | solution.py:254
  24.5 0.1 collective-permute-start.14
  24.6 1.2 %attend.5.refs_0_ = bf16[544,128]{1,0:T(8,128)(2,1)S(1)} custom-call(bf16[528,128]{1,0:T(8,128)(2,1)S(1)} %collective-permute-done.4.q_ref, bf16[1040,128]{1,0:T(8,128)(2,1)S(1)} %get-tuple-element.21.refs_0_, bf16[1040,128]{1,0:T(8,128)(2,1)S(1)} %collective-permute-done.6.refs_1_, bf16[1040,128]{1,0:T(8,128)(2,1)S(1)} %collective-permute-done.7.refs_2_, ...), custom_call_target="tpu_custom_call" | custom-call | flops 268435456 | bytes 1048576 | tf_op jit(solution)/shard_map/attend/attend/pallas_call | solution.py:225
  25.7 1.2 %attend.6 = (bf16[272,128]{1,0:T(8,128)(2,1)S(1)}, bf16[272,128]{1,0:T(8,128)(2,1)S(1)}) custom-call(bf16[528,128]{1,0:T(8,128)(2,1)S(1)} %get-tuple-element.29.q_ref, bf16[1040,128]{1,0:T(8,128)(2,1)S(1)} %get-tuple-element.21.refs_0_, bf16[1040,128]{1,0:T(8,128)(2,1)S(1)} %collective-permute-done.6.refs_1_, ...), custom_call_target="tpu_custom_call" | custom-call | flops 268435456 | bytes 1048576 | tf_op jit(solution)/shard_map/attend/attend/pallas_call | solution.py:225
  26.9 2.0 %collective-permute-done.10.refs_1_ = bf16[544,128]{1,0:T(8,128)(2,1)S(1)} collective-permute-done((bf16[544,128]{1,0:T(8,128)(2,1)S(1)}, bf16[544,128]{1,0:T(8,128)(2,1)S(1)}, u32[]{:S(2)}, u32[]{:S(2)}) %collective-permute-start.10) | collective-permute-done | bytes 139296 | tf_op jit(solution)/shard_map/return/ppermute | solution.py:254
  29.0 0.1 add.1
  29.0 0.1 collective-permute-start.11
  29.1 4.0 %collective-permute-start.12 = (bf16[272,128]{1,0:T(8,128)(2,1)S(1)}, bf16[272,128]{1,0:T(8,128)(2,1)S(1)}, u32[]{:S(2)}, u32[]{:S(2)}) collective-permute-start(bf16[272,128]{1,0:T(8,128)(2,1)S(1)} %get-tuple-element.26), channel_id=1, source_target_pairs={{0,4},{1,5},{2,6},{3,7},{4,0},{5,1},{6,2},{7,3},{8,12},{9,13},{10,... | collective-permute-start | bytes 208904 | tf_op jit(solution)/shard_map/return/ppermute | solution.py:252
  33.2 0.1 collective-permute-start.13
  33.2 0.0 collective-permute-done.14.q_ref
  33.2 0.0 collective-permute-done.11.refs_1_
  33.2 1.2 %attend.7 = (bf16[272,128]{1,0:T(8,128)(2,1)S(1)}, bf16[272,128]{1,0:T(8,128)(2,1)S(1)}) custom-call(bf16[528,128]{1,0:T(8,128)(2,1)S(1)} %collective-permute-done.14.q_ref, bf16[1040,128]{1,0:T(8,128)(2,1)S(1)} %get-tuple-element.21.refs_0_, bf16[1040,128]{1,0:T(8,128)(2,1)S(1)} %collective-permute-done.6.refs_1_, ...), custom_call_target="tpu_custom_call" | custom-call | flops 268435456 | bytes 1048576 | tf_op jit(solution)/shard_map/attend/attend/pallas_call | solution.py:225
  34.4 0.8 %collective-permute-start.15 = (bf16[272,128]{1,0:T(8,128)(2,1)S(1)}, bf16[272,128]{1,0:T(8,128)(2,1)S(1)}, u32[]{:S(2)}, u32[]{:S(2)}) collective-permute-start(bf16[272,128]{1,0:T(8,128)(2,1)S(1)} %get-tuple-element.31), channel_id=1, source_target_pairs={{0,2},{1,3},{2,0},{3,1},{4,6},{5,7},{6,4},{7,5},{8,10},{9,11},{10,... | collective-permute-start | bytes 208904 | tf_op jit(solution)/shard_map/return/ppermute | solution.py:252
  35.2 0.8 %collective-permute-start.16 = (bf16[272,128]{1,0:T(8,128)(2,1)S(1)}, bf16[272,128]{1,0:T(8,128)(2,1)S(1)}, u32[]{:S(2)}, u32[]{:S(2)}) collective-permute-start(bf16[272,128]{1,0:T(8,128)(2,1)S(1)} %get-tuple-element.32), channel_id=1, source_target_pairs={{0,3},{1,2},{2,1},{3,0},{4,7},{5,6},{6,5},{7,4},{8,11},{9,10},{10,... | collective-permute-start | bytes 208904 | tf_op jit(solution)/shard_map/return/ppermute | solution.py:252
  36.0 3.3 %collective-permute-done.12.refs_2_ = bf16[272,128]{1,0:T(8,128)(2,1)S(1)} collective-permute-done((bf16[272,128]{1,0:T(8,128)(2,1)S(1)}, bf16[272,128]{1,0:T(8,128)(2,1)S(1)}, u32[]{:S(2)}, u32[]{:S(2)}) %collective-permute-start.12) | collective-permute-done | bytes 69664 | tf_op jit(solution)/shard_map/return/ppermute | solution.py:252
  39.3 1.0 %collective-permute-done.13.refs_3_ = bf16[272,128]{1,0:T(8,128)(2,1)S(1)} collective-permute-done((bf16[272,128]{1,0:T(8,128)(2,1)S(1)}, bf16[272,128]{1,0:T(8,128)(2,1)S(1)}, u32[]{:S(2)}, u32[]{:S(2)}) %collective-permute-start.13) | collective-permute-done | bytes 69664 | tf_op jit(solution)/shard_map/return/ppermute | solution.py:252
  40.3 1.7 %collective-permute-done.15.refs_4_ = bf16[272,128]{1,0:T(8,128)(2,1)S(1)} collective-permute-done((bf16[272,128]{1,0:T(8,128)(2,1)S(1)}, bf16[272,128]{1,0:T(8,128)(2,1)S(1)}, u32[]{:S(2)}, u32[]{:S(2)}) %collective-permute-start.15) | collective-permute-done | bytes 69664 | tf_op jit(solution)/shard_map/return/ppermute | solution.py:252
  41.9 0.0 collective-permute-done.16.refs_5_
  41.9 0.8 %combine.1 = bf16[128,512]{1,0:T(8,128)(2,1)} custom-call(bf16[272,128]{1,0:T(8,128)(2,1)S(1)} %get-tuple-element.24.refs_0_, bf16[272,128]{1,0:T(8,128)(2,1)S(1)} %collective-permute-done.11.refs_1_, bf16[272,128]{1,0:T(8,128)(2,1)S(1)} %collective-permute-done.12.refs_2_, bf16[272,128]{1,0:T(8,128)(2,1)S(1)} %collective-permute-done.13.refs_3_, ...), custom_call_target="tpu_custom_call" | custom-call | tf_op jit(solution)/shard_map/combine/combine/pallas_call | solution.py:275
  (2 shorter events, 0.0 us)
Async XLA Ops:
  0.0 2.7 %collective-permute-start.1 = (bf16[128,512]{1,0:T(8,128)(2,1)}, bf16[128,512]{1,0:T(8,128)(2,1)S(1)}, u32[]{:S(2)}, u32[]{:S(2)}) collective-permute-start(bf16[128,512]{1,0:T(8,128)(2,1)} %param.4), channel_id=1, source_target_pairs={{0,1},{1,0},{2,3},{3,2},{4,5},{5,4},{6,7},{7,6},{8,9},{9,8},{10,11... | collective-permute-start | bytes 393224 | tf_op jit(solution)/shard_map/swap/ppermute | solution.py:158
  0.5 2.3 %collective-permute-start.2 = (bf16[128,512]{1,0:T(8,128)(2,1)}, bf16[128,512]{1,0:T(8,128)(2,1)S(1)}, u32[]{:S(2)}, u32[]{:S(2)}) collective-permute-start(bf16[128,512]{1,0:T(8,128)(2,1)} %param.5), channel_id=1, source_target_pairs={{0,1},{1,0},{2,3},{3,2},{4,5},{5,4},{6,7},{7,6},{8,9},{9,8},{10,11... | collective-permute-start | bytes 393224 | tf_op jit(solution)/shard_map/swap/ppermute | solution.py:158
  0.5 2.3 %collective-permute-start.3 = (bf16[128,512]{1,0:T(8,128)(2,1)}, bf16[128,512]{1,0:T(8,128)(2,1)S(1)}, u32[]{:S(2)}, u32[]{:S(2)}) collective-permute-start(bf16[128,512]{1,0:T(8,128)(2,1)} %param.6), channel_id=1, source_target_pairs={{0,1},{1,0},{2,3},{3,2},{4,5},{5,4},{6,7},{7,6},{8,9},{9,8},{10,11... | collective-permute-start | bytes 393224 | tf_op jit(solution)/shard_map/swap/ppermute | solution.py:158
  1.0 1.8 %collective-permute-start = (s32[1]{0:T(128)}, s32[1]{0:T(128)}, u32[]{:S(2)}, u32[]{:S(2)}) collective-permute-start(s32[1]{0:T(128)} %param.7), channel_id=1, source_target_pairs={{0,1},{1,0},{2,3},{3,2},{4,5},{5,4},{6,7},{7,6},{8,9},{9,8},{10,11... | collective-permute-start | bytes 20 | tf_op jit(solution)/shard_map/swap/ppermute | solution.py:158
  3.5 9.6 %collective-permute-start.6 = (bf16[1040,128]{1,0:T(8,128)(2,1)S(1)}, bf16[1040,128]{1,0:T(8,128)(2,1)S(1)}, u32[]{:S(2)}, u32[]{:S(2)}) collective-permute-start(bf16[1040,128]{1,0:T(8,128)(2,1)S(1)} %get-tuple-element.21.refs_0_), channel_id=1, source_target_pairs={{0,8},{8,0},{16,24},{24,16},{1,9},{9,1},{17,25},{25,17},{2,10},{10... | collective-permute-start | bytes 798728 | tf_op jit(solution)/shard_map/exchange/ppermute | solution.py:189
  6.5 8.4 %collective-permute-start.7 = (bf16[1040,128]{1,0:T(8,128)(2,1)S(1)}, bf16[1040,128]{1,0:T(8,128)(2,1)S(1)}, u32[]{:S(2)}, u32[]{:S(2)}) collective-permute-start(bf16[1040,128]{1,0:T(8,128)(2,1)S(1)} %get-tuple-element.21.refs_0_), channel_id=1, source_target_pairs={{0,16},{8,24},{16,0},{24,8},{1,17},{9,25},{17,1},{25,9},{2,18},{10... | collective-permute-start | bytes 798728 | tf_op jit(solution)/shard_map/exchange/ppermute | solution.py:189
  8.0 12.8 %collective-permute-start.4 = (bf16[528,128]{1,0:T(8,128)(2,1)S(1)}, bf16[528,128]{1,0:T(8,128)(2,1)S(1)}, u32[]{:S(2)}, u32[]{:S(2)}) collective-permute-start(bf16[528,128]{1,0:T(8,128)(2,1)S(1)} %get-tuple-element.29.q_ref), channel_id=1, source_target_pairs={{0,4},{1,5},{2,6},{3,7},{4,0},{5,1},{6,2},{7,3},{8,12},{9,13},{10,... | collective-permute-start | bytes 405512 | tf_op jit(solution)/shard_map/exchange/ppermute | solution.py:207
  10.6 10.2 %collective-permute-start.5 = (bf16[528,128]{1,0:T(8,128)(2,1)S(1)}, bf16[528,128]{1,0:T(8,128)(2,1)S(1)}, u32[]{:S(2)}, u32[]{:S(2)}) collective-permute-start(bf16[528,128]{1,0:T(8,128)(2,1)S(1)} %get-tuple-element.29.q_ref), channel_id=1, source_target_pairs={{0,6},{1,7},{2,4},{3,5},{4,2},{5,3},{6,0},{7,1},{8,14},{9,15},{10,... | collective-permute-start | bytes 405512 | tf_op jit(solution)/shard_map/exchange/ppermute | solution.py:207
  13.1 7.8 %collective-permute-start.8 = (bf16[528,128]{1,0:T(8,128)(2,1)S(1)}, bf16[528,128]{1,0:T(8,128)(2,1)S(1)}, u32[]{:S(2)}, u32[]{:S(2)}) collective-permute-start(bf16[528,128]{1,0:T(8,128)(2,1)S(1)} %slice.8), channel_id=1, source_target_pairs={{0,16},{8,24},{16,0},{24,8},{1,17},{9,25},{17,1},{25,9},{2,18},{10... | collective-permute-start | bytes 405512 | tf_op jit(solution)/shard_map/exchange/ppermute | solution.py:189
  14.9 5.9 %collective-permute-start.9 = (bf16[512,128]{1,0:T(8,128)(2,1)S(1)}, bf16[512,128]{1,0:T(8,128)(2,1)S(1)}, u32[]{:S(2)}, u32[]{:S(2)}) collective-permute-start(bf16[512,128]{1,0:T(8,128)(2,1)S(1)} %slice.9), channel_id=1, source_target_pairs={{0,8},{8,0},{16,24},{24,16},{1,9},{9,1},{17,25},{25,17},{2,10},{10... | collective-permute-start | bytes 393224 | tf_op jit(solution)/shard_map/exchange/ppermute | solution.py:189
  22.0 6.9 %collective-permute-start.10 = (bf16[544,128]{1,0:T(8,128)(2,1)S(1)}, bf16[544,128]{1,0:T(8,128)(2,1)S(1)}, u32[]{:S(2)}, u32[]{:S(2)}) collective-permute-start(bf16[544,128]{1,0:T(8,128)(2,1)S(1)} %attend.4), channel_id=1, source_target_pairs={{0,2},{1,3},{2,0},{3,1},{4,6},{5,7},{6,4},{7,5},{8,10},{9,11},{10,... | collective-permute-start | bytes 417800 | tf_op jit(solution)/shard_map/return/ppermute | solution.py:254
  24.5 8.7 %collective-permute-start.14 = (bf16[528,128]{1,0:T(8,128)(2,1)S(1)}, bf16[528,128]{1,0:T(8,128)(2,1)S(1)}, u32[]{:S(2)}, u32[]{:S(2)}) collective-permute-start(bf16[528,128]{1,0:T(8,128)(2,1)S(1)} %get-tuple-element.29.q_ref), channel_id=1, source_target_pairs={{0,2},{1,3},{2,0},{3,1},{4,6},{5,7},{6,4},{7,5},{8,10},{9,11},{10,... | collective-permute-start | bytes 405512 | tf_op jit(solution)/shard_map/exchange/ppermute | solution.py:207
  29.0 4.2 %collective-permute-start.11 = (bf16[272,128]{1,0:T(8,128)(2,1)S(1)}, bf16[272,128]{1,0:T(8,128)(2,1)S(1)}, u32[]{:S(2)}, u32[]{:S(2)}) collective-permute-start(bf16[272,128]{1,0:T(8,128)(2,1)S(1)} %get-tuple-element.27), channel_id=1, source_target_pairs={{0,1},{1,0},{2,3},{3,2},{4,5},{5,4},{6,7},{7,6},{8,9},{9,8},{10,11... | collective-permute-start | bytes 208904 | tf_op jit(solution)/shard_map/return/ppermute | solution.py:270
  29.1 10.1 %collective-permute-start.12 = (bf16[272,128]{1,0:T(8,128)(2,1)S(1)}, bf16[272,128]{1,0:T(8,128)(2,1)S(1)}, u32[]{:S(2)}, u32[]{:S(2)}) collective-permute-start(bf16[272,128]{1,0:T(8,128)(2,1)S(1)} %get-tuple-element.26), channel_id=1, source_target_pairs={{0,4},{1,5},{2,6},{3,7},{4,0},{5,1},{6,2},{7,3},{8,12},{9,13},{10,... | collective-permute-start | bytes 208904 | tf_op jit(solution)/shard_map/return/ppermute | solution.py:252
  33.2 7.1 %collective-permute-start.13 = (bf16[272,128]{1,0:T(8,128)(2,1)S(1)}, bf16[272,128]{1,0:T(8,128)(2,1)S(1)}, u32[]{:S(2)}, u32[]{:S(2)}) collective-permute-start(bf16[272,128]{1,0:T(8,128)(2,1)S(1)} %get-tuple-element.28), channel_id=1, source_target_pairs={{0,5},{1,4},{2,7},{3,6},{4,1},{5,0},{6,3},{7,2},{8,13},{9,12},{10,... | collective-permute-start | bytes 208904 | tf_op jit(solution)/shard_map/return/ppermute | solution.py:252
  34.4 7.5 %collective-permute-start.15 = (bf16[272,128]{1,0:T(8,128)(2,1)S(1)}, bf16[272,128]{1,0:T(8,128)(2,1)S(1)}, u32[]{:S(2)}, u32[]{:S(2)}) collective-permute-start(bf16[272,128]{1,0:T(8,128)(2,1)S(1)} %get-tuple-element.31), channel_id=1, source_target_pairs={{0,2},{1,3},{2,0},{3,1},{4,6},{5,7},{6,4},{7,5},{8,10},{9,11},{10,... | collective-permute-start | bytes 208904 | tf_op jit(solution)/shard_map/return/ppermute | solution.py:252
  35.2 6.7 %collective-permute-start.16 = (bf16[272,128]{1,0:T(8,128)(2,1)S(1)}, bf16[272,128]{1,0:T(8,128)(2,1)S(1)}, u32[]{:S(2)}, u32[]{:S(2)}) collective-permute-start(bf16[272,128]{1,0:T(8,128)(2,1)S(1)} %get-tuple-element.32), channel_id=1, source_target_pairs={{0,3},{1,2},{2,1},{3,0},{4,7},{5,6},{6,5},{7,4},{8,11},{9,10},{10,... | collective-permute-start | bytes 208904 | tf_op jit(solution)/shard_map/return/ppermute | solution.py:252

commit v7 on v6

--- a/solution.py
+++ b/solution.py
@@ -176,43 +176,19 @@
     def low(r):
         return r & -r
 
-    def high(r):
-        return 1 << (r.bit_length() - 1)
-
     def single(r):
         return r == low(r)
 
     def after(a, b):
         return lax.optimization_barrier((a, b))[0]
 
-    def over(a, r):
-        return lax.ppermute(a, "outer", [(o, o ^ r) for o in range(n_out)])
-
     with jax.named_scope("exchange"):
-        whole = {0: kv_piece}
-        for r in range(1, n_out):
-            if single(r):
-                whole[r] = over(kv_piece, r)
-        k_part = {r: a[:half, :] for r, a in whole.items() if r}
-        v_part = {r: a[half:, :] for r, a in whole.items() if r}
-        for r in range(1, n_out):
-            if not single(r):
-                k_part[r] = over(k_part[r - high(r)], high(r))
-        for r in sorted(range(1, n_out), key=lambda r: r.bit_count()):
-            if not single(r):
-                v_part[r] = over(v_part[r - low(r)], low(r))
+        kv = [kv_piece] + [lax.ppermute(kv_piece, "outer", [(o, o ^ r) for o in range(n_out)]) for r in range(1, n_out)]
         q_by = {0: q_piece}
         for r in reversed(range(1, chips)):
-            piece = after(q_piece, whole[1]) if r == 1 else q_piece
+            piece = after(q_piece, kv[1]) if r == 1 else q_piece
             q_by[r] = lax.ppermute(piece, "inner", along_inner(r, 0))
-    kv, where = [], []
-    for r in range(n_out):
-        if r in whole:
-            where.append((len(kv), 0, len(kv), half))
-            kv.append(whole[r])
-        else:
-            where.append((len(kv), 0, len(kv) + 1, 0))
-            kv += [k_part[r], v_part[r]]
+    where = tuple((r, 0, r, half) for r in range(n_out))
 
     def shapes(wide):
         rows = CORES * block if wide else block
@@ -223,7 +199,7 @@
         work = 4 * PER * both * n_out * both * size
         with jax.named_scope("attend"):
             return pl.pallas_call(
-                functools.partial(attend_kernel, wide, tuple(where)),
+                functools.partial(attend_kernel, wide, where),
                 out_shape=shapes(wide),
                 in_specs=vmem(1 + len(kv)),
                 out_specs=tuple(vmem(len(shapes(wide)))),
@@ -253,7 +229,7 @@
             else:
                 arrived[r - low(r)].append(lax.ppermute(parts[0], "inner", along_inner(low(r), 0)))
 
-    done = q_by[2] if chips > 2 else None
+    done = (q_by[2], q_by[1]) if chips > 2 else None
     partial = {}
     for r in reversed(range(2, chips)):
         partial[r] = attend(r, True, done)

time: 43 us -> 41.9 us (0.974)
  starting transfers between devices: 21.1 us -> 19.1 us
  waiting for transfers between devices: 13.4 us -> 14.4 us
    ppermute x4 -> x3, starting transfers between devices: 7.91 us -> 4.54 us  [shards(): lax.ppermute(kv_piece, 'outer', [(o, o ^ r) for o in range(n_out)])]
    ppermute x3, starting transfers between devices: 4.02 us -> 6.54 us  [shards(): q_by[r] = lax.ppermute(piece, 'inner', along_inner(r, 0))]
    ppermute x3, waiting for transfers between devices: 4.34 us -> 6.11 us  [shards(): q_by[r] = lax.ppermute(piece, 'inner', along_inner(r, 0))]
    ppermute x1, starting transfers between devices: 2.45 us -> 1.57 us  [send(): lax.ppermute(parts[0], 'inner', along_inner(low(r), 0))]
    ppermute x1, waiting for transfers between devices: 2.02 us -> 1.47 us  [send(): lax.ppermute(parts[0], 'inner', along_inner(low(r), 0))]
    ppermute x4, waiting for transfers between devices: 5.95 us -> 5.51 us  [send(): lax.ppermute(parts[x], 'inner', along_inner(r, x))]
    ppermute x4 -> x3, waiting for transfers between devices: 1.11 us -> 1.27 us  [shards(): lax.ppermute(kv_piece, 'outer', [(o, o ^ r) for o in range(n_out)])]
  transfers between devices with their start and end apart: 17 -> 16, of which waited for: 6 -> 8; matrix products, arithmetic and copies ran while one was open for 3% -> 3% of each run, Pallas kernels for 8% -> 8%
where the time goes in v7:
time: 41.9 us; the launch traced here: 41.8 us
  starting transfers between devices  19.1 us (46%)
  waiting for transfers between devices  14.4 us (34%)
  Pallas kernels  6.48 us (15%)
  other arithmetic  1.06 us (3%)
  between operations  0.75 us (2%)
    ppermute x3, starting transfers between devices, shards(): q_by[r] = lax.ppermute(piece, 'inner', along_inner(r, 0))  6.54 us
    ppermute x3, waiting for transfers between devices, shards(): q_by[r] = lax.ppermute(piece, 'inner', along_inner(r, 0))  6.11 us
    ppermute x4, waiting for transfers between devices, send(): lax.ppermute(parts[x], 'inner', along_inner(r, x))  5.51 us
    ppermute x4, starting transfers between devices, send(): lax.ppermute(parts[x], 'inner', along_inner(r, x))  5.35 us
    pallas_call x4, Pallas kernels, attend(): pl.pallas_call(functools.partial(attend_kernel, wide, where), out_shape=s...  4.72 us
    ppermute x3, starting transfers between devices, shards(): lax.ppermute(kv_piece, 'outer', [(o, o ^ r) for o in range(n_out)])  4.54 us
    ppermute x1, starting transfers between devices, send(): lax.ppermute(parts[0], 'inner', along_inner(low(r), 0))  1.57 us
    ppermute x1, waiting for transfers between devices, send(): lax.ppermute(parts[0], 'inner', along_inner(low(r), 0))  1.47 us
  transfers between devices with their start and end apart: 16, of which 8 were waited for; matrix products, arithmetic and copies ran while one was open for 3% of the time, Pallas kernels for 8%

profile of v7, /device:TPU:0, one launch (start us, length us, event | category | flops | bytes accessed | tf_op | source)
XLA Modules:
  0.0 41.8 jit_solution(5748361434465576500)
XLA Ops:
  0.0 0.5 %collective-permute-start.1 = (bf16[128,512]{1,0:T(8,128)(2,1)}, bf16[128,512]{1,0:T(8,128)(2,1)S(1)}, u32[]{:S(2)}, u32[]{:S(2)}) collective-permute-start(bf16[128,512]{1,0:T(8,128)(2,1)} %param.4), channel_id=1, source_target_pairs={{0,1},{1,0},{2,3},{3,2},{4,5},{5,4},{6,7},{7,6},{8,9},{9,8},{10,11... | collective-permute-start | bytes 393224 | tf_op jit(solution)/shard_map/swap/ppermute | solution.py:158
  0.5 0.1 collective-permute-start.2
  0.5 0.5 %collective-permute-start.3 = (bf16[128,512]{1,0:T(8,128)(2,1)}, bf16[128,512]{1,0:T(8,128)(2,1)S(1)}, u32[]{:S(2)}, u32[]{:S(2)}) collective-permute-start(bf16[128,512]{1,0:T(8,128)(2,1)} %param.6), channel_id=1, source_target_pairs={{0,1},{1,0},{2,3},{3,2},{4,5},{5,4},{6,7},{7,6},{8,9},{9,8},{10,11... | collective-permute-start | bytes 393224 | tf_op jit(solution)/shard_map/swap/ppermute | solution.py:158
  1.0 0.1 collective-permute-start
  1.7 1.1 %pad_maximum_fusion.own = bf16[384,512]{1,0:T(8,128)(2,1)S(1)} fusion(bf16[128,512]{1,0:T(8,128)(2,1)} %param.6, bf16[128,512]{1,0:T(8,128)(2,1)} %param.5, bf16[128,512]{1,0:T(8,128)(2,1)} %param.4), kind=kLoop, calls=%fused_computation | loop fusion | flops 1179648 | bytes 786432 | tf_op jit(solution)/shard_map/swap/concatenate | solution.py:159
  2.7 0.0 collective-permute-done.p1
  2.7 0.0 collective-permute-done.1.q1
  2.8 0.0 collective-permute-done.2.k1
  2.8 0.0 collective-permute-done.3.v1
  2.8 0.8 %merge.1 = (bf16[528,128]{1,0:T(8,128)(2,1)S(1)}, bf16[1040,128]{1,0:T(8,128)(2,1)S(1)}) custom-call(s32[1]{0:T(128)S(6)} %copy.5.p0, s32[1]{0:T(128)} %collective-permute-done.p1, bf16[384,512]{1,0:T(8,128)(2,1)S(1)} %pad_maximum_fusion.own, bf16[128,512]{1,0:T(8,128)(2,1)S(1)} %collective-permute-done.1.q1, ...), custom_call_target="tpu_custom_call" | custom-call | tf_op jit(solution)/shard_map/merge/merge/pallas_call | solution.py:162
  3.6 3.0 %collective-permute-start.6 = (bf16[1040,128]{1,0:T(8,128)(2,1)S(1)}, bf16[1040,128]{1,0:T(8,128)(2,1)S(1)}, u32[]{:S(2)}, u32[]{:S(2)}) collective-permute-start(bf16[1040,128]{1,0:T(8,128)(2,1)S(1)} %get-tuple-element.20.refs_0_), channel_id=1, source_target_pairs={{0,8},{8,0},{16,24},{24,16},{1,9},{9,1},{17,25},{25,17},{2,10},{10... | collective-permute-start | bytes 798728 | tf_op jit(solution)/shard_map/exchange/ppermute | solution.py:186
  6.6 1.5 %collective-permute-start.8 = (bf16[1040,128]{1,0:T(8,128)(2,1)S(1)}, bf16[1040,128]{1,0:T(8,128)(2,1)S(1)}, u32[]{:S(2)}, u32[]{:S(2)}) collective-permute-start(bf16[1040,128]{1,0:T(8,128)(2,1)S(1)} %get-tuple-element.20.refs_0_), channel_id=1, source_target_pairs={{0,16},{8,24},{16,0},{24,8},{1,17},{9,25},{17,1},{25,9},{2,18},{10... | collective-permute-start | bytes 798728 | tf_op jit(solution)/shard_map/exchange/ppermute | solution.py:186
  8.2 0.0 collective-permute-start.9
  8.2 3.0 %collective-permute-start.4 = (bf16[528,128]{1,0:T(8,128)(2,1)S(1)}, bf16[528,128]{1,0:T(8,128)(2,1)S(1)}, u32[]{:S(2)}, u32[]{:S(2)}) collective-permute-start(bf16[528,128]{1,0:T(8,128)(2,1)S(1)} %get-tuple-element.24.q_ref), channel_id=1, source_target_pairs={{0,4},{1,5},{2,6},{3,7},{4,0},{5,1},{6,2},{7,3},{8,12},{9,13},{10,... | collective-permute-start | bytes 405512 | tf_op jit(solution)/shard_map/exchange/ppermute | solution.py:190
  11.2 1.3 %collective-permute-start.5 = (bf16[528,128]{1,0:T(8,128)(2,1)S(1)}, bf16[528,128]{1,0:T(8,128)(2,1)S(1)}, u32[]{:S(2)}, u32[]{:S(2)}) collective-permute-start(bf16[528,128]{1,0:T(8,128)(2,1)S(1)} %get-tuple-element.24.q_ref), channel_id=1, source_target_pairs={{0,6},{1,7},{2,4},{3,5},{4,2},{5,3},{6,0},{7,1},{8,14},{9,15},{10,... | collective-permute-start | bytes 405512 | tf_op jit(solution)/shard_map/exchange/ppermute | solution.py:190
  12.6 1.3 %collective-permute-done.6.refs_1_ = bf16[1040,128]{1,0:T(8,128)(2,1)S(1)} collective-permute-done((bf16[1040,128]{1,0:T(8,128)(2,1)S(1)}, bf16[1040,128]{1,0:T(8,128)(2,1)S(1)}, u32[]{:S(2)}, u32[]{:S(2)}) %collective-permute-start.6) | collective-permute-done | bytes 266272 | tf_op jit(solution)/shard_map/exchange/ppermute | solution.py:186
  13.8 2.1 %collective-permute-start.7 = (bf16[528,128]{1,0:T(8,128)(2,1)S(1)}, bf16[528,128]{1,0:T(8,128)(2,1)S(1)}, u32[]{:S(2)}, u32[]{:S(2)}) collective-permute-start(bf16[528,128]{1,0:T(8,128)(2,1)S(1)} %get-tuple-element.24.q_ref), channel_id=1, source_target_pairs={{0,2},{1,3},{2,0},{3,1},{4,6},{5,7},{6,4},{7,5},{8,10},{9,11},{10,... | collective-permute-start | bytes 405512 | tf_op jit(solution)/shard_map/exchange/ppermute | solution.py:190
  16.0 5.2 %collective-permute-done.4.q_ref = bf16[528,128]{1,0:T(8,128)(2,1)S(1)} collective-permute-done((bf16[528,128]{1,0:T(8,128)(2,1)S(1)}, bf16[528,128]{1,0:T(8,128)(2,1)S(1)}, u32[]{:S(2)}, u32[]{:S(2)}) %collective-permute-start.4) | collective-permute-done | bytes 135200 | tf_op jit(solution)/shard_map/exchange/ppermute | solution.py:190
  21.2 0.0 collective-permute-done.5.q_ref
  21.2 0.9 %collective-permute-done.7.q_ref = bf16[528,128]{1,0:T(8,128)(2,1)S(1)} collective-permute-done((bf16[528,128]{1,0:T(8,128)(2,1)S(1)}, bf16[528,128]{1,0:T(8,128)(2,1)S(1)}, u32[]{:S(2)}, u32[]{:S(2)}) %collective-permute-start.7) | collective-permute-done | bytes 135200 | tf_op jit(solution)/shard_map/exchange/ppermute | solution.py:190
  22.1 0.0 collective-permute-done.8.refs_2_
  22.1 0.0 collective-permute-done.9.refs_3_
  22.1 1.2 %attend.4 = bf16[544,128]{1,0:T(8,128)(2,1)S(1)} custom-call(bf16[528,128]{1,0:T(8,128)(2,1)S(1)} %collective-permute-done.5.q_ref, bf16[1040,128]{1,0:T(8,128)(2,1)S(1)} %get-tuple-element.20.refs_0_, bf16[1040,128]{1,0:T(8,128)(2,1)S(1)} %collective-permute-done.6.refs_1_, bf16[1040,128]{1,0:T(8,128)(2,1)S(1)} %collective-permute-done.8.refs_2_, ...), custom_call_target="tpu_custom_call" | custom-call | flops 268435456 | bytes 1048576 | tf_op jit(solution)/shard_map/attend/attend/pallas_call | solution.py:201
  23.3 1.6 %collective-permute-start.10 = (bf16[544,128]{1,0:T(8,128)(2,1)S(1)}, bf16[544,128]{1,0:T(8,128)(2,1)S(1)}, u32[]{:S(2)}, u32[]{:S(2)}) collective-permute-start(bf16[544,128]{1,0:T(8,128)(2,1)S(1)} %attend.4), channel_id=1, source_target_pairs={{0,2},{1,3},{2,0},{3,1},{4,6},{5,7},{6,4},{7,5},{8,10},{9,11},{10,... | collective-permute-start | bytes 417800 | tf_op jit(solution)/shard_map/return/ppermute | solution.py:230
  24.9 1.2 %attend.5.refs_0_ = bf16[544,128]{1,0:T(8,128)(2,1)S(1)} custom-call(bf16[528,128]{1,0:T(8,128)(2,1)S(1)} %collective-permute-done.4.q_ref, bf16[1040,128]{1,0:T(8,128)(2,1)S(1)} %get-tuple-element.20.refs_0_, bf16[1040,128]{1,0:T(8,128)(2,1)S(1)} %collective-permute-done.6.refs_1_, bf16[1040,128]{1,0:T(8,128)(2,1)S(1)} %collective-permute-done.8.refs_2_, ...), custom_call_target="tpu_custom_call" | custom-call | flops 268435456 | bytes 1048576 | tf_op jit(solution)/shard_map/attend/attend/pallas_call | solution.py:201
  26.0 1.2 %attend.6 = (bf16[272,128]{1,0:T(8,128)(2,1)S(1)}, bf16[272,128]{1,0:T(8,128)(2,1)S(1)}) custom-call(bf16[528,128]{1,0:T(8,128)(2,1)S(1)} %get-tuple-element.24.q_ref, bf16[1040,128]{1,0:T(8,128)(2,1)S(1)} %get-tuple-element.20.refs_0_, bf16[1040,128]{1,0:T(8,128)(2,1)S(1)} %collective-permute-done.6.refs_1_, ...), custom_call_target="tpu_custom_call" | custom-call | flops 268435456 | bytes 1048576 | tf_op jit(solution)/shard_map/attend/attend/pallas_call | solution.py:201
  27.2 1.5 %collective-permute-done.10.refs_1_ = bf16[544,128]{1,0:T(8,128)(2,1)S(1)} collective-permute-done((bf16[544,128]{1,0:T(8,128)(2,1)S(1)}, bf16[544,128]{1,0:T(8,128)(2,1)S(1)}, u32[]{:S(2)}, u32[]{:S(2)}) %collective-permute-start.10) | collective-permute-done | bytes 139296 | tf_op jit(solution)/shard_map/return/ppermute | solution.py:230
  28.7 0.1 add.1
  28.8 0.1 collective-permute-start.11
  28.9 3.7 %collective-permute-start.12 = (bf16[272,128]{1,0:T(8,128)(2,1)S(1)}, bf16[272,128]{1,0:T(8,128)(2,1)S(1)}, u32[]{:S(2)}, u32[]{:S(2)}) collective-permute-start(bf16[272,128]{1,0:T(8,128)(2,1)S(1)} %get-tuple-element.27), channel_id=1, source_target_pairs={{0,4},{1,5},{2,6},{3,7},{4,0},{5,1},{6,2},{7,3},{8,12},{9,13},{10,... | collective-permute-start | bytes 208904 | tf_op jit(solution)/shard_map/return/ppermute | solution.py:228
  32.6 0.1 collective-permute-start.13
  32.7 0.0 collective-permute-done.11.refs_1_
  32.7 1.2 %attend.7 = (bf16[272,128]{1,0:T(8,128)(2,1)S(1)}, bf16[272,128]{1,0:T(8,128)(2,1)S(1)}) custom-call(bf16[528,128]{1,0:T(8,128)(2,1)S(1)} %collective-permute-done.7.q_ref, bf16[1040,128]{1,0:T(8,128)(2,1)S(1)} %get-tuple-element.20.refs_0_, bf16[1040,128]{1,0:T(8,128)(2,1)S(1)} %collective-permute-done.6.refs_1_, ...), custom_call_target="tpu_custom_call" | custom-call | flops 268435456 | bytes 1048576 | tf_op jit(solution)/shard_map/attend/attend/pallas_call | solution.py:201
  33.9 0.8 %collective-permute-start.14 = (bf16[272,128]{1,0:T(8,128)(2,1)S(1)}, bf16[272,128]{1,0:T(8,128)(2,1)S(1)}, u32[]{:S(2)}, u32[]{:S(2)}) collective-permute-start(bf16[272,128]{1,0:T(8,128)(2,1)S(1)} %get-tuple-element.31), channel_id=1, source_target_pairs={{0,2},{1,3},{2,0},{3,1},{4,6},{5,7},{6,4},{7,5},{8,10},{9,11},{10,... | collective-permute-start | bytes 208904 | tf_op jit(solution)/shard_map/return/ppermute | solution.py:228
  34.6 0.8 %collective-permute-start.15 = (bf16[272,128]{1,0:T(8,128)(2,1)S(1)}, bf16[272,128]{1,0:T(8,128)(2,1)S(1)}, u32[]{:S(2)}, u32[]{:S(2)}) collective-permute-start(bf16[272,128]{1,0:T(8,128)(2,1)S(1)} %get-tuple-element.32), channel_id=1, source_target_pairs={{0,3},{1,2},{2,1},{3,0},{4,7},{5,6},{6,5},{7,4},{8,11},{9,10},{10,... | collective-permute-start | bytes 208904 | tf_op jit(solution)/shard_map/return/ppermute | solution.py:228
  35.4 3.3 %collective-permute-done.12.refs_2_ = bf16[272,128]{1,0:T(8,128)(2,1)S(1)} collective-permute-done((bf16[272,128]{1,0:T(8,128)(2,1)S(1)}, bf16[272,128]{1,0:T(8,128)(2,1)S(1)}, u32[]{:S(2)}, u32[]{:S(2)}) %collective-permute-start.12) | collective-permute-done | bytes 69664 | tf_op jit(solution)/shard_map/return/ppermute | solution.py:228
  38.7 1.0 %collective-permute-done.13.refs_3_ = bf16[272,128]{1,0:T(8,128)(2,1)S(1)} collective-permute-done((bf16[272,128]{1,0:T(8,128)(2,1)S(1)}, bf16[272,128]{1,0:T(8,128)(2,1)S(1)}, u32[]{:S(2)}, u32[]{:S(2)}) %collective-permute-start.13) | collective-permute-done | bytes 69664 | tf_op jit(solution)/shard_map/return/ppermute | solution.py:228
  39.7 1.0 %collective-permute-done.14.refs_4_ = bf16[272,128]{1,0:T(8,128)(2,1)S(1)} collective-permute-done((bf16[272,128]{1,0:T(8,128)(2,1)S(1)}, bf16[272,128]{1,0:T(8,128)(2,1)S(1)}, u32[]{:S(2)}, u32[]{:S(2)}) %collective-permute-start.14) | collective-permute-done | bytes 69664 | tf_op jit(solution)/shard_map/return/ppermute | solution.py:228
  40.7 0.3 collective-permute-done.15.refs_5_
  40.9 0.8 %combine.1 = bf16[128,512]{1,0:T(8,128)(2,1)} custom-call(bf16[272,128]{1,0:T(8,128)(2,1)S(1)} %get-tuple-element.25.refs_0_, bf16[272,128]{1,0:T(8,128)(2,1)S(1)} %collective-permute-done.11.refs_1_, bf16[272,128]{1,0:T(8,128)(2,1)S(1)} %collective-permute-done.12.refs_2_, bf16[272,128]{1,0:T(8,128)(2,1)S(1)} %collective-permute-done.13.refs_3_, ...), custom_call_target="tpu_custom_call" | custom-call | tf_op jit(solution)/shard_map/combine/combine/pallas_call | solution.py:251
Async XLA Ops:
  0.0 2.7 %collective-permute-start.1 = (bf16[128,512]{1,0:T(8,128)(2,1)}, bf16[128,512]{1,0:T(8,128)(2,1)S(1)}, u32[]{:S(2)}, u32[]{:S(2)}) collective-permute-start(bf16[128,512]{1,0:T(8,128)(2,1)} %param.4), channel_id=1, source_target_pairs={{0,1},{1,0},{2,3},{3,2},{4,5},{5,4},{6,7},{7,6},{8,9},{9,8},{10,11... | collective-permute-start | bytes 393224 | tf_op jit(solution)/shard_map/swap/ppermute | solution.py:158
  0.5 2.3 %collective-permute-start.2 = (bf16[128,512]{1,0:T(8,128)(2,1)}, bf16[128,512]{1,0:T(8,128)(2,1)S(1)}, u32[]{:S(2)}, u32[]{:S(2)}) collective-permute-start(bf16[128,512]{1,0:T(8,128)(2,1)} %param.5), channel_id=1, source_target_pairs={{0,1},{1,0},{2,3},{3,2},{4,5},{5,4},{6,7},{7,6},{8,9},{9,8},{10,11... | collective-permute-start | bytes 393224 | tf_op jit(solution)/shard_map/swap/ppermute | solution.py:158
  0.5 2.3 %collective-permute-start.3 = (bf16[128,512]{1,0:T(8,128)(2,1)}, bf16[128,512]{1,0:T(8,128)(2,1)S(1)}, u32[]{:S(2)}, u32[]{:S(2)}) collective-permute-start(bf16[128,512]{1,0:T(8,128)(2,1)} %param.6), channel_id=1, source_target_pairs={{0,1},{1,0},{2,3},{3,2},{4,5},{5,4},{6,7},{7,6},{8,9},{9,8},{10,11... | collective-permute-start | bytes 393224 | tf_op jit(solution)/shard_map/swap/ppermute | solution.py:158
  1.0 1.8 %collective-permute-start = (s32[1]{0:T(128)}, s32[1]{0:T(128)}, u32[]{:S(2)}, u32[]{:S(2)}) collective-permute-start(s32[1]{0:T(128)} %param.7), channel_id=1, source_target_pairs={{0,1},{1,0},{2,3},{3,2},{4,5},{5,4},{6,7},{7,6},{8,9},{9,8},{10,11... | collective-permute-start | bytes 20 | tf_op jit(solution)/shard_map/swap/ppermute | solution.py:158
  3.6 10.2 %collective-permute-start.6 = (bf16[1040,128]{1,0:T(8,128)(2,1)S(1)}, bf16[1040,128]{1,0:T(8,128)(2,1)S(1)}, u32[]{:S(2)}, u32[]{:S(2)}) collective-permute-start(bf16[1040,128]{1,0:T(8,128)(2,1)S(1)} %get-tuple-element.20.refs_0_), channel_id=1, source_target_pairs={{0,8},{8,0},{16,24},{24,16},{1,9},{9,1},{17,25},{25,17},{2,10},{10... | collective-permute-start | bytes 798728 | tf_op jit(solution)/shard_map/exchange/ppermute | solution.py:186
  6.6 15.5 %collective-permute-start.8 = (bf16[1040,128]{1,0:T(8,128)(2,1)S(1)}, bf16[1040,128]{1,0:T(8,128)(2,1)S(1)}, u32[]{:S(2)}, u32[]{:S(2)}) collective-permute-start(bf16[1040,128]{1,0:T(8,128)(2,1)S(1)} %get-tuple-element.20.refs_0_), channel_id=1, source_target_pairs={{0,16},{8,24},{16,0},{24,8},{1,17},{9,25},{17,1},{25,9},{2,18},{10... | collective-permute-start | bytes 798728 | tf_op jit(solution)/shard_map/exchange/ppermute | solution.py:186
  8.2 13.9 %collective-permute-start.9 = (bf16[1040,128]{1,0:T(8,128)(2,1)S(1)}, bf16[1040,128]{1,0:T(8,128)(2,1)S(1)}, u32[]{:S(2)}, u32[]{:S(2)}) collective-permute-start(bf16[1040,128]{1,0:T(8,128)(2,1)S(1)} %get-tuple-element.20.refs_0_), channel_id=1, source_target_pairs={{0,24},{8,16},{16,8},{24,0},{1,25},{9,17},{17,9},{25,1},{2,26},{10... | collective-permute-start | bytes 798728 | tf_op jit(solution)/shard_map/exchange/ppermute | solution.py:186
  8.2 13.0 %collective-permute-start.4 = (bf16[528,128]{1,0:T(8,128)(2,1)S(1)}, bf16[528,128]{1,0:T(8,128)(2,1)S(1)}, u32[]{:S(2)}, u32[]{:S(2)}) collective-permute-start(bf16[528,128]{1,0:T(8,128)(2,1)S(1)} %get-tuple-element.24.q_ref), channel_id=1, source_target_pairs={{0,4},{1,5},{2,6},{3,7},{4,0},{5,1},{6,2},{7,3},{8,12},{9,13},{10,... | collective-permute-start | bytes 405512 | tf_op jit(solution)/shard_map/exchange/ppermute | solution.py:190
  11.2 10.0 %collective-permute-start.5 = (bf16[528,128]{1,0:T(8,128)(2,1)S(1)}, bf16[528,128]{1,0:T(8,128)(2,1)S(1)}, u32[]{:S(2)}, u32[]{:S(2)}) collective-permute-start(bf16[528,128]{1,0:T(8,128)(2,1)S(1)} %get-tuple-element.24.q_ref), channel_id=1, source_target_pairs={{0,6},{1,7},{2,4},{3,5},{4,2},{5,3},{6,0},{7,1},{8,14},{9,15},{10,... | collective-permute-start | bytes 405512 | tf_op jit(solution)/shard_map/exchange/ppermute | solution.py:190
  13.8 8.3 %collective-permute-start.7 = (bf16[528,128]{1,0:T(8,128)(2,1)S(1)}, bf16[528,128]{1,0:T(8,128)(2,1)S(1)}, u32[]{:S(2)}, u32[]{:S(2)}) collective-permute-start(bf16[528,128]{1,0:T(8,128)(2,1)S(1)} %get-tuple-element.24.q_ref), channel_id=1, source_target_pairs={{0,2},{1,3},{2,0},{3,1},{4,6},{5,7},{6,4},{7,5},{8,10},{9,11},{10,... | collective-permute-start | bytes 405512 | tf_op jit(solution)/shard_map/exchange/ppermute | solution.py:190
  23.3 5.4 %collective-permute-start.10 = (bf16[544,128]{1,0:T(8,128)(2,1)S(1)}, bf16[544,128]{1,0:T(8,128)(2,1)S(1)}, u32[]{:S(2)}, u32[]{:S(2)}) collective-permute-start(bf16[544,128]{1,0:T(8,128)(2,1)S(1)} %attend.4), channel_id=1, source_target_pairs={{0,2},{1,3},{2,0},{3,1},{4,6},{5,7},{6,4},{7,5},{8,10},{9,11},{10,... | collective-permute-start | bytes 417800 | tf_op jit(solution)/shard_map/return/ppermute | solution.py:230
  28.8 3.9 %collective-permute-start.11 = (bf16[272,128]{1,0:T(8,128)(2,1)S(1)}, bf16[272,128]{1,0:T(8,128)(2,1)S(1)}, u32[]{:S(2)}, u32[]{:S(2)}) collective-permute-start(bf16[272,128]{1,0:T(8,128)(2,1)S(1)} %get-tuple-element.28), channel_id=1, source_target_pairs={{0,1},{1,0},{2,3},{3,2},{4,5},{5,4},{6,7},{7,6},{8,9},{9,8},{10,11... | collective-permute-start | bytes 208904 | tf_op jit(solution)/shard_map/return/ppermute | solution.py:246
  28.9 9.8 %collective-permute-start.12 = (bf16[272,128]{1,0:T(8,128)(2,1)S(1)}, bf16[272,128]{1,0:T(8,128)(2,1)S(1)}, u32[]{:S(2)}, u32[]{:S(2)}) collective-permute-start(bf16[272,128]{1,0:T(8,128)(2,1)S(1)} %get-tuple-element.27), channel_id=1, source_target_pairs={{0,4},{1,5},{2,6},{3,7},{4,0},{5,1},{6,2},{7,3},{8,12},{9,13},{10,... | collective-permute-start | bytes 208904 | tf_op jit(solution)/shard_map/return/ppermute | solution.py:228
  32.6 7.1 %collective-permute-start.13 = (bf16[272,128]{1,0:T(8,128)(2,1)S(1)}, bf16[272,128]{1,0:T(8,128)(2,1)S(1)}, u32[]{:S(2)}, u32[]{:S(2)}) collective-permute-start(bf16[272,128]{1,0:T(8,128)(2,1)S(1)} %get-tuple-element.29), channel_id=1, source_target_pairs={{0,5},{1,4},{2,7},{3,6},{4,1},{5,0},{6,3},{7,2},{8,13},{9,12},{10,... | collective-permute-start | bytes 208904 | tf_op jit(solution)/shard_map/return/ppermute | solution.py:228
  33.9 6.8 %collective-permute-start.14 = (bf16[272,128]{1,0:T(8,128)(2,1)S(1)}, bf16[272,128]{1,0:T(8,128)(2,1)S(1)}, u32[]{:S(2)}, u32[]{:S(2)}) collective-permute-start(bf16[272,128]{1,0:T(8,128)(2,1)S(1)} %get-tuple-element.31), channel_id=1, source_target_pairs={{0,2},{1,3},{2,0},{3,1},{4,6},{5,7},{6,4},{7,5},{8,10},{9,11},{10,... | collective-permute-start | bytes 208904 | tf_op jit(solution)/shard_map/return/ppermute | solution.py:228
  34.6 6.3 %collective-permute-start.15 = (bf16[272,128]{1,0:T(8,128)(2,1)S(1)}, bf16[272,128]{1,0:T(8,128)(2,1)S(1)}, u32[]{:S(2)}, u32[]{:S(2)}) collective-permute-start(bf16[272,128]{1,0:T(8,128)(2,1)S(1)} %get-tuple-element.32), channel_id=1, source_target_pairs={{0,3},{1,2},{2,1},{3,0},{4,7},{5,6},{6,5},{7,4},{8,11},{9,10},{10,... | collective-permute-start | bytes 208904 | tf_op jit(solution)/shard_map/return/ppermute | solution.py:228

commit v8 on v7

--- a/solution.py
+++ b/solution.py
@@ -22,23 +22,37 @@
     return lax.dot_general(a, b, (((1,), (1,)), ((), ())), preferred_element_type=F32)
 
 
-def merge_kernel(p0, p1, own, q1, k1, v1, q_out, kv_out):
+def place(own, other, out, at, turned=False):
+    tok = own.shape[0]
+    size = own.shape[1] // HEADS
+    core = lax.rem(lax.axis_index("inner"), CORES)
+    for b, ref in enumerate((own, other)):
+        for j in range(PER):
+            piece = ref[:, pl.ds(pl.multiple_of((core * PER + j) * size, size), size)]
+            if turned:
+                piece = piece.astype(F32).T.astype(BF16)
+            row = at + j * CORES * tok + b * tok
+            out[row : row + tok, :] = piece
+
+
+def starts(p0, p1, size):
+    half = PAD // CORES
+    return jnp.concatenate([jnp.full((half, size), p[0].astype(F32), F32) for p in (p0, p1)], axis=0).astype(BF16)
+
+
+def merge_q_kernel(p0, p1, own, q1, out):
     tok = q1.shape[0]
-    size = q1.shape[1] // HEADS
-    q0, k0, v0 = (own.at[i * tok : (i + 1) * tok, :] for i in range(3))
-    core = lax.rem(lax.axis_index("inner"), CORES)
-    both = CORES * tok
-    for b, (q, k, v) in enumerate(((q0, k0, v0), (q1, k1, v1))):
-        for j in range(PER):
-            cols = pl.ds(pl.multiple_of((core * PER + j) * size, size), size)
-            q_out[j * both + b * tok : j * both + (b + 1) * tok, :] = q[:, cols]
-            kv_out[j * both + b * tok : j * both + (b + 1) * tok, :] = k[:, cols]
-            at = PAD + (PER + j) * both + b * tok
-            kv_out[at : at + tok, :] = v[:, cols].astype(F32).T.astype(BF16)
-    half = PAD // CORES
-    pos = jnp.concatenate([jnp.full((half, size), p[0].astype(F32), F32) for p in (p0, p1)], axis=0).astype(BF16)
-    q_out[PER * both :, :] = pos
-    kv_out[PER * both : PER * both + PAD, :] = pos
+    rows = PER * CORES * tok
+    place(own.at[0:tok, :], q1, out, 0)
+    out[rows:, :] = starts(p0, p1, out.shape[1])
+
+
+def merge_kv_kernel(p0, p1, own, k1, v1, out):
+    tok = k1.shape[0]
+    rows = PER * CORES * tok
+    place(own.at[tok : 2 * tok, :], k1, out, 0)
+    out[rows : rows + PAD, :] = starts(p0, p1, out.shape[1])
+    place(own.at[2 * tok : 3 * tok, :], v1, out, rows + PAD, turned=True)
 
 
 def attend_kernel(wide, where, q_ref, *refs):
@@ -154,22 +168,30 @@
     def along_inner(r, x):
         return [(w * CORES + c, (w ^ r) * CORES + (c ^ x)) for w in range(chips) for c in range(CORES)]
 
+    def after(a, b):
+        return lax.optimization_barrier((a, b))[0]
+
     with jax.named_scope("swap"):
         other = [lax.ppermute(a, "inner", along_inner(0, 1)) for a in (queries, keys, values, block_pos)]
         own = jnp.concatenate([queries, keys, values], axis=0)
     with jax.named_scope("merge"):
         smem = [pl.BlockSpec(memory_space=pltpu.SMEM)]
-        q_piece, kv_piece = pl.pallas_call(
-            merge_kernel,
-            out_shape=(
-                jax.ShapeDtypeStruct((PER * both + PAD, size), BF16),
-                jax.ShapeDtypeStruct((2 * PER * both + PAD, size), BF16),
-            ),
-            in_specs=smem * 2 + vmem(4),
-            out_specs=tuple(vmem(2)),
+        q_piece = pl.pallas_call(
+            merge_q_kernel,
+            out_shape=jax.ShapeDtypeStruct((PER * both + PAD, size), BF16),
+            in_specs=smem * 2 + vmem(2),
+            out_specs=vmem()[0],
             compiler_params=params,
-            name="merge",
-        )(block_pos, other[3], own, *other[:3])
+            name="merge_q",
+        )(block_pos, other[3], own, other[0])
+        kv_piece = pl.pallas_call(
+            merge_kv_kernel,
+            out_shape=jax.ShapeDtypeStruct((2 * PER * both + PAD, size), BF16),
+            in_specs=smem * 2 + vmem(3),
+            out_specs=vmem()[0],
+            compiler_params=params,
+            name="merge_kv",
+        )(block_pos, other[3], own, after(other[1], q_piece), other[2])
     half = PER * both + PAD
     block = PER * size + PAD
 
@@ -178,16 +200,15 @@
 
     def single(r):
         return r == low(r)
-
-    def after(a, b):
-        return lax.optimization_barrier((a, b))[0]
 
     with jax.named_scope("exchange"):
         kv = [kv_piece] + [lax.ppermute(kv_piece, "outer", [(o, o ^ r) for o in range(n_out)]) for r in range(1, n_out)]
         q_by = {0: q_piece}
-        for r in reversed(range(1, chips)):
-            piece = after(q_piece, kv[1]) if r == 1 else q_piece
-            q_by[r] = lax.ppermute(piece, "inner", along_inner(r, 0))
+        bit = chips // 2
+        while bit:
+            for r in sorted(q_by):
+                q_by[r | bit] = lax.ppermute(q_by[r], "inner", along_inner(bit, 0))
+            bit //= 2
     where = tuple((r, 0, r, half) for r in range(n_out))
 
     def shapes(wide):
@@ -229,24 +250,19 @@
             else:
                 arrived[r - low(r)].append(lax.ppermute(parts[0], "inner", along_inner(low(r), 0)))
 
-    done = (q_by[2], q_by[1]) if chips > 2 else None
+    done = None
     partial = {}
-    for r in reversed(range(2, chips)):
-        partial[r] = attend(r, True, done)
+    for r in reversed(range(1, chips)):
+        partial[r] = attend(r, r > 1, done)
         done = partial[r][0]
     own = attend(0, False, done)
-    for r in reversed(range(2, chips)):
+    for r in reversed(range(1, chips)):
         parts = partial[r]
         if arrived[r]:
             parts = add([parts[0], *arrived[r]], not single(r))
-        done = parts[0]
         send(r, parts)
     with jax.named_scope("return"):
-        piece = own[1] if done is None else after(own[1], done)
-        across = lax.ppermute(piece, "inner", along_inner(0, 1))
-    if chips > 1:
-        send(1, attend(1, False, across))
-    ends = [own[0], across] + ends
+        ends = [own[0], lax.ppermute(own[1], "inner", along_inner(0, 1))] + ends
     with jax.named_scope("combine"):
         return pl.pallas_call(
             functools.partial(combine_kernel, len(ends)),

time: 41.9 us -> 42.5 us (1.014)
  starting transfers between devices: 19.1 us -> 17 us
  waiting for transfers between devices: 14.4 us -> 16.5 us
  local copies, waits for them, and re-layouts: 0 us -> 1.15 us
  other arithmetic: 1.06 us -> 0 us
  Pallas kernels: 6.48 us -> 6.91 us
    ppermute x3, waiting for transfers between devices: 1.27 us -> 7.04 us  [shards(): lax.ppermute(kv_piece, 'outer', [(o, o ^ r) for o in range(n_out)])]
    ppermute x4, waiting for transfers between devices: 6.12 us -> 2.46 us  [the longest x3 2.45 us: shards(): q_by[r | bit] = lax.ppermute(q_by[r], 'inner', along_inner(bit, 0))]
    ppermute x4, waiting for transfers between devices: 5.51 us -> 7 us  [send(): lax.ppermute(parts[x], 'inner', along_inner(r, x))]
    ppermute x1, waiting for transfers between devices: 1.47 us -> 0.01 us  [send(): lax.ppermute(parts[0], 'inner', along_inner(low(r), 0))]
    unnamed x0 -> x6, local copies, waits for them, and re-layouts: none -> 1.14 us
    concatenate x1 -> x0, other arithmetic: 1.06 us -> none  [shards(): own = jnp.concatenate([queries, keys, values], axis=0)]
    ppermute x3, starting transfers between devices: 4.54 us -> 3.55 us  [shards(): lax.ppermute(kv_piece, 'outer', [(o, o ^ r) for o in range(n_out)])]
    ppermute x4, starting transfers between devices: 5.35 us -> 4.59 us  [send(): lax.ppermute(parts[x], 'inner', along_inner(r, x))]
  transfers between devices with their start and end apart: 16 -> 16, of which waited for: 8 -> 5; matrix products, arithmetic and copies ran while one was open for 3% -> 2% of each run, Pallas kernels for 8% -> 14%
where the time goes in v8:
time: 42.5 us; the launch traced here: 42.4 us
  starting transfers between devices  17 us (40%)
  waiting for transfers between devices  16.5 us (39%)
  Pallas kernels  6.91 us (16%)
  local copies, waits for them, and re-layouts  1.15 us (3%)
  between operations  0.81 us (2%)
    ppermute x3, waiting for transfers between devices, shards(): lax.ppermute(kv_piece, 'outer', [(o, o ^ r) for o in range(n_out)])  7.04 us
    ppermute x4, waiting for transfers between devices, send(): lax.ppermute(parts[x], 'inner', along_inner(r, x))  7 us
    ppermute x3, starting transfers between devices, shards(): q_by[r | bit] = lax.ppermute(q_by[r], 'inner', along_inner(bit, 0))  6.12 us
    pallas_call x4, Pallas kernels, attend(): pl.pallas_call(functools.partial(attend_kernel, wide, where), out_shape=s...  4.71 us
    ppermute x4, starting transfers between devices, send(): lax.ppermute(parts[x], 'inner', along_inner(r, x))  4.59 us
    ppermute x3, starting transfers between devices, shards(): lax.ppermute(kv_piece, 'outer', [(o, o ^ r) for o in range(n_out)])  3.55 us
    ppermute x3, waiting for transfers between devices, shards(): q_by[r | bit] = lax.ppermute(q_by[r], 'inner', along_inner(bit, 0))  2.45 us
    ppermute x1, starting transfers between devices, send(): lax.ppermute(parts[0], 'inner', along_inner(low(r), 0))  1.64 us
  transfers between devices with their start and end apart: 16, of which 5 were waited for; matrix products, arithmetic and copies ran while one was open for 2% of the time, Pallas kernels for 14%

profile of v8, /device:TPU:0, one launch (start us, length us, event | category | flops | bytes accessed | tf_op | source)
XLA Modules:
  0.0 42.4 jit_solution(3973522123518135056)
XLA Ops:
  0.0 0.0 copy-start
  0.0 0.5 %collective-permute-start = (s32[1]{0:T(128)}, s32[1]{0:T(128)}, u32[]{:S(2)}, u32[]{:S(2)}) collective-permute-start(s32[1]{0:T(128)} %param.7), channel_id=1, source_target_pairs={{0,1},{1,0},{2,3},{3,2},{4,5},{5,4},{6,7},{7,6},{8,9},{9,8},{10,11... | collective-permute-start | bytes 20 | tf_op jit(solution)/shard_map/swap/ppermute | solution.py:175
  0.5 0.1 collective-permute-start.1
  0.5 0.4 %collective-permute-start.5 = (bf16[128,512]{1,0:T(8,128)(2,1)}, bf16[128,512]{1,0:T(8,128)(2,1)S(1)}, u32[]{:S(2)}, u32[]{:S(2)}) collective-permute-start(bf16[128,512]{1,0:T(8,128)(2,1)} %param.5), channel_id=1, source_target_pairs={{0,1},{1,0},{2,3},{3,2},{4,5},{5,4},{6,7},{7,6},{8,9},{9,8},{10,11... | collective-permute-start | bytes 393224 | tf_op jit(solution)/shard_map/swap/ppermute | solution.py:175
  1.0 0.1 collective-permute-start.6
  1.0 0.9 %constant_dynamic-update-slice_fusion.2 = bf16[384,512]{1,0:T(8,128)(2,1)S(1)} fusion(bf16[128,512]{1,0:T(8,128)(2,1)} %param.4), kind=kLoop, calls=%fused_computation.2 | loop fusion | bytes 262144
  1.9 0.0 copy-done
  2.0 0.0 copy-start.1
  2.7 0.2 copy-done.1
  2.9 0.0 collective-permute-done.p1
  2.9 0.0 collective-permute-done.1.q1
  2.9 0.6 %merge_q.1.q_ref = bf16[528,128]{1,0:T(8,128)(2,1)S(1)} custom-call(s32[1]{0:T(128)S(6)} %copy.7.p0, s32[1]{0:T(128)} %collective-permute-done.p1, bf16[384,512]{1,0:T(8,128)(2,1)S(1)} %constant_dynamic-update-slice_fusion.own, bf16[128,512]{1,0:T(8,128)(2,1)S(1)} %collective-permute-done.1.q1), custom_call_target="tpu_custom_call" | custom-call | tf_op jit(solution)/shard_map/merge/merge_q/pallas_call | solution.py:179
  3.5 4.1 %collective-permute-start.3 = (bf16[528,128]{1,0:T(8,128)(2,1)S(1)}, bf16[528,128]{1,0:T(8,128)(2,1)S(1)}, u32[]{:S(2)}, u32[]{:S(2)}) collective-permute-start(bf16[528,128]{1,0:T(8,128)(2,1)S(1)} %merge_q.1.q_ref), channel_id=1, source_target_pairs={{0,4},{1,5},{2,6},{3,7},{4,0},{5,1},{6,2},{7,3},{8,12},{9,13},{10,... | collective-permute-start | bytes 405512 | tf_op jit(solution)/shard_map/exchange/ppermute | solution.py:210
  7.6 0.0 collective-permute-done.5.k1
  7.6 0.0 collective-permute-done.6.v1
  7.6 0.7 %merge_kv.1.refs_0_ = bf16[1040,128]{1,0:T(8,128)(2,1)S(1)} custom-call(s32[1]{0:T(128)S(6)} %copy.7.p0, s32[1]{0:T(128)} %collective-permute-done.p1, bf16[384,512]{1,0:T(8,128)(2,1)S(1)} %constant_dynamic-update-slice_fusion.own, bf16[128,512]{1,0:T(8,128)(2,1)S(1)} %collective-permute-done.5.k1, bf16[128,512]{1,0:T(8,128)(2,1)S(1)} %collective-permute-done.6.v1), custom_call_target="tpu_custom_call" | custom-call | tf_op jit(solution)/shard_map/merge/merge_kv/pallas_call | solution.py:187
  8.3 1.6 %collective-permute-start.7 = (bf16[1040,128]{1,0:T(8,128)(2,1)S(1)}, bf16[1040,128]{1,0:T(8,128)(2,1)S(1)}, u32[]{:S(2)}, u32[]{:S(2)}) collective-permute-start(bf16[1040,128]{1,0:T(8,128)(2,1)S(1)} %merge_kv.1.refs_0_), channel_id=1, source_target_pairs={{0,8},{8,0},{16,24},{24,16},{1,9},{9,1},{17,25},{25,17},{2,10},{10... | collective-permute-start | bytes 798728 | tf_op jit(solution)/shard_map/exchange/ppermute | solution.py:205
  9.9 1.5 %collective-permute-start.8 = (bf16[1040,128]{1,0:T(8,128)(2,1)S(1)}, bf16[1040,128]{1,0:T(8,128)(2,1)S(1)}, u32[]{:S(2)}, u32[]{:S(2)}) collective-permute-start(bf16[1040,128]{1,0:T(8,128)(2,1)S(1)} %merge_kv.1.refs_0_), channel_id=1, source_target_pairs={{0,16},{8,24},{16,0},{24,8},{1,17},{9,25},{17,1},{25,9},{2,18},{10... | collective-permute-start | bytes 798728 | tf_op jit(solution)/shard_map/exchange/ppermute | solution.py:205
  11.4 0.5 %collective-permute-start.9 = (bf16[1040,128]{1,0:T(8,128)(2,1)S(1)}, bf16[1040,128]{1,0:T(8,128)(2,1)S(1)}, u32[]{:S(2)}, u32[]{:S(2)}) collective-permute-start(bf16[1040,128]{1,0:T(8,128)(2,1)S(1)} %merge_kv.1.refs_0_), channel_id=1, source_target_pairs={{0,24},{8,16},{16,8},{24,0},{1,25},{9,17},{17,9},{25,1},{2,26},{10... | collective-permute-start | bytes 798728 | tf_op jit(solution)/shard_map/exchange/ppermute | solution.py:205
  11.9 2.4 %collective-permute-done.3.q_ref = bf16[528,128]{1,0:T(8,128)(2,1)S(1)} collective-permute-done((bf16[528,128]{1,0:T(8,128)(2,1)S(1)}, bf16[528,128]{1,0:T(8,128)(2,1)S(1)}, u32[]{:S(2)}, u32[]{:S(2)}) %collective-permute-start.3) | collective-permute-done | bytes 135200 | tf_op jit(solution)/shard_map/exchange/ppermute | solution.py:210
  14.3 0.7 %collective-permute-start.4 = (bf16[528,128]{1,0:T(8,128)(2,1)S(1)}, bf16[528,128]{1,0:T(8,128)(2,1)S(1)}, u32[]{:S(2)}, u32[]{:S(2)}) collective-permute-start(bf16[528,128]{1,0:T(8,128)(2,1)S(1)} %collective-permute-done.3.q_ref), channel_id=1, source_target_pairs={{0,2},{1,3},{2,0},{3,1},{4,6},{5,7},{6,4},{7,5},{8,10},{9,11},{10,... | collective-permute-start | bytes 405512 | tf_op jit(solution)/shard_map/exchange/ppermute | solution.py:210
  15.0 1.3 %collective-permute-start.2 = (bf16[528,128]{1,0:T(8,128)(2,1)S(1)}, bf16[528,128]{1,0:T(8,128)(2,1)S(1)}, u32[]{:S(2)}, u32[]{:S(2)}) collective-permute-start(bf16[528,128]{1,0:T(8,128)(2,1)S(1)} %merge_q.1.q_ref), channel_id=1, source_target_pairs={{0,2},{1,3},{2,0},{3,1},{4,6},{5,7},{6,4},{7,5},{8,10},{9,11},{10,... | collective-permute-start | bytes 405512 | tf_op jit(solution)/shard_map/exchange/ppermute | solution.py:210
  16.3 1.3 %collective-permute-done.7.refs_1_ = bf16[1040,128]{1,0:T(8,128)(2,1)S(1)} collective-permute-done((bf16[1040,128]{1,0:T(8,128)(2,1)S(1)}, bf16[1040,128]{1,0:T(8,128)(2,1)S(1)}, u32[]{:S(2)}, u32[]{:S(2)}) %collective-permute-start.7) | collective-permute-done | bytes 266272 | tf_op jit(solution)/shard_map/exchange/ppermute | solution.py:205
  17.7 5.7 %collective-permute-done.8.refs_2_ = bf16[1040,128]{1,0:T(8,128)(2,1)S(1)} collective-permute-done((bf16[1040,128]{1,0:T(8,128)(2,1)S(1)}, bf16[1040,128]{1,0:T(8,128)(2,1)S(1)}, u32[]{:S(2)}, u32[]{:S(2)}) %collective-permute-start.8) | collective-permute-done | bytes 266272 | tf_op jit(solution)/shard_map/exchange/ppermute | solution.py:205
  23.4 0.0 collective-permute-done.9.refs_3_
  23.4 0.0 collective-permute-done.4.q_ref
  23.4 1.2 %attend.4 = bf16[544,128]{1,0:T(8,128)(2,1)S(1)} custom-call(bf16[528,128]{1,0:T(8,128)(2,1)S(1)} %collective-permute-done.4.q_ref, bf16[1040,128]{1,0:T(8,128)(2,1)S(1)} %merge_kv.1.refs_0_, bf16[1040,128]{1,0:T(8,128)(2,1)S(1)} %collective-permute-done.7.refs_1_, bf16[1040,128]{1,0:T(8,128)(2,1)S(1)} %collective-permute-done.8.refs_2_, ...), custom_call_target="tpu_custom_call" | custom-call | flops 268435456 | bytes 1048576 | tf_op jit(solution)/shard_map/attend/attend/pallas_call | solution.py:222
  24.6 1.6 %collective-permute-start.11 = (bf16[544,128]{1,0:T(8,128)(2,1)S(1)}, bf16[544,128]{1,0:T(8,128)(2,1)S(1)}, u32[]{:S(2)}, u32[]{:S(2)}) collective-permute-start(bf16[544,128]{1,0:T(8,128)(2,1)S(1)} %attend.4), channel_id=1, source_target_pairs={{0,2},{1,3},{2,0},{3,1},{4,6},{5,7},{6,4},{7,5},{8,10},{9,11},{10,... | collective-permute-start | bytes 417800 | tf_op jit(solution)/shard_map/return/ppermute | solution.py:251
  26.2 1.2 %attend.5.refs_0_ = bf16[544,128]{1,0:T(8,128)(2,1)S(1)} custom-call(bf16[528,128]{1,0:T(8,128)(2,1)S(1)} %collective-permute-done.3.q_ref, bf16[1040,128]{1,0:T(8,128)(2,1)S(1)} %merge_kv.1.refs_0_, bf16[1040,128]{1,0:T(8,128)(2,1)S(1)} %collective-permute-done.7.refs_1_, bf16[1040,128]{1,0:T(8,128)(2,1)S(1)} %collective-permute-done.8.refs_2_, ...), custom_call_target="tpu_custom_call" | custom-call | flops 268435456 | bytes 1048576 | tf_op jit(solution)/shard_map/attend/attend/pallas_call | solution.py:222
  27.4 0.0 collective-permute-done.2.q_ref
  27.4 1.2 %attend.6 = (bf16[272,128]{1,0:T(8,128)(2,1)S(1)}, bf16[272,128]{1,0:T(8,128)(2,1)S(1)}) custom-call(bf16[528,128]{1,0:T(8,128)(2,1)S(1)} %collective-permute-done.2.q_ref, bf16[1040,128]{1,0:T(8,128)(2,1)S(1)} %merge_kv.1.refs_0_, bf16[1040,128]{1,0:T(8,128)(2,1)S(1)} %collective-permute-done.7.refs_1_, ...), custom_call_target="tpu_custom_call" | custom-call | flops 268435456 | bytes 1048576 | tf_op jit(solution)/shard_map/attend/attend/pallas_call | solution.py:222
  28.6 0.5 %collective-permute-start.14 = (bf16[272,128]{1,0:T(8,128)(2,1)S(1)}, bf16[272,128]{1,0:T(8,128)(2,1)S(1)}, u32[]{:S(2)}, u32[]{:S(2)}) collective-permute-start(bf16[272,128]{1,0:T(8,128)(2,1)S(1)} %get-tuple-element.18), channel_id=1, source_target_pairs={{0,2},{1,3},{2,0},{3,1},{4,6},{5,7},{6,4},{7,5},{8,10},{9,11},{10,... | collective-permute-start | bytes 208904 | tf_op jit(solution)/shard_map/return/ppermute | solution.py:249
  29.1 1.2 %attend.7 = (bf16[272,128]{1,0:T(8,128)(2,1)S(1)}, bf16[272,128]{1,0:T(8,128)(2,1)S(1)}) custom-call(bf16[528,128]{1,0:T(8,128)(2,1)S(1)} %merge_q.1.q_ref, bf16[1040,128]{1,0:T(8,128)(2,1)S(1)} %merge_kv.1.refs_0_, bf16[1040,128]{1,0:T(8,128)(2,1)S(1)} %collective-permute-done.7.refs_1_, bf16[1040,128]{1,0:T(8,128)(2,1)S(1)} %collective-permute-done.8.refs_2_, ...), custom_call_target="tpu_custom_call" | custom-call | flops 268435456 | bytes 1048576 | tf_op jit(solution)/shard_map/attend/attend/pallas_call | solution.py:222
  30.3 0.1 collective-permute-start.10
  30.4 1.7 %collective-permute-start.15 = (bf16[272,128]{1,0:T(8,128)(2,1)S(1)}, bf16[272,128]{1,0:T(8,128)(2,1)S(1)}, u32[]{:S(2)}, u32[]{:S(2)}) collective-permute-start(bf16[272,128]{1,0:T(8,128)(2,1)S(1)} %get-tuple-element.24), channel_id=1, source_target_pairs={{0,3},{1,2},{2,1},{3,0},{4,7},{5,6},{6,5},{7,4},{8,11},{9,10},{10,... | collective-permute-start | bytes 208904 | tf_op jit(solution)/shard_map/return/ppermute | solution.py:249
  32.1 0.0 collective-permute-done.11.refs_1_
  32.1 0.1 add.1
  32.2 0.4 collective-permute-start.12
  32.6 2.0 %collective-permute-start.13 = (bf16[272,128]{1,0:T(8,128)(2,1)S(1)}, bf16[272,128]{1,0:T(8,128)(2,1)S(1)}, u32[]{:S(2)}, u32[]{:S(2)}) collective-permute-start(bf16[272,128]{1,0:T(8,128)(2,1)S(1)} %get-tuple-element.23), channel_id=1, source_target_pairs={{0,5},{1,4},{2,7},{3,6},{4,1},{5,0},{6,3},{7,2},{8,13},{9,12},{10,... | collective-permute-start | bytes 208904 | tf_op jit(solution)/shard_map/return/ppermute | solution.py:249
  34.5 0.0 collective-permute-done.10.refs_1_
  34.5 0.0 collective-permute-done.14.refs_4_
  34.5 0.0 collective-permute-done.15.refs_5_
  34.6 5.6 %collective-permute-done.12.refs_2_ = bf16[272,128]{1,0:T(8,128)(2,1)S(1)} collective-permute-done((bf16[272,128]{1,0:T(8,128)(2,1)S(1)}, bf16[272,128]{1,0:T(8,128)(2,1)S(1)}, u32[]{:S(2)}, u32[]{:S(2)}) %collective-permute-start.12) | collective-permute-done | bytes 69664 | tf_op jit(solution)/shard_map/return/ppermute | solution.py:249
  40.2 1.3 %collective-permute-done.13.refs_3_ = bf16[272,128]{1,0:T(8,128)(2,1)S(1)} collective-permute-done((bf16[272,128]{1,0:T(8,128)(2,1)S(1)}, bf16[272,128]{1,0:T(8,128)(2,1)S(1)}, u32[]{:S(2)}, u32[]{:S(2)}) %collective-permute-start.13) | collective-permute-done | bytes 69664 | tf_op jit(solution)/shard_map/return/ppermute | solution.py:249
  41.5 0.8 %combine.1 = bf16[128,512]{1,0:T(8,128)(2,1)} custom-call(bf16[272,128]{1,0:T(8,128)(2,1)S(1)} %get-tuple-element.20.refs_0_, bf16[272,128]{1,0:T(8,128)(2,1)S(1)} %collective-permute-done.10.refs_1_, bf16[272,128]{1,0:T(8,128)(2,1)S(1)} %collective-permute-done.12.refs_2_, bf16[272,128]{1,0:T(8,128)(2,1)S(1)} %collective-permute-done.13.refs_3_, ...), custom_call_target="tpu_custom_call" | custom-call | tf_op jit(solution)/shard_map/combine/combine/pallas_call | solution.py:267
  (2 shorter events, 0.0 us)
Async XLA Ops:
  0.0 1.9 %copy-start = (bf16[128,512]{1,0:T(8,128)(2,1)S(1)}, bf16[128,512]{1,0:T(8,128)(2,1)}, u32[]{:S(2)}) copy-start(bf16[128,512]{1,0:T(8,128)(2,1)} %param.5) | copy-start | bytes 393220
  0.0 2.9 %collective-permute-start = (s32[1]{0:T(128)}, s32[1]{0:T(128)}, u32[]{:S(2)}, u32[]{:S(2)}) collective-permute-start(s32[1]{0:T(128)} %param.7), channel_id=1, source_target_pairs={{0,1},{1,0},{2,3},{3,2},{4,5},{5,4},{6,7},{7,6},{8,9},{9,8},{10,11... | collective-permute-start | bytes 20 | tf_op jit(solution)/shard_map/swap/ppermute | solution.py:175
  0.5 2.5 %collective-permute-start.1 = (bf16[128,512]{1,0:T(8,128)(2,1)}, bf16[128,512]{1,0:T(8,128)(2,1)S(1)}, u32[]{:S(2)}, u32[]{:S(2)}) collective-permute-start(bf16[128,512]{1,0:T(8,128)(2,1)} %param.4), channel_id=1, source_target_pairs={{0,1},{1,0},{2,3},{3,2},{4,5},{5,4},{6,7},{7,6},{8,9},{9,8},{10,11... | collective-permute-start | bytes 393224 | tf_op jit(solution)/shard_map/swap/ppermute | solution.py:175
  0.5 7.1 %collective-permute-start.5 = (bf16[128,512]{1,0:T(8,128)(2,1)}, bf16[128,512]{1,0:T(8,128)(2,1)S(1)}, u32[]{:S(2)}, u32[]{:S(2)}) collective-permute-start(bf16[128,512]{1,0:T(8,128)(2,1)} %param.5), channel_id=1, source_target_pairs={{0,1},{1,0},{2,3},{3,2},{4,5},{5,4},{6,7},{7,6},{8,9},{9,8},{10,11... | collective-permute-start | bytes 393224 | tf_op jit(solution)/shard_map/swap/ppermute | solution.py:175
  1.0 6.7 %collective-permute-start.6 = (bf16[128,512]{1,0:T(8,128)(2,1)}, bf16[128,512]{1,0:T(8,128)(2,1)S(1)}, u32[]{:S(2)}, u32[]{:S(2)}) collective-permute-start(bf16[128,512]{1,0:T(8,128)(2,1)} %param.6), channel_id=1, source_target_pairs={{0,1},{1,0},{2,3},{3,2},{4,5},{5,4},{6,7},{7,6},{8,9},{9,8},{10,11... | collective-permute-start | bytes 393224 | tf_op jit(solution)/shard_map/swap/ppermute | solution.py:175
  2.0 0.9 %copy-start.1 = (bf16[128,512]{1,0:T(8,128)(2,1)S(1)}, bf16[128,512]{1,0:T(8,128)(2,1)}, u32[]{:S(2)}) copy-start(bf16[128,512]{1,0:T(8,128)(2,1)} %param.6) | copy-start | bytes 393220
  3.5 10.8 %collective-permute-start.3 = (bf16[528,128]{1,0:T(8,128)(2,1)S(1)}, bf16[528,128]{1,0:T(8,128)(2,1)S(1)}, u32[]{:S(2)}, u32[]{:S(2)}) collective-permute-start(bf16[528,128]{1,0:T(8,128)(2,1)S(1)} %merge_q.1.q_ref), channel_id=1, source_target_pairs={{0,4},{1,5},{2,6},{3,7},{4,0},{5,1},{6,2},{7,3},{8,12},{9,13},{10,... | collective-permute-start | bytes 405512 | tf_op jit(solution)/shard_map/exchange/ppermute | solution.py:210
  8.3 9.4 %collective-permute-start.7 = (bf16[1040,128]{1,0:T(8,128)(2,1)S(1)}, bf16[1040,128]{1,0:T(8,128)(2,1)S(1)}, u32[]{:S(2)}, u32[]{:S(2)}) collective-permute-start(bf16[1040,128]{1,0:T(8,128)(2,1)S(1)} %merge_kv.1.refs_0_), channel_id=1, source_target_pairs={{0,8},{8,0},{16,24},{24,16},{1,9},{9,1},{17,25},{25,17},{2,10},{10... | collective-permute-start | bytes 798728 | tf_op jit(solution)/shard_map/exchange/ppermute | solution.py:205
  9.9 13.5 %collective-permute-start.8 = (bf16[1040,128]{1,0:T(8,128)(2,1)S(1)}, bf16[1040,128]{1,0:T(8,128)(2,1)S(1)}, u32[]{:S(2)}, u32[]{:S(2)}) collective-permute-start(bf16[1040,128]{1,0:T(8,128)(2,1)S(1)} %merge_kv.1.refs_0_), channel_id=1, source_target_pairs={{0,16},{8,24},{16,0},{24,8},{1,17},{9,25},{17,1},{25,9},{2,18},{10... | collective-permute-start | bytes 798728 | tf_op jit(solution)/shard_map/exchange/ppermute | solution.py:205
  11.4 12.0 %collective-permute-start.9 = (bf16[1040,128]{1,0:T(8,128)(2,1)S(1)}, bf16[1040,128]{1,0:T(8,128)(2,1)S(1)}, u32[]{:S(2)}, u32[]{:S(2)}) collective-permute-start(bf16[1040,128]{1,0:T(8,128)(2,1)S(1)} %merge_kv.1.refs_0_), channel_id=1, source_target_pairs={{0,24},{8,16},{16,8},{24,0},{1,25},{9,17},{17,9},{25,1},{2,26},{10... | collective-permute-start | bytes 798728 | tf_op jit(solution)/shard_map/exchange/ppermute | solution.py:205
  14.3 9.1 %collective-permute-start.4 = (bf16[528,128]{1,0:T(8,128)(2,1)S(1)}, bf16[528,128]{1,0:T(8,128)(2,1)S(1)}, u32[]{:S(2)}, u32[]{:S(2)}) collective-permute-start(bf16[528,128]{1,0:T(8,128)(2,1)S(1)} %collective-permute-done.3.q_ref), channel_id=1, source_target_pairs={{0,2},{1,3},{2,0},{3,1},{4,6},{5,7},{6,4},{7,5},{8,10},{9,11},{10,... | collective-permute-start | bytes 405512 | tf_op jit(solution)/shard_map/exchange/ppermute | solution.py:210
  15.0 12.4 %collective-permute-start.2 = (bf16[528,128]{1,0:T(8,128)(2,1)S(1)}, bf16[528,128]{1,0:T(8,128)(2,1)S(1)}, u32[]{:S(2)}, u32[]{:S(2)}) collective-permute-start(bf16[528,128]{1,0:T(8,128)(2,1)S(1)} %merge_q.1.q_ref), channel_id=1, source_target_pairs={{0,2},{1,3},{2,0},{3,1},{4,6},{5,7},{6,4},{7,5},{8,10},{9,11},{10,... | collective-permute-start | bytes 405512 | tf_op jit(solution)/shard_map/exchange/ppermute | solution.py:210
  24.6 7.5 %collective-permute-start.11 = (bf16[544,128]{1,0:T(8,128)(2,1)S(1)}, bf16[544,128]{1,0:T(8,128)(2,1)S(1)}, u32[]{:S(2)}, u32[]{:S(2)}) collective-permute-start(bf16[544,128]{1,0:T(8,128)(2,1)S(1)} %attend.4), channel_id=1, source_target_pairs={{0,2},{1,3},{2,0},{3,1},{4,6},{5,7},{6,4},{7,5},{8,10},{9,11},{10,... | collective-permute-start | bytes 417800 | tf_op jit(solution)/shard_map/return/ppermute | solution.py:251
  28.6 5.9 %collective-permute-start.14 = (bf16[272,128]{1,0:T(8,128)(2,1)S(1)}, bf16[272,128]{1,0:T(8,128)(2,1)S(1)}, u32[]{:S(2)}, u32[]{:S(2)}) collective-permute-start(bf16[272,128]{1,0:T(8,128)(2,1)S(1)} %get-tuple-element.18), channel_id=1, source_target_pairs={{0,2},{1,3},{2,0},{3,1},{4,6},{5,7},{6,4},{7,5},{8,10},{9,11},{10,... | collective-permute-start | bytes 208904 | tf_op jit(solution)/shard_map/return/ppermute | solution.py:249
  30.3 4.2 %collective-permute-start.10 = (bf16[272,128]{1,0:T(8,128)(2,1)S(1)}, bf16[272,128]{1,0:T(8,128)(2,1)S(1)}, u32[]{:S(2)}, u32[]{:S(2)}) collective-permute-start(bf16[272,128]{1,0:T(8,128)(2,1)S(1)} %get-tuple-element.21), channel_id=1, source_target_pairs={{0,1},{1,0},{2,3},{3,2},{4,5},{5,4},{6,7},{7,6},{8,9},{9,8},{10,11... | collective-permute-start | bytes 208904 | tf_op jit(solution)/shard_map/return/ppermute | solution.py:265
  30.4 4.2 %collective-permute-start.15 = (bf16[272,128]{1,0:T(8,128)(2,1)S(1)}, bf16[272,128]{1,0:T(8,128)(2,1)S(1)}, u32[]{:S(2)}, u32[]{:S(2)}) collective-permute-start(bf16[272,128]{1,0:T(8,128)(2,1)S(1)} %get-tuple-element.24), channel_id=1, source_target_pairs={{0,3},{1,2},{2,1},{3,0},{4,7},{5,6},{6,5},{7,4},{8,11},{9,10},{10,... | collective-permute-start | bytes 208904 | tf_op jit(solution)/shard_map/return/ppermute | solution.py:249
  32.2 8.1 %collective-permute-start.12 = (bf16[272,128]{1,0:T(8,128)(2,1)S(1)}, bf16[272,128]{1,0:T(8,128)(2,1)S(1)}, u32[]{:S(2)}, u32[]{:S(2)}) collective-permute-start(bf16[272,128]{1,0:T(8,128)(2,1)S(1)} %get-tuple-element.22), channel_id=1, source_target_pairs={{0,4},{1,5},{2,6},{3,7},{4,0},{5,1},{6,2},{7,3},{8,12},{9,13},{10,... | collective-permute-start | bytes 208904 | tf_op jit(solution)/shard_map/return/ppermute | solution.py:249
  32.6 9.0 %collective-permute-start.13 = (bf16[272,128]{1,0:T(8,128)(2,1)S(1)}, bf16[272,128]{1,0:T(8,128)(2,1)S(1)}, u32[]{:S(2)}, u32[]{:S(2)}) collective-permute-start(bf16[272,128]{1,0:T(8,128)(2,1)S(1)} %get-tuple-element.23), channel_id=1, source_target_pairs={{0,5},{1,4},{2,7},{3,6},{4,1},{5,0},{6,3},{7,2},{8,13},{9,12},{10,... | collective-permute-start | bytes 208904 | tf_op jit(solution)/shard_map/return/ppermute | solution.py:249

commit v9 on v8

--- a/solution.py
+++ b/solution.py
@@ -55,21 +55,20 @@
     place(own.at[2 * tok : 3 * tok, :], v1, out, rows + PAD, turned=True)
 
 
-def attend_kernel(wide, where, q_ref, *refs):
-    n = 1 + max(w[2] for w in where)
-    kv_refs, out_refs = refs[:n], refs[n:]
+def attend_kernel(wide, same, q_ref, *refs):
+    nk = len(refs) - (1 if wide else CORES)
+    kv_refs, out_refs = refs[:nk], refs[nk:]
     size = q_ref.shape[1]
     tok = size
     both = CORES * tok
     half = PAD // CORES
     block = PER * size + PAD
     rate = size ** -0.5 * math.log2(math.e)
-    rows = lax.broadcasted_iota(jnp.int32, (tok, both), 0).astype(F32)
-    lanes = lax.broadcasted_iota(jnp.int32, (1, tok), 1).astype(F32)
-
-    def start_of(ref, at):
+    at_or_before = lax.broadcasted_iota(jnp.int32, (tok, tok), 0) <= lax.broadcasted_iota(jnp.int32, (tok, tok), 1)
+
+    def block_of(ref, at):
         first = ref[at : at + PAD, :].astype(F32)
-        return [first[b * half : b * half + 1, :] * tok for b in range(CORES)]
+        return [first[b * half : b * half + 1, :] for b in range(CORES)]
 
     def store(b, at, value):
         if wide:
@@ -77,24 +76,31 @@
         else:
             out_refs[b][at : at + value.shape[0], :] = value
 
-    qpos = jnp.concatenate([s + lanes for s in start_of(q_ref, PER * both)], axis=1)
-    limits = []
-    for k, k_at, _, _ in where:
-        for s in start_of(kv_refs[k], k_at + PER * both):
-            limits.append(qpos - jnp.concatenate([s] * CORES, axis=1))
+    q_block = jnp.concatenate(block_of(q_ref, PER * both), axis=1)
+    kept = [
+        jnp.concatenate([p] * CORES, axis=1) <= q_block for ref in kv_refs for p in block_of(ref, PER * both)
+    ]
     stats = [[] for _ in range(CORES)]
     for h in range(PER):
         q = q_ref[h * both : (h + 1) * both, :]
-        parts, vals = [], []
-        for j, (k, k_at, v, v_at) in enumerate(where):
-            s = nt_dot(kv_refs[k][k_at + h * both : k_at + (h + 1) * both, :], q)
+        scores, vals = [], []
+        for j, ref in enumerate(kv_refs):
+            s = nt_dot(ref[h * both : (h + 1) * both, :], q)
             for b in range(CORES):
-                parts.append(jnp.where(rows <= limits[j * CORES + b], s[b * tok : (b + 1) * tok, :], LOW))
-                at = v_at + h * both + b * tok
-                vals.append(kv_refs[v][at : at + tok, :])
-        s = jnp.concatenate(parts, axis=0)
-        top = jnp.maximum(jnp.max(s, axis=0, keepdims=True), FLOOR).astype(BF16)
-        p = jnp.exp2((s - top.astype(F32)) * rate).astype(BF16)
+                part = s[b * tok : (b + 1) * tok, :]
+                if same and j == 0:
+                    cols = [part[:, c * tok : (c + 1) * tok] for c in range(CORES)]
+                    cols[b] = jnp.where(at_or_before, cols[b], LOW)
+                    part = jnp.concatenate(cols, axis=1)
+                scores.append(part)
+                at = PAD + (PER + h) * both + b * tok
+                vals.append(ref[at : at + tok, :])
+        tops = [jnp.where(k, jnp.max(s, axis=0, keepdims=True), FLOOR) for k, s in zip(kept, scores)]
+        top = jnp.maximum(functools.reduce(jnp.maximum, tops), FLOOR).astype(BF16)
+        shift = top.astype(F32)
+        p = jnp.concatenate(
+            [jnp.exp2((s - jnp.where(k, shift, -LOW)) * rate).astype(BF16) for k, s in zip(kept, scores)], axis=0
+        )
         vt = jnp.concatenate(vals, axis=1)
         vt = jnp.concatenate([vt, jnp.ones((PAD, vt.shape[1]), BF16)], axis=0)
         o = jnp.dot(vt, p, preferred_element_type=F32)
@@ -104,7 +110,7 @@
         for b in range(CORES):
             cols = slice(b * tok, (b + 1) * tok)
             store(b, h * size, o[0:size, cols].astype(BF16))
-            stats[b] += [top[:, cols].astype(F32), hi[:, cols].astype(F32), lo[:, cols].astype(F32)]
+            stats[b] += [shift[:, cols], hi[:, cols].astype(F32), lo[:, cols].astype(F32)]
     for b in range(CORES):
         rest = jnp.zeros((PAD - 3 * PER, tok), F32)
         store(b, PER * size, jnp.concatenate(stats[b] + [rest], axis=0).astype(BF16))
@@ -151,7 +157,7 @@
         for h in range(PER):
             _, total, numer = joined([part[h * size : (h + 1) * size, :] for part in mine], stats, h, rate)
             cols = pl.ds(pl.multiple_of((pair * PER + h) * size, size), size)
-            out_ref[:, cols] = (numer / total).T.astype(BF16)
+            out_ref[:, cols] = (numer * (1.0 / total)).T.astype(BF16)
 
 
 def vmem(n=1):
@@ -192,7 +198,6 @@
             compiler_params=params,
             name="merge_kv",
         )(block_pos, other[3], own, after(other[1], q_piece), other[2])
-    half = PER * both + PAD
     block = PER * size + PAD
 
     def low(r):
@@ -209,8 +214,6 @@
             for r in sorted(q_by):
                 q_by[r | bit] = lax.ppermute(q_by[r], "inner", along_inner(bit, 0))
             bit //= 2
-    where = tuple((r, 0, r, half) for r in range(n_out))
-
     def shapes(wide):
         rows = CORES * block if wide else block
         return (jax.ShapeDtypeStruct((rows, tok), BF16),) * (1 if wide else CORES)
@@ -220,7 +223,7 @@
         work = 4 * PER * both * n_out * both * size
         with jax.named_scope("attend"):
             return pl.pallas_call(
-                functools.partial(attend_kernel, wide, where),
+                functools.partial(attend_kernel, wide, r == 0),
                 out_shape=shapes(wide),
                 in_specs=vmem(1 + len(kv)),
                 out_specs=tuple(vmem(len(shapes(wide)))),

time: 42.5 us -> 42.3 us (level)
  no operation moved by 1% of the time
where the time goes in v9:
time: 42.3 us; the launch traced here: 42.1 us
  starting transfers between devices  17 us (40%)
  waiting for transfers between devices  16.5 us (39%)
  Pallas kernels  6.65 us (16%)
  local copies, waits for them, and re-layouts  1.15 us (3%)
  between operations  0.81 us (2%)
    ppermute x3, waiting for transfers between devices, shards(): lax.ppermute(kv_piece, 'outer', [(o, o ^ r) for o in range(n_out)])  7.04 us
    ppermute x4, waiting for transfers between devices, send(): lax.ppermute(parts[x], 'inner', along_inner(r, x))  7.01 us
    ppermute x3, starting transfers between devices, shards(): q_by[r | bit] = lax.ppermute(q_by[r], 'inner', along_inner(bit, 0))  6.12 us
    ppermute x4, starting transfers between devices, send(): lax.ppermute(parts[x], 'inner', along_inner(r, x))  4.58 us
    pallas_call x4, Pallas kernels, attend(): pl.pallas_call(functools.partial(attend_kernel, wide, r == 0), out_shape=...  4.45 us
    ppermute x3, starting transfers between devices, shards(): lax.ppermute(kv_piece, 'outer', [(o, o ^ r) for o in range(n_out)])  3.55 us
    ppermute x3, waiting for transfers between devices, shards(): q_by[r | bit] = lax.ppermute(q_by[r], 'inner', along_inner(bit, 0))  2.45 us
    ppermute x1, starting transfers between devices, send(): lax.ppermute(parts[0], 'inner', along_inner(low(r), 0))  1.64 us
  transfers between devices with their start and end apart: 16, of which 5 were waited for; matrix products, arithmetic and copies ran while one was open for 2% of the time, Pallas kernels for 14%

profile of v9, /device:TPU:0, one launch (start us, length us, event | category | flops | bytes accessed | tf_op | source)
XLA Modules:
  0.0 42.1 jit_solution(3471607053383663694)
XLA Ops:
  0.0 0.0 copy-start
  0.0 0.5 %collective-permute-start = (s32[1]{0:T(128)}, s32[1]{0:T(128)}, u32[]{:S(2)}, u32[]{:S(2)}) collective-permute-start(s32[1]{0:T(128)} %param.7), channel_id=1, source_target_pairs={{0,1},{1,0},{2,3},{3,2},{4,5},{5,4},{6,7},{7,6},{8,9},{9,8},{10,11... | collective-permute-start | bytes 20 | tf_op jit(solution)/shard_map/swap/ppermute | solution.py:181
  0.5 0.1 collective-permute-start.1
  0.5 0.4 %collective-permute-start.5 = (bf16[128,512]{1,0:T(8,128)(2,1)}, bf16[128,512]{1,0:T(8,128)(2,1)S(1)}, u32[]{:S(2)}, u32[]{:S(2)}) collective-permute-start(bf16[128,512]{1,0:T(8,128)(2,1)} %param.5), channel_id=1, source_target_pairs={{0,1},{1,0},{2,3},{3,2},{4,5},{5,4},{6,7},{7,6},{8,9},{9,8},{10,11... | collective-permute-start | bytes 393224 | tf_op jit(solution)/shard_map/swap/ppermute | solution.py:181
  1.0 0.1 collective-permute-start.6
  1.0 0.9 %constant_dynamic-update-slice_fusion.2 = bf16[384,512]{1,0:T(8,128)(2,1)S(1)} fusion(bf16[128,512]{1,0:T(8,128)(2,1)} %param.4), kind=kLoop, calls=%fused_computation.2 | loop fusion | bytes 262144
  1.9 0.0 copy-done
  2.0 0.0 copy-start.1
  2.7 0.2 copy-done.1
  2.9 0.0 collective-permute-done.p1
  2.9 0.0 collective-permute-done.1.q1
  2.9 0.6 %merge_q.1.q_ref = bf16[528,128]{1,0:T(8,128)(2,1)S(1)} custom-call(s32[1]{0:T(128)S(6)} %copy.7.p0, s32[1]{0:T(128)} %collective-permute-done.p1, bf16[384,512]{1,0:T(8,128)(2,1)S(1)} %constant_dynamic-update-slice_fusion.own, bf16[128,512]{1,0:T(8,128)(2,1)S(1)} %collective-permute-done.1.q1), custom_call_target="tpu_custom_call" | custom-call | tf_op jit(solution)/shard_map/merge/merge_q/pallas_call | solution.py:185
  3.5 4.1 %collective-permute-start.3 = (bf16[528,128]{1,0:T(8,128)(2,1)S(1)}, bf16[528,128]{1,0:T(8,128)(2,1)S(1)}, u32[]{:S(2)}, u32[]{:S(2)}) collective-permute-start(bf16[528,128]{1,0:T(8,128)(2,1)S(1)} %merge_q.1.q_ref), channel_id=1, source_target_pairs={{0,4},{1,5},{2,6},{3,7},{4,0},{5,1},{6,2},{7,3},{8,12},{9,13},{10,... | collective-permute-start | bytes 405512 | tf_op jit(solution)/shard_map/exchange/ppermute | solution.py:215
  7.6 0.0 collective-permute-done.5.k1
  7.6 0.0 collective-permute-done.6.v1
  7.6 0.7 %merge_kv.1.refs_0_ = bf16[1040,128]{1,0:T(8,128)(2,1)S(1)} custom-call(s32[1]{0:T(128)S(6)} %copy.7.p0, s32[1]{0:T(128)} %collective-permute-done.p1, bf16[384,512]{1,0:T(8,128)(2,1)S(1)} %constant_dynamic-update-slice_fusion.own, bf16[128,512]{1,0:T(8,128)(2,1)S(1)} %collective-permute-done.5.k1, bf16[128,512]{1,0:T(8,128)(2,1)S(1)} %collective-permute-done.6.v1), custom_call_target="tpu_custom_call" | custom-call | tf_op jit(solution)/shard_map/merge/merge_kv/pallas_call | solution.py:193
  8.3 1.6 %collective-permute-start.7 = (bf16[1040,128]{1,0:T(8,128)(2,1)S(1)}, bf16[1040,128]{1,0:T(8,128)(2,1)S(1)}, u32[]{:S(2)}, u32[]{:S(2)}) collective-permute-start(bf16[1040,128]{1,0:T(8,128)(2,1)S(1)} %merge_kv.1.refs_0_), channel_id=1, source_target_pairs={{0,8},{8,0},{16,24},{24,16},{1,9},{9,1},{17,25},{25,17},{2,10},{10... | collective-permute-start | bytes 798728 | tf_op jit(solution)/shard_map/exchange/ppermute | solution.py:210
  9.9 1.5 %collective-permute-start.8 = (bf16[1040,128]{1,0:T(8,128)(2,1)S(1)}, bf16[1040,128]{1,0:T(8,128)(2,1)S(1)}, u32[]{:S(2)}, u32[]{:S(2)}) collective-permute-start(bf16[1040,128]{1,0:T(8,128)(2,1)S(1)} %merge_kv.1.refs_0_), channel_id=1, source_target_pairs={{0,16},{8,24},{16,0},{24,8},{1,17},{9,25},{17,1},{25,9},{2,18},{10... | collective-permute-start | bytes 798728 | tf_op jit(solution)/shard_map/exchange/ppermute | solution.py:210
  11.4 0.5 %collective-permute-start.9 = (bf16[1040,128]{1,0:T(8,128)(2,1)S(1)}, bf16[1040,128]{1,0:T(8,128)(2,1)S(1)}, u32[]{:S(2)}, u32[]{:S(2)}) collective-permute-start(bf16[1040,128]{1,0:T(8,128)(2,1)S(1)} %merge_kv.1.refs_0_), channel_id=1, source_target_pairs={{0,24},{8,16},{16,8},{24,0},{1,25},{9,17},{17,9},{25,1},{2,26},{10... | collective-permute-start | bytes 798728 | tf_op jit(solution)/shard_map/exchange/ppermute | solution.py:210
  11.9 2.4 %collective-permute-done.3.q_ref = bf16[528,128]{1,0:T(8,128)(2,1)S(1)} collective-permute-done((bf16[528,128]{1,0:T(8,128)(2,1)S(1)}, bf16[528,128]{1,0:T(8,128)(2,1)S(1)}, u32[]{:S(2)}, u32[]{:S(2)}) %collective-permute-start.3) | collective-permute-done | bytes 135200 | tf_op jit(solution)/shard_map/exchange/ppermute | solution.py:215
  14.3 0.7 %collective-permute-start.4 = (bf16[528,128]{1,0:T(8,128)(2,1)S(1)}, bf16[528,128]{1,0:T(8,128)(2,1)S(1)}, u32[]{:S(2)}, u32[]{:S(2)}) collective-permute-start(bf16[528,128]{1,0:T(8,128)(2,1)S(1)} %collective-permute-done.3.q_ref), channel_id=1, source_target_pairs={{0,2},{1,3},{2,0},{3,1},{4,6},{5,7},{6,4},{7,5},{8,10},{9,11},{10,... | collective-permute-start | bytes 405512 | tf_op jit(solution)/shard_map/exchange/ppermute | solution.py:215
  15.0 1.3 %collective-permute-start.2 = (bf16[528,128]{1,0:T(8,128)(2,1)S(1)}, bf16[528,128]{1,0:T(8,128)(2,1)S(1)}, u32[]{:S(2)}, u32[]{:S(2)}) collective-permute-start(bf16[528,128]{1,0:T(8,128)(2,1)S(1)} %merge_q.1.q_ref), channel_id=1, source_target_pairs={{0,2},{1,3},{2,0},{3,1},{4,6},{5,7},{6,4},{7,5},{8,10},{9,11},{10,... | collective-permute-start | bytes 405512 | tf_op jit(solution)/shard_map/exchange/ppermute | solution.py:215
  16.3 1.3 %collective-permute-done.7.refs_1_ = bf16[1040,128]{1,0:T(8,128)(2,1)S(1)} collective-permute-done((bf16[1040,128]{1,0:T(8,128)(2,1)S(1)}, bf16[1040,128]{1,0:T(8,128)(2,1)S(1)}, u32[]{:S(2)}, u32[]{:S(2)}) %collective-permute-start.7) | collective-permute-done | bytes 266272 | tf_op jit(solution)/shard_map/exchange/ppermute | solution.py:210
  17.7 5.7 %collective-permute-done.8.refs_2_ = bf16[1040,128]{1,0:T(8,128)(2,1)S(1)} collective-permute-done((bf16[1040,128]{1,0:T(8,128)(2,1)S(1)}, bf16[1040,128]{1,0:T(8,128)(2,1)S(1)}, u32[]{:S(2)}, u32[]{:S(2)}) %collective-permute-start.8) | collective-permute-done | bytes 266272 | tf_op jit(solution)/shard_map/exchange/ppermute | solution.py:210
  23.4 0.0 collective-permute-done.9.refs_3_
  23.4 0.0 collective-permute-done.4.q_ref
  23.4 1.1 %attend.4 = bf16[544,128]{1,0:T(8,128)(2,1)S(1)} custom-call(bf16[528,128]{1,0:T(8,128)(2,1)S(1)} %collective-permute-done.4.q_ref, bf16[1040,128]{1,0:T(8,128)(2,1)S(1)} %merge_kv.1.refs_0_, bf16[1040,128]{1,0:T(8,128)(2,1)S(1)} %collective-permute-done.7.refs_1_, bf16[1040,128]{1,0:T(8,128)(2,1)S(1)} %collective-permute-done.8.refs_2_, ...), custom_call_target="tpu_custom_call" | custom-call | flops 268435456 | bytes 1048576 | tf_op jit(solution)/shard_map/attend/attend/pallas_call | solution.py:225
  24.5 1.6 %collective-permute-start.11 = (bf16[544,128]{1,0:T(8,128)(2,1)S(1)}, bf16[544,128]{1,0:T(8,128)(2,1)S(1)}, u32[]{:S(2)}, u32[]{:S(2)}) collective-permute-start(bf16[544,128]{1,0:T(8,128)(2,1)S(1)} %attend.4), channel_id=1, source_target_pairs={{0,2},{1,3},{2,0},{3,1},{4,6},{5,7},{6,4},{7,5},{8,10},{9,11},{10,... | collective-permute-start | bytes 417800 | tf_op jit(solution)/shard_map/return/ppermute | solution.py:254
  26.1 1.1 %attend.5.refs_0_ = bf16[544,128]{1,0:T(8,128)(2,1)S(1)} custom-call(bf16[528,128]{1,0:T(8,128)(2,1)S(1)} %collective-permute-done.3.q_ref, bf16[1040,128]{1,0:T(8,128)(2,1)S(1)} %merge_kv.1.refs_0_, bf16[1040,128]{1,0:T(8,128)(2,1)S(1)} %collective-permute-done.7.refs_1_, bf16[1040,128]{1,0:T(8,128)(2,1)S(1)} %collective-permute-done.8.refs_2_, ...), custom_call_target="tpu_custom_call" | custom-call | flops 268435456 | bytes 1048576 | tf_op jit(solution)/shard_map/attend/attend/pallas_call | solution.py:225
  27.3 0.0 collective-permute-done.2.q_ref
  27.3 1.1 %attend.6 = (bf16[272,128]{1,0:T(8,128)(2,1)S(1)}, bf16[272,128]{1,0:T(8,128)(2,1)S(1)}) custom-call(bf16[528,128]{1,0:T(8,128)(2,1)S(1)} %collective-permute-done.2.q_ref, bf16[1040,128]{1,0:T(8,128)(2,1)S(1)} %merge_kv.1.refs_0_, bf16[1040,128]{1,0:T(8,128)(2,1)S(1)} %collective-permute-done.7.refs_1_, ...), custom_call_target="tpu_custom_call" | custom-call | flops 268435456 | bytes 1048576 | tf_op jit(solution)/shard_map/attend/attend/pallas_call | solution.py:225
  28.4 0.5 %collective-permute-start.14 = (bf16[272,128]{1,0:T(8,128)(2,1)S(1)}, bf16[272,128]{1,0:T(8,128)(2,1)S(1)}, u32[]{:S(2)}, u32[]{:S(2)}) collective-permute-start(bf16[272,128]{1,0:T(8,128)(2,1)S(1)} %get-tuple-element.18), channel_id=1, source_target_pairs={{0,2},{1,3},{2,0},{3,1},{4,6},{5,7},{6,4},{7,5},{8,10},{9,11},{10,... | collective-permute-start | bytes 208904 | tf_op jit(solution)/shard_map/return/ppermute | solution.py:252
  28.9 1.1 %attend.7 = (bf16[272,128]{1,0:T(8,128)(2,1)S(1)}, bf16[272,128]{1,0:T(8,128)(2,1)S(1)}) custom-call(bf16[528,128]{1,0:T(8,128)(2,1)S(1)} %merge_q.1.q_ref, bf16[1040,128]{1,0:T(8,128)(2,1)S(1)} %merge_kv.1.refs_0_, bf16[1040,128]{1,0:T(8,128)(2,1)S(1)} %collective-permute-done.7.refs_1_, bf16[1040,128]{1,0:T(8,128)(2,1)S(1)} %collective-permute-done.8.refs_2_, ...), custom_call_target="tpu_custom_call" | custom-call | flops 268435456 | bytes 1048576 | tf_op jit(solution)/shard_map/attend/attend/pallas_call | solution.py:225
  30.0 0.1 collective-permute-start.10
  30.1 1.7 %collective-permute-start.15 = (bf16[272,128]{1,0:T(8,128)(2,1)S(1)}, bf16[272,128]{1,0:T(8,128)(2,1)S(1)}, u32[]{:S(2)}, u32[]{:S(2)}) collective-permute-start(bf16[272,128]{1,0:T(8,128)(2,1)S(1)} %get-tuple-element.24), channel_id=1, source_target_pairs={{0,3},{1,2},{2,1},{3,0},{4,7},{5,6},{6,5},{7,4},{8,11},{9,10},{10,... | collective-permute-start | bytes 208904 | tf_op jit(solution)/shard_map/return/ppermute | solution.py:252
  31.8 0.0 collective-permute-done.11.refs_1_
  31.8 0.1 add.1
  31.9 0.4 collective-permute-start.12
  32.3 2.0 %collective-permute-start.13 = (bf16[272,128]{1,0:T(8,128)(2,1)S(1)}, bf16[272,128]{1,0:T(8,128)(2,1)S(1)}, u32[]{:S(2)}, u32[]{:S(2)}) collective-permute-start(bf16[272,128]{1,0:T(8,128)(2,1)S(1)} %get-tuple-element.23), channel_id=1, source_target_pairs={{0,5},{1,4},{2,7},{3,6},{4,1},{5,0},{6,3},{7,2},{8,13},{9,12},{10,... | collective-permute-start | bytes 208904 | tf_op jit(solution)/shard_map/return/ppermute | solution.py:252
  34.3 0.0 collective-permute-done.10.refs_1_
  34.3 0.0 collective-permute-done.14.refs_4_
  34.3 0.0 collective-permute-done.15.refs_5_
  34.3 5.6 %collective-permute-done.12.refs_2_ = bf16[272,128]{1,0:T(8,128)(2,1)S(1)} collective-permute-done((bf16[272,128]{1,0:T(8,128)(2,1)S(1)}, bf16[272,128]{1,0:T(8,128)(2,1)S(1)}, u32[]{:S(2)}, u32[]{:S(2)}) %collective-permute-start.12) | collective-permute-done | bytes 69664 | tf_op jit(solution)/shard_map/return/ppermute | solution.py:252
  40.0 1.3 %collective-permute-done.13.refs_3_ = bf16[272,128]{1,0:T(8,128)(2,1)S(1)} collective-permute-done((bf16[272,128]{1,0:T(8,128)(2,1)S(1)}, bf16[272,128]{1,0:T(8,128)(2,1)S(1)}, u32[]{:S(2)}, u32[]{:S(2)}) %collective-permute-start.13) | collective-permute-done | bytes 69664 | tf_op jit(solution)/shard_map/return/ppermute | solution.py:252
  41.3 0.8 %combine.1 = bf16[128,512]{1,0:T(8,128)(2,1)} custom-call(bf16[272,128]{1,0:T(8,128)(2,1)S(1)} %get-tuple-element.20.refs_0_, bf16[272,128]{1,0:T(8,128)(2,1)S(1)} %collective-permute-done.10.refs_1_, bf16[272,128]{1,0:T(8,128)(2,1)S(1)} %collective-permute-done.12.refs_2_, bf16[272,128]{1,0:T(8,128)(2,1)S(1)} %collective-permute-done.13.refs_3_, ...), custom_call_target="tpu_custom_call" | custom-call | tf_op jit(solution)/shard_map/combine/combine/pallas_call | solution.py:270
  (2 shorter events, 0.0 us)
Async XLA Ops:
  0.0 1.9 %copy-start = (bf16[128,512]{1,0:T(8,128)(2,1)S(1)}, bf16[128,512]{1,0:T(8,128)(2,1)}, u32[]{:S(2)}) copy-start(bf16[128,512]{1,0:T(8,128)(2,1)} %param.5) | copy-start | bytes 393220
  0.0 2.9 %collective-permute-start = (s32[1]{0:T(128)}, s32[1]{0:T(128)}, u32[]{:S(2)}, u32[]{:S(2)}) collective-permute-start(s32[1]{0:T(128)} %param.7), channel_id=1, source_target_pairs={{0,1},{1,0},{2,3},{3,2},{4,5},{5,4},{6,7},{7,6},{8,9},{9,8},{10,11... | collective-permute-start | bytes 20 | tf_op jit(solution)/shard_map/swap/ppermute | solution.py:181
  0.5 2.5 %collective-permute-start.1 = (bf16[128,512]{1,0:T(8,128)(2,1)}, bf16[128,512]{1,0:T(8,128)(2,1)S(1)}, u32[]{:S(2)}, u32[]{:S(2)}) collective-permute-start(bf16[128,512]{1,0:T(8,128)(2,1)} %param.4), channel_id=1, source_target_pairs={{0,1},{1,0},{2,3},{3,2},{4,5},{5,4},{6,7},{7,6},{8,9},{9,8},{10,11... | collective-permute-start | bytes 393224 | tf_op jit(solution)/shard_map/swap/ppermute | solution.py:181
  0.5 7.1 %collective-permute-start.5 = (bf16[128,512]{1,0:T(8,128)(2,1)}, bf16[128,512]{1,0:T(8,128)(2,1)S(1)}, u32[]{:S(2)}, u32[]{:S(2)}) collective-permute-start(bf16[128,512]{1,0:T(8,128)(2,1)} %param.5), channel_id=1, source_target_pairs={{0,1},{1,0},{2,3},{3,2},{4,5},{5,4},{6,7},{7,6},{8,9},{9,8},{10,11... | collective-permute-start | bytes 393224 | tf_op jit(solution)/shard_map/swap/ppermute | solution.py:181
  1.0 6.7 %collective-permute-start.6 = (bf16[128,512]{1,0:T(8,128)(2,1)}, bf16[128,512]{1,0:T(8,128)(2,1)S(1)}, u32[]{:S(2)}, u32[]{:S(2)}) collective-permute-start(bf16[128,512]{1,0:T(8,128)(2,1)} %param.6), channel_id=1, source_target_pairs={{0,1},{1,0},{2,3},{3,2},{4,5},{5,4},{6,7},{7,6},{8,9},{9,8},{10,11... | collective-permute-start | bytes 393224 | tf_op jit(solution)/shard_map/swap/ppermute | solution.py:181
  2.0 0.9 %copy-start.1 = (bf16[128,512]{1,0:T(8,128)(2,1)S(1)}, bf16[128,512]{1,0:T(8,128)(2,1)}, u32[]{:S(2)}) copy-start(bf16[128,512]{1,0:T(8,128)(2,1)} %param.6) | copy-start | bytes 393220
  3.5 10.8 %collective-permute-start.3 = (bf16[528,128]{1,0:T(8,128)(2,1)S(1)}, bf16[528,128]{1,0:T(8,128)(2,1)S(1)}, u32[]{:S(2)}, u32[]{:S(2)}) collective-permute-start(bf16[528,128]{1,0:T(8,128)(2,1)S(1)} %merge_q.1.q_ref), channel_id=1, source_target_pairs={{0,4},{1,5},{2,6},{3,7},{4,0},{5,1},{6,2},{7,3},{8,12},{9,13},{10,... | collective-permute-start | bytes 405512 | tf_op jit(solution)/shard_map/exchange/ppermute | solution.py:215
  8.3 9.4 %collective-permute-start.7 = (bf16[1040,128]{1,0:T(8,128)(2,1)S(1)}, bf16[1040,128]{1,0:T(8,128)(2,1)S(1)}, u32[]{:S(2)}, u32[]{:S(2)}) collective-permute-start(bf16[1040,128]{1,0:T(8,128)(2,1)S(1)} %merge_kv.1.refs_0_), channel_id=1, source_target_pairs={{0,8},{8,0},{16,24},{24,16},{1,9},{9,1},{17,25},{25,17},{2,10},{10... | collective-permute-start | bytes 798728 | tf_op jit(solution)/shard_map/exchange/ppermute | solution.py:210
  9.9 13.5 %collective-permute-start.8 = (bf16[1040,128]{1,0:T(8,128)(2,1)S(1)}, bf16[1040,128]{1,0:T(8,128)(2,1)S(1)}, u32[]{:S(2)}, u32[]{:S(2)}) collective-permute-start(bf16[1040,128]{1,0:T(8,128)(2,1)S(1)} %merge_kv.1.refs_0_), channel_id=1, source_target_pairs={{0,16},{8,24},{16,0},{24,8},{1,17},{9,25},{17,1},{25,9},{2,18},{10... | collective-permute-start | bytes 798728 | tf_op jit(solution)/shard_map/exchange/ppermute | solution.py:210
  11.4 12.0 %collective-permute-start.9 = (bf16[1040,128]{1,0:T(8,128)(2,1)S(1)}, bf16[1040,128]{1,0:T(8,128)(2,1)S(1)}, u32[]{:S(2)}, u32[]{:S(2)}) collective-permute-start(bf16[1040,128]{1,0:T(8,128)(2,1)S(1)} %merge_kv.1.refs_0_), channel_id=1, source_target_pairs={{0,24},{8,16},{16,8},{24,0},{1,25},{9,17},{17,9},{25,1},{2,26},{10... | collective-permute-start | bytes 798728 | tf_op jit(solution)/shard_map/exchange/ppermute | solution.py:210
  14.3 9.1 %collective-permute-start.4 = (bf16[528,128]{1,0:T(8,128)(2,1)S(1)}, bf16[528,128]{1,0:T(8,128)(2,1)S(1)}, u32[]{:S(2)}, u32[]{:S(2)}) collective-permute-start(bf16[528,128]{1,0:T(8,128)(2,1)S(1)} %collective-permute-done.3.q_ref), channel_id=1, source_target_pairs={{0,2},{1,3},{2,0},{3,1},{4,6},{5,7},{6,4},{7,5},{8,10},{9,11},{10,... | collective-permute-start | bytes 405512 | tf_op jit(solution)/shard_map/exchange/ppermute | solution.py:215
  15.0 12.2 %collective-permute-start.2 = (bf16[528,128]{1,0:T(8,128)(2,1)S(1)}, bf16[528,128]{1,0:T(8,128)(2,1)S(1)}, u32[]{:S(2)}, u32[]{:S(2)}) collective-permute-start(bf16[528,128]{1,0:T(8,128)(2,1)S(1)} %merge_q.1.q_ref), channel_id=1, source_target_pairs={{0,2},{1,3},{2,0},{3,1},{4,6},{5,7},{6,4},{7,5},{8,10},{9,11},{10,... | collective-permute-start | bytes 405512 | tf_op jit(solution)/shard_map/exchange/ppermute | solution.py:215
  24.5 7.3 %collective-permute-start.11 = (bf16[544,128]{1,0:T(8,128)(2,1)S(1)}, bf16[544,128]{1,0:T(8,128)(2,1)S(1)}, u32[]{:S(2)}, u32[]{:S(2)}) collective-permute-start(bf16[544,128]{1,0:T(8,128)(2,1)S(1)} %attend.4), channel_id=1, source_target_pairs={{0,2},{1,3},{2,0},{3,1},{4,6},{5,7},{6,4},{7,5},{8,10},{9,11},{10,... | collective-permute-start | bytes 417800 | tf_op jit(solution)/shard_map/return/ppermute | solution.py:254
  28.4 5.9 %collective-permute-start.14 = (bf16[272,128]{1,0:T(8,128)(2,1)S(1)}, bf16[272,128]{1,0:T(8,128)(2,1)S(1)}, u32[]{:S(2)}, u32[]{:S(2)}) collective-permute-start(bf16[272,128]{1,0:T(8,128)(2,1)S(1)} %get-tuple-element.18), channel_id=1, source_target_pairs={{0,2},{1,3},{2,0},{3,1},{4,6},{5,7},{6,4},{7,5},{8,10},{9,11},{10,... | collective-permute-start | bytes 208904 | tf_op jit(solution)/shard_map/return/ppermute | solution.py:252
  30.0 4.2 %collective-permute-start.10 = (bf16[272,128]{1,0:T(8,128)(2,1)S(1)}, bf16[272,128]{1,0:T(8,128)(2,1)S(1)}, u32[]{:S(2)}, u32[]{:S(2)}) collective-permute-start(bf16[272,128]{1,0:T(8,128)(2,1)S(1)} %get-tuple-element.21), channel_id=1, source_target_pairs={{0,1},{1,0},{2,3},{3,2},{4,5},{5,4},{6,7},{7,6},{8,9},{9,8},{10,11... | collective-permute-start | bytes 208904 | tf_op jit(solution)/shard_map/return/ppermute | solution.py:268
  30.1 4.2 %collective-permute-start.15 = (bf16[272,128]{1,0:T(8,128)(2,1)S(1)}, bf16[272,128]{1,0:T(8,128)(2,1)S(1)}, u32[]{:S(2)}, u32[]{:S(2)}) collective-permute-start(bf16[272,128]{1,0:T(8,128)(2,1)S(1)} %get-tuple-element.24), channel_id=1, source_target_pairs={{0,3},{1,2},{2,1},{3,0},{4,7},{5,6},{6,5},{7,4},{8,11},{9,10},{10,... | collective-permute-start | bytes 208904 | tf_op jit(solution)/shard_map/return/ppermute | solution.py:252
  31.9 8.1 %collective-permute-start.12 = (bf16[272,128]{1,0:T(8,128)(2,1)S(1)}, bf16[272,128]{1,0:T(8,128)(2,1)S(1)}, u32[]{:S(2)}, u32[]{:S(2)}) collective-permute-start(bf16[272,128]{1,0:T(8,128)(2,1)S(1)} %get-tuple-element.22), channel_id=1, source_target_pairs={{0,4},{1,5},{2,6},{3,7},{4,0},{5,1},{6,2},{7,3},{8,12},{9,13},{10,... | collective-permute-start | bytes 208904 | tf_op jit(solution)/shard_map/return/ppermute | solution.py:252
  32.3 9.0 %collective-permute-start.13 = (bf16[272,128]{1,0:T(8,128)(2,1)S(1)}, bf16[272,128]{1,0:T(8,128)(2,1)S(1)}, u32[]{:S(2)}, u32[]{:S(2)}) collective-permute-start(bf16[272,128]{1,0:T(8,128)(2,1)S(1)} %get-tuple-element.23), channel_id=1, source_target_pairs={{0,5},{1,4},{2,7},{3,6},{4,1},{5,0},{6,3},{7,2},{8,13},{9,12},{10,... | collective-permute-start | bytes 208904 | tf_op jit(solution)/shard_map/return/ppermute | solution.py:252

commit v10 on v9

--- a/solution.py
+++ b/solution.py
@@ -47,44 +47,33 @@
     out[rows:, :] = starts(p0, p1, out.shape[1])
 
 
-def merge_kv_kernel(p0, p1, own, k1, v1, out):
+def merge_kv_kernel(p0, p1, own, k1, v1, k_out, v_out):
     tok = k1.shape[0]
     rows = PER * CORES * tok
-    place(own.at[tok : 2 * tok, :], k1, out, 0)
-    out[rows : rows + PAD, :] = starts(p0, p1, out.shape[1])
-    place(own.at[2 * tok : 3 * tok, :], v1, out, rows + PAD, turned=True)
-
-
-def attend_kernel(wide, same, q_ref, *refs):
-    nk = len(refs) - (1 if wide else CORES)
-    kv_refs, out_refs = refs[:nk], refs[nk:]
+    place(own.at[tok : 2 * tok, :], k1, k_out, 0)
+    k_out[rows:, :] = starts(p0, p1, k_out.shape[1])
+    place(own.at[2 * tok : 3 * tok, :], v1, v_out, 0, turned=True)
+
+
+def score_kernel(same, q_ref, *refs):
+    k_refs, (p_ref, top_ref) = refs[:-2], refs[-2:]
     size = q_ref.shape[1]
     tok = size
     both = CORES * tok
     half = PAD // CORES
-    block = PER * size + PAD
     rate = size ** -0.5 * math.log2(math.e)
     at_or_before = lax.broadcasted_iota(jnp.int32, (tok, tok), 0) <= lax.broadcasted_iota(jnp.int32, (tok, tok), 1)
 
-    def block_of(ref, at):
-        first = ref[at : at + PAD, :].astype(F32)
+    def block_of(ref):
+        first = ref[PER * both :, :].astype(F32)
         return [first[b * half : b * half + 1, :] for b in range(CORES)]
 
-    def store(b, at, value):
-        if wide:
-            out_refs[0][b * block + at : b * block + at + value.shape[0], :] = value
-        else:
-            out_refs[b][at : at + value.shape[0], :] = value
-
-    q_block = jnp.concatenate(block_of(q_ref, PER * both), axis=1)
-    kept = [
-        jnp.concatenate([p] * CORES, axis=1) <= q_block for ref in kv_refs for p in block_of(ref, PER * both)
-    ]
-    stats = [[] for _ in range(CORES)]
+    q_block = jnp.concatenate(block_of(q_ref), axis=1)
+    kept = [jnp.concatenate([p] * CORES, axis=1) <= q_block for ref in k_refs for p in block_of(ref)]
     for h in range(PER):
         q = q_ref[h * both : (h + 1) * both, :]
-        scores, vals = [], []
-        for j, ref in enumerate(kv_refs):
+        scores = []
+        for j, ref in enumerate(k_refs):
             s = nt_dot(ref[h * both : (h + 1) * both, :], q)
             for b in range(CORES):
                 part = s[b * tok : (b + 1) * tok, :]
@@ -93,24 +82,40 @@
                     cols[b] = jnp.where(at_or_before, cols[b], LOW)
                     part = jnp.concatenate(cols, axis=1)
                 scores.append(part)
-                at = PAD + (PER + h) * both + b * tok
-                vals.append(ref[at : at + tok, :])
         tops = [jnp.where(k, jnp.max(s, axis=0, keepdims=True), FLOOR) for k, s in zip(kept, scores)]
-        top = jnp.maximum(functools.reduce(jnp.maximum, tops), FLOOR).astype(BF16)
-        shift = top.astype(F32)
-        p = jnp.concatenate(
-            [jnp.exp2((s - jnp.where(k, shift, -LOW)) * rate).astype(BF16) for k, s in zip(kept, scores)], axis=0
-        )
+        top = jnp.maximum(functools.reduce(jnp.maximum, tops), FLOOR).astype(BF16).astype(F32)
+        for i, (k, s) in enumerate(zip(kept, scores)):
+            p_ref[h, i * tok : (i + 1) * tok, :] = jnp.exp2((s - jnp.where(k, top, -LOW)) * rate).astype(BF16)
+        top_ref[h * 8 : (h + 1) * 8, :] = jnp.broadcast_to(top, (8, both))
+
+
+def apply_kernel(wide, p_ref, top_ref, *refs):
+    nv = len(refs) - (1 if wide else CORES)
+    v_refs, out_refs = refs[:nv], refs[nv:]
+    size = v_refs[0].shape[1]
+    tok = size
+    both = CORES * tok
+    block = PER * size + PAD
+
+    def store(b, at, value):
+        if wide:
+            out_refs[0][b * block + at : b * block + at + value.shape[0], :] = value
+        else:
+            out_refs[b][at : at + value.shape[0], :] = value
+
+    stats = [[] for _ in range(CORES)]
+    for h in range(PER):
+        vals = [ref[h * both + b * tok : h * both + (b + 1) * tok, :] for ref in v_refs for b in range(CORES)]
         vt = jnp.concatenate(vals, axis=1)
         vt = jnp.concatenate([vt, jnp.ones((PAD, vt.shape[1]), BF16)], axis=0)
-        o = jnp.dot(vt, p, preferred_element_type=F32)
+        o = jnp.dot(vt, p_ref[h], preferred_element_type=F32)
         total = o[size : size + 1, :]
-        hi = total.astype(BF16)
-        lo = (total - hi.astype(F32)).astype(BF16)
+        hi = total.astype(BF16).astype(F32)
+        top = top_ref[h * 8 : h * 8 + 1, :]
         for b in range(CORES):
             cols = slice(b * tok, (b + 1) * tok)
             store(b, h * size, o[0:size, cols].astype(BF16))
-            stats[b] += [shift[:, cols], hi[:, cols].astype(F32), lo[:, cols].astype(F32)]
+            stats[b] += [top[:, cols], hi[:, cols], (total - hi)[:, cols]]
     for b in range(CORES):
         rest = jnp.zeros((PAD - 3 * PER, tok), F32)
         store(b, PER * size, jnp.concatenate(stats[b] + [rest], axis=0).astype(BF16))
@@ -190,11 +195,14 @@
             compiler_params=params,
             name="merge_q",
         )(block_pos, other[3], own, other[0])
-        kv_piece = pl.pallas_call(
+        k_piece, v_piece = pl.pallas_call(
             merge_kv_kernel,
-            out_shape=jax.ShapeDtypeStruct((2 * PER * both + PAD, size), BF16),
+            out_shape=(
+                jax.ShapeDtypeStruct((PER * both + PAD, size), BF16),
+                jax.ShapeDtypeStruct((PER * both, size), BF16),
+            ),
             in_specs=smem * 2 + vmem(3),
-            out_specs=vmem()[0],
+            out_specs=tuple(vmem(2)),
             compiler_params=params,
             name="merge_kv",
         )(block_pos, other[3], own, after(other[1], q_piece), other[2])
@@ -203,11 +211,22 @@
     def low(r):
         return r & -r
 
+    def high(r):
+        return 1 << (r.bit_length() - 1)
+
     def single(r):
         return r == low(r)
 
+    def over(a, r):
+        return lax.ppermute(a, "outer", [(o, o ^ r) for o in range(n_out)])
+
     with jax.named_scope("exchange"):
-        kv = [kv_piece] + [lax.ppermute(kv_piece, "outer", [(o, o ^ r) for o in range(n_out)]) for r in range(1, n_out)]
+        k_by, v_by = {0: k_piece}, {0: v_piece}
+        for r in range(1, n_out):
+            k_by[r] = over(k_by[r - high(r)], high(r))
+        for r in sorted(range(1, n_out), key=lambda r: r.bit_count()):
+            v_by[r] = over(v_by[r - low(r)], low(r))
+        ks, vs = [k_by[r] for r in range(n_out)], [v_by[r] for r in range(n_out)]
         q_by = {0: q_piece}
         bit = chips // 2
         while bit:
@@ -218,19 +237,35 @@
         rows = CORES * block if wide else block
         return (jax.ShapeDtypeStruct((rows, tok), BF16),) * (1 if wide else CORES)
 
-    def attend(r, wide, done=None):
-        q = q_by[r] if done is None else after(q_by[r], done)
-        work = 4 * PER * both * n_out * both * size
-        with jax.named_scope("attend"):
+    work = 2 * PER * both * n_out * both * size
+
+    def score(r, done):
+        with jax.named_scope("score"):
             return pl.pallas_call(
-                functools.partial(attend_kernel, wide, r == 0),
+                functools.partial(score_kernel, r == 0),
+                out_shape=(
+                    jax.ShapeDtypeStruct((PER, n_out * both, both), BF16),
+                    jax.ShapeDtypeStruct((PER * 8, both), F32),
+                ),
+                in_specs=vmem(1 + n_out),
+                out_specs=tuple(vmem(2)),
+                compiler_params=params,
+                cost_estimate=pl.CostEstimate(flops=work, bytes_accessed=2**20, transcendentals=work // (2 * size)),
+                name="score",
+            )(after(q_by[r], done), *ks)
+
+    def apply(r, wide, done):
+        with jax.named_scope("apply"):
+            weights, tops = weights_by[r]
+            return pl.pallas_call(
+                functools.partial(apply_kernel, wide),
                 out_shape=shapes(wide),
-                in_specs=vmem(1 + len(kv)),
+                in_specs=vmem(2 + n_out),
                 out_specs=tuple(vmem(len(shapes(wide)))),
                 compiler_params=params,
-                cost_estimate=pl.CostEstimate(flops=work, bytes_accessed=2**20, transcendentals=work // (4 * size)),
-                name="attend",
-            )(q, *kv)
+                cost_estimate=pl.CostEstimate(flops=work, bytes_accessed=2**20, transcendentals=0),
+                name="apply",
+            )(weights, tops if done is None else after(tops, done), *vs)
 
     def add(arrays, wide):
         with jax.named_scope("add"):
@@ -253,12 +288,17 @@
             else:
                 arrived[r - low(r)].append(lax.ppermute(parts[0], "inner", along_inner(low(r), 0)))
 
+    weights_by = {}
+    done = [v_by[r] for r in range(1, n_out) if single(r)]
+    for r in range(chips):
+        weights_by[r] = score(r, done)
+        done = weights_by[r][1]
     done = None
     partial = {}
     for r in reversed(range(1, chips)):
-        partial[r] = attend(r, r > 1, done)
+        partial[r] = apply(r, r > 1, done)
         done = partial[r][0]
-    own = attend(0, False, done)
+    own = apply(0, False, done)
     for r in reversed(range(1, chips)):
         parts = partial[r]
         if arrived[r]:

time: 42.3 us -> 40.1 us (0.948)
  waiting for transfers between devices: 16.5 us -> 9.98 us
  starting transfers between devices: 17 us -> 21.1 us
    ppermute x3 -> x6, waiting for transfers between devices: 7.04 us -> 2.06 us  [over(): return lax.ppermute(a, 'outer', [(o, o ^ r) for o in range(n_out)])]
    ppermute x3 -> x6, starting transfers between devices: 3.55 us -> 8.11 us  [over(): return lax.ppermute(a, 'outer', [(o, o ^ r) for o in range(n_out)])]
    ppermute x3, waiting for transfers between devices: 2.45 us -> 0.88 us  [shards(): q_by[r | bit] = lax.ppermute(q_by[r], 'inner', along_inner(bit, 0))]
    ppermute x3, starting transfers between devices: 6.12 us -> 5.48 us  [shards(): q_by[r | bit] = lax.ppermute(q_by[r], 'inner', along_inner(bit, 0))]
    pallas_call x5 -> x9, Pallas kernels: 5.14 us -> 5.18 us  [the longest x4 3.03 us: score(): pl.pallas_call(functools.partial(score_kernel, r == 0), out_shape=(jax.Sh...]
  transfers between devices with their start and end apart: 16 -> 19, of which waited for: 5 -> 6; matrix products, arithmetic and copies ran while one was open for 2% -> 2% of each run, Pallas kernels for 14% -> 12%
where the time goes in v10:
time: 40.1 us; the launch traced here: 39.9 us
  starting transfers between devices  21.1 us (53%)
  waiting for transfers between devices  9.98 us (25%)
  Pallas kernels  6.81 us (17%)
  local copies, waits for them, and re-layouts  1.15 us (3%)
  between operations  0.88 us (2%)
    ppermute x6, starting transfers between devices, over(): return lax.ppermute(a, 'outer', [(o, o ^ r) for o in range(n_out)])  8.11 us
    ppermute x4, waiting for transfers between devices, send(): lax.ppermute(parts[x], 'inner', along_inner(r, x))  6.73 us
    ppermute x3, starting transfers between devices, shards(): q_by[r | bit] = lax.ppermute(q_by[r], 'inner', along_inner(bit, 0))  5.48 us
    ppermute x4, starting transfers between devices, send(): lax.ppermute(parts[x], 'inner', along_inner(r, x))  4.79 us
    pallas_call x4, Pallas kernels, score(): pl.pallas_call(functools.partial(score_kernel, r == 0), out_shape=(jax.Sh...  3.03 us
    ppermute x6, waiting for transfers between devices, over(): return lax.ppermute(a, 'outer', [(o, o ^ r) for o in range(n_out)])  2.06 us
    ppermute x1, starting transfers between devices, send(): lax.ppermute(parts[0], 'inner', along_inner(low(r), 0))  1.64 us
    pallas_call x4, Pallas kernels, apply(): pl.pallas_call(functools.partial(apply_kernel, wide), out_shape=shapes(wi...  1.32 us
  transfers between devices with their start and end apart: 19, of which 6 were waited for; matrix products, arithmetic and copies ran while one was open for 2% of the time, Pallas kernels for 12%

profile of v10, /device:TPU:0, one launch (start us, length us, event | category | flops | bytes accessed | tf_op | source)
XLA Modules:
  0.0 39.9 jit_solution(5276632460576932428)
XLA Ops:
  0.0 0.5 %collective-permute-start = (s32[1]{0:T(128)}, s32[1]{0:T(128)}, u32[]{:S(2)}, u32[]{:S(2)}) collective-permute-start(s32[1]{0:T(128)} %param.7), channel_id=1, source_target_pairs={{0,1},{1,0},{2,3},{3,2},{4,5},{5,4},{6,7},{7,6},{8,9},{9,8},{10,11... | collective-permute-start | bytes 20 | tf_op jit(solution)/shard_map/swap/ppermute | solution.py:186
  0.5 0.1 collective-permute-start.1
  0.5 0.4 %collective-permute-start.2 = (bf16[128,512]{1,0:T(8,128)(2,1)}, bf16[128,512]{1,0:T(8,128)(2,1)S(1)}, u32[]{:S(2)}, u32[]{:S(2)}) collective-permute-start(bf16[128,512]{1,0:T(8,128)(2,1)} %param.5), channel_id=1, source_target_pairs={{0,1},{1,0},{2,3},{3,2},{4,5},{5,4},{6,7},{7,6},{8,9},{9,8},{10,11... | collective-permute-start | bytes 393224 | tf_op jit(solution)/shard_map/swap/ppermute | solution.py:186
  1.0 0.1 collective-permute-start.3
  1.0 0.9 %constant_dynamic-update-slice_fusion.2 = bf16[384,512]{1,0:T(8,128)(2,1)S(1)} fusion(bf16[128,512]{1,0:T(8,128)(2,1)} %param.4), kind=kLoop, calls=%fused_computation.2 | loop fusion | bytes 262144
  2.0 0.0 copy-start.1
  2.7 0.2 copy-done.1
  2.9 0.0 collective-permute-done.p1
  2.9 0.0 collective-permute-done.1.q1
  2.9 0.7 %merge_q.1.q_ref = bf16[528,128]{1,0:T(8,128)(2,1)S(1)} custom-call(s32[1]{0:T(128)S(6)} %copy.7.p0, s32[1]{0:T(128)} %collective-permute-done.p1, bf16[384,512]{1,0:T(8,128)(2,1)S(1)} %constant_dynamic-update-slice_fusion.own, bf16[128,512]{1,0:T(8,128)(2,1)S(1)} %collective-permute-done.1.q1), custom_call_target="tpu_custom_call" | custom-call | tf_op jit(solution)/shard_map/merge/merge_q/pallas_call | solution.py:190
  3.6 0.0 collective-permute-done.2.k1
  3.7 0.8 %merge_kv.1 = (bf16[528,128]{1,0:T(8,128)(2,1)S(1)}, bf16[512,128]{1,0:T(8,128)(2,1)S(1)}) custom-call(s32[1]{0:T(128)S(6)} %copy.7.p0, s32[1]{0:T(128)} %collective-permute-done.p1, bf16[384,512]{1,0:T(8,128)(2,1)S(1)} %constant_dynamic-update-slice_fusion.own, bf16[128,512]{1,0:T(8,128)(2,1)S(1)} %collective-permute-done.2.k1, ...), custom_call_target="tpu_custom_call" | custom-call | tf_op jit(solution)/shard_map/merge/merge_kv/pallas_call | solution.py:198
  4.5 3.0 %collective-permute-start.6 = (bf16[528,128]{1,0:T(8,128)(2,1)S(1)}, bf16[528,128]{1,0:T(8,128)(2,1)S(1)}, u32[]{:S(2)}, u32[]{:S(2)}) collective-permute-start(bf16[528,128]{1,0:T(8,128)(2,1)S(1)} %get-tuple-element.32.refs_0_), channel_id=1, source_target_pairs={{0,8},{8,0},{16,24},{24,16},{1,9},{9,1},{17,25},{25,17},{2,10},{10... | collective-permute-start | bytes 405512 | tf_op jit(solution)/shard_map/exchange/ppermute | solution.py:221
  7.5 0.1 collective-permute-start.4
  7.6 3.0 %collective-permute-start.10 = (bf16[528,128]{1,0:T(8,128)(2,1)S(1)}, bf16[528,128]{1,0:T(8,128)(2,1)S(1)}, u32[]{:S(2)}, u32[]{:S(2)}) collective-permute-start(bf16[528,128]{1,0:T(8,128)(2,1)S(1)} %merge_q.1.q_ref), channel_id=1, source_target_pairs={{0,4},{1,5},{2,6},{3,7},{4,0},{5,1},{6,2},{7,3},{8,12},{9,13},{10,... | collective-permute-start | bytes 405512 | tf_op jit(solution)/shard_map/exchange/ppermute | solution.py:234
  10.6 1.5 %collective-permute-start.5 = (bf16[512,128]{1,0:T(8,128)(2,1)S(1)}, bf16[512,128]{1,0:T(8,128)(2,1)S(1)}, u32[]{:S(2)}, u32[]{:S(2)}) collective-permute-start(bf16[512,128]{1,0:T(8,128)(2,1)S(1)} %get-tuple-element.30.refs_0_), channel_id=1, source_target_pairs={{0,16},{8,24},{16,0},{24,8},{1,17},{9,25},{17,1},{25,9},{2,18},{10... | collective-permute-start | bytes 393224 | tf_op jit(solution)/shard_map/exchange/ppermute | solution.py:221
  12.1 0.5 %collective-permute-start.7 = (bf16[528,128]{1,0:T(8,128)(2,1)S(1)}, bf16[528,128]{1,0:T(8,128)(2,1)S(1)}, u32[]{:S(2)}, u32[]{:S(2)}) collective-permute-start(bf16[528,128]{1,0:T(8,128)(2,1)S(1)} %get-tuple-element.32.refs_0_), channel_id=1, source_target_pairs={{0,16},{8,24},{16,0},{24,8},{1,17},{9,25},{17,1},{25,9},{2,18},{10... | collective-permute-start | bytes 405512 | tf_op jit(solution)/shard_map/exchange/ppermute | solution.py:221
  12.6 1.5 %collective-permute-start.8 = (bf16[528,128]{1,0:T(8,128)(2,1)S(1)}, bf16[528,128]{1,0:T(8,128)(2,1)S(1)}, u32[]{:S(2)}, u32[]{:S(2)}) collective-permute-start(bf16[528,128]{1,0:T(8,128)(2,1)S(1)} %collective-permute-done.6.refs_1_), channel_id=1, source_target_pairs={{0,16},{8,24},{16,0},{24,8},{1,17},{9,25},{17,1},{25,9},{2,18},{10... | collective-permute-start | bytes 405512 | tf_op jit(solution)/shard_map/exchange/ppermute | solution.py:221
  14.2 0.0 collective-permute-done.4.refs_1_
  14.2 1.8 %collective-permute-start.9 = (bf16[528,128]{1,0:T(8,128)(2,1)S(1)}, bf16[528,128]{1,0:T(8,128)(2,1)S(1)}, u32[]{:S(2)}, u32[]{:S(2)}) collective-permute-start(bf16[528,128]{1,0:T(8,128)(2,1)S(1)} %merge_q.1.q_ref), channel_id=1, source_target_pairs={{0,2},{1,3},{2,0},{3,1},{4,6},{5,7},{6,4},{7,5},{8,10},{9,11},{10,... | collective-permute-start | bytes 405512 | tf_op jit(solution)/shard_map/exchange/ppermute | solution.py:234
  15.9 0.9 %collective-permute-done.10.q_ref = bf16[528,128]{1,0:T(8,128)(2,1)S(1)} collective-permute-done((bf16[528,128]{1,0:T(8,128)(2,1)S(1)}, bf16[528,128]{1,0:T(8,128)(2,1)S(1)}, u32[]{:S(2)}, u32[]{:S(2)}) %collective-permute-start.10) | collective-permute-done | bytes 135200 | tf_op jit(solution)/shard_map/exchange/ppermute | solution.py:234
  16.8 0.7 %collective-permute-start.11 = (bf16[528,128]{1,0:T(8,128)(2,1)S(1)}, bf16[528,128]{1,0:T(8,128)(2,1)S(1)}, u32[]{:S(2)}, u32[]{:S(2)}) collective-permute-start(bf16[528,128]{1,0:T(8,128)(2,1)S(1)} %collective-permute-done.10.q_ref), channel_id=1, source_target_pairs={{0,2},{1,3},{2,0},{3,1},{4,6},{5,7},{6,4},{7,5},{8,10},{9,11},{10,... | collective-permute-start | bytes 405512 | tf_op jit(solution)/shard_map/exchange/ppermute | solution.py:234
  17.5 1.5 %collective-permute-start.12 = (bf16[512,128]{1,0:T(8,128)(2,1)S(1)}, bf16[512,128]{1,0:T(8,128)(2,1)S(1)}, u32[]{:S(2)}, u32[]{:S(2)}) collective-permute-start(bf16[512,128]{1,0:T(8,128)(2,1)S(1)} %collective-permute-done.5.refs_2_), channel_id=1, source_target_pairs={{0,8},{8,0},{16,24},{24,16},{1,9},{9,1},{17,25},{25,17},{2,10},{10... | collective-permute-start | bytes 393224 | tf_op jit(solution)/shard_map/exchange/ppermute | solution.py:221
  19.0 0.6 %collective-permute-done.7.refs_2_ = bf16[528,128]{1,0:T(8,128)(2,1)S(1)} collective-permute-done((bf16[528,128]{1,0:T(8,128)(2,1)S(1)}, bf16[528,128]{1,0:T(8,128)(2,1)S(1)}, u32[]{:S(2)}, u32[]{:S(2)}) %collective-permute-start.7) | collective-permute-done | bytes 135200 | tf_op jit(solution)/shard_map/exchange/ppermute | solution.py:221
  19.6 1.4 %collective-permute-done.8.refs_3_ = bf16[528,128]{1,0:T(8,128)(2,1)S(1)} collective-permute-done((bf16[528,128]{1,0:T(8,128)(2,1)S(1)}, bf16[528,128]{1,0:T(8,128)(2,1)S(1)}, u32[]{:S(2)}, u32[]{:S(2)}) %collective-permute-start.8) | collective-permute-done | bytes 135200 | tf_op jit(solution)/shard_map/exchange/ppermute | solution.py:221
  21.0 0.8 %score.4 = (bf16[2,1024,256]{2,1,0:T(8,128)(2,1)S(1)}, f32[16,256]{1,0:T(8,128)S(1)}) custom-call(bf16[528,128]{1,0:T(8,128)(2,1)S(1)} %merge_q.1.q_ref, bf16[528,128]{1,0:T(8,128)(2,1)S(1)} %get-tuple-element.32.refs_0_, bf16[528,128]{1,0:T(8,128)(2,1)S(1)} %collective-permute-done.6.refs_1_, bf16[528,128]{1,0:T(8,128)(2,1)S(1)} %collective-permute-done.7.refs_2_, ...), custom_call_target="tpu_custom_call" | custom-call | flops 134217728 | bytes 1048576 | tf_op jit(solution)/shard_map/score/score/pallas_call | solution.py:244
  21.8 0.0 collective-permute-done.9.q_ref
  21.8 0.8 %score.5 = (bf16[2,1024,256]{2,1,0:T(8,128)(2,1)S(1)}, f32[16,256]{1,0:T(8,128)S(1)}) custom-call(bf16[528,128]{1,0:T(8,128)(2,1)S(1)} %collective-permute-done.9.q_ref, bf16[528,128]{1,0:T(8,128)(2,1)S(1)} %get-tuple-element.32.refs_0_, bf16[528,128]{1,0:T(8,128)(2,1)S(1)} %collective-permute-done.6.refs_1_, ...), custom_call_target="tpu_custom_call" | custom-call | flops 134217728 | bytes 1048576 | tf_op jit(solution)/shard_map/score/score/pallas_call | solution.py:244
  22.6 0.8 %score.6 = (bf16[2,1024,256]{2,1,0:T(8,128)(2,1)S(1)}, f32[16,256]{1,0:T(8,128)S(1)}) custom-call(bf16[528,128]{1,0:T(8,128)(2,1)S(1)} %collective-permute-done.10.q_ref, bf16[528,128]{1,0:T(8,128)(2,1)S(1)} %get-tuple-element.32.refs_0_, bf16[528,128]{1,0:T(8,128)(2,1)S(1)} %collective-permute-done.6.refs_1_, ...), custom_call_target="tpu_custom_call" | custom-call | flops 134217728 | bytes 1048576 | tf_op jit(solution)/shard_map/score/score/pallas_call | solution.py:244
  23.4 0.8 %score.7 = (bf16[2,1024,256]{2,1,0:T(8,128)(2,1)S(1)}, f32[16,256]{1,0:T(8,128)S(1)}) custom-call(bf16[528,128]{1,0:T(8,128)(2,1)S(1)} %collective-permute-done.11.q_ref, bf16[528,128]{1,0:T(8,128)(2,1)S(1)} %get-tuple-element.32.refs_0_, bf16[528,128]{1,0:T(8,128)(2,1)S(1)} %collective-permute-done.6.refs_1_, ...), custom_call_target="tpu_custom_call" | custom-call | flops 134217728 | bytes 1048576 | tf_op jit(solution)/shard_map/score/score/pallas_call | solution.py:244
  24.1 0.0 collective-permute-done.12.refs_3_
  24.1 0.3 apply.4
  24.5 1.6 %collective-permute-start.14 = (bf16[544,128]{1,0:T(8,128)(2,1)S(1)}, bf16[544,128]{1,0:T(8,128)(2,1)S(1)}, u32[]{:S(2)}, u32[]{:S(2)}) collective-permute-start(bf16[544,128]{1,0:T(8,128)(2,1)S(1)} %apply.4), channel_id=1, source_target_pairs={{0,2},{1,3},{2,0},{3,1},{4,6},{5,7},{6,4},{7,5},{8,10},{9,11},{10,... | collective-permute-start | bytes 417800 | tf_op jit(solution)/shard_map/return/ppermute | solution.py:289
  26.1 0.3 apply.5.refs_0_
  26.4 0.3 apply.6
  26.8 0.5 %collective-permute-start.17 = (bf16[272,128]{1,0:T(8,128)(2,1)S(1)}, bf16[272,128]{1,0:T(8,128)(2,1)S(1)}, u32[]{:S(2)}, u32[]{:S(2)}) collective-permute-start(bf16[272,128]{1,0:T(8,128)(2,1)S(1)} %get-tuple-element.46), channel_id=1, source_target_pairs={{0,2},{1,3},{2,0},{3,1},{4,6},{5,7},{6,4},{7,5},{8,10},{9,11},{10,... | collective-permute-start | bytes 208904 | tf_op jit(solution)/shard_map/return/ppermute | solution.py:287
  27.3 0.3 apply.7
  27.6 0.1 collective-permute-start.13
  27.7 1.7 %collective-permute-start.18 = (bf16[272,128]{1,0:T(8,128)(2,1)S(1)}, bf16[272,128]{1,0:T(8,128)(2,1)S(1)}, u32[]{:S(2)}, u32[]{:S(2)}) collective-permute-start(bf16[272,128]{1,0:T(8,128)(2,1)S(1)} %get-tuple-element.52), channel_id=1, source_target_pairs={{0,3},{1,2},{2,1},{3,0},{4,7},{5,6},{6,5},{7,4},{8,11},{9,10},{10,... | collective-permute-start | bytes 208904 | tf_op jit(solution)/shard_map/return/ppermute | solution.py:287
  29.4 0.3 collective-permute-done.14.refs_1_
  29.7 0.1 add.1
  29.8 2.6 %collective-permute-start.15 = (bf16[272,128]{1,0:T(8,128)(2,1)S(1)}, bf16[272,128]{1,0:T(8,128)(2,1)S(1)}, u32[]{:S(2)}, u32[]{:S(2)}) collective-permute-start(bf16[272,128]{1,0:T(8,128)(2,1)S(1)} %get-tuple-element.50), channel_id=1, source_target_pairs={{0,4},{1,5},{2,6},{3,7},{4,0},{5,1},{6,2},{7,3},{8,12},{9,13},{10,... | collective-permute-start | bytes 208904 | tf_op jit(solution)/shard_map/return/ppermute | solution.py:287
  32.4 0.0 collective-permute-start.16
  32.4 0.0 collective-permute-done.13.refs_1_
  32.4 0.0 collective-permute-done.17.refs_4_
  32.4 4.5 %collective-permute-done.15.refs_2_ = bf16[272,128]{1,0:T(8,128)(2,1)S(1)} collective-permute-done((bf16[272,128]{1,0:T(8,128)(2,1)S(1)}, bf16[272,128]{1,0:T(8,128)(2,1)S(1)}, u32[]{:S(2)}, u32[]{:S(2)}) %collective-permute-start.15) | collective-permute-done | bytes 69664 | tf_op jit(solution)/shard_map/return/ppermute | solution.py:287
  36.9 2.2 %collective-permute-done.16.refs_3_ = bf16[272,128]{1,0:T(8,128)(2,1)S(1)} collective-permute-done((bf16[272,128]{1,0:T(8,128)(2,1)S(1)}, bf16[272,128]{1,0:T(8,128)(2,1)S(1)}, u32[]{:S(2)}, u32[]{:S(2)}) %collective-permute-start.16) | collective-permute-done | bytes 69664 | tf_op jit(solution)/shard_map/return/ppermute | solution.py:287
  39.1 0.8 %combine.1 = bf16[128,512]{1,0:T(8,128)(2,1)} custom-call(bf16[272,128]{1,0:T(8,128)(2,1)S(1)} %get-tuple-element.48.refs_0_, bf16[272,128]{1,0:T(8,128)(2,1)S(1)} %collective-permute-done.13.refs_1_, bf16[272,128]{1,0:T(8,128)(2,1)S(1)} %collective-permute-done.15.refs_2_, bf16[272,128]{1,0:T(8,128)(2,1)S(1)} %collective-permute-done.16.refs_3_, ...), custom_call_target="tpu_custom_call" | custom-call | tf_op jit(solution)/shard_map/combine/combine/pallas_call | solution.py:310
  (9 shorter events, 0.0 us)
Async XLA Ops:
  0.0 1.9 %copy-start = (bf16[128,512]{1,0:T(8,128)(2,1)S(1)}, bf16[128,512]{1,0:T(8,128)(2,1)}, u32[]{:S(2)}) copy-start(bf16[128,512]{1,0:T(8,128)(2,1)} %param.5) | copy-start | bytes 393220
  0.0 2.9 %collective-permute-start = (s32[1]{0:T(128)}, s32[1]{0:T(128)}, u32[]{:S(2)}, u32[]{:S(2)}) collective-permute-start(s32[1]{0:T(128)} %param.7), channel_id=1, source_target_pairs={{0,1},{1,0},{2,3},{3,2},{4,5},{5,4},{6,7},{7,6},{8,9},{9,8},{10,11... | collective-permute-start | bytes 20 | tf_op jit(solution)/shard_map/swap/ppermute | solution.py:186
  0.5 2.5 %collective-permute-start.1 = (bf16[128,512]{1,0:T(8,128)(2,1)}, bf16[128,512]{1,0:T(8,128)(2,1)S(1)}, u32[]{:S(2)}, u32[]{:S(2)}) collective-permute-start(bf16[128,512]{1,0:T(8,128)(2,1)} %param.4), channel_id=1, source_target_pairs={{0,1},{1,0},{2,3},{3,2},{4,5},{5,4},{6,7},{7,6},{8,9},{9,8},{10,11... | collective-permute-start | bytes 393224 | tf_op jit(solution)/shard_map/swap/ppermute | solution.py:186
  0.5 3.1 %collective-permute-start.2 = (bf16[128,512]{1,0:T(8,128)(2,1)}, bf16[128,512]{1,0:T(8,128)(2,1)S(1)}, u32[]{:S(2)}, u32[]{:S(2)}) collective-permute-start(bf16[128,512]{1,0:T(8,128)(2,1)} %param.5), channel_id=1, source_target_pairs={{0,1},{1,0},{2,3},{3,2},{4,5},{5,4},{6,7},{7,6},{8,9},{9,8},{10,11... | collective-permute-start | bytes 393224 | tf_op jit(solution)/shard_map/swap/ppermute | solution.py:186
  1.0 2.7 %collective-permute-start.3 = (bf16[128,512]{1,0:T(8,128)(2,1)}, bf16[128,512]{1,0:T(8,128)(2,1)S(1)}, u32[]{:S(2)}, u32[]{:S(2)}) collective-permute-start(bf16[128,512]{1,0:T(8,128)(2,1)} %param.6), channel_id=1, source_target_pairs={{0,1},{1,0},{2,3},{3,2},{4,5},{5,4},{6,7},{7,6},{8,9},{9,8},{10,11... | collective-permute-start | bytes 393224 | tf_op jit(solution)/shard_map/swap/ppermute | solution.py:186
  2.0 0.9 %copy-start.1 = (bf16[128,512]{1,0:T(8,128)(2,1)S(1)}, bf16[128,512]{1,0:T(8,128)(2,1)}, u32[]{:S(2)}) copy-start(bf16[128,512]{1,0:T(8,128)(2,1)} %param.6) | copy-start | bytes 393220
  4.5 8.2 %collective-permute-start.6 = (bf16[528,128]{1,0:T(8,128)(2,1)S(1)}, bf16[528,128]{1,0:T(8,128)(2,1)S(1)}, u32[]{:S(2)}, u32[]{:S(2)}) collective-permute-start(bf16[528,128]{1,0:T(8,128)(2,1)S(1)} %get-tuple-element.32.refs_0_), channel_id=1, source_target_pairs={{0,8},{8,0},{16,24},{24,16},{1,9},{9,1},{17,25},{25,17},{2,10},{10... | collective-permute-start | bytes 405512 | tf_op jit(solution)/shard_map/exchange/ppermute | solution.py:221
  7.5 6.7 %collective-permute-start.4 = (bf16[512,128]{1,0:T(8,128)(2,1)S(1)}, bf16[512,128]{1,0:T(8,128)(2,1)S(1)}, u32[]{:S(2)}, u32[]{:S(2)}) collective-permute-start(bf16[512,128]{1,0:T(8,128)(2,1)S(1)} %get-tuple-element.30.refs_0_), channel_id=1, source_target_pairs={{0,8},{8,0},{16,24},{24,16},{1,9},{9,1},{17,25},{25,17},{2,10},{10... | collective-permute-start | bytes 393224 | tf_op jit(solution)/shard_map/exchange/ppermute | solution.py:221
  7.6 9.2 %collective-permute-start.10 = (bf16[528,128]{1,0:T(8,128)(2,1)S(1)}, bf16[528,128]{1,0:T(8,128)(2,1)S(1)}, u32[]{:S(2)}, u32[]{:S(2)}) collective-permute-start(bf16[528,128]{1,0:T(8,128)(2,1)S(1)} %merge_q.1.q_ref), channel_id=1, source_target_pairs={{0,4},{1,5},{2,6},{3,7},{4,0},{5,1},{6,2},{7,3},{8,12},{9,13},{10,... | collective-permute-start | bytes 405512 | tf_op jit(solution)/shard_map/exchange/ppermute | solution.py:234
  10.6 6.9 %collective-permute-start.5 = (bf16[512,128]{1,0:T(8,128)(2,1)S(1)}, bf16[512,128]{1,0:T(8,128)(2,1)S(1)}, u32[]{:S(2)}, u32[]{:S(2)}) collective-permute-start(bf16[512,128]{1,0:T(8,128)(2,1)S(1)} %get-tuple-element.30.refs_0_), channel_id=1, source_target_pairs={{0,16},{8,24},{16,0},{24,8},{1,17},{9,25},{17,1},{25,9},{2,18},{10... | collective-permute-start | bytes 393224 | tf_op jit(solution)/shard_map/exchange/ppermute | solution.py:221
  12.1 7.5 %collective-permute-start.7 = (bf16[528,128]{1,0:T(8,128)(2,1)S(1)}, bf16[528,128]{1,0:T(8,128)(2,1)S(1)}, u32[]{:S(2)}, u32[]{:S(2)}) collective-permute-start(bf16[528,128]{1,0:T(8,128)(2,1)S(1)} %get-tuple-element.32.refs_0_), channel_id=1, source_target_pairs={{0,16},{8,24},{16,0},{24,8},{1,17},{9,25},{17,1},{25,9},{2,18},{10... | collective-permute-start | bytes 405512 | tf_op jit(solution)/shard_map/exchange/ppermute | solution.py:221
  12.6 8.4 %collective-permute-start.8 = (bf16[528,128]{1,0:T(8,128)(2,1)S(1)}, bf16[528,128]{1,0:T(8,128)(2,1)S(1)}, u32[]{:S(2)}, u32[]{:S(2)}) collective-permute-start(bf16[528,128]{1,0:T(8,128)(2,1)S(1)} %collective-permute-done.6.refs_1_), channel_id=1, source_target_pairs={{0,16},{8,24},{16,0},{24,8},{1,17},{9,25},{17,1},{25,9},{2,18},{10... | collective-permute-start | bytes 405512 | tf_op jit(solution)/shard_map/exchange/ppermute | solution.py:221
  14.2 7.6 %collective-permute-start.9 = (bf16[528,128]{1,0:T(8,128)(2,1)S(1)}, bf16[528,128]{1,0:T(8,128)(2,1)S(1)}, u32[]{:S(2)}, u32[]{:S(2)}) collective-permute-start(bf16[528,128]{1,0:T(8,128)(2,1)S(1)} %merge_q.1.q_ref), channel_id=1, source_target_pairs={{0,2},{1,3},{2,0},{3,1},{4,6},{5,7},{6,4},{7,5},{8,10},{9,11},{10,... | collective-permute-start | bytes 405512 | tf_op jit(solution)/shard_map/exchange/ppermute | solution.py:234
  16.8 6.5 %collective-permute-start.11 = (bf16[528,128]{1,0:T(8,128)(2,1)S(1)}, bf16[528,128]{1,0:T(8,128)(2,1)S(1)}, u32[]{:S(2)}, u32[]{:S(2)}) collective-permute-start(bf16[528,128]{1,0:T(8,128)(2,1)S(1)} %collective-permute-done.10.q_ref), channel_id=1, source_target_pairs={{0,2},{1,3},{2,0},{3,1},{4,6},{5,7},{6,4},{7,5},{8,10},{9,11},{10,... | collective-permute-start | bytes 405512 | tf_op jit(solution)/shard_map/exchange/ppermute | solution.py:234
  17.5 6.6 %collective-permute-start.12 = (bf16[512,128]{1,0:T(8,128)(2,1)S(1)}, bf16[512,128]{1,0:T(8,128)(2,1)S(1)}, u32[]{:S(2)}, u32[]{:S(2)}) collective-permute-start(bf16[512,128]{1,0:T(8,128)(2,1)S(1)} %collective-permute-done.5.refs_2_), channel_id=1, source_target_pairs={{0,8},{8,0},{16,24},{24,16},{1,9},{9,1},{17,25},{25,17},{2,10},{10... | collective-permute-start | bytes 393224 | tf_op jit(solution)/shard_map/exchange/ppermute | solution.py:221
  24.5 5.2 %collective-permute-start.14 = (bf16[544,128]{1,0:T(8,128)(2,1)S(1)}, bf16[544,128]{1,0:T(8,128)(2,1)S(1)}, u32[]{:S(2)}, u32[]{:S(2)}) collective-permute-start(bf16[544,128]{1,0:T(8,128)(2,1)S(1)} %apply.4), channel_id=1, source_target_pairs={{0,2},{1,3},{2,0},{3,1},{4,6},{5,7},{6,4},{7,5},{8,10},{9,11},{10,... | collective-permute-start | bytes 417800 | tf_op jit(solution)/shard_map/return/ppermute | solution.py:289
  26.8 5.6 %collective-permute-start.17 = (bf16[272,128]{1,0:T(8,128)(2,1)S(1)}, bf16[272,128]{1,0:T(8,128)(2,1)S(1)}, u32[]{:S(2)}, u32[]{:S(2)}) collective-permute-start(bf16[272,128]{1,0:T(8,128)(2,1)S(1)} %get-tuple-element.46), channel_id=1, source_target_pairs={{0,2},{1,3},{2,0},{3,1},{4,6},{5,7},{6,4},{7,5},{8,10},{9,11},{10,... | collective-permute-start | bytes 208904 | tf_op jit(solution)/shard_map/return/ppermute | solution.py:287
  27.6 4.7 %collective-permute-start.13 = (bf16[272,128]{1,0:T(8,128)(2,1)S(1)}, bf16[272,128]{1,0:T(8,128)(2,1)S(1)}, u32[]{:S(2)}, u32[]{:S(2)}) collective-permute-start(bf16[272,128]{1,0:T(8,128)(2,1)S(1)} %get-tuple-element.49), channel_id=1, source_target_pairs={{0,1},{1,0},{2,3},{3,2},{4,5},{5,4},{6,7},{7,6},{8,9},{9,8},{10,11... | collective-permute-start | bytes 208904 | tf_op jit(solution)/shard_map/return/ppermute | solution.py:308
  27.7 4.7 %collective-permute-start.18 = (bf16[272,128]{1,0:T(8,128)(2,1)S(1)}, bf16[272,128]{1,0:T(8,128)(2,1)S(1)}, u32[]{:S(2)}, u32[]{:S(2)}) collective-permute-start(bf16[272,128]{1,0:T(8,128)(2,1)S(1)} %get-tuple-element.52), channel_id=1, source_target_pairs={{0,3},{1,2},{2,1},{3,0},{4,7},{5,6},{6,5},{7,4},{8,11},{9,10},{10,... | collective-permute-start | bytes 208904 | tf_op jit(solution)/shard_map/return/ppermute | solution.py:287
  29.8 7.1 %collective-permute-start.15 = (bf16[272,128]{1,0:T(8,128)(2,1)S(1)}, bf16[272,128]{1,0:T(8,128)(2,1)S(1)}, u32[]{:S(2)}, u32[]{:S(2)}) collective-permute-start(bf16[272,128]{1,0:T(8,128)(2,1)S(1)} %get-tuple-element.50), channel_id=1, source_target_pairs={{0,4},{1,5},{2,6},{3,7},{4,0},{5,1},{6,2},{7,3},{8,12},{9,13},{10,... | collective-permute-start | bytes 208904 | tf_op jit(solution)/shard_map/return/ppermute | solution.py:287
  32.4 6.8 %collective-permute-start.16 = (bf16[272,128]{1,0:T(8,128)(2,1)S(1)}, bf16[272,128]{1,0:T(8,128)(2,1)S(1)}, u32[]{:S(2)}, u32[]{:S(2)}) collective-permute-start(bf16[272,128]{1,0:T(8,128)(2,1)S(1)} %get-tuple-element.51), channel_id=1, source_target_pairs={{0,5},{1,4},{2,7},{3,6},{4,1},{5,0},{6,3},{7,2},{8,13},{9,12},{10,... | collective-permute-start | bytes 208904 | tf_op jit(solution)/shard_map/return/ppermute | solution.py:287

commit v11 on v10

--- a/solution.py
+++ b/solution.py
@@ -40,18 +40,14 @@
     return jnp.concatenate([jnp.full((half, size), p[0].astype(F32), F32) for p in (p0, p1)], axis=0).astype(BF16)
 
 
-def merge_q_kernel(p0, p1, own, q1, out):
+def merge_kernel(p0, p1, own, q1, k1, v1, q_out, k_out, v_out):
     tok = q1.shape[0]
     rows = PER * CORES * tok
-    place(own.at[0:tok, :], q1, out, 0)
-    out[rows:, :] = starts(p0, p1, out.shape[1])
-
-
-def merge_kv_kernel(p0, p1, own, k1, v1, k_out, v_out):
-    tok = k1.shape[0]
-    rows = PER * CORES * tok
+    pos = starts(p0, p1, q_out.shape[1])
+    place(own.at[0:tok, :], q1, q_out, 0)
+    q_out[rows:, :] = pos
     place(own.at[tok : 2 * tok, :], k1, k_out, 0)
-    k_out[rows:, :] = starts(p0, p1, k_out.shape[1])
+    k_out[rows:, :] = pos
     place(own.at[2 * tok : 3 * tok, :], v1, v_out, 0, turned=True)
 
 
@@ -187,25 +183,15 @@
         own = jnp.concatenate([queries, keys, values], axis=0)
     with jax.named_scope("merge"):
         smem = [pl.BlockSpec(memory_space=pltpu.SMEM)]
-        q_piece = pl.pallas_call(
-            merge_q_kernel,
-            out_shape=jax.ShapeDtypeStruct((PER * both + PAD, size), BF16),
-            in_specs=smem * 2 + vmem(2),
-            out_specs=vmem()[0],
+        piece = jax.ShapeDtypeStruct((PER * both + PAD, size), BF16)
+        q_piece, k_piece, v_piece = pl.pallas_call(
+            merge_kernel,
+            out_shape=(piece, piece, jax.ShapeDtypeStruct((PER * both, size), BF16)),
+            in_specs=smem * 2 + vmem(4),
+            out_specs=tuple(vmem(3)),
             compiler_params=params,
-            name="merge_q",
-        )(block_pos, other[3], own, other[0])
-        k_piece, v_piece = pl.pallas_call(
-            merge_kv_kernel,
-            out_shape=(
-                jax.ShapeDtypeStruct((PER * both + PAD, size), BF16),
-                jax.ShapeDtypeStruct((PER * both, size), BF16),
-            ),
-            in_specs=smem * 2 + vmem(3),
-            out_specs=tuple(vmem(2)),
-            compiler_params=params,
-            name="merge_kv",
-        )(block_pos, other[3], own, after(other[1], q_piece), other[2])
+            name="merge",
+        )(block_pos, other[3], own, *other[:3])
     block = PER * size + PAD
 
     def low(r):
@@ -227,12 +213,15 @@
         for r in sorted(range(1, n_out), key=lambda r: r.bit_count()):
             v_by[r] = over(v_by[r - low(r)], low(r))
         ks, vs = [k_by[r] for r in range(n_out)], [v_by[r] for r in range(n_out)]
+        passed = v_by[n_out // 2] if n_out > 1 else v_piece
         q_by = {0: q_piece}
         bit = chips // 2
         while bit:
             for r in sorted(q_by):
-                q_by[r | bit] = lax.ppermute(q_by[r], "inner", along_inner(bit, 0))
+                piece = q_by[r] if bit == chips // 2 else after(q_by[r], passed)
+                q_by[r | bit] = lax.ppermute(piece, "inner", along_inner(bit, 0))
             bit //= 2
+
     def shapes(wide):
         rows = CORES * block if wide else block
         return (jax.ShapeDtypeStruct((rows, tok), BF16),) * (1 if wide else CORES)
@@ -289,23 +278,26 @@
                 arrived[r - low(r)].append(lax.ppermute(parts[0], "inner", along_inner(low(r), 0)))
 
     weights_by = {}
-    done = [v_by[r] for r in range(1, n_out) if single(r)]
+    done = passed
     for r in range(chips):
         weights_by[r] = score(r, done)
         done = weights_by[r][1]
     done = None
     partial = {}
-    for r in reversed(range(1, chips)):
+    for r in reversed(range(chips)):
         partial[r] = apply(r, r > 1, done)
         done = partial[r][0]
-    own = apply(0, False, done)
-    for r in reversed(range(1, chips)):
+    for r in reversed(range(2, chips)):
         parts = partial[r]
         if arrived[r]:
             parts = add([parts[0], *arrived[r]], not single(r))
+            done = parts[0]
         send(r, parts)
     with jax.named_scope("return"):
-        ends = [own[0], lax.ppermute(own[1], "inner", along_inner(0, 1))] + ends
+        across = lax.ppermute(after(partial[0][1], done), "inner", along_inner(0, 1))
+    if chips > 1:
+        send(1, [after(part, across) for part in partial[1]])
+    ends = [partial[0][0], across] + ends
     with jax.named_scope("combine"):
         return pl.pallas_call(
             functools.partial(combine_kernel, len(ends)),

time: 40.1 us -> 43.9 us (1.095)
  waiting for transfers between devices: 9.98 us -> 16.1 us
  starting transfers between devices: 21.1 us -> 19.8 us
  local copies, waits for them, and re-layouts: 1.15 us -> 0 us
  other arithmetic: 0 us -> 1.06 us
  Pallas kernels: 6.81 us -> 5.99 us
    ppermute x1, waiting for transfers between devices: 0.28 us -> 3.76 us  [send(): lax.ppermute(parts[0], 'inner', along_inner(low(r), 0))]
    ppermute x4, waiting for transfers between devices: 0.89 us -> 2.7 us  [the longest x3 2.7 us: shards(): q_by[r | bit] = lax.ppermute(piece, 'inner', along_inner(bit, 0))]
    ppermute x1, starting transfers between devices: 1.64 us -> 0.35 us  [send(): lax.ppermute(parts[0], 'inner', along_inner(low(r), 0))]
    unnamed x6 -> x0, local copies, waits for them, and re-layouts: 1.14 us -> none
    concatenate x0 -> x1, other arithmetic: none -> 1.06 us  [shards(): own = jnp.concatenate([queries, keys, values], axis=0)]
    pallas_call x2 -> x1, Pallas kernels: 1.54 us -> 0.73 us  [shards(): pl.pallas_call(merge_kernel, out_shape=(piece, piece, jax.ShapeDtypeStruc...]
    ppermute x6, waiting for transfers between devices: 2.06 us -> 2.8 us  [over(): return lax.ppermute(a, 'outer', [(o, o ^ r) for o in range(n_out)])]
    ppermute x4, starting transfers between devices: 5.56 us -> 4.85 us  [the longest x3 4.77 us: shards(): q_by[r | bit] = lax.ppermute(piece, 'inner', along_inner(bit, 0))]
  transfers between devices with their start and end apart: 19 -> 19, of which waited for: 6 -> 8; matrix products, arithmetic and copies ran while one was open for 2% -> 2% of each run, Pallas kernels for 12% -> 9%
where the time goes in v11:
time: 43.9 us; the launch traced here: 43.7 us
  starting transfers between devices  19.8 us (45%)
  waiting for transfers between devices  16.1 us (37%)
  Pallas kernels  5.99 us (14%)
  other arithmetic  1.06 us (2%)
  between operations  0.79 us (2%)
    ppermute x6, starting transfers between devices, over(): return lax.ppermute(a, 'outer', [(o, o ^ r) for o in range(n_out)])  8.58 us
    ppermute x4, waiting for transfers between devices, send(): lax.ppermute(parts[x], 'inner', along_inner(r, x))  6.82 us
    ppermute x4, starting transfers between devices, send(): lax.ppermute(parts[x], 'inner', along_inner(r, x))  5 us
    ppermute x3, starting transfers between devices, shards(): q_by[r | bit] = lax.ppermute(piece, 'inner', along_inner(bit, 0))  4.77 us
    ppermute x1, waiting for transfers between devices, send(): lax.ppermute(parts[0], 'inner', along_inner(low(r), 0))  3.76 us
    pallas_call x4, Pallas kernels, score(): pl.pallas_call(functools.partial(score_kernel, r == 0), out_shape=(jax.Sh...  3.03 us
    ppermute x6, waiting for transfers between devices, over(): return lax.ppermute(a, 'outer', [(o, o ^ r) for o in range(n_out)])  2.8 us
    ppermute x3, waiting for transfers between devices, shards(): q_by[r | bit] = lax.ppermute(piece, 'inner', along_inner(bit, 0))  2.7 us
  transfers between devices with their start and end apart: 19, of which 8 were waited for; matrix products, arithmetic and copies ran while one was open for 2% of the time, Pallas kernels for 9%

profile of v11, /device:TPU:0, one launch (start us, length us, event | category | flops | bytes accessed | tf_op | source)
XLA Modules:
  0.0 43.7 jit_solution(12813931981927599191)
XLA Ops:
  0.0 0.5 %collective-permute-start.1 = (bf16[128,512]{1,0:T(8,128)(2,1)}, bf16[128,512]{1,0:T(8,128)(2,1)S(1)}, u32[]{:S(2)}, u32[]{:S(2)}) collective-permute-start(bf16[128,512]{1,0:T(8,128)(2,1)} %param.4), channel_id=1, source_target_pairs={{0,1},{1,0},{2,3},{3,2},{4,5},{5,4},{6,7},{7,6},{8,9},{9,8},{10,11... | collective-permute-start | bytes 393224 | tf_op jit(solution)/shard_map/swap/ppermute | solution.py:182
  0.5 0.1 collective-permute-start.2
  0.5 0.5 %collective-permute-start.3 = (bf16[128,512]{1,0:T(8,128)(2,1)}, bf16[128,512]{1,0:T(8,128)(2,1)S(1)}, u32[]{:S(2)}, u32[]{:S(2)}) collective-permute-start(bf16[128,512]{1,0:T(8,128)(2,1)} %param.6), channel_id=1, source_target_pairs={{0,1},{1,0},{2,3},{3,2},{4,5},{5,4},{6,7},{7,6},{8,9},{9,8},{10,11... | collective-permute-start | bytes 393224 | tf_op jit(solution)/shard_map/swap/ppermute | solution.py:182
  1.0 0.1 collective-permute-start
  1.7 1.1 %pad_maximum_fusion.own = bf16[384,512]{1,0:T(8,128)(2,1)S(1)} fusion(bf16[128,512]{1,0:T(8,128)(2,1)} %param.6, bf16[128,512]{1,0:T(8,128)(2,1)} %param.5, bf16[128,512]{1,0:T(8,128)(2,1)} %param.4), kind=kLoop, calls=%fused_computation | loop fusion | flops 1179648 | bytes 786432 | tf_op jit(solution)/shard_map/swap/concatenate | solution.py:183
  2.7 0.0 collective-permute-done.p1
  2.7 0.0 collective-permute-done.1.q1
  2.8 0.0 collective-permute-done.2.k1
  2.8 0.0 collective-permute-done.3.v1
  2.8 0.7 %merge.1 = (bf16[528,128]{1,0:T(8,128)(2,1)S(1)}, bf16[528,128]{1,0:T(8,128)(2,1)S(1)}, bf16[512,128]{1,0:T(8,128)(2,1)S(1)}) custom-call(s32[1]{0:T(128)S(6)} %copy.5.p0, s32[1]{0:T(128)} %collective-permute-done.p1, bf16[384,512]{1,0:T(8,128)(2,1)S(1)} %pad_maximum_fusion.own, bf16[128,512]{1,0:T(8,128)(2,1)S(1)} %collective-permute-done.1.q1, ...), custom_call_target="tpu_custom_call" | custom-call | tf_op jit(solution)/shard_map/merge/merge/pallas_call | solution.py:187
  3.5 3.0 %collective-permute-start.5 = (bf16[528,128]{1,0:T(8,128)(2,1)S(1)}, bf16[528,128]{1,0:T(8,128)(2,1)S(1)}, u32[]{:S(2)}, u32[]{:S(2)}) collective-permute-start(bf16[528,128]{1,0:T(8,128)(2,1)S(1)} %get-tuple-element.36.refs_0_), channel_id=1, source_target_pairs={{0,8},{8,0},{16,24},{24,16},{1,9},{9,1},{17,25},{25,17},{2,10},{10... | collective-permute-start | bytes 405512 | tf_op jit(solution)/shard_map/exchange/ppermute | solution.py:207
  6.5 1.5 %collective-permute-start.4 = (bf16[512,128]{1,0:T(8,128)(2,1)S(1)}, bf16[512,128]{1,0:T(8,128)(2,1)S(1)}, u32[]{:S(2)}, u32[]{:S(2)}) collective-permute-start(bf16[512,128]{1,0:T(8,128)(2,1)S(1)} %get-tuple-element.34.refs_0_), channel_id=1, source_target_pairs={{0,16},{8,24},{16,0},{24,8},{1,17},{9,25},{17,1},{25,9},{2,18},{10... | collective-permute-start | bytes 393224 | tf_op jit(solution)/shard_map/exchange/ppermute | solution.py:207
  8.0 2.6 %collective-permute-start.9 = (bf16[528,128]{1,0:T(8,128)(2,1)S(1)}, bf16[528,128]{1,0:T(8,128)(2,1)S(1)}, u32[]{:S(2)}, u32[]{:S(2)}) collective-permute-start(bf16[528,128]{1,0:T(8,128)(2,1)S(1)} %get-tuple-element.35.q_ref), channel_id=1, source_target_pairs={{0,4},{1,5},{2,6},{3,7},{4,0},{5,1},{6,2},{7,3},{8,12},{9,13},{10,... | collective-permute-start | bytes 405512 | tf_op jit(solution)/shard_map/exchange/ppermute | solution.py:222
  10.6 0.5 %collective-permute-start.6 = (bf16[528,128]{1,0:T(8,128)(2,1)S(1)}, bf16[528,128]{1,0:T(8,128)(2,1)S(1)}, u32[]{:S(2)}, u32[]{:S(2)}) collective-permute-start(bf16[528,128]{1,0:T(8,128)(2,1)S(1)} %get-tuple-element.36.refs_0_), channel_id=1, source_target_pairs={{0,16},{8,24},{16,0},{24,8},{1,17},{9,25},{17,1},{25,9},{2,18},{10... | collective-permute-start | bytes 405512 | tf_op jit(solution)/shard_map/exchange/ppermute | solution.py:207
  11.1 0.0 collective-permute-done.5.refs_1_
  11.1 1.5 %collective-permute-start.7 = (bf16[528,128]{1,0:T(8,128)(2,1)S(1)}, bf16[528,128]{1,0:T(8,128)(2,1)S(1)}, u32[]{:S(2)}, u32[]{:S(2)}) collective-permute-start(bf16[528,128]{1,0:T(8,128)(2,1)S(1)} %collective-permute-done.5.refs_1_), channel_id=1, source_target_pairs={{0,16},{8,24},{16,0},{24,8},{1,17},{9,25},{17,1},{25,9},{2,18},{10... | collective-permute-start | bytes 405512 | tf_op jit(solution)/shard_map/exchange/ppermute | solution.py:207
  12.7 0.0 collective-permute-done.4.refs_2_
  12.7 1.6 %collective-permute-start.8 = (bf16[528,128]{1,0:T(8,128)(2,1)S(1)}, bf16[528,128]{1,0:T(8,128)(2,1)S(1)}, u32[]{:S(2)}, u32[]{:S(2)}) collective-permute-start(bf16[528,128]{1,0:T(8,128)(2,1)S(1)} %get-tuple-element.35.q_ref), channel_id=1, source_target_pairs={{0,2},{1,3},{2,0},{3,1},{4,6},{5,7},{6,4},{7,5},{8,10},{9,11},{10,... | collective-permute-start | bytes 405512 | tf_op jit(solution)/shard_map/exchange/ppermute | solution.py:222
  14.2 2.6 %collective-permute-done.9.q_ref = bf16[528,128]{1,0:T(8,128)(2,1)S(1)} collective-permute-done((bf16[528,128]{1,0:T(8,128)(2,1)S(1)}, bf16[528,128]{1,0:T(8,128)(2,1)S(1)}, u32[]{:S(2)}, u32[]{:S(2)}) %collective-permute-start.9) | collective-permute-done | bytes 135200 | tf_op jit(solution)/shard_map/exchange/ppermute | solution.py:222
  16.9 0.6 %collective-permute-start.10 = (bf16[528,128]{1,0:T(8,128)(2,1)S(1)}, bf16[528,128]{1,0:T(8,128)(2,1)S(1)}, u32[]{:S(2)}, u32[]{:S(2)}) collective-permute-start(bf16[528,128]{1,0:T(8,128)(2,1)S(1)} %collective-permute-done.9.q_ref), channel_id=1, source_target_pairs={{0,2},{1,3},{2,0},{3,1},{4,6},{5,7},{6,4},{7,5},{8,10},{9,11},{10,... | collective-permute-start | bytes 405512 | tf_op jit(solution)/shard_map/exchange/ppermute | solution.py:222
  17.5 0.5 %collective-permute-start.11 = (bf16[512,128]{1,0:T(8,128)(2,1)S(1)}, bf16[512,128]{1,0:T(8,128)(2,1)S(1)}, u32[]{:S(2)}, u32[]{:S(2)}) collective-permute-start(bf16[512,128]{1,0:T(8,128)(2,1)S(1)} %get-tuple-element.34.refs_0_), channel_id=1, source_target_pairs={{0,8},{8,0},{16,24},{24,16},{1,9},{9,1},{17,25},{25,17},{2,10},{10... | collective-permute-start | bytes 393224 | tf_op jit(solution)/shard_map/exchange/ppermute | solution.py:207
  18.0 0.0 collective-permute-done.6.refs_2_
  18.0 1.5 %collective-permute-start.12 = (bf16[512,128]{1,0:T(8,128)(2,1)S(1)}, bf16[512,128]{1,0:T(8,128)(2,1)S(1)}, u32[]{:S(2)}, u32[]{:S(2)}) collective-permute-start(bf16[512,128]{1,0:T(8,128)(2,1)S(1)} %collective-permute-done.4.refs_2_), channel_id=1, source_target_pairs={{0,8},{8,0},{16,24},{24,16},{1,9},{9,1},{17,25},{25,17},{2,10},{10... | collective-permute-start | bytes 393224 | tf_op jit(solution)/shard_map/exchange/ppermute | solution.py:207
  19.5 0.0 collective-permute-done.7.refs_3_
  19.5 0.8 %score.4 = (bf16[2,1024,256]{2,1,0:T(8,128)(2,1)S(1)}, f32[16,256]{1,0:T(8,128)S(1)}) custom-call(bf16[528,128]{1,0:T(8,128)(2,1)S(1)} %get-tuple-element.35.q_ref, bf16[528,128]{1,0:T(8,128)(2,1)S(1)} %get-tuple-element.36.refs_0_, bf16[528,128]{1,0:T(8,128)(2,1)S(1)} %collective-permute-done.5.refs_1_, ...), custom_call_target="tpu_custom_call" | custom-call | flops 134217728 | bytes 1048576 | tf_op jit(solution)/shard_map/score/score/pallas_call | solution.py:233
  20.3 0.0 collective-permute-done.8.q_ref
  20.3 0.8 %score.5 = (bf16[2,1024,256]{2,1,0:T(8,128)(2,1)S(1)}, f32[16,256]{1,0:T(8,128)S(1)}) custom-call(bf16[528,128]{1,0:T(8,128)(2,1)S(1)} %collective-permute-done.8.q_ref, bf16[528,128]{1,0:T(8,128)(2,1)S(1)} %get-tuple-element.36.refs_0_, bf16[528,128]{1,0:T(8,128)(2,1)S(1)} %collective-permute-done.5.refs_1_, ...), custom_call_target="tpu_custom_call" | custom-call | flops 134217728 | bytes 1048576 | tf_op jit(solution)/shard_map/score/score/pallas_call | solution.py:233
  21.1 0.8 %score.6 = (bf16[2,1024,256]{2,1,0:T(8,128)(2,1)S(1)}, f32[16,256]{1,0:T(8,128)S(1)}) custom-call(bf16[528,128]{1,0:T(8,128)(2,1)S(1)} %collective-permute-done.9.q_ref, bf16[528,128]{1,0:T(8,128)(2,1)S(1)} %get-tuple-element.36.refs_0_, bf16[528,128]{1,0:T(8,128)(2,1)S(1)} %collective-permute-done.5.refs_1_, ...), custom_call_target="tpu_custom_call" | custom-call | flops 134217728 | bytes 1048576 | tf_op jit(solution)/shard_map/score/score/pallas_call | solution.py:233
  21.8 0.1 collective-permute-done.10.q_ref
  21.9 0.8 %score.7 = (bf16[2,1024,256]{2,1,0:T(8,128)(2,1)S(1)}, f32[16,256]{1,0:T(8,128)S(1)}) custom-call(bf16[528,128]{1,0:T(8,128)(2,1)S(1)} %collective-permute-done.10.q_ref, bf16[528,128]{1,0:T(8,128)(2,1)S(1)} %get-tuple-element.36.refs_0_, bf16[528,128]{1,0:T(8,128)(2,1)S(1)} %collective-permute-done.5.refs_1_, ...), custom_call_target="tpu_custom_call" | custom-call | flops 134217728 | bytes 1048576 | tf_op jit(solution)/shard_map/score/score/pallas_call | solution.py:233
  22.6 1.2 %collective-permute-done.11.refs_1_ = bf16[512,128]{1,0:T(8,128)(2,1)S(1)} collective-permute-done((bf16[512,128]{1,0:T(8,128)(2,1)S(1)}, bf16[512,128]{1,0:T(8,128)(2,1)S(1)}, u32[]{:S(2)}, u32[]{:S(2)}) %collective-permute-start.11) | collective-permute-done | bytes 131104 | tf_op jit(solution)/shard_map/exchange/ppermute | solution.py:207
  23.9 1.5 %collective-permute-done.12.refs_3_ = bf16[512,128]{1,0:T(8,128)(2,1)S(1)} collective-permute-done((bf16[512,128]{1,0:T(8,128)(2,1)S(1)}, bf16[512,128]{1,0:T(8,128)(2,1)S(1)}, u32[]{:S(2)}, u32[]{:S(2)}) %collective-permute-start.12) | collective-permute-done | bytes 131104 | tf_op jit(solution)/shard_map/exchange/ppermute | solution.py:207
  25.4 0.3 apply.4
  25.8 0.3 collective-permute-start.13
  26.1 0.3 apply.5.refs_0_
  26.5 0.3 apply.6
  26.8 0.3 apply.7
  27.1 3.8 %collective-permute-done.13.refs_1_ = bf16[544,128]{1,0:T(8,128)(2,1)S(1)} collective-permute-done((bf16[544,128]{1,0:T(8,128)(2,1)S(1)}, bf16[544,128]{1,0:T(8,128)(2,1)S(1)}, u32[]{:S(2)}, u32[]{:S(2)}) %collective-permute-start.13) | collective-permute-done | bytes 139296 | tf_op jit(solution)/shard_map/return/ppermute | solution.py:278
  30.9 0.1 add.1
  31.0 0.1 collective-permute-start.14
  31.1 3.4 %collective-permute-start.15 = (bf16[272,128]{1,0:T(8,128)(2,1)S(1)}, bf16[272,128]{1,0:T(8,128)(2,1)S(1)}, u32[]{:S(2)}, u32[]{:S(2)}) collective-permute-start(bf16[272,128]{1,0:T(8,128)(2,1)S(1)} %get-tuple-element.55), channel_id=1, source_target_pairs={{0,4},{1,5},{2,6},{3,7},{4,0},{5,1},{6,2},{7,3},{8,12},{9,13},{10,... | collective-permute-start | bytes 208904 | tf_op jit(solution)/shard_map/return/ppermute | solution.py:276
  34.5 0.1 collective-permute-start.16
  34.6 0.3 collective-permute-start.17
  34.9 1.2 %collective-permute-start.18 = (bf16[272,128]{1,0:T(8,128)(2,1)S(1)}, bf16[272,128]{1,0:T(8,128)(2,1)S(1)}, u32[]{:S(2)}, u32[]{:S(2)}) collective-permute-start(bf16[272,128]{1,0:T(8,128)(2,1)S(1)} %get-tuple-element.60), channel_id=1, source_target_pairs={{0,3},{1,2},{2,1},{3,0},{4,7},{5,6},{6,5},{7,4},{8,11},{9,10},{10,... | collective-permute-start | bytes 208904 | tf_op jit(solution)/shard_map/return/ppermute | solution.py:276
  36.1 4.0 %collective-permute-done.15.refs_2_ = bf16[272,128]{1,0:T(8,128)(2,1)S(1)} collective-permute-done((bf16[272,128]{1,0:T(8,128)(2,1)S(1)}, bf16[272,128]{1,0:T(8,128)(2,1)S(1)}, u32[]{:S(2)}, u32[]{:S(2)}) %collective-permute-start.15) | collective-permute-done | bytes 69664 | tf_op jit(solution)/shard_map/return/ppermute | solution.py:276
  40.1 1.5 %collective-permute-done.16.refs_3_ = bf16[272,128]{1,0:T(8,128)(2,1)S(1)} collective-permute-done((bf16[272,128]{1,0:T(8,128)(2,1)S(1)}, bf16[272,128]{1,0:T(8,128)(2,1)S(1)}, u32[]{:S(2)}, u32[]{:S(2)}) %collective-permute-start.16) | collective-permute-done | bytes 69664 | tf_op jit(solution)/shard_map/return/ppermute | solution.py:276
  41.5 1.3 %collective-permute-done.18.refs_5_ = bf16[272,128]{1,0:T(8,128)(2,1)S(1)} collective-permute-done((bf16[272,128]{1,0:T(8,128)(2,1)S(1)}, bf16[272,128]{1,0:T(8,128)(2,1)S(1)}, u32[]{:S(2)}, u32[]{:S(2)}) %collective-permute-start.18) | collective-permute-done | bytes 69664 | tf_op jit(solution)/shard_map/return/ppermute | solution.py:276
  42.9 0.8 %combine.1 = bf16[128,512]{1,0:T(8,128)(2,1)} custom-call(bf16[272,128]{1,0:T(8,128)(2,1)S(1)} %get-tuple-element.53.refs_0_, bf16[272,128]{1,0:T(8,128)(2,1)S(1)} %collective-permute-done.14.refs_1_, bf16[272,128]{1,0:T(8,128)(2,1)S(1)} %collective-permute-done.15.refs_2_, bf16[272,128]{1,0:T(8,128)(2,1)S(1)} %collective-permute-done.16.refs_3_, ...), custom_call_target="tpu_custom_call" | custom-call | tf_op jit(solution)/shard_map/combine/combine/pallas_call | solution.py:302
  (2 shorter events, 0.0 us)
Async XLA Ops:
  0.0 2.7 %collective-permute-start.1 = (bf16[128,512]{1,0:T(8,128)(2,1)}, bf16[128,512]{1,0:T(8,128)(2,1)S(1)}, u32[]{:S(2)}, u32[]{:S(2)}) collective-permute-start(bf16[128,512]{1,0:T(8,128)(2,1)} %param.4), channel_id=1, source_target_pairs={{0,1},{1,0},{2,3},{3,2},{4,5},{5,4},{6,7},{7,6},{8,9},{9,8},{10,11... | collective-permute-start | bytes 393224 | tf_op jit(solution)/shard_map/swap/ppermute | solution.py:182
  0.5 2.3 %collective-permute-start.2 = (bf16[128,512]{1,0:T(8,128)(2,1)}, bf16[128,512]{1,0:T(8,128)(2,1)S(1)}, u32[]{:S(2)}, u32[]{:S(2)}) collective-permute-start(bf16[128,512]{1,0:T(8,128)(2,1)} %param.5), channel_id=1, source_target_pairs={{0,1},{1,0},{2,3},{3,2},{4,5},{5,4},{6,7},{7,6},{8,9},{9,8},{10,11... | collective-permute-start | bytes 393224 | tf_op jit(solution)/shard_map/swap/ppermute | solution.py:182
  0.5 2.3 %collective-permute-start.3 = (bf16[128,512]{1,0:T(8,128)(2,1)}, bf16[128,512]{1,0:T(8,128)(2,1)S(1)}, u32[]{:S(2)}, u32[]{:S(2)}) collective-permute-start(bf16[128,512]{1,0:T(8,128)(2,1)} %param.6), channel_id=1, source_target_pairs={{0,1},{1,0},{2,3},{3,2},{4,5},{5,4},{6,7},{7,6},{8,9},{9,8},{10,11... | collective-permute-start | bytes 393224 | tf_op jit(solution)/shard_map/swap/ppermute | solution.py:182
  1.0 1.8 %collective-permute-start = (s32[1]{0:T(128)}, s32[1]{0:T(128)}, u32[]{:S(2)}, u32[]{:S(2)}) collective-permute-start(s32[1]{0:T(128)} %param.7), channel_id=1, source_target_pairs={{0,1},{1,0},{2,3},{3,2},{4,5},{5,4},{6,7},{7,6},{8,9},{9,8},{10,11... | collective-permute-start | bytes 20 | tf_op jit(solution)/shard_map/swap/ppermute | solution.py:182
  3.5 7.6 %collective-permute-start.5 = (bf16[528,128]{1,0:T(8,128)(2,1)S(1)}, bf16[528,128]{1,0:T(8,128)(2,1)S(1)}, u32[]{:S(2)}, u32[]{:S(2)}) collective-permute-start(bf16[528,128]{1,0:T(8,128)(2,1)S(1)} %get-tuple-element.36.refs_0_), channel_id=1, source_target_pairs={{0,8},{8,0},{16,24},{24,16},{1,9},{9,1},{17,25},{25,17},{2,10},{10... | collective-permute-start | bytes 405512 | tf_op jit(solution)/shard_map/exchange/ppermute | solution.py:207
  6.5 6.1 %collective-permute-start.4 = (bf16[512,128]{1,0:T(8,128)(2,1)S(1)}, bf16[512,128]{1,0:T(8,128)(2,1)S(1)}, u32[]{:S(2)}, u32[]{:S(2)}) collective-permute-start(bf16[512,128]{1,0:T(8,128)(2,1)S(1)} %get-tuple-element.34.refs_0_), channel_id=1, source_target_pairs={{0,16},{8,24},{16,0},{24,8},{1,17},{9,25},{17,1},{25,9},{2,18},{10... | collective-permute-start | bytes 393224 | tf_op jit(solution)/shard_map/exchange/ppermute | solution.py:207
  8.0 8.8 %collective-permute-start.9 = (bf16[528,128]{1,0:T(8,128)(2,1)S(1)}, bf16[528,128]{1,0:T(8,128)(2,1)S(1)}, u32[]{:S(2)}, u32[]{:S(2)}) collective-permute-start(bf16[528,128]{1,0:T(8,128)(2,1)S(1)} %get-tuple-element.35.q_ref), channel_id=1, source_target_pairs={{0,4},{1,5},{2,6},{3,7},{4,0},{5,1},{6,2},{7,3},{8,12},{9,13},{10,... | collective-permute-start | bytes 405512 | tf_op jit(solution)/shard_map/exchange/ppermute | solution.py:222
  10.6 7.4 %collective-permute-start.6 = (bf16[528,128]{1,0:T(8,128)(2,1)S(1)}, bf16[528,128]{1,0:T(8,128)(2,1)S(1)}, u32[]{:S(2)}, u32[]{:S(2)}) collective-permute-start(bf16[528,128]{1,0:T(8,128)(2,1)S(1)} %get-tuple-element.36.refs_0_), channel_id=1, source_target_pairs={{0,16},{8,24},{16,0},{24,8},{1,17},{9,25},{17,1},{25,9},{2,18},{10... | collective-permute-start | bytes 405512 | tf_op jit(solution)/shard_map/exchange/ppermute | solution.py:207
  11.1 8.4 %collective-permute-start.7 = (bf16[528,128]{1,0:T(8,128)(2,1)S(1)}, bf16[528,128]{1,0:T(8,128)(2,1)S(1)}, u32[]{:S(2)}, u32[]{:S(2)}) collective-permute-start(bf16[528,128]{1,0:T(8,128)(2,1)S(1)} %collective-permute-done.5.refs_1_), channel_id=1, source_target_pairs={{0,16},{8,24},{16,0},{24,8},{1,17},{9,25},{17,1},{25,9},{2,18},{10... | collective-permute-start | bytes 405512 | tf_op jit(solution)/shard_map/exchange/ppermute | solution.py:207
  12.7 7.6 %collective-permute-start.8 = (bf16[528,128]{1,0:T(8,128)(2,1)S(1)}, bf16[528,128]{1,0:T(8,128)(2,1)S(1)}, u32[]{:S(2)}, u32[]{:S(2)}) collective-permute-start(bf16[528,128]{1,0:T(8,128)(2,1)S(1)} %get-tuple-element.35.q_ref), channel_id=1, source_target_pairs={{0,2},{1,3},{2,0},{3,1},{4,6},{5,7},{6,4},{7,5},{8,10},{9,11},{10,... | collective-permute-start | bytes 405512 | tf_op jit(solution)/shard_map/exchange/ppermute | solution.py:222
  16.9 5.0 %collective-permute-start.10 = (bf16[528,128]{1,0:T(8,128)(2,1)S(1)}, bf16[528,128]{1,0:T(8,128)(2,1)S(1)}, u32[]{:S(2)}, u32[]{:S(2)}) collective-permute-start(bf16[528,128]{1,0:T(8,128)(2,1)S(1)} %collective-permute-done.9.q_ref), channel_id=1, source_target_pairs={{0,2},{1,3},{2,0},{3,1},{4,6},{5,7},{6,4},{7,5},{8,10},{9,11},{10,... | collective-permute-start | bytes 405512 | tf_op jit(solution)/shard_map/exchange/ppermute | solution.py:222
  17.5 6.4 %collective-permute-start.11 = (bf16[512,128]{1,0:T(8,128)(2,1)S(1)}, bf16[512,128]{1,0:T(8,128)(2,1)S(1)}, u32[]{:S(2)}, u32[]{:S(2)}) collective-permute-start(bf16[512,128]{1,0:T(8,128)(2,1)S(1)} %get-tuple-element.34.refs_0_), channel_id=1, source_target_pairs={{0,8},{8,0},{16,24},{24,16},{1,9},{9,1},{17,25},{25,17},{2,10},{10... | collective-permute-start | bytes 393224 | tf_op jit(solution)/shard_map/exchange/ppermute | solution.py:207
  18.0 7.4 %collective-permute-start.12 = (bf16[512,128]{1,0:T(8,128)(2,1)S(1)}, bf16[512,128]{1,0:T(8,128)(2,1)S(1)}, u32[]{:S(2)}, u32[]{:S(2)}) collective-permute-start(bf16[512,128]{1,0:T(8,128)(2,1)S(1)} %collective-permute-done.4.refs_2_), channel_id=1, source_target_pairs={{0,8},{8,0},{16,24},{24,16},{1,9},{9,1},{17,25},{25,17},{2,10},{10... | collective-permute-start | bytes 393224 | tf_op jit(solution)/shard_map/exchange/ppermute | solution.py:207
  25.8 5.1 %collective-permute-start.13 = (bf16[544,128]{1,0:T(8,128)(2,1)S(1)}, bf16[544,128]{1,0:T(8,128)(2,1)S(1)}, u32[]{:S(2)}, u32[]{:S(2)}) collective-permute-start(bf16[544,128]{1,0:T(8,128)(2,1)S(1)} %apply.4), channel_id=1, source_target_pairs={{0,2},{1,3},{2,0},{3,1},{4,6},{5,7},{6,4},{7,5},{8,10},{9,11},{10,... | collective-permute-start | bytes 417800 | tf_op jit(solution)/shard_map/return/ppermute | solution.py:278
  31.0 3.6 %collective-permute-start.14 = (bf16[272,128]{1,0:T(8,128)(2,1)S(1)}, bf16[272,128]{1,0:T(8,128)(2,1)S(1)}, u32[]{:S(2)}, u32[]{:S(2)}) collective-permute-start(bf16[272,128]{1,0:T(8,128)(2,1)S(1)} %get-tuple-element.56), channel_id=1, source_target_pairs={{0,1},{1,0},{2,3},{3,2},{4,5},{5,4},{6,7},{7,6},{8,9},{9,8},{10,11... | collective-permute-start | bytes 208904 | tf_op jit(solution)/shard_map/return/ppermute | solution.py:297
  31.1 9.0 %collective-permute-start.15 = (bf16[272,128]{1,0:T(8,128)(2,1)S(1)}, bf16[272,128]{1,0:T(8,128)(2,1)S(1)}, u32[]{:S(2)}, u32[]{:S(2)}) collective-permute-start(bf16[272,128]{1,0:T(8,128)(2,1)S(1)} %get-tuple-element.55), channel_id=1, source_target_pairs={{0,4},{1,5},{2,6},{3,7},{4,0},{5,1},{6,2},{7,3},{8,12},{9,13},{10,... | collective-permute-start | bytes 208904 | tf_op jit(solution)/shard_map/return/ppermute | solution.py:276
  34.5 7.0 %collective-permute-start.16 = (bf16[272,128]{1,0:T(8,128)(2,1)S(1)}, bf16[272,128]{1,0:T(8,128)(2,1)S(1)}, u32[]{:S(2)}, u32[]{:S(2)}) collective-permute-start(bf16[272,128]{1,0:T(8,128)(2,1)S(1)} %get-tuple-element.57), channel_id=1, source_target_pairs={{0,5},{1,4},{2,7},{3,6},{4,1},{5,0},{6,3},{7,2},{8,13},{9,12},{10,... | collective-permute-start | bytes 208904 | tf_op jit(solution)/shard_map/return/ppermute | solution.py:276
  34.6 7.0 %collective-permute-start.17 = (bf16[272,128]{1,0:T(8,128)(2,1)S(1)}, bf16[272,128]{1,0:T(8,128)(2,1)S(1)}, u32[]{:S(2)}, u32[]{:S(2)}) collective-permute-start(bf16[272,128]{1,0:T(8,128)(2,1)S(1)} %get-tuple-element.58), channel_id=1, source_target_pairs={{0,2},{1,3},{2,0},{3,1},{4,6},{5,7},{6,4},{7,5},{8,10},{9,11},{10,... | collective-permute-start | bytes 208904 | tf_op jit(solution)/shard_map/return/ppermute | solution.py:276
  34.9 8.0 %collective-permute-start.18 = (bf16[272,128]{1,0:T(8,128)(2,1)S(1)}, bf16[272,128]{1,0:T(8,128)(2,1)S(1)}, u32[]{:S(2)}, u32[]{:S(2)}) collective-permute-start(bf16[272,128]{1,0:T(8,128)(2,1)S(1)} %get-tuple-element.60), channel_id=1, source_target_pairs={{0,3},{1,2},{2,1},{3,0},{4,7},{5,6},{6,5},{7,4},{8,11},{9,10},{10,... | collective-permute-start | bytes 208904 | tf_op jit(solution)/shard_map/return/ppermute | solution.py:276

commit v12 on v11

--- a/solution.py
+++ b/solution.py
@@ -218,7 +218,11 @@
         bit = chips // 2
         while bit:
             for r in sorted(q_by):
-                piece = q_by[r] if bit == chips // 2 else after(q_by[r], passed)
+                piece = q_by[r]
+                if r:
+                    piece = after(piece, passed)
+                elif bit == 1:
+                    piece = after(piece, k_by[n_out - 1])
                 q_by[r | bit] = lax.ppermute(piece, "inner", along_inner(bit, 0))
             bit //= 2
 
@@ -278,8 +282,8 @@
                 arrived[r - low(r)].append(lax.ppermute(parts[0], "inner", along_inner(low(r), 0)))
 
     weights_by = {}
-    done = passed
-    for r in range(chips):
+    done = [v_by[r] for r in range(1, n_out) if single(r)]
+    for r in sorted(range(chips), key=lambda r: (r == 1, r)):
         weights_by[r] = score(r, done)
         done = weights_by[r][1]
     done = None
@@ -287,17 +291,13 @@
     for r in reversed(range(chips)):
         partial[r] = apply(r, r > 1, done)
         done = partial[r][0]
-    for r in reversed(range(2, chips)):
+    for r in reversed(range(1, chips)):
         parts = partial[r]
         if arrived[r]:
             parts = add([parts[0], *arrived[r]], not single(r))
-            done = parts[0]
         send(r, parts)
     with jax.named_scope("return"):
-        across = lax.ppermute(after(partial[0][1], done), "inner", along_inner(0, 1))
-    if chips > 1:
-        send(1, [after(part, across) for part in partial[1]])
-    ends = [partial[0][0], across] + ends
+        ends = [partial[0][0], lax.ppermute(partial[0][1], "inner", along_inner(0, 1))] + ends
     with jax.named_scope("combine"):
         return pl.pallas_call(
             functools.partial(combine_kernel, len(ends)),

time: 43.9 us -> 39.4 us (0.90)
  waiting for transfers between devices: 16.1 us -> 10.2 us
  starting transfers between devices: 19.8 us -> 21.3 us
    ppermute x1, waiting for transfers between devices: 3.76 us -> 0.22 us  [send(): lax.ppermute(parts[0], 'inner', along_inner(low(r), 0))]
    ppermute x3, waiting for transfers between devices: 2.7 us -> 0.27 us  [shards(): q_by[r | bit] = lax.ppermute(piece, 'inner', along_inner(bit, 0))]
    ppermute x1, starting transfers between devices: 0.35 us -> 1.53 us  [send(): lax.ppermute(parts[0], 'inner', along_inner(low(r), 0))]
    ppermute x3, starting transfers between devices: 4.77 us -> 5.74 us  [shards(): q_by[r | bit] = lax.ppermute(piece, 'inner', along_inner(bit, 0))]
    ppermute x6, starting transfers between devices: 8.58 us -> 7.96 us  [over(): return lax.ppermute(a, 'outer', [(o, o ^ r) for o in range(n_out)])]
  transfers between devices with their start and end apart: 19 -> 19, of which waited for: 8 -> 7; matrix products, arithmetic and copies ran while one was open for 2% -> 3% of each run, Pallas kernels for 9% -> 11%
where the time goes in v12:
time: 39.4 us; the launch traced here: 39.3 us
  starting transfers between devices  21.3 us (54%)
  waiting for transfers between devices  10.2 us (26%)
  Pallas kernels  5.99 us (15%)
  other arithmetic  1.06 us (3%)
  between operations  0.81 us (2%)
    ppermute x6, starting transfers between devices, over(): return lax.ppermute(a, 'outer', [(o, o ^ r) for o in range(n_out)])  7.96 us
    ppermute x4, waiting for transfers between devices, send(): lax.ppermute(parts[x], 'inner', along_inner(r, x))  7.01 us
    ppermute x3, starting transfers between devices, shards(): q_by[r | bit] = lax.ppermute(piece, 'inner', along_inner(bit, 0))  5.74 us
    ppermute x4, starting transfers between devices, send(): lax.ppermute(parts[x], 'inner', along_inner(r, x))  4.93 us
    pallas_call x4, Pallas kernels, score(): pl.pallas_call(functools.partial(score_kernel, r == 0), out_shape=(jax.Sh...  3.04 us
    ppermute x6, waiting for transfers between devices, over(): return lax.ppermute(a, 'outer', [(o, o ^ r) for o in range(n_out)])  2.65 us
    ppermute x1, starting transfers between devices, send(): lax.ppermute(parts[0], 'inner', along_inner(low(r), 0))  1.53 us
    pallas_call x4, Pallas kernels, apply(): pl.pallas_call(functools.partial(apply_kernel, wide), out_shape=shapes(wi...  1.32 us
  transfers between devices with their start and end apart: 19, of which 7 were waited for; matrix products, arithmetic and copies ran while one was open for 3% of the time, Pallas kernels for 11%

profile of v12, /device:TPU:0, one launch (start us, length us, event | category | flops | bytes accessed | tf_op | source)
XLA Modules:
  0.0 39.3 jit_solution(9102462015889076154)
XLA Ops:
  0.0 0.5 %collective-permute-start.1 = (bf16[128,512]{1,0:T(8,128)(2,1)}, bf16[128,512]{1,0:T(8,128)(2,1)S(1)}, u32[]{:S(2)}, u32[]{:S(2)}) collective-permute-start(bf16[128,512]{1,0:T(8,128)(2,1)} %param.4), channel_id=1, source_target_pairs={{0,1},{1,0},{2,3},{3,2},{4,5},{5,4},{6,7},{7,6},{8,9},{9,8},{10,11... | collective-permute-start | bytes 393224 | tf_op jit(solution)/shard_map/swap/ppermute | solution.py:182
  0.5 0.1 collective-permute-start.2
  0.5 0.5 %collective-permute-start.3 = (bf16[128,512]{1,0:T(8,128)(2,1)}, bf16[128,512]{1,0:T(8,128)(2,1)S(1)}, u32[]{:S(2)}, u32[]{:S(2)}) collective-permute-start(bf16[128,512]{1,0:T(8,128)(2,1)} %param.6), channel_id=1, source_target_pairs={{0,1},{1,0},{2,3},{3,2},{4,5},{5,4},{6,7},{7,6},{8,9},{9,8},{10,11... | collective-permute-start | bytes 393224 | tf_op jit(solution)/shard_map/swap/ppermute | solution.py:182
  1.0 0.1 collective-permute-start
  1.7 1.1 %pad_maximum_fusion.own = bf16[384,512]{1,0:T(8,128)(2,1)S(1)} fusion(bf16[128,512]{1,0:T(8,128)(2,1)} %param.6, bf16[128,512]{1,0:T(8,128)(2,1)} %param.5, bf16[128,512]{1,0:T(8,128)(2,1)} %param.4), kind=kLoop, calls=%fused_computation | loop fusion | flops 1179648 | bytes 786432 | tf_op jit(solution)/shard_map/swap/concatenate | solution.py:183
  2.7 0.0 collective-permute-done.p1
  2.7 0.0 collective-permute-done.1.q1
  2.8 0.0 collective-permute-done.2.k1
  2.8 0.0 collective-permute-done.3.v1
  2.8 0.7 %merge.1 = (bf16[528,128]{1,0:T(8,128)(2,1)S(1)}, bf16[528,128]{1,0:T(8,128)(2,1)S(1)}, bf16[512,128]{1,0:T(8,128)(2,1)S(1)}) custom-call(s32[1]{0:T(128)S(6)} %copy.5.p0, s32[1]{0:T(128)} %collective-permute-done.p1, bf16[384,512]{1,0:T(8,128)(2,1)S(1)} %pad_maximum_fusion.own, bf16[128,512]{1,0:T(8,128)(2,1)S(1)} %collective-permute-done.1.q1, ...), custom_call_target="tpu_custom_call" | custom-call | tf_op jit(solution)/shard_map/merge/merge/pallas_call | solution.py:187
  3.5 3.0 %collective-permute-start.6 = (bf16[528,128]{1,0:T(8,128)(2,1)S(1)}, bf16[528,128]{1,0:T(8,128)(2,1)S(1)}, u32[]{:S(2)}, u32[]{:S(2)}) collective-permute-start(bf16[528,128]{1,0:T(8,128)(2,1)S(1)} %get-tuple-element.34.refs_0_), channel_id=1, source_target_pairs={{0,8},{8,0},{16,24},{24,16},{1,9},{9,1},{17,25},{25,17},{2,10},{10... | collective-permute-start | bytes 405512 | tf_op jit(solution)/shard_map/exchange/ppermute | solution.py:207
  6.5 2.6 %collective-permute-start.10 = (bf16[528,128]{1,0:T(8,128)(2,1)S(1)}, bf16[528,128]{1,0:T(8,128)(2,1)S(1)}, u32[]{:S(2)}, u32[]{:S(2)}) collective-permute-start(bf16[528,128]{1,0:T(8,128)(2,1)S(1)} %get-tuple-element.37.q_ref), channel_id=1, source_target_pairs={{0,4},{1,5},{2,6},{3,7},{4,0},{5,1},{6,2},{7,3},{8,12},{9,13},{10,... | collective-permute-start | bytes 405512 | tf_op jit(solution)/shard_map/exchange/ppermute | solution.py:226
  9.1 1.5 %collective-permute-start.5 = (bf16[512,128]{1,0:T(8,128)(2,1)S(1)}, bf16[512,128]{1,0:T(8,128)(2,1)S(1)}, u32[]{:S(2)}, u32[]{:S(2)}) collective-permute-start(bf16[512,128]{1,0:T(8,128)(2,1)S(1)} %get-tuple-element.32.refs_0_), channel_id=1, source_target_pairs={{0,16},{8,24},{16,0},{24,8},{1,17},{9,25},{17,1},{25,9},{2,18},{10... | collective-permute-start | bytes 393224 | tf_op jit(solution)/shard_map/exchange/ppermute | solution.py:207
  10.6 0.0 collective-permute-done.6.refs_1_
  10.6 1.4 %collective-permute-start.8 = (bf16[528,128]{1,0:T(8,128)(2,1)S(1)}, bf16[528,128]{1,0:T(8,128)(2,1)S(1)}, u32[]{:S(2)}, u32[]{:S(2)}) collective-permute-start(bf16[528,128]{1,0:T(8,128)(2,1)S(1)} %collective-permute-done.6.refs_1_), channel_id=1, source_target_pairs={{0,16},{8,24},{16,0},{24,8},{1,17},{9,25},{17,1},{25,9},{2,18},{10... | collective-permute-start | bytes 405512 | tf_op jit(solution)/shard_map/exchange/ppermute | solution.py:207
  12.0 0.6 %collective-permute-start.7 = (bf16[528,128]{1,0:T(8,128)(2,1)S(1)}, bf16[528,128]{1,0:T(8,128)(2,1)S(1)}, u32[]{:S(2)}, u32[]{:S(2)}) collective-permute-start(bf16[528,128]{1,0:T(8,128)(2,1)S(1)} %get-tuple-element.34.refs_0_), channel_id=1, source_target_pairs={{0,16},{8,24},{16,0},{24,8},{1,17},{9,25},{17,1},{25,9},{2,18},{10... | collective-permute-start | bytes 405512 | tf_op jit(solution)/shard_map/exchange/ppermute | solution.py:207
  12.7 1.4 %collective-permute-start.4 = (bf16[512,128]{1,0:T(8,128)(2,1)S(1)}, bf16[512,128]{1,0:T(8,128)(2,1)S(1)}, u32[]{:S(2)}, u32[]{:S(2)}) collective-permute-start(bf16[512,128]{1,0:T(8,128)(2,1)S(1)} %get-tuple-element.32.refs_0_), channel_id=1, source_target_pairs={{0,8},{8,0},{16,24},{24,16},{1,9},{9,1},{17,25},{25,17},{2,10},{10... | collective-permute-start | bytes 393224 | tf_op jit(solution)/shard_map/exchange/ppermute | solution.py:207
  14.1 1.5 %collective-permute-done.5.refs_2_ = bf16[512,128]{1,0:T(8,128)(2,1)S(1)} collective-permute-done((bf16[512,128]{1,0:T(8,128)(2,1)S(1)}, bf16[512,128]{1,0:T(8,128)(2,1)S(1)}, u32[]{:S(2)}, u32[]{:S(2)}) %collective-permute-start.5) | collective-permute-done | bytes 131104 | tf_op jit(solution)/shard_map/exchange/ppermute | solution.py:207
  15.5 0.0 collective-permute-done.10.q_ref
  15.5 1.6 %collective-permute-start.11 = (bf16[528,128]{1,0:T(8,128)(2,1)S(1)}, bf16[528,128]{1,0:T(8,128)(2,1)S(1)}, u32[]{:S(2)}, u32[]{:S(2)}) collective-permute-start(bf16[528,128]{1,0:T(8,128)(2,1)S(1)} %collective-permute-done.10.q_ref), channel_id=1, source_target_pairs={{0,2},{1,3},{2,0},{3,1},{4,6},{5,7},{6,4},{7,5},{8,10},{9,11},{10,... | collective-permute-start | bytes 405512 | tf_op jit(solution)/shard_map/exchange/ppermute | solution.py:226
  17.1 0.0 collective-permute-start.12
  17.1 0.5 %collective-permute-done.4.refs_1_ = bf16[512,128]{1,0:T(8,128)(2,1)S(1)} collective-permute-done((bf16[512,128]{1,0:T(8,128)(2,1)S(1)}, bf16[512,128]{1,0:T(8,128)(2,1)S(1)}, u32[]{:S(2)}, u32[]{:S(2)}) %collective-permute-start.4) | collective-permute-done | bytes 131104 | tf_op jit(solution)/shard_map/exchange/ppermute | solution.py:207
  17.6 0.7 %collective-permute-done.8.refs_3_ = bf16[528,128]{1,0:T(8,128)(2,1)S(1)} collective-permute-done((bf16[528,128]{1,0:T(8,128)(2,1)S(1)}, bf16[528,128]{1,0:T(8,128)(2,1)S(1)}, u32[]{:S(2)}, u32[]{:S(2)}) %collective-permute-start.8) | collective-permute-done | bytes 135200 | tf_op jit(solution)/shard_map/exchange/ppermute | solution.py:207
  18.3 1.6 %collective-permute-start.9 = (bf16[528,128]{1,0:T(8,128)(2,1)S(1)}, bf16[528,128]{1,0:T(8,128)(2,1)S(1)}, u32[]{:S(2)}, u32[]{:S(2)}) collective-permute-start(bf16[528,128]{1,0:T(8,128)(2,1)S(1)} %get-tuple-element.37.q_ref), channel_id=1, source_target_pairs={{0,2},{1,3},{2,0},{3,1},{4,6},{5,7},{6,4},{7,5},{8,10},{9,11},{10,... | collective-permute-start | bytes 405512 | tf_op jit(solution)/shard_map/exchange/ppermute | solution.py:226
  19.9 0.0 collective-permute-done.7.refs_2_
  19.9 0.8 %score.4 = (bf16[2,1024,256]{2,1,0:T(8,128)(2,1)S(1)}, f32[16,256]{1,0:T(8,128)S(1)}) custom-call(bf16[528,128]{1,0:T(8,128)(2,1)S(1)} %get-tuple-element.37.q_ref, bf16[528,128]{1,0:T(8,128)(2,1)S(1)} %get-tuple-element.34.refs_0_, bf16[528,128]{1,0:T(8,128)(2,1)S(1)} %collective-permute-done.6.refs_1_, ...), custom_call_target="tpu_custom_call" | custom-call | flops 134217728 | bytes 1048576 | tf_op jit(solution)/shard_map/score/score/pallas_call | solution.py:237
  20.7 0.8 %score.5 = (bf16[2,1024,256]{2,1,0:T(8,128)(2,1)S(1)}, f32[16,256]{1,0:T(8,128)S(1)}) custom-call(bf16[528,128]{1,0:T(8,128)(2,1)S(1)} %collective-permute-done.10.q_ref, bf16[528,128]{1,0:T(8,128)(2,1)S(1)} %get-tuple-element.34.refs_0_, bf16[528,128]{1,0:T(8,128)(2,1)S(1)} %collective-permute-done.6.refs_1_, ...), custom_call_target="tpu_custom_call" | custom-call | flops 134217728 | bytes 1048576 | tf_op jit(solution)/shard_map/score/score/pallas_call | solution.py:237
  21.4 0.3 collective-permute-done.11.q_ref
  21.7 0.8 %score.6 = (bf16[2,1024,256]{2,1,0:T(8,128)(2,1)S(1)}, f32[16,256]{1,0:T(8,128)S(1)}) custom-call(bf16[528,128]{1,0:T(8,128)(2,1)S(1)} %collective-permute-done.11.q_ref, bf16[528,128]{1,0:T(8,128)(2,1)S(1)} %get-tuple-element.34.refs_0_, bf16[528,128]{1,0:T(8,128)(2,1)S(1)} %collective-permute-done.6.refs_1_, ...), custom_call_target="tpu_custom_call" | custom-call | flops 134217728 | bytes 1048576 | tf_op jit(solution)/shard_map/score/score/pallas_call | solution.py:237
  22.4 0.0 collective-permute-done.12.refs_3_
  22.5 0.3 apply.4
  22.8 1.5 %collective-permute-start.14 = (bf16[544,128]{1,0:T(8,128)(2,1)S(1)}, bf16[544,128]{1,0:T(8,128)(2,1)S(1)}, u32[]{:S(2)}, u32[]{:S(2)}) collective-permute-start(bf16[544,128]{1,0:T(8,128)(2,1)S(1)} %apply.4), channel_id=1, source_target_pairs={{0,2},{1,3},{2,0},{3,1},{4,6},{5,7},{6,4},{7,5},{8,10},{9,11},{10,... | collective-permute-start | bytes 417800 | tf_op jit(solution)/shard_map/return/ppermute | solution.py:282
  24.3 0.3 apply.5.refs_0_
  24.7 0.0 collective-permute-done.9.q_ref
  24.7 0.8 %score.7 = (bf16[2,1024,256]{2,1,0:T(8,128)(2,1)S(1)}, f32[16,256]{1,0:T(8,128)S(1)}) custom-call(bf16[528,128]{1,0:T(8,128)(2,1)S(1)} %collective-permute-done.9.q_ref, bf16[528,128]{1,0:T(8,128)(2,1)S(1)} %get-tuple-element.34.refs_0_, bf16[528,128]{1,0:T(8,128)(2,1)S(1)} %collective-permute-done.6.refs_1_, ...), custom_call_target="tpu_custom_call" | custom-call | flops 134217728 | bytes 1048576 | tf_op jit(solution)/shard_map/score/score/pallas_call | solution.py:237
  25.4 0.3 apply.6
  25.8 0.6 %collective-permute-start.17 = (bf16[272,128]{1,0:T(8,128)(2,1)S(1)}, bf16[272,128]{1,0:T(8,128)(2,1)S(1)}, u32[]{:S(2)}, u32[]{:S(2)}) collective-permute-start(bf16[272,128]{1,0:T(8,128)(2,1)S(1)} %get-tuple-element.50), channel_id=1, source_target_pairs={{0,2},{1,3},{2,0},{3,1},{4,6},{5,7},{6,4},{7,5},{8,10},{9,11},{10,... | collective-permute-start | bytes 208904 | tf_op jit(solution)/shard_map/return/ppermute | solution.py:280
  26.4 0.3 apply.7
  26.7 0.1 collective-permute-start.13
  26.8 1.6 %collective-permute-start.18 = (bf16[272,128]{1,0:T(8,128)(2,1)S(1)}, bf16[272,128]{1,0:T(8,128)(2,1)S(1)}, u32[]{:S(2)}, u32[]{:S(2)}) collective-permute-start(bf16[272,128]{1,0:T(8,128)(2,1)S(1)} %get-tuple-element.56), channel_id=1, source_target_pairs={{0,3},{1,2},{2,1},{3,0},{4,7},{5,6},{6,5},{7,4},{8,11},{9,10},{10,... | collective-permute-start | bytes 208904 | tf_op jit(solution)/shard_map/return/ppermute | solution.py:280
  28.4 0.2 collective-permute-done.14.refs_1_
  28.6 0.1 add.1
  28.7 2.7 %collective-permute-start.15 = (bf16[272,128]{1,0:T(8,128)(2,1)S(1)}, bf16[272,128]{1,0:T(8,128)(2,1)S(1)}, u32[]{:S(2)}, u32[]{:S(2)}) collective-permute-start(bf16[272,128]{1,0:T(8,128)(2,1)S(1)} %get-tuple-element.54), channel_id=1, source_target_pairs={{0,4},{1,5},{2,6},{3,7},{4,0},{5,1},{6,2},{7,3},{8,12},{9,13},{10,... | collective-permute-start | bytes 208904 | tf_op jit(solution)/shard_map/return/ppermute | solution.py:280
  31.4 0.0 collective-permute-done.13.refs_1_
  31.4 0.0 collective-permute-done.18.refs_5_
  31.4 3.0 %collective-permute-done.15.refs_2_ = bf16[272,128]{1,0:T(8,128)(2,1)S(1)} collective-permute-done((bf16[272,128]{1,0:T(8,128)(2,1)S(1)}, bf16[272,128]{1,0:T(8,128)(2,1)S(1)}, u32[]{:S(2)}, u32[]{:S(2)}) %collective-permute-start.15) | collective-permute-done | bytes 69664 | tf_op jit(solution)/shard_map/return/ppermute | solution.py:280
  34.5 4.0 %collective-permute-done.16.refs_3_ = bf16[272,128]{1,0:T(8,128)(2,1)S(1)} collective-permute-done((bf16[272,128]{1,0:T(8,128)(2,1)S(1)}, bf16[272,128]{1,0:T(8,128)(2,1)S(1)}, u32[]{:S(2)}, u32[]{:S(2)}) %collective-permute-start.16) | collective-permute-done | bytes 69664 | tf_op jit(solution)/shard_map/return/ppermute | solution.py:280
  38.5 0.8 %combine.1 = bf16[128,512]{1,0:T(8,128)(2,1)} custom-call(bf16[272,128]{1,0:T(8,128)(2,1)S(1)} %get-tuple-element.52.refs_0_, bf16[272,128]{1,0:T(8,128)(2,1)S(1)} %collective-permute-done.13.refs_1_, bf16[272,128]{1,0:T(8,128)(2,1)S(1)} %collective-permute-done.15.refs_2_, bf16[272,128]{1,0:T(8,128)(2,1)S(1)} %collective-permute-done.16.refs_3_, ...), custom_call_target="tpu_custom_call" | custom-call | tf_op jit(solution)/shard_map/combine/combine/pallas_call | solution.py:302
  (2 shorter events, 0.0 us)
Async XLA Ops:
  0.0 2.7 %collective-permute-start.1 = (bf16[128,512]{1,0:T(8,128)(2,1)}, bf16[128,512]{1,0:T(8,128)(2,1)S(1)}, u32[]{:S(2)}, u32[]{:S(2)}) collective-permute-start(bf16[128,512]{1,0:T(8,128)(2,1)} %param.4), channel_id=1, source_target_pairs={{0,1},{1,0},{2,3},{3,2},{4,5},{5,4},{6,7},{7,6},{8,9},{9,8},{10,11... | collective-permute-start | bytes 393224 | tf_op jit(solution)/shard_map/swap/ppermute | solution.py:182
  0.5 2.3 %collective-permute-start.2 = (bf16[128,512]{1,0:T(8,128)(2,1)}, bf16[128,512]{1,0:T(8,128)(2,1)S(1)}, u32[]{:S(2)}, u32[]{:S(2)}) collective-permute-start(bf16[128,512]{1,0:T(8,128)(2,1)} %param.5), channel_id=1, source_target_pairs={{0,1},{1,0},{2,3},{3,2},{4,5},{5,4},{6,7},{7,6},{8,9},{9,8},{10,11... | collective-permute-start | bytes 393224 | tf_op jit(solution)/shard_map/swap/ppermute | solution.py:182
  0.5 2.3 %collective-permute-start.3 = (bf16[128,512]{1,0:T(8,128)(2,1)}, bf16[128,512]{1,0:T(8,128)(2,1)S(1)}, u32[]{:S(2)}, u32[]{:S(2)}) collective-permute-start(bf16[128,512]{1,0:T(8,128)(2,1)} %param.6), channel_id=1, source_target_pairs={{0,1},{1,0},{2,3},{3,2},{4,5},{5,4},{6,7},{7,6},{8,9},{9,8},{10,11... | collective-permute-start | bytes 393224 | tf_op jit(solution)/shard_map/swap/ppermute | solution.py:182
  1.0 1.8 %collective-permute-start = (s32[1]{0:T(128)}, s32[1]{0:T(128)}, u32[]{:S(2)}, u32[]{:S(2)}) collective-permute-start(s32[1]{0:T(128)} %param.7), channel_id=1, source_target_pairs={{0,1},{1,0},{2,3},{3,2},{4,5},{5,4},{6,7},{7,6},{8,9},{9,8},{10,11... | collective-permute-start | bytes 20 | tf_op jit(solution)/shard_map/swap/ppermute | solution.py:182
  3.5 7.1 %collective-permute-start.6 = (bf16[528,128]{1,0:T(8,128)(2,1)S(1)}, bf16[528,128]{1,0:T(8,128)(2,1)S(1)}, u32[]{:S(2)}, u32[]{:S(2)}) collective-permute-start(bf16[528,128]{1,0:T(8,128)(2,1)S(1)} %get-tuple-element.34.refs_0_), channel_id=1, source_target_pairs={{0,8},{8,0},{16,24},{24,16},{1,9},{9,1},{17,25},{25,17},{2,10},{10... | collective-permute-start | bytes 405512 | tf_op jit(solution)/shard_map/exchange/ppermute | solution.py:207
  6.5 9.0 %collective-permute-start.10 = (bf16[528,128]{1,0:T(8,128)(2,1)S(1)}, bf16[528,128]{1,0:T(8,128)(2,1)S(1)}, u32[]{:S(2)}, u32[]{:S(2)}) collective-permute-start(bf16[528,128]{1,0:T(8,128)(2,1)S(1)} %get-tuple-element.37.q_ref), channel_id=1, source_target_pairs={{0,4},{1,5},{2,6},{3,7},{4,0},{5,1},{6,2},{7,3},{8,12},{9,13},{10,... | collective-permute-start | bytes 405512 | tf_op jit(solution)/shard_map/exchange/ppermute | solution.py:226
  9.1 6.4 %collective-permute-start.5 = (bf16[512,128]{1,0:T(8,128)(2,1)S(1)}, bf16[512,128]{1,0:T(8,128)(2,1)S(1)}, u32[]{:S(2)}, u32[]{:S(2)}) collective-permute-start(bf16[512,128]{1,0:T(8,128)(2,1)S(1)} %get-tuple-element.32.refs_0_), channel_id=1, source_target_pairs={{0,16},{8,24},{16,0},{24,8},{1,17},{9,25},{17,1},{25,9},{2,18},{10... | collective-permute-start | bytes 393224 | tf_op jit(solution)/shard_map/exchange/ppermute | solution.py:207
  10.6 7.7 %collective-permute-start.8 = (bf16[528,128]{1,0:T(8,128)(2,1)S(1)}, bf16[528,128]{1,0:T(8,128)(2,1)S(1)}, u32[]{:S(2)}, u32[]{:S(2)}) collective-permute-start(bf16[528,128]{1,0:T(8,128)(2,1)S(1)} %collective-permute-done.6.refs_1_), channel_id=1, source_target_pairs={{0,16},{8,24},{16,0},{24,8},{1,17},{9,25},{17,1},{25,9},{2,18},{10... | collective-permute-start | bytes 405512 | tf_op jit(solution)/shard_map/exchange/ppermute | solution.py:207
  12.0 7.8 %collective-permute-start.7 = (bf16[528,128]{1,0:T(8,128)(2,1)S(1)}, bf16[528,128]{1,0:T(8,128)(2,1)S(1)}, u32[]{:S(2)}, u32[]{:S(2)}) collective-permute-start(bf16[528,128]{1,0:T(8,128)(2,1)S(1)} %get-tuple-element.34.refs_0_), channel_id=1, source_target_pairs={{0,16},{8,24},{16,0},{24,8},{1,17},{9,25},{17,1},{25,9},{2,18},{10... | collective-permute-start | bytes 405512 | tf_op jit(solution)/shard_map/exchange/ppermute | solution.py:207
  12.7 5.0 %collective-permute-start.4 = (bf16[512,128]{1,0:T(8,128)(2,1)S(1)}, bf16[512,128]{1,0:T(8,128)(2,1)S(1)}, u32[]{:S(2)}, u32[]{:S(2)}) collective-permute-start(bf16[512,128]{1,0:T(8,128)(2,1)S(1)} %get-tuple-element.32.refs_0_), channel_id=1, source_target_pairs={{0,8},{8,0},{16,24},{24,16},{1,9},{9,1},{17,25},{25,17},{2,10},{10... | collective-permute-start | bytes 393224 | tf_op jit(solution)/shard_map/exchange/ppermute | solution.py:207
  15.5 6.1 %collective-permute-start.11 = (bf16[528,128]{1,0:T(8,128)(2,1)S(1)}, bf16[528,128]{1,0:T(8,128)(2,1)S(1)}, u32[]{:S(2)}, u32[]{:S(2)}) collective-permute-start(bf16[528,128]{1,0:T(8,128)(2,1)S(1)} %collective-permute-done.10.q_ref), channel_id=1, source_target_pairs={{0,2},{1,3},{2,0},{3,1},{4,6},{5,7},{6,4},{7,5},{8,10},{9,11},{10,... | collective-permute-start | bytes 405512 | tf_op jit(solution)/shard_map/exchange/ppermute | solution.py:226
  17.1 5.3 %collective-permute-start.12 = (bf16[512,128]{1,0:T(8,128)(2,1)S(1)}, bf16[512,128]{1,0:T(8,128)(2,1)S(1)}, u32[]{:S(2)}, u32[]{:S(2)}) collective-permute-start(bf16[512,128]{1,0:T(8,128)(2,1)S(1)} %collective-permute-done.5.refs_2_), channel_id=1, source_target_pairs={{0,8},{8,0},{16,24},{24,16},{1,9},{9,1},{17,25},{25,17},{2,10},{10... | collective-permute-start | bytes 393224 | tf_op jit(solution)/shard_map/exchange/ppermute | solution.py:207
  18.3 6.4 %collective-permute-start.9 = (bf16[528,128]{1,0:T(8,128)(2,1)S(1)}, bf16[528,128]{1,0:T(8,128)(2,1)S(1)}, u32[]{:S(2)}, u32[]{:S(2)}) collective-permute-start(bf16[528,128]{1,0:T(8,128)(2,1)S(1)} %get-tuple-element.37.q_ref), channel_id=1, source_target_pairs={{0,2},{1,3},{2,0},{3,1},{4,6},{5,7},{6,4},{7,5},{8,10},{9,11},{10,... | collective-permute-start | bytes 405512 | tf_op jit(solution)/shard_map/exchange/ppermute | solution.py:226
  22.8 5.8 %collective-permute-start.14 = (bf16[544,128]{1,0:T(8,128)(2,1)S(1)}, bf16[544,128]{1,0:T(8,128)(2,1)S(1)}, u32[]{:S(2)}, u32[]{:S(2)}) collective-permute-start(bf16[544,128]{1,0:T(8,128)(2,1)S(1)} %apply.4), channel_id=1, source_target_pairs={{0,2},{1,3},{2,0},{3,1},{4,6},{5,7},{6,4},{7,5},{8,10},{9,11},{10,... | collective-permute-start | bytes 417800 | tf_op jit(solution)/shard_map/return/ppermute | solution.py:282
  25.8 5.7 %collective-permute-start.17 = (bf16[272,128]{1,0:T(8,128)(2,1)S(1)}, bf16[272,128]{1,0:T(8,128)(2,1)S(1)}, u32[]{:S(2)}, u32[]{:S(2)}) collective-permute-start(bf16[272,128]{1,0:T(8,128)(2,1)S(1)} %get-tuple-element.50), channel_id=1, source_target_pairs={{0,2},{1,3},{2,0},{3,1},{4,6},{5,7},{6,4},{7,5},{8,10},{9,11},{10,... | collective-permute-start | bytes 208904 | tf_op jit(solution)/shard_map/return/ppermute | solution.py:280
  26.7 4.7 %collective-permute-start.13 = (bf16[272,128]{1,0:T(8,128)(2,1)S(1)}, bf16[272,128]{1,0:T(8,128)(2,1)S(1)}, u32[]{:S(2)}, u32[]{:S(2)}) collective-permute-start(bf16[272,128]{1,0:T(8,128)(2,1)S(1)} %get-tuple-element.53), channel_id=1, source_target_pairs={{0,1},{1,0},{2,3},{3,2},{4,5},{5,4},{6,7},{7,6},{8,9},{9,8},{10,11... | collective-permute-start | bytes 208904 | tf_op jit(solution)/shard_map/return/ppermute | solution.py:300
  26.8 4.6 %collective-permute-start.18 = (bf16[272,128]{1,0:T(8,128)(2,1)S(1)}, bf16[272,128]{1,0:T(8,128)(2,1)S(1)}, u32[]{:S(2)}, u32[]{:S(2)}) collective-permute-start(bf16[272,128]{1,0:T(8,128)(2,1)S(1)} %get-tuple-element.56), channel_id=1, source_target_pairs={{0,3},{1,2},{2,1},{3,0},{4,7},{5,6},{6,5},{7,4},{8,11},{9,10},{10,... | collective-permute-start | bytes 208904 | tf_op jit(solution)/shard_map/return/ppermute | solution.py:280
  28.7 5.8 %collective-permute-start.15 = (bf16[272,128]{1,0:T(8,128)(2,1)S(1)}, bf16[272,128]{1,0:T(8,128)(2,1)S(1)}, u32[]{:S(2)}, u32[]{:S(2)}) collective-permute-start(bf16[272,128]{1,0:T(8,128)(2,1)S(1)} %get-tuple-element.54), channel_id=1, source_target_pairs={{0,4},{1,5},{2,6},{3,7},{4,0},{5,1},{6,2},{7,3},{8,12},{9,13},{10,... | collective-permute-start | bytes 208904 | tf_op jit(solution)/shard_map/return/ppermute | solution.py:280
  31.4 7.0 %collective-permute-start.16 = (bf16[272,128]{1,0:T(8,128)(2,1)S(1)}, bf16[272,128]{1,0:T(8,128)(2,1)S(1)}, u32[]{:S(2)}, u32[]{:S(2)}) collective-permute-start(bf16[272,128]{1,0:T(8,128)(2,1)S(1)} %get-tuple-element.55), channel_id=1, source_target_pairs={{0,5},{1,4},{2,7},{3,6},{4,1},{5,0},{6,3},{7,2},{8,13},{9,12},{10,... | collective-permute-start | bytes 208904 | tf_op jit(solution)/shard_map/return/ppermute | solution.py:280

commit v13 on v12

--- a/solution.py
+++ b/solution.py
@@ -40,15 +40,15 @@
     return jnp.concatenate([jnp.full((half, size), p[0].astype(F32), F32) for p in (p0, p1)], axis=0).astype(BF16)
 
 
-def merge_kernel(p0, p1, own, q1, k1, v1, q_out, k_out, v_out):
+def merge_kernel(p0, p1, own, q1, k1, v1, q_out, kv_out):
     tok = q1.shape[0]
     rows = PER * CORES * tok
     pos = starts(p0, p1, q_out.shape[1])
     place(own.at[0:tok, :], q1, q_out, 0)
     q_out[rows:, :] = pos
-    place(own.at[tok : 2 * tok, :], k1, k_out, 0)
-    k_out[rows:, :] = pos
-    place(own.at[2 * tok : 3 * tok, :], v1, v_out, 0, turned=True)
+    place(own.at[tok : 2 * tok, :], k1, kv_out, 0)
+    kv_out[rows : rows + PAD, :] = pos
+    place(own.at[2 * tok : 3 * tok, :], v1, kv_out, rows + PAD, turned=True)
 
 
 def score_kernel(same, q_ref, *refs):
@@ -61,7 +61,7 @@
     at_or_before = lax.broadcasted_iota(jnp.int32, (tok, tok), 0) <= lax.broadcasted_iota(jnp.int32, (tok, tok), 1)
 
     def block_of(ref):
-        first = ref[PER * both :, :].astype(F32)
+        first = ref[PER * both : PER * both + PAD, :].astype(F32)
         return [first[b * half : b * half + 1, :] for b in range(CORES)]
 
     q_block = jnp.concatenate(block_of(q_ref), axis=1)
@@ -85,7 +85,7 @@
         top_ref[h * 8 : (h + 1) * 8, :] = jnp.broadcast_to(top, (8, both))
 
 
-def apply_kernel(wide, p_ref, top_ref, *refs):
+def apply_kernel(wide, rows, p_ref, top_ref, *refs):
     nv = len(refs) - (1 if wide else CORES)
     v_refs, out_refs = refs[:nv], refs[nv:]
     size = v_refs[0].shape[1]
@@ -101,7 +101,11 @@
 
     stats = [[] for _ in range(CORES)]
     for h in range(PER):
-        vals = [ref[h * both + b * tok : h * both + (b + 1) * tok, :] for ref in v_refs for b in range(CORES)]
+        vals = []
+        for ref, row in zip(v_refs, rows):
+            for b in range(CORES):
+                at = row + h * both + b * tok
+                vals.append(ref[at : at + tok, :])
         vt = jnp.concatenate(vals, axis=1)
         vt = jnp.concatenate([vt, jnp.ones((PAD, vt.shape[1]), BF16)], axis=0)
         o = jnp.dot(vt, p_ref[h], preferred_element_type=F32)
@@ -183,15 +187,18 @@
         own = jnp.concatenate([queries, keys, values], axis=0)
     with jax.named_scope("merge"):
         smem = [pl.BlockSpec(memory_space=pltpu.SMEM)]
-        piece = jax.ShapeDtypeStruct((PER * both + PAD, size), BF16)
-        q_piece, k_piece, v_piece = pl.pallas_call(
+        q_piece, kv_piece = pl.pallas_call(
             merge_kernel,
-            out_shape=(piece, piece, jax.ShapeDtypeStruct((PER * both, size), BF16)),
+            out_shape=(
+                jax.ShapeDtypeStruct((PER * both + PAD, size), BF16),
+                jax.ShapeDtypeStruct((2 * PER * both + PAD, size), BF16),
+            ),
             in_specs=smem * 2 + vmem(4),
-            out_specs=tuple(vmem(3)),
+            out_specs=tuple(vmem(2)),
             compiler_params=params,
             name="merge",
         )(block_pos, other[3], own, *other[:3])
+    half = PER * both + PAD
     block = PER * size + PAD
 
     def low(r):
@@ -207,24 +214,27 @@
         return lax.ppermute(a, "outer", [(o, o ^ r) for o in range(n_out)])
 
     with jax.named_scope("exchange"):
-        k_by, v_by = {0: k_piece}, {0: v_piece}
-        for r in range(1, n_out):
-            k_by[r] = over(k_by[r - high(r)], high(r))
-        for r in sorted(range(1, n_out), key=lambda r: r.bit_count()):
-            v_by[r] = over(v_by[r - low(r)], low(r))
-        ks, vs = [k_by[r] for r in range(n_out)], [v_by[r] for r in range(n_out)]
-        passed = v_by[n_out // 2] if n_out > 1 else v_piece
+        whole = {r: over(kv_piece, r) if r else kv_piece for r in range(n_out) if single(r)}
         q_by = {0: q_piece}
         bit = chips // 2
         while bit:
             for r in sorted(q_by):
-                piece = q_by[r]
-                if r:
-                    piece = after(piece, passed)
-                elif bit == 1:
-                    piece = after(piece, k_by[n_out - 1])
+                piece = after(q_by[r], list(whole.values())[1:]) if r else q_piece
                 q_by[r | bit] = lax.ppermute(piece, "inner", along_inner(bit, 0))
             bit //= 2
+        k_by = {r: a[:half, :] for r, a in whole.items() if r}
+        v_by = {r: a[half:, :] for r, a in whole.items() if r}
+        if chips > 1:
+            k_by = {r: after(a, q_by[1]) for r, a in k_by.items()}
+        for r in range(1, n_out):
+            if not single(r):
+                k_by[r] = over(k_by[r - high(r)], high(r))
+        for r in sorted(range(1, n_out), key=lambda r: r.bit_count()):
+            if not single(r):
+                v_by[r] = over(v_by[r - low(r)], low(r))
+        ks = [whole[r] if r in whole else k_by[r] for r in range(n_out)]
+        vs = [whole[r] if r in whole else v_by[r] for r in range(n_out)]
+        rows = tuple(half if r in whole else 0 for r in range(n_out))
 
     def shapes(wide):
         rows = CORES * block if wide else block
@@ -245,13 +255,13 @@
                 compiler_params=params,
                 cost_estimate=pl.CostEstimate(flops=work, bytes_accessed=2**20, transcendentals=work // (2 * size)),
                 name="score",
-            )(after(q_by[r], done), *ks)
+            )(q_by[r] if done is None else after(q_by[r], done), *ks)
 
     def apply(r, wide, done):
         with jax.named_scope("apply"):
             weights, tops = weights_by[r]
             return pl.pallas_call(
-                functools.partial(apply_kernel, wide),
+                functools.partial(apply_kernel, wide, rows),
                 out_shape=shapes(wide),
                 in_specs=vmem(2 + n_out),
                 out_specs=tuple(vmem(len(shapes(wide)))),
@@ -282,8 +292,8 @@
                 arrived[r - low(r)].append(lax.ppermute(parts[0], "inner", along_inner(low(r), 0)))
 
     weights_by = {}
-    done = [v_by[r] for r in range(1, n_out) if single(r)]
-    for r in sorted(range(chips), key=lambda r: (r == 1, r)):
+    done = None
+    for r in range(chips):
         weights_by[r] = score(r, done)
         done = weights_by[r][1]
     done = None

time: 39.4 us -> 39.6 us (level)
  starting transfers between devices: 21.3 us -> 17 us
  waiting for transfers between devices: 10.2 us -> 14.5 us
    ppermute x3, waiting for transfers between devices: 0.27 us -> 5.66 us  [shards(): q_by[r | bit] = lax.ppermute(piece, 'inner', along_inner(bit, 0))]
    ppermute x6 -> x4, starting transfers between devices: 7.96 us -> 5.63 us  [over(): return lax.ppermute(a, 'outer', [(o, o ^ r) for o in range(n_out)])]
    ppermute x3, starting transfers between devices: 5.74 us -> 4.41 us  [shards(): q_by[r | bit] = lax.ppermute(piece, 'inner', along_inner(bit, 0))]
    ppermute x6 -> x4, waiting for transfers between devices: 2.65 us -> 1.69 us  [over(): return lax.ppermute(a, 'outer', [(o, o ^ r) for o in range(n_out)])]
  transfers between devices with their start and end apart: 19 -> 17, of which waited for: 7 -> 8; matrix products, arithmetic and copies ran while one was open for 3% -> 3% of each run, Pallas kernels for 11% -> 10%
where the time goes in v13:
time: 39.6 us; the launch traced here: 39.5 us
  starting transfers between devices  17 us (43%)
  waiting for transfers between devices  14.5 us (37%)
  Pallas kernels  6.06 us (15%)
  other arithmetic  1.06 us (3%)
  between operations  0.81 us (2%)
    ppermute x4, waiting for transfers between devices, send(): lax.ppermute(parts[x], 'inner', along_inner(r, x))  6.71 us
    ppermute x3, waiting for transfers between devices, shards(): q_by[r | bit] = lax.ppermute(piece, 'inner', along_inner(bit, 0))  5.66 us
    ppermute x4, starting transfers between devices, over(): return lax.ppermute(a, 'outer', [(o, o ^ r) for o in range(n_out)])  5.63 us
    ppermute x4, starting transfers between devices, send(): lax.ppermute(parts[x], 'inner', along_inner(r, x))  4.53 us
    ppermute x3, starting transfers between devices, shards(): q_by[r | bit] = lax.ppermute(piece, 'inner', along_inner(bit, 0))  4.41 us
    pallas_call x4, Pallas kernels, score(): pl.pallas_call(functools.partial(score_kernel, r == 0), out_shape=(jax.Sh...  3.02 us
    ppermute x4, waiting for transfers between devices, over(): return lax.ppermute(a, 'outer', [(o, o ^ r) for o in range(n_out)])  1.69 us
    ppermute x1, starting transfers between devices, send(): lax.ppermute(parts[0], 'inner', along_inner(low(r), 0))  1.36 us
  transfers between devices with their start and end apart: 17, of which 8 were waited for; matrix products, arithmetic and copies ran while one was open for 3% of the time, Pallas kernels for 10%

profile of v13, /device:TPU:0, one launch (start us, length us, event | category | flops | bytes accessed | tf_op | source)
XLA Modules:
  0.0 39.5 jit_solution(343880394495143184)
XLA Ops:
  0.0 0.5 %collective-permute-start.1 = (bf16[128,512]{1,0:T(8,128)(2,1)}, bf16[128,512]{1,0:T(8,128)(2,1)S(1)}, u32[]{:S(2)}, u32[]{:S(2)}) collective-permute-start(bf16[128,512]{1,0:T(8,128)(2,1)} %param.4), channel_id=1, source_target_pairs={{0,1},{1,0},{2,3},{3,2},{4,5},{5,4},{6,7},{7,6},{8,9},{9,8},{10,11... | collective-permute-start | bytes 393224 | tf_op jit(solution)/shard_map/swap/ppermute | solution.py:186
  0.5 0.1 collective-permute-start.2
  0.5 0.5 %collective-permute-start.3 = (bf16[128,512]{1,0:T(8,128)(2,1)}, bf16[128,512]{1,0:T(8,128)(2,1)S(1)}, u32[]{:S(2)}, u32[]{:S(2)}) collective-permute-start(bf16[128,512]{1,0:T(8,128)(2,1)} %param.6), channel_id=1, source_target_pairs={{0,1},{1,0},{2,3},{3,2},{4,5},{5,4},{6,7},{7,6},{8,9},{9,8},{10,11... | collective-permute-start | bytes 393224 | tf_op jit(solution)/shard_map/swap/ppermute | solution.py:186
  1.0 0.1 collective-permute-start
  1.7 1.1 %pad_maximum_fusion.own = bf16[384,512]{1,0:T(8,128)(2,1)S(1)} fusion(bf16[128,512]{1,0:T(8,128)(2,1)} %param.6, bf16[128,512]{1,0:T(8,128)(2,1)} %param.5, bf16[128,512]{1,0:T(8,128)(2,1)} %param.4), kind=kLoop, calls=%fused_computation | loop fusion | flops 1179648 | bytes 786432 | tf_op jit(solution)/shard_map/swap/concatenate | solution.py:187
  2.7 0.0 collective-permute-done.p1
  2.7 0.0 collective-permute-done.1.q1
  2.8 0.0 collective-permute-done.2.k1
  2.8 0.0 collective-permute-done.3.v1
  2.8 0.8 %merge.1 = (bf16[528,128]{1,0:T(8,128)(2,1)S(1)}, bf16[1040,128]{1,0:T(8,128)(2,1)S(1)}) custom-call(s32[1]{0:T(128)S(6)} %copy.5.p0, s32[1]{0:T(128)} %collective-permute-done.p1, bf16[384,512]{1,0:T(8,128)(2,1)S(1)} %pad_maximum_fusion.own, bf16[128,512]{1,0:T(8,128)(2,1)S(1)} %collective-permute-done.1.q1, ...), custom_call_target="tpu_custom_call" | custom-call | tf_op jit(solution)/shard_map/merge/merge/pallas_call | solution.py:190
  3.6 3.0 %collective-permute-start.4 = (bf16[1040,128]{1,0:T(8,128)(2,1)S(1)}, bf16[1040,128]{1,0:T(8,128)(2,1)S(1)}, u32[]{:S(2)}, u32[]{:S(2)}) collective-permute-start(bf16[1040,128]{1,0:T(8,128)(2,1)S(1)} %get-tuple-element.30.refs_0_), channel_id=1, source_target_pairs={{0,8},{8,0},{16,24},{24,16},{1,9},{9,1},{17,25},{25,17},{2,10},{10... | collective-permute-start | bytes 798728 | tf_op jit(solution)/shard_map/exchange/ppermute | solution.py:214
  6.6 1.5 %collective-permute-start.5 = (bf16[1040,128]{1,0:T(8,128)(2,1)S(1)}, bf16[1040,128]{1,0:T(8,128)(2,1)S(1)}, u32[]{:S(2)}, u32[]{:S(2)}) collective-permute-start(bf16[1040,128]{1,0:T(8,128)(2,1)S(1)} %get-tuple-element.30.refs_0_), channel_id=1, source_target_pairs={{0,16},{8,24},{16,0},{24,8},{1,17},{9,25},{17,1},{25,9},{2,18},{10... | collective-permute-start | bytes 798728 | tf_op jit(solution)/shard_map/exchange/ppermute | solution.py:214
  8.1 1.6 %collective-permute-start.6 = (bf16[528,128]{1,0:T(8,128)(2,1)S(1)}, bf16[528,128]{1,0:T(8,128)(2,1)S(1)}, u32[]{:S(2)}, u32[]{:S(2)}) collective-permute-start(bf16[528,128]{1,0:T(8,128)(2,1)S(1)} %get-tuple-element.29.q_ref), channel_id=1, source_target_pairs={{0,2},{1,3},{2,0},{3,1},{4,6},{5,7},{6,4},{7,5},{8,10},{9,11},{10,... | collective-permute-start | bytes 405512 | tf_op jit(solution)/shard_map/exchange/ppermute | solution.py:223
  9.7 2.6 %collective-permute-start.8 = (bf16[528,128]{1,0:T(8,128)(2,1)S(1)}, bf16[528,128]{1,0:T(8,128)(2,1)S(1)}, u32[]{:S(2)}, u32[]{:S(2)}) collective-permute-start(bf16[528,128]{1,0:T(8,128)(2,1)S(1)} %get-tuple-element.29.q_ref), channel_id=1, source_target_pairs={{0,4},{1,5},{2,6},{3,7},{4,0},{5,1},{6,2},{7,3},{8,12},{9,13},{10,... | collective-permute-start | bytes 405512 | tf_op jit(solution)/shard_map/exchange/ppermute | solution.py:223
  12.3 0.9 %collective-permute-done.4.refs_1_ = bf16[1040,128]{1,0:T(8,128)(2,1)S(1)} collective-permute-done((bf16[1040,128]{1,0:T(8,128)(2,1)S(1)}, bf16[1040,128]{1,0:T(8,128)(2,1)S(1)}, u32[]{:S(2)}, u32[]{:S(2)}) %collective-permute-start.4) | collective-permute-done | bytes 266272 | tf_op jit(solution)/shard_map/exchange/ppermute | solution.py:214
  13.1 1.8 %collective-permute-done.6.q_ref = bf16[528,128]{1,0:T(8,128)(2,1)S(1)} collective-permute-done((bf16[528,128]{1,0:T(8,128)(2,1)S(1)}, bf16[528,128]{1,0:T(8,128)(2,1)S(1)}, u32[]{:S(2)}, u32[]{:S(2)}) %collective-permute-start.6) | collective-permute-done | bytes 135200 | tf_op jit(solution)/shard_map/exchange/ppermute | solution.py:223
  14.9 0.5 %collective-permute-start.7 = (bf16[528,128]{1,0:T(8,128)(2,1)S(1)}, bf16[528,128]{1,0:T(8,128)(2,1)S(1)}, u32[]{:S(2)}, u32[]{:S(2)}) collective-permute-start(bf16[528,128]{1,0:T(8,128)(2,1)S(1)} %slice.8), channel_id=1, source_target_pairs={{0,16},{8,24},{16,0},{24,8},{1,17},{9,25},{17,1},{25,9},{2,18},{10... | collective-permute-start | bytes 405512 | tf_op jit(solution)/shard_map/exchange/ppermute | solution.py:214
  15.4 2.8 %collective-permute-done.8.q_ref = bf16[528,128]{1,0:T(8,128)(2,1)S(1)} collective-permute-done((bf16[528,128]{1,0:T(8,128)(2,1)S(1)}, bf16[528,128]{1,0:T(8,128)(2,1)S(1)}, u32[]{:S(2)}, u32[]{:S(2)}) %collective-permute-start.8) | collective-permute-done | bytes 135200 | tf_op jit(solution)/shard_map/exchange/ppermute | solution.py:223
  18.3 0.0 collective-permute-done.5.refs_2_
  18.3 0.2 collective-permute-start.9
  18.5 0.6 %collective-permute-start.10 = (bf16[512,128]{1,0:T(8,128)(2,1)S(1)}, bf16[512,128]{1,0:T(8,128)(2,1)S(1)}, u32[]{:S(2)}, u32[]{:S(2)}) collective-permute-start(bf16[512,128]{1,0:T(8,128)(2,1)S(1)} %slice.9), channel_id=1, source_target_pairs={{0,8},{8,0},{16,24},{24,16},{1,9},{9,1},{17,25},{25,17},{2,10},{10... | collective-permute-start | bytes 393224 | tf_op jit(solution)/shard_map/exchange/ppermute | solution.py:214
  19.1 0.8 %collective-permute-done.7.refs_3_ = bf16[528,128]{1,0:T(8,128)(2,1)S(1)} collective-permute-done((bf16[528,128]{1,0:T(8,128)(2,1)S(1)}, bf16[528,128]{1,0:T(8,128)(2,1)S(1)}, u32[]{:S(2)}, u32[]{:S(2)}) %collective-permute-start.7) | collective-permute-done | bytes 135200 | tf_op jit(solution)/shard_map/exchange/ppermute | solution.py:214
  19.9 0.8 %score.4 = (bf16[2,1024,256]{2,1,0:T(8,128)(2,1)S(1)}, f32[16,256]{1,0:T(8,128)S(1)}) custom-call(bf16[528,128]{1,0:T(8,128)(2,1)S(1)} %get-tuple-element.29.q_ref, bf16[1040,128]{1,0:T(8,128)(2,1)S(1)} %get-tuple-element.30.refs_0_, bf16[1040,128]{1,0:T(8,128)(2,1)S(1)} %collective-permute-done.4.refs_1_, ...), custom_call_target="tpu_custom_call" | custom-call | flops 134217728 | bytes 1048576 | tf_op jit(solution)/shard_map/score/score/pallas_call | solution.py:247
  20.7 0.8 %score.5 = (bf16[2,1024,256]{2,1,0:T(8,128)(2,1)S(1)}, f32[16,256]{1,0:T(8,128)S(1)}) custom-call(bf16[528,128]{1,0:T(8,128)(2,1)S(1)} %collective-permute-done.6.q_ref, bf16[1040,128]{1,0:T(8,128)(2,1)S(1)} %get-tuple-element.30.refs_0_, bf16[1040,128]{1,0:T(8,128)(2,1)S(1)} %collective-permute-done.4.refs_1_, ...), custom_call_target="tpu_custom_call" | custom-call | flops 134217728 | bytes 1048576 | tf_op jit(solution)/shard_map/score/score/pallas_call | solution.py:247
  21.5 0.8 %score.6 = (bf16[2,1024,256]{2,1,0:T(8,128)(2,1)S(1)}, f32[16,256]{1,0:T(8,128)S(1)}) custom-call(bf16[528,128]{1,0:T(8,128)(2,1)S(1)} %collective-permute-done.8.q_ref, bf16[1040,128]{1,0:T(8,128)(2,1)S(1)} %get-tuple-element.30.refs_0_, bf16[1040,128]{1,0:T(8,128)(2,1)S(1)} %collective-permute-done.4.refs_1_, ...), custom_call_target="tpu_custom_call" | custom-call | flops 134217728 | bytes 1048576 | tf_op jit(solution)/shard_map/score/score/pallas_call | solution.py:247
  22.2 1.0 %collective-permute-done.9.q_ref = bf16[528,128]{1,0:T(8,128)(2,1)S(1)} collective-permute-done((bf16[528,128]{1,0:T(8,128)(2,1)S(1)}, bf16[528,128]{1,0:T(8,128)(2,1)S(1)}, u32[]{:S(2)}, u32[]{:S(2)}) %collective-permute-start.9) | collective-permute-done | bytes 135200 | tf_op jit(solution)/shard_map/exchange/ppermute | solution.py:223
  23.3 0.7 %score.7 = (bf16[2,1024,256]{2,1,0:T(8,128)(2,1)S(1)}, f32[16,256]{1,0:T(8,128)S(1)}) custom-call(bf16[528,128]{1,0:T(8,128)(2,1)S(1)} %collective-permute-done.9.q_ref, bf16[1040,128]{1,0:T(8,128)(2,1)S(1)} %get-tuple-element.30.refs_0_, bf16[1040,128]{1,0:T(8,128)(2,1)S(1)} %collective-permute-done.4.refs_1_, ...), custom_call_target="tpu_custom_call" | custom-call | flops 134217728 | bytes 1048576 | tf_op jit(solution)/shard_map/score/score/pallas_call | solution.py:247
  24.0 0.0 collective-permute-done.10.refs_3_
  24.0 0.3 apply.4
  24.4 1.4 %collective-permute-start.12 = (bf16[544,128]{1,0:T(8,128)(2,1)S(1)}, bf16[544,128]{1,0:T(8,128)(2,1)S(1)}, u32[]{:S(2)}, u32[]{:S(2)}) collective-permute-start(bf16[544,128]{1,0:T(8,128)(2,1)S(1)} %apply.4), channel_id=1, source_target_pairs={{0,2},{1,3},{2,0},{3,1},{4,6},{5,7},{6,4},{7,5},{8,10},{9,11},{10,... | collective-permute-start | bytes 417800 | tf_op jit(solution)/shard_map/return/ppermute | solution.py:292
  25.8 0.3 apply.5.refs_0_
  26.1 0.3 apply.6
  26.4 0.8 %collective-permute-start.15 = (bf16[272,128]{1,0:T(8,128)(2,1)S(1)}, bf16[272,128]{1,0:T(8,128)(2,1)S(1)}, u32[]{:S(2)}, u32[]{:S(2)}) collective-permute-start(bf16[272,128]{1,0:T(8,128)(2,1)S(1)} %get-tuple-element.46), channel_id=1, source_target_pairs={{0,2},{1,3},{2,0},{3,1},{4,6},{5,7},{6,4},{7,5},{8,10},{9,11},{10,... | collective-permute-start | bytes 208904 | tf_op jit(solution)/shard_map/return/ppermute | solution.py:290
  27.2 0.3 apply.7
  27.6 0.1 collective-permute-start.11
  27.7 1.4 %collective-permute-start.16 = (bf16[272,128]{1,0:T(8,128)(2,1)S(1)}, bf16[272,128]{1,0:T(8,128)(2,1)S(1)}, u32[]{:S(2)}, u32[]{:S(2)}) collective-permute-start(bf16[272,128]{1,0:T(8,128)(2,1)S(1)} %get-tuple-element.52), channel_id=1, source_target_pairs={{0,3},{1,2},{2,1},{3,0},{4,7},{5,6},{6,5},{7,4},{8,11},{9,10},{10,... | collective-permute-start | bytes 208904 | tf_op jit(solution)/shard_map/return/ppermute | solution.py:290
  29.1 0.4 %collective-permute-done.12.refs_1_ = bf16[544,128]{1,0:T(8,128)(2,1)S(1)} collective-permute-done((bf16[544,128]{1,0:T(8,128)(2,1)S(1)}, bf16[544,128]{1,0:T(8,128)(2,1)S(1)}, u32[]{:S(2)}, u32[]{:S(2)}) %collective-permute-start.12) | collective-permute-done | bytes 139296 | tf_op jit(solution)/shard_map/return/ppermute | solution.py:292
  29.5 0.1 add.1
  29.6 2.3 %collective-permute-start.13 = (bf16[272,128]{1,0:T(8,128)(2,1)S(1)}, bf16[272,128]{1,0:T(8,128)(2,1)S(1)}, u32[]{:S(2)}, u32[]{:S(2)}) collective-permute-start(bf16[272,128]{1,0:T(8,128)(2,1)S(1)} %get-tuple-element.50), channel_id=1, source_target_pairs={{0,4},{1,5},{2,6},{3,7},{4,0},{5,1},{6,2},{7,3},{8,12},{9,13},{10,... | collective-permute-start | bytes 208904 | tf_op jit(solution)/shard_map/return/ppermute | solution.py:290
  31.9 0.0 collective-permute-start.14
  31.9 0.0 collective-permute-done.11.refs_1_
  31.9 0.0 collective-permute-done.15.refs_4_
  31.9 0.0 collective-permute-done.16.refs_5_
  31.9 5.8 %collective-permute-done.13.refs_2_ = bf16[272,128]{1,0:T(8,128)(2,1)S(1)} collective-permute-done((bf16[272,128]{1,0:T(8,128)(2,1)S(1)}, bf16[272,128]{1,0:T(8,128)(2,1)S(1)}, u32[]{:S(2)}, u32[]{:S(2)}) %collective-permute-start.13) | collective-permute-done | bytes 69664 | tf_op jit(solution)/shard_map/return/ppermute | solution.py:290
  37.8 0.9 %collective-permute-done.14.refs_3_ = bf16[272,128]{1,0:T(8,128)(2,1)S(1)} collective-permute-done((bf16[272,128]{1,0:T(8,128)(2,1)S(1)}, bf16[272,128]{1,0:T(8,128)(2,1)S(1)}, u32[]{:S(2)}, u32[]{:S(2)}) %collective-permute-start.14) | collective-permute-done | bytes 69664 | tf_op jit(solution)/shard_map/return/ppermute | solution.py:290
  38.6 0.8 %combine.1 = bf16[128,512]{1,0:T(8,128)(2,1)} custom-call(bf16[272,128]{1,0:T(8,128)(2,1)S(1)} %get-tuple-element.48.refs_0_, bf16[272,128]{1,0:T(8,128)(2,1)S(1)} %collective-permute-done.11.refs_1_, bf16[272,128]{1,0:T(8,128)(2,1)S(1)} %collective-permute-done.13.refs_2_, bf16[272,128]{1,0:T(8,128)(2,1)S(1)} %collective-permute-done.14.refs_3_, ...), custom_call_target="tpu_custom_call" | custom-call | tf_op jit(solution)/shard_map/combine/combine/pallas_call | solution.py:312
  (2 shorter events, 0.0 us)
Async XLA Ops:
  0.0 2.7 %collective-permute-start.1 = (bf16[128,512]{1,0:T(8,128)(2,1)}, bf16[128,512]{1,0:T(8,128)(2,1)S(1)}, u32[]{:S(2)}, u32[]{:S(2)}) collective-permute-start(bf16[128,512]{1,0:T(8,128)(2,1)} %param.4), channel_id=1, source_target_pairs={{0,1},{1,0},{2,3},{3,2},{4,5},{5,4},{6,7},{7,6},{8,9},{9,8},{10,11... | collective-permute-start | bytes 393224 | tf_op jit(solution)/shard_map/swap/ppermute | solution.py:186
  0.5 2.3 %collective-permute-start.2 = (bf16[128,512]{1,0:T(8,128)(2,1)}, bf16[128,512]{1,0:T(8,128)(2,1)S(1)}, u32[]{:S(2)}, u32[]{:S(2)}) collective-permute-start(bf16[128,512]{1,0:T(8,128)(2,1)} %param.5), channel_id=1, source_target_pairs={{0,1},{1,0},{2,3},{3,2},{4,5},{5,4},{6,7},{7,6},{8,9},{9,8},{10,11... | collective-permute-start | bytes 393224 | tf_op jit(solution)/shard_map/swap/ppermute | solution.py:186
  0.5 2.3 %collective-permute-start.3 = (bf16[128,512]{1,0:T(8,128)(2,1)}, bf16[128,512]{1,0:T(8,128)(2,1)S(1)}, u32[]{:S(2)}, u32[]{:S(2)}) collective-permute-start(bf16[128,512]{1,0:T(8,128)(2,1)} %param.6), channel_id=1, source_target_pairs={{0,1},{1,0},{2,3},{3,2},{4,5},{5,4},{6,7},{7,6},{8,9},{9,8},{10,11... | collective-permute-start | bytes 393224 | tf_op jit(solution)/shard_map/swap/ppermute | solution.py:186
  1.0 1.8 %collective-permute-start = (s32[1]{0:T(128)}, s32[1]{0:T(128)}, u32[]{:S(2)}, u32[]{:S(2)}) collective-permute-start(s32[1]{0:T(128)} %param.7), channel_id=1, source_target_pairs={{0,1},{1,0},{2,3},{3,2},{4,5},{5,4},{6,7},{7,6},{8,9},{9,8},{10,11... | collective-permute-start | bytes 20 | tf_op jit(solution)/shard_map/swap/ppermute | solution.py:186
  3.6 9.6 %collective-permute-start.4 = (bf16[1040,128]{1,0:T(8,128)(2,1)S(1)}, bf16[1040,128]{1,0:T(8,128)(2,1)S(1)}, u32[]{:S(2)}, u32[]{:S(2)}) collective-permute-start(bf16[1040,128]{1,0:T(8,128)(2,1)S(1)} %get-tuple-element.30.refs_0_), channel_id=1, source_target_pairs={{0,8},{8,0},{16,24},{24,16},{1,9},{9,1},{17,25},{25,17},{2,10},{10... | collective-permute-start | bytes 798728 | tf_op jit(solution)/shard_map/exchange/ppermute | solution.py:214
  6.6 11.7 %collective-permute-start.5 = (bf16[1040,128]{1,0:T(8,128)(2,1)S(1)}, bf16[1040,128]{1,0:T(8,128)(2,1)S(1)}, u32[]{:S(2)}, u32[]{:S(2)}) collective-permute-start(bf16[1040,128]{1,0:T(8,128)(2,1)S(1)} %get-tuple-element.30.refs_0_), channel_id=1, source_target_pairs={{0,16},{8,24},{16,0},{24,8},{1,17},{9,25},{17,1},{25,9},{2,18},{10... | collective-permute-start | bytes 798728 | tf_op jit(solution)/shard_map/exchange/ppermute | solution.py:214
  8.1 6.8 %collective-permute-start.6 = (bf16[528,128]{1,0:T(8,128)(2,1)S(1)}, bf16[528,128]{1,0:T(8,128)(2,1)S(1)}, u32[]{:S(2)}, u32[]{:S(2)}) collective-permute-start(bf16[528,128]{1,0:T(8,128)(2,1)S(1)} %get-tuple-element.29.q_ref), channel_id=1, source_target_pairs={{0,2},{1,3},{2,0},{3,1},{4,6},{5,7},{6,4},{7,5},{8,10},{9,11},{10,... | collective-permute-start | bytes 405512 | tf_op jit(solution)/shard_map/exchange/ppermute | solution.py:223
  9.7 8.6 %collective-permute-start.8 = (bf16[528,128]{1,0:T(8,128)(2,1)S(1)}, bf16[528,128]{1,0:T(8,128)(2,1)S(1)}, u32[]{:S(2)}, u32[]{:S(2)}) collective-permute-start(bf16[528,128]{1,0:T(8,128)(2,1)S(1)} %get-tuple-element.29.q_ref), channel_id=1, source_target_pairs={{0,4},{1,5},{2,6},{3,7},{4,0},{5,1},{6,2},{7,3},{8,12},{9,13},{10,... | collective-permute-start | bytes 405512 | tf_op jit(solution)/shard_map/exchange/ppermute | solution.py:223
  14.9 5.0 %collective-permute-start.7 = (bf16[528,128]{1,0:T(8,128)(2,1)S(1)}, bf16[528,128]{1,0:T(8,128)(2,1)S(1)}, u32[]{:S(2)}, u32[]{:S(2)}) collective-permute-start(bf16[528,128]{1,0:T(8,128)(2,1)S(1)} %slice.8), channel_id=1, source_target_pairs={{0,16},{8,24},{16,0},{24,8},{1,17},{9,25},{17,1},{25,9},{2,18},{10... | collective-permute-start | bytes 405512 | tf_op jit(solution)/shard_map/exchange/ppermute | solution.py:214
  18.3 5.0 %collective-permute-start.9 = (bf16[528,128]{1,0:T(8,128)(2,1)S(1)}, bf16[528,128]{1,0:T(8,128)(2,1)S(1)}, u32[]{:S(2)}, u32[]{:S(2)}) collective-permute-start(bf16[528,128]{1,0:T(8,128)(2,1)S(1)} %collective-permute-done.8.q_ref), channel_id=1, source_target_pairs={{0,2},{1,3},{2,0},{3,1},{4,6},{5,7},{6,4},{7,5},{8,10},{9,11},{10,... | collective-permute-start | bytes 405512 | tf_op jit(solution)/shard_map/exchange/ppermute | solution.py:223
  18.5 5.5 %collective-permute-start.10 = (bf16[512,128]{1,0:T(8,128)(2,1)S(1)}, bf16[512,128]{1,0:T(8,128)(2,1)S(1)}, u32[]{:S(2)}, u32[]{:S(2)}) collective-permute-start(bf16[512,128]{1,0:T(8,128)(2,1)S(1)} %slice.9), channel_id=1, source_target_pairs={{0,8},{8,0},{16,24},{24,16},{1,9},{9,1},{17,25},{25,17},{2,10},{10... | collective-permute-start | bytes 393224 | tf_op jit(solution)/shard_map/exchange/ppermute | solution.py:214
  24.4 5.1 %collective-permute-start.12 = (bf16[544,128]{1,0:T(8,128)(2,1)S(1)}, bf16[544,128]{1,0:T(8,128)(2,1)S(1)}, u32[]{:S(2)}, u32[]{:S(2)}) collective-permute-start(bf16[544,128]{1,0:T(8,128)(2,1)S(1)} %apply.4), channel_id=1, source_target_pairs={{0,2},{1,3},{2,0},{3,1},{4,6},{5,7},{6,4},{7,5},{8,10},{9,11},{10,... | collective-permute-start | bytes 417800 | tf_op jit(solution)/shard_map/return/ppermute | solution.py:292
  26.4 5.5 %collective-permute-start.15 = (bf16[272,128]{1,0:T(8,128)(2,1)S(1)}, bf16[272,128]{1,0:T(8,128)(2,1)S(1)}, u32[]{:S(2)}, u32[]{:S(2)}) collective-permute-start(bf16[272,128]{1,0:T(8,128)(2,1)S(1)} %get-tuple-element.46), channel_id=1, source_target_pairs={{0,2},{1,3},{2,0},{3,1},{4,6},{5,7},{6,4},{7,5},{8,10},{9,11},{10,... | collective-permute-start | bytes 208904 | tf_op jit(solution)/shard_map/return/ppermute | solution.py:290
  27.6 4.3 %collective-permute-start.11 = (bf16[272,128]{1,0:T(8,128)(2,1)S(1)}, bf16[272,128]{1,0:T(8,128)(2,1)S(1)}, u32[]{:S(2)}, u32[]{:S(2)}) collective-permute-start(bf16[272,128]{1,0:T(8,128)(2,1)S(1)} %get-tuple-element.49), channel_id=1, source_target_pairs={{0,1},{1,0},{2,3},{3,2},{4,5},{5,4},{6,7},{7,6},{8,9},{9,8},{10,11... | collective-permute-start | bytes 208904 | tf_op jit(solution)/shard_map/return/ppermute | solution.py:310
  27.7 4.3 %collective-permute-start.16 = (bf16[272,128]{1,0:T(8,128)(2,1)S(1)}, bf16[272,128]{1,0:T(8,128)(2,1)S(1)}, u32[]{:S(2)}, u32[]{:S(2)}) collective-permute-start(bf16[272,128]{1,0:T(8,128)(2,1)S(1)} %get-tuple-element.52), channel_id=1, source_target_pairs={{0,3},{1,2},{2,1},{3,0},{4,7},{5,6},{6,5},{7,4},{8,11},{9,10},{10,... | collective-permute-start | bytes 208904 | tf_op jit(solution)/shard_map/return/ppermute | solution.py:290
  29.6 8.2 %collective-permute-start.13 = (bf16[272,128]{1,0:T(8,128)(2,1)S(1)}, bf16[272,128]{1,0:T(8,128)(2,1)S(1)}, u32[]{:S(2)}, u32[]{:S(2)}) collective-permute-start(bf16[272,128]{1,0:T(8,128)(2,1)S(1)} %get-tuple-element.50), channel_id=1, source_target_pairs={{0,4},{1,5},{2,6},{3,7},{4,0},{5,1},{6,2},{7,3},{8,12},{9,13},{10,... | collective-permute-start | bytes 208904 | tf_op jit(solution)/shard_map/return/ppermute | solution.py:290
  31.9 6.7 %collective-permute-start.14 = (bf16[272,128]{1,0:T(8,128)(2,1)S(1)}, bf16[272,128]{1,0:T(8,128)(2,1)S(1)}, u32[]{:S(2)}, u32[]{:S(2)}) collective-permute-start(bf16[272,128]{1,0:T(8,128)(2,1)S(1)} %get-tuple-element.51), channel_id=1, source_target_pairs={{0,5},{1,4},{2,7},{3,6},{4,1},{5,0},{6,3},{7,2},{8,13},{9,12},{10,... | collective-permute-start | bytes 208904 | tf_op jit(solution)/shard_map/return/ppermute | solution.py:290

commit v14 on v13

--- a/solution.py
+++ b/solution.py
@@ -216,12 +216,8 @@
     with jax.named_scope("exchange"):
         whole = {r: over(kv_piece, r) if r else kv_piece for r in range(n_out) if single(r)}
         q_by = {0: q_piece}
-        bit = chips // 2
-        while bit:
-            for r in sorted(q_by):
-                piece = after(q_by[r], list(whole.values())[1:]) if r else q_piece
-                q_by[r | bit] = lax.ppermute(piece, "inner", along_inner(bit, 0))
-            bit //= 2
+        for r in reversed(range(1, chips)):
+            q_by[r] = lax.ppermute(q_piece, "inner", along_inner(r, 0))
         k_by = {r: a[:half, :] for r, a in whole.items() if r}
         v_by = {r: a[half:, :] for r, a in whole.items() if r}
         if chips > 1:
@@ -257,9 +253,8 @@
                 name="score",
             )(q_by[r] if done is None else after(q_by[r], done), *ks)
 
-    def apply(r, wide, done):
+    def apply(r, wide):
         with jax.named_scope("apply"):
-            weights, tops = weights_by[r]
             return pl.pallas_call(
                 functools.partial(apply_kernel, wide, rows),
                 out_shape=shapes(wide),
@@ -268,7 +263,7 @@
                 compiler_params=params,
                 cost_estimate=pl.CostEstimate(flops=work, bytes_accessed=2**20, transcendentals=0),
                 name="apply",
-            )(weights, tops if done is None else after(tops, done), *vs)
+            )(*weights_by[r], *vs)
 
     def add(arrays, wide):
         with jax.named_scope("add"):
@@ -291,15 +286,11 @@
             else:
                 arrived[r - low(r)].append(lax.ppermute(parts[0], "inner", along_inner(low(r), 0)))
 
-    weights_by = {}
     done = None
-    for r in range(chips):
+    weights_by, partial = {}, {}
+    for r in reversed(range(chips)):
         weights_by[r] = score(r, done)
-        done = weights_by[r][1]
-    done = None
-    partial = {}
-    for r in reversed(range(chips)):
-        partial[r] = apply(r, r > 1, done)
+        partial[r] = apply(r, r > 1)
         done = partial[r][0]
     for r in reversed(range(1, chips)):
         parts = partial[r]

time: 39.6 us -> 40.3 us (1.018)
  starting transfers between devices: 17 us -> 22.5 us
  waiting for transfers between devices: 14.5 us -> 9.71 us
    ppermute x3, waiting for transfers between devices: 5.66 us -> 1.69 us  [shards(): q_by[r] = lax.ppermute(q_piece, 'inner', along_inner(r, 0))]
    ppermute x4, starting transfers between devices: 5.63 us -> 7.91 us  [over(): return lax.ppermute(a, 'outer', [(o, o ^ r) for o in range(n_out)])]
    ppermute x3, starting transfers between devices: 4.41 us -> 6.64 us  [shards(): q_by[r] = lax.ppermute(q_piece, 'inner', along_inner(r, 0))]
    ppermute x1, starting transfers between devices: 0.07 us -> 1.1 us  [shards(): lax.ppermute(partial[0][1], 'inner', along_inner(0, 1))]
    ppermute x4, starting transfers between devices: 4.53 us -> 3.69 us  [send(): lax.ppermute(parts[x], 'inner', along_inner(r, x))]
    ppermute x1, starting transfers between devices: 1.36 us -> 2.09 us  [send(): lax.ppermute(parts[0], 'inner', along_inner(low(r), 0))]
    ppermute x4, waiting for transfers between devices: 1.69 us -> 1.11 us  [over(): return lax.ppermute(a, 'outer', [(o, o ^ r) for o in range(n_out)])]
    ppermute x1, waiting for transfers between devices: 0.44 us -> 0.01 us  [send(): lax.ppermute(parts[0], 'inner', along_inner(low(r), 0))]
  transfers between devices with their start and end apart: 17 -> 17, of which waited for: 8 -> 5; matrix products, arithmetic and copies ran while one was open for 3% -> 3% of each run, Pallas kernels for 10% -> 11%
where the time goes in v14:
time: 40.3 us; the launch traced here: 40.1 us
  starting transfers between devices  22.5 us (56%)
  waiting for transfers between devices  9.71 us (24%)
  Pallas kernels  6.07 us (15%)
  other arithmetic  1.06 us (3%)
  between operations  0.8 us (2%)
    ppermute x4, starting transfers between devices, over(): return lax.ppermute(a, 'outer', [(o, o ^ r) for o in range(n_out)])  7.91 us
    ppermute x4, waiting for transfers between devices, send(): lax.ppermute(parts[x], 'inner', along_inner(r, x))  6.89 us
    ppermute x3, starting transfers between devices, shards(): q_by[r] = lax.ppermute(q_piece, 'inner', along_inner(r, 0))  6.64 us
    ppermute x4, starting transfers between devices, send(): lax.ppermute(parts[x], 'inner', along_inner(r, x))  3.69 us
    pallas_call x4, Pallas kernels, score(): pl.pallas_call(functools.partial(score_kernel, r == 0), out_shape=(jax.Sh...  3.03 us
    ppermute x1, starting transfers between devices, send(): lax.ppermute(parts[0], 'inner', along_inner(low(r), 0))  2.09 us
    ppermute x3, waiting for transfers between devices, shards(): q_by[r] = lax.ppermute(q_piece, 'inner', along_inner(r, 0))  1.69 us
    pallas_call x4, Pallas kernels, apply(): pl.pallas_call(functools.partial(apply_kernel, wide, rows), out_shape=sha...  1.35 us
  transfers between devices with their start and end apart: 17, of which 5 were waited for; matrix products, arithmetic and copies ran while one was open for 3% of the time, Pallas kernels for 11%

profile of v14, /device:TPU:0, one launch (start us, length us, event | category | flops | bytes accessed | tf_op | source)
XLA Modules:
  0.0 40.1 jit_solution(7258603924440255140)
XLA Ops:
  0.0 0.5 %collective-permute-start.1 = (bf16[128,512]{1,0:T(8,128)(2,1)}, bf16[128,512]{1,0:T(8,128)(2,1)S(1)}, u32[]{:S(2)}, u32[]{:S(2)}) collective-permute-start(bf16[128,512]{1,0:T(8,128)(2,1)} %param.4), channel_id=1, source_target_pairs={{0,1},{1,0},{2,3},{3,2},{4,5},{5,4},{6,7},{7,6},{8,9},{9,8},{10,11... | collective-permute-start | bytes 393224 | tf_op jit(solution)/shard_map/swap/ppermute | solution.py:186
  0.5 0.1 collective-permute-start.2
  0.5 0.5 %collective-permute-start.3 = (bf16[128,512]{1,0:T(8,128)(2,1)}, bf16[128,512]{1,0:T(8,128)(2,1)S(1)}, u32[]{:S(2)}, u32[]{:S(2)}) collective-permute-start(bf16[128,512]{1,0:T(8,128)(2,1)} %param.6), channel_id=1, source_target_pairs={{0,1},{1,0},{2,3},{3,2},{4,5},{5,4},{6,7},{7,6},{8,9},{9,8},{10,11... | collective-permute-start | bytes 393224 | tf_op jit(solution)/shard_map/swap/ppermute | solution.py:186
  1.0 0.1 collective-permute-start
  1.7 1.1 %pad_maximum_fusion.own = bf16[384,512]{1,0:T(8,128)(2,1)S(1)} fusion(bf16[128,512]{1,0:T(8,128)(2,1)} %param.6, bf16[128,512]{1,0:T(8,128)(2,1)} %param.5, bf16[128,512]{1,0:T(8,128)(2,1)} %param.4), kind=kLoop, calls=%fused_computation | loop fusion | flops 1179648 | bytes 786432 | tf_op jit(solution)/shard_map/swap/concatenate | solution.py:187
  2.7 0.0 collective-permute-done.p1
  2.7 0.0 collective-permute-done.1.q1
  2.8 0.0 collective-permute-done.2.k1
  2.8 0.0 collective-permute-done.3.v1
  2.8 0.8 %merge.1 = (bf16[528,128]{1,0:T(8,128)(2,1)S(1)}, bf16[1040,128]{1,0:T(8,128)(2,1)S(1)}) custom-call(s32[1]{0:T(128)S(6)} %copy.5.p0, s32[1]{0:T(128)} %collective-permute-done.p1, bf16[384,512]{1,0:T(8,128)(2,1)S(1)} %pad_maximum_fusion.own, bf16[128,512]{1,0:T(8,128)(2,1)S(1)} %collective-permute-done.1.q1, ...), custom_call_target="tpu_custom_call" | custom-call | tf_op jit(solution)/shard_map/merge/merge/pallas_call | solution.py:190
  3.6 3.0 %collective-permute-start.7 = (bf16[1040,128]{1,0:T(8,128)(2,1)S(1)}, bf16[1040,128]{1,0:T(8,128)(2,1)S(1)}, u32[]{:S(2)}, u32[]{:S(2)}) collective-permute-start(bf16[1040,128]{1,0:T(8,128)(2,1)S(1)} %get-tuple-element.26.refs_0_), channel_id=1, source_target_pairs={{0,8},{8,0},{16,24},{24,16},{1,9},{9,1},{17,25},{25,17},{2,10},{10... | collective-permute-start | bytes 798728 | tf_op jit(solution)/shard_map/exchange/ppermute | solution.py:214
  6.6 1.5 %collective-permute-start.8 = (bf16[1040,128]{1,0:T(8,128)(2,1)S(1)}, bf16[1040,128]{1,0:T(8,128)(2,1)S(1)}, u32[]{:S(2)}, u32[]{:S(2)}) collective-permute-start(bf16[1040,128]{1,0:T(8,128)(2,1)S(1)} %get-tuple-element.26.refs_0_), channel_id=1, source_target_pairs={{0,16},{8,24},{16,0},{24,8},{1,17},{9,25},{17,1},{25,9},{2,18},{10... | collective-permute-start | bytes 798728 | tf_op jit(solution)/shard_map/exchange/ppermute | solution.py:214
  8.1 1.6 %collective-permute-start.4 = (bf16[528,128]{1,0:T(8,128)(2,1)S(1)}, bf16[528,128]{1,0:T(8,128)(2,1)S(1)}, u32[]{:S(2)}, u32[]{:S(2)}) collective-permute-start(bf16[528,128]{1,0:T(8,128)(2,1)S(1)} %get-tuple-element.37.q_ref), channel_id=1, source_target_pairs={{0,2},{1,3},{2,0},{3,1},{4,6},{5,7},{6,4},{7,5},{8,10},{9,11},{10,... | collective-permute-start | bytes 405512 | tf_op jit(solution)/shard_map/exchange/ppermute | solution.py:220
  9.7 2.5 %collective-permute-start.6 = (bf16[528,128]{1,0:T(8,128)(2,1)S(1)}, bf16[528,128]{1,0:T(8,128)(2,1)S(1)}, u32[]{:S(2)}, u32[]{:S(2)}) collective-permute-start(bf16[528,128]{1,0:T(8,128)(2,1)S(1)} %get-tuple-element.37.q_ref), channel_id=1, source_target_pairs={{0,6},{1,7},{2,4},{3,5},{4,2},{5,3},{6,0},{7,1},{8,14},{9,15},{10,... | collective-permute-start | bytes 405512 | tf_op jit(solution)/shard_map/exchange/ppermute | solution.py:220
  12.1 1.0 %collective-permute-done.7.refs_1_ = bf16[1040,128]{1,0:T(8,128)(2,1)S(1)} collective-permute-done((bf16[1040,128]{1,0:T(8,128)(2,1)S(1)}, bf16[1040,128]{1,0:T(8,128)(2,1)S(1)}, u32[]{:S(2)}, u32[]{:S(2)}) %collective-permute-start.7) | collective-permute-done | bytes 266272 | tf_op jit(solution)/shard_map/exchange/ppermute | solution.py:214
  13.1 0.0 collective-permute-done.4.q_ref
  13.2 1.8 %collective-permute-start.9 = (bf16[528,128]{1,0:T(8,128)(2,1)S(1)}, bf16[528,128]{1,0:T(8,128)(2,1)S(1)}, u32[]{:S(2)}, u32[]{:S(2)}) collective-permute-start(bf16[528,128]{1,0:T(8,128)(2,1)S(1)} %slice.8), channel_id=1, source_target_pairs={{0,16},{8,24},{16,0},{24,8},{1,17},{9,25},{17,1},{25,9},{2,18},{10... | collective-permute-start | bytes 405512 | tf_op jit(solution)/shard_map/exchange/ppermute | solution.py:214
  15.0 0.0 collective-permute-done.8.refs_2_
  15.0 1.6 %collective-permute-start.10 = (bf16[512,128]{1,0:T(8,128)(2,1)S(1)}, bf16[512,128]{1,0:T(8,128)(2,1)S(1)}, u32[]{:S(2)}, u32[]{:S(2)}) collective-permute-start(bf16[512,128]{1,0:T(8,128)(2,1)S(1)} %slice.9), channel_id=1, source_target_pairs={{0,8},{8,0},{16,24},{24,16},{1,9},{9,1},{17,25},{25,17},{2,10},{10... | collective-permute-start | bytes 393224 | tf_op jit(solution)/shard_map/exchange/ppermute | solution.py:214
  16.6 2.6 %collective-permute-start.5 = (bf16[528,128]{1,0:T(8,128)(2,1)S(1)}, bf16[528,128]{1,0:T(8,128)(2,1)S(1)}, u32[]{:S(2)}, u32[]{:S(2)}) collective-permute-start(bf16[528,128]{1,0:T(8,128)(2,1)S(1)} %get-tuple-element.37.q_ref), channel_id=1, source_target_pairs={{0,4},{1,5},{2,6},{3,7},{4,0},{5,1},{6,2},{7,3},{8,12},{9,13},{10,... | collective-permute-start | bytes 405512 | tf_op jit(solution)/shard_map/exchange/ppermute | solution.py:220
  19.2 0.0 collective-permute-done.6.q_ref
  19.2 0.0 collective-permute-done.9.refs_3_
  19.2 0.8 %score.4 = (bf16[2,1024,256]{2,1,0:T(8,128)(2,1)S(1)}, f32[16,256]{1,0:T(8,128)S(1)}) custom-call(bf16[528,128]{1,0:T(8,128)(2,1)S(1)} %collective-permute-done.6.q_ref, bf16[1040,128]{1,0:T(8,128)(2,1)S(1)} %get-tuple-element.26.refs_0_, bf16[1040,128]{1,0:T(8,128)(2,1)S(1)} %collective-permute-done.7.refs_1_, ...), custom_call_target="tpu_custom_call" | custom-call | flops 134217728 | bytes 1048576 | tf_op jit(solution)/shard_map/score/score/pallas_call | solution.py:243
  19.9 0.1 collective-permute-done.10.refs_3_
  20.0 0.3 apply.4
  20.4 2.1 %collective-permute-start.12 = (bf16[544,128]{1,0:T(8,128)(2,1)S(1)}, bf16[544,128]{1,0:T(8,128)(2,1)S(1)}, u32[]{:S(2)}, u32[]{:S(2)}) collective-permute-start(bf16[544,128]{1,0:T(8,128)(2,1)S(1)} %apply.4), channel_id=1, source_target_pairs={{0,2},{1,3},{2,0},{3,1},{4,6},{5,7},{6,4},{7,5},{8,10},{9,11},{10,... | collective-permute-start | bytes 417800 | tf_op jit(solution)/shard_map/return/ppermute | solution.py:287
  22.5 1.7 %collective-permute-done.5.q_ref = bf16[528,128]{1,0:T(8,128)(2,1)S(1)} collective-permute-done((bf16[528,128]{1,0:T(8,128)(2,1)S(1)}, bf16[528,128]{1,0:T(8,128)(2,1)S(1)}, u32[]{:S(2)}, u32[]{:S(2)}) %collective-permute-start.5) | collective-permute-done | bytes 135200 | tf_op jit(solution)/shard_map/exchange/ppermute | solution.py:220
  24.2 0.8 %score.5 = (bf16[2,1024,256]{2,1,0:T(8,128)(2,1)S(1)}, f32[16,256]{1,0:T(8,128)S(1)}) custom-call(bf16[528,128]{1,0:T(8,128)(2,1)S(1)} %collective-permute-done.5.q_ref, bf16[1040,128]{1,0:T(8,128)(2,1)S(1)} %get-tuple-element.26.refs_0_, bf16[1040,128]{1,0:T(8,128)(2,1)S(1)} %collective-permute-done.7.refs_1_, ...), custom_call_target="tpu_custom_call" | custom-call | flops 134217728 | bytes 1048576 | tf_op jit(solution)/shard_map/score/score/pallas_call | solution.py:243
  24.9 0.3 apply.5.refs_0_
  25.3 0.8 %score.6 = (bf16[2,1024,256]{2,1,0:T(8,128)(2,1)S(1)}, f32[16,256]{1,0:T(8,128)S(1)}) custom-call(bf16[528,128]{1,0:T(8,128)(2,1)S(1)} %collective-permute-done.4.q_ref, bf16[1040,128]{1,0:T(8,128)(2,1)S(1)} %get-tuple-element.26.refs_0_, bf16[1040,128]{1,0:T(8,128)(2,1)S(1)} %collective-permute-done.7.refs_1_, ...), custom_call_target="tpu_custom_call" | custom-call | flops 134217728 | bytes 1048576 | tf_op jit(solution)/shard_map/score/score/pallas_call | solution.py:243
  26.0 0.3 apply.6
  26.4 1.2 %collective-permute-start.15 = (bf16[272,128]{1,0:T(8,128)(2,1)S(1)}, bf16[272,128]{1,0:T(8,128)(2,1)S(1)}, u32[]{:S(2)}, u32[]{:S(2)}) collective-permute-start(bf16[272,128]{1,0:T(8,128)(2,1)S(1)} %get-tuple-element.36), channel_id=1, source_target_pairs={{0,2},{1,3},{2,0},{3,1},{4,6},{5,7},{6,4},{7,5},{8,10},{9,11},{10,... | collective-permute-start | bytes 208904 | tf_op jit(solution)/shard_map/return/ppermute | solution.py:285
  27.6 0.0 collective-permute-start.16
  27.6 0.8 %score.7 = (bf16[2,1024,256]{2,1,0:T(8,128)(2,1)S(1)}, f32[16,256]{1,0:T(8,128)S(1)}) custom-call(bf16[528,128]{1,0:T(8,128)(2,1)S(1)} %get-tuple-element.37.q_ref, bf16[1040,128]{1,0:T(8,128)(2,1)S(1)} %get-tuple-element.26.refs_0_, bf16[1040,128]{1,0:T(8,128)(2,1)S(1)} %collective-permute-done.7.refs_1_, ...), custom_call_target="tpu_custom_call" | custom-call | flops 134217728 | bytes 1048576 | tf_op jit(solution)/shard_map/score/score/pallas_call | solution.py:243
  28.3 0.3 apply.7
  28.7 1.1 %collective-permute-start.11 = (bf16[272,128]{1,0:T(8,128)(2,1)S(1)}, bf16[272,128]{1,0:T(8,128)(2,1)S(1)}, u32[]{:S(2)}, u32[]{:S(2)}) collective-permute-start(bf16[272,128]{1,0:T(8,128)(2,1)S(1)} %get-tuple-element.41), channel_id=1, source_target_pairs={{0,1},{1,0},{2,3},{3,2},{4,5},{5,4},{6,7},{7,6},{8,9},{9,8},{10,11... | collective-permute-start | bytes 208904 | tf_op jit(solution)/shard_map/return/ppermute | solution.py:301
  29.8 0.0 collective-permute-done.12.refs_1_
  29.8 0.1 add.1
  29.9 2.5 %collective-permute-start.13 = (bf16[272,128]{1,0:T(8,128)(2,1)S(1)}, bf16[272,128]{1,0:T(8,128)(2,1)S(1)}, u32[]{:S(2)}, u32[]{:S(2)}) collective-permute-start(bf16[272,128]{1,0:T(8,128)(2,1)S(1)} %get-tuple-element.42), channel_id=1, source_target_pairs={{0,4},{1,5},{2,6},{3,7},{4,0},{5,1},{6,2},{7,3},{8,12},{9,13},{10,... | collective-permute-start | bytes 208904 | tf_op jit(solution)/shard_map/return/ppermute | solution.py:285
  32.3 0.0 collective-permute-start.14
  32.4 0.0 collective-permute-done.16.refs_5_
  32.4 0.0 collective-permute-done.15.refs_4_
  32.4 0.0 collective-permute-done.11.refs_1_
  32.4 4.6 %collective-permute-done.13.refs_2_ = bf16[272,128]{1,0:T(8,128)(2,1)S(1)} collective-permute-done((bf16[272,128]{1,0:T(8,128)(2,1)S(1)}, bf16[272,128]{1,0:T(8,128)(2,1)S(1)}, u32[]{:S(2)}, u32[]{:S(2)}) %collective-permute-start.13) | collective-permute-done | bytes 69664 | tf_op jit(solution)/shard_map/return/ppermute | solution.py:285
  36.9 2.3 %collective-permute-done.14.refs_3_ = bf16[272,128]{1,0:T(8,128)(2,1)S(1)} collective-permute-done((bf16[272,128]{1,0:T(8,128)(2,1)S(1)}, bf16[272,128]{1,0:T(8,128)(2,1)S(1)}, u32[]{:S(2)}, u32[]{:S(2)}) %collective-permute-start.14) | collective-permute-done | bytes 69664 | tf_op jit(solution)/shard_map/return/ppermute | solution.py:285
  39.3 0.8 %combine.1 = bf16[128,512]{1,0:T(8,128)(2,1)} custom-call(bf16[272,128]{1,0:T(8,128)(2,1)S(1)} %get-tuple-element.40.refs_0_, bf16[272,128]{1,0:T(8,128)(2,1)S(1)} %collective-permute-done.11.refs_1_, bf16[272,128]{1,0:T(8,128)(2,1)S(1)} %collective-permute-done.13.refs_2_, bf16[272,128]{1,0:T(8,128)(2,1)S(1)} %collective-permute-done.14.refs_3_, ...), custom_call_target="tpu_custom_call" | custom-call | tf_op jit(solution)/shard_map/combine/combine/pallas_call | solution.py:303
  (2 shorter events, 0.0 us)
Async XLA Ops:
  0.0 2.7 %collective-permute-start.1 = (bf16[128,512]{1,0:T(8,128)(2,1)}, bf16[128,512]{1,0:T(8,128)(2,1)S(1)}, u32[]{:S(2)}, u32[]{:S(2)}) collective-permute-start(bf16[128,512]{1,0:T(8,128)(2,1)} %param.4), channel_id=1, source_target_pairs={{0,1},{1,0},{2,3},{3,2},{4,5},{5,4},{6,7},{7,6},{8,9},{9,8},{10,11... | collective-permute-start | bytes 393224 | tf_op jit(solution)/shard_map/swap/ppermute | solution.py:186
  0.5 2.3 %collective-permute-start.2 = (bf16[128,512]{1,0:T(8,128)(2,1)}, bf16[128,512]{1,0:T(8,128)(2,1)S(1)}, u32[]{:S(2)}, u32[]{:S(2)}) collective-permute-start(bf16[128,512]{1,0:T(8,128)(2,1)} %param.5), channel_id=1, source_target_pairs={{0,1},{1,0},{2,3},{3,2},{4,5},{5,4},{6,7},{7,6},{8,9},{9,8},{10,11... | collective-permute-start | bytes 393224 | tf_op jit(solution)/shard_map/swap/ppermute | solution.py:186
  0.5 2.3 %collective-permute-start.3 = (bf16[128,512]{1,0:T(8,128)(2,1)}, bf16[128,512]{1,0:T(8,128)(2,1)S(1)}, u32[]{:S(2)}, u32[]{:S(2)}) collective-permute-start(bf16[128,512]{1,0:T(8,128)(2,1)} %param.6), channel_id=1, source_target_pairs={{0,1},{1,0},{2,3},{3,2},{4,5},{5,4},{6,7},{7,6},{8,9},{9,8},{10,11... | collective-permute-start | bytes 393224 | tf_op jit(solution)/shard_map/swap/ppermute | solution.py:186
  1.0 1.8 %collective-permute-start = (s32[1]{0:T(128)}, s32[1]{0:T(128)}, u32[]{:S(2)}, u32[]{:S(2)}) collective-permute-start(s32[1]{0:T(128)} %param.7), channel_id=1, source_target_pairs={{0,1},{1,0},{2,3},{3,2},{4,5},{5,4},{6,7},{7,6},{8,9},{9,8},{10,11... | collective-permute-start | bytes 20 | tf_op jit(solution)/shard_map/swap/ppermute | solution.py:186
  3.6 9.6 %collective-permute-start.7 = (bf16[1040,128]{1,0:T(8,128)(2,1)S(1)}, bf16[1040,128]{1,0:T(8,128)(2,1)S(1)}, u32[]{:S(2)}, u32[]{:S(2)}) collective-permute-start(bf16[1040,128]{1,0:T(8,128)(2,1)S(1)} %get-tuple-element.26.refs_0_), channel_id=1, source_target_pairs={{0,8},{8,0},{16,24},{24,16},{1,9},{9,1},{17,25},{25,17},{2,10},{10... | collective-permute-start | bytes 798728 | tf_op jit(solution)/shard_map/exchange/ppermute | solution.py:214
  6.6 8.4 %collective-permute-start.8 = (bf16[1040,128]{1,0:T(8,128)(2,1)S(1)}, bf16[1040,128]{1,0:T(8,128)(2,1)S(1)}, u32[]{:S(2)}, u32[]{:S(2)}) collective-permute-start(bf16[1040,128]{1,0:T(8,128)(2,1)S(1)} %get-tuple-element.26.refs_0_), channel_id=1, source_target_pairs={{0,16},{8,24},{16,0},{24,8},{1,17},{9,25},{17,1},{25,9},{2,18},{10... | collective-permute-start | bytes 798728 | tf_op jit(solution)/shard_map/exchange/ppermute | solution.py:214
  8.1 5.1 %collective-permute-start.4 = (bf16[528,128]{1,0:T(8,128)(2,1)S(1)}, bf16[528,128]{1,0:T(8,128)(2,1)S(1)}, u32[]{:S(2)}, u32[]{:S(2)}) collective-permute-start(bf16[528,128]{1,0:T(8,128)(2,1)S(1)} %get-tuple-element.37.q_ref), channel_id=1, source_target_pairs={{0,2},{1,3},{2,0},{3,1},{4,6},{5,7},{6,4},{7,5},{8,10},{9,11},{10,... | collective-permute-start | bytes 405512 | tf_op jit(solution)/shard_map/exchange/ppermute | solution.py:220
  9.7 9.5 %collective-permute-start.6 = (bf16[528,128]{1,0:T(8,128)(2,1)S(1)}, bf16[528,128]{1,0:T(8,128)(2,1)S(1)}, u32[]{:S(2)}, u32[]{:S(2)}) collective-permute-start(bf16[528,128]{1,0:T(8,128)(2,1)S(1)} %get-tuple-element.37.q_ref), channel_id=1, source_target_pairs={{0,6},{1,7},{2,4},{3,5},{4,2},{5,3},{6,0},{7,1},{8,14},{9,15},{10,... | collective-permute-start | bytes 405512 | tf_op jit(solution)/shard_map/exchange/ppermute | solution.py:220
  13.2 6.0 %collective-permute-start.9 = (bf16[528,128]{1,0:T(8,128)(2,1)S(1)}, bf16[528,128]{1,0:T(8,128)(2,1)S(1)}, u32[]{:S(2)}, u32[]{:S(2)}) collective-permute-start(bf16[528,128]{1,0:T(8,128)(2,1)S(1)} %slice.8), channel_id=1, source_target_pairs={{0,16},{8,24},{16,0},{24,8},{1,17},{9,25},{17,1},{25,9},{2,18},{10... | collective-permute-start | bytes 405512 | tf_op jit(solution)/shard_map/exchange/ppermute | solution.py:214
  15.0 5.0 %collective-permute-start.10 = (bf16[512,128]{1,0:T(8,128)(2,1)S(1)}, bf16[512,128]{1,0:T(8,128)(2,1)S(1)}, u32[]{:S(2)}, u32[]{:S(2)}) collective-permute-start(bf16[512,128]{1,0:T(8,128)(2,1)S(1)} %slice.9), channel_id=1, source_target_pairs={{0,8},{8,0},{16,24},{24,16},{1,9},{9,1},{17,25},{25,17},{2,10},{10... | collective-permute-start | bytes 393224 | tf_op jit(solution)/shard_map/exchange/ppermute | solution.py:214
  16.6 7.6 %collective-permute-start.5 = (bf16[528,128]{1,0:T(8,128)(2,1)S(1)}, bf16[528,128]{1,0:T(8,128)(2,1)S(1)}, u32[]{:S(2)}, u32[]{:S(2)}) collective-permute-start(bf16[528,128]{1,0:T(8,128)(2,1)S(1)} %get-tuple-element.37.q_ref), channel_id=1, source_target_pairs={{0,4},{1,5},{2,6},{3,7},{4,0},{5,1},{6,2},{7,3},{8,12},{9,13},{10,... | collective-permute-start | bytes 405512 | tf_op jit(solution)/shard_map/exchange/ppermute | solution.py:220
  20.4 9.4 %collective-permute-start.12 = (bf16[544,128]{1,0:T(8,128)(2,1)S(1)}, bf16[544,128]{1,0:T(8,128)(2,1)S(1)}, u32[]{:S(2)}, u32[]{:S(2)}) collective-permute-start(bf16[544,128]{1,0:T(8,128)(2,1)S(1)} %apply.4), channel_id=1, source_target_pairs={{0,2},{1,3},{2,0},{3,1},{4,6},{5,7},{6,4},{7,5},{8,10},{9,11},{10,... | collective-permute-start | bytes 417800 | tf_op jit(solution)/shard_map/return/ppermute | solution.py:287
  26.4 6.0 %collective-permute-start.15 = (bf16[272,128]{1,0:T(8,128)(2,1)S(1)}, bf16[272,128]{1,0:T(8,128)(2,1)S(1)}, u32[]{:S(2)}, u32[]{:S(2)}) collective-permute-start(bf16[272,128]{1,0:T(8,128)(2,1)S(1)} %get-tuple-element.36), channel_id=1, source_target_pairs={{0,2},{1,3},{2,0},{3,1},{4,6},{5,7},{6,4},{7,5},{8,10},{9,11},{10,... | collective-permute-start | bytes 208904 | tf_op jit(solution)/shard_map/return/ppermute | solution.py:285
  27.6 4.8 %collective-permute-start.16 = (bf16[272,128]{1,0:T(8,128)(2,1)S(1)}, bf16[272,128]{1,0:T(8,128)(2,1)S(1)}, u32[]{:S(2)}, u32[]{:S(2)}) collective-permute-start(bf16[272,128]{1,0:T(8,128)(2,1)S(1)} %get-tuple-element.44), channel_id=1, source_target_pairs={{0,3},{1,2},{2,1},{3,0},{4,7},{5,6},{6,5},{7,4},{8,11},{9,10},{10,... | collective-permute-start | bytes 208904 | tf_op jit(solution)/shard_map/return/ppermute | solution.py:285
  28.7 3.7 %collective-permute-start.11 = (bf16[272,128]{1,0:T(8,128)(2,1)S(1)}, bf16[272,128]{1,0:T(8,128)(2,1)S(1)}, u32[]{:S(2)}, u32[]{:S(2)}) collective-permute-start(bf16[272,128]{1,0:T(8,128)(2,1)S(1)} %get-tuple-element.41), channel_id=1, source_target_pairs={{0,1},{1,0},{2,3},{3,2},{4,5},{5,4},{6,7},{7,6},{8,9},{9,8},{10,11... | collective-permute-start | bytes 208904 | tf_op jit(solution)/shard_map/return/ppermute | solution.py:301
  29.9 7.1 %collective-permute-start.13 = (bf16[272,128]{1,0:T(8,128)(2,1)S(1)}, bf16[272,128]{1,0:T(8,128)(2,1)S(1)}, u32[]{:S(2)}, u32[]{:S(2)}) collective-permute-start(bf16[272,128]{1,0:T(8,128)(2,1)S(1)} %get-tuple-element.42), channel_id=1, source_target_pairs={{0,4},{1,5},{2,6},{3,7},{4,0},{5,1},{6,2},{7,3},{8,12},{9,13},{10,... | collective-permute-start | bytes 208904 | tf_op jit(solution)/shard_map/return/ppermute | solution.py:285
  32.3 6.9 %collective-permute-start.14 = (bf16[272,128]{1,0:T(8,128)(2,1)S(1)}, bf16[272,128]{1,0:T(8,128)(2,1)S(1)}, u32[]{:S(2)}, u32[]{:S(2)}) collective-permute-start(bf16[272,128]{1,0:T(8,128)(2,1)S(1)} %get-tuple-element.43), channel_id=1, source_target_pairs={{0,5},{1,4},{2,7},{3,6},{4,1},{5,0},{6,3},{7,2},{8,13},{9,12},{10,... | collective-permute-start | bytes 208904 | tf_op jit(solution)/shard_map/return/ppermute | solution.py:285

commit v15 on v14

--- a/solution.py
+++ b/solution.py
@@ -286,17 +286,24 @@
             else:
                 arrived[r - low(r)].append(lax.ppermute(parts[0], "inner", along_inner(low(r), 0)))
 
+    def both_kernels(r, done):
+        weights_by[r] = score(r, done)
+        partial[r] = apply(r, r > 1)
+        return partial[r][0]
+
     done = None
     weights_by, partial = {}, {}
-    for r in reversed(range(chips)):
-        weights_by[r] = score(r, done)
-        partial[r] = apply(r, r > 1)
-        done = partial[r][0]
+    for r in reversed(range(1, chips)):
+        done = both_kernels(r, done)
     for r in reversed(range(1, chips)):
         parts = partial[r]
         if arrived[r]:
             parts = add([parts[0], *arrived[r]], not single(r))
+            done = parts[0]
+        if r == 1:
+            parts = [parts[0], after(parts[1], done)]
         send(r, parts)
+    both_kernels(0, done)
     with jax.named_scope("return"):
         ends = [partial[0][0], lax.ppermute(partial[0][1], "inner", along_inner(0, 1))] + ends
     with jax.named_scope("combine"):

time: 40.3 us -> 38.3 us (0.950)
  waiting for transfers between devices: 9.71 us -> 7.24 us
    ppermute x4, waiting for transfers between devices: 6.89 us -> 4.43 us  [send(): lax.ppermute(parts[x], 'inner', along_inner(r, x))]
    ppermute x4, starting transfers between devices: 3.69 us -> 4.89 us  [send(): lax.ppermute(parts[x], 'inner', along_inner(r, x))]
    ppermute x1, starting transfers between devices: 1.1 us -> 0.39 us  [shards(): lax.ppermute(partial[0][1], 'inner', along_inner(0, 1))]
  transfers between devices with their start and end apart: 17 -> 17, of which waited for: 5 -> 5; matrix products, arithmetic and copies ran while one was open for 3% -> 3% of each run, Pallas kernels for 11% -> 12%
where the time goes in v15:
time: 38.3 us; the launch traced here: 38.1 us
  starting transfers between devices  22.9 us (60%)
  waiting for transfers between devices  7.24 us (19%)
  Pallas kernels  6.06 us (16%)
  other arithmetic  1.06 us (3%)
  between operations  0.79 us (2%)
    ppermute x4, starting transfers between devices, over(): return lax.ppermute(a, 'outer', [(o, o ^ r) for o in range(n_out)])  7.91 us
    ppermute x3, starting transfers between devices, shards(): q_by[r] = lax.ppermute(q_piece, 'inner', along_inner(r, 0))  6.64 us
    ppermute x4, starting transfers between devices, send(): lax.ppermute(parts[x], 'inner', along_inner(r, x))  4.89 us
    ppermute x4, waiting for transfers between devices, send(): lax.ppermute(parts[x], 'inner', along_inner(r, x))  4.43 us
    pallas_call x4, Pallas kernels, score(): pl.pallas_call(functools.partial(score_kernel, r == 0), out_shape=(jax.Sh...  3.03 us
    ppermute x1, starting transfers between devices, send(): lax.ppermute(parts[0], 'inner', along_inner(low(r), 0))  2.09 us
    ppermute x3, waiting for transfers between devices, shards(): q_by[r] = lax.ppermute(q_piece, 'inner', along_inner(r, 0))  1.69 us
    pallas_call x4, Pallas kernels, apply(): pl.pallas_call(functools.partial(apply_kernel, wide, rows), out_shape=sha...  1.35 us
  transfers between devices with their start and end apart: 17, of which 5 were waited for; matrix products, arithmetic and copies ran while one was open for 3% of the time, Pallas kernels for 12%

profile of v15, /device:TPU:0, one launch (start us, length us, event | category | flops | bytes accessed | tf_op | source)
XLA Modules:
  0.0 38.1 jit_solution(14540807937846096464)
XLA Ops:
  0.0 0.5 %collective-permute-start.1 = (bf16[128,512]{1,0:T(8,128)(2,1)}, bf16[128,512]{1,0:T(8,128)(2,1)S(1)}, u32[]{:S(2)}, u32[]{:S(2)}) collective-permute-start(bf16[128,512]{1,0:T(8,128)(2,1)} %param.4), channel_id=1, source_target_pairs={{0,1},{1,0},{2,3},{3,2},{4,5},{5,4},{6,7},{7,6},{8,9},{9,8},{10,11... | collective-permute-start | bytes 393224 | tf_op jit(solution)/shard_map/swap/ppermute | solution.py:186
  0.5 0.1 collective-permute-start.2
  0.5 0.5 %collective-permute-start.3 = (bf16[128,512]{1,0:T(8,128)(2,1)}, bf16[128,512]{1,0:T(8,128)(2,1)S(1)}, u32[]{:S(2)}, u32[]{:S(2)}) collective-permute-start(bf16[128,512]{1,0:T(8,128)(2,1)} %param.6), channel_id=1, source_target_pairs={{0,1},{1,0},{2,3},{3,2},{4,5},{5,4},{6,7},{7,6},{8,9},{9,8},{10,11... | collective-permute-start | bytes 393224 | tf_op jit(solution)/shard_map/swap/ppermute | solution.py:186
  1.0 0.1 collective-permute-start
  1.7 1.1 %pad_maximum_fusion.own = bf16[384,512]{1,0:T(8,128)(2,1)S(1)} fusion(bf16[128,512]{1,0:T(8,128)(2,1)} %param.6, bf16[128,512]{1,0:T(8,128)(2,1)} %param.5, bf16[128,512]{1,0:T(8,128)(2,1)} %param.4), kind=kLoop, calls=%fused_computation | loop fusion | flops 1179648 | bytes 786432 | tf_op jit(solution)/shard_map/swap/concatenate | solution.py:187
  2.7 0.0 collective-permute-done.p1
  2.7 0.0 collective-permute-done.1.q1
  2.8 0.0 collective-permute-done.2.k1
  2.8 0.0 collective-permute-done.3.v1
  2.8 0.8 %merge.1 = (bf16[528,128]{1,0:T(8,128)(2,1)S(1)}, bf16[1040,128]{1,0:T(8,128)(2,1)S(1)}) custom-call(s32[1]{0:T(128)S(6)} %copy.5.p0, s32[1]{0:T(128)} %collective-permute-done.p1, bf16[384,512]{1,0:T(8,128)(2,1)S(1)} %pad_maximum_fusion.own, bf16[128,512]{1,0:T(8,128)(2,1)S(1)} %collective-permute-done.1.q1, ...), custom_call_target="tpu_custom_call" | custom-call | tf_op jit(solution)/shard_map/merge/merge/pallas_call | solution.py:190
  3.6 3.0 %collective-permute-start.6 = (bf16[1040,128]{1,0:T(8,128)(2,1)S(1)}, bf16[1040,128]{1,0:T(8,128)(2,1)S(1)}, u32[]{:S(2)}, u32[]{:S(2)}) collective-permute-start(bf16[1040,128]{1,0:T(8,128)(2,1)S(1)} %get-tuple-element.27.refs_0_), channel_id=1, source_target_pairs={{0,8},{8,0},{16,24},{24,16},{1,9},{9,1},{17,25},{25,17},{2,10},{10... | collective-permute-start | bytes 798728 | tf_op jit(solution)/shard_map/exchange/ppermute | solution.py:214
  6.6 1.5 %collective-permute-start.7 = (bf16[1040,128]{1,0:T(8,128)(2,1)S(1)}, bf16[1040,128]{1,0:T(8,128)(2,1)S(1)}, u32[]{:S(2)}, u32[]{:S(2)}) collective-permute-start(bf16[1040,128]{1,0:T(8,128)(2,1)S(1)} %get-tuple-element.27.refs_0_), channel_id=1, source_target_pairs={{0,16},{8,24},{16,0},{24,8},{1,17},{9,25},{17,1},{25,9},{2,18},{10... | collective-permute-start | bytes 798728 | tf_op jit(solution)/shard_map/exchange/ppermute | solution.py:214
  8.1 1.6 %collective-permute-start.8 = (bf16[528,128]{1,0:T(8,128)(2,1)S(1)}, bf16[528,128]{1,0:T(8,128)(2,1)S(1)}, u32[]{:S(2)}, u32[]{:S(2)}) collective-permute-start(bf16[528,128]{1,0:T(8,128)(2,1)S(1)} %get-tuple-element.35.q_ref), channel_id=1, source_target_pairs={{0,2},{1,3},{2,0},{3,1},{4,6},{5,7},{6,4},{7,5},{8,10},{9,11},{10,... | collective-permute-start | bytes 405512 | tf_op jit(solution)/shard_map/exchange/ppermute | solution.py:220
  9.7 2.5 %collective-permute-start.5 = (bf16[528,128]{1,0:T(8,128)(2,1)S(1)}, bf16[528,128]{1,0:T(8,128)(2,1)S(1)}, u32[]{:S(2)}, u32[]{:S(2)}) collective-permute-start(bf16[528,128]{1,0:T(8,128)(2,1)S(1)} %get-tuple-element.35.q_ref), channel_id=1, source_target_pairs={{0,6},{1,7},{2,4},{3,5},{4,2},{5,3},{6,0},{7,1},{8,14},{9,15},{10,... | collective-permute-start | bytes 405512 | tf_op jit(solution)/shard_map/exchange/ppermute | solution.py:220
  12.1 1.0 %collective-permute-done.6.refs_1_ = bf16[1040,128]{1,0:T(8,128)(2,1)S(1)} collective-permute-done((bf16[1040,128]{1,0:T(8,128)(2,1)S(1)}, bf16[1040,128]{1,0:T(8,128)(2,1)S(1)}, u32[]{:S(2)}, u32[]{:S(2)}) %collective-permute-start.6) | collective-permute-done | bytes 266272 | tf_op jit(solution)/shard_map/exchange/ppermute | solution.py:214
  13.1 0.0 collective-permute-done.8.q_ref
  13.2 1.8 %collective-permute-start.9 = (bf16[528,128]{1,0:T(8,128)(2,1)S(1)}, bf16[528,128]{1,0:T(8,128)(2,1)S(1)}, u32[]{:S(2)}, u32[]{:S(2)}) collective-permute-start(bf16[528,128]{1,0:T(8,128)(2,1)S(1)} %slice.8), channel_id=1, source_target_pairs={{0,16},{8,24},{16,0},{24,8},{1,17},{9,25},{17,1},{25,9},{2,18},{10... | collective-permute-start | bytes 405512 | tf_op jit(solution)/shard_map/exchange/ppermute | solution.py:214
  15.0 0.0 collective-permute-done.7.refs_2_
  15.0 1.6 %collective-permute-start.10 = (bf16[512,128]{1,0:T(8,128)(2,1)S(1)}, bf16[512,128]{1,0:T(8,128)(2,1)S(1)}, u32[]{:S(2)}, u32[]{:S(2)}) collective-permute-start(bf16[512,128]{1,0:T(8,128)(2,1)S(1)} %slice.9), channel_id=1, source_target_pairs={{0,8},{8,0},{16,24},{24,16},{1,9},{9,1},{17,25},{25,17},{2,10},{10... | collective-permute-start | bytes 393224 | tf_op jit(solution)/shard_map/exchange/ppermute | solution.py:214
  16.6 2.6 %collective-permute-start.4 = (bf16[528,128]{1,0:T(8,128)(2,1)S(1)}, bf16[528,128]{1,0:T(8,128)(2,1)S(1)}, u32[]{:S(2)}, u32[]{:S(2)}) collective-permute-start(bf16[528,128]{1,0:T(8,128)(2,1)S(1)} %get-tuple-element.35.q_ref), channel_id=1, source_target_pairs={{0,4},{1,5},{2,6},{3,7},{4,0},{5,1},{6,2},{7,3},{8,12},{9,13},{10,... | collective-permute-start | bytes 405512 | tf_op jit(solution)/shard_map/exchange/ppermute | solution.py:220
  19.2 0.0 collective-permute-done.5.q_ref
  19.2 0.0 collective-permute-done.9.refs_3_
  19.2 0.8 %score.4 = (bf16[2,1024,256]{2,1,0:T(8,128)(2,1)S(1)}, f32[16,256]{1,0:T(8,128)S(1)}) custom-call(bf16[528,128]{1,0:T(8,128)(2,1)S(1)} %collective-permute-done.5.q_ref, bf16[1040,128]{1,0:T(8,128)(2,1)S(1)} %get-tuple-element.27.refs_0_, bf16[1040,128]{1,0:T(8,128)(2,1)S(1)} %collective-permute-done.6.refs_1_, ...), custom_call_target="tpu_custom_call" | custom-call | flops 134217728 | bytes 1048576 | tf_op jit(solution)/shard_map/score/score/pallas_call | solution.py:243
  19.9 0.1 collective-permute-done.10.refs_3_
  20.0 0.3 apply.4
  20.4 2.1 %collective-permute-start.11 = (bf16[544,128]{1,0:T(8,128)(2,1)S(1)}, bf16[544,128]{1,0:T(8,128)(2,1)S(1)}, u32[]{:S(2)}, u32[]{:S(2)}) collective-permute-start(bf16[544,128]{1,0:T(8,128)(2,1)S(1)} %apply.4), channel_id=1, source_target_pairs={{0,2},{1,3},{2,0},{3,1},{4,6},{5,7},{6,4},{7,5},{8,10},{9,11},{10,... | collective-permute-start | bytes 417800 | tf_op jit(solution)/shard_map/return/ppermute | solution.py:287
  22.5 1.7 %collective-permute-done.4.q_ref = bf16[528,128]{1,0:T(8,128)(2,1)S(1)} collective-permute-done((bf16[528,128]{1,0:T(8,128)(2,1)S(1)}, bf16[528,128]{1,0:T(8,128)(2,1)S(1)}, u32[]{:S(2)}, u32[]{:S(2)}) %collective-permute-start.4) | collective-permute-done | bytes 135200 | tf_op jit(solution)/shard_map/exchange/ppermute | solution.py:220
  24.2 0.7 %score.5 = (bf16[2,1024,256]{2,1,0:T(8,128)(2,1)S(1)}, f32[16,256]{1,0:T(8,128)S(1)}) custom-call(bf16[528,128]{1,0:T(8,128)(2,1)S(1)} %collective-permute-done.4.q_ref, bf16[1040,128]{1,0:T(8,128)(2,1)S(1)} %get-tuple-element.27.refs_0_, bf16[1040,128]{1,0:T(8,128)(2,1)S(1)} %collective-permute-done.6.refs_1_, ...), custom_call_target="tpu_custom_call" | custom-call | flops 134217728 | bytes 1048576 | tf_op jit(solution)/shard_map/score/score/pallas_call | solution.py:243
  24.9 0.3 apply.5.refs_0_
  25.3 0.8 %score.7 = (bf16[2,1024,256]{2,1,0:T(8,128)(2,1)S(1)}, f32[16,256]{1,0:T(8,128)S(1)}) custom-call(bf16[528,128]{1,0:T(8,128)(2,1)S(1)} %collective-permute-done.8.q_ref, bf16[1040,128]{1,0:T(8,128)(2,1)S(1)} %get-tuple-element.27.refs_0_, bf16[1040,128]{1,0:T(8,128)(2,1)S(1)} %collective-permute-done.6.refs_1_, ...), custom_call_target="tpu_custom_call" | custom-call | flops 134217728 | bytes 1048576 | tf_op jit(solution)/shard_map/score/score/pallas_call | solution.py:243
  26.0 0.3 apply.7
  26.4 1.2 %collective-permute-start.15 = (bf16[272,128]{1,0:T(8,128)(2,1)S(1)}, bf16[272,128]{1,0:T(8,128)(2,1)S(1)}, u32[]{:S(2)}, u32[]{:S(2)}) collective-permute-start(bf16[272,128]{1,0:T(8,128)(2,1)S(1)} %get-tuple-element.44), channel_id=1, source_target_pairs={{0,2},{1,3},{2,0},{3,1},{4,6},{5,7},{6,4},{7,5},{8,10},{9,11},{10,... | collective-permute-start | bytes 208904 | tf_op jit(solution)/shard_map/return/ppermute | solution.py:285
  27.6 0.0 collective-permute-done.11.refs_1_
  27.6 0.1 add.1
  27.6 3.3 %collective-permute-start.13 = (bf16[272,128]{1,0:T(8,128)(2,1)S(1)}, bf16[272,128]{1,0:T(8,128)(2,1)S(1)}, u32[]{:S(2)}, u32[]{:S(2)}) collective-permute-start(bf16[272,128]{1,0:T(8,128)(2,1)S(1)} %get-tuple-element.34), channel_id=1, source_target_pairs={{0,4},{1,5},{2,6},{3,7},{4,0},{5,1},{6,2},{7,3},{8,12},{9,13},{10,... | collective-permute-start | bytes 208904 | tf_op jit(solution)/shard_map/return/ppermute | solution.py:285
  31.0 0.0 collective-permute-start.14
  31.0 0.4 %collective-permute-start.16 = (bf16[272,128]{1,0:T(8,128)(2,1)S(1)}, bf16[272,128]{1,0:T(8,128)(2,1)S(1)}, u32[]{:S(2)}, u32[]{:S(2)}) collective-permute-start(bf16[272,128]{1,0:T(8,128)(2,1)S(1)} %get-tuple-element.46), channel_id=1, source_target_pairs={{0,3},{1,2},{2,1},{3,0},{4,7},{5,6},{6,5},{7,4},{8,11},{9,10},{10,... | collective-permute-start | bytes 208904 | tf_op jit(solution)/shard_map/return/ppermute | solution.py:285
  31.4 0.8 %score.6 = (bf16[2,1024,256]{2,1,0:T(8,128)(2,1)S(1)}, f32[16,256]{1,0:T(8,128)S(1)}) custom-call(bf16[528,128]{1,0:T(8,128)(2,1)S(1)} %get-tuple-element.35.q_ref, bf16[1040,128]{1,0:T(8,128)(2,1)S(1)} %get-tuple-element.27.refs_0_, bf16[1040,128]{1,0:T(8,128)(2,1)S(1)} %collective-permute-done.6.refs_1_, ...), custom_call_target="tpu_custom_call" | custom-call | flops 134217728 | bytes 1048576 | tf_op jit(solution)/shard_map/score/score/pallas_call | solution.py:243
  32.1 0.3 apply.6
  32.5 0.4 %collective-permute-start.12 = (bf16[272,128]{1,0:T(8,128)(2,1)S(1)}, bf16[272,128]{1,0:T(8,128)(2,1)S(1)}, u32[]{:S(2)}, u32[]{:S(2)}) collective-permute-start(bf16[272,128]{1,0:T(8,128)(2,1)S(1)} %get-tuple-element.39), channel_id=1, source_target_pairs={{0,1},{1,0},{2,3},{3,2},{4,5},{5,4},{6,7},{7,6},{8,9},{9,8},{10,11... | collective-permute-start | bytes 208904 | tf_op jit(solution)/shard_map/return/ppermute | solution.py:308
  32.9 0.0 collective-permute-done.15.refs_4_
  32.9 4.2 %collective-permute-done.14.refs_3_ = bf16[272,128]{1,0:T(8,128)(2,1)S(1)} collective-permute-done((bf16[272,128]{1,0:T(8,128)(2,1)S(1)}, bf16[272,128]{1,0:T(8,128)(2,1)S(1)}, u32[]{:S(2)}, u32[]{:S(2)}) %collective-permute-start.14) | collective-permute-done | bytes 69664 | tf_op jit(solution)/shard_map/return/ppermute | solution.py:285
  37.1 0.0 collective-permute-done.13.refs_2_
  37.1 0.2 collective-permute-done.16.refs_5_
  37.3 0.0 collective-permute-done.12.refs_1_
  37.3 0.8 %combine.1 = bf16[128,512]{1,0:T(8,128)(2,1)} custom-call(bf16[272,128]{1,0:T(8,128)(2,1)S(1)} %get-tuple-element.38.refs_0_, bf16[272,128]{1,0:T(8,128)(2,1)S(1)} %collective-permute-done.12.refs_1_, bf16[272,128]{1,0:T(8,128)(2,1)S(1)} %collective-permute-done.13.refs_2_, bf16[272,128]{1,0:T(8,128)(2,1)S(1)} %collective-permute-done.14.refs_3_, ...), custom_call_target="tpu_custom_call" | custom-call | tf_op jit(solution)/shard_map/combine/combine/pallas_call | solution.py:310
  (2 shorter events, 0.0 us)
Async XLA Ops:
  0.0 2.7 %collective-permute-start.1 = (bf16[128,512]{1,0:T(8,128)(2,1)}, bf16[128,512]{1,0:T(8,128)(2,1)S(1)}, u32[]{:S(2)}, u32[]{:S(2)}) collective-permute-start(bf16[128,512]{1,0:T(8,128)(2,1)} %param.4), channel_id=1, source_target_pairs={{0,1},{1,0},{2,3},{3,2},{4,5},{5,4},{6,7},{7,6},{8,9},{9,8},{10,11... | collective-permute-start | bytes 393224 | tf_op jit(solution)/shard_map/swap/ppermute | solution.py:186
  0.5 2.3 %collective-permute-start.2 = (bf16[128,512]{1,0:T(8,128)(2,1)}, bf16[128,512]{1,0:T(8,128)(2,1)S(1)}, u32[]{:S(2)}, u32[]{:S(2)}) collective-permute-start(bf16[128,512]{1,0:T(8,128)(2,1)} %param.5), channel_id=1, source_target_pairs={{0,1},{1,0},{2,3},{3,2},{4,5},{5,4},{6,7},{7,6},{8,9},{9,8},{10,11... | collective-permute-start | bytes 393224 | tf_op jit(solution)/shard_map/swap/ppermute | solution.py:186
  0.5 2.3 %collective-permute-start.3 = (bf16[128,512]{1,0:T(8,128)(2,1)}, bf16[128,512]{1,0:T(8,128)(2,1)S(1)}, u32[]{:S(2)}, u32[]{:S(2)}) collective-permute-start(bf16[128,512]{1,0:T(8,128)(2,1)} %param.6), channel_id=1, source_target_pairs={{0,1},{1,0},{2,3},{3,2},{4,5},{5,4},{6,7},{7,6},{8,9},{9,8},{10,11... | collective-permute-start | bytes 393224 | tf_op jit(solution)/shard_map/swap/ppermute | solution.py:186
  1.0 1.8 %collective-permute-start = (s32[1]{0:T(128)}, s32[1]{0:T(128)}, u32[]{:S(2)}, u32[]{:S(2)}) collective-permute-start(s32[1]{0:T(128)} %param.7), channel_id=1, source_target_pairs={{0,1},{1,0},{2,3},{3,2},{4,5},{5,4},{6,7},{7,6},{8,9},{9,8},{10,11... | collective-permute-start | bytes 20 | tf_op jit(solution)/shard_map/swap/ppermute | solution.py:186
  3.6 9.6 %collective-permute-start.6 = (bf16[1040,128]{1,0:T(8,128)(2,1)S(1)}, bf16[1040,128]{1,0:T(8,128)(2,1)S(1)}, u32[]{:S(2)}, u32[]{:S(2)}) collective-permute-start(bf16[1040,128]{1,0:T(8,128)(2,1)S(1)} %get-tuple-element.27.refs_0_), channel_id=1, source_target_pairs={{0,8},{8,0},{16,24},{24,16},{1,9},{9,1},{17,25},{25,17},{2,10},{10... | collective-permute-start | bytes 798728 | tf_op jit(solution)/shard_map/exchange/ppermute | solution.py:214
  6.6 8.4 %collective-permute-start.7 = (bf16[1040,128]{1,0:T(8,128)(2,1)S(1)}, bf16[1040,128]{1,0:T(8,128)(2,1)S(1)}, u32[]{:S(2)}, u32[]{:S(2)}) collective-permute-start(bf16[1040,128]{1,0:T(8,128)(2,1)S(1)} %get-tuple-element.27.refs_0_), channel_id=1, source_target_pairs={{0,16},{8,24},{16,0},{24,8},{1,17},{9,25},{17,1},{25,9},{2,18},{10... | collective-permute-start | bytes 798728 | tf_op jit(solution)/shard_map/exchange/ppermute | solution.py:214
  8.1 5.1 %collective-permute-start.8 = (bf16[528,128]{1,0:T(8,128)(2,1)S(1)}, bf16[528,128]{1,0:T(8,128)(2,1)S(1)}, u32[]{:S(2)}, u32[]{:S(2)}) collective-permute-start(bf16[528,128]{1,0:T(8,128)(2,1)S(1)} %get-tuple-element.35.q_ref), channel_id=1, source_target_pairs={{0,2},{1,3},{2,0},{3,1},{4,6},{5,7},{6,4},{7,5},{8,10},{9,11},{10,... | collective-permute-start | bytes 405512 | tf_op jit(solution)/shard_map/exchange/ppermute | solution.py:220
  9.7 9.5 %collective-permute-start.5 = (bf16[528,128]{1,0:T(8,128)(2,1)S(1)}, bf16[528,128]{1,0:T(8,128)(2,1)S(1)}, u32[]{:S(2)}, u32[]{:S(2)}) collective-permute-start(bf16[528,128]{1,0:T(8,128)(2,1)S(1)} %get-tuple-element.35.q_ref), channel_id=1, source_target_pairs={{0,6},{1,7},{2,4},{3,5},{4,2},{5,3},{6,0},{7,1},{8,14},{9,15},{10,... | collective-permute-start | bytes 405512 | tf_op jit(solution)/shard_map/exchange/ppermute | solution.py:220
  13.2 6.0 %collective-permute-start.9 = (bf16[528,128]{1,0:T(8,128)(2,1)S(1)}, bf16[528,128]{1,0:T(8,128)(2,1)S(1)}, u32[]{:S(2)}, u32[]{:S(2)}) collective-permute-start(bf16[528,128]{1,0:T(8,128)(2,1)S(1)} %slice.8), channel_id=1, source_target_pairs={{0,16},{8,24},{16,0},{24,8},{1,17},{9,25},{17,1},{25,9},{2,18},{10... | collective-permute-start | bytes 405512 | tf_op jit(solution)/shard_map/exchange/ppermute | solution.py:214
  15.0 5.0 %collective-permute-start.10 = (bf16[512,128]{1,0:T(8,128)(2,1)S(1)}, bf16[512,128]{1,0:T(8,128)(2,1)S(1)}, u32[]{:S(2)}, u32[]{:S(2)}) collective-permute-start(bf16[512,128]{1,0:T(8,128)(2,1)S(1)} %slice.9), channel_id=1, source_target_pairs={{0,8},{8,0},{16,24},{24,16},{1,9},{9,1},{17,25},{25,17},{2,10},{10... | collective-permute-start | bytes 393224 | tf_op jit(solution)/shard_map/exchange/ppermute | solution.py:214
  16.6 7.6 %collective-permute-start.4 = (bf16[528,128]{1,0:T(8,128)(2,1)S(1)}, bf16[528,128]{1,0:T(8,128)(2,1)S(1)}, u32[]{:S(2)}, u32[]{:S(2)}) collective-permute-start(bf16[528,128]{1,0:T(8,128)(2,1)S(1)} %get-tuple-element.35.q_ref), channel_id=1, source_target_pairs={{0,4},{1,5},{2,6},{3,7},{4,0},{5,1},{6,2},{7,3},{8,12},{9,13},{10,... | collective-permute-start | bytes 405512 | tf_op jit(solution)/shard_map/exchange/ppermute | solution.py:220
  20.4 7.2 %collective-permute-start.11 = (bf16[544,128]{1,0:T(8,128)(2,1)S(1)}, bf16[544,128]{1,0:T(8,128)(2,1)S(1)}, u32[]{:S(2)}, u32[]{:S(2)}) collective-permute-start(bf16[544,128]{1,0:T(8,128)(2,1)S(1)} %apply.4), channel_id=1, source_target_pairs={{0,2},{1,3},{2,0},{3,1},{4,6},{5,7},{6,4},{7,5},{8,10},{9,11},{10,... | collective-permute-start | bytes 417800 | tf_op jit(solution)/shard_map/return/ppermute | solution.py:287
  26.4 6.5 %collective-permute-start.15 = (bf16[272,128]{1,0:T(8,128)(2,1)S(1)}, bf16[272,128]{1,0:T(8,128)(2,1)S(1)}, u32[]{:S(2)}, u32[]{:S(2)}) collective-permute-start(bf16[272,128]{1,0:T(8,128)(2,1)S(1)} %get-tuple-element.44), channel_id=1, source_target_pairs={{0,2},{1,3},{2,0},{3,1},{4,6},{5,7},{6,4},{7,5},{8,10},{9,11},{10,... | collective-permute-start | bytes 208904 | tf_op jit(solution)/shard_map/return/ppermute | solution.py:285
  27.6 9.5 %collective-permute-start.13 = (bf16[272,128]{1,0:T(8,128)(2,1)S(1)}, bf16[272,128]{1,0:T(8,128)(2,1)S(1)}, u32[]{:S(2)}, u32[]{:S(2)}) collective-permute-start(bf16[272,128]{1,0:T(8,128)(2,1)S(1)} %get-tuple-element.34), channel_id=1, source_target_pairs={{0,4},{1,5},{2,6},{3,7},{4,0},{5,1},{6,2},{7,3},{8,12},{9,13},{10,... | collective-permute-start | bytes 208904 | tf_op jit(solution)/shard_map/return/ppermute | solution.py:285
  31.0 6.1 %collective-permute-start.14 = (bf16[272,128]{1,0:T(8,128)(2,1)S(1)}, bf16[272,128]{1,0:T(8,128)(2,1)S(1)}, u32[]{:S(2)}, u32[]{:S(2)}) collective-permute-start(bf16[272,128]{1,0:T(8,128)(2,1)S(1)} %get-tuple-element.40), channel_id=1, source_target_pairs={{0,5},{1,4},{2,7},{3,6},{4,1},{5,0},{6,3},{7,2},{8,13},{9,12},{10,... | collective-permute-start | bytes 208904 | tf_op jit(solution)/shard_map/return/ppermute | solution.py:285
  31.0 6.3 %collective-permute-start.16 = (bf16[272,128]{1,0:T(8,128)(2,1)S(1)}, bf16[272,128]{1,0:T(8,128)(2,1)S(1)}, u32[]{:S(2)}, u32[]{:S(2)}) collective-permute-start(bf16[272,128]{1,0:T(8,128)(2,1)S(1)} %get-tuple-element.46), channel_id=1, source_target_pairs={{0,3},{1,2},{2,1},{3,0},{4,7},{5,6},{6,5},{7,4},{8,11},{9,10},{10,... | collective-permute-start | bytes 208904 | tf_op jit(solution)/shard_map/return/ppermute | solution.py:285
  32.5 4.8 %collective-permute-start.12 = (bf16[272,128]{1,0:T(8,128)(2,1)S(1)}, bf16[272,128]{1,0:T(8,128)(2,1)S(1)}, u32[]{:S(2)}, u32[]{:S(2)}) collective-permute-start(bf16[272,128]{1,0:T(8,128)(2,1)S(1)} %get-tuple-element.39), channel_id=1, source_target_pairs={{0,1},{1,0},{2,3},{3,2},{4,5},{5,4},{6,7},{7,6},{8,9},{9,8},{10,11... | collective-permute-start | bytes 208904 | tf_op jit(solution)/shard_map/return/ppermute | solution.py:308

commit v16 on v15

--- a/solution.py
+++ b/solution.py
@@ -214,19 +214,18 @@
         return lax.ppermute(a, "outer", [(o, o ^ r) for o in range(n_out)])
 
     with jax.named_scope("exchange"):
-        whole = {r: over(kv_piece, r) if r else kv_piece for r in range(n_out) if single(r)}
+        whole = {r: over(kv_piece, r) if r else kv_piece for r in range(n_out) if single(r) and r != 1}
+        k_by = {r: a[:half, :] for r, a in whole.items()}
+        v_by = {r: a[half:, :] for r, a in whole.items()}
+        if n_out > 1:
+            k_by[1], v_by[1] = over(k_by[0], 1), over(v_by[0], 1)
         q_by = {0: q_piece}
         for r in reversed(range(1, chips)):
             q_by[r] = lax.ppermute(q_piece, "inner", along_inner(r, 0))
-        k_by = {r: a[:half, :] for r, a in whole.items() if r}
-        v_by = {r: a[half:, :] for r, a in whole.items() if r}
-        if chips > 1:
-            k_by = {r: after(a, q_by[1]) for r, a in k_by.items()}
-        for r in range(1, n_out):
-            if not single(r):
-                k_by[r] = over(k_by[r - high(r)], high(r))
         for r in sorted(range(1, n_out), key=lambda r: r.bit_count()):
             if not single(r):
+                k = k_by[r - high(r)]
+                k_by[r] = over(after(k, q_by[1]) if chips > 1 else k, high(r))
                 v_by[r] = over(v_by[r - low(r)], low(r))
         ks = [whole[r] if r in whole else k_by[r] for r in range(n_out)]
         vs = [whole[r] if r in whole else v_by[r] for r in range(n_out)]

time: 38.3 us -> 38.8 us (1.013)
  starting transfers between devices: 22.9 us -> 25.6 us
  waiting for transfers between devices: 7.24 us -> 4.93 us
    ppermute x3, starting transfers between devices: 6.64 us -> 8.01 us  [shards(): q_by[r] = lax.ppermute(q_piece, 'inner', along_inner(r, 0))]
    ppermute x4 -> x5, waiting for transfers between devices: 1.11 us -> 0.01 us  [over(): return lax.ppermute(a, 'outer', [(o, o ^ r) for o in range(n_out)])]
    ppermute x1, starting transfers between devices: 2.09 us -> 3.18 us  [send(): lax.ppermute(parts[0], 'inner', along_inner(low(r), 0))]
    ppermute x4, starting transfers between devices: 4.89 us -> 5.79 us  [send(): lax.ppermute(parts[x], 'inner', along_inner(r, x))]
    ppermute x4, waiting for transfers between devices: 4.43 us -> 3.57 us  [send(): lax.ppermute(parts[x], 'inner', along_inner(r, x))]
    ppermute x3, waiting for transfers between devices: 1.69 us -> 0.96 us  [shards(): q_by[r] = lax.ppermute(q_piece, 'inner', along_inner(r, 0))]
    ppermute x4 -> x5, starting transfers between devices: 7.91 us -> 7.25 us  [over(): return lax.ppermute(a, 'outer', [(o, o ^ r) for o in range(n_out)])]
  transfers between devices with their start and end apart: 17 -> 18, of which waited for: 5 -> 3; matrix products, arithmetic and copies ran while one was open for 3% -> 3% of each run, Pallas kernels for 12% -> 12%
where the time goes in v16:
time: 38.8 us; the launch traced here: 38.6 us
  starting transfers between devices  25.6 us (66%)
  Pallas kernels  6.14 us (16%)
  waiting for transfers between devices  4.93 us (13%)
  other arithmetic  1.06 us (3%)
  between operations  0.81 us (2%)
    ppermute x3, starting transfers between devices, shards(): q_by[r] = lax.ppermute(q_piece, 'inner', along_inner(r, 0))  8.01 us
    ppermute x5, starting transfers between devices, over(): return lax.ppermute(a, 'outer', [(o, o ^ r) for o in range(n_out)])  7.25 us
    ppermute x4, starting transfers between devices, send(): lax.ppermute(parts[x], 'inner', along_inner(r, x))  5.79 us
    ppermute x4, waiting for transfers between devices, send(): lax.ppermute(parts[x], 'inner', along_inner(r, x))  3.57 us
    ppermute x1, starting transfers between devices, send(): lax.ppermute(parts[0], 'inner', along_inner(low(r), 0))  3.18 us
    pallas_call x4, Pallas kernels, score(): pl.pallas_call(functools.partial(score_kernel, r == 0), out_shape=(jax.Sh...  3.02 us
    pallas_call x4, Pallas kernels, apply(): pl.pallas_call(functools.partial(apply_kernel, wide, rows), out_shape=sha...  1.36 us
    concatenate x1, other arithmetic, shards(): own = jnp.concatenate([queries, keys, values], axis=0)  1.06 us
  transfers between devices with their start and end apart: 18, of which 3 were waited for; matrix products, arithmetic and copies ran while one was open for 3% of the time, Pallas kernels for 12%

profile of v16, /device:TPU:0, one launch (start us, length us, event | category | flops | bytes accessed | tf_op | source)
XLA Modules:
  0.0 38.6 jit_solution(7355927995412512292)
XLA Ops:
  0.0 0.5 %collective-permute-start.1 = (bf16[128,512]{1,0:T(8,128)(2,1)}, bf16[128,512]{1,0:T(8,128)(2,1)S(1)}, u32[]{:S(2)}, u32[]{:S(2)}) collective-permute-start(bf16[128,512]{1,0:T(8,128)(2,1)} %param.4), channel_id=1, source_target_pairs={{0,1},{1,0},{2,3},{3,2},{4,5},{5,4},{6,7},{7,6},{8,9},{9,8},{10,11... | collective-permute-start | bytes 393224 | tf_op jit(solution)/shard_map/swap/ppermute | solution.py:186
  0.5 0.1 collective-permute-start.2
  0.5 0.5 %collective-permute-start.3 = (bf16[128,512]{1,0:T(8,128)(2,1)}, bf16[128,512]{1,0:T(8,128)(2,1)S(1)}, u32[]{:S(2)}, u32[]{:S(2)}) collective-permute-start(bf16[128,512]{1,0:T(8,128)(2,1)} %param.6), channel_id=1, source_target_pairs={{0,1},{1,0},{2,3},{3,2},{4,5},{5,4},{6,7},{7,6},{8,9},{9,8},{10,11... | collective-permute-start | bytes 393224 | tf_op jit(solution)/shard_map/swap/ppermute | solution.py:186
  1.0 0.1 collective-permute-start
  1.7 1.1 %pad_maximum_fusion.own = bf16[384,512]{1,0:T(8,128)(2,1)S(1)} fusion(bf16[128,512]{1,0:T(8,128)(2,1)} %param.6, bf16[128,512]{1,0:T(8,128)(2,1)} %param.5, bf16[128,512]{1,0:T(8,128)(2,1)} %param.4), kind=kLoop, calls=%fused_computation | loop fusion | flops 1179648 | bytes 786432 | tf_op jit(solution)/shard_map/swap/concatenate | solution.py:187
  2.7 0.0 collective-permute-done.p1
  2.7 0.0 collective-permute-done.1.q1
  2.8 0.0 collective-permute-done.2.k1
  2.8 0.0 collective-permute-done.3.v1
  2.8 0.8 %merge.1 = (bf16[528,128]{1,0:T(8,128)(2,1)S(1)}, bf16[1040,128]{1,0:T(8,128)(2,1)S(1)}) custom-call(s32[1]{0:T(128)S(6)} %copy.5.p0, s32[1]{0:T(128)} %collective-permute-done.p1, bf16[384,512]{1,0:T(8,128)(2,1)S(1)} %pad_maximum_fusion.own, bf16[128,512]{1,0:T(8,128)(2,1)S(1)} %collective-permute-done.1.q1, ...), custom_call_target="tpu_custom_call" | custom-call | tf_op jit(solution)/shard_map/merge/merge/pallas_call | solution.py:190
  3.6 3.0 %collective-permute-start.7 = (bf16[1040,128]{1,0:T(8,128)(2,1)S(1)}, bf16[1040,128]{1,0:T(8,128)(2,1)S(1)}, u32[]{:S(2)}, u32[]{:S(2)}) collective-permute-start(bf16[1040,128]{1,0:T(8,128)(2,1)S(1)} %get-tuple-element.27.refs_0_), channel_id=1, source_target_pairs={{0,16},{8,24},{16,0},{24,8},{1,17},{9,25},{17,1},{25,9},{2,18},{10... | collective-permute-start | bytes 798728 | tf_op jit(solution)/shard_map/exchange/ppermute | solution.py:214
  6.7 1.6 %collective-permute-start.6 = (bf16[528,128]{1,0:T(8,128)(2,1)S(1)}, bf16[528,128]{1,0:T(8,128)(2,1)S(1)}, u32[]{:S(2)}, u32[]{:S(2)}) collective-permute-start(bf16[528,128]{1,0:T(8,128)(2,1)S(1)} %slice.9), channel_id=1, source_target_pairs={{0,8},{8,0},{16,24},{24,16},{1,9},{9,1},{17,25},{25,17},{2,10},{10... | collective-permute-start | bytes 405512 | tf_op jit(solution)/shard_map/exchange/ppermute | solution.py:214
  8.2 1.6 %collective-permute-start.8 = (bf16[528,128]{1,0:T(8,128)(2,1)S(1)}, bf16[528,128]{1,0:T(8,128)(2,1)S(1)}, u32[]{:S(2)}, u32[]{:S(2)}) collective-permute-start(bf16[528,128]{1,0:T(8,128)(2,1)S(1)} %get-tuple-element.35.q_ref), channel_id=1, source_target_pairs={{0,2},{1,3},{2,0},{3,1},{4,6},{5,7},{6,4},{7,5},{8,10},{9,11},{10,... | collective-permute-start | bytes 405512 | tf_op jit(solution)/shard_map/exchange/ppermute | solution.py:224
  9.8 2.5 %collective-permute-start.5 = (bf16[528,128]{1,0:T(8,128)(2,1)S(1)}, bf16[528,128]{1,0:T(8,128)(2,1)S(1)}, u32[]{:S(2)}, u32[]{:S(2)}) collective-permute-start(bf16[528,128]{1,0:T(8,128)(2,1)S(1)} %get-tuple-element.35.q_ref), channel_id=1, source_target_pairs={{0,6},{1,7},{2,4},{3,5},{4,2},{5,3},{6,0},{7,1},{8,14},{9,15},{10,... | collective-permute-start | bytes 405512 | tf_op jit(solution)/shard_map/exchange/ppermute | solution.py:224
  12.3 0.0 collective-permute-done.6.refs_1_
  12.3 1.0 %collective-permute-done.8.q_ref = bf16[528,128]{1,0:T(8,128)(2,1)S(1)} collective-permute-done((bf16[528,128]{1,0:T(8,128)(2,1)S(1)}, bf16[528,128]{1,0:T(8,128)(2,1)S(1)}, u32[]{:S(2)}, u32[]{:S(2)}) %collective-permute-start.8) | collective-permute-done | bytes 135200 | tf_op jit(solution)/shard_map/exchange/ppermute | solution.py:224
  13.2 0.5 %collective-permute-start.9 = (bf16[528,128]{1,0:T(8,128)(2,1)S(1)}, bf16[528,128]{1,0:T(8,128)(2,1)S(1)}, u32[]{:S(2)}, u32[]{:S(2)}) collective-permute-start(bf16[528,128]{1,0:T(8,128)(2,1)S(1)} %collective-permute-done.6.refs_1_), channel_id=1, source_target_pairs={{0,16},{8,24},{16,0},{24,8},{1,17},{9,25},{17,1},{25,9},{2,18},{10... | collective-permute-start | bytes 405512 | tf_op jit(solution)/shard_map/exchange/ppermute | solution.py:214
  13.8 0.5 %collective-permute-start.10 = (bf16[512,128]{1,0:T(8,128)(2,1)S(1)}, bf16[512,128]{1,0:T(8,128)(2,1)S(1)}, u32[]{:S(2)}, u32[]{:S(2)}) collective-permute-start(bf16[512,128]{1,0:T(8,128)(2,1)S(1)} %slice.10), channel_id=1, source_target_pairs={{0,8},{8,0},{16,24},{24,16},{1,9},{9,1},{17,25},{25,17},{2,10},{10... | collective-permute-start | bytes 393224 | tf_op jit(solution)/shard_map/exchange/ppermute | solution.py:214
  14.3 0.0 collective-permute-done.7.refs_2_
  14.3 1.6 %collective-permute-start.11 = (bf16[512,128]{1,0:T(8,128)(2,1)S(1)}, bf16[512,128]{1,0:T(8,128)(2,1)S(1)}, u32[]{:S(2)}, u32[]{:S(2)}) collective-permute-start(bf16[512,128]{1,0:T(8,128)(2,1)S(1)} %slice.12), channel_id=1, source_target_pairs={{0,8},{8,0},{16,24},{24,16},{1,9},{9,1},{17,25},{25,17},{2,10},{10... | collective-permute-start | bytes 393224 | tf_op jit(solution)/shard_map/exchange/ppermute | solution.py:214
  15.9 4.0 %collective-permute-start.4 = (bf16[528,128]{1,0:T(8,128)(2,1)S(1)}, bf16[528,128]{1,0:T(8,128)(2,1)S(1)}, u32[]{:S(2)}, u32[]{:S(2)}) collective-permute-start(bf16[528,128]{1,0:T(8,128)(2,1)S(1)} %get-tuple-element.35.q_ref), channel_id=1, source_target_pairs={{0,4},{1,5},{2,6},{3,7},{4,0},{5,1},{6,2},{7,3},{8,12},{9,13},{10,... | collective-permute-start | bytes 405512 | tf_op jit(solution)/shard_map/exchange/ppermute | solution.py:224
  19.9 0.0 collective-permute-done.5.q_ref
  19.9 0.0 collective-permute-done.9.refs_3_
  19.9 0.8 %score.4 = (bf16[2,1024,256]{2,1,0:T(8,128)(2,1)S(1)}, f32[16,256]{1,0:T(8,128)S(1)}) custom-call(bf16[528,128]{1,0:T(8,128)(2,1)S(1)} %collective-permute-done.5.q_ref, bf16[1040,128]{1,0:T(8,128)(2,1)S(1)} %get-tuple-element.27.refs_0_, bf16[528,128]{1,0:T(8,128)(2,1)S(1)} %collective-permute-done.6.refs_1_, ...), custom_call_target="tpu_custom_call" | custom-call | flops 134217728 | bytes 1048576 | tf_op jit(solution)/shard_map/score/score/pallas_call | solution.py:242
  20.7 0.0 collective-permute-done.10.refs_1_
  20.7 0.0 collective-permute-done.11.refs_3_
  20.7 0.3 apply.4
  21.0 3.2 %collective-permute-start.12 = (bf16[544,128]{1,0:T(8,128)(2,1)S(1)}, bf16[544,128]{1,0:T(8,128)(2,1)S(1)}, u32[]{:S(2)}, u32[]{:S(2)}) collective-permute-start(bf16[544,128]{1,0:T(8,128)(2,1)S(1)} %apply.4), channel_id=1, source_target_pairs={{0,2},{1,3},{2,0},{3,1},{4,6},{5,7},{6,4},{7,5},{8,10},{9,11},{10,... | collective-permute-start | bytes 417800 | tf_op jit(solution)/shard_map/return/ppermute | solution.py:286
  24.2 0.0 collective-permute-done.4.q_ref
  24.2 0.8 %score.5 = (bf16[2,1024,256]{2,1,0:T(8,128)(2,1)S(1)}, f32[16,256]{1,0:T(8,128)S(1)}) custom-call(bf16[528,128]{1,0:T(8,128)(2,1)S(1)} %collective-permute-done.4.q_ref, bf16[1040,128]{1,0:T(8,128)(2,1)S(1)} %get-tuple-element.27.refs_0_, bf16[528,128]{1,0:T(8,128)(2,1)S(1)} %collective-permute-done.6.refs_1_, ...), custom_call_target="tpu_custom_call" | custom-call | flops 134217728 | bytes 1048576 | tf_op jit(solution)/shard_map/score/score/pallas_call | solution.py:242
  25.0 0.3 apply.5.refs_0_
  25.3 0.8 %score.7 = (bf16[2,1024,256]{2,1,0:T(8,128)(2,1)S(1)}, f32[16,256]{1,0:T(8,128)S(1)}) custom-call(bf16[528,128]{1,0:T(8,128)(2,1)S(1)} %collective-permute-done.8.q_ref, bf16[1040,128]{1,0:T(8,128)(2,1)S(1)} %get-tuple-element.27.refs_0_, bf16[528,128]{1,0:T(8,128)(2,1)S(1)} %collective-permute-done.6.refs_1_, ...), custom_call_target="tpu_custom_call" | custom-call | flops 134217728 | bytes 1048576 | tf_op jit(solution)/shard_map/score/score/pallas_call | solution.py:242
  26.1 0.3 apply.7
  26.4 1.9 %collective-permute-start.16 = (bf16[272,128]{1,0:T(8,128)(2,1)S(1)}, bf16[272,128]{1,0:T(8,128)(2,1)S(1)}, u32[]{:S(2)}, u32[]{:S(2)}) collective-permute-start(bf16[272,128]{1,0:T(8,128)(2,1)S(1)} %get-tuple-element.44), channel_id=1, source_target_pairs={{0,2},{1,3},{2,0},{3,1},{4,6},{5,7},{6,4},{7,5},{8,10},{9,11},{10,... | collective-permute-start | bytes 208904 | tf_op jit(solution)/shard_map/return/ppermute | solution.py:284
  28.3 0.4 collective-permute-done.12.refs_1_
  28.7 0.1 add.1
  28.7 2.6 %collective-permute-start.14 = (bf16[272,128]{1,0:T(8,128)(2,1)S(1)}, bf16[272,128]{1,0:T(8,128)(2,1)S(1)}, u32[]{:S(2)}, u32[]{:S(2)}) collective-permute-start(bf16[272,128]{1,0:T(8,128)(2,1)S(1)} %get-tuple-element.34), channel_id=1, source_target_pairs={{0,4},{1,5},{2,6},{3,7},{4,0},{5,1},{6,2},{7,3},{8,12},{9,13},{10,... | collective-permute-start | bytes 208904 | tf_op jit(solution)/shard_map/return/ppermute | solution.py:284
  31.4 0.0 collective-permute-start.15
  31.4 1.3 %collective-permute-start.17 = (bf16[272,128]{1,0:T(8,128)(2,1)S(1)}, bf16[272,128]{1,0:T(8,128)(2,1)S(1)}, u32[]{:S(2)}, u32[]{:S(2)}) collective-permute-start(bf16[272,128]{1,0:T(8,128)(2,1)S(1)} %get-tuple-element.46), channel_id=1, source_target_pairs={{0,3},{1,2},{2,1},{3,0},{4,7},{5,6},{6,5},{7,4},{8,11},{9,10},{10,... | collective-permute-start | bytes 208904 | tf_op jit(solution)/shard_map/return/ppermute | solution.py:284
  32.7 0.8 %score.6 = (bf16[2,1024,256]{2,1,0:T(8,128)(2,1)S(1)}, f32[16,256]{1,0:T(8,128)S(1)}) custom-call(bf16[528,128]{1,0:T(8,128)(2,1)S(1)} %get-tuple-element.35.q_ref, bf16[1040,128]{1,0:T(8,128)(2,1)S(1)} %get-tuple-element.27.refs_0_, bf16[528,128]{1,0:T(8,128)(2,1)S(1)} %collective-permute-done.6.refs_1_, ...), custom_call_target="tpu_custom_call" | custom-call | flops 134217728 | bytes 1048576 | tf_op jit(solution)/shard_map/score/score/pallas_call | solution.py:242
  33.4 0.3 apply.6
  33.8 0.4 %collective-permute-start.13 = (bf16[272,128]{1,0:T(8,128)(2,1)S(1)}, bf16[272,128]{1,0:T(8,128)(2,1)S(1)}, u32[]{:S(2)}, u32[]{:S(2)}) collective-permute-start(bf16[272,128]{1,0:T(8,128)(2,1)S(1)} %get-tuple-element.39), channel_id=1, source_target_pairs={{0,1},{1,0},{2,3},{3,2},{4,5},{5,4},{6,7},{7,6},{8,9},{9,8},{10,11... | collective-permute-start | bytes 208904 | tf_op jit(solution)/shard_map/return/ppermute | solution.py:307
  34.2 0.0 collective-permute-done.16.refs_4_
  34.2 3.6 %collective-permute-done.15.refs_3_ = bf16[272,128]{1,0:T(8,128)(2,1)S(1)} collective-permute-done((bf16[272,128]{1,0:T(8,128)(2,1)S(1)}, bf16[272,128]{1,0:T(8,128)(2,1)S(1)}, u32[]{:S(2)}, u32[]{:S(2)}) %collective-permute-start.15) | collective-permute-done | bytes 69664 | tf_op jit(solution)/shard_map/return/ppermute | solution.py:284
  37.7 0.0 collective-permute-done.14.refs_2_
  37.8 0.0 collective-permute-done.17.refs_5_
  37.8 0.0 collective-permute-done.13.refs_1_
  37.8 0.8 %combine.1 = bf16[128,512]{1,0:T(8,128)(2,1)} custom-call(bf16[272,128]{1,0:T(8,128)(2,1)S(1)} %get-tuple-element.38.refs_0_, bf16[272,128]{1,0:T(8,128)(2,1)S(1)} %collective-permute-done.13.refs_1_, bf16[272,128]{1,0:T(8,128)(2,1)S(1)} %collective-permute-done.14.refs_2_, bf16[272,128]{1,0:T(8,128)(2,1)S(1)} %collective-permute-done.15.refs_3_, ...), custom_call_target="tpu_custom_call" | custom-call | tf_op jit(solution)/shard_map/combine/combine/pallas_call | solution.py:309
  (3 shorter events, 0.0 us)
Async XLA Ops:
  0.0 2.7 %collective-permute-start.1 = (bf16[128,512]{1,0:T(8,128)(2,1)}, bf16[128,512]{1,0:T(8,128)(2,1)S(1)}, u32[]{:S(2)}, u32[]{:S(2)}) collective-permute-start(bf16[128,512]{1,0:T(8,128)(2,1)} %param.4), channel_id=1, source_target_pairs={{0,1},{1,0},{2,3},{3,2},{4,5},{5,4},{6,7},{7,6},{8,9},{9,8},{10,11... | collective-permute-start | bytes 393224 | tf_op jit(solution)/shard_map/swap/ppermute | solution.py:186
  0.5 2.3 %collective-permute-start.2 = (bf16[128,512]{1,0:T(8,128)(2,1)}, bf16[128,512]{1,0:T(8,128)(2,1)S(1)}, u32[]{:S(2)}, u32[]{:S(2)}) collective-permute-start(bf16[128,512]{1,0:T(8,128)(2,1)} %param.5), channel_id=1, source_target_pairs={{0,1},{1,0},{2,3},{3,2},{4,5},{5,4},{6,7},{7,6},{8,9},{9,8},{10,11... | collective-permute-start | bytes 393224 | tf_op jit(solution)/shard_map/swap/ppermute | solution.py:186
  0.5 2.3 %collective-permute-start.3 = (bf16[128,512]{1,0:T(8,128)(2,1)}, bf16[128,512]{1,0:T(8,128)(2,1)S(1)}, u32[]{:S(2)}, u32[]{:S(2)}) collective-permute-start(bf16[128,512]{1,0:T(8,128)(2,1)} %param.6), channel_id=1, source_target_pairs={{0,1},{1,0},{2,3},{3,2},{4,5},{5,4},{6,7},{7,6},{8,9},{9,8},{10,11... | collective-permute-start | bytes 393224 | tf_op jit(solution)/shard_map/swap/ppermute | solution.py:186
  1.0 1.8 %collective-permute-start = (s32[1]{0:T(128)}, s32[1]{0:T(128)}, u32[]{:S(2)}, u32[]{:S(2)}) collective-permute-start(s32[1]{0:T(128)} %param.7), channel_id=1, source_target_pairs={{0,1},{1,0},{2,3},{3,2},{4,5},{5,4},{6,7},{7,6},{8,9},{9,8},{10,11... | collective-permute-start | bytes 20 | tf_op jit(solution)/shard_map/swap/ppermute | solution.py:186
  3.6 10.7 %collective-permute-start.7 = (bf16[1040,128]{1,0:T(8,128)(2,1)S(1)}, bf16[1040,128]{1,0:T(8,128)(2,1)S(1)}, u32[]{:S(2)}, u32[]{:S(2)}) collective-permute-start(bf16[1040,128]{1,0:T(8,128)(2,1)S(1)} %get-tuple-element.27.refs_0_), channel_id=1, source_target_pairs={{0,16},{8,24},{16,0},{24,8},{1,17},{9,25},{17,1},{25,9},{2,18},{10... | collective-permute-start | bytes 798728 | tf_op jit(solution)/shard_map/exchange/ppermute | solution.py:214
  6.7 5.6 %collective-permute-start.6 = (bf16[528,128]{1,0:T(8,128)(2,1)S(1)}, bf16[528,128]{1,0:T(8,128)(2,1)S(1)}, u32[]{:S(2)}, u32[]{:S(2)}) collective-permute-start(bf16[528,128]{1,0:T(8,128)(2,1)S(1)} %slice.9), channel_id=1, source_target_pairs={{0,8},{8,0},{16,24},{24,16},{1,9},{9,1},{17,25},{25,17},{2,10},{10... | collective-permute-start | bytes 405512 | tf_op jit(solution)/shard_map/exchange/ppermute | solution.py:214
  8.2 5.0 %collective-permute-start.8 = (bf16[528,128]{1,0:T(8,128)(2,1)S(1)}, bf16[528,128]{1,0:T(8,128)(2,1)S(1)}, u32[]{:S(2)}, u32[]{:S(2)}) collective-permute-start(bf16[528,128]{1,0:T(8,128)(2,1)S(1)} %get-tuple-element.35.q_ref), channel_id=1, source_target_pairs={{0,2},{1,3},{2,0},{3,1},{4,6},{5,7},{6,4},{7,5},{8,10},{9,11},{10,... | collective-permute-start | bytes 405512 | tf_op jit(solution)/shard_map/exchange/ppermute | solution.py:224
  9.8 10.1 %collective-permute-start.5 = (bf16[528,128]{1,0:T(8,128)(2,1)S(1)}, bf16[528,128]{1,0:T(8,128)(2,1)S(1)}, u32[]{:S(2)}, u32[]{:S(2)}) collective-permute-start(bf16[528,128]{1,0:T(8,128)(2,1)S(1)} %get-tuple-element.35.q_ref), channel_id=1, source_target_pairs={{0,6},{1,7},{2,4},{3,5},{4,2},{5,3},{6,0},{7,1},{8,14},{9,15},{10,... | collective-permute-start | bytes 405512 | tf_op jit(solution)/shard_map/exchange/ppermute | solution.py:224
  13.2 6.7 %collective-permute-start.9 = (bf16[528,128]{1,0:T(8,128)(2,1)S(1)}, bf16[528,128]{1,0:T(8,128)(2,1)S(1)}, u32[]{:S(2)}, u32[]{:S(2)}) collective-permute-start(bf16[528,128]{1,0:T(8,128)(2,1)S(1)} %collective-permute-done.6.refs_1_), channel_id=1, source_target_pairs={{0,16},{8,24},{16,0},{24,8},{1,17},{9,25},{17,1},{25,9},{2,18},{10... | collective-permute-start | bytes 405512 | tf_op jit(solution)/shard_map/exchange/ppermute | solution.py:214
  13.8 6.9 %collective-permute-start.10 = (bf16[512,128]{1,0:T(8,128)(2,1)S(1)}, bf16[512,128]{1,0:T(8,128)(2,1)S(1)}, u32[]{:S(2)}, u32[]{:S(2)}) collective-permute-start(bf16[512,128]{1,0:T(8,128)(2,1)S(1)} %slice.10), channel_id=1, source_target_pairs={{0,8},{8,0},{16,24},{24,16},{1,9},{9,1},{17,25},{25,17},{2,10},{10... | collective-permute-start | bytes 393224 | tf_op jit(solution)/shard_map/exchange/ppermute | solution.py:214
  14.3 6.4 %collective-permute-start.11 = (bf16[512,128]{1,0:T(8,128)(2,1)S(1)}, bf16[512,128]{1,0:T(8,128)(2,1)S(1)}, u32[]{:S(2)}, u32[]{:S(2)}) collective-permute-start(bf16[512,128]{1,0:T(8,128)(2,1)S(1)} %slice.12), channel_id=1, source_target_pairs={{0,8},{8,0},{16,24},{24,16},{1,9},{9,1},{17,25},{25,17},{2,10},{10... | collective-permute-start | bytes 393224 | tf_op jit(solution)/shard_map/exchange/ppermute | solution.py:214
  15.9 8.3 %collective-permute-start.4 = (bf16[528,128]{1,0:T(8,128)(2,1)S(1)}, bf16[528,128]{1,0:T(8,128)(2,1)S(1)}, u32[]{:S(2)}, u32[]{:S(2)}) collective-permute-start(bf16[528,128]{1,0:T(8,128)(2,1)S(1)} %get-tuple-element.35.q_ref), channel_id=1, source_target_pairs={{0,4},{1,5},{2,6},{3,7},{4,0},{5,1},{6,2},{7,3},{8,12},{9,13},{10,... | collective-permute-start | bytes 405512 | tf_op jit(solution)/shard_map/exchange/ppermute | solution.py:224
  21.0 7.6 %collective-permute-start.12 = (bf16[544,128]{1,0:T(8,128)(2,1)S(1)}, bf16[544,128]{1,0:T(8,128)(2,1)S(1)}, u32[]{:S(2)}, u32[]{:S(2)}) collective-permute-start(bf16[544,128]{1,0:T(8,128)(2,1)S(1)} %apply.4), channel_id=1, source_target_pairs={{0,2},{1,3},{2,0},{3,1},{4,6},{5,7},{6,4},{7,5},{8,10},{9,11},{10,... | collective-permute-start | bytes 417800 | tf_op jit(solution)/shard_map/return/ppermute | solution.py:286
  26.4 7.7 %collective-permute-start.16 = (bf16[272,128]{1,0:T(8,128)(2,1)S(1)}, bf16[272,128]{1,0:T(8,128)(2,1)S(1)}, u32[]{:S(2)}, u32[]{:S(2)}) collective-permute-start(bf16[272,128]{1,0:T(8,128)(2,1)S(1)} %get-tuple-element.44), channel_id=1, source_target_pairs={{0,2},{1,3},{2,0},{3,1},{4,6},{5,7},{6,4},{7,5},{8,10},{9,11},{10,... | collective-permute-start | bytes 208904 | tf_op jit(solution)/shard_map/return/ppermute | solution.py:284
  28.7 9.0 %collective-permute-start.14 = (bf16[272,128]{1,0:T(8,128)(2,1)S(1)}, bf16[272,128]{1,0:T(8,128)(2,1)S(1)}, u32[]{:S(2)}, u32[]{:S(2)}) collective-permute-start(bf16[272,128]{1,0:T(8,128)(2,1)S(1)} %get-tuple-element.34), channel_id=1, source_target_pairs={{0,4},{1,5},{2,6},{3,7},{4,0},{5,1},{6,2},{7,3},{8,12},{9,13},{10,... | collective-permute-start | bytes 208904 | tf_op jit(solution)/shard_map/return/ppermute | solution.py:284
  31.4 6.4 %collective-permute-start.15 = (bf16[272,128]{1,0:T(8,128)(2,1)S(1)}, bf16[272,128]{1,0:T(8,128)(2,1)S(1)}, u32[]{:S(2)}, u32[]{:S(2)}) collective-permute-start(bf16[272,128]{1,0:T(8,128)(2,1)S(1)} %get-tuple-element.40), channel_id=1, source_target_pairs={{0,5},{1,4},{2,7},{3,6},{4,1},{5,0},{6,3},{7,2},{8,13},{9,12},{10,... | collective-permute-start | bytes 208904 | tf_op jit(solution)/shard_map/return/ppermute | solution.py:284
  31.4 6.4 %collective-permute-start.17 = (bf16[272,128]{1,0:T(8,128)(2,1)S(1)}, bf16[272,128]{1,0:T(8,128)(2,1)S(1)}, u32[]{:S(2)}, u32[]{:S(2)}) collective-permute-start(bf16[272,128]{1,0:T(8,128)(2,1)S(1)} %get-tuple-element.46), channel_id=1, source_target_pairs={{0,3},{1,2},{2,1},{3,0},{4,7},{5,6},{6,5},{7,4},{8,11},{9,10},{10,... | collective-permute-start | bytes 208904 | tf_op jit(solution)/shard_map/return/ppermute | solution.py:284
  33.8 4.0 %collective-permute-start.13 = (bf16[272,128]{1,0:T(8,128)(2,1)S(1)}, bf16[272,128]{1,0:T(8,128)(2,1)S(1)}, u32[]{:S(2)}, u32[]{:S(2)}) collective-permute-start(bf16[272,128]{1,0:T(8,128)(2,1)S(1)} %get-tuple-element.39), channel_id=1, source_target_pairs={{0,1},{1,0},{2,3},{3,2},{4,5},{5,4},{6,7},{7,6},{8,9},{9,8},{10,11... | collective-permute-start | bytes 208904 | tf_op jit(solution)/shard_map/return/ppermute | solution.py:307

commit v17 on v16

--- a/solution.py
+++ b/solution.py
@@ -85,7 +85,7 @@
         top_ref[h * 8 : (h + 1) * 8, :] = jnp.broadcast_to(top, (8, both))
 
 
-def apply_kernel(wide, rows, p_ref, top_ref, *refs):
+def apply_kernel(wide, row, p_ref, top_ref, *refs):
     nv = len(refs) - (1 if wide else CORES)
     v_refs, out_refs = refs[:nv], refs[nv:]
     size = v_refs[0].shape[1]
@@ -102,7 +102,7 @@
     stats = [[] for _ in range(CORES)]
     for h in range(PER):
         vals = []
-        for ref, row in zip(v_refs, rows):
+        for ref in v_refs:
             for b in range(CORES):
                 at = row + h * both + b * tok
                 vals.append(ref[at : at + tok, :])
@@ -204,32 +204,27 @@
     def low(r):
         return r & -r
 
-    def high(r):
-        return 1 << (r.bit_length() - 1)
-
     def single(r):
         return r == low(r)
 
-    def over(a, r):
-        return lax.ppermute(a, "outer", [(o, o ^ r) for o in range(n_out)])
+    def over(a, step):
+        bits = n_out.bit_length() - 1
+        flip = [1 << (step + c) % bits for c in range(CORES)]
+        pairs = [
+            (o * n_in + w * CORES + c, (o ^ flip[c]) * n_in + w * CORES + c)
+            for o in range(n_out)
+            for w in range(chips)
+            for c in range(CORES)
+        ]
+        return lax.ppermute(a, ("outer", "inner"), pairs)
 
     with jax.named_scope("exchange"):
-        whole = {r: over(kv_piece, r) if r else kv_piece for r in range(n_out) if single(r) and r != 1}
-        k_by = {r: a[:half, :] for r, a in whole.items()}
-        v_by = {r: a[half:, :] for r, a in whole.items()}
-        if n_out > 1:
-            k_by[1], v_by[1] = over(k_by[0], 1), over(v_by[0], 1)
+        kv = [kv_piece]
+        for step in range(n_out.bit_length() - 1):
+            kv += [over(a, step) for a in kv]
         q_by = {0: q_piece}
         for r in reversed(range(1, chips)):
             q_by[r] = lax.ppermute(q_piece, "inner", along_inner(r, 0))
-        for r in sorted(range(1, n_out), key=lambda r: r.bit_count()):
-            if not single(r):
-                k = k_by[r - high(r)]
-                k_by[r] = over(after(k, q_by[1]) if chips > 1 else k, high(r))
-                v_by[r] = over(v_by[r - low(r)], low(r))
-        ks = [whole[r] if r in whole else k_by[r] for r in range(n_out)]
-        vs = [whole[r] if r in whole else v_by[r] for r in range(n_out)]
-        rows = tuple(half if r in whole else 0 for r in range(n_out))
 
     def shapes(wide):
         rows = CORES * block if wide else block
@@ -250,19 +245,19 @@
                 compiler_params=params,
                 cost_estimate=pl.CostEstimate(flops=work, bytes_accessed=2**20, transcendentals=work // (2 * size)),
                 name="score",
-            )(q_by[r] if done is None else after(q_by[r], done), *ks)
+            )(q_by[r] if done is None else after(q_by[r], done), *kv)
 
     def apply(r, wide):
         with jax.named_scope("apply"):
             return pl.pallas_call(
-                functools.partial(apply_kernel, wide, rows),
+                functools.partial(apply_kernel, wide, half),
                 out_shape=shapes(wide),
                 in_specs=vmem(2 + n_out),
                 out_specs=tuple(vmem(len(shapes(wide)))),
                 compiler_params=params,
                 cost_estimate=pl.CostEstimate(flops=work, bytes_accessed=2**20, transcendentals=0),
                 name="apply",
-            )(*weights_by[r], *vs)
+            )(*weights_by[r], *kv)
 
     def add(arrays, wide):
         with jax.named_scope("add"):

time: 38.8 us -> 42.5 us (1.095)
  waiting for transfers between devices: 4.93 us -> 13 us
  starting transfers between devices: 25.6 us -> 21.4 us
    ppermute x5 -> x3, waiting for transfers between devices: 0.01 us -> 5 us  [over(): return lax.ppermute(a, ('outer', 'inner'), pairs)]
    ppermute x3, starting transfers between devices: 8.01 us -> 4.39 us  [shards(): q_by[r] = lax.ppermute(q_piece, 'inner', along_inner(r, 0))]
    ppermute x3, waiting for transfers between devices: 0.96 us -> 3.94 us  [shards(): q_by[r] = lax.ppermute(q_piece, 'inner', along_inner(r, 0))]
    ppermute x1, starting transfers between devices: 3.18 us -> 4.21 us  [send(): lax.ppermute(parts[0], 'inner', along_inner(low(r), 0))]
    ppermute x5 -> x3, starting transfers between devices: 7.25 us -> 6.42 us  [over(): return lax.ppermute(a, ('outer', 'inner'), pairs)]
    ppermute x1, waiting for transfers between devices: 0.37 us -> 1.03 us  [send(): lax.ppermute(parts[0], 'inner', along_inner(low(r), 0))]
    ppermute x4, waiting for transfers between devices: 3.57 us -> 3.04 us  [send(): lax.ppermute(parts[x], 'inner', along_inner(r, x))]
    ppermute x4, starting transfers between devices: 5.79 us -> 5.28 us  [send(): lax.ppermute(parts[x], 'inner', along_inner(r, x))]
  transfers between devices with their start and end apart: 18 -> 16, of which waited for: 3 -> 4; matrix products, arithmetic and copies ran while one was open for 3% -> 3% of each run, Pallas kernels for 12% -> 11%
where the time goes in v17:
time: 42.5 us; the launch traced here: 42.3 us
  starting transfers between devices  21.4 us (50%)
  waiting for transfers between devices  13 us (31%)
  Pallas kernels  6.07 us (14%)
  other arithmetic  1.06 us (2%)
  between operations  0.8 us (2%)
    ppermute x3, starting transfers between devices, over(): return lax.ppermute(a, ('outer', 'inner'), pairs)  6.42 us
    ppermute x4, starting transfers between devices, send(): lax.ppermute(parts[x], 'inner', along_inner(r, x))  5.28 us
    ppermute x3, waiting for transfers between devices, over(): return lax.ppermute(a, ('outer', 'inner'), pairs)  5 us
    ppermute x3, starting transfers between devices, shards(): q_by[r] = lax.ppermute(q_piece, 'inner', along_inner(r, 0))  4.39 us
    ppermute x1, starting transfers between devices, send(): lax.ppermute(parts[0], 'inner', along_inner(low(r), 0))  4.21 us
    ppermute x3, waiting for transfers between devices, shards(): q_by[r] = lax.ppermute(q_piece, 'inner', along_inner(r, 0))  3.94 us
    ppermute x4, waiting for transfers between devices, send(): lax.ppermute(parts[x], 'inner', along_inner(r, x))  3.04 us
    pallas_call x4, Pallas kernels, score(): pl.pallas_call(functools.partial(score_kernel, r == 0), out_shape=(jax.Sh...  3.04 us
  transfers between devices with their start and end apart: 16, of which 4 were waited for; matrix products, arithmetic and copies ran while one was open for 3% of the time, Pallas kernels for 11%

profile of v17, /device:TPU:0, one launch (start us, length us, event | category | flops | bytes accessed | tf_op | source)
XLA Modules:
  0.0 42.3 jit_solution(11899240442637181483)
XLA Ops:
  0.0 0.5 %collective-permute-start.1 = (bf16[128,512]{1,0:T(8,128)(2,1)}, bf16[128,512]{1,0:T(8,128)(2,1)S(1)}, u32[]{:S(2)}, u32[]{:S(2)}) collective-permute-start(bf16[128,512]{1,0:T(8,128)(2,1)} %param.4), channel_id=1, source_target_pairs={{0,1},{1,0},{2,3},{3,2},{4,5},{5,4},{6,7},{7,6},{8,9},{9,8},{10,11... | collective-permute-start | bytes 393224 | tf_op jit(solution)/shard_map/swap/ppermute | solution.py:186
  0.5 0.1 collective-permute-start.2
  0.5 0.5 %collective-permute-start.3 = (bf16[128,512]{1,0:T(8,128)(2,1)}, bf16[128,512]{1,0:T(8,128)(2,1)S(1)}, u32[]{:S(2)}, u32[]{:S(2)}) collective-permute-start(bf16[128,512]{1,0:T(8,128)(2,1)} %param.6), channel_id=1, source_target_pairs={{0,1},{1,0},{2,3},{3,2},{4,5},{5,4},{6,7},{7,6},{8,9},{9,8},{10,11... | collective-permute-start | bytes 393224 | tf_op jit(solution)/shard_map/swap/ppermute | solution.py:186
  1.0 0.1 collective-permute-start
  1.7 1.1 %pad_maximum_fusion.own = bf16[384,512]{1,0:T(8,128)(2,1)S(1)} fusion(bf16[128,512]{1,0:T(8,128)(2,1)} %param.6, bf16[128,512]{1,0:T(8,128)(2,1)} %param.5, bf16[128,512]{1,0:T(8,128)(2,1)} %param.4), kind=kLoop, calls=%fused_computation | loop fusion | flops 1179648 | bytes 786432 | tf_op jit(solution)/shard_map/swap/concatenate | solution.py:187
  2.7 0.0 collective-permute-done.p1
  2.7 0.0 collective-permute-done.1.q1
  2.8 0.0 collective-permute-done.2.k1
  2.8 0.0 collective-permute-done.3.v1
  2.8 0.8 %merge.1 = (bf16[528,128]{1,0:T(8,128)(2,1)S(1)}, bf16[1040,128]{1,0:T(8,128)(2,1)S(1)}) custom-call(s32[1]{0:T(128)S(6)} %copy.5.p0, s32[1]{0:T(128)} %collective-permute-done.p1, bf16[384,512]{1,0:T(8,128)(2,1)S(1)} %pad_maximum_fusion.own, bf16[128,512]{1,0:T(8,128)(2,1)S(1)} %collective-permute-done.1.q1, ...), custom_call_target="tpu_custom_call" | custom-call | tf_op jit(solution)/shard_map/merge/merge/pallas_call | solution.py:190
  3.6 3.0 %collective-permute-start.6 = (bf16[1040,128]{1,0:T(8,128)(2,1)S(1)}, bf16[1040,128]{1,0:T(8,128)(2,1)S(1)}, u32[]{:S(2)}, u32[]{:S(2)}) collective-permute-start(bf16[1040,128]{1,0:T(8,128)(2,1)S(1)} %get-tuple-element.26.refs_0_), channel_id=1, source_target_pairs={{0,8},{1,17},{2,10},{3,19},{4,12},{5,21},{6,14},{7,23},{8,0},{9,25... | collective-permute-start | bytes 798728 | tf_op jit(solution)/shard_map/exchange/ppermute | solution.py:219
  6.6 1.5 %collective-permute-start.7 = (bf16[1040,128]{1,0:T(8,128)(2,1)S(1)}, bf16[1040,128]{1,0:T(8,128)(2,1)S(1)}, u32[]{:S(2)}, u32[]{:S(2)}) collective-permute-start(bf16[1040,128]{1,0:T(8,128)(2,1)S(1)} %get-tuple-element.26.refs_0_), channel_id=1, source_target_pairs={{0,16},{1,9},{2,18},{3,11},{4,20},{5,13},{6,22},{7,15},{8,24},{9,1... | collective-permute-start | bytes 798728 | tf_op jit(solution)/shard_map/exchange/ppermute | solution.py:219
  8.1 5.0 %collective-permute-done.6.refs_1_ = bf16[1040,128]{1,0:T(8,128)(2,1)S(1)} collective-permute-done((bf16[1040,128]{1,0:T(8,128)(2,1)S(1)}, bf16[1040,128]{1,0:T(8,128)(2,1)S(1)}, u32[]{:S(2)}, u32[]{:S(2)}) %collective-permute-start.6) | collective-permute-done | bytes 266272 | tf_op jit(solution)/shard_map/exchange/ppermute | solution.py:219
  13.1 1.9 %collective-permute-start.8 = (bf16[1040,128]{1,0:T(8,128)(2,1)S(1)}, bf16[1040,128]{1,0:T(8,128)(2,1)S(1)}, u32[]{:S(2)}, u32[]{:S(2)}) collective-permute-start(bf16[1040,128]{1,0:T(8,128)(2,1)S(1)} %collective-permute-done.6.refs_1_), channel_id=1, source_target_pairs={{0,16},{1,9},{2,18},{3,11},{4,20},{5,13},{6,22},{7,15},{8,24},{9,1... | collective-permute-start | bytes 798728 | tf_op jit(solution)/shard_map/exchange/ppermute | solution.py:219
  15.0 3.7 %collective-permute-start.5 = (bf16[528,128]{1,0:T(8,128)(2,1)S(1)}, bf16[528,128]{1,0:T(8,128)(2,1)S(1)}, u32[]{:S(2)}, u32[]{:S(2)}) collective-permute-start(bf16[528,128]{1,0:T(8,128)(2,1)S(1)} %get-tuple-element.33.q_ref), channel_id=1, source_target_pairs={{0,6},{1,7},{2,4},{3,5},{4,2},{5,3},{6,0},{7,1},{8,14},{9,15},{10,... | collective-permute-start | bytes 405512 | tf_op jit(solution)/shard_map/exchange/ppermute | solution.py:227
  18.7 0.0 collective-permute-start.4
  18.7 0.6 %collective-permute-start.13 = (bf16[528,128]{1,0:T(8,128)(2,1)S(1)}, bf16[528,128]{1,0:T(8,128)(2,1)S(1)}, u32[]{:S(2)}, u32[]{:S(2)}) collective-permute-start(bf16[528,128]{1,0:T(8,128)(2,1)S(1)} %get-tuple-element.33.q_ref), channel_id=1, source_target_pairs={{0,2},{1,3},{2,0},{3,1},{4,6},{5,7},{6,4},{7,5},{8,10},{9,11},{10,... | collective-permute-start | bytes 405512 | tf_op jit(solution)/shard_map/exchange/ppermute | solution.py:227
  19.4 3.9 %collective-permute-done.5.q_ref = bf16[528,128]{1,0:T(8,128)(2,1)S(1)} collective-permute-done((bf16[528,128]{1,0:T(8,128)(2,1)S(1)}, bf16[528,128]{1,0:T(8,128)(2,1)S(1)}, u32[]{:S(2)}, u32[]{:S(2)}) %collective-permute-start.5) | collective-permute-done | bytes 135200 | tf_op jit(solution)/shard_map/exchange/ppermute | solution.py:227
  23.3 0.0 collective-permute-done.7.refs_2_
  23.3 0.0 collective-permute-done.8.refs_3_
  23.3 0.8 %score.4 = (bf16[2,1024,256]{2,1,0:T(8,128)(2,1)S(1)}, f32[16,256]{1,0:T(8,128)S(1)}) custom-call(bf16[528,128]{1,0:T(8,128)(2,1)S(1)} %collective-permute-done.5.q_ref, bf16[1040,128]{1,0:T(8,128)(2,1)S(1)} %get-tuple-element.26.refs_0_, bf16[1040,128]{1,0:T(8,128)(2,1)S(1)} %collective-permute-done.6.refs_1_, ...), custom_call_target="tpu_custom_call" | custom-call | flops 134217728 | bytes 1048576 | tf_op jit(solution)/shard_map/score/score/pallas_call | solution.py:237
  24.1 0.3 apply.4
  24.4 4.2 %collective-permute-start.9 = (bf16[544,128]{1,0:T(8,128)(2,1)S(1)}, bf16[544,128]{1,0:T(8,128)(2,1)S(1)}, u32[]{:S(2)}, u32[]{:S(2)}) collective-permute-start(bf16[544,128]{1,0:T(8,128)(2,1)S(1)} %apply.4), channel_id=1, source_target_pairs={{0,2},{1,3},{2,0},{3,1},{4,6},{5,7},{6,4},{7,5},{8,10},{9,11},{10,... | collective-permute-start | bytes 417800 | tf_op jit(solution)/shard_map/return/ppermute | solution.py:281
  28.6 0.0 collective-permute-done.4.q_ref
  28.6 0.8 %score.5 = (bf16[2,1024,256]{2,1,0:T(8,128)(2,1)S(1)}, f32[16,256]{1,0:T(8,128)S(1)}) custom-call(bf16[528,128]{1,0:T(8,128)(2,1)S(1)} %collective-permute-done.4.q_ref, bf16[1040,128]{1,0:T(8,128)(2,1)S(1)} %get-tuple-element.26.refs_0_, bf16[1040,128]{1,0:T(8,128)(2,1)S(1)} %collective-permute-done.6.refs_1_, ...), custom_call_target="tpu_custom_call" | custom-call | flops 134217728 | bytes 1048576 | tf_op jit(solution)/shard_map/score/score/pallas_call | solution.py:237
  29.4 0.3 apply.5.refs_0_
  29.7 0.0 collective-permute-done.13.q_ref
  29.7 0.8 %score.7 = (bf16[2,1024,256]{2,1,0:T(8,128)(2,1)S(1)}, f32[16,256]{1,0:T(8,128)S(1)}) custom-call(bf16[528,128]{1,0:T(8,128)(2,1)S(1)} %collective-permute-done.13.q_ref, bf16[1040,128]{1,0:T(8,128)(2,1)S(1)} %get-tuple-element.26.refs_0_, bf16[1040,128]{1,0:T(8,128)(2,1)S(1)} %collective-permute-done.6.refs_1_, ...), custom_call_target="tpu_custom_call" | custom-call | flops 134217728 | bytes 1048576 | tf_op jit(solution)/shard_map/score/score/pallas_call | solution.py:237
  30.5 0.3 apply.7
  30.9 0.1 collective-permute-start.14
  30.9 1.0 %collective-permute-done.9.refs_1_ = bf16[544,128]{1,0:T(8,128)(2,1)S(1)} collective-permute-done((bf16[544,128]{1,0:T(8,128)(2,1)S(1)}, bf16[544,128]{1,0:T(8,128)(2,1)S(1)}, u32[]{:S(2)}, u32[]{:S(2)}) %collective-permute-start.9) | collective-permute-done | bytes 139296 | tf_op jit(solution)/shard_map/return/ppermute | solution.py:281
  32.0 0.1 add.1
  32.1 3.1 %collective-permute-start.11 = (bf16[272,128]{1,0:T(8,128)(2,1)S(1)}, bf16[272,128]{1,0:T(8,128)(2,1)S(1)}, u32[]{:S(2)}, u32[]{:S(2)}) collective-permute-start(bf16[272,128]{1,0:T(8,128)(2,1)S(1)} %get-tuple-element.32), channel_id=1, source_target_pairs={{0,4},{1,5},{2,6},{3,7},{4,0},{5,1},{6,2},{7,3},{8,12},{9,13},{10,... | collective-permute-start | bytes 208904 | tf_op jit(solution)/shard_map/return/ppermute | solution.py:279
  35.2 0.0 collective-permute-start.12
  35.2 2.0 %collective-permute-start.15 = (bf16[272,128]{1,0:T(8,128)(2,1)S(1)}, bf16[272,128]{1,0:T(8,128)(2,1)S(1)}, u32[]{:S(2)}, u32[]{:S(2)}) collective-permute-start(bf16[272,128]{1,0:T(8,128)(2,1)S(1)} %get-tuple-element.44), channel_id=1, source_target_pairs={{0,3},{1,2},{2,1},{3,0},{4,7},{5,6},{6,5},{7,4},{8,11},{9,10},{10,... | collective-permute-start | bytes 208904 | tf_op jit(solution)/shard_map/return/ppermute | solution.py:279
  37.2 0.8 %score.6 = (bf16[2,1024,256]{2,1,0:T(8,128)(2,1)S(1)}, f32[16,256]{1,0:T(8,128)S(1)}) custom-call(bf16[528,128]{1,0:T(8,128)(2,1)S(1)} %get-tuple-element.33.q_ref, bf16[1040,128]{1,0:T(8,128)(2,1)S(1)} %get-tuple-element.26.refs_0_, bf16[1040,128]{1,0:T(8,128)(2,1)S(1)} %collective-permute-done.6.refs_1_, ...), custom_call_target="tpu_custom_call" | custom-call | flops 134217728 | bytes 1048576 | tf_op jit(solution)/shard_map/score/score/pallas_call | solution.py:237
  38.0 0.3 apply.6
  38.4 0.1 collective-permute-start.10
  38.4 0.0 collective-permute-done.14.refs_4_
  38.5 3.0 %collective-permute-done.12.refs_3_ = bf16[272,128]{1,0:T(8,128)(2,1)S(1)} collective-permute-done((bf16[272,128]{1,0:T(8,128)(2,1)S(1)}, bf16[272,128]{1,0:T(8,128)(2,1)S(1)}, u32[]{:S(2)}, u32[]{:S(2)}) %collective-permute-start.12) | collective-permute-done | bytes 69664 | tf_op jit(solution)/shard_map/return/ppermute | solution.py:279
  41.5 0.0 collective-permute-done.11.refs_2_
  41.5 0.0 collective-permute-done.15.refs_5_
  41.5 0.0 collective-permute-done.10.refs_1_
  41.5 0.8 %combine.1 = bf16[128,512]{1,0:T(8,128)(2,1)} custom-call(bf16[272,128]{1,0:T(8,128)(2,1)S(1)} %get-tuple-element.36.refs_0_, bf16[272,128]{1,0:T(8,128)(2,1)S(1)} %collective-permute-done.10.refs_1_, bf16[272,128]{1,0:T(8,128)(2,1)S(1)} %collective-permute-done.11.refs_2_, bf16[272,128]{1,0:T(8,128)(2,1)S(1)} %collective-permute-done.12.refs_3_, ...), custom_call_target="tpu_custom_call" | custom-call | tf_op jit(solution)/shard_map/combine/combine/pallas_call | solution.py:304
Async XLA Ops:
  0.0 2.7 %collective-permute-start.1 = (bf16[128,512]{1,0:T(8,128)(2,1)}, bf16[128,512]{1,0:T(8,128)(2,1)S(1)}, u32[]{:S(2)}, u32[]{:S(2)}) collective-permute-start(bf16[128,512]{1,0:T(8,128)(2,1)} %param.4), channel_id=1, source_target_pairs={{0,1},{1,0},{2,3},{3,2},{4,5},{5,4},{6,7},{7,6},{8,9},{9,8},{10,11... | collective-permute-start | bytes 393224 | tf_op jit(solution)/shard_map/swap/ppermute | solution.py:186
  0.5 2.3 %collective-permute-start.2 = (bf16[128,512]{1,0:T(8,128)(2,1)}, bf16[128,512]{1,0:T(8,128)(2,1)S(1)}, u32[]{:S(2)}, u32[]{:S(2)}) collective-permute-start(bf16[128,512]{1,0:T(8,128)(2,1)} %param.5), channel_id=1, source_target_pairs={{0,1},{1,0},{2,3},{3,2},{4,5},{5,4},{6,7},{7,6},{8,9},{9,8},{10,11... | collective-permute-start | bytes 393224 | tf_op jit(solution)/shard_map/swap/ppermute | solution.py:186
  0.5 2.3 %collective-permute-start.3 = (bf16[128,512]{1,0:T(8,128)(2,1)}, bf16[128,512]{1,0:T(8,128)(2,1)S(1)}, u32[]{:S(2)}, u32[]{:S(2)}) collective-permute-start(bf16[128,512]{1,0:T(8,128)(2,1)} %param.6), channel_id=1, source_target_pairs={{0,1},{1,0},{2,3},{3,2},{4,5},{5,4},{6,7},{7,6},{8,9},{9,8},{10,11... | collective-permute-start | bytes 393224 | tf_op jit(solution)/shard_map/swap/ppermute | solution.py:186
  1.0 1.8 %collective-permute-start = (s32[1]{0:T(128)}, s32[1]{0:T(128)}, u32[]{:S(2)}, u32[]{:S(2)}) collective-permute-start(s32[1]{0:T(128)} %param.7), channel_id=1, source_target_pairs={{0,1},{1,0},{2,3},{3,2},{4,5},{5,4},{6,7},{7,6},{8,9},{9,8},{10,11... | collective-permute-start | bytes 20 | tf_op jit(solution)/shard_map/swap/ppermute | solution.py:186
  3.6 9.5 %collective-permute-start.6 = (bf16[1040,128]{1,0:T(8,128)(2,1)S(1)}, bf16[1040,128]{1,0:T(8,128)(2,1)S(1)}, u32[]{:S(2)}, u32[]{:S(2)}) collective-permute-start(bf16[1040,128]{1,0:T(8,128)(2,1)S(1)} %get-tuple-element.26.refs_0_), channel_id=1, source_target_pairs={{0,8},{1,17},{2,10},{3,19},{4,12},{5,21},{6,14},{7,23},{8,0},{9,25... | collective-permute-start | bytes 798728 | tf_op jit(solution)/shard_map/exchange/ppermute | solution.py:219
  6.6 16.7 %collective-permute-start.7 = (bf16[1040,128]{1,0:T(8,128)(2,1)S(1)}, bf16[1040,128]{1,0:T(8,128)(2,1)S(1)}, u32[]{:S(2)}, u32[]{:S(2)}) collective-permute-start(bf16[1040,128]{1,0:T(8,128)(2,1)S(1)} %get-tuple-element.26.refs_0_), channel_id=1, source_target_pairs={{0,16},{1,9},{2,18},{3,11},{4,20},{5,13},{6,22},{7,15},{8,24},{9,1... | collective-permute-start | bytes 798728 | tf_op jit(solution)/shard_map/exchange/ppermute | solution.py:219
  13.1 10.2 %collective-permute-start.8 = (bf16[1040,128]{1,0:T(8,128)(2,1)S(1)}, bf16[1040,128]{1,0:T(8,128)(2,1)S(1)}, u32[]{:S(2)}, u32[]{:S(2)}) collective-permute-start(bf16[1040,128]{1,0:T(8,128)(2,1)S(1)} %collective-permute-done.6.refs_1_), channel_id=1, source_target_pairs={{0,16},{1,9},{2,18},{3,11},{4,20},{5,13},{6,22},{7,15},{8,24},{9,1... | collective-permute-start | bytes 798728 | tf_op jit(solution)/shard_map/exchange/ppermute | solution.py:219
  15.0 8.3 %collective-permute-start.5 = (bf16[528,128]{1,0:T(8,128)(2,1)S(1)}, bf16[528,128]{1,0:T(8,128)(2,1)S(1)}, u32[]{:S(2)}, u32[]{:S(2)}) collective-permute-start(bf16[528,128]{1,0:T(8,128)(2,1)S(1)} %get-tuple-element.33.q_ref), channel_id=1, source_target_pairs={{0,6},{1,7},{2,4},{3,5},{4,2},{5,3},{6,0},{7,1},{8,14},{9,15},{10,... | collective-permute-start | bytes 405512 | tf_op jit(solution)/shard_map/exchange/ppermute | solution.py:227
  18.7 9.9 %collective-permute-start.4 = (bf16[528,128]{1,0:T(8,128)(2,1)S(1)}, bf16[528,128]{1,0:T(8,128)(2,1)S(1)}, u32[]{:S(2)}, u32[]{:S(2)}) collective-permute-start(bf16[528,128]{1,0:T(8,128)(2,1)S(1)} %get-tuple-element.33.q_ref), channel_id=1, source_target_pairs={{0,4},{1,5},{2,6},{3,7},{4,0},{5,1},{6,2},{7,3},{8,12},{9,13},{10,... | collective-permute-start | bytes 405512 | tf_op jit(solution)/shard_map/exchange/ppermute | solution.py:227
  18.7 11.0 %collective-permute-start.13 = (bf16[528,128]{1,0:T(8,128)(2,1)S(1)}, bf16[528,128]{1,0:T(8,128)(2,1)S(1)}, u32[]{:S(2)}, u32[]{:S(2)}) collective-permute-start(bf16[528,128]{1,0:T(8,128)(2,1)S(1)} %get-tuple-element.33.q_ref), channel_id=1, source_target_pairs={{0,2},{1,3},{2,0},{3,1},{4,6},{5,7},{6,4},{7,5},{8,10},{9,11},{10,... | collective-permute-start | bytes 405512 | tf_op jit(solution)/shard_map/exchange/ppermute | solution.py:227
  24.4 7.6 %collective-permute-start.9 = (bf16[544,128]{1,0:T(8,128)(2,1)S(1)}, bf16[544,128]{1,0:T(8,128)(2,1)S(1)}, u32[]{:S(2)}, u32[]{:S(2)}) collective-permute-start(bf16[544,128]{1,0:T(8,128)(2,1)S(1)} %apply.4), channel_id=1, source_target_pairs={{0,2},{1,3},{2,0},{3,1},{4,6},{5,7},{6,4},{7,5},{8,10},{9,11},{10,... | collective-permute-start | bytes 417800 | tf_op jit(solution)/shard_map/return/ppermute | solution.py:281
  30.9 7.6 %collective-permute-start.14 = (bf16[272,128]{1,0:T(8,128)(2,1)S(1)}, bf16[272,128]{1,0:T(8,128)(2,1)S(1)}, u32[]{:S(2)}, u32[]{:S(2)}) collective-permute-start(bf16[272,128]{1,0:T(8,128)(2,1)S(1)} %get-tuple-element.42), channel_id=1, source_target_pairs={{0,2},{1,3},{2,0},{3,1},{4,6},{5,7},{6,4},{7,5},{8,10},{9,11},{10,... | collective-permute-start | bytes 208904 | tf_op jit(solution)/shard_map/return/ppermute | solution.py:279
  32.1 9.4 %collective-permute-start.11 = (bf16[272,128]{1,0:T(8,128)(2,1)S(1)}, bf16[272,128]{1,0:T(8,128)(2,1)S(1)}, u32[]{:S(2)}, u32[]{:S(2)}) collective-permute-start(bf16[272,128]{1,0:T(8,128)(2,1)S(1)} %get-tuple-element.32), channel_id=1, source_target_pairs={{0,4},{1,5},{2,6},{3,7},{4,0},{5,1},{6,2},{7,3},{8,12},{9,13},{10,... | collective-permute-start | bytes 208904 | tf_op jit(solution)/shard_map/return/ppermute | solution.py:279
  35.2 6.3 %collective-permute-start.12 = (bf16[272,128]{1,0:T(8,128)(2,1)S(1)}, bf16[272,128]{1,0:T(8,128)(2,1)S(1)}, u32[]{:S(2)}, u32[]{:S(2)}) collective-permute-start(bf16[272,128]{1,0:T(8,128)(2,1)S(1)} %get-tuple-element.38), channel_id=1, source_target_pairs={{0,5},{1,4},{2,7},{3,6},{4,1},{5,0},{6,3},{7,2},{8,13},{9,12},{10,... | collective-permute-start | bytes 208904 | tf_op jit(solution)/shard_map/return/ppermute | solution.py:279
  35.2 6.3 %collective-permute-start.15 = (bf16[272,128]{1,0:T(8,128)(2,1)S(1)}, bf16[272,128]{1,0:T(8,128)(2,1)S(1)}, u32[]{:S(2)}, u32[]{:S(2)}) collective-permute-start(bf16[272,128]{1,0:T(8,128)(2,1)S(1)} %get-tuple-element.44), channel_id=1, source_target_pairs={{0,3},{1,2},{2,1},{3,0},{4,7},{5,6},{6,5},{7,4},{8,11},{9,10},{10,... | collective-permute-start | bytes 208904 | tf_op jit(solution)/shard_map/return/ppermute | solution.py:279
  38.4 3.1 %collective-permute-start.10 = (bf16[272,128]{1,0:T(8,128)(2,1)S(1)}, bf16[272,128]{1,0:T(8,128)(2,1)S(1)}, u32[]{:S(2)}, u32[]{:S(2)}) collective-permute-start(bf16[272,128]{1,0:T(8,128)(2,1)S(1)} %get-tuple-element.37), channel_id=1, source_target_pairs={{0,1},{1,0},{2,3},{3,2},{4,5},{5,4},{6,7},{7,6},{8,9},{9,8},{10,11... | collective-permute-start | bytes 208904 | tf_op jit(solution)/shard_map/return/ppermute | solution.py:302

commit v18 on v15

--- a/solution.py
+++ b/solution.py
@@ -220,8 +220,6 @@
             q_by[r] = lax.ppermute(q_piece, "inner", along_inner(r, 0))
         k_by = {r: a[:half, :] for r, a in whole.items() if r}
         v_by = {r: a[half:, :] for r, a in whole.items() if r}
-        if chips > 1:
-            k_by = {r: after(a, q_by[1]) for r, a in k_by.items()}
         for r in range(1, n_out):
             if not single(r):
                 k_by[r] = over(k_by[r - high(r)], high(r))

time: 38.3 us -> 38.8 us (1.013)
  waiting for transfers between devices: 7.24 us -> 8.17 us
  starting transfers between devices: 22.9 us -> 22.5 us
    ppermute x1, starting transfers between devices: 2.09 us -> 0.51 us  [send(): lax.ppermute(parts[0], 'inner', along_inner(low(r), 0))]
    ppermute x3, starting transfers between devices: 6.64 us -> 7.77 us  [shards(): q_by[r] = lax.ppermute(q_piece, 'inner', along_inner(r, 0))]
    ppermute x3, waiting for transfers between devices: 1.69 us -> 2.75 us  [shards(): q_by[r] = lax.ppermute(q_piece, 'inner', along_inner(r, 0))]
    ppermute x4, waiting for transfers between devices: 4.43 us -> 3.96 us  [send(): lax.ppermute(parts[x], 'inner', along_inner(r, x))]
  transfers between devices with their start and end apart: 17 -> 17, of which waited for: 5 -> 4; matrix products, arithmetic and copies ran while one was open for 3% -> 3% of each run, Pallas kernels for 12% -> 12%
where the time goes in v18:
time: 38.8 us; the launch traced here: 38.6 us
  starting transfers between devices  22.5 us (58%)
  waiting for transfers between devices  8.17 us (21%)
  Pallas kernels  6.07 us (16%)
  other arithmetic  1.06 us (3%)
  between operations  0.81 us (2%)
    ppermute x4, starting transfers between devices, over(): return lax.ppermute(a, 'outer', [(o, o ^ r) for o in range(n_out)])  7.91 us
    ppermute x3, starting transfers between devices, shards(): q_by[r] = lax.ppermute(q_piece, 'inner', along_inner(r, 0))  7.77 us
    ppermute x4, starting transfers between devices, send(): lax.ppermute(parts[x], 'inner', along_inner(r, x))  5.23 us
    ppermute x4, waiting for transfers between devices, send(): lax.ppermute(parts[x], 'inner', along_inner(r, x))  3.96 us
    pallas_call x4, Pallas kernels, score(): pl.pallas_call(functools.partial(score_kernel, r == 0), out_shape=(jax.Sh...  3.02 us
    ppermute x3, waiting for transfers between devices, shards(): q_by[r] = lax.ppermute(q_piece, 'inner', along_inner(r, 0))  2.75 us
    ppermute x4, waiting for transfers between devices, over(): return lax.ppermute(a, 'outer', [(o, o ^ r) for o in range(n_out)])  1.45 us
    pallas_call x4, Pallas kernels, apply(): pl.pallas_call(functools.partial(apply_kernel, wide, rows), out_shape=sha...  1.35 us
  transfers between devices with their start and end apart: 17, of which 4 were waited for; matrix products, arithmetic and copies ran while one was open for 3% of the time, Pallas kernels for 12%

profile of v18, /device:TPU:0, one launch (start us, length us, event | category | flops | bytes accessed | tf_op | source)
XLA Modules:
  0.0 38.6 jit_solution(3836526047793860058)
XLA Ops:
  0.0 0.5 %collective-permute-start.1 = (bf16[128,512]{1,0:T(8,128)(2,1)}, bf16[128,512]{1,0:T(8,128)(2,1)S(1)}, u32[]{:S(2)}, u32[]{:S(2)}) collective-permute-start(bf16[128,512]{1,0:T(8,128)(2,1)} %param.4), channel_id=1, source_target_pairs={{0,1},{1,0},{2,3},{3,2},{4,5},{5,4},{6,7},{7,6},{8,9},{9,8},{10,11... | collective-permute-start | bytes 393224 | tf_op jit(solution)/shard_map/swap/ppermute | solution.py:186
  0.5 0.1 collective-permute-start.2
  0.5 0.5 %collective-permute-start.3 = (bf16[128,512]{1,0:T(8,128)(2,1)}, bf16[128,512]{1,0:T(8,128)(2,1)S(1)}, u32[]{:S(2)}, u32[]{:S(2)}) collective-permute-start(bf16[128,512]{1,0:T(8,128)(2,1)} %param.6), channel_id=1, source_target_pairs={{0,1},{1,0},{2,3},{3,2},{4,5},{5,4},{6,7},{7,6},{8,9},{9,8},{10,11... | collective-permute-start | bytes 393224 | tf_op jit(solution)/shard_map/swap/ppermute | solution.py:186
  1.0 0.1 collective-permute-start
  1.7 1.1 %pad_maximum_fusion.own = bf16[384,512]{1,0:T(8,128)(2,1)S(1)} fusion(bf16[128,512]{1,0:T(8,128)(2,1)} %param.6, bf16[128,512]{1,0:T(8,128)(2,1)} %param.5, bf16[128,512]{1,0:T(8,128)(2,1)} %param.4), kind=kLoop, calls=%fused_computation | loop fusion | flops 1179648 | bytes 786432 | tf_op jit(solution)/shard_map/swap/concatenate | solution.py:187
  2.7 0.0 collective-permute-done.p1
  2.7 0.0 collective-permute-done.1.q1
  2.8 0.0 collective-permute-done.2.k1
  2.8 0.0 collective-permute-done.3.v1
  2.8 0.8 %merge.1 = (bf16[528,128]{1,0:T(8,128)(2,1)S(1)}, bf16[1040,128]{1,0:T(8,128)(2,1)S(1)}) custom-call(s32[1]{0:T(128)S(6)} %copy.5.p0, s32[1]{0:T(128)} %collective-permute-done.p1, bf16[384,512]{1,0:T(8,128)(2,1)S(1)} %pad_maximum_fusion.own, bf16[128,512]{1,0:T(8,128)(2,1)S(1)} %collective-permute-done.1.q1, ...), custom_call_target="tpu_custom_call" | custom-call | tf_op jit(solution)/shard_map/merge/merge/pallas_call | solution.py:190
  3.6 3.0 %collective-permute-start.6 = (bf16[1040,128]{1,0:T(8,128)(2,1)S(1)}, bf16[1040,128]{1,0:T(8,128)(2,1)S(1)}, u32[]{:S(2)}, u32[]{:S(2)}) collective-permute-start(bf16[1040,128]{1,0:T(8,128)(2,1)S(1)} %get-tuple-element.26.refs_0_), channel_id=1, source_target_pairs={{0,8},{8,0},{16,24},{24,16},{1,9},{9,1},{17,25},{25,17},{2,10},{10... | collective-permute-start | bytes 798728 | tf_op jit(solution)/shard_map/exchange/ppermute | solution.py:214
  6.6 1.5 %collective-permute-start.7 = (bf16[1040,128]{1,0:T(8,128)(2,1)S(1)}, bf16[1040,128]{1,0:T(8,128)(2,1)S(1)}, u32[]{:S(2)}, u32[]{:S(2)}) collective-permute-start(bf16[1040,128]{1,0:T(8,128)(2,1)S(1)} %get-tuple-element.26.refs_0_), channel_id=1, source_target_pairs={{0,16},{8,24},{16,0},{24,8},{1,17},{9,25},{17,1},{25,9},{2,18},{10... | collective-permute-start | bytes 798728 | tf_op jit(solution)/shard_map/exchange/ppermute | solution.py:214
  8.1 3.6 %collective-permute-start.5 = (bf16[528,128]{1,0:T(8,128)(2,1)S(1)}, bf16[528,128]{1,0:T(8,128)(2,1)S(1)}, u32[]{:S(2)}, u32[]{:S(2)}) collective-permute-start(bf16[528,128]{1,0:T(8,128)(2,1)S(1)} %get-tuple-element.33.q_ref), channel_id=1, source_target_pairs={{0,6},{1,7},{2,4},{3,5},{4,2},{5,3},{6,0},{7,1},{8,14},{9,15},{10,... | collective-permute-start | bytes 405512 | tf_op jit(solution)/shard_map/exchange/ppermute | solution.py:220
  11.7 1.4 %collective-permute-done.6.refs_1_ = bf16[1040,128]{1,0:T(8,128)(2,1)S(1)} collective-permute-done((bf16[1040,128]{1,0:T(8,128)(2,1)S(1)}, bf16[1040,128]{1,0:T(8,128)(2,1)S(1)}, u32[]{:S(2)}, u32[]{:S(2)}) %collective-permute-start.6) | collective-permute-done | bytes 266272 | tf_op jit(solution)/shard_map/exchange/ppermute | solution.py:214
  13.1 1.8 %collective-permute-start.8 = (bf16[528,128]{1,0:T(8,128)(2,1)S(1)}, bf16[528,128]{1,0:T(8,128)(2,1)S(1)}, u32[]{:S(2)}, u32[]{:S(2)}) collective-permute-start(bf16[528,128]{1,0:T(8,128)(2,1)S(1)} %slice.8), channel_id=1, source_target_pairs={{0,16},{8,24},{16,0},{24,8},{1,17},{9,25},{17,1},{25,9},{2,18},{10... | collective-permute-start | bytes 405512 | tf_op jit(solution)/shard_map/exchange/ppermute | solution.py:214
  15.0 0.0 collective-permute-done.7.refs_2_
  15.0 1.6 %collective-permute-start.9 = (bf16[512,128]{1,0:T(8,128)(2,1)S(1)}, bf16[512,128]{1,0:T(8,128)(2,1)S(1)}, u32[]{:S(2)}, u32[]{:S(2)}) collective-permute-start(bf16[512,128]{1,0:T(8,128)(2,1)S(1)} %slice.9), channel_id=1, source_target_pairs={{0,8},{8,0},{16,24},{24,16},{1,9},{9,1},{17,25},{25,17},{2,10},{10... | collective-permute-start | bytes 393224 | tf_op jit(solution)/shard_map/exchange/ppermute | solution.py:214
  16.6 2.6 %collective-permute-start.4 = (bf16[528,128]{1,0:T(8,128)(2,1)S(1)}, bf16[528,128]{1,0:T(8,128)(2,1)S(1)}, u32[]{:S(2)}, u32[]{:S(2)}) collective-permute-start(bf16[528,128]{1,0:T(8,128)(2,1)S(1)} %get-tuple-element.33.q_ref), channel_id=1, source_target_pairs={{0,4},{1,5},{2,6},{3,7},{4,0},{5,1},{6,2},{7,3},{8,12},{9,13},{10,... | collective-permute-start | bytes 405512 | tf_op jit(solution)/shard_map/exchange/ppermute | solution.py:220
  19.1 1.6 %collective-permute-start.14 = (bf16[528,128]{1,0:T(8,128)(2,1)S(1)}, bf16[528,128]{1,0:T(8,128)(2,1)S(1)}, u32[]{:S(2)}, u32[]{:S(2)}) collective-permute-start(bf16[528,128]{1,0:T(8,128)(2,1)S(1)} %get-tuple-element.33.q_ref), channel_id=1, source_target_pairs={{0,2},{1,3},{2,0},{3,1},{4,6},{5,7},{6,4},{7,5},{8,10},{9,11},{10,... | collective-permute-start | bytes 405512 | tf_op jit(solution)/shard_map/exchange/ppermute | solution.py:220
  20.7 0.0 collective-permute-done.5.q_ref
  20.7 0.0 collective-permute-done.8.refs_3_
  20.7 0.8 %score.4 = (bf16[2,1024,256]{2,1,0:T(8,128)(2,1)S(1)}, f32[16,256]{1,0:T(8,128)S(1)}) custom-call(bf16[528,128]{1,0:T(8,128)(2,1)S(1)} %collective-permute-done.5.q_ref, bf16[1040,128]{1,0:T(8,128)(2,1)S(1)} %get-tuple-element.26.refs_0_, bf16[1040,128]{1,0:T(8,128)(2,1)S(1)} %collective-permute-done.6.refs_1_, ...), custom_call_target="tpu_custom_call" | custom-call | flops 134217728 | bytes 1048576 | tf_op jit(solution)/shard_map/score/score/pallas_call | solution.py:241
  21.5 0.0 collective-permute-done.9.refs_3_
  21.5 0.3 apply.4
  21.8 0.5 %collective-permute-start.10 = (bf16[544,128]{1,0:T(8,128)(2,1)S(1)}, bf16[544,128]{1,0:T(8,128)(2,1)S(1)}, u32[]{:S(2)}, u32[]{:S(2)}) collective-permute-start(bf16[544,128]{1,0:T(8,128)(2,1)S(1)} %apply.4), channel_id=1, source_target_pairs={{0,2},{1,3},{2,0},{3,1},{4,6},{5,7},{6,4},{7,5},{8,10},{9,11},{10,... | collective-permute-start | bytes 417800 | tf_op jit(solution)/shard_map/return/ppermute | solution.py:285
  22.4 1.5 %collective-permute-done.4.q_ref = bf16[528,128]{1,0:T(8,128)(2,1)S(1)} collective-permute-done((bf16[528,128]{1,0:T(8,128)(2,1)S(1)}, bf16[528,128]{1,0:T(8,128)(2,1)S(1)}, u32[]{:S(2)}, u32[]{:S(2)}) %collective-permute-start.4) | collective-permute-done | bytes 135200 | tf_op jit(solution)/shard_map/exchange/ppermute | solution.py:220
  23.9 0.8 %score.5 = (bf16[2,1024,256]{2,1,0:T(8,128)(2,1)S(1)}, f32[16,256]{1,0:T(8,128)S(1)}) custom-call(bf16[528,128]{1,0:T(8,128)(2,1)S(1)} %collective-permute-done.4.q_ref, bf16[1040,128]{1,0:T(8,128)(2,1)S(1)} %get-tuple-element.26.refs_0_, bf16[1040,128]{1,0:T(8,128)(2,1)S(1)} %collective-permute-done.6.refs_1_, ...), custom_call_target="tpu_custom_call" | custom-call | flops 134217728 | bytes 1048576 | tf_op jit(solution)/shard_map/score/score/pallas_call | solution.py:241
  24.6 0.3 apply.5.refs_0_
  25.0 1.2 %collective-permute-done.14.q_ref = bf16[528,128]{1,0:T(8,128)(2,1)S(1)} collective-permute-done((bf16[528,128]{1,0:T(8,128)(2,1)S(1)}, bf16[528,128]{1,0:T(8,128)(2,1)S(1)}, u32[]{:S(2)}, u32[]{:S(2)}) %collective-permute-start.14) | collective-permute-done | bytes 135200 | tf_op jit(solution)/shard_map/exchange/ppermute | solution.py:220
  26.2 0.8 %score.7 = (bf16[2,1024,256]{2,1,0:T(8,128)(2,1)S(1)}, f32[16,256]{1,0:T(8,128)S(1)}) custom-call(bf16[528,128]{1,0:T(8,128)(2,1)S(1)} %collective-permute-done.14.q_ref, bf16[1040,128]{1,0:T(8,128)(2,1)S(1)} %get-tuple-element.26.refs_0_, bf16[1040,128]{1,0:T(8,128)(2,1)S(1)} %collective-permute-done.6.refs_1_, ...), custom_call_target="tpu_custom_call" | custom-call | flops 134217728 | bytes 1048576 | tf_op jit(solution)/shard_map/score/score/pallas_call | solution.py:241
  27.0 0.3 apply.7
  27.3 1.5 %collective-permute-start.15 = (bf16[272,128]{1,0:T(8,128)(2,1)S(1)}, bf16[272,128]{1,0:T(8,128)(2,1)S(1)}, u32[]{:S(2)}, u32[]{:S(2)}) collective-permute-start(bf16[272,128]{1,0:T(8,128)(2,1)S(1)} %get-tuple-element.42), channel_id=1, source_target_pairs={{0,2},{1,3},{2,0},{3,1},{4,6},{5,7},{6,4},{7,5},{8,10},{9,11},{10,... | collective-permute-start | bytes 208904 | tf_op jit(solution)/shard_map/return/ppermute | solution.py:283
  28.8 0.0 collective-permute-done.10.refs_1_
  28.8 0.1 add.1
  28.9 2.3 %collective-permute-start.12 = (bf16[272,128]{1,0:T(8,128)(2,1)S(1)}, bf16[272,128]{1,0:T(8,128)(2,1)S(1)}, u32[]{:S(2)}, u32[]{:S(2)}) collective-permute-start(bf16[272,128]{1,0:T(8,128)(2,1)S(1)} %get-tuple-element.32), channel_id=1, source_target_pairs={{0,4},{1,5},{2,6},{3,7},{4,0},{5,1},{6,2},{7,3},{8,12},{9,13},{10,... | collective-permute-start | bytes 208904 | tf_op jit(solution)/shard_map/return/ppermute | solution.py:283
  31.2 0.0 collective-permute-start.13
  31.2 1.4 %collective-permute-start.16 = (bf16[272,128]{1,0:T(8,128)(2,1)S(1)}, bf16[272,128]{1,0:T(8,128)(2,1)S(1)}, u32[]{:S(2)}, u32[]{:S(2)}) collective-permute-start(bf16[272,128]{1,0:T(8,128)(2,1)S(1)} %get-tuple-element.44), channel_id=1, source_target_pairs={{0,3},{1,2},{2,1},{3,0},{4,7},{5,6},{6,5},{7,4},{8,11},{9,10},{10,... | collective-permute-start | bytes 208904 | tf_op jit(solution)/shard_map/return/ppermute | solution.py:283
  32.6 0.8 %score.6 = (bf16[2,1024,256]{2,1,0:T(8,128)(2,1)S(1)}, f32[16,256]{1,0:T(8,128)S(1)}) custom-call(bf16[528,128]{1,0:T(8,128)(2,1)S(1)} %get-tuple-element.33.q_ref, bf16[1040,128]{1,0:T(8,128)(2,1)S(1)} %get-tuple-element.26.refs_0_, bf16[1040,128]{1,0:T(8,128)(2,1)S(1)} %collective-permute-done.6.refs_1_, ...), custom_call_target="tpu_custom_call" | custom-call | flops 134217728 | bytes 1048576 | tf_op jit(solution)/shard_map/score/score/pallas_call | solution.py:241
  33.4 0.3 apply.6
  33.7 0.1 collective-permute-start.11
  33.8 0.0 collective-permute-done.15.refs_4_
  33.8 3.9 %collective-permute-done.13.refs_3_ = bf16[272,128]{1,0:T(8,128)(2,1)S(1)} collective-permute-done((bf16[272,128]{1,0:T(8,128)(2,1)S(1)}, bf16[272,128]{1,0:T(8,128)(2,1)S(1)}, u32[]{:S(2)}, u32[]{:S(2)}) %collective-permute-start.13) | collective-permute-done | bytes 69664 | tf_op jit(solution)/shard_map/return/ppermute | solution.py:283
  37.8 0.0 collective-permute-done.12.refs_2_
  37.8 0.0 collective-permute-done.16.refs_5_
  37.8 0.0 collective-permute-done.11.refs_1_
  37.8 0.8 %combine.1 = bf16[128,512]{1,0:T(8,128)(2,1)} custom-call(bf16[272,128]{1,0:T(8,128)(2,1)S(1)} %get-tuple-element.36.refs_0_, bf16[272,128]{1,0:T(8,128)(2,1)S(1)} %collective-permute-done.11.refs_1_, bf16[272,128]{1,0:T(8,128)(2,1)S(1)} %collective-permute-done.12.refs_2_, bf16[272,128]{1,0:T(8,128)(2,1)S(1)} %collective-permute-done.13.refs_3_, ...), custom_call_target="tpu_custom_call" | custom-call | tf_op jit(solution)/shard_map/combine/combine/pallas_call | solution.py:308
  (2 shorter events, 0.0 us)
Async XLA Ops:
  0.0 2.7 %collective-permute-start.1 = (bf16[128,512]{1,0:T(8,128)(2,1)}, bf16[128,512]{1,0:T(8,128)(2,1)S(1)}, u32[]{:S(2)}, u32[]{:S(2)}) collective-permute-start(bf16[128,512]{1,0:T(8,128)(2,1)} %param.4), channel_id=1, source_target_pairs={{0,1},{1,0},{2,3},{3,2},{4,5},{5,4},{6,7},{7,6},{8,9},{9,8},{10,11... | collective-permute-start | bytes 393224 | tf_op jit(solution)/shard_map/swap/ppermute | solution.py:186
  0.5 2.3 %collective-permute-start.2 = (bf16[128,512]{1,0:T(8,128)(2,1)}, bf16[128,512]{1,0:T(8,128)(2,1)S(1)}, u32[]{:S(2)}, u32[]{:S(2)}) collective-permute-start(bf16[128,512]{1,0:T(8,128)(2,1)} %param.5), channel_id=1, source_target_pairs={{0,1},{1,0},{2,3},{3,2},{4,5},{5,4},{6,7},{7,6},{8,9},{9,8},{10,11... | collective-permute-start | bytes 393224 | tf_op jit(solution)/shard_map/swap/ppermute | solution.py:186
  0.5 2.3 %collective-permute-start.3 = (bf16[128,512]{1,0:T(8,128)(2,1)}, bf16[128,512]{1,0:T(8,128)(2,1)S(1)}, u32[]{:S(2)}, u32[]{:S(2)}) collective-permute-start(bf16[128,512]{1,0:T(8,128)(2,1)} %param.6), channel_id=1, source_target_pairs={{0,1},{1,0},{2,3},{3,2},{4,5},{5,4},{6,7},{7,6},{8,9},{9,8},{10,11... | collective-permute-start | bytes 393224 | tf_op jit(solution)/shard_map/swap/ppermute | solution.py:186
  1.0 1.8 %collective-permute-start = (s32[1]{0:T(128)}, s32[1]{0:T(128)}, u32[]{:S(2)}, u32[]{:S(2)}) collective-permute-start(s32[1]{0:T(128)} %param.7), channel_id=1, source_target_pairs={{0,1},{1,0},{2,3},{3,2},{4,5},{5,4},{6,7},{7,6},{8,9},{9,8},{10,11... | collective-permute-start | bytes 20 | tf_op jit(solution)/shard_map/swap/ppermute | solution.py:186
  3.6 9.6 %collective-permute-start.6 = (bf16[1040,128]{1,0:T(8,128)(2,1)S(1)}, bf16[1040,128]{1,0:T(8,128)(2,1)S(1)}, u32[]{:S(2)}, u32[]{:S(2)}) collective-permute-start(bf16[1040,128]{1,0:T(8,128)(2,1)S(1)} %get-tuple-element.26.refs_0_), channel_id=1, source_target_pairs={{0,8},{8,0},{16,24},{24,16},{1,9},{9,1},{17,25},{25,17},{2,10},{10... | collective-permute-start | bytes 798728 | tf_op jit(solution)/shard_map/exchange/ppermute | solution.py:214
  6.6 8.4 %collective-permute-start.7 = (bf16[1040,128]{1,0:T(8,128)(2,1)S(1)}, bf16[1040,128]{1,0:T(8,128)(2,1)S(1)}, u32[]{:S(2)}, u32[]{:S(2)}) collective-permute-start(bf16[1040,128]{1,0:T(8,128)(2,1)S(1)} %get-tuple-element.26.refs_0_), channel_id=1, source_target_pairs={{0,16},{8,24},{16,0},{24,8},{1,17},{9,25},{17,1},{25,9},{2,18},{10... | collective-permute-start | bytes 798728 | tf_op jit(solution)/shard_map/exchange/ppermute | solution.py:214
  8.1 12.6 %collective-permute-start.5 = (bf16[528,128]{1,0:T(8,128)(2,1)S(1)}, bf16[528,128]{1,0:T(8,128)(2,1)S(1)}, u32[]{:S(2)}, u32[]{:S(2)}) collective-permute-start(bf16[528,128]{1,0:T(8,128)(2,1)S(1)} %get-tuple-element.33.q_ref), channel_id=1, source_target_pairs={{0,6},{1,7},{2,4},{3,5},{4,2},{5,3},{6,0},{7,1},{8,14},{9,15},{10,... | collective-permute-start | bytes 405512 | tf_op jit(solution)/shard_map/exchange/ppermute | solution.py:220
  13.1 7.6 %collective-permute-start.8 = (bf16[528,128]{1,0:T(8,128)(2,1)S(1)}, bf16[528,128]{1,0:T(8,128)(2,1)S(1)}, u32[]{:S(2)}, u32[]{:S(2)}) collective-permute-start(bf16[528,128]{1,0:T(8,128)(2,1)S(1)} %slice.8), channel_id=1, source_target_pairs={{0,16},{8,24},{16,0},{24,8},{1,17},{9,25},{17,1},{25,9},{2,18},{10... | collective-permute-start | bytes 405512 | tf_op jit(solution)/shard_map/exchange/ppermute | solution.py:214
  15.0 6.5 %collective-permute-start.9 = (bf16[512,128]{1,0:T(8,128)(2,1)S(1)}, bf16[512,128]{1,0:T(8,128)(2,1)S(1)}, u32[]{:S(2)}, u32[]{:S(2)}) collective-permute-start(bf16[512,128]{1,0:T(8,128)(2,1)S(1)} %slice.9), channel_id=1, source_target_pairs={{0,8},{8,0},{16,24},{24,16},{1,9},{9,1},{17,25},{25,17},{2,10},{10... | collective-permute-start | bytes 393224 | tf_op jit(solution)/shard_map/exchange/ppermute | solution.py:214
  16.6 7.3 %collective-permute-start.4 = (bf16[528,128]{1,0:T(8,128)(2,1)S(1)}, bf16[528,128]{1,0:T(8,128)(2,1)S(1)}, u32[]{:S(2)}, u32[]{:S(2)}) collective-permute-start(bf16[528,128]{1,0:T(8,128)(2,1)S(1)} %get-tuple-element.33.q_ref), channel_id=1, source_target_pairs={{0,4},{1,5},{2,6},{3,7},{4,0},{5,1},{6,2},{7,3},{8,12},{9,13},{10,... | collective-permute-start | bytes 405512 | tf_op jit(solution)/shard_map/exchange/ppermute | solution.py:220
  19.1 7.1 %collective-permute-start.14 = (bf16[528,128]{1,0:T(8,128)(2,1)S(1)}, bf16[528,128]{1,0:T(8,128)(2,1)S(1)}, u32[]{:S(2)}, u32[]{:S(2)}) collective-permute-start(bf16[528,128]{1,0:T(8,128)(2,1)S(1)} %get-tuple-element.33.q_ref), channel_id=1, source_target_pairs={{0,2},{1,3},{2,0},{3,1},{4,6},{5,7},{6,4},{7,5},{8,10},{9,11},{10,... | collective-permute-start | bytes 405512 | tf_op jit(solution)/shard_map/exchange/ppermute | solution.py:220
  21.8 6.9 %collective-permute-start.10 = (bf16[544,128]{1,0:T(8,128)(2,1)S(1)}, bf16[544,128]{1,0:T(8,128)(2,1)S(1)}, u32[]{:S(2)}, u32[]{:S(2)}) collective-permute-start(bf16[544,128]{1,0:T(8,128)(2,1)S(1)} %apply.4), channel_id=1, source_target_pairs={{0,2},{1,3},{2,0},{3,1},{4,6},{5,7},{6,4},{7,5},{8,10},{9,11},{10,... | collective-permute-start | bytes 417800 | tf_op jit(solution)/shard_map/return/ppermute | solution.py:285
  27.3 6.5 %collective-permute-start.15 = (bf16[272,128]{1,0:T(8,128)(2,1)S(1)}, bf16[272,128]{1,0:T(8,128)(2,1)S(1)}, u32[]{:S(2)}, u32[]{:S(2)}) collective-permute-start(bf16[272,128]{1,0:T(8,128)(2,1)S(1)} %get-tuple-element.42), channel_id=1, source_target_pairs={{0,2},{1,3},{2,0},{3,1},{4,6},{5,7},{6,4},{7,5},{8,10},{9,11},{10,... | collective-permute-start | bytes 208904 | tf_op jit(solution)/shard_map/return/ppermute | solution.py:283
  28.9 8.9 %collective-permute-start.12 = (bf16[272,128]{1,0:T(8,128)(2,1)S(1)}, bf16[272,128]{1,0:T(8,128)(2,1)S(1)}, u32[]{:S(2)}, u32[]{:S(2)}) collective-permute-start(bf16[272,128]{1,0:T(8,128)(2,1)S(1)} %get-tuple-element.32), channel_id=1, source_target_pairs={{0,4},{1,5},{2,6},{3,7},{4,0},{5,1},{6,2},{7,3},{8,12},{9,13},{10,... | collective-permute-start | bytes 208904 | tf_op jit(solution)/shard_map/return/ppermute | solution.py:283
  31.2 6.6 %collective-permute-start.13 = (bf16[272,128]{1,0:T(8,128)(2,1)S(1)}, bf16[272,128]{1,0:T(8,128)(2,1)S(1)}, u32[]{:S(2)}, u32[]{:S(2)}) collective-permute-start(bf16[272,128]{1,0:T(8,128)(2,1)S(1)} %get-tuple-element.38), channel_id=1, source_target_pairs={{0,5},{1,4},{2,7},{3,6},{4,1},{5,0},{6,3},{7,2},{8,13},{9,12},{10,... | collective-permute-start | bytes 208904 | tf_op jit(solution)/shard_map/return/ppermute | solution.py:283
  31.2 6.6 %collective-permute-start.16 = (bf16[272,128]{1,0:T(8,128)(2,1)S(1)}, bf16[272,128]{1,0:T(8,128)(2,1)S(1)}, u32[]{:S(2)}, u32[]{:S(2)}) collective-permute-start(bf16[272,128]{1,0:T(8,128)(2,1)S(1)} %get-tuple-element.44), channel_id=1, source_target_pairs={{0,3},{1,2},{2,1},{3,0},{4,7},{5,6},{6,5},{7,4},{8,11},{9,10},{10,... | collective-permute-start | bytes 208904 | tf_op jit(solution)/shard_map/return/ppermute | solution.py:283
  33.7 4.0 %collective-permute-start.11 = (bf16[272,128]{1,0:T(8,128)(2,1)S(1)}, bf16[272,128]{1,0:T(8,128)(2,1)S(1)}, u32[]{:S(2)}, u32[]{:S(2)}) collective-permute-start(bf16[272,128]{1,0:T(8,128)(2,1)S(1)} %get-tuple-element.37), channel_id=1, source_target_pairs={{0,1},{1,0},{2,3},{3,2},{4,5},{5,4},{6,7},{7,6},{8,9},{9,8},{10,11... | collective-permute-start | bytes 208904 | tf_op jit(solution)/shard_map/return/ppermute | solution.py:306

commit v19 on v18

--- a/solution.py
+++ b/solution.py
@@ -225,7 +225,8 @@
                 k_by[r] = over(k_by[r - high(r)], high(r))
         for r in sorted(range(1, n_out), key=lambda r: r.bit_count()):
             if not single(r):
-                v_by[r] = over(v_by[r - low(r)], low(r))
+                v = v_by[r - low(r)]
+                v_by[r] = over(after(v, q_by[1]) if chips > 1 else v, low(r))
         ks = [whole[r] if r in whole else k_by[r] for r in range(n_out)]
         vs = [whole[r] if r in whole else v_by[r] for r in range(n_out)]
         rows = tuple(half if r in whole else 0 for r in range(n_out))

time: 38.8 us -> 37.9 us (0.977)
  waiting for transfers between devices: 8.17 us -> 7.69 us
  starting transfers between devices: 22.5 us -> 22.1 us
    ppermute x1, starting transfers between devices: 0.51 us -> 1.64 us  [send(): lax.ppermute(parts[0], 'inner', along_inner(low(r), 0))]
    ppermute x3, starting transfers between devices: 7.77 us -> 6.64 us  [shards(): q_by[r] = lax.ppermute(q_piece, 'inner', along_inner(r, 0))]
    ppermute x4, starting transfers between devices: 5.23 us -> 4.8 us  [send(): lax.ppermute(parts[x], 'inner', along_inner(r, x))]
where the time goes in v19:
time: 37.9 us; the launch traced here: 37.7 us
  starting transfers between devices  22.1 us (58%)
  waiting for transfers between devices  7.69 us (20%)
  Pallas kernels  6.07 us (16%)
  other arithmetic  1.06 us (3%)
  between operations  0.81 us (2%)
    ppermute x4, starting transfers between devices, over(): return lax.ppermute(a, 'outer', [(o, o ^ r) for o in range(n_out)])  7.91 us
    ppermute x3, starting transfers between devices, shards(): q_by[r] = lax.ppermute(q_piece, 'inner', along_inner(r, 0))  6.64 us
    ppermute x4, starting transfers between devices, send(): lax.ppermute(parts[x], 'inner', along_inner(r, x))  4.8 us
    ppermute x4, waiting for transfers between devices, send(): lax.ppermute(parts[x], 'inner', along_inner(r, x))  4.05 us
    pallas_call x4, Pallas kernels, score(): pl.pallas_call(functools.partial(score_kernel, r == 0), out_shape=(jax.Sh...  3.03 us
    ppermute x3, waiting for transfers between devices, shards(): q_by[r] = lax.ppermute(q_piece, 'inner', along_inner(r, 0))  2.51 us
    ppermute x1, starting transfers between devices, send(): lax.ppermute(parts[0], 'inner', along_inner(low(r), 0))  1.64 us
    pallas_call x4, Pallas kernels, apply(): pl.pallas_call(functools.partial(apply_kernel, wide, rows), out_shape=sha...  1.36 us
  transfers between devices with their start and end apart: 17, of which 4 were waited for; matrix products, arithmetic and copies ran while one was open for 3% of the time, Pallas kernels for 12%

profile of v19, /device:TPU:0, one launch (start us, length us, event | category | flops | bytes accessed | tf_op | source)
XLA Modules:
  0.0 37.7 jit_solution(14868998892651575501)
XLA Ops:
  0.0 0.5 %collective-permute-start.1 = (bf16[128,512]{1,0:T(8,128)(2,1)}, bf16[128,512]{1,0:T(8,128)(2,1)S(1)}, u32[]{:S(2)}, u32[]{:S(2)}) collective-permute-start(bf16[128,512]{1,0:T(8,128)(2,1)} %param.4), channel_id=1, source_target_pairs={{0,1},{1,0},{2,3},{3,2},{4,5},{5,4},{6,7},{7,6},{8,9},{9,8},{10,11... | collective-permute-start | bytes 393224 | tf_op jit(solution)/shard_map/swap/ppermute | solution.py:186
  0.5 0.1 collective-permute-start.2
  0.5 0.5 %collective-permute-start.3 = (bf16[128,512]{1,0:T(8,128)(2,1)}, bf16[128,512]{1,0:T(8,128)(2,1)S(1)}, u32[]{:S(2)}, u32[]{:S(2)}) collective-permute-start(bf16[128,512]{1,0:T(8,128)(2,1)} %param.6), channel_id=1, source_target_pairs={{0,1},{1,0},{2,3},{3,2},{4,5},{5,4},{6,7},{7,6},{8,9},{9,8},{10,11... | collective-permute-start | bytes 393224 | tf_op jit(solution)/shard_map/swap/ppermute | solution.py:186
  1.0 0.1 collective-permute-start
  1.7 1.1 %pad_maximum_fusion.own = bf16[384,512]{1,0:T(8,128)(2,1)S(1)} fusion(bf16[128,512]{1,0:T(8,128)(2,1)} %param.6, bf16[128,512]{1,0:T(8,128)(2,1)} %param.5, bf16[128,512]{1,0:T(8,128)(2,1)} %param.4), kind=kLoop, calls=%fused_computation | loop fusion | flops 1179648 | bytes 786432 | tf_op jit(solution)/shard_map/swap/concatenate | solution.py:187
  2.7 0.0 collective-permute-done.p1
  2.7 0.0 collective-permute-done.1.q1
  2.8 0.0 collective-permute-done.2.k1
  2.8 0.0 collective-permute-done.3.v1
  2.8 0.8 %merge.1 = (bf16[528,128]{1,0:T(8,128)(2,1)S(1)}, bf16[1040,128]{1,0:T(8,128)(2,1)S(1)}) custom-call(s32[1]{0:T(128)S(6)} %copy.5.p0, s32[1]{0:T(128)} %collective-permute-done.p1, bf16[384,512]{1,0:T(8,128)(2,1)S(1)} %pad_maximum_fusion.own, bf16[128,512]{1,0:T(8,128)(2,1)S(1)} %collective-permute-done.1.q1, ...), custom_call_target="tpu_custom_call" | custom-call | tf_op jit(solution)/shard_map/merge/merge/pallas_call | solution.py:190
  3.6 3.0 %collective-permute-start.6 = (bf16[1040,128]{1,0:T(8,128)(2,1)S(1)}, bf16[1040,128]{1,0:T(8,128)(2,1)S(1)}, u32[]{:S(2)}, u32[]{:S(2)}) collective-permute-start(bf16[1040,128]{1,0:T(8,128)(2,1)S(1)} %get-tuple-element.27.refs_0_), channel_id=1, source_target_pairs={{0,8},{8,0},{16,24},{24,16},{1,9},{9,1},{17,25},{25,17},{2,10},{10... | collective-permute-start | bytes 798728 | tf_op jit(solution)/shard_map/exchange/ppermute | solution.py:214
  6.6 1.5 %collective-permute-start.7 = (bf16[1040,128]{1,0:T(8,128)(2,1)S(1)}, bf16[1040,128]{1,0:T(8,128)(2,1)S(1)}, u32[]{:S(2)}, u32[]{:S(2)}) collective-permute-start(bf16[1040,128]{1,0:T(8,128)(2,1)S(1)} %get-tuple-element.27.refs_0_), channel_id=1, source_target_pairs={{0,16},{8,24},{16,0},{24,8},{1,17},{9,25},{17,1},{25,9},{2,18},{10... | collective-permute-start | bytes 798728 | tf_op jit(solution)/shard_map/exchange/ppermute | solution.py:214
  8.1 1.6 %collective-permute-start.9 = (bf16[528,128]{1,0:T(8,128)(2,1)S(1)}, bf16[528,128]{1,0:T(8,128)(2,1)S(1)}, u32[]{:S(2)}, u32[]{:S(2)}) collective-permute-start(bf16[528,128]{1,0:T(8,128)(2,1)S(1)} %get-tuple-element.35.q_ref), channel_id=1, source_target_pairs={{0,2},{1,3},{2,0},{3,1},{4,6},{5,7},{6,4},{7,5},{8,10},{9,11},{10,... | collective-permute-start | bytes 405512 | tf_op jit(solution)/shard_map/exchange/ppermute | solution.py:220
  9.7 2.5 %collective-permute-start.5 = (bf16[528,128]{1,0:T(8,128)(2,1)S(1)}, bf16[528,128]{1,0:T(8,128)(2,1)S(1)}, u32[]{:S(2)}, u32[]{:S(2)}) collective-permute-start(bf16[528,128]{1,0:T(8,128)(2,1)S(1)} %get-tuple-element.35.q_ref), channel_id=1, source_target_pairs={{0,6},{1,7},{2,4},{3,5},{4,2},{5,3},{6,0},{7,1},{8,14},{9,15},{10,... | collective-permute-start | bytes 405512 | tf_op jit(solution)/shard_map/exchange/ppermute | solution.py:220
  12.1 1.0 %collective-permute-done.6.refs_1_ = bf16[1040,128]{1,0:T(8,128)(2,1)S(1)} collective-permute-done((bf16[1040,128]{1,0:T(8,128)(2,1)S(1)}, bf16[1040,128]{1,0:T(8,128)(2,1)S(1)}, u32[]{:S(2)}, u32[]{:S(2)}) %collective-permute-start.6) | collective-permute-done | bytes 266272 | tf_op jit(solution)/shard_map/exchange/ppermute | solution.py:214
  13.1 1.8 %collective-permute-start.8 = (bf16[528,128]{1,0:T(8,128)(2,1)S(1)}, bf16[528,128]{1,0:T(8,128)(2,1)S(1)}, u32[]{:S(2)}, u32[]{:S(2)}) collective-permute-start(bf16[528,128]{1,0:T(8,128)(2,1)S(1)} %slice.8), channel_id=1, source_target_pairs={{0,16},{8,24},{16,0},{24,8},{1,17},{9,25},{17,1},{25,9},{2,18},{10... | collective-permute-start | bytes 405512 | tf_op jit(solution)/shard_map/exchange/ppermute | solution.py:214
  15.0 0.0 collective-permute-done.7.refs_2_
  15.0 0.0 collective-permute-done.9.q_ref
  15.0 1.6 %collective-permute-start.10 = (bf16[512,128]{1,0:T(8,128)(2,1)S(1)}, bf16[512,128]{1,0:T(8,128)(2,1)S(1)}, u32[]{:S(2)}, u32[]{:S(2)}) collective-permute-start(bf16[512,128]{1,0:T(8,128)(2,1)S(1)} %slice.9), channel_id=1, source_target_pairs={{0,8},{8,0},{16,24},{24,16},{1,9},{9,1},{17,25},{25,17},{2,10},{10... | collective-permute-start | bytes 393224 | tf_op jit(solution)/shard_map/exchange/ppermute | solution.py:214
  16.6 2.6 %collective-permute-start.4 = (bf16[528,128]{1,0:T(8,128)(2,1)S(1)}, bf16[528,128]{1,0:T(8,128)(2,1)S(1)}, u32[]{:S(2)}, u32[]{:S(2)}) collective-permute-start(bf16[528,128]{1,0:T(8,128)(2,1)S(1)} %get-tuple-element.35.q_ref), channel_id=1, source_target_pairs={{0,4},{1,5},{2,6},{3,7},{4,0},{5,1},{6,2},{7,3},{8,12},{9,13},{10,... | collective-permute-start | bytes 405512 | tf_op jit(solution)/shard_map/exchange/ppermute | solution.py:220
  19.2 0.0 collective-permute-done.5.q_ref
  19.2 0.0 collective-permute-done.8.refs_3_
  19.2 0.8 %score.4 = (bf16[2,1024,256]{2,1,0:T(8,128)(2,1)S(1)}, f32[16,256]{1,0:T(8,128)S(1)}) custom-call(bf16[528,128]{1,0:T(8,128)(2,1)S(1)} %collective-permute-done.5.q_ref, bf16[1040,128]{1,0:T(8,128)(2,1)S(1)} %get-tuple-element.27.refs_0_, bf16[1040,128]{1,0:T(8,128)(2,1)S(1)} %collective-permute-done.6.refs_1_, ...), custom_call_target="tpu_custom_call" | custom-call | flops 134217728 | bytes 1048576 | tf_op jit(solution)/shard_map/score/score/pallas_call | solution.py:242
  19.9 0.1 collective-permute-done.10.refs_3_
  20.0 0.3 apply.4
  20.4 1.6 %collective-permute-start.11 = (bf16[544,128]{1,0:T(8,128)(2,1)S(1)}, bf16[544,128]{1,0:T(8,128)(2,1)S(1)}, u32[]{:S(2)}, u32[]{:S(2)}) collective-permute-start(bf16[544,128]{1,0:T(8,128)(2,1)S(1)} %apply.4), channel_id=1, source_target_pairs={{0,2},{1,3},{2,0},{3,1},{4,6},{5,7},{6,4},{7,5},{8,10},{9,11},{10,... | collective-permute-start | bytes 417800 | tf_op jit(solution)/shard_map/return/ppermute | solution.py:286
  22.0 2.5 %collective-permute-done.4.q_ref = bf16[528,128]{1,0:T(8,128)(2,1)S(1)} collective-permute-done((bf16[528,128]{1,0:T(8,128)(2,1)S(1)}, bf16[528,128]{1,0:T(8,128)(2,1)S(1)}, u32[]{:S(2)}, u32[]{:S(2)}) %collective-permute-start.4) | collective-permute-done | bytes 135200 | tf_op jit(solution)/shard_map/exchange/ppermute | solution.py:220
  24.5 0.8 %score.5 = (bf16[2,1024,256]{2,1,0:T(8,128)(2,1)S(1)}, f32[16,256]{1,0:T(8,128)S(1)}) custom-call(bf16[528,128]{1,0:T(8,128)(2,1)S(1)} %collective-permute-done.4.q_ref, bf16[1040,128]{1,0:T(8,128)(2,1)S(1)} %get-tuple-element.27.refs_0_, bf16[1040,128]{1,0:T(8,128)(2,1)S(1)} %collective-permute-done.6.refs_1_, ...), custom_call_target="tpu_custom_call" | custom-call | flops 134217728 | bytes 1048576 | tf_op jit(solution)/shard_map/score/score/pallas_call | solution.py:242
  25.3 0.3 apply.5.refs_0_
  25.6 0.8 %score.7 = (bf16[2,1024,256]{2,1,0:T(8,128)(2,1)S(1)}, f32[16,256]{1,0:T(8,128)S(1)}) custom-call(bf16[528,128]{1,0:T(8,128)(2,1)S(1)} %collective-permute-done.9.q_ref, bf16[1040,128]{1,0:T(8,128)(2,1)S(1)} %get-tuple-element.27.refs_0_, bf16[1040,128]{1,0:T(8,128)(2,1)S(1)} %collective-permute-done.6.refs_1_, ...), custom_call_target="tpu_custom_call" | custom-call | flops 134217728 | bytes 1048576 | tf_op jit(solution)/shard_map/score/score/pallas_call | solution.py:242
  26.4 0.3 apply.7
  26.8 0.6 %collective-permute-start.15 = (bf16[272,128]{1,0:T(8,128)(2,1)S(1)}, bf16[272,128]{1,0:T(8,128)(2,1)S(1)}, u32[]{:S(2)}, u32[]{:S(2)}) collective-permute-start(bf16[272,128]{1,0:T(8,128)(2,1)S(1)} %get-tuple-element.44), channel_id=1, source_target_pairs={{0,2},{1,3},{2,0},{3,1},{4,6},{5,7},{6,4},{7,5},{8,10},{9,11},{10,... | collective-permute-start | bytes 208904 | tf_op jit(solution)/shard_map/return/ppermute | solution.py:284
  27.4 0.0 collective-permute-done.11.refs_1_
  27.4 0.1 add.1
  27.5 3.5 %collective-permute-start.13 = (bf16[272,128]{1,0:T(8,128)(2,1)S(1)}, bf16[272,128]{1,0:T(8,128)(2,1)S(1)}, u32[]{:S(2)}, u32[]{:S(2)}) collective-permute-start(bf16[272,128]{1,0:T(8,128)(2,1)S(1)} %get-tuple-element.34), channel_id=1, source_target_pairs={{0,4},{1,5},{2,6},{3,7},{4,0},{5,1},{6,2},{7,3},{8,12},{9,13},{10,... | collective-permute-start | bytes 208904 | tf_op jit(solution)/shard_map/return/ppermute | solution.py:284
  31.0 0.0 collective-permute-start.14
  31.0 0.6 %collective-permute-start.16 = (bf16[272,128]{1,0:T(8,128)(2,1)S(1)}, bf16[272,128]{1,0:T(8,128)(2,1)S(1)}, u32[]{:S(2)}, u32[]{:S(2)}) collective-permute-start(bf16[272,128]{1,0:T(8,128)(2,1)S(1)} %get-tuple-element.46), channel_id=1, source_target_pairs={{0,3},{1,2},{2,1},{3,0},{4,7},{5,6},{6,5},{7,4},{8,11},{9,10},{10,... | collective-permute-start | bytes 208904 | tf_op jit(solution)/shard_map/return/ppermute | solution.py:284
  31.6 0.8 %score.6 = (bf16[2,1024,256]{2,1,0:T(8,128)(2,1)S(1)}, f32[16,256]{1,0:T(8,128)S(1)}) custom-call(bf16[528,128]{1,0:T(8,128)(2,1)S(1)} %get-tuple-element.35.q_ref, bf16[1040,128]{1,0:T(8,128)(2,1)S(1)} %get-tuple-element.27.refs_0_, bf16[1040,128]{1,0:T(8,128)(2,1)S(1)} %collective-permute-done.6.refs_1_, ...), custom_call_target="tpu_custom_call" | custom-call | flops 134217728 | bytes 1048576 | tf_op jit(solution)/shard_map/score/score/pallas_call | solution.py:242
  32.4 0.3 apply.6
  32.8 0.1 collective-permute-start.12
  32.8 0.0 collective-permute-done.15.refs_4_
  32.8 4.0 %collective-permute-done.14.refs_3_ = bf16[272,128]{1,0:T(8,128)(2,1)S(1)} collective-permute-done((bf16[272,128]{1,0:T(8,128)(2,1)S(1)}, bf16[272,128]{1,0:T(8,128)(2,1)S(1)}, u32[]{:S(2)}, u32[]{:S(2)}) %collective-permute-start.14) | collective-permute-done | bytes 69664 | tf_op jit(solution)/shard_map/return/ppermute | solution.py:284
  36.9 0.0 collective-permute-done.13.refs_2_
  36.9 0.0 collective-permute-done.16.refs_5_
  36.9 0.0 collective-permute-done.12.refs_1_
  36.9 0.8 %combine.1 = bf16[128,512]{1,0:T(8,128)(2,1)} custom-call(bf16[272,128]{1,0:T(8,128)(2,1)S(1)} %get-tuple-element.38.refs_0_, bf16[272,128]{1,0:T(8,128)(2,1)S(1)} %collective-permute-done.12.refs_1_, bf16[272,128]{1,0:T(8,128)(2,1)S(1)} %collective-permute-done.13.refs_2_, bf16[272,128]{1,0:T(8,128)(2,1)S(1)} %collective-permute-done.14.refs_3_, ...), custom_call_target="tpu_custom_call" | custom-call | tf_op jit(solution)/shard_map/combine/combine/pallas_call | solution.py:309
  (2 shorter events, 0.0 us)
Async XLA Ops:
  0.0 2.7 %collective-permute-start.1 = (bf16[128,512]{1,0:T(8,128)(2,1)}, bf16[128,512]{1,0:T(8,128)(2,1)S(1)}, u32[]{:S(2)}, u32[]{:S(2)}) collective-permute-start(bf16[128,512]{1,0:T(8,128)(2,1)} %param.4), channel_id=1, source_target_pairs={{0,1},{1,0},{2,3},{3,2},{4,5},{5,4},{6,7},{7,6},{8,9},{9,8},{10,11... | collective-permute-start | bytes 393224 | tf_op jit(solution)/shard_map/swap/ppermute | solution.py:186
  0.5 2.3 %collective-permute-start.2 = (bf16[128,512]{1,0:T(8,128)(2,1)}, bf16[128,512]{1,0:T(8,128)(2,1)S(1)}, u32[]{:S(2)}, u32[]{:S(2)}) collective-permute-start(bf16[128,512]{1,0:T(8,128)(2,1)} %param.5), channel_id=1, source_target_pairs={{0,1},{1,0},{2,3},{3,2},{4,5},{5,4},{6,7},{7,6},{8,9},{9,8},{10,11... | collective-permute-start | bytes 393224 | tf_op jit(solution)/shard_map/swap/ppermute | solution.py:186
  0.5 2.3 %collective-permute-start.3 = (bf16[128,512]{1,0:T(8,128)(2,1)}, bf16[128,512]{1,0:T(8,128)(2,1)S(1)}, u32[]{:S(2)}, u32[]{:S(2)}) collective-permute-start(bf16[128,512]{1,0:T(8,128)(2,1)} %param.6), channel_id=1, source_target_pairs={{0,1},{1,0},{2,3},{3,2},{4,5},{5,4},{6,7},{7,6},{8,9},{9,8},{10,11... | collective-permute-start | bytes 393224 | tf_op jit(solution)/shard_map/swap/ppermute | solution.py:186
  1.0 1.8 %collective-permute-start = (s32[1]{0:T(128)}, s32[1]{0:T(128)}, u32[]{:S(2)}, u32[]{:S(2)}) collective-permute-start(s32[1]{0:T(128)} %param.7), channel_id=1, source_target_pairs={{0,1},{1,0},{2,3},{3,2},{4,5},{5,4},{6,7},{7,6},{8,9},{9,8},{10,11... | collective-permute-start | bytes 20 | tf_op jit(solution)/shard_map/swap/ppermute | solution.py:186
  3.6 9.6 %collective-permute-start.6 = (bf16[1040,128]{1,0:T(8,128)(2,1)S(1)}, bf16[1040,128]{1,0:T(8,128)(2,1)S(1)}, u32[]{:S(2)}, u32[]{:S(2)}) collective-permute-start(bf16[1040,128]{1,0:T(8,128)(2,1)S(1)} %get-tuple-element.27.refs_0_), channel_id=1, source_target_pairs={{0,8},{8,0},{16,24},{24,16},{1,9},{9,1},{17,25},{25,17},{2,10},{10... | collective-permute-start | bytes 798728 | tf_op jit(solution)/shard_map/exchange/ppermute | solution.py:214
  6.6 8.4 %collective-permute-start.7 = (bf16[1040,128]{1,0:T(8,128)(2,1)S(1)}, bf16[1040,128]{1,0:T(8,128)(2,1)S(1)}, u32[]{:S(2)}, u32[]{:S(2)}) collective-permute-start(bf16[1040,128]{1,0:T(8,128)(2,1)S(1)} %get-tuple-element.27.refs_0_), channel_id=1, source_target_pairs={{0,16},{8,24},{16,0},{24,8},{1,17},{9,25},{17,1},{25,9},{2,18},{10... | collective-permute-start | bytes 798728 | tf_op jit(solution)/shard_map/exchange/ppermute | solution.py:214
  8.1 6.9 %collective-permute-start.9 = (bf16[528,128]{1,0:T(8,128)(2,1)S(1)}, bf16[528,128]{1,0:T(8,128)(2,1)S(1)}, u32[]{:S(2)}, u32[]{:S(2)}) collective-permute-start(bf16[528,128]{1,0:T(8,128)(2,1)S(1)} %get-tuple-element.35.q_ref), channel_id=1, source_target_pairs={{0,2},{1,3},{2,0},{3,1},{4,6},{5,7},{6,4},{7,5},{8,10},{9,11},{10,... | collective-permute-start | bytes 405512 | tf_op jit(solution)/shard_map/exchange/ppermute | solution.py:220
  9.7 9.5 %collective-permute-start.5 = (bf16[528,128]{1,0:T(8,128)(2,1)S(1)}, bf16[528,128]{1,0:T(8,128)(2,1)S(1)}, u32[]{:S(2)}, u32[]{:S(2)}) collective-permute-start(bf16[528,128]{1,0:T(8,128)(2,1)S(1)} %get-tuple-element.35.q_ref), channel_id=1, source_target_pairs={{0,6},{1,7},{2,4},{3,5},{4,2},{5,3},{6,0},{7,1},{8,14},{9,15},{10,... | collective-permute-start | bytes 405512 | tf_op jit(solution)/shard_map/exchange/ppermute | solution.py:220
  13.1 6.0 %collective-permute-start.8 = (bf16[528,128]{1,0:T(8,128)(2,1)S(1)}, bf16[528,128]{1,0:T(8,128)(2,1)S(1)}, u32[]{:S(2)}, u32[]{:S(2)}) collective-permute-start(bf16[528,128]{1,0:T(8,128)(2,1)S(1)} %slice.8), channel_id=1, source_target_pairs={{0,16},{8,24},{16,0},{24,8},{1,17},{9,25},{17,1},{25,9},{2,18},{10... | collective-permute-start | bytes 405512 | tf_op jit(solution)/shard_map/exchange/ppermute | solution.py:214
  15.0 5.0 %collective-permute-start.10 = (bf16[512,128]{1,0:T(8,128)(2,1)S(1)}, bf16[512,128]{1,0:T(8,128)(2,1)S(1)}, u32[]{:S(2)}, u32[]{:S(2)}) collective-permute-start(bf16[512,128]{1,0:T(8,128)(2,1)S(1)} %slice.9), channel_id=1, source_target_pairs={{0,8},{8,0},{16,24},{24,16},{1,9},{9,1},{17,25},{25,17},{2,10},{10... | collective-permute-start | bytes 393224 | tf_op jit(solution)/shard_map/exchange/ppermute | solution.py:214
  16.6 8.0 %collective-permute-start.4 = (bf16[528,128]{1,0:T(8,128)(2,1)S(1)}, bf16[528,128]{1,0:T(8,128)(2,1)S(1)}, u32[]{:S(2)}, u32[]{:S(2)}) collective-permute-start(bf16[528,128]{1,0:T(8,128)(2,1)S(1)} %get-tuple-element.35.q_ref), channel_id=1, source_target_pairs={{0,4},{1,5},{2,6},{3,7},{4,0},{5,1},{6,2},{7,3},{8,12},{9,13},{10,... | collective-permute-start | bytes 405512 | tf_op jit(solution)/shard_map/exchange/ppermute | solution.py:220
  20.4 7.0 %collective-permute-start.11 = (bf16[544,128]{1,0:T(8,128)(2,1)S(1)}, bf16[544,128]{1,0:T(8,128)(2,1)S(1)}, u32[]{:S(2)}, u32[]{:S(2)}) collective-permute-start(bf16[544,128]{1,0:T(8,128)(2,1)S(1)} %apply.4), channel_id=1, source_target_pairs={{0,2},{1,3},{2,0},{3,1},{4,6},{5,7},{6,4},{7,5},{8,10},{9,11},{10,... | collective-permute-start | bytes 417800 | tf_op jit(solution)/shard_map/return/ppermute | solution.py:286
  26.8 6.1 %collective-permute-start.15 = (bf16[272,128]{1,0:T(8,128)(2,1)S(1)}, bf16[272,128]{1,0:T(8,128)(2,1)S(1)}, u32[]{:S(2)}, u32[]{:S(2)}) collective-permute-start(bf16[272,128]{1,0:T(8,128)(2,1)S(1)} %get-tuple-element.44), channel_id=1, source_target_pairs={{0,2},{1,3},{2,0},{3,1},{4,6},{5,7},{6,4},{7,5},{8,10},{9,11},{10,... | collective-permute-start | bytes 208904 | tf_op jit(solution)/shard_map/return/ppermute | solution.py:284
  27.5 9.4 %collective-permute-start.13 = (bf16[272,128]{1,0:T(8,128)(2,1)S(1)}, bf16[272,128]{1,0:T(8,128)(2,1)S(1)}, u32[]{:S(2)}, u32[]{:S(2)}) collective-permute-start(bf16[272,128]{1,0:T(8,128)(2,1)S(1)} %get-tuple-element.34), channel_id=1, source_target_pairs={{0,4},{1,5},{2,6},{3,7},{4,0},{5,1},{6,2},{7,3},{8,12},{9,13},{10,... | collective-permute-start | bytes 208904 | tf_op jit(solution)/shard_map/return/ppermute | solution.py:284
  31.0 5.9 %collective-permute-start.14 = (bf16[272,128]{1,0:T(8,128)(2,1)S(1)}, bf16[272,128]{1,0:T(8,128)(2,1)S(1)}, u32[]{:S(2)}, u32[]{:S(2)}) collective-permute-start(bf16[272,128]{1,0:T(8,128)(2,1)S(1)} %get-tuple-element.40), channel_id=1, source_target_pairs={{0,5},{1,4},{2,7},{3,6},{4,1},{5,0},{6,3},{7,2},{8,13},{9,12},{10,... | collective-permute-start | bytes 208904 | tf_op jit(solution)/shard_map/return/ppermute | solution.py:284
  31.0 5.9 %collective-permute-start.16 = (bf16[272,128]{1,0:T(8,128)(2,1)S(1)}, bf16[272,128]{1,0:T(8,128)(2,1)S(1)}, u32[]{:S(2)}, u32[]{:S(2)}) collective-permute-start(bf16[272,128]{1,0:T(8,128)(2,1)S(1)} %get-tuple-element.46), channel_id=1, source_target_pairs={{0,3},{1,2},{2,1},{3,0},{4,7},{5,6},{6,5},{7,4},{8,11},{9,10},{10,... | collective-permute-start | bytes 208904 | tf_op jit(solution)/shard_map/return/ppermute | solution.py:284
  32.8 4.1 %collective-permute-start.12 = (bf16[272,128]{1,0:T(8,128)(2,1)S(1)}, bf16[272,128]{1,0:T(8,128)(2,1)S(1)}, u32[]{:S(2)}, u32[]{:S(2)}) collective-permute-start(bf16[272,128]{1,0:T(8,128)(2,1)S(1)} %get-tuple-element.39), channel_id=1, source_target_pairs={{0,1},{1,0},{2,3},{3,2},{4,5},{5,4},{6,7},{7,6},{8,9},{9,8},{10,11... | collective-permute-start | bytes 208904 | tf_op jit(solution)/shard_map/return/ppermute | solution.py:307

commit v20 on v19

--- a/solution.py
+++ b/solution.py
@@ -292,17 +292,17 @@
 
     done = None
     weights_by, partial = {}, {}
-    for r in reversed(range(1, chips)):
+    for r in sorted(range(1, chips), key=lambda r: (r != chips - 1, r != 1, -r)):
         done = both_kernels(r, done)
-    for r in reversed(range(1, chips)):
+    for r in reversed(range(2, chips)):
         parts = partial[r]
         if arrived[r]:
             parts = add([parts[0], *arrived[r]], not single(r))
             done = parts[0]
-        if r == 1:
-            parts = [parts[0], after(parts[1], done)]
         send(r, parts)
-    both_kernels(0, done)
+    done = both_kernels(0, done)
+    if chips > 1:
+        send(1, [partial[1][0], after(partial[1][1], done)])
     with jax.named_scope("return"):
         ends = [partial[0][0], lax.ppermute(partial[0][1], "inner", along_inner(0, 1))] + ends
     with jax.named_scope("combine"):

time: 37.9 us -> 36.9 us (0.974)
  waiting for transfers between devices: 7.69 us -> 6.75 us
    ppermute x3, waiting for transfers between devices: 2.51 us -> 0.89 us  [shards(): q_by[r] = lax.ppermute(q_piece, 'inner', along_inner(r, 0))]
    ppermute x1, waiting for transfers between devices: 0.01 us -> 1.07 us  [send(): lax.ppermute(parts[0], 'inner', along_inner(low(r), 0))]
    ppermute x4, waiting for transfers between devices: 4.05 us -> 3.66 us  [send(): lax.ppermute(parts[x], 'inner', along_inner(r, x))]
  transfers between devices with their start and end apart: 17 -> 17, of which waited for: 4 -> 5; matrix products, arithmetic and copies ran while one was open for 3% -> 3% of each run, Pallas kernels for 12% -> 12%
where the time goes in v20:
time: 36.9 us; the launch traced here: 36.8 us
  starting transfers between devices  22.1 us (60%)
  waiting for transfers between devices  6.75 us (18%)
  Pallas kernels  6.07 us (16%)
  other arithmetic  1.06 us (3%)
  between operations  0.8 us (2%)
    ppermute x4, starting transfers between devices, over(): return lax.ppermute(a, 'outer', [(o, o ^ r) for o in range(n_out)])  7.91 us
    ppermute x3, starting transfers between devices, shards(): q_by[r] = lax.ppermute(q_piece, 'inner', along_inner(r, 0))  6.64 us
    ppermute x4, starting transfers between devices, send(): lax.ppermute(parts[x], 'inner', along_inner(r, x))  4.54 us
    ppermute x4, waiting for transfers between devices, send(): lax.ppermute(parts[x], 'inner', along_inner(r, x))  3.66 us
    pallas_call x4, Pallas kernels, score(): pl.pallas_call(functools.partial(score_kernel, r == 0), out_shape=(jax.Sh...  3.02 us
    ppermute x1, starting transfers between devices, send(): lax.ppermute(parts[0], 'inner', along_inner(low(r), 0))  1.64 us
    pallas_call x4, Pallas kernels, apply(): pl.pallas_call(functools.partial(apply_kernel, wide, rows), out_shape=sha...  1.36 us
    ppermute x4, waiting for transfers between devices, over(): return lax.ppermute(a, 'outer', [(o, o ^ r) for o in range(n_out)])  1.12 us
  transfers between devices with their start and end apart: 17, of which 5 were waited for; matrix products, arithmetic and copies ran while one was open for 3% of the time, Pallas kernels for 12%

profile of v20, /device:TPU:0, one launch (start us, length us, event | category | flops | bytes accessed | tf_op | source)
XLA Modules:
  0.0 36.8 jit_solution(9071287510963184183)
XLA Ops:
  0.0 0.5 %collective-permute-start.1 = (bf16[128,512]{1,0:T(8,128)(2,1)}, bf16[128,512]{1,0:T(8,128)(2,1)S(1)}, u32[]{:S(2)}, u32[]{:S(2)}) collective-permute-start(bf16[128,512]{1,0:T(8,128)(2,1)} %param.4), channel_id=1, source_target_pairs={{0,1},{1,0},{2,3},{3,2},{4,5},{5,4},{6,7},{7,6},{8,9},{9,8},{10,11... | collective-permute-start | bytes 393224 | tf_op jit(solution)/shard_map/swap/ppermute | solution.py:186
  0.5 0.1 collective-permute-start.2
  0.5 0.5 %collective-permute-start.3 = (bf16[128,512]{1,0:T(8,128)(2,1)}, bf16[128,512]{1,0:T(8,128)(2,1)S(1)}, u32[]{:S(2)}, u32[]{:S(2)}) collective-permute-start(bf16[128,512]{1,0:T(8,128)(2,1)} %param.6), channel_id=1, source_target_pairs={{0,1},{1,0},{2,3},{3,2},{4,5},{5,4},{6,7},{7,6},{8,9},{9,8},{10,11... | collective-permute-start | bytes 393224 | tf_op jit(solution)/shard_map/swap/ppermute | solution.py:186
  1.0 0.1 collective-permute-start
  1.7 1.1 %pad_maximum_fusion.own = bf16[384,512]{1,0:T(8,128)(2,1)S(1)} fusion(bf16[128,512]{1,0:T(8,128)(2,1)} %param.6, bf16[128,512]{1,0:T(8,128)(2,1)} %param.5, bf16[128,512]{1,0:T(8,128)(2,1)} %param.4), kind=kLoop, calls=%fused_computation | loop fusion | flops 1179648 | bytes 786432 | tf_op jit(solution)/shard_map/swap/concatenate | solution.py:187
  2.7 0.0 collective-permute-done.p1
  2.7 0.0 collective-permute-done.1.q1
  2.8 0.0 collective-permute-done.2.k1
  2.8 0.0 collective-permute-done.3.v1
  2.8 0.8 %merge.1 = (bf16[528,128]{1,0:T(8,128)(2,1)S(1)}, bf16[1040,128]{1,0:T(8,128)(2,1)S(1)}) custom-call(s32[1]{0:T(128)S(6)} %copy.5.p0, s32[1]{0:T(128)} %collective-permute-done.p1, bf16[384,512]{1,0:T(8,128)(2,1)S(1)} %pad_maximum_fusion.own, bf16[128,512]{1,0:T(8,128)(2,1)S(1)} %collective-permute-done.1.q1, ...), custom_call_target="tpu_custom_call" | custom-call | tf_op jit(solution)/shard_map/merge/merge/pallas_call | solution.py:190
  3.6 3.0 %collective-permute-start.7 = (bf16[1040,128]{1,0:T(8,128)(2,1)S(1)}, bf16[1040,128]{1,0:T(8,128)(2,1)S(1)}, u32[]{:S(2)}, u32[]{:S(2)}) collective-permute-start(bf16[1040,128]{1,0:T(8,128)(2,1)S(1)} %get-tuple-element.27.refs_0_), channel_id=1, source_target_pairs={{0,8},{8,0},{16,24},{24,16},{1,9},{9,1},{17,25},{25,17},{2,10},{10... | collective-permute-start | bytes 798728 | tf_op jit(solution)/shard_map/exchange/ppermute | solution.py:214
  6.6 1.5 %collective-permute-start.8 = (bf16[1040,128]{1,0:T(8,128)(2,1)S(1)}, bf16[1040,128]{1,0:T(8,128)(2,1)S(1)}, u32[]{:S(2)}, u32[]{:S(2)}) collective-permute-start(bf16[1040,128]{1,0:T(8,128)(2,1)S(1)} %get-tuple-element.27.refs_0_), channel_id=1, source_target_pairs={{0,16},{8,24},{16,0},{24,8},{1,17},{9,25},{17,1},{25,9},{2,18},{10... | collective-permute-start | bytes 798728 | tf_op jit(solution)/shard_map/exchange/ppermute | solution.py:214
  8.1 1.6 %collective-permute-start.5 = (bf16[528,128]{1,0:T(8,128)(2,1)S(1)}, bf16[528,128]{1,0:T(8,128)(2,1)S(1)}, u32[]{:S(2)}, u32[]{:S(2)}) collective-permute-start(bf16[528,128]{1,0:T(8,128)(2,1)S(1)} %get-tuple-element.39.q_ref), channel_id=1, source_target_pairs={{0,2},{1,3},{2,0},{3,1},{4,6},{5,7},{6,4},{7,5},{8,10},{9,11},{10,... | collective-permute-start | bytes 405512 | tf_op jit(solution)/shard_map/exchange/ppermute | solution.py:220
  9.7 2.5 %collective-permute-start.6 = (bf16[528,128]{1,0:T(8,128)(2,1)S(1)}, bf16[528,128]{1,0:T(8,128)(2,1)S(1)}, u32[]{:S(2)}, u32[]{:S(2)}) collective-permute-start(bf16[528,128]{1,0:T(8,128)(2,1)S(1)} %get-tuple-element.39.q_ref), channel_id=1, source_target_pairs={{0,6},{1,7},{2,4},{3,5},{4,2},{5,3},{6,0},{7,1},{8,14},{9,15},{10,... | collective-permute-start | bytes 405512 | tf_op jit(solution)/shard_map/exchange/ppermute | solution.py:220
  12.1 1.0 %collective-permute-done.7.refs_1_ = bf16[1040,128]{1,0:T(8,128)(2,1)S(1)} collective-permute-done((bf16[1040,128]{1,0:T(8,128)(2,1)S(1)}, bf16[1040,128]{1,0:T(8,128)(2,1)S(1)}, u32[]{:S(2)}, u32[]{:S(2)}) %collective-permute-start.7) | collective-permute-done | bytes 266272 | tf_op jit(solution)/shard_map/exchange/ppermute | solution.py:214
  13.1 1.8 %collective-permute-start.9 = (bf16[528,128]{1,0:T(8,128)(2,1)S(1)}, bf16[528,128]{1,0:T(8,128)(2,1)S(1)}, u32[]{:S(2)}, u32[]{:S(2)}) collective-permute-start(bf16[528,128]{1,0:T(8,128)(2,1)S(1)} %slice.8), channel_id=1, source_target_pairs={{0,16},{8,24},{16,0},{24,8},{1,17},{9,25},{17,1},{25,9},{2,18},{10... | collective-permute-start | bytes 405512 | tf_op jit(solution)/shard_map/exchange/ppermute | solution.py:214
  15.0 0.0 collective-permute-done.8.refs_2_
  15.0 0.0 collective-permute-done.5.q_ref
  15.0 1.6 %collective-permute-start.10 = (bf16[512,128]{1,0:T(8,128)(2,1)S(1)}, bf16[512,128]{1,0:T(8,128)(2,1)S(1)}, u32[]{:S(2)}, u32[]{:S(2)}) collective-permute-start(bf16[512,128]{1,0:T(8,128)(2,1)S(1)} %slice.9), channel_id=1, source_target_pairs={{0,8},{8,0},{16,24},{24,16},{1,9},{9,1},{17,25},{25,17},{2,10},{10... | collective-permute-start | bytes 393224 | tf_op jit(solution)/shard_map/exchange/ppermute | solution.py:214
  16.6 2.6 %collective-permute-start.4 = (bf16[528,128]{1,0:T(8,128)(2,1)S(1)}, bf16[528,128]{1,0:T(8,128)(2,1)S(1)}, u32[]{:S(2)}, u32[]{:S(2)}) collective-permute-start(bf16[528,128]{1,0:T(8,128)(2,1)S(1)} %get-tuple-element.39.q_ref), channel_id=1, source_target_pairs={{0,4},{1,5},{2,6},{3,7},{4,0},{5,1},{6,2},{7,3},{8,12},{9,13},{10,... | collective-permute-start | bytes 405512 | tf_op jit(solution)/shard_map/exchange/ppermute | solution.py:220
  19.2 0.0 collective-permute-done.6.q_ref
  19.2 0.0 collective-permute-done.9.refs_3_
  19.2 0.8 %score.4 = (bf16[2,1024,256]{2,1,0:T(8,128)(2,1)S(1)}, f32[16,256]{1,0:T(8,128)S(1)}) custom-call(bf16[528,128]{1,0:T(8,128)(2,1)S(1)} %collective-permute-done.6.q_ref, bf16[1040,128]{1,0:T(8,128)(2,1)S(1)} %get-tuple-element.27.refs_0_, bf16[1040,128]{1,0:T(8,128)(2,1)S(1)} %collective-permute-done.7.refs_1_, ...), custom_call_target="tpu_custom_call" | custom-call | flops 134217728 | bytes 1048576 | tf_op jit(solution)/shard_map/score/score/pallas_call | solution.py:242
  19.9 0.1 collective-permute-done.10.refs_3_
  20.0 0.3 apply.4
  20.4 1.6 %collective-permute-start.11 = (bf16[544,128]{1,0:T(8,128)(2,1)S(1)}, bf16[544,128]{1,0:T(8,128)(2,1)S(1)}, u32[]{:S(2)}, u32[]{:S(2)}) collective-permute-start(bf16[544,128]{1,0:T(8,128)(2,1)S(1)} %apply.4), channel_id=1, source_target_pairs={{0,2},{1,3},{2,0},{3,1},{4,6},{5,7},{6,4},{7,5},{8,10},{9,11},{10,... | collective-permute-start | bytes 417800 | tf_op jit(solution)/shard_map/return/ppermute | solution.py:286
  22.0 0.8 %score.5 = (bf16[2,1024,256]{2,1,0:T(8,128)(2,1)S(1)}, f32[16,256]{1,0:T(8,128)S(1)}) custom-call(bf16[528,128]{1,0:T(8,128)(2,1)S(1)} %collective-permute-done.5.q_ref, bf16[1040,128]{1,0:T(8,128)(2,1)S(1)} %get-tuple-element.27.refs_0_, bf16[1040,128]{1,0:T(8,128)(2,1)S(1)} %collective-permute-done.7.refs_1_, ...), custom_call_target="tpu_custom_call" | custom-call | flops 134217728 | bytes 1048576 | tf_op jit(solution)/shard_map/score/score/pallas_call | solution.py:242
  22.8 0.3 apply.5
  23.1 0.5 %collective-permute-start.15 = (bf16[272,128]{1,0:T(8,128)(2,1)S(1)}, bf16[272,128]{1,0:T(8,128)(2,1)S(1)}, u32[]{:S(2)}, u32[]{:S(2)}) collective-permute-start(bf16[272,128]{1,0:T(8,128)(2,1)S(1)} %get-tuple-element.34), channel_id=1, source_target_pairs={{0,2},{1,3},{2,0},{3,1},{4,6},{5,7},{6,4},{7,5},{8,10},{9,11},{10,... | collective-permute-start | bytes 208904 | tf_op jit(solution)/shard_map/return/ppermute | solution.py:284
  23.7 0.9 %collective-permute-done.4.q_ref = bf16[528,128]{1,0:T(8,128)(2,1)S(1)} collective-permute-done((bf16[528,128]{1,0:T(8,128)(2,1)S(1)}, bf16[528,128]{1,0:T(8,128)(2,1)S(1)}, u32[]{:S(2)}, u32[]{:S(2)}) %collective-permute-start.4) | collective-permute-done | bytes 135200 | tf_op jit(solution)/shard_map/exchange/ppermute | solution.py:220
  24.5 0.8 %score.6 = (bf16[2,1024,256]{2,1,0:T(8,128)(2,1)S(1)}, f32[16,256]{1,0:T(8,128)S(1)}) custom-call(bf16[528,128]{1,0:T(8,128)(2,1)S(1)} %collective-permute-done.4.q_ref, bf16[1040,128]{1,0:T(8,128)(2,1)S(1)} %get-tuple-element.27.refs_0_, bf16[1040,128]{1,0:T(8,128)(2,1)S(1)} %collective-permute-done.7.refs_1_, ...), custom_call_target="tpu_custom_call" | custom-call | flops 134217728 | bytes 1048576 | tf_op jit(solution)/shard_map/score/score/pallas_call | solution.py:242
  25.3 0.3 apply.6.refs_0_
  25.6 1.1 %collective-permute-done.11.refs_1_ = bf16[544,128]{1,0:T(8,128)(2,1)S(1)} collective-permute-done((bf16[544,128]{1,0:T(8,128)(2,1)S(1)}, bf16[544,128]{1,0:T(8,128)(2,1)S(1)}, u32[]{:S(2)}, u32[]{:S(2)}) %collective-permute-start.11) | collective-permute-done | bytes 139296 | tf_op jit(solution)/shard_map/return/ppermute | solution.py:286
  26.7 0.1 add.1
  26.8 1.9 %collective-permute-start.13 = (bf16[272,128]{1,0:T(8,128)(2,1)S(1)}, bf16[272,128]{1,0:T(8,128)(2,1)S(1)}, u32[]{:S(2)}, u32[]{:S(2)}) collective-permute-start(bf16[272,128]{1,0:T(8,128)(2,1)S(1)} %get-tuple-element.38), channel_id=1, source_target_pairs={{0,4},{1,5},{2,6},{3,7},{4,0},{5,1},{6,2},{7,3},{8,12},{9,13},{10,... | collective-permute-start | bytes 208904 | tf_op jit(solution)/shard_map/return/ppermute | solution.py:284
  28.7 0.0 collective-permute-start.14
  28.7 0.8 %score.7 = (bf16[2,1024,256]{2,1,0:T(8,128)(2,1)S(1)}, f32[16,256]{1,0:T(8,128)S(1)}) custom-call(bf16[528,128]{1,0:T(8,128)(2,1)S(1)} %get-tuple-element.39.q_ref, bf16[1040,128]{1,0:T(8,128)(2,1)S(1)} %get-tuple-element.27.refs_0_, bf16[1040,128]{1,0:T(8,128)(2,1)S(1)} %collective-permute-done.7.refs_1_, ...), custom_call_target="tpu_custom_call" | custom-call | flops 134217728 | bytes 1048576 | tf_op jit(solution)/shard_map/score/score/pallas_call | solution.py:242
  29.5 0.3 apply.7
  29.8 2.1 %collective-permute-start.16 = (bf16[272,128]{1,0:T(8,128)(2,1)S(1)}, bf16[272,128]{1,0:T(8,128)(2,1)S(1)}, u32[]{:S(2)}, u32[]{:S(2)}) collective-permute-start(bf16[272,128]{1,0:T(8,128)(2,1)S(1)} %get-tuple-element.46), channel_id=1, source_target_pairs={{0,3},{1,2},{2,1},{3,0},{4,7},{5,6},{6,5},{7,4},{8,11},{9,10},{10,... | collective-permute-start | bytes 208904 | tf_op jit(solution)/shard_map/return/ppermute | solution.py:284
  31.9 0.3 collective-permute-start.12
  32.3 0.0 collective-permute-done.15.refs_4_
  32.3 3.7 %collective-permute-done.14.refs_3_ = bf16[272,128]{1,0:T(8,128)(2,1)S(1)} collective-permute-done((bf16[272,128]{1,0:T(8,128)(2,1)S(1)}, bf16[272,128]{1,0:T(8,128)(2,1)S(1)}, u32[]{:S(2)}, u32[]{:S(2)}) %collective-permute-start.14) | collective-permute-done | bytes 69664 | tf_op jit(solution)/shard_map/return/ppermute | solution.py:284
  35.9 0.0 collective-permute-done.13.refs_2_
  35.9 0.0 collective-permute-done.16.refs_5_
  35.9 0.0 collective-permute-done.12.refs_1_
  35.9 0.8 %combine.1 = bf16[128,512]{1,0:T(8,128)(2,1)} custom-call(bf16[272,128]{1,0:T(8,128)(2,1)S(1)} %get-tuple-element.42.refs_0_, bf16[272,128]{1,0:T(8,128)(2,1)S(1)} %collective-permute-done.12.refs_1_, bf16[272,128]{1,0:T(8,128)(2,1)S(1)} %collective-permute-done.13.refs_2_, bf16[272,128]{1,0:T(8,128)(2,1)S(1)} %collective-permute-done.14.refs_3_, ...), custom_call_target="tpu_custom_call" | custom-call | tf_op jit(solution)/shard_map/combine/combine/pallas_call | solution.py:309
  (2 shorter events, 0.0 us)
Async XLA Ops:
  0.0 2.7 %collective-permute-start.1 = (bf16[128,512]{1,0:T(8,128)(2,1)}, bf16[128,512]{1,0:T(8,128)(2,1)S(1)}, u32[]{:S(2)}, u32[]{:S(2)}) collective-permute-start(bf16[128,512]{1,0:T(8,128)(2,1)} %param.4), channel_id=1, source_target_pairs={{0,1},{1,0},{2,3},{3,2},{4,5},{5,4},{6,7},{7,6},{8,9},{9,8},{10,11... | collective-permute-start | bytes 393224 | tf_op jit(solution)/shard_map/swap/ppermute | solution.py:186
  0.5 2.3 %collective-permute-start.2 = (bf16[128,512]{1,0:T(8,128)(2,1)}, bf16[128,512]{1,0:T(8,128)(2,1)S(1)}, u32[]{:S(2)}, u32[]{:S(2)}) collective-permute-start(bf16[128,512]{1,0:T(8,128)(2,1)} %param.5), channel_id=1, source_target_pairs={{0,1},{1,0},{2,3},{3,2},{4,5},{5,4},{6,7},{7,6},{8,9},{9,8},{10,11... | collective-permute-start | bytes 393224 | tf_op jit(solution)/shard_map/swap/ppermute | solution.py:186
  0.5 2.3 %collective-permute-start.3 = (bf16[128,512]{1,0:T(8,128)(2,1)}, bf16[128,512]{1,0:T(8,128)(2,1)S(1)}, u32[]{:S(2)}, u32[]{:S(2)}) collective-permute-start(bf16[128,512]{1,0:T(8,128)(2,1)} %param.6), channel_id=1, source_target_pairs={{0,1},{1,0},{2,3},{3,2},{4,5},{5,4},{6,7},{7,6},{8,9},{9,8},{10,11... | collective-permute-start | bytes 393224 | tf_op jit(solution)/shard_map/swap/ppermute | solution.py:186
  1.0 1.8 %collective-permute-start = (s32[1]{0:T(128)}, s32[1]{0:T(128)}, u32[]{:S(2)}, u32[]{:S(2)}) collective-permute-start(s32[1]{0:T(128)} %param.7), channel_id=1, source_target_pairs={{0,1},{1,0},{2,3},{3,2},{4,5},{5,4},{6,7},{7,6},{8,9},{9,8},{10,11... | collective-permute-start | bytes 20 | tf_op jit(solution)/shard_map/swap/ppermute | solution.py:186
  3.6 9.6 %collective-permute-start.7 = (bf16[1040,128]{1,0:T(8,128)(2,1)S(1)}, bf16[1040,128]{1,0:T(8,128)(2,1)S(1)}, u32[]{:S(2)}, u32[]{:S(2)}) collective-permute-start(bf16[1040,128]{1,0:T(8,128)(2,1)S(1)} %get-tuple-element.27.refs_0_), channel_id=1, source_target_pairs={{0,8},{8,0},{16,24},{24,16},{1,9},{9,1},{17,25},{25,17},{2,10},{10... | collective-permute-start | bytes 798728 | tf_op jit(solution)/shard_map/exchange/ppermute | solution.py:214
  6.6 8.4 %collective-permute-start.8 = (bf16[1040,128]{1,0:T(8,128)(2,1)S(1)}, bf16[1040,128]{1,0:T(8,128)(2,1)S(1)}, u32[]{:S(2)}, u32[]{:S(2)}) collective-permute-start(bf16[1040,128]{1,0:T(8,128)(2,1)S(1)} %get-tuple-element.27.refs_0_), channel_id=1, source_target_pairs={{0,16},{8,24},{16,0},{24,8},{1,17},{9,25},{17,1},{25,9},{2,18},{10... | collective-permute-start | bytes 798728 | tf_op jit(solution)/shard_map/exchange/ppermute | solution.py:214
  8.1 6.9 %collective-permute-start.5 = (bf16[528,128]{1,0:T(8,128)(2,1)S(1)}, bf16[528,128]{1,0:T(8,128)(2,1)S(1)}, u32[]{:S(2)}, u32[]{:S(2)}) collective-permute-start(bf16[528,128]{1,0:T(8,128)(2,1)S(1)} %get-tuple-element.39.q_ref), channel_id=1, source_target_pairs={{0,2},{1,3},{2,0},{3,1},{4,6},{5,7},{6,4},{7,5},{8,10},{9,11},{10,... | collective-permute-start | bytes 405512 | tf_op jit(solution)/shard_map/exchange/ppermute | solution.py:220
  9.7 9.5 %collective-permute-start.6 = (bf16[528,128]{1,0:T(8,128)(2,1)S(1)}, bf16[528,128]{1,0:T(8,128)(2,1)S(1)}, u32[]{:S(2)}, u32[]{:S(2)}) collective-permute-start(bf16[528,128]{1,0:T(8,128)(2,1)S(1)} %get-tuple-element.39.q_ref), channel_id=1, source_target_pairs={{0,6},{1,7},{2,4},{3,5},{4,2},{5,3},{6,0},{7,1},{8,14},{9,15},{10,... | collective-permute-start | bytes 405512 | tf_op jit(solution)/shard_map/exchange/ppermute | solution.py:220
  13.1 6.0 %collective-permute-start.9 = (bf16[528,128]{1,0:T(8,128)(2,1)S(1)}, bf16[528,128]{1,0:T(8,128)(2,1)S(1)}, u32[]{:S(2)}, u32[]{:S(2)}) collective-permute-start(bf16[528,128]{1,0:T(8,128)(2,1)S(1)} %slice.8), channel_id=1, source_target_pairs={{0,16},{8,24},{16,0},{24,8},{1,17},{9,25},{17,1},{25,9},{2,18},{10... | collective-permute-start | bytes 405512 | tf_op jit(solution)/shard_map/exchange/ppermute | solution.py:214
  15.0 5.0 %collective-permute-start.10 = (bf16[512,128]{1,0:T(8,128)(2,1)S(1)}, bf16[512,128]{1,0:T(8,128)(2,1)S(1)}, u32[]{:S(2)}, u32[]{:S(2)}) collective-permute-start(bf16[512,128]{1,0:T(8,128)(2,1)S(1)} %slice.9), channel_id=1, source_target_pairs={{0,8},{8,0},{16,24},{24,16},{1,9},{9,1},{17,25},{25,17},{2,10},{10... | collective-permute-start | bytes 393224 | tf_op jit(solution)/shard_map/exchange/ppermute | solution.py:214
  16.6 8.0 %collective-permute-start.4 = (bf16[528,128]{1,0:T(8,128)(2,1)S(1)}, bf16[528,128]{1,0:T(8,128)(2,1)S(1)}, u32[]{:S(2)}, u32[]{:S(2)}) collective-permute-start(bf16[528,128]{1,0:T(8,128)(2,1)S(1)} %get-tuple-element.39.q_ref), channel_id=1, source_target_pairs={{0,4},{1,5},{2,6},{3,7},{4,0},{5,1},{6,2},{7,3},{8,12},{9,13},{10,... | collective-permute-start | bytes 405512 | tf_op jit(solution)/shard_map/exchange/ppermute | solution.py:220
  20.4 6.3 %collective-permute-start.11 = (bf16[544,128]{1,0:T(8,128)(2,1)S(1)}, bf16[544,128]{1,0:T(8,128)(2,1)S(1)}, u32[]{:S(2)}, u32[]{:S(2)}) collective-permute-start(bf16[544,128]{1,0:T(8,128)(2,1)S(1)} %apply.4), channel_id=1, source_target_pairs={{0,2},{1,3},{2,0},{3,1},{4,6},{5,7},{6,4},{7,5},{8,10},{9,11},{10,... | collective-permute-start | bytes 417800 | tf_op jit(solution)/shard_map/return/ppermute | solution.py:286
  23.1 9.1 %collective-permute-start.15 = (bf16[272,128]{1,0:T(8,128)(2,1)S(1)}, bf16[272,128]{1,0:T(8,128)(2,1)S(1)}, u32[]{:S(2)}, u32[]{:S(2)}) collective-permute-start(bf16[272,128]{1,0:T(8,128)(2,1)S(1)} %get-tuple-element.34), channel_id=1, source_target_pairs={{0,2},{1,3},{2,0},{3,1},{4,6},{5,7},{6,4},{7,5},{8,10},{9,11},{10,... | collective-permute-start | bytes 208904 | tf_op jit(solution)/shard_map/return/ppermute | solution.py:284
  26.8 9.1 %collective-permute-start.13 = (bf16[272,128]{1,0:T(8,128)(2,1)S(1)}, bf16[272,128]{1,0:T(8,128)(2,1)S(1)}, u32[]{:S(2)}, u32[]{:S(2)}) collective-permute-start(bf16[272,128]{1,0:T(8,128)(2,1)S(1)} %get-tuple-element.38), channel_id=1, source_target_pairs={{0,4},{1,5},{2,6},{3,7},{4,0},{5,1},{6,2},{7,3},{8,12},{9,13},{10,... | collective-permute-start | bytes 208904 | tf_op jit(solution)/shard_map/return/ppermute | solution.py:284
  28.7 7.2 %collective-permute-start.14 = (bf16[272,128]{1,0:T(8,128)(2,1)S(1)}, bf16[272,128]{1,0:T(8,128)(2,1)S(1)}, u32[]{:S(2)}, u32[]{:S(2)}) collective-permute-start(bf16[272,128]{1,0:T(8,128)(2,1)S(1)} %get-tuple-element.44), channel_id=1, source_target_pairs={{0,5},{1,4},{2,7},{3,6},{4,1},{5,0},{6,3},{7,2},{8,13},{9,12},{10,... | collective-permute-start | bytes 208904 | tf_op jit(solution)/shard_map/return/ppermute | solution.py:284
  29.8 6.1 %collective-permute-start.16 = (bf16[272,128]{1,0:T(8,128)(2,1)S(1)}, bf16[272,128]{1,0:T(8,128)(2,1)S(1)}, u32[]{:S(2)}, u32[]{:S(2)}) collective-permute-start(bf16[272,128]{1,0:T(8,128)(2,1)S(1)} %get-tuple-element.46), channel_id=1, source_target_pairs={{0,3},{1,2},{2,1},{3,0},{4,7},{5,6},{6,5},{7,4},{8,11},{9,10},{10,... | collective-permute-start | bytes 208904 | tf_op jit(solution)/shard_map/return/ppermute | solution.py:284
  31.9 4.0 %collective-permute-start.12 = (bf16[272,128]{1,0:T(8,128)(2,1)S(1)}, bf16[272,128]{1,0:T(8,128)(2,1)S(1)}, u32[]{:S(2)}, u32[]{:S(2)}) collective-permute-start(bf16[272,128]{1,0:T(8,128)(2,1)S(1)} %get-tuple-element.43), channel_id=1, source_target_pairs={{0,1},{1,0},{2,3},{3,2},{4,5},{5,4},{6,7},{7,6},{8,9},{9,8},{10,11... | collective-permute-start | bytes 208904 | tf_op jit(solution)/shard_map/return/ppermute | solution.py:307

commit v21 on v19

--- a/solution.py
+++ b/solution.py
@@ -292,7 +292,7 @@
 
     done = None
     weights_by, partial = {}, {}
-    for r in reversed(range(1, chips)):
+    for r in sorted(range(1, chips), key=lambda r: (r != chips - 1, r != 1, -r)):
         done = both_kernels(r, done)
     for r in reversed(range(1, chips)):
         parts = partial[r]

time: 37.9 us -> 36.9 us (0.974)
  the two profiles are of different devices: /device:TPU:0 before, /device:TPU:1 now
where the time goes in v21:
time: 36.9 us; the launch traced here: 36.7 us
  starting transfers between devices  21.5 us (58%)
  waiting for transfers between devices  7.24 us (20%)
  Pallas kernels  6.08 us (16%)
  other arithmetic  1.06 us (3%)
  between operations  0.8 us (2%)
    ppermute x4, starting transfers between devices, send(): lax.ppermute(parts[x], 'inner', along_inner(r, x))  7.09 us
    ppermute x4, starting transfers between devices, over(): return lax.ppermute(a, 'outer', [(o, o ^ r) for o in range(n_out)])  6.03 us
    ppermute x3, starting transfers between devices, shards(): q_by[r] = lax.ppermute(q_piece, 'inner', along_inner(r, 0))  5.8 us
    ppermute x4, waiting for transfers between devices, send(): lax.ppermute(parts[x], 'inner', along_inner(r, x))  3.9 us
    pallas_call x4, Pallas kernels, score(): pl.pallas_call(functools.partial(score_kernel, r == 0), out_shape=(jax.Sh...  3.03 us
    ppermute x4, waiting for transfers between devices, over(): return lax.ppermute(a, 'outer', [(o, o ^ r) for o in range(n_out)])  1.58 us
    ppermute x1, starting transfers between devices, send(): lax.ppermute(parts[0], 'inner', along_inner(low(r), 0))  1.37 us
    pallas_call x4, Pallas kernels, apply(): pl.pallas_call(functools.partial(apply_kernel, wide, rows), out_shape=sha...  1.35 us
  transfers between devices with their start and end apart: 17, of which 5 were waited for; matrix products, arithmetic and copies ran while one was open for 3% of the time, Pallas kernels for 12%

profile of v21, /device:TPU:1, one launch (start us, length us, event | category | flops | bytes accessed | tf_op | source)
XLA Modules:
  0.0 36.7 jit_solution(3095697808685115258)
XLA Ops:
  0.0 0.1 collective-permute-start.1
  0.1 0.5 %collective-permute-start.2 = (bf16[128,512]{1,0:T(8,128)(2,1)}, bf16[128,512]{1,0:T(8,128)(2,1)S(1)}, u32[]{:S(2)}, u32[]{:S(2)}) collective-permute-start(bf16[128,512]{1,0:T(8,128)(2,1)} %param.5), channel_id=1, source_target_pairs={{0,1},{1,0},{2,3},{3,2},{4,5},{5,4},{6,7},{7,6},{8,9},{9,8},{10,11... | collective-permute-start | bytes 393224 | tf_op jit(solution)/shard_map/swap/ppermute | solution.py:186
  0.5 0.1 collective-permute-start.3
  0.6 0.5 %collective-permute-start = (s32[1]{0:T(128)}, s32[1]{0:T(128)}, u32[]{:S(2)}, u32[]{:S(2)}) collective-permute-start(s32[1]{0:T(128)} %param.7), channel_id=1, source_target_pairs={{0,1},{1,0},{2,3},{3,2},{4,5},{5,4},{6,7},{7,6},{8,9},{9,8},{10,11... | collective-permute-start | bytes 20 | tf_op jit(solution)/shard_map/swap/ppermute | solution.py:186
  1.7 1.1 %pad_maximum_fusion.own = bf16[384,512]{1,0:T(8,128)(2,1)S(1)} fusion(bf16[128,512]{1,0:T(8,128)(2,1)} %param.6, bf16[128,512]{1,0:T(8,128)(2,1)} %param.5, bf16[128,512]{1,0:T(8,128)(2,1)} %param.4), kind=kLoop, calls=%fused_computation | loop fusion | flops 1179648 | bytes 786432 | tf_op jit(solution)/shard_map/swap/concatenate | solution.py:187
  2.7 0.0 collective-permute-done.p1
  2.7 0.0 collective-permute-done.1.q1
  2.8 0.0 collective-permute-done.2.k1
  2.8 0.0 collective-permute-done.3.v1
  2.8 0.8 %merge.1 = (bf16[528,128]{1,0:T(8,128)(2,1)S(1)}, bf16[1040,128]{1,0:T(8,128)(2,1)S(1)}) custom-call(s32[1]{0:T(128)S(6)} %copy.5.p0, s32[1]{0:T(128)} %collective-permute-done.p1, bf16[384,512]{1,0:T(8,128)(2,1)S(1)} %pad_maximum_fusion.own, bf16[128,512]{1,0:T(8,128)(2,1)S(1)} %collective-permute-done.1.q1, ...), custom_call_target="tpu_custom_call" | custom-call | tf_op jit(solution)/shard_map/merge/merge/pallas_call | solution.py:190
  3.6 2.3 %collective-permute-start.7 = (bf16[1040,128]{1,0:T(8,128)(2,1)S(1)}, bf16[1040,128]{1,0:T(8,128)(2,1)S(1)}, u32[]{:S(2)}, u32[]{:S(2)}) collective-permute-start(bf16[1040,128]{1,0:T(8,128)(2,1)S(1)} %get-tuple-element.27.refs_0_), channel_id=1, source_target_pairs={{0,8},{8,0},{16,24},{24,16},{1,9},{9,1},{17,25},{25,17},{2,10},{10... | collective-permute-start | bytes 798728 | tf_op jit(solution)/shard_map/exchange/ppermute | solution.py:214
  5.8 1.2 %collective-permute-start.8 = (bf16[1040,128]{1,0:T(8,128)(2,1)S(1)}, bf16[1040,128]{1,0:T(8,128)(2,1)S(1)}, u32[]{:S(2)}, u32[]{:S(2)}) collective-permute-start(bf16[1040,128]{1,0:T(8,128)(2,1)S(1)} %get-tuple-element.27.refs_0_), channel_id=1, source_target_pairs={{0,16},{8,24},{16,0},{24,8},{1,17},{9,25},{17,1},{25,9},{2,18},{10... | collective-permute-start | bytes 798728 | tf_op jit(solution)/shard_map/exchange/ppermute | solution.py:214
  7.1 1.3 %collective-permute-start.5 = (bf16[528,128]{1,0:T(8,128)(2,1)S(1)}, bf16[528,128]{1,0:T(8,128)(2,1)S(1)}, u32[]{:S(2)}, u32[]{:S(2)}) collective-permute-start(bf16[528,128]{1,0:T(8,128)(2,1)S(1)} %get-tuple-element.39.q_ref), channel_id=1, source_target_pairs={{0,2},{1,3},{2,0},{3,1},{4,6},{5,7},{6,4},{7,5},{8,10},{9,11},{10,... | collective-permute-start | bytes 405512 | tf_op jit(solution)/shard_map/exchange/ppermute | solution.py:220
  8.4 2.2 %collective-permute-start.6 = (bf16[528,128]{1,0:T(8,128)(2,1)S(1)}, bf16[528,128]{1,0:T(8,128)(2,1)S(1)}, u32[]{:S(2)}, u32[]{:S(2)}) collective-permute-start(bf16[528,128]{1,0:T(8,128)(2,1)S(1)} %get-tuple-element.39.q_ref), channel_id=1, source_target_pairs={{0,6},{1,7},{2,4},{3,5},{4,2},{5,3},{6,0},{7,1},{8,14},{9,15},{10,... | collective-permute-start | bytes 405512 | tf_op jit(solution)/shard_map/exchange/ppermute | solution.py:220
  10.6 1.6 %collective-permute-done.7.refs_1_ = bf16[1040,128]{1,0:T(8,128)(2,1)S(1)} collective-permute-done((bf16[1040,128]{1,0:T(8,128)(2,1)S(1)}, bf16[1040,128]{1,0:T(8,128)(2,1)S(1)}, u32[]{:S(2)}, u32[]{:S(2)}) %collective-permute-start.7) | collective-permute-done | bytes 266272 | tf_op jit(solution)/shard_map/exchange/ppermute | solution.py:214
  12.2 1.2 %collective-permute-start.9 = (bf16[528,128]{1,0:T(8,128)(2,1)S(1)}, bf16[528,128]{1,0:T(8,128)(2,1)S(1)}, u32[]{:S(2)}, u32[]{:S(2)}) collective-permute-start(bf16[528,128]{1,0:T(8,128)(2,1)S(1)} %slice.8), channel_id=1, source_target_pairs={{0,16},{8,24},{16,0},{24,8},{1,17},{9,25},{17,1},{25,9},{2,18},{10... | collective-permute-start | bytes 405512 | tf_op jit(solution)/shard_map/exchange/ppermute | solution.py:214
  13.4 0.0 collective-permute-done.8.refs_2_
  13.4 0.0 collective-permute-done.5.q_ref
  13.4 1.3 %collective-permute-start.10 = (bf16[512,128]{1,0:T(8,128)(2,1)S(1)}, bf16[512,128]{1,0:T(8,128)(2,1)S(1)}, u32[]{:S(2)}, u32[]{:S(2)}) collective-permute-start(bf16[512,128]{1,0:T(8,128)(2,1)S(1)} %slice.9), channel_id=1, source_target_pairs={{0,8},{8,0},{16,24},{24,16},{1,9},{9,1},{17,25},{25,17},{2,10},{10... | collective-permute-start | bytes 393224 | tf_op jit(solution)/shard_map/exchange/ppermute | solution.py:214
  14.7 2.3 %collective-permute-start.4 = (bf16[528,128]{1,0:T(8,128)(2,1)S(1)}, bf16[528,128]{1,0:T(8,128)(2,1)S(1)}, u32[]{:S(2)}, u32[]{:S(2)}) collective-permute-start(bf16[528,128]{1,0:T(8,128)(2,1)S(1)} %get-tuple-element.39.q_ref), channel_id=1, source_target_pairs={{0,4},{1,5},{2,6},{3,7},{4,0},{5,1},{6,2},{7,3},{8,12},{9,13},{10,... | collective-permute-start | bytes 405512 | tf_op jit(solution)/shard_map/exchange/ppermute | solution.py:220
  17.0 0.0 collective-permute-done.6.q_ref
  17.0 0.0 collective-permute-done.9.refs_3_
  17.0 0.8 %score.4 = (bf16[2,1024,256]{2,1,0:T(8,128)(2,1)S(1)}, f32[16,256]{1,0:T(8,128)S(1)}) custom-call(bf16[528,128]{1,0:T(8,128)(2,1)S(1)} %collective-permute-done.6.q_ref, bf16[1040,128]{1,0:T(8,128)(2,1)S(1)} %get-tuple-element.27.refs_0_, bf16[1040,128]{1,0:T(8,128)(2,1)S(1)} %collective-permute-done.7.refs_1_, ...), custom_call_target="tpu_custom_call" | custom-call | flops 134217728 | bytes 1048576 | tf_op jit(solution)/shard_map/score/score/pallas_call | solution.py:242
  17.8 0.0 collective-permute-done.10.refs_3_
  17.8 0.3 apply.4
  18.1 1.4 %collective-permute-start.11 = (bf16[544,128]{1,0:T(8,128)(2,1)S(1)}, bf16[544,128]{1,0:T(8,128)(2,1)S(1)}, u32[]{:S(2)}, u32[]{:S(2)}) collective-permute-start(bf16[544,128]{1,0:T(8,128)(2,1)S(1)} %apply.4), channel_id=1, source_target_pairs={{0,2},{1,3},{2,0},{3,1},{4,6},{5,7},{6,4},{7,5},{8,10},{9,11},{10,... | collective-permute-start | bytes 417800 | tf_op jit(solution)/shard_map/return/ppermute | solution.py:286
  19.5 0.8 %score.5 = (bf16[2,1024,256]{2,1,0:T(8,128)(2,1)S(1)}, f32[16,256]{1,0:T(8,128)S(1)}) custom-call(bf16[528,128]{1,0:T(8,128)(2,1)S(1)} %collective-permute-done.5.q_ref, bf16[1040,128]{1,0:T(8,128)(2,1)S(1)} %get-tuple-element.27.refs_0_, bf16[1040,128]{1,0:T(8,128)(2,1)S(1)} %collective-permute-done.7.refs_1_, ...), custom_call_target="tpu_custom_call" | custom-call | flops 134217728 | bytes 1048576 | tf_op jit(solution)/shard_map/score/score/pallas_call | solution.py:242
  20.3 0.3 apply.5
  20.6 0.2 collective-permute-start.15
  20.8 0.6 %collective-permute-done.4.q_ref = bf16[528,128]{1,0:T(8,128)(2,1)S(1)} collective-permute-done((bf16[528,128]{1,0:T(8,128)(2,1)S(1)}, bf16[528,128]{1,0:T(8,128)(2,1)S(1)}, u32[]{:S(2)}, u32[]{:S(2)}) %collective-permute-start.4) | collective-permute-done | bytes 135200 | tf_op jit(solution)/shard_map/exchange/ppermute | solution.py:220
  21.5 0.8 %score.6 = (bf16[2,1024,256]{2,1,0:T(8,128)(2,1)S(1)}, f32[16,256]{1,0:T(8,128)S(1)}) custom-call(bf16[528,128]{1,0:T(8,128)(2,1)S(1)} %collective-permute-done.4.q_ref, bf16[1040,128]{1,0:T(8,128)(2,1)S(1)} %get-tuple-element.27.refs_0_, bf16[1040,128]{1,0:T(8,128)(2,1)S(1)} %collective-permute-done.7.refs_1_, ...), custom_call_target="tpu_custom_call" | custom-call | flops 134217728 | bytes 1048576 | tf_op jit(solution)/shard_map/score/score/pallas_call | solution.py:242
  22.2 0.3 apply.6.refs_0_
  22.6 1.1 %collective-permute-done.11.refs_1_ = bf16[544,128]{1,0:T(8,128)(2,1)S(1)} collective-permute-done((bf16[544,128]{1,0:T(8,128)(2,1)S(1)}, bf16[544,128]{1,0:T(8,128)(2,1)S(1)}, u32[]{:S(2)}, u32[]{:S(2)}) %collective-permute-start.11) | collective-permute-done | bytes 139296 | tf_op jit(solution)/shard_map/return/ppermute | solution.py:286
  23.7 0.1 add.1
  23.8 1.3 %collective-permute-start.13 = (bf16[272,128]{1,0:T(8,128)(2,1)S(1)}, bf16[272,128]{1,0:T(8,128)(2,1)S(1)}, u32[]{:S(2)}, u32[]{:S(2)}) collective-permute-start(bf16[272,128]{1,0:T(8,128)(2,1)S(1)} %get-tuple-element.38), channel_id=1, source_target_pairs={{0,4},{1,5},{2,6},{3,7},{4,0},{5,1},{6,2},{7,3},{8,12},{9,13},{10,... | collective-permute-start | bytes 208904 | tf_op jit(solution)/shard_map/return/ppermute | solution.py:284
  25.1 5.5 %collective-permute-start.16 = (bf16[272,128]{1,0:T(8,128)(2,1)S(1)}, bf16[272,128]{1,0:T(8,128)(2,1)S(1)}, u32[]{:S(2)}, u32[]{:S(2)}) collective-permute-start(bf16[272,128]{1,0:T(8,128)(2,1)S(1)} %get-tuple-element.46), channel_id=1, source_target_pairs={{0,3},{1,2},{2,1},{3,0},{4,7},{5,6},{6,5},{7,4},{8,11},{9,10},{10,... | collective-permute-start | bytes 208904 | tf_op jit(solution)/shard_map/return/ppermute | solution.py:284
  30.6 0.0 collective-permute-start.14
  30.6 0.8 %score.7 = (bf16[2,1024,256]{2,1,0:T(8,128)(2,1)S(1)}, f32[16,256]{1,0:T(8,128)S(1)}) custom-call(bf16[528,128]{1,0:T(8,128)(2,1)S(1)} %get-tuple-element.39.q_ref, bf16[1040,128]{1,0:T(8,128)(2,1)S(1)} %get-tuple-element.27.refs_0_, bf16[1040,128]{1,0:T(8,128)(2,1)S(1)} %collective-permute-done.7.refs_1_, ...), custom_call_target="tpu_custom_call" | custom-call | flops 134217728 | bytes 1048576 | tf_op jit(solution)/shard_map/score/score/pallas_call | solution.py:242
  31.4 0.3 apply.7
  31.8 0.2 collective-permute-start.12
  32.0 0.0 collective-permute-done.15.refs_4_
  32.0 1.7 %collective-permute-done.16.refs_5_ = bf16[272,128]{1,0:T(8,128)(2,1)S(1)} collective-permute-done((bf16[272,128]{1,0:T(8,128)(2,1)S(1)}, bf16[272,128]{1,0:T(8,128)(2,1)S(1)}, u32[]{:S(2)}, u32[]{:S(2)}) %collective-permute-start.16) | collective-permute-done | bytes 69664 | tf_op jit(solution)/shard_map/return/ppermute | solution.py:284
  33.7 2.2 %collective-permute-done.14.refs_3_ = bf16[272,128]{1,0:T(8,128)(2,1)S(1)} collective-permute-done((bf16[272,128]{1,0:T(8,128)(2,1)S(1)}, bf16[272,128]{1,0:T(8,128)(2,1)S(1)}, u32[]{:S(2)}, u32[]{:S(2)}) %collective-permute-start.14) | collective-permute-done | bytes 69664 | tf_op jit(solution)/shard_map/return/ppermute | solution.py:284
  35.9 0.0 collective-permute-done.13.refs_2_
  35.9 0.0 collective-permute-done.12.refs_1_
  35.9 0.8 %combine.1 = bf16[128,512]{1,0:T(8,128)(2,1)} custom-call(bf16[272,128]{1,0:T(8,128)(2,1)S(1)} %get-tuple-element.42.refs_0_, bf16[272,128]{1,0:T(8,128)(2,1)S(1)} %collective-permute-done.12.refs_1_, bf16[272,128]{1,0:T(8,128)(2,1)S(1)} %collective-permute-done.13.refs_2_, bf16[272,128]{1,0:T(8,128)(2,1)S(1)} %collective-permute-done.14.refs_3_, ...), custom_call_target="tpu_custom_call" | custom-call | tf_op jit(solution)/shard_map/combine/combine/pallas_call | solution.py:309
  (2 shorter events, 0.0 us)
Async XLA Ops:
  0.0 2.7 %collective-permute-start.1 = (bf16[128,512]{1,0:T(8,128)(2,1)}, bf16[128,512]{1,0:T(8,128)(2,1)S(1)}, u32[]{:S(2)}, u32[]{:S(2)}) collective-permute-start(bf16[128,512]{1,0:T(8,128)(2,1)} %param.4), channel_id=1, source_target_pairs={{0,1},{1,0},{2,3},{3,2},{4,5},{5,4},{6,7},{7,6},{8,9},{9,8},{10,11... | collective-permute-start | bytes 393224 | tf_op jit(solution)/shard_map/swap/ppermute | solution.py:186
  0.1 2.7 %collective-permute-start.2 = (bf16[128,512]{1,0:T(8,128)(2,1)}, bf16[128,512]{1,0:T(8,128)(2,1)S(1)}, u32[]{:S(2)}, u32[]{:S(2)}) collective-permute-start(bf16[128,512]{1,0:T(8,128)(2,1)} %param.5), channel_id=1, source_target_pairs={{0,1},{1,0},{2,3},{3,2},{4,5},{5,4},{6,7},{7,6},{8,9},{9,8},{10,11... | collective-permute-start | bytes 393224 | tf_op jit(solution)/shard_map/swap/ppermute | solution.py:186
  0.5 2.3 %collective-permute-start.3 = (bf16[128,512]{1,0:T(8,128)(2,1)}, bf16[128,512]{1,0:T(8,128)(2,1)S(1)}, u32[]{:S(2)}, u32[]{:S(2)}) collective-permute-start(bf16[128,512]{1,0:T(8,128)(2,1)} %param.6), channel_id=1, source_target_pairs={{0,1},{1,0},{2,3},{3,2},{4,5},{5,4},{6,7},{7,6},{8,9},{9,8},{10,11... | collective-permute-start | bytes 393224 | tf_op jit(solution)/shard_map/swap/ppermute | solution.py:186
  0.6 2.2 %collective-permute-start = (s32[1]{0:T(128)}, s32[1]{0:T(128)}, u32[]{:S(2)}, u32[]{:S(2)}) collective-permute-start(s32[1]{0:T(128)} %param.7), channel_id=1, source_target_pairs={{0,1},{1,0},{2,3},{3,2},{4,5},{5,4},{6,7},{7,6},{8,9},{9,8},{10,11... | collective-permute-start | bytes 20 | tf_op jit(solution)/shard_map/swap/ppermute | solution.py:186
  3.6 8.6 %collective-permute-start.7 = (bf16[1040,128]{1,0:T(8,128)(2,1)S(1)}, bf16[1040,128]{1,0:T(8,128)(2,1)S(1)}, u32[]{:S(2)}, u32[]{:S(2)}) collective-permute-start(bf16[1040,128]{1,0:T(8,128)(2,1)S(1)} %get-tuple-element.27.refs_0_), channel_id=1, source_target_pairs={{0,8},{8,0},{16,24},{24,16},{1,9},{9,1},{17,25},{25,17},{2,10},{10... | collective-permute-start | bytes 798728 | tf_op jit(solution)/shard_map/exchange/ppermute | solution.py:214
  5.8 7.6 %collective-permute-start.8 = (bf16[1040,128]{1,0:T(8,128)(2,1)S(1)}, bf16[1040,128]{1,0:T(8,128)(2,1)S(1)}, u32[]{:S(2)}, u32[]{:S(2)}) collective-permute-start(bf16[1040,128]{1,0:T(8,128)(2,1)S(1)} %get-tuple-element.27.refs_0_), channel_id=1, source_target_pairs={{0,16},{8,24},{16,0},{24,8},{1,17},{9,25},{17,1},{25,9},{2,18},{10... | collective-permute-start | bytes 798728 | tf_op jit(solution)/shard_map/exchange/ppermute | solution.py:214
  7.1 6.3 %collective-permute-start.5 = (bf16[528,128]{1,0:T(8,128)(2,1)S(1)}, bf16[528,128]{1,0:T(8,128)(2,1)S(1)}, u32[]{:S(2)}, u32[]{:S(2)}) collective-permute-start(bf16[528,128]{1,0:T(8,128)(2,1)S(1)} %get-tuple-element.39.q_ref), channel_id=1, source_target_pairs={{0,2},{1,3},{2,0},{3,1},{4,6},{5,7},{6,4},{7,5},{8,10},{9,11},{10,... | collective-permute-start | bytes 405512 | tf_op jit(solution)/shard_map/exchange/ppermute | solution.py:220
  8.4 8.6 %collective-permute-start.6 = (bf16[528,128]{1,0:T(8,128)(2,1)S(1)}, bf16[528,128]{1,0:T(8,128)(2,1)S(1)}, u32[]{:S(2)}, u32[]{:S(2)}) collective-permute-start(bf16[528,128]{1,0:T(8,128)(2,1)S(1)} %get-tuple-element.39.q_ref), channel_id=1, source_target_pairs={{0,6},{1,7},{2,4},{3,5},{4,2},{5,3},{6,0},{7,1},{8,14},{9,15},{10,... | collective-permute-start | bytes 405512 | tf_op jit(solution)/shard_map/exchange/ppermute | solution.py:220
  12.2 4.9 %collective-permute-start.9 = (bf16[528,128]{1,0:T(8,128)(2,1)S(1)}, bf16[528,128]{1,0:T(8,128)(2,1)S(1)}, u32[]{:S(2)}, u32[]{:S(2)}) collective-permute-start(bf16[528,128]{1,0:T(8,128)(2,1)S(1)} %slice.8), channel_id=1, source_target_pairs={{0,16},{8,24},{16,0},{24,8},{1,17},{9,25},{17,1},{25,9},{2,18},{10... | collective-permute-start | bytes 405512 | tf_op jit(solution)/shard_map/exchange/ppermute | solution.py:214
  13.4 4.4 %collective-permute-start.10 = (bf16[512,128]{1,0:T(8,128)(2,1)S(1)}, bf16[512,128]{1,0:T(8,128)(2,1)S(1)}, u32[]{:S(2)}, u32[]{:S(2)}) collective-permute-start(bf16[512,128]{1,0:T(8,128)(2,1)S(1)} %slice.9), channel_id=1, source_target_pairs={{0,8},{8,0},{16,24},{24,16},{1,9},{9,1},{17,25},{25,17},{2,10},{10... | collective-permute-start | bytes 393224 | tf_op jit(solution)/shard_map/exchange/ppermute | solution.py:214
  14.7 6.8 %collective-permute-start.4 = (bf16[528,128]{1,0:T(8,128)(2,1)S(1)}, bf16[528,128]{1,0:T(8,128)(2,1)S(1)}, u32[]{:S(2)}, u32[]{:S(2)}) collective-permute-start(bf16[528,128]{1,0:T(8,128)(2,1)S(1)} %get-tuple-element.39.q_ref), channel_id=1, source_target_pairs={{0,4},{1,5},{2,6},{3,7},{4,0},{5,1},{6,2},{7,3},{8,12},{9,13},{10,... | collective-permute-start | bytes 405512 | tf_op jit(solution)/shard_map/exchange/ppermute | solution.py:220
  18.1 5.6 %collective-permute-start.11 = (bf16[544,128]{1,0:T(8,128)(2,1)S(1)}, bf16[544,128]{1,0:T(8,128)(2,1)S(1)}, u32[]{:S(2)}, u32[]{:S(2)}) collective-permute-start(bf16[544,128]{1,0:T(8,128)(2,1)S(1)} %apply.4), channel_id=1, source_target_pairs={{0,2},{1,3},{2,0},{3,1},{4,6},{5,7},{6,4},{7,5},{8,10},{9,11},{10,... | collective-permute-start | bytes 417800 | tf_op jit(solution)/shard_map/return/ppermute | solution.py:286
  20.6 11.4 %collective-permute-start.15 = (bf16[272,128]{1,0:T(8,128)(2,1)S(1)}, bf16[272,128]{1,0:T(8,128)(2,1)S(1)}, u32[]{:S(2)}, u32[]{:S(2)}) collective-permute-start(bf16[272,128]{1,0:T(8,128)(2,1)S(1)} %get-tuple-element.34), channel_id=1, source_target_pairs={{0,2},{1,3},{2,0},{3,1},{4,6},{5,7},{6,4},{7,5},{8,10},{9,11},{10,... | collective-permute-start | bytes 208904 | tf_op jit(solution)/shard_map/return/ppermute | solution.py:284
  23.8 12.1 %collective-permute-start.13 = (bf16[272,128]{1,0:T(8,128)(2,1)S(1)}, bf16[272,128]{1,0:T(8,128)(2,1)S(1)}, u32[]{:S(2)}, u32[]{:S(2)}) collective-permute-start(bf16[272,128]{1,0:T(8,128)(2,1)S(1)} %get-tuple-element.38), channel_id=1, source_target_pairs={{0,4},{1,5},{2,6},{3,7},{4,0},{5,1},{6,2},{7,3},{8,12},{9,13},{10,... | collective-permute-start | bytes 208904 | tf_op jit(solution)/shard_map/return/ppermute | solution.py:284
  25.1 8.6 %collective-permute-start.16 = (bf16[272,128]{1,0:T(8,128)(2,1)S(1)}, bf16[272,128]{1,0:T(8,128)(2,1)S(1)}, u32[]{:S(2)}, u32[]{:S(2)}) collective-permute-start(bf16[272,128]{1,0:T(8,128)(2,1)S(1)} %get-tuple-element.46), channel_id=1, source_target_pairs={{0,3},{1,2},{2,1},{3,0},{4,7},{5,6},{6,5},{7,4},{8,11},{9,10},{10,... | collective-permute-start | bytes 208904 | tf_op jit(solution)/shard_map/return/ppermute | solution.py:284
  30.6 5.3 %collective-permute-start.14 = (bf16[272,128]{1,0:T(8,128)(2,1)S(1)}, bf16[272,128]{1,0:T(8,128)(2,1)S(1)}, u32[]{:S(2)}, u32[]{:S(2)}) collective-permute-start(bf16[272,128]{1,0:T(8,128)(2,1)S(1)} %get-tuple-element.44), channel_id=1, source_target_pairs={{0,5},{1,4},{2,7},{3,6},{4,1},{5,0},{6,3},{7,2},{8,13},{9,12},{10,... | collective-permute-start | bytes 208904 | tf_op jit(solution)/shard_map/return/ppermute | solution.py:284
  31.8 4.2 %collective-permute-start.12 = (bf16[272,128]{1,0:T(8,128)(2,1)S(1)}, bf16[272,128]{1,0:T(8,128)(2,1)S(1)}, u32[]{:S(2)}, u32[]{:S(2)}) collective-permute-start(bf16[272,128]{1,0:T(8,128)(2,1)S(1)} %get-tuple-element.43), channel_id=1, source_target_pairs={{0,1},{1,0},{2,3},{3,2},{4,5},{5,4},{6,7},{7,6},{8,9},{9,8},{10,11... | collective-permute-start | bytes 208904 | tf_op jit(solution)/shard_map/return/ppermute | solution.py:307

commit v22 on v21

--- a/solution.py
+++ b/solution.py
@@ -294,13 +294,14 @@
     weights_by, partial = {}, {}
     for r in sorted(range(1, chips), key=lambda r: (r != chips - 1, r != 1, -r)):
         done = both_kernels(r, done)
+    last = done
     for r in reversed(range(1, chips)):
         parts = partial[r]
         if arrived[r]:
             parts = add([parts[0], *arrived[r]], not single(r))
             done = parts[0]
         if r == 1:
-            parts = [parts[0], after(parts[1], done)]
+            parts = [parts[0], after(parts[1], last)]
         send(r, parts)
     both_kernels(0, done)
     with jax.named_scope("return"):

time: 36.9 us -> 37.7 us (1.022)
  the two profiles are of different devices: /device:TPU:1 before, /device:TPU:0 now
where the time goes in v22:
time: 37.7 us; the launch traced here: 37.6 us
  starting transfers between devices  21 us (56%)
  waiting for transfers between devices  8.6 us (23%)
  Pallas kernels  6.07 us (16%)
  other arithmetic  1.06 us (3%)
  between operations  0.8 us (2%)
    ppermute x4, starting transfers between devices, over(): return lax.ppermute(a, 'outer', [(o, o ^ r) for o in range(n_out)])  7.91 us
    ppermute x3, starting transfers between devices, shards(): q_by[r] = lax.ppermute(q_piece, 'inner', along_inner(r, 0))  6.64 us
    ppermute x4, waiting for transfers between devices, send(): lax.ppermute(parts[x], 'inner', along_inner(r, x))  5.59 us
    ppermute x4, starting transfers between devices, send(): lax.ppermute(parts[x], 'inner', along_inner(r, x))  3.66 us
    pallas_call x4, Pallas kernels, score(): pl.pallas_call(functools.partial(score_kernel, r == 0), out_shape=(jax.Sh...  3.02 us
    ppermute x1, starting transfers between devices, send(): lax.ppermute(parts[0], 'inner', along_inner(low(r), 0))  1.64 us
    pallas_call x4, Pallas kernels, apply(): pl.pallas_call(functools.partial(apply_kernel, wide, rows), out_shape=sha...  1.36 us
    ppermute x4, waiting for transfers between devices, over(): return lax.ppermute(a, 'outer', [(o, o ^ r) for o in range(n_out)])  1.12 us
  transfers between devices with their start and end apart: 17, of which 5 were waited for; matrix products, arithmetic and copies ran while one was open for 3% of the time, Pallas kernels for 12%

profile of v22, /device:TPU:0, one launch (start us, length us, event | category | flops | bytes accessed | tf_op | source)
XLA Modules:
  0.0 37.6 jit_solution(5074652245016097537)
XLA Ops:
  0.0 0.5 %collective-permute-start.1 = (bf16[128,512]{1,0:T(8,128)(2,1)}, bf16[128,512]{1,0:T(8,128)(2,1)S(1)}, u32[]{:S(2)}, u32[]{:S(2)}) collective-permute-start(bf16[128,512]{1,0:T(8,128)(2,1)} %param.4), channel_id=1, source_target_pairs={{0,1},{1,0},{2,3},{3,2},{4,5},{5,4},{6,7},{7,6},{8,9},{9,8},{10,11... | collective-permute-start | bytes 393224 | tf_op jit(solution)/shard_map/swap/ppermute | solution.py:186
  0.5 0.1 collective-permute-start.2
  0.5 0.5 %collective-permute-start.3 = (bf16[128,512]{1,0:T(8,128)(2,1)}, bf16[128,512]{1,0:T(8,128)(2,1)S(1)}, u32[]{:S(2)}, u32[]{:S(2)}) collective-permute-start(bf16[128,512]{1,0:T(8,128)(2,1)} %param.6), channel_id=1, source_target_pairs={{0,1},{1,0},{2,3},{3,2},{4,5},{5,4},{6,7},{7,6},{8,9},{9,8},{10,11... | collective-permute-start | bytes 393224 | tf_op jit(solution)/shard_map/swap/ppermute | solution.py:186
  1.0 0.1 collective-permute-start
  1.7 1.1 %pad_maximum_fusion.own = bf16[384,512]{1,0:T(8,128)(2,1)S(1)} fusion(bf16[128,512]{1,0:T(8,128)(2,1)} %param.6, bf16[128,512]{1,0:T(8,128)(2,1)} %param.5, bf16[128,512]{1,0:T(8,128)(2,1)} %param.4), kind=kLoop, calls=%fused_computation | loop fusion | flops 1179648 | bytes 786432 | tf_op jit(solution)/shard_map/swap/concatenate | solution.py:187
  2.7 0.0 collective-permute-done.p1
  2.7 0.0 collective-permute-done.1.q1
  2.8 0.0 collective-permute-done.2.k1
  2.8 0.0 collective-permute-done.3.v1
  2.8 0.8 %merge.1 = (bf16[528,128]{1,0:T(8,128)(2,1)S(1)}, bf16[1040,128]{1,0:T(8,128)(2,1)S(1)}) custom-call(s32[1]{0:T(128)S(6)} %copy.5.p0, s32[1]{0:T(128)} %collective-permute-done.p1, bf16[384,512]{1,0:T(8,128)(2,1)S(1)} %pad_maximum_fusion.own, bf16[128,512]{1,0:T(8,128)(2,1)S(1)} %collective-permute-done.1.q1, ...), custom_call_target="tpu_custom_call" | custom-call | tf_op jit(solution)/shard_map/merge/merge/pallas_call | solution.py:190
  3.6 3.0 %collective-permute-start.7 = (bf16[1040,128]{1,0:T(8,128)(2,1)S(1)}, bf16[1040,128]{1,0:T(8,128)(2,1)S(1)}, u32[]{:S(2)}, u32[]{:S(2)}) collective-permute-start(bf16[1040,128]{1,0:T(8,128)(2,1)S(1)} %get-tuple-element.27.refs_0_), channel_id=1, source_target_pairs={{0,8},{8,0},{16,24},{24,16},{1,9},{9,1},{17,25},{25,17},{2,10},{10... | collective-permute-start | bytes 798728 | tf_op jit(solution)/shard_map/exchange/ppermute | solution.py:214
  6.6 1.5 %collective-permute-start.8 = (bf16[1040,128]{1,0:T(8,128)(2,1)S(1)}, bf16[1040,128]{1,0:T(8,128)(2,1)S(1)}, u32[]{:S(2)}, u32[]{:S(2)}) collective-permute-start(bf16[1040,128]{1,0:T(8,128)(2,1)S(1)} %get-tuple-element.27.refs_0_), channel_id=1, source_target_pairs={{0,16},{8,24},{16,0},{24,8},{1,17},{9,25},{17,1},{25,9},{2,18},{10... | collective-permute-start | bytes 798728 | tf_op jit(solution)/shard_map/exchange/ppermute | solution.py:214
  8.1 1.6 %collective-permute-start.5 = (bf16[528,128]{1,0:T(8,128)(2,1)S(1)}, bf16[528,128]{1,0:T(8,128)(2,1)S(1)}, u32[]{:S(2)}, u32[]{:S(2)}) collective-permute-start(bf16[528,128]{1,0:T(8,128)(2,1)S(1)} %get-tuple-element.39.q_ref), channel_id=1, source_target_pairs={{0,2},{1,3},{2,0},{3,1},{4,6},{5,7},{6,4},{7,5},{8,10},{9,11},{10,... | collective-permute-start | bytes 405512 | tf_op jit(solution)/shard_map/exchange/ppermute | solution.py:220
  9.7 2.5 %collective-permute-start.6 = (bf16[528,128]{1,0:T(8,128)(2,1)S(1)}, bf16[528,128]{1,0:T(8,128)(2,1)S(1)}, u32[]{:S(2)}, u32[]{:S(2)}) collective-permute-start(bf16[528,128]{1,0:T(8,128)(2,1)S(1)} %get-tuple-element.39.q_ref), channel_id=1, source_target_pairs={{0,6},{1,7},{2,4},{3,5},{4,2},{5,3},{6,0},{7,1},{8,14},{9,15},{10,... | collective-permute-start | bytes 405512 | tf_op jit(solution)/shard_map/exchange/ppermute | solution.py:220
  12.1 1.0 %collective-permute-done.7.refs_1_ = bf16[1040,128]{1,0:T(8,128)(2,1)S(1)} collective-permute-done((bf16[1040,128]{1,0:T(8,128)(2,1)S(1)}, bf16[1040,128]{1,0:T(8,128)(2,1)S(1)}, u32[]{:S(2)}, u32[]{:S(2)}) %collective-permute-start.7) | collective-permute-done | bytes 266272 | tf_op jit(solution)/shard_map/exchange/ppermute | solution.py:214
  13.1 1.8 %collective-permute-start.9 = (bf16[528,128]{1,0:T(8,128)(2,1)S(1)}, bf16[528,128]{1,0:T(8,128)(2,1)S(1)}, u32[]{:S(2)}, u32[]{:S(2)}) collective-permute-start(bf16[528,128]{1,0:T(8,128)(2,1)S(1)} %slice.8), channel_id=1, source_target_pairs={{0,16},{8,24},{16,0},{24,8},{1,17},{9,25},{17,1},{25,9},{2,18},{10... | collective-permute-start | bytes 405512 | tf_op jit(solution)/shard_map/exchange/ppermute | solution.py:214
  15.0 0.0 collective-permute-done.8.refs_2_
  15.0 0.0 collective-permute-done.5.q_ref
  15.0 1.6 %collective-permute-start.10 = (bf16[512,128]{1,0:T(8,128)(2,1)S(1)}, bf16[512,128]{1,0:T(8,128)(2,1)S(1)}, u32[]{:S(2)}, u32[]{:S(2)}) collective-permute-start(bf16[512,128]{1,0:T(8,128)(2,1)S(1)} %slice.9), channel_id=1, source_target_pairs={{0,8},{8,0},{16,24},{24,16},{1,9},{9,1},{17,25},{25,17},{2,10},{10... | collective-permute-start | bytes 393224 | tf_op jit(solution)/shard_map/exchange/ppermute | solution.py:214
  16.6 2.6 %collective-permute-start.4 = (bf16[528,128]{1,0:T(8,128)(2,1)S(1)}, bf16[528,128]{1,0:T(8,128)(2,1)S(1)}, u32[]{:S(2)}, u32[]{:S(2)}) collective-permute-start(bf16[528,128]{1,0:T(8,128)(2,1)S(1)} %get-tuple-element.39.q_ref), channel_id=1, source_target_pairs={{0,4},{1,5},{2,6},{3,7},{4,0},{5,1},{6,2},{7,3},{8,12},{9,13},{10,... | collective-permute-start | bytes 405512 | tf_op jit(solution)/shard_map/exchange/ppermute | solution.py:220
  19.2 0.0 collective-permute-done.6.q_ref
  19.2 0.0 collective-permute-done.9.refs_3_
  19.2 0.8 %score.4 = (bf16[2,1024,256]{2,1,0:T(8,128)(2,1)S(1)}, f32[16,256]{1,0:T(8,128)S(1)}) custom-call(bf16[528,128]{1,0:T(8,128)(2,1)S(1)} %collective-permute-done.6.q_ref, bf16[1040,128]{1,0:T(8,128)(2,1)S(1)} %get-tuple-element.27.refs_0_, bf16[1040,128]{1,0:T(8,128)(2,1)S(1)} %collective-permute-done.7.refs_1_, ...), custom_call_target="tpu_custom_call" | custom-call | flops 134217728 | bytes 1048576 | tf_op jit(solution)/shard_map/score/score/pallas_call | solution.py:242
  19.9 0.1 collective-permute-done.10.refs_3_
  20.0 0.3 apply.4
  20.4 1.6 %collective-permute-start.11 = (bf16[544,128]{1,0:T(8,128)(2,1)S(1)}, bf16[544,128]{1,0:T(8,128)(2,1)S(1)}, u32[]{:S(2)}, u32[]{:S(2)}) collective-permute-start(bf16[544,128]{1,0:T(8,128)(2,1)S(1)} %apply.4), channel_id=1, source_target_pairs={{0,2},{1,3},{2,0},{3,1},{4,6},{5,7},{6,4},{7,5},{8,10},{9,11},{10,... | collective-permute-start | bytes 417800 | tf_op jit(solution)/shard_map/return/ppermute | solution.py:286
  22.0 0.8 %score.5 = (bf16[2,1024,256]{2,1,0:T(8,128)(2,1)S(1)}, f32[16,256]{1,0:T(8,128)S(1)}) custom-call(bf16[528,128]{1,0:T(8,128)(2,1)S(1)} %collective-permute-done.5.q_ref, bf16[1040,128]{1,0:T(8,128)(2,1)S(1)} %get-tuple-element.27.refs_0_, bf16[1040,128]{1,0:T(8,128)(2,1)S(1)} %collective-permute-done.7.refs_1_, ...), custom_call_target="tpu_custom_call" | custom-call | flops 134217728 | bytes 1048576 | tf_op jit(solution)/shard_map/score/score/pallas_call | solution.py:242
  22.8 0.3 apply.5
  23.1 0.5 %collective-permute-start.15 = (bf16[272,128]{1,0:T(8,128)(2,1)S(1)}, bf16[272,128]{1,0:T(8,128)(2,1)S(1)}, u32[]{:S(2)}, u32[]{:S(2)}) collective-permute-start(bf16[272,128]{1,0:T(8,128)(2,1)S(1)} %get-tuple-element.34), channel_id=1, source_target_pairs={{0,2},{1,3},{2,0},{3,1},{4,6},{5,7},{6,4},{7,5},{8,10},{9,11},{10,... | collective-permute-start | bytes 208904 | tf_op jit(solution)/shard_map/return/ppermute | solution.py:284
  23.7 0.9 %collective-permute-done.4.q_ref = bf16[528,128]{1,0:T(8,128)(2,1)S(1)} collective-permute-done((bf16[528,128]{1,0:T(8,128)(2,1)S(1)}, bf16[528,128]{1,0:T(8,128)(2,1)S(1)}, u32[]{:S(2)}, u32[]{:S(2)}) %collective-permute-start.4) | collective-permute-done | bytes 135200 | tf_op jit(solution)/shard_map/exchange/ppermute | solution.py:220
  24.5 0.8 %score.6 = (bf16[2,1024,256]{2,1,0:T(8,128)(2,1)S(1)}, f32[16,256]{1,0:T(8,128)S(1)}) custom-call(bf16[528,128]{1,0:T(8,128)(2,1)S(1)} %collective-permute-done.4.q_ref, bf16[1040,128]{1,0:T(8,128)(2,1)S(1)} %get-tuple-element.27.refs_0_, bf16[1040,128]{1,0:T(8,128)(2,1)S(1)} %collective-permute-done.7.refs_1_, ...), custom_call_target="tpu_custom_call" | custom-call | flops 134217728 | bytes 1048576 | tf_op jit(solution)/shard_map/score/score/pallas_call | solution.py:242
  25.3 0.3 apply.6.refs_0_
  25.6 0.1 collective-permute-start.16
  25.7 1.0 %collective-permute-done.11.refs_1_ = bf16[544,128]{1,0:T(8,128)(2,1)S(1)} collective-permute-done((bf16[544,128]{1,0:T(8,128)(2,1)S(1)}, bf16[544,128]{1,0:T(8,128)(2,1)S(1)}, u32[]{:S(2)}, u32[]{:S(2)}) %collective-permute-start.11) | collective-permute-done | bytes 139296 | tf_op jit(solution)/shard_map/return/ppermute | solution.py:286
  26.7 0.1 add.1
  26.8 1.9 %collective-permute-start.13 = (bf16[272,128]{1,0:T(8,128)(2,1)S(1)}, bf16[272,128]{1,0:T(8,128)(2,1)S(1)}, u32[]{:S(2)}, u32[]{:S(2)}) collective-permute-start(bf16[272,128]{1,0:T(8,128)(2,1)S(1)} %get-tuple-element.38), channel_id=1, source_target_pairs={{0,4},{1,5},{2,6},{3,7},{4,0},{5,1},{6,2},{7,3},{8,12},{9,13},{10,... | collective-permute-start | bytes 208904 | tf_op jit(solution)/shard_map/return/ppermute | solution.py:284
  28.7 1.1 %collective-permute-start.14 = (bf16[272,128]{1,0:T(8,128)(2,1)S(1)}, bf16[272,128]{1,0:T(8,128)(2,1)S(1)}, u32[]{:S(2)}, u32[]{:S(2)}) collective-permute-start(bf16[272,128]{1,0:T(8,128)(2,1)S(1)} %get-tuple-element.44), channel_id=1, source_target_pairs={{0,5},{1,4},{2,7},{3,6},{4,1},{5,0},{6,3},{7,2},{8,13},{9,12},{10,... | collective-permute-start | bytes 208904 | tf_op jit(solution)/shard_map/return/ppermute | solution.py:284
  29.9 0.8 %score.7 = (bf16[2,1024,256]{2,1,0:T(8,128)(2,1)S(1)}, f32[16,256]{1,0:T(8,128)S(1)}) custom-call(bf16[528,128]{1,0:T(8,128)(2,1)S(1)} %get-tuple-element.39.q_ref, bf16[1040,128]{1,0:T(8,128)(2,1)S(1)} %get-tuple-element.27.refs_0_, bf16[1040,128]{1,0:T(8,128)(2,1)S(1)} %collective-permute-done.7.refs_1_, ...), custom_call_target="tpu_custom_call" | custom-call | flops 134217728 | bytes 1048576 | tf_op jit(solution)/shard_map/score/score/pallas_call | solution.py:242
  30.6 0.3 apply.7
  31.0 0.1 collective-permute-start.12
  31.1 0.0 collective-permute-done.15.refs_4_
  31.1 0.0 collective-permute-done.16.refs_5_
  31.1 5.6 %collective-permute-done.14.refs_3_ = bf16[272,128]{1,0:T(8,128)(2,1)S(1)} collective-permute-done((bf16[272,128]{1,0:T(8,128)(2,1)S(1)}, bf16[272,128]{1,0:T(8,128)(2,1)S(1)}, u32[]{:S(2)}, u32[]{:S(2)}) %collective-permute-start.14) | collective-permute-done | bytes 69664 | tf_op jit(solution)/shard_map/return/ppermute | solution.py:284
  36.7 0.0 collective-permute-done.13.refs_2_
  36.7 0.0 collective-permute-done.12.refs_1_
  36.7 0.8 %combine.1 = bf16[128,512]{1,0:T(8,128)(2,1)} custom-call(bf16[272,128]{1,0:T(8,128)(2,1)S(1)} %get-tuple-element.42.refs_0_, bf16[272,128]{1,0:T(8,128)(2,1)S(1)} %collective-permute-done.12.refs_1_, bf16[272,128]{1,0:T(8,128)(2,1)S(1)} %collective-permute-done.13.refs_2_, bf16[272,128]{1,0:T(8,128)(2,1)S(1)} %collective-permute-done.14.refs_3_, ...), custom_call_target="tpu_custom_call" | custom-call | tf_op jit(solution)/shard_map/combine/combine/pallas_call | solution.py:310
  (2 shorter events, 0.0 us)
Async XLA Ops:
  0.0 2.7 %collective-permute-start.1 = (bf16[128,512]{1,0:T(8,128)(2,1)}, bf16[128,512]{1,0:T(8,128)(2,1)S(1)}, u32[]{:S(2)}, u32[]{:S(2)}) collective-permute-start(bf16[128,512]{1,0:T(8,128)(2,1)} %param.4), channel_id=1, source_target_pairs={{0,1},{1,0},{2,3},{3,2},{4,5},{5,4},{6,7},{7,6},{8,9},{9,8},{10,11... | collective-permute-start | bytes 393224 | tf_op jit(solution)/shard_map/swap/ppermute | solution.py:186
  0.5 2.3 %collective-permute-start.2 = (bf16[128,512]{1,0:T(8,128)(2,1)}, bf16[128,512]{1,0:T(8,128)(2,1)S(1)}, u32[]{:S(2)}, u32[]{:S(2)}) collective-permute-start(bf16[128,512]{1,0:T(8,128)(2,1)} %param.5), channel_id=1, source_target_pairs={{0,1},{1,0},{2,3},{3,2},{4,5},{5,4},{6,7},{7,6},{8,9},{9,8},{10,11... | collective-permute-start | bytes 393224 | tf_op jit(solution)/shard_map/swap/ppermute | solution.py:186
  0.5 2.3 %collective-permute-start.3 = (bf16[128,512]{1,0:T(8,128)(2,1)}, bf16[128,512]{1,0:T(8,128)(2,1)S(1)}, u32[]{:S(2)}, u32[]{:S(2)}) collective-permute-start(bf16[128,512]{1,0:T(8,128)(2,1)} %param.6), channel_id=1, source_target_pairs={{0,1},{1,0},{2,3},{3,2},{4,5},{5,4},{6,7},{7,6},{8,9},{9,8},{10,11... | collective-permute-start | bytes 393224 | tf_op jit(solution)/shard_map/swap/ppermute | solution.py:186
  1.0 1.8 %collective-permute-start = (s32[1]{0:T(128)}, s32[1]{0:T(128)}, u32[]{:S(2)}, u32[]{:S(2)}) collective-permute-start(s32[1]{0:T(128)} %param.7), channel_id=1, source_target_pairs={{0,1},{1,0},{2,3},{3,2},{4,5},{5,4},{6,7},{7,6},{8,9},{9,8},{10,11... | collective-permute-start | bytes 20 | tf_op jit(solution)/shard_map/swap/ppermute | solution.py:186
  3.6 9.6 %collective-permute-start.7 = (bf16[1040,128]{1,0:T(8,128)(2,1)S(1)}, bf16[1040,128]{1,0:T(8,128)(2,1)S(1)}, u32[]{:S(2)}, u32[]{:S(2)}) collective-permute-start(bf16[1040,128]{1,0:T(8,128)(2,1)S(1)} %get-tuple-element.27.refs_0_), channel_id=1, source_target_pairs={{0,8},{8,0},{16,24},{24,16},{1,9},{9,1},{17,25},{25,17},{2,10},{10... | collective-permute-start | bytes 798728 | tf_op jit(solution)/shard_map/exchange/ppermute | solution.py:214
  6.6 8.4 %collective-permute-start.8 = (bf16[1040,128]{1,0:T(8,128)(2,1)S(1)}, bf16[1040,128]{1,0:T(8,128)(2,1)S(1)}, u32[]{:S(2)}, u32[]{:S(2)}) collective-permute-start(bf16[1040,128]{1,0:T(8,128)(2,1)S(1)} %get-tuple-element.27.refs_0_), channel_id=1, source_target_pairs={{0,16},{8,24},{16,0},{24,8},{1,17},{9,25},{17,1},{25,9},{2,18},{10... | collective-permute-start | bytes 798728 | tf_op jit(solution)/shard_map/exchange/ppermute | solution.py:214
  8.1 6.9 %collective-permute-start.5 = (bf16[528,128]{1,0:T(8,128)(2,1)S(1)}, bf16[528,128]{1,0:T(8,128)(2,1)S(1)}, u32[]{:S(2)}, u32[]{:S(2)}) collective-permute-start(bf16[528,128]{1,0:T(8,128)(2,1)S(1)} %get-tuple-element.39.q_ref), channel_id=1, source_target_pairs={{0,2},{1,3},{2,0},{3,1},{4,6},{5,7},{6,4},{7,5},{8,10},{9,11},{10,... | collective-permute-start | bytes 405512 | tf_op jit(solution)/shard_map/exchange/ppermute | solution.py:220
  9.7 9.5 %collective-permute-start.6 = (bf16[528,128]{1,0:T(8,128)(2,1)S(1)}, bf16[528,128]{1,0:T(8,128)(2,1)S(1)}, u32[]{:S(2)}, u32[]{:S(2)}) collective-permute-start(bf16[528,128]{1,0:T(8,128)(2,1)S(1)} %get-tuple-element.39.q_ref), channel_id=1, source_target_pairs={{0,6},{1,7},{2,4},{3,5},{4,2},{5,3},{6,0},{7,1},{8,14},{9,15},{10,... | collective-permute-start | bytes 405512 | tf_op jit(solution)/shard_map/exchange/ppermute | solution.py:220
  13.1 6.0 %collective-permute-start.9 = (bf16[528,128]{1,0:T(8,128)(2,1)S(1)}, bf16[528,128]{1,0:T(8,128)(2,1)S(1)}, u32[]{:S(2)}, u32[]{:S(2)}) collective-permute-start(bf16[528,128]{1,0:T(8,128)(2,1)S(1)} %slice.8), channel_id=1, source_target_pairs={{0,16},{8,24},{16,0},{24,8},{1,17},{9,25},{17,1},{25,9},{2,18},{10... | collective-permute-start | bytes 405512 | tf_op jit(solution)/shard_map/exchange/ppermute | solution.py:214
  15.0 5.0 %collective-permute-start.10 = (bf16[512,128]{1,0:T(8,128)(2,1)S(1)}, bf16[512,128]{1,0:T(8,128)(2,1)S(1)}, u32[]{:S(2)}, u32[]{:S(2)}) collective-permute-start(bf16[512,128]{1,0:T(8,128)(2,1)S(1)} %slice.9), channel_id=1, source_target_pairs={{0,8},{8,0},{16,24},{24,16},{1,9},{9,1},{17,25},{25,17},{2,10},{10... | collective-permute-start | bytes 393224 | tf_op jit(solution)/shard_map/exchange/ppermute | solution.py:214
  16.6 8.0 %collective-permute-start.4 = (bf16[528,128]{1,0:T(8,128)(2,1)S(1)}, bf16[528,128]{1,0:T(8,128)(2,1)S(1)}, u32[]{:S(2)}, u32[]{:S(2)}) collective-permute-start(bf16[528,128]{1,0:T(8,128)(2,1)S(1)} %get-tuple-element.39.q_ref), channel_id=1, source_target_pairs={{0,4},{1,5},{2,6},{3,7},{4,0},{5,1},{6,2},{7,3},{8,12},{9,13},{10,... | collective-permute-start | bytes 405512 | tf_op jit(solution)/shard_map/exchange/ppermute | solution.py:220
  20.4 6.3 %collective-permute-start.11 = (bf16[544,128]{1,0:T(8,128)(2,1)S(1)}, bf16[544,128]{1,0:T(8,128)(2,1)S(1)}, u32[]{:S(2)}, u32[]{:S(2)}) collective-permute-start(bf16[544,128]{1,0:T(8,128)(2,1)S(1)} %apply.4), channel_id=1, source_target_pairs={{0,2},{1,3},{2,0},{3,1},{4,6},{5,7},{6,4},{7,5},{8,10},{9,11},{10,... | collective-permute-start | bytes 417800 | tf_op jit(solution)/shard_map/return/ppermute | solution.py:286
  23.1 8.0 %collective-permute-start.15 = (bf16[272,128]{1,0:T(8,128)(2,1)S(1)}, bf16[272,128]{1,0:T(8,128)(2,1)S(1)}, u32[]{:S(2)}, u32[]{:S(2)}) collective-permute-start(bf16[272,128]{1,0:T(8,128)(2,1)S(1)} %get-tuple-element.34), channel_id=1, source_target_pairs={{0,2},{1,3},{2,0},{3,1},{4,6},{5,7},{6,4},{7,5},{8,10},{9,11},{10,... | collective-permute-start | bytes 208904 | tf_op jit(solution)/shard_map/return/ppermute | solution.py:284
  25.6 5.5 %collective-permute-start.16 = (bf16[272,128]{1,0:T(8,128)(2,1)S(1)}, bf16[272,128]{1,0:T(8,128)(2,1)S(1)}, u32[]{:S(2)}, u32[]{:S(2)}) collective-permute-start(bf16[272,128]{1,0:T(8,128)(2,1)S(1)} %get-tuple-element.46), channel_id=1, source_target_pairs={{0,3},{1,2},{2,1},{3,0},{4,7},{5,6},{6,5},{7,4},{8,11},{9,10},{10,... | collective-permute-start | bytes 208904 | tf_op jit(solution)/shard_map/return/ppermute | solution.py:284
  26.8 9.9 %collective-permute-start.13 = (bf16[272,128]{1,0:T(8,128)(2,1)S(1)}, bf16[272,128]{1,0:T(8,128)(2,1)S(1)}, u32[]{:S(2)}, u32[]{:S(2)}) collective-permute-start(bf16[272,128]{1,0:T(8,128)(2,1)S(1)} %get-tuple-element.38), channel_id=1, source_target_pairs={{0,4},{1,5},{2,6},{3,7},{4,0},{5,1},{6,2},{7,3},{8,12},{9,13},{10,... | collective-permute-start | bytes 208904 | tf_op jit(solution)/shard_map/return/ppermute | solution.py:284
  28.7 8.0 %collective-permute-start.14 = (bf16[272,128]{1,0:T(8,128)(2,1)S(1)}, bf16[272,128]{1,0:T(8,128)(2,1)S(1)}, u32[]{:S(2)}, u32[]{:S(2)}) collective-permute-start(bf16[272,128]{1,0:T(8,128)(2,1)S(1)} %get-tuple-element.44), channel_id=1, source_target_pairs={{0,5},{1,4},{2,7},{3,6},{4,1},{5,0},{6,3},{7,2},{8,13},{9,12},{10,... | collective-permute-start | bytes 208904 | tf_op jit(solution)/shard_map/return/ppermute | solution.py:284
  31.0 5.7 %collective-permute-start.12 = (bf16[272,128]{1,0:T(8,128)(2,1)S(1)}, bf16[272,128]{1,0:T(8,128)(2,1)S(1)}, u32[]{:S(2)}, u32[]{:S(2)}) collective-permute-start(bf16[272,128]{1,0:T(8,128)(2,1)S(1)} %get-tuple-element.43), channel_id=1, source_target_pairs={{0,1},{1,0},{2,3},{3,2},{4,5},{5,4},{6,7},{7,6},{8,9},{9,8},{10,11... | collective-permute-start | bytes 208904 | tf_op jit(solution)/shard_map/return/ppermute | solution.py:308

commit v23 on v20

--- a/solution.py
+++ b/solution.py
@@ -35,20 +35,21 @@
             out[row : row + tok, :] = piece
 
 
-def starts(p0, p1, size):
+def merge_kernel(p0, p1, own, q1, k1, v1, q_out, kv_out, pos, sem):
+    tok = q1.shape[0]
+    size = q_out.shape[1]
+    rows = PER * CORES * tok
+    copy = pltpu.make_async_copy(p1, pos, sem)
+    copy.start()
+    place(own.at[tok : 2 * tok, :], k1, kv_out, 0)
+    place(own.at[2 * tok : 3 * tok, :], v1, kv_out, rows + PAD, turned=True)
+    place(own.at[0:tok, :], q1, q_out, 0)
+    copy.wait()
     half = PAD // CORES
-    return jnp.concatenate([jnp.full((half, size), p[0].astype(F32), F32) for p in (p0, p1)], axis=0).astype(BF16)
-
-
-def merge_kernel(p0, p1, own, q1, k1, v1, q_out, kv_out):
-    tok = q1.shape[0]
-    rows = PER * CORES * tok
-    pos = starts(p0, p1, q_out.shape[1])
-    place(own.at[0:tok, :], q1, q_out, 0)
-    q_out[rows:, :] = pos
-    place(own.at[tok : 2 * tok, :], k1, kv_out, 0)
-    kv_out[rows : rows + PAD, :] = pos
-    place(own.at[2 * tok : 3 * tok, :], v1, kv_out, rows + PAD, turned=True)
+    starts = [jnp.full((half, size), p[0].astype(F32), F32) for p in (p0, pos)]
+    starts = jnp.concatenate(starts, axis=0).astype(BF16)
+    q_out[rows:, :] = starts
+    kv_out[rows : rows + PAD, :] = starts
 
 
 def score_kernel(same, q_ref, *refs):
@@ -151,18 +152,24 @@
 
 
 def combine_kernel(n, *refs):
-    parts, out_ref = refs[:n], refs[n]
+    parts, out_ref, heads, sems = refs[:n], *refs[n:]
     size = parts[0].shape[1]
     rate = size ** -0.5 * math.log2(math.e)
     core = lax.rem(lax.axis_index("inner"), CORES)
+    copies = []
     for x in range(CORES):
         mine = parts[x::CORES]
         pair = jnp.bitwise_xor(core, x)
         stats = [part[PER * size :, :].astype(F32) for part in mine]
         for h in range(PER):
+            at = x * PER + h
             _, total, numer = joined([part[h * size : (h + 1) * size, :] for part in mine], stats, h, rate)
+            heads[at] = (numer * (1.0 / total)).T.astype(BF16)
             cols = pl.ds(pl.multiple_of((pair * PER + h) * size, size), size)
-            out_ref[:, cols] = (numer * (1.0 / total)).T.astype(BF16)
+            copies.append(pltpu.make_async_copy(heads.at[at], out_ref.at[:, cols], sems.at[at]))
+            copies[-1].start()
+    for copy in copies:
+        copy.wait()
 
 
 def vmem(n=1):
@@ -193,8 +200,9 @@
                 jax.ShapeDtypeStruct((PER * both + PAD, size), BF16),
                 jax.ShapeDtypeStruct((2 * PER * both + PAD, size), BF16),
             ),
-            in_specs=smem * 2 + vmem(4),
+            in_specs=smem + [pl.BlockSpec(memory_space=pl.ANY)] + vmem(4),
             out_specs=tuple(vmem(2)),
+            scratch_shapes=[pltpu.SMEM((1,), jnp.int32), pltpu.SemaphoreType.DMA],
             compiler_params=params,
             name="merge",
         )(block_pos, other[3], own, *other[:3])
@@ -310,7 +318,8 @@
             functools.partial(combine_kernel, len(ends)),
             out_shape=jax.ShapeDtypeStruct((tok, width), BF16),
             in_specs=vmem(len(ends)),
-            out_specs=vmem()[0],
+            out_specs=pl.BlockSpec(memory_space=pl.ANY),
+            scratch_shapes=[pltpu.VMEM((HEADS, tok, size), BF16), pltpu.SemaphoreType.DMA((HEADS,))],
             compiler_params=params,
             name="combine",
         )(*ends)

time: 36.9 us -> 37.4 us (1.014)
  Pallas kernels: 6.07 us -> 6.55 us
    pallas_call x1, Pallas kernels: 0.78 us -> 1.25 us  [shards(): pl.pallas_call(merge_kernel, out_shape=(jax.ShapeDtypeStruct((PER * both...]
where the time goes in v23:
time: 37.4 us; the launch traced here: 37.3 us
  starting transfers between devices  22.1 us (59%)
  waiting for transfers between devices  6.75 us (18%)
  Pallas kernels  6.55 us (18%)
  other arithmetic  1.06 us (3%)
  between operations  0.8 us (2%)
    ppermute x4, starting transfers between devices, over(): return lax.ppermute(a, 'outer', [(o, o ^ r) for o in range(n_out)])  7.91 us
    ppermute x3, starting transfers between devices, shards(): q_by[r] = lax.ppermute(q_piece, 'inner', along_inner(r, 0))  6.64 us
    ppermute x4, starting transfers between devices, send(): lax.ppermute(parts[x], 'inner', along_inner(r, x))  4.54 us
    ppermute x4, waiting for transfers between devices, send(): lax.ppermute(parts[x], 'inner', along_inner(r, x))  3.66 us
    pallas_call x4, Pallas kernels, score(): pl.pallas_call(functools.partial(score_kernel, r == 0), out_shape=(jax.Sh...  3.03 us
    ppermute x1, starting transfers between devices, send(): lax.ppermute(parts[0], 'inner', along_inner(low(r), 0))  1.64 us
    pallas_call x4, Pallas kernels, apply(): pl.pallas_call(functools.partial(apply_kernel, wide, rows), out_shape=sha...  1.34 us
    pallas_call x1, Pallas kernels, shards(): pl.pallas_call(merge_kernel, out_shape=(jax.ShapeDtypeStruct((PER * both...  1.25 us
  transfers between devices with their start and end apart: 17, of which 5 were waited for; matrix products, arithmetic and copies ran while one was open for 3% of the time, Pallas kernels for 12%

profile of v23, /device:TPU:0, one launch (start us, length us, event | category | flops | bytes accessed | tf_op | source)
XLA Modules:
  0.0 37.3 jit_solution(16972115631980527999)
XLA Ops:
  0.0 0.5 %collective-permute-start.1 = (bf16[128,512]{1,0:T(8,128)(2,1)}, bf16[128,512]{1,0:T(8,128)(2,1)S(1)}, u32[]{:S(2)}, u32[]{:S(2)}) collective-permute-start(bf16[128,512]{1,0:T(8,128)(2,1)} %param.4), channel_id=1, source_target_pairs={{0,1},{1,0},{2,3},{3,2},{4,5},{5,4},{6,7},{7,6},{8,9},{9,8},{10,11... | collective-permute-start | bytes 393224 | tf_op jit(solution)/shard_map/swap/ppermute | solution.py:193
  0.5 0.1 collective-permute-start.2
  0.5 0.5 %collective-permute-start.3 = (bf16[128,512]{1,0:T(8,128)(2,1)}, bf16[128,512]{1,0:T(8,128)(2,1)S(1)}, u32[]{:S(2)}, u32[]{:S(2)}) collective-permute-start(bf16[128,512]{1,0:T(8,128)(2,1)} %param.6), channel_id=1, source_target_pairs={{0,1},{1,0},{2,3},{3,2},{4,5},{5,4},{6,7},{7,6},{8,9},{9,8},{10,11... | collective-permute-start | bytes 393224 | tf_op jit(solution)/shard_map/swap/ppermute | solution.py:193
  1.0 0.1 collective-permute-start
  1.7 1.1 %pad_maximum_fusion.own = bf16[384,512]{1,0:T(8,128)(2,1)S(1)} fusion(bf16[128,512]{1,0:T(8,128)(2,1)} %param.6, bf16[128,512]{1,0:T(8,128)(2,1)} %param.5, bf16[128,512]{1,0:T(8,128)(2,1)} %param.4), kind=kLoop, calls=%fused_computation | loop fusion | flops 1179648 | bytes 786432 | tf_op jit(solution)/shard_map/swap/concatenate | solution.py:194
  2.7 0.0 collective-permute-done.p1
  2.7 0.0 collective-permute-done.1.q1
  2.8 0.0 collective-permute-done.2.k1
  2.8 0.0 collective-permute-done.3.v1
  2.8 1.2 %merge.1 = (bf16[528,128]{1,0:T(8,128)(2,1)S(1)}, bf16[1040,128]{1,0:T(8,128)(2,1)S(1)}) custom-call(s32[1]{0:T(128)S(6)} %copy.5.p0, s32[1]{0:T(128)} %collective-permute-done.p1, bf16[384,512]{1,0:T(8,128)(2,1)S(1)} %pad_maximum_fusion.own, bf16[128,512]{1,0:T(8,128)(2,1)S(1)} %collective-permute-done.1.q1, ...), custom_call_target="tpu_custom_call" | custom-call | tf_op jit(solution)/shard_map/merge/merge/pallas_call | solution.py:197
  4.0 3.0 %collective-permute-start.7 = (bf16[1040,128]{1,0:T(8,128)(2,1)S(1)}, bf16[1040,128]{1,0:T(8,128)(2,1)S(1)}, u32[]{:S(2)}, u32[]{:S(2)}) collective-permute-start(bf16[1040,128]{1,0:T(8,128)(2,1)S(1)} %get-tuple-element.27.refs_0_), channel_id=1, source_target_pairs={{0,8},{8,0},{16,24},{24,16},{1,9},{9,1},{17,25},{25,17},{2,10},{10... | collective-permute-start | bytes 798728 | tf_op jit(solution)/shard_map/exchange/ppermute | solution.py:222
  7.0 1.5 %collective-permute-start.8 = (bf16[1040,128]{1,0:T(8,128)(2,1)S(1)}, bf16[1040,128]{1,0:T(8,128)(2,1)S(1)}, u32[]{:S(2)}, u32[]{:S(2)}) collective-permute-start(bf16[1040,128]{1,0:T(8,128)(2,1)S(1)} %get-tuple-element.27.refs_0_), channel_id=1, source_target_pairs={{0,16},{8,24},{16,0},{24,8},{1,17},{9,25},{17,1},{25,9},{2,18},{10... | collective-permute-start | bytes 798728 | tf_op jit(solution)/shard_map/exchange/ppermute | solution.py:222
  8.6 1.6 %collective-permute-start.5 = (bf16[528,128]{1,0:T(8,128)(2,1)S(1)}, bf16[528,128]{1,0:T(8,128)(2,1)S(1)}, u32[]{:S(2)}, u32[]{:S(2)}) collective-permute-start(bf16[528,128]{1,0:T(8,128)(2,1)S(1)} %get-tuple-element.39.q_ref), channel_id=1, source_target_pairs={{0,2},{1,3},{2,0},{3,1},{4,6},{5,7},{6,4},{7,5},{8,10},{9,11},{10,... | collective-permute-start | bytes 405512 | tf_op jit(solution)/shard_map/exchange/ppermute | solution.py:228
  10.1 2.5 %collective-permute-start.6 = (bf16[528,128]{1,0:T(8,128)(2,1)S(1)}, bf16[528,128]{1,0:T(8,128)(2,1)S(1)}, u32[]{:S(2)}, u32[]{:S(2)}) collective-permute-start(bf16[528,128]{1,0:T(8,128)(2,1)S(1)} %get-tuple-element.39.q_ref), channel_id=1, source_target_pairs={{0,6},{1,7},{2,4},{3,5},{4,2},{5,3},{6,0},{7,1},{8,14},{9,15},{10,... | collective-permute-start | bytes 405512 | tf_op jit(solution)/shard_map/exchange/ppermute | solution.py:228
  12.6 1.0 %collective-permute-done.7.refs_1_ = bf16[1040,128]{1,0:T(8,128)(2,1)S(1)} collective-permute-done((bf16[1040,128]{1,0:T(8,128)(2,1)S(1)}, bf16[1040,128]{1,0:T(8,128)(2,1)S(1)}, u32[]{:S(2)}, u32[]{:S(2)}) %collective-permute-start.7) | collective-permute-done | bytes 266272 | tf_op jit(solution)/shard_map/exchange/ppermute | solution.py:222
  13.6 1.8 %collective-permute-start.9 = (bf16[528,128]{1,0:T(8,128)(2,1)S(1)}, bf16[528,128]{1,0:T(8,128)(2,1)S(1)}, u32[]{:S(2)}, u32[]{:S(2)}) collective-permute-start(bf16[528,128]{1,0:T(8,128)(2,1)S(1)} %slice.8), channel_id=1, source_target_pairs={{0,16},{8,24},{16,0},{24,8},{1,17},{9,25},{17,1},{25,9},{2,18},{10... | collective-permute-start | bytes 405512 | tf_op jit(solution)/shard_map/exchange/ppermute | solution.py:222
  15.4 0.0 collective-permute-done.8.refs_2_
  15.5 0.0 collective-permute-done.5.q_ref
  15.5 1.6 %collective-permute-start.10 = (bf16[512,128]{1,0:T(8,128)(2,1)S(1)}, bf16[512,128]{1,0:T(8,128)(2,1)S(1)}, u32[]{:S(2)}, u32[]{:S(2)}) collective-permute-start(bf16[512,128]{1,0:T(8,128)(2,1)S(1)} %slice.9), channel_id=1, source_target_pairs={{0,8},{8,0},{16,24},{24,16},{1,9},{9,1},{17,25},{25,17},{2,10},{10... | collective-permute-start | bytes 393224 | tf_op jit(solution)/shard_map/exchange/ppermute | solution.py:222
  17.0 2.6 %collective-permute-start.4 = (bf16[528,128]{1,0:T(8,128)(2,1)S(1)}, bf16[528,128]{1,0:T(8,128)(2,1)S(1)}, u32[]{:S(2)}, u32[]{:S(2)}) collective-permute-start(bf16[528,128]{1,0:T(8,128)(2,1)S(1)} %get-tuple-element.39.q_ref), channel_id=1, source_target_pairs={{0,4},{1,5},{2,6},{3,7},{4,0},{5,1},{6,2},{7,3},{8,12},{9,13},{10,... | collective-permute-start | bytes 405512 | tf_op jit(solution)/shard_map/exchange/ppermute | solution.py:228
  19.6 0.0 collective-permute-done.6.q_ref
  19.6 0.0 collective-permute-done.9.refs_3_
  19.6 0.8 %score.4 = (bf16[2,1024,256]{2,1,0:T(8,128)(2,1)S(1)}, f32[16,256]{1,0:T(8,128)S(1)}) custom-call(bf16[528,128]{1,0:T(8,128)(2,1)S(1)} %collective-permute-done.6.q_ref, bf16[1040,128]{1,0:T(8,128)(2,1)S(1)} %get-tuple-element.27.refs_0_, bf16[1040,128]{1,0:T(8,128)(2,1)S(1)} %collective-permute-done.7.refs_1_, ...), custom_call_target="tpu_custom_call" | custom-call | flops 134217728 | bytes 1048576 | tf_op jit(solution)/shard_map/score/score/pallas_call | solution.py:250
  20.4 0.1 collective-permute-done.10.refs_3_
  20.5 0.3 apply.4
  20.9 1.6 %collective-permute-start.11 = (bf16[544,128]{1,0:T(8,128)(2,1)S(1)}, bf16[544,128]{1,0:T(8,128)(2,1)S(1)}, u32[]{:S(2)}, u32[]{:S(2)}) collective-permute-start(bf16[544,128]{1,0:T(8,128)(2,1)S(1)} %apply.4), channel_id=1, source_target_pairs={{0,2},{1,3},{2,0},{3,1},{4,6},{5,7},{6,4},{7,5},{8,10},{9,11},{10,... | collective-permute-start | bytes 417800 | tf_op jit(solution)/shard_map/return/ppermute | solution.py:294
  22.5 0.8 %score.5 = (bf16[2,1024,256]{2,1,0:T(8,128)(2,1)S(1)}, f32[16,256]{1,0:T(8,128)S(1)}) custom-call(bf16[528,128]{1,0:T(8,128)(2,1)S(1)} %collective-permute-done.5.q_ref, bf16[1040,128]{1,0:T(8,128)(2,1)S(1)} %get-tuple-element.27.refs_0_, bf16[1040,128]{1,0:T(8,128)(2,1)S(1)} %collective-permute-done.7.refs_1_, ...), custom_call_target="tpu_custom_call" | custom-call | flops 134217728 | bytes 1048576 | tf_op jit(solution)/shard_map/score/score/pallas_call | solution.py:250
  23.3 0.3 apply.5
  23.6 0.5 %collective-permute-start.15 = (bf16[272,128]{1,0:T(8,128)(2,1)S(1)}, bf16[272,128]{1,0:T(8,128)(2,1)S(1)}, u32[]{:S(2)}, u32[]{:S(2)}) collective-permute-start(bf16[272,128]{1,0:T(8,128)(2,1)S(1)} %get-tuple-element.34), channel_id=1, source_target_pairs={{0,2},{1,3},{2,0},{3,1},{4,6},{5,7},{6,4},{7,5},{8,10},{9,11},{10,... | collective-permute-start | bytes 208904 | tf_op jit(solution)/shard_map/return/ppermute | solution.py:292
  24.1 0.9 %collective-permute-done.4.q_ref = bf16[528,128]{1,0:T(8,128)(2,1)S(1)} collective-permute-done((bf16[528,128]{1,0:T(8,128)(2,1)S(1)}, bf16[528,128]{1,0:T(8,128)(2,1)S(1)}, u32[]{:S(2)}, u32[]{:S(2)}) %collective-permute-start.4) | collective-permute-done | bytes 135200 | tf_op jit(solution)/shard_map/exchange/ppermute | solution.py:228
  25.0 0.8 %score.6 = (bf16[2,1024,256]{2,1,0:T(8,128)(2,1)S(1)}, f32[16,256]{1,0:T(8,128)S(1)}) custom-call(bf16[528,128]{1,0:T(8,128)(2,1)S(1)} %collective-permute-done.4.q_ref, bf16[1040,128]{1,0:T(8,128)(2,1)S(1)} %get-tuple-element.27.refs_0_, bf16[1040,128]{1,0:T(8,128)(2,1)S(1)} %collective-permute-done.7.refs_1_, ...), custom_call_target="tpu_custom_call" | custom-call | flops 134217728 | bytes 1048576 | tf_op jit(solution)/shard_map/score/score/pallas_call | solution.py:250
  25.8 0.3 apply.6.refs_0_
  26.1 1.1 %collective-permute-done.11.refs_1_ = bf16[544,128]{1,0:T(8,128)(2,1)S(1)} collective-permute-done((bf16[544,128]{1,0:T(8,128)(2,1)S(1)}, bf16[544,128]{1,0:T(8,128)(2,1)S(1)}, u32[]{:S(2)}, u32[]{:S(2)}) %collective-permute-start.11) | collective-permute-done | bytes 139296 | tf_op jit(solution)/shard_map/return/ppermute | solution.py:294
  27.2 0.1 add.1
  27.3 1.9 %collective-permute-start.13 = (bf16[272,128]{1,0:T(8,128)(2,1)S(1)}, bf16[272,128]{1,0:T(8,128)(2,1)S(1)}, u32[]{:S(2)}, u32[]{:S(2)}) collective-permute-start(bf16[272,128]{1,0:T(8,128)(2,1)S(1)} %get-tuple-element.38), channel_id=1, source_target_pairs={{0,4},{1,5},{2,6},{3,7},{4,0},{5,1},{6,2},{7,3},{8,12},{9,13},{10,... | collective-permute-start | bytes 208904 | tf_op jit(solution)/shard_map/return/ppermute | solution.py:292
  29.2 0.0 collective-permute-start.14
  29.2 0.8 %score.7 = (bf16[2,1024,256]{2,1,0:T(8,128)(2,1)S(1)}, f32[16,256]{1,0:T(8,128)S(1)}) custom-call(bf16[528,128]{1,0:T(8,128)(2,1)S(1)} %get-tuple-element.39.q_ref, bf16[1040,128]{1,0:T(8,128)(2,1)S(1)} %get-tuple-element.27.refs_0_, bf16[1040,128]{1,0:T(8,128)(2,1)S(1)} %collective-permute-done.7.refs_1_, ...), custom_call_target="tpu_custom_call" | custom-call | flops 134217728 | bytes 1048576 | tf_op jit(solution)/shard_map/score/score/pallas_call | solution.py:250
  30.0 0.3 apply.7
  30.3 2.1 %collective-permute-start.16 = (bf16[272,128]{1,0:T(8,128)(2,1)S(1)}, bf16[272,128]{1,0:T(8,128)(2,1)S(1)}, u32[]{:S(2)}, u32[]{:S(2)}) collective-permute-start(bf16[272,128]{1,0:T(8,128)(2,1)S(1)} %get-tuple-element.46), channel_id=1, source_target_pairs={{0,3},{1,2},{2,1},{3,0},{4,7},{5,6},{6,5},{7,4},{8,11},{9,10},{10,... | collective-permute-start | bytes 208904 | tf_op jit(solution)/shard_map/return/ppermute | solution.py:292
  32.4 0.3 collective-permute-start.12
  32.7 0.0 collective-permute-done.15.refs_4_
  32.7 3.7 %collective-permute-done.14.refs_3_ = bf16[272,128]{1,0:T(8,128)(2,1)S(1)} collective-permute-done((bf16[272,128]{1,0:T(8,128)(2,1)S(1)}, bf16[272,128]{1,0:T(8,128)(2,1)S(1)}, u32[]{:S(2)}, u32[]{:S(2)}) %collective-permute-start.14) | collective-permute-done | bytes 69664 | tf_op jit(solution)/shard_map/return/ppermute | solution.py:292
  36.4 0.0 collective-permute-done.13.refs_2_
  36.4 0.0 collective-permute-done.16.refs_5_
  36.4 0.0 collective-permute-done.12.refs_1_
  36.4 0.9 %combine.1 = bf16[128,512]{1,0:T(8,128)(2,1)} custom-call(bf16[272,128]{1,0:T(8,128)(2,1)S(1)} %get-tuple-element.42.refs_0_, bf16[272,128]{1,0:T(8,128)(2,1)S(1)} %collective-permute-done.12.refs_1_, bf16[272,128]{1,0:T(8,128)(2,1)S(1)} %collective-permute-done.13.refs_2_, bf16[272,128]{1,0:T(8,128)(2,1)S(1)} %collective-permute-done.14.refs_3_, ...), custom_call_target="tpu_custom_call" | custom-call | tf_op jit(solution)/shard_map/combine/combine/pallas_call | solution.py:317
  (2 shorter events, 0.0 us)
Async XLA Ops:
  0.0 2.7 %collective-permute-start.1 = (bf16[128,512]{1,0:T(8,128)(2,1)}, bf16[128,512]{1,0:T(8,128)(2,1)S(1)}, u32[]{:S(2)}, u32[]{:S(2)}) collective-permute-start(bf16[128,512]{1,0:T(8,128)(2,1)} %param.4), channel_id=1, source_target_pairs={{0,1},{1,0},{2,3},{3,2},{4,5},{5,4},{6,7},{7,6},{8,9},{9,8},{10,11... | collective-permute-start | bytes 393224 | tf_op jit(solution)/shard_map/swap/ppermute | solution.py:193
  0.5 2.3 %collective-permute-start.2 = (bf16[128,512]{1,0:T(8,128)(2,1)}, bf16[128,512]{1,0:T(8,128)(2,1)S(1)}, u32[]{:S(2)}, u32[]{:S(2)}) collective-permute-start(bf16[128,512]{1,0:T(8,128)(2,1)} %param.5), channel_id=1, source_target_pairs={{0,1},{1,0},{2,3},{3,2},{4,5},{5,4},{6,7},{7,6},{8,9},{9,8},{10,11... | collective-permute-start | bytes 393224 | tf_op jit(solution)/shard_map/swap/ppermute | solution.py:193
  0.5 2.3 %collective-permute-start.3 = (bf16[128,512]{1,0:T(8,128)(2,1)}, bf16[128,512]{1,0:T(8,128)(2,1)S(1)}, u32[]{:S(2)}, u32[]{:S(2)}) collective-permute-start(bf16[128,512]{1,0:T(8,128)(2,1)} %param.6), channel_id=1, source_target_pairs={{0,1},{1,0},{2,3},{3,2},{4,5},{5,4},{6,7},{7,6},{8,9},{9,8},{10,11... | collective-permute-start | bytes 393224 | tf_op jit(solution)/shard_map/swap/ppermute | solution.py:193
  1.0 1.8 %collective-permute-start = (s32[1]{0:T(128)}, s32[1]{0:T(128)}, u32[]{:S(2)}, u32[]{:S(2)}) collective-permute-start(s32[1]{0:T(128)} %param.7), channel_id=1, source_target_pairs={{0,1},{1,0},{2,3},{3,2},{4,5},{5,4},{6,7},{7,6},{8,9},{9,8},{10,11... | collective-permute-start | bytes 20 | tf_op jit(solution)/shard_map/swap/ppermute | solution.py:193
  4.0 9.6 %collective-permute-start.7 = (bf16[1040,128]{1,0:T(8,128)(2,1)S(1)}, bf16[1040,128]{1,0:T(8,128)(2,1)S(1)}, u32[]{:S(2)}, u32[]{:S(2)}) collective-permute-start(bf16[1040,128]{1,0:T(8,128)(2,1)S(1)} %get-tuple-element.27.refs_0_), channel_id=1, source_target_pairs={{0,8},{8,0},{16,24},{24,16},{1,9},{9,1},{17,25},{25,17},{2,10},{10... | collective-permute-start | bytes 798728 | tf_op jit(solution)/shard_map/exchange/ppermute | solution.py:222
  7.0 8.4 %collective-permute-start.8 = (bf16[1040,128]{1,0:T(8,128)(2,1)S(1)}, bf16[1040,128]{1,0:T(8,128)(2,1)S(1)}, u32[]{:S(2)}, u32[]{:S(2)}) collective-permute-start(bf16[1040,128]{1,0:T(8,128)(2,1)S(1)} %get-tuple-element.27.refs_0_), channel_id=1, source_target_pairs={{0,16},{8,24},{16,0},{24,8},{1,17},{9,25},{17,1},{25,9},{2,18},{10... | collective-permute-start | bytes 798728 | tf_op jit(solution)/shard_map/exchange/ppermute | solution.py:222
  8.6 6.9 %collective-permute-start.5 = (bf16[528,128]{1,0:T(8,128)(2,1)S(1)}, bf16[528,128]{1,0:T(8,128)(2,1)S(1)}, u32[]{:S(2)}, u32[]{:S(2)}) collective-permute-start(bf16[528,128]{1,0:T(8,128)(2,1)S(1)} %get-tuple-element.39.q_ref), channel_id=1, source_target_pairs={{0,2},{1,3},{2,0},{3,1},{4,6},{5,7},{6,4},{7,5},{8,10},{9,11},{10,... | collective-permute-start | bytes 405512 | tf_op jit(solution)/shard_map/exchange/ppermute | solution.py:228
  10.1 9.5 %collective-permute-start.6 = (bf16[528,128]{1,0:T(8,128)(2,1)S(1)}, bf16[528,128]{1,0:T(8,128)(2,1)S(1)}, u32[]{:S(2)}, u32[]{:S(2)}) collective-permute-start(bf16[528,128]{1,0:T(8,128)(2,1)S(1)} %get-tuple-element.39.q_ref), channel_id=1, source_target_pairs={{0,6},{1,7},{2,4},{3,5},{4,2},{5,3},{6,0},{7,1},{8,14},{9,15},{10,... | collective-permute-start | bytes 405512 | tf_op jit(solution)/shard_map/exchange/ppermute | solution.py:228
  13.6 6.0 %collective-permute-start.9 = (bf16[528,128]{1,0:T(8,128)(2,1)S(1)}, bf16[528,128]{1,0:T(8,128)(2,1)S(1)}, u32[]{:S(2)}, u32[]{:S(2)}) collective-permute-start(bf16[528,128]{1,0:T(8,128)(2,1)S(1)} %slice.8), channel_id=1, source_target_pairs={{0,16},{8,24},{16,0},{24,8},{1,17},{9,25},{17,1},{25,9},{2,18},{10... | collective-permute-start | bytes 405512 | tf_op jit(solution)/shard_map/exchange/ppermute | solution.py:222
  15.5 5.0 %collective-permute-start.10 = (bf16[512,128]{1,0:T(8,128)(2,1)S(1)}, bf16[512,128]{1,0:T(8,128)(2,1)S(1)}, u32[]{:S(2)}, u32[]{:S(2)}) collective-permute-start(bf16[512,128]{1,0:T(8,128)(2,1)S(1)} %slice.9), channel_id=1, source_target_pairs={{0,8},{8,0},{16,24},{24,16},{1,9},{9,1},{17,25},{25,17},{2,10},{10... | collective-permute-start | bytes 393224 | tf_op jit(solution)/shard_map/exchange/ppermute | solution.py:222
  17.0 8.0 %collective-permute-start.4 = (bf16[528,128]{1,0:T(8,128)(2,1)S(1)}, bf16[528,128]{1,0:T(8,128)(2,1)S(1)}, u32[]{:S(2)}, u32[]{:S(2)}) collective-permute-start(bf16[528,128]{1,0:T(8,128)(2,1)S(1)} %get-tuple-element.39.q_ref), channel_id=1, source_target_pairs={{0,4},{1,5},{2,6},{3,7},{4,0},{5,1},{6,2},{7,3},{8,12},{9,13},{10,... | collective-permute-start | bytes 405512 | tf_op jit(solution)/shard_map/exchange/ppermute | solution.py:228
  20.9 6.3 %collective-permute-start.11 = (bf16[544,128]{1,0:T(8,128)(2,1)S(1)}, bf16[544,128]{1,0:T(8,128)(2,1)S(1)}, u32[]{:S(2)}, u32[]{:S(2)}) collective-permute-start(bf16[544,128]{1,0:T(8,128)(2,1)S(1)} %apply.4), channel_id=1, source_target_pairs={{0,2},{1,3},{2,0},{3,1},{4,6},{5,7},{6,4},{7,5},{8,10},{9,11},{10,... | collective-permute-start | bytes 417800 | tf_op jit(solution)/shard_map/return/ppermute | solution.py:294
  23.6 9.1 %collective-permute-start.15 = (bf16[272,128]{1,0:T(8,128)(2,1)S(1)}, bf16[272,128]{1,0:T(8,128)(2,1)S(1)}, u32[]{:S(2)}, u32[]{:S(2)}) collective-permute-start(bf16[272,128]{1,0:T(8,128)(2,1)S(1)} %get-tuple-element.34), channel_id=1, source_target_pairs={{0,2},{1,3},{2,0},{3,1},{4,6},{5,7},{6,4},{7,5},{8,10},{9,11},{10,... | collective-permute-start | bytes 208904 | tf_op jit(solution)/shard_map/return/ppermute | solution.py:292
  27.3 9.1 %collective-permute-start.13 = (bf16[272,128]{1,0:T(8,128)(2,1)S(1)}, bf16[272,128]{1,0:T(8,128)(2,1)S(1)}, u32[]{:S(2)}, u32[]{:S(2)}) collective-permute-start(bf16[272,128]{1,0:T(8,128)(2,1)S(1)} %get-tuple-element.38), channel_id=1, source_target_pairs={{0,4},{1,5},{2,6},{3,7},{4,0},{5,1},{6,2},{7,3},{8,12},{9,13},{10,... | collective-permute-start | bytes 208904 | tf_op jit(solution)/shard_map/return/ppermute | solution.py:292
  29.2 7.2 %collective-permute-start.14 = (bf16[272,128]{1,0:T(8,128)(2,1)S(1)}, bf16[272,128]{1,0:T(8,128)(2,1)S(1)}, u32[]{:S(2)}, u32[]{:S(2)}) collective-permute-start(bf16[272,128]{1,0:T(8,128)(2,1)S(1)} %get-tuple-element.44), channel_id=1, source_target_pairs={{0,5},{1,4},{2,7},{3,6},{4,1},{5,0},{6,3},{7,2},{8,13},{9,12},{10,... | collective-permute-start | bytes 208904 | tf_op jit(solution)/shard_map/return/ppermute | solution.py:292
  30.3 6.1 %collective-permute-start.16 = (bf16[272,128]{1,0:T(8,128)(2,1)S(1)}, bf16[272,128]{1,0:T(8,128)(2,1)S(1)}, u32[]{:S(2)}, u32[]{:S(2)}) collective-permute-start(bf16[272,128]{1,0:T(8,128)(2,1)S(1)} %get-tuple-element.46), channel_id=1, source_target_pairs={{0,3},{1,2},{2,1},{3,0},{4,7},{5,6},{6,5},{7,4},{8,11},{9,10},{10,... | collective-permute-start | bytes 208904 | tf_op jit(solution)/shard_map/return/ppermute | solution.py:292
  32.4 4.0 %collective-permute-start.12 = (bf16[272,128]{1,0:T(8,128)(2,1)S(1)}, bf16[272,128]{1,0:T(8,128)(2,1)S(1)}, u32[]{:S(2)}, u32[]{:S(2)}) collective-permute-start(bf16[272,128]{1,0:T(8,128)(2,1)S(1)} %get-tuple-element.43), channel_id=1, source_target_pairs={{0,1},{1,0},{2,3},{3,2},{4,5},{5,4},{6,7},{7,6},{8,9},{9,8},{10,11... | collective-permute-start | bytes 208904 | tf_op jit(solution)/shard_map/return/ppermute | solution.py:315

commit v24 on v20

--- a/solution.py
+++ b/solution.py
@@ -37,7 +37,7 @@
 
 def starts(p0, p1, size):
     half = PAD // CORES
-    return jnp.concatenate([jnp.full((half, size), p[0].astype(F32), F32) for p in (p0, p1)], axis=0).astype(BF16)
+    return jnp.concatenate([jnp.broadcast_to(p[...].astype(F32), (half, size)) for p in (p0, p1)], axis=0).astype(BF16)
 
 
 def merge_kernel(p0, p1, own, q1, k1, v1, q_out, kv_out):
@@ -183,21 +183,21 @@
         return lax.optimization_barrier((a, b))[0]
 
     with jax.named_scope("swap"):
-        other = [lax.ppermute(a, "inner", along_inner(0, 1)) for a in (queries, keys, values, block_pos)]
+        here = block_pos.reshape(1, 1)
+        other = [lax.ppermute(a, "inner", along_inner(0, 1)) for a in (queries, keys, values, here)]
         own = jnp.concatenate([queries, keys, values], axis=0)
     with jax.named_scope("merge"):
-        smem = [pl.BlockSpec(memory_space=pltpu.SMEM)]
         q_piece, kv_piece = pl.pallas_call(
             merge_kernel,
             out_shape=(
                 jax.ShapeDtypeStruct((PER * both + PAD, size), BF16),
                 jax.ShapeDtypeStruct((2 * PER * both + PAD, size), BF16),
             ),
-            in_specs=smem * 2 + vmem(4),
+            in_specs=vmem(6),
             out_specs=tuple(vmem(2)),
             compiler_params=params,
             name="merge",
-        )(block_pos, other[3], own, *other[:3])
+        )(here, other[3], own, *other[:3])
     half = PER * both + PAD
     block = PER * size + PAD
 

time: 36.9 us -> 36.9 us (level)
  no operation moved by 1% of the time
where the time goes in v24:
time: 36.9 us; the launch traced here: 36.8 us
  starting transfers between devices  22.1 us (60%)
  waiting for transfers between devices  6.75 us (18%)
  Pallas kernels  6.07 us (16%)
  other arithmetic  1.06 us (3%)
  between operations  0.79 us (2%)
    ppermute x4, starting transfers between devices, over(): return lax.ppermute(a, 'outer', [(o, o ^ r) for o in range(n_out)])  7.91 us
    ppermute x3, starting transfers between devices, shards(): q_by[r] = lax.ppermute(q_piece, 'inner', along_inner(r, 0))  6.64 us
    ppermute x4, starting transfers between devices, send(): lax.ppermute(parts[x], 'inner', along_inner(r, x))  4.55 us
    ppermute x4, waiting for transfers between devices, send(): lax.ppermute(parts[x], 'inner', along_inner(r, x))  3.65 us
    pallas_call x4, Pallas kernels, score(): pl.pallas_call(functools.partial(score_kernel, r == 0), out_shape=(jax.Sh...  3.03 us
    ppermute x1, starting transfers between devices, send(): lax.ppermute(parts[0], 'inner', along_inner(low(r), 0))  1.64 us
    pallas_call x4, Pallas kernels, apply(): pl.pallas_call(functools.partial(apply_kernel, wide, rows), out_shape=sha...  1.35 us
    ppermute x4, waiting for transfers between devices, over(): return lax.ppermute(a, 'outer', [(o, o ^ r) for o in range(n_out)])  1.11 us
  transfers between devices with their start and end apart: 17, of which 5 were waited for; matrix products, arithmetic and copies ran while one was open for 3% of the time, Pallas kernels for 12%

profile of v24, /device:TPU:0, one launch (start us, length us, event | category | flops | bytes accessed | tf_op | source)
XLA Modules:
  0.0 36.8 jit_solution(3319858795241411200)
XLA Ops:
  0.0 0.5 %collective-permute-start.1 = (bf16[128,512]{1,0:T(8,128)(2,1)}, bf16[128,512]{1,0:T(8,128)(2,1)S(1)}, u32[]{:S(2)}, u32[]{:S(2)}) collective-permute-start(bf16[128,512]{1,0:T(8,128)(2,1)} %param.4), channel_id=1, source_target_pairs={{0,1},{1,0},{2,3},{3,2},{4,5},{5,4},{6,7},{7,6},{8,9},{9,8},{10,11... | collective-permute-start | bytes 393224 | tf_op jit(solution)/shard_map/swap/ppermute | solution.py:187
  0.5 0.1 collective-permute-start.2
  0.5 0.5 %collective-permute-start.3 = (bf16[128,512]{1,0:T(8,128)(2,1)}, bf16[128,512]{1,0:T(8,128)(2,1)S(1)}, u32[]{:S(2)}, u32[]{:S(2)}) collective-permute-start(bf16[128,512]{1,0:T(8,128)(2,1)} %param.6), channel_id=1, source_target_pairs={{0,1},{1,0},{2,3},{3,2},{4,5},{5,4},{6,7},{7,6},{8,9},{9,8},{10,11... | collective-permute-start | bytes 393224 | tf_op jit(solution)/shard_map/swap/ppermute | solution.py:187
  1.0 0.1 collective-permute-start
  1.7 1.1 %pad_maximum_fusion.own = bf16[384,512]{1,0:T(8,128)(2,1)S(1)} fusion(bf16[128,512]{1,0:T(8,128)(2,1)} %param.6, bf16[128,512]{1,0:T(8,128)(2,1)} %param.5, bf16[128,512]{1,0:T(8,128)(2,1)} %param.4), kind=kLoop, calls=%fused_computation | loop fusion | flops 1179648 | bytes 786432 | tf_op jit(solution)/shard_map/swap/concatenate | solution.py:188
  2.7 0.0 collective-permute-done.p1
  2.7 0.0 collective-permute-done.1.q1
  2.8 0.0 collective-permute-done.2.k1
  2.8 0.0 collective-permute-done.3.v1
  2.8 0.8 %merge.1 = (bf16[528,128]{1,0:T(8,128)(2,1)S(1)}, bf16[1040,128]{1,0:T(8,128)(2,1)S(1)}) custom-call(s32[1,1]{1,0:T(1,128)} %bitcast.1.p0, s32[1,1]{1,0:T(1,128)} %collective-permute-done.p1, bf16[384,512]{1,0:T(8,128)(2,1)S(1)} %pad_maximum_fusion.own, bf16[128,512]{1,0:T(8,128)(2,1)S(1)} %collective-permute-done.1.q1, ...), custom_call_target="tpu_custom_call" | custom-call | tf_op jit(solution)/shard_map/merge/merge/pallas_call | solution.py:190
  3.6 3.0 %collective-permute-start.7 = (bf16[1040,128]{1,0:T(8,128)(2,1)S(1)}, bf16[1040,128]{1,0:T(8,128)(2,1)S(1)}, u32[]{:S(2)}, u32[]{:S(2)}) collective-permute-start(bf16[1040,128]{1,0:T(8,128)(2,1)S(1)} %get-tuple-element.27.refs_0_), channel_id=1, source_target_pairs={{0,8},{8,0},{16,24},{24,16},{1,9},{9,1},{17,25},{25,17},{2,10},{10... | collective-permute-start | bytes 798728 | tf_op jit(solution)/shard_map/exchange/ppermute | solution.py:214
  6.6 1.5 %collective-permute-start.8 = (bf16[1040,128]{1,0:T(8,128)(2,1)S(1)}, bf16[1040,128]{1,0:T(8,128)(2,1)S(1)}, u32[]{:S(2)}, u32[]{:S(2)}) collective-permute-start(bf16[1040,128]{1,0:T(8,128)(2,1)S(1)} %get-tuple-element.27.refs_0_), channel_id=1, source_target_pairs={{0,16},{8,24},{16,0},{24,8},{1,17},{9,25},{17,1},{25,9},{2,18},{10... | collective-permute-start | bytes 798728 | tf_op jit(solution)/shard_map/exchange/ppermute | solution.py:214
  8.1 1.6 %collective-permute-start.5 = (bf16[528,128]{1,0:T(8,128)(2,1)S(1)}, bf16[528,128]{1,0:T(8,128)(2,1)S(1)}, u32[]{:S(2)}, u32[]{:S(2)}) collective-permute-start(bf16[528,128]{1,0:T(8,128)(2,1)S(1)} %get-tuple-element.39.q_ref), channel_id=1, source_target_pairs={{0,2},{1,3},{2,0},{3,1},{4,6},{5,7},{6,4},{7,5},{8,10},{9,11},{10,... | collective-permute-start | bytes 405512 | tf_op jit(solution)/shard_map/exchange/ppermute | solution.py:220
  9.7 2.5 %collective-permute-start.6 = (bf16[528,128]{1,0:T(8,128)(2,1)S(1)}, bf16[528,128]{1,0:T(8,128)(2,1)S(1)}, u32[]{:S(2)}, u32[]{:S(2)}) collective-permute-start(bf16[528,128]{1,0:T(8,128)(2,1)S(1)} %get-tuple-element.39.q_ref), channel_id=1, source_target_pairs={{0,6},{1,7},{2,4},{3,5},{4,2},{5,3},{6,0},{7,1},{8,14},{9,15},{10,... | collective-permute-start | bytes 405512 | tf_op jit(solution)/shard_map/exchange/ppermute | solution.py:220
  12.1 1.0 %collective-permute-done.7.refs_1_ = bf16[1040,128]{1,0:T(8,128)(2,1)S(1)} collective-permute-done((bf16[1040,128]{1,0:T(8,128)(2,1)S(1)}, bf16[1040,128]{1,0:T(8,128)(2,1)S(1)}, u32[]{:S(2)}, u32[]{:S(2)}) %collective-permute-start.7) | collective-permute-done | bytes 266272 | tf_op jit(solution)/shard_map/exchange/ppermute | solution.py:214
  13.1 1.8 %collective-permute-start.9 = (bf16[528,128]{1,0:T(8,128)(2,1)S(1)}, bf16[528,128]{1,0:T(8,128)(2,1)S(1)}, u32[]{:S(2)}, u32[]{:S(2)}) collective-permute-start(bf16[528,128]{1,0:T(8,128)(2,1)S(1)} %slice.8), channel_id=1, source_target_pairs={{0,16},{8,24},{16,0},{24,8},{1,17},{9,25},{17,1},{25,9},{2,18},{10... | collective-permute-start | bytes 405512 | tf_op jit(solution)/shard_map/exchange/ppermute | solution.py:214
  15.0 0.0 collective-permute-done.8.refs_2_
  15.0 0.0 collective-permute-done.5.q_ref
  15.0 1.6 %collective-permute-start.10 = (bf16[512,128]{1,0:T(8,128)(2,1)S(1)}, bf16[512,128]{1,0:T(8,128)(2,1)S(1)}, u32[]{:S(2)}, u32[]{:S(2)}) collective-permute-start(bf16[512,128]{1,0:T(8,128)(2,1)S(1)} %slice.9), channel_id=1, source_target_pairs={{0,8},{8,0},{16,24},{24,16},{1,9},{9,1},{17,25},{25,17},{2,10},{10... | collective-permute-start | bytes 393224 | tf_op jit(solution)/shard_map/exchange/ppermute | solution.py:214
  16.6 2.6 %collective-permute-start.4 = (bf16[528,128]{1,0:T(8,128)(2,1)S(1)}, bf16[528,128]{1,0:T(8,128)(2,1)S(1)}, u32[]{:S(2)}, u32[]{:S(2)}) collective-permute-start(bf16[528,128]{1,0:T(8,128)(2,1)S(1)} %get-tuple-element.39.q_ref), channel_id=1, source_target_pairs={{0,4},{1,5},{2,6},{3,7},{4,0},{5,1},{6,2},{7,3},{8,12},{9,13},{10,... | collective-permute-start | bytes 405512 | tf_op jit(solution)/shard_map/exchange/ppermute | solution.py:220
  19.2 0.0 collective-permute-done.6.q_ref
  19.2 0.0 collective-permute-done.9.refs_3_
  19.2 0.8 %score.4 = (bf16[2,1024,256]{2,1,0:T(8,128)(2,1)S(1)}, f32[16,256]{1,0:T(8,128)S(1)}) custom-call(bf16[528,128]{1,0:T(8,128)(2,1)S(1)} %collective-permute-done.6.q_ref, bf16[1040,128]{1,0:T(8,128)(2,1)S(1)} %get-tuple-element.27.refs_0_, bf16[1040,128]{1,0:T(8,128)(2,1)S(1)} %collective-permute-done.7.refs_1_, ...), custom_call_target="tpu_custom_call" | custom-call | flops 134217728 | bytes 1048576 | tf_op jit(solution)/shard_map/score/score/pallas_call | solution.py:242
  19.9 0.1 collective-permute-done.10.refs_3_
  20.0 0.3 apply.4
  20.4 1.6 %collective-permute-start.11 = (bf16[544,128]{1,0:T(8,128)(2,1)S(1)}, bf16[544,128]{1,0:T(8,128)(2,1)S(1)}, u32[]{:S(2)}, u32[]{:S(2)}) collective-permute-start(bf16[544,128]{1,0:T(8,128)(2,1)S(1)} %apply.4), channel_id=1, source_target_pairs={{0,2},{1,3},{2,0},{3,1},{4,6},{5,7},{6,4},{7,5},{8,10},{9,11},{10,... | collective-permute-start | bytes 417800 | tf_op jit(solution)/shard_map/return/ppermute | solution.py:286
  22.0 0.8 %score.5 = (bf16[2,1024,256]{2,1,0:T(8,128)(2,1)S(1)}, f32[16,256]{1,0:T(8,128)S(1)}) custom-call(bf16[528,128]{1,0:T(8,128)(2,1)S(1)} %collective-permute-done.5.q_ref, bf16[1040,128]{1,0:T(8,128)(2,1)S(1)} %get-tuple-element.27.refs_0_, bf16[1040,128]{1,0:T(8,128)(2,1)S(1)} %collective-permute-done.7.refs_1_, ...), custom_call_target="tpu_custom_call" | custom-call | flops 134217728 | bytes 1048576 | tf_op jit(solution)/shard_map/score/score/pallas_call | solution.py:242
  22.8 0.3 apply.5
  23.1 0.5 %collective-permute-start.15 = (bf16[272,128]{1,0:T(8,128)(2,1)S(1)}, bf16[272,128]{1,0:T(8,128)(2,1)S(1)}, u32[]{:S(2)}, u32[]{:S(2)}) collective-permute-start(bf16[272,128]{1,0:T(8,128)(2,1)S(1)} %get-tuple-element.34), channel_id=1, source_target_pairs={{0,2},{1,3},{2,0},{3,1},{4,6},{5,7},{6,4},{7,5},{8,10},{9,11},{10,... | collective-permute-start | bytes 208904 | tf_op jit(solution)/shard_map/return/ppermute | solution.py:284
  23.7 0.9 %collective-permute-done.4.q_ref = bf16[528,128]{1,0:T(8,128)(2,1)S(1)} collective-permute-done((bf16[528,128]{1,0:T(8,128)(2,1)S(1)}, bf16[528,128]{1,0:T(8,128)(2,1)S(1)}, u32[]{:S(2)}, u32[]{:S(2)}) %collective-permute-start.4) | collective-permute-done | bytes 135200 | tf_op jit(solution)/shard_map/exchange/ppermute | solution.py:220
  24.5 0.8 %score.6 = (bf16[2,1024,256]{2,1,0:T(8,128)(2,1)S(1)}, f32[16,256]{1,0:T(8,128)S(1)}) custom-call(bf16[528,128]{1,0:T(8,128)(2,1)S(1)} %collective-permute-done.4.q_ref, bf16[1040,128]{1,0:T(8,128)(2,1)S(1)} %get-tuple-element.27.refs_0_, bf16[1040,128]{1,0:T(8,128)(2,1)S(1)} %collective-permute-done.7.refs_1_, ...), custom_call_target="tpu_custom_call" | custom-call | flops 134217728 | bytes 1048576 | tf_op jit(solution)/shard_map/score/score/pallas_call | solution.py:242
  25.3 0.3 apply.6.refs_0_
  25.7 1.1 %collective-permute-done.11.refs_1_ = bf16[544,128]{1,0:T(8,128)(2,1)S(1)} collective-permute-done((bf16[544,128]{1,0:T(8,128)(2,1)S(1)}, bf16[544,128]{1,0:T(8,128)(2,1)S(1)}, u32[]{:S(2)}, u32[]{:S(2)}) %collective-permute-start.11) | collective-permute-done | bytes 139296 | tf_op jit(solution)/shard_map/return/ppermute | solution.py:286
  26.7 0.1 add.1
  26.8 1.9 %collective-permute-start.13 = (bf16[272,128]{1,0:T(8,128)(2,1)S(1)}, bf16[272,128]{1,0:T(8,128)(2,1)S(1)}, u32[]{:S(2)}, u32[]{:S(2)}) collective-permute-start(bf16[272,128]{1,0:T(8,128)(2,1)S(1)} %get-tuple-element.38), channel_id=1, source_target_pairs={{0,4},{1,5},{2,6},{3,7},{4,0},{5,1},{6,2},{7,3},{8,12},{9,13},{10,... | collective-permute-start | bytes 208904 | tf_op jit(solution)/shard_map/return/ppermute | solution.py:284
  28.7 0.0 collective-permute-start.14
  28.7 0.8 %score.7 = (bf16[2,1024,256]{2,1,0:T(8,128)(2,1)S(1)}, f32[16,256]{1,0:T(8,128)S(1)}) custom-call(bf16[528,128]{1,0:T(8,128)(2,1)S(1)} %get-tuple-element.39.q_ref, bf16[1040,128]{1,0:T(8,128)(2,1)S(1)} %get-tuple-element.27.refs_0_, bf16[1040,128]{1,0:T(8,128)(2,1)S(1)} %collective-permute-done.7.refs_1_, ...), custom_call_target="tpu_custom_call" | custom-call | flops 134217728 | bytes 1048576 | tf_op jit(solution)/shard_map/score/score/pallas_call | solution.py:242
  29.5 0.3 apply.7
  29.8 2.1 %collective-permute-start.16 = (bf16[272,128]{1,0:T(8,128)(2,1)S(1)}, bf16[272,128]{1,0:T(8,128)(2,1)S(1)}, u32[]{:S(2)}, u32[]{:S(2)}) collective-permute-start(bf16[272,128]{1,0:T(8,128)(2,1)S(1)} %get-tuple-element.46), channel_id=1, source_target_pairs={{0,3},{1,2},{2,1},{3,0},{4,7},{5,6},{6,5},{7,4},{8,11},{9,10},{10,... | collective-permute-start | bytes 208904 | tf_op jit(solution)/shard_map/return/ppermute | solution.py:284
  32.0 0.3 collective-permute-start.12
  32.3 0.0 collective-permute-done.15.refs_4_
  32.3 3.6 %collective-permute-done.14.refs_3_ = bf16[272,128]{1,0:T(8,128)(2,1)S(1)} collective-permute-done((bf16[272,128]{1,0:T(8,128)(2,1)S(1)}, bf16[272,128]{1,0:T(8,128)(2,1)S(1)}, u32[]{:S(2)}, u32[]{:S(2)}) %collective-permute-start.14) | collective-permute-done | bytes 69664 | tf_op jit(solution)/shard_map/return/ppermute | solution.py:284
  35.9 0.0 collective-permute-done.13.refs_2_
  35.9 0.0 collective-permute-done.16.refs_5_
  35.9 0.0 collective-permute-done.12.refs_1_
  35.9 0.8 %combine.1 = bf16[128,512]{1,0:T(8,128)(2,1)} custom-call(bf16[272,128]{1,0:T(8,128)(2,1)S(1)} %get-tuple-element.42.refs_0_, bf16[272,128]{1,0:T(8,128)(2,1)S(1)} %collective-permute-done.12.refs_1_, bf16[272,128]{1,0:T(8,128)(2,1)S(1)} %collective-permute-done.13.refs_2_, bf16[272,128]{1,0:T(8,128)(2,1)S(1)} %collective-permute-done.14.refs_3_, ...), custom_call_target="tpu_custom_call" | custom-call | tf_op jit(solution)/shard_map/combine/combine/pallas_call | solution.py:309
  (2 shorter events, 0.0 us)
Async XLA Ops:
  0.0 2.7 %collective-permute-start.1 = (bf16[128,512]{1,0:T(8,128)(2,1)}, bf16[128,512]{1,0:T(8,128)(2,1)S(1)}, u32[]{:S(2)}, u32[]{:S(2)}) collective-permute-start(bf16[128,512]{1,0:T(8,128)(2,1)} %param.4), channel_id=1, source_target_pairs={{0,1},{1,0},{2,3},{3,2},{4,5},{5,4},{6,7},{7,6},{8,9},{9,8},{10,11... | collective-permute-start | bytes 393224 | tf_op jit(solution)/shard_map/swap/ppermute | solution.py:187
  0.5 2.3 %collective-permute-start.2 = (bf16[128,512]{1,0:T(8,128)(2,1)}, bf16[128,512]{1,0:T(8,128)(2,1)S(1)}, u32[]{:S(2)}, u32[]{:S(2)}) collective-permute-start(bf16[128,512]{1,0:T(8,128)(2,1)} %param.5), channel_id=1, source_target_pairs={{0,1},{1,0},{2,3},{3,2},{4,5},{5,4},{6,7},{7,6},{8,9},{9,8},{10,11... | collective-permute-start | bytes 393224 | tf_op jit(solution)/shard_map/swap/ppermute | solution.py:187
  0.5 2.3 %collective-permute-start.3 = (bf16[128,512]{1,0:T(8,128)(2,1)}, bf16[128,512]{1,0:T(8,128)(2,1)S(1)}, u32[]{:S(2)}, u32[]{:S(2)}) collective-permute-start(bf16[128,512]{1,0:T(8,128)(2,1)} %param.6), channel_id=1, source_target_pairs={{0,1},{1,0},{2,3},{3,2},{4,5},{5,4},{6,7},{7,6},{8,9},{9,8},{10,11... | collective-permute-start | bytes 393224 | tf_op jit(solution)/shard_map/swap/ppermute | solution.py:187
  1.0 1.8 %collective-permute-start = (s32[1,1]{1,0:T(1,128)}, s32[1,1]{1,0:T(1,128)}, u32[]{:S(2)}, u32[]{:S(2)}) collective-permute-start(s32[1,1]{1,0:T(1,128)} %bitcast), channel_id=1, source_target_pairs={{0,1},{1,0},{2,3},{3,2},{4,5},{5,4},{6,7},{7,6},{8,9},{9,8},{10,11... | collective-permute-start | bytes 20 | tf_op jit(solution)/shard_map/swap/ppermute | solution.py:187
  3.6 9.6 %collective-permute-start.7 = (bf16[1040,128]{1,0:T(8,128)(2,1)S(1)}, bf16[1040,128]{1,0:T(8,128)(2,1)S(1)}, u32[]{:S(2)}, u32[]{:S(2)}) collective-permute-start(bf16[1040,128]{1,0:T(8,128)(2,1)S(1)} %get-tuple-element.27.refs_0_), channel_id=1, source_target_pairs={{0,8},{8,0},{16,24},{24,16},{1,9},{9,1},{17,25},{25,17},{2,10},{10... | collective-permute-start | bytes 798728 | tf_op jit(solution)/shard_map/exchange/ppermute | solution.py:214
  6.6 8.4 %collective-permute-start.8 = (bf16[1040,128]{1,0:T(8,128)(2,1)S(1)}, bf16[1040,128]{1,0:T(8,128)(2,1)S(1)}, u32[]{:S(2)}, u32[]{:S(2)}) collective-permute-start(bf16[1040,128]{1,0:T(8,128)(2,1)S(1)} %get-tuple-element.27.refs_0_), channel_id=1, source_target_pairs={{0,16},{8,24},{16,0},{24,8},{1,17},{9,25},{17,1},{25,9},{2,18},{10... | collective-permute-start | bytes 798728 | tf_op jit(solution)/shard_map/exchange/ppermute | solution.py:214
  8.1 6.9 %collective-permute-start.5 = (bf16[528,128]{1,0:T(8,128)(2,1)S(1)}, bf16[528,128]{1,0:T(8,128)(2,1)S(1)}, u32[]{:S(2)}, u32[]{:S(2)}) collective-permute-start(bf16[528,128]{1,0:T(8,128)(2,1)S(1)} %get-tuple-element.39.q_ref), channel_id=1, source_target_pairs={{0,2},{1,3},{2,0},{3,1},{4,6},{5,7},{6,4},{7,5},{8,10},{9,11},{10,... | collective-permute-start | bytes 405512 | tf_op jit(solution)/shard_map/exchange/ppermute | solution.py:220
  9.7 9.5 %collective-permute-start.6 = (bf16[528,128]{1,0:T(8,128)(2,1)S(1)}, bf16[528,128]{1,0:T(8,128)(2,1)S(1)}, u32[]{:S(2)}, u32[]{:S(2)}) collective-permute-start(bf16[528,128]{1,0:T(8,128)(2,1)S(1)} %get-tuple-element.39.q_ref), channel_id=1, source_target_pairs={{0,6},{1,7},{2,4},{3,5},{4,2},{5,3},{6,0},{7,1},{8,14},{9,15},{10,... | collective-permute-start | bytes 405512 | tf_op jit(solution)/shard_map/exchange/ppermute | solution.py:220
  13.1 6.0 %collective-permute-start.9 = (bf16[528,128]{1,0:T(8,128)(2,1)S(1)}, bf16[528,128]{1,0:T(8,128)(2,1)S(1)}, u32[]{:S(2)}, u32[]{:S(2)}) collective-permute-start(bf16[528,128]{1,0:T(8,128)(2,1)S(1)} %slice.8), channel_id=1, source_target_pairs={{0,16},{8,24},{16,0},{24,8},{1,17},{9,25},{17,1},{25,9},{2,18},{10... | collective-permute-start | bytes 405512 | tf_op jit(solution)/shard_map/exchange/ppermute | solution.py:214
  15.0 5.0 %collective-permute-start.10 = (bf16[512,128]{1,0:T(8,128)(2,1)S(1)}, bf16[512,128]{1,0:T(8,128)(2,1)S(1)}, u32[]{:S(2)}, u32[]{:S(2)}) collective-permute-start(bf16[512,128]{1,0:T(8,128)(2,1)S(1)} %slice.9), channel_id=1, source_target_pairs={{0,8},{8,0},{16,24},{24,16},{1,9},{9,1},{17,25},{25,17},{2,10},{10... | collective-permute-start | bytes 393224 | tf_op jit(solution)/shard_map/exchange/ppermute | solution.py:214
  16.6 8.0 %collective-permute-start.4 = (bf16[528,128]{1,0:T(8,128)(2,1)S(1)}, bf16[528,128]{1,0:T(8,128)(2,1)S(1)}, u32[]{:S(2)}, u32[]{:S(2)}) collective-permute-start(bf16[528,128]{1,0:T(8,128)(2,1)S(1)} %get-tuple-element.39.q_ref), channel_id=1, source_target_pairs={{0,4},{1,5},{2,6},{3,7},{4,0},{5,1},{6,2},{7,3},{8,12},{9,13},{10,... | collective-permute-start | bytes 405512 | tf_op jit(solution)/shard_map/exchange/ppermute | solution.py:220
  20.4 6.3 %collective-permute-start.11 = (bf16[544,128]{1,0:T(8,128)(2,1)S(1)}, bf16[544,128]{1,0:T(8,128)(2,1)S(1)}, u32[]{:S(2)}, u32[]{:S(2)}) collective-permute-start(bf16[544,128]{1,0:T(8,128)(2,1)S(1)} %apply.4), channel_id=1, source_target_pairs={{0,2},{1,3},{2,0},{3,1},{4,6},{5,7},{6,4},{7,5},{8,10},{9,11},{10,... | collective-permute-start | bytes 417800 | tf_op jit(solution)/shard_map/return/ppermute | solution.py:286
  23.1 9.1 %collective-permute-start.15 = (bf16[272,128]{1,0:T(8,128)(2,1)S(1)}, bf16[272,128]{1,0:T(8,128)(2,1)S(1)}, u32[]{:S(2)}, u32[]{:S(2)}) collective-permute-start(bf16[272,128]{1,0:T(8,128)(2,1)S(1)} %get-tuple-element.34), channel_id=1, source_target_pairs={{0,2},{1,3},{2,0},{3,1},{4,6},{5,7},{6,4},{7,5},{8,10},{9,11},{10,... | collective-permute-start | bytes 208904 | tf_op jit(solution)/shard_map/return/ppermute | solution.py:284
  26.8 9.1 %collective-permute-start.13 = (bf16[272,128]{1,0:T(8,128)(2,1)S(1)}, bf16[272,128]{1,0:T(8,128)(2,1)S(1)}, u32[]{:S(2)}, u32[]{:S(2)}) collective-permute-start(bf16[272,128]{1,0:T(8,128)(2,1)S(1)} %get-tuple-element.38), channel_id=1, source_target_pairs={{0,4},{1,5},{2,6},{3,7},{4,0},{5,1},{6,2},{7,3},{8,12},{9,13},{10,... | collective-permute-start | bytes 208904 | tf_op jit(solution)/shard_map/return/ppermute | solution.py:284
  28.7 7.2 %collective-permute-start.14 = (bf16[272,128]{1,0:T(8,128)(2,1)S(1)}, bf16[272,128]{1,0:T(8,128)(2,1)S(1)}, u32[]{:S(2)}, u32[]{:S(2)}) collective-permute-start(bf16[272,128]{1,0:T(8,128)(2,1)S(1)} %get-tuple-element.44), channel_id=1, source_target_pairs={{0,5},{1,4},{2,7},{3,6},{4,1},{5,0},{6,3},{7,2},{8,13},{9,12},{10,... | collective-permute-start | bytes 208904 | tf_op jit(solution)/shard_map/return/ppermute | solution.py:284
  29.8 6.1 %collective-permute-start.16 = (bf16[272,128]{1,0:T(8,128)(2,1)S(1)}, bf16[272,128]{1,0:T(8,128)(2,1)S(1)}, u32[]{:S(2)}, u32[]{:S(2)}) collective-permute-start(bf16[272,128]{1,0:T(8,128)(2,1)S(1)} %get-tuple-element.46), channel_id=1, source_target_pairs={{0,3},{1,2},{2,1},{3,0},{4,7},{5,6},{6,5},{7,4},{8,11},{9,10},{10,... | collective-permute-start | bytes 208904 | tf_op jit(solution)/shard_map/return/ppermute | solution.py:284
  32.0 4.0 %collective-permute-start.12 = (bf16[272,128]{1,0:T(8,128)(2,1)S(1)}, bf16[272,128]{1,0:T(8,128)(2,1)S(1)}, u32[]{:S(2)}, u32[]{:S(2)}) collective-permute-start(bf16[272,128]{1,0:T(8,128)(2,1)S(1)} %get-tuple-element.43), channel_id=1, source_target_pairs={{0,1},{1,0},{2,3},{3,2},{4,5},{5,4},{6,7},{7,6},{8,9},{9,8},{10,11... | collective-permute-start | bytes 208904 | tf_op jit(solution)/shard_map/return/ppermute | solution.py:307

commit v25 on v20

--- a/solution.py
+++ b/solution.py
@@ -216,8 +216,9 @@
     with jax.named_scope("exchange"):
         whole = {r: over(kv_piece, r) if r else kv_piece for r in range(n_out) if single(r)}
         q_by = {0: q_piece}
-        for r in reversed(range(1, chips)):
-            q_by[r] = lax.ppermute(q_piece, "inner", along_inner(r, 0))
+        for r in sorted(range(1, chips), key=lambda r: (r != chips - 1, r)):
+            piece = q_piece if r in (1, chips - 1) else after(q_piece, q_by[1])
+            q_by[r] = lax.ppermute(piece, "inner", along_inner(r, 0))
         k_by = {r: a[:half, :] for r, a in whole.items() if r}
         v_by = {r: a[half:, :] for r, a in whole.items() if r}
         for r in range(1, n_out):
@@ -225,8 +226,7 @@
                 k_by[r] = over(k_by[r - high(r)], high(r))
         for r in sorted(range(1, n_out), key=lambda r: r.bit_count()):
             if not single(r):
-                v = v_by[r - low(r)]
-                v_by[r] = over(after(v, q_by[1]) if chips > 1 else v, low(r))
+                v_by[r] = over(v_by[r - low(r)], low(r))
         ks = [whole[r] if r in whole else k_by[r] for r in range(n_out)]
         vs = [whole[r] if r in whole else v_by[r] for r in range(n_out)]
         rows = tuple(half if r in whole else 0 for r in range(n_out))

time: 36.9 us -> 36.9 us (level)
  no operation moved by 1% of the time
where the time goes in v25:
time: 36.9 us; the launch traced here: 36.7 us
  starting transfers between devices  22.1 us (60%)
  waiting for transfers between devices  6.72 us (18%)
  Pallas kernels  6.06 us (16%)
  other arithmetic  1.06 us (3%)
  between operations  0.79 us (2%)
    ppermute x4, starting transfers between devices, over(): return lax.ppermute(a, 'outer', [(o, o ^ r) for o in range(n_out)])  7.91 us
    ppermute x3, starting transfers between devices, shards(): q_by[r] = lax.ppermute(piece, 'inner', along_inner(r, 0))  6.64 us
    ppermute x4, starting transfers between devices, send(): lax.ppermute(parts[x], 'inner', along_inner(r, x))  4.54 us
    ppermute x4, waiting for transfers between devices, send(): lax.ppermute(parts[x], 'inner', along_inner(r, x))  3.62 us
    pallas_call x4, Pallas kernels, score(): pl.pallas_call(functools.partial(score_kernel, r == 0), out_shape=(jax.Sh...  3.02 us
    ppermute x1, starting transfers between devices, send(): lax.ppermute(parts[0], 'inner', along_inner(low(r), 0))  1.64 us
    pallas_call x4, Pallas kernels, apply(): pl.pallas_call(functools.partial(apply_kernel, wide, rows), out_shape=sha...  1.35 us
    ppermute x4, waiting for transfers between devices, over(): return lax.ppermute(a, 'outer', [(o, o ^ r) for o in range(n_out)])  1.11 us
  transfers between devices with their start and end apart: 17, of which 5 were waited for; matrix products, arithmetic and copies ran while one was open for 3% of the time, Pallas kernels for 12%

profile of v25, /device:TPU:0, one launch (start us, length us, event | category | flops | bytes accessed | tf_op | source)
XLA Modules:
  0.0 36.7 jit_solution(12860983655189660889)
XLA Ops:
  0.0 0.5 %collective-permute-start.1 = (bf16[128,512]{1,0:T(8,128)(2,1)}, bf16[128,512]{1,0:T(8,128)(2,1)S(1)}, u32[]{:S(2)}, u32[]{:S(2)}) collective-permute-start(bf16[128,512]{1,0:T(8,128)(2,1)} %param.4), channel_id=1, source_target_pairs={{0,1},{1,0},{2,3},{3,2},{4,5},{5,4},{6,7},{7,6},{8,9},{9,8},{10,11... | collective-permute-start | bytes 393224 | tf_op jit(solution)/shard_map/swap/ppermute | solution.py:186
  0.5 0.1 collective-permute-start.2
  0.5 0.5 %collective-permute-start.3 = (bf16[128,512]{1,0:T(8,128)(2,1)}, bf16[128,512]{1,0:T(8,128)(2,1)S(1)}, u32[]{:S(2)}, u32[]{:S(2)}) collective-permute-start(bf16[128,512]{1,0:T(8,128)(2,1)} %param.6), channel_id=1, source_target_pairs={{0,1},{1,0},{2,3},{3,2},{4,5},{5,4},{6,7},{7,6},{8,9},{9,8},{10,11... | collective-permute-start | bytes 393224 | tf_op jit(solution)/shard_map/swap/ppermute | solution.py:186
  1.0 0.1 collective-permute-start
  1.7 1.1 %pad_maximum_fusion.own = bf16[384,512]{1,0:T(8,128)(2,1)S(1)} fusion(bf16[128,512]{1,0:T(8,128)(2,1)} %param.6, bf16[128,512]{1,0:T(8,128)(2,1)} %param.5, bf16[128,512]{1,0:T(8,128)(2,1)} %param.4), kind=kLoop, calls=%fused_computation | loop fusion | flops 1179648 | bytes 786432 | tf_op jit(solution)/shard_map/swap/concatenate | solution.py:187
  2.7 0.0 collective-permute-done.p1
  2.7 0.0 collective-permute-done.1.q1
  2.8 0.0 collective-permute-done.2.k1
  2.8 0.0 collective-permute-done.3.v1
  2.8 0.8 %merge.1 = (bf16[528,128]{1,0:T(8,128)(2,1)S(1)}, bf16[1040,128]{1,0:T(8,128)(2,1)S(1)}) custom-call(s32[1]{0:T(128)S(6)} %copy.5.p0, s32[1]{0:T(128)} %collective-permute-done.p1, bf16[384,512]{1,0:T(8,128)(2,1)S(1)} %pad_maximum_fusion.own, bf16[128,512]{1,0:T(8,128)(2,1)S(1)} %collective-permute-done.1.q1, ...), custom_call_target="tpu_custom_call" | custom-call | tf_op jit(solution)/shard_map/merge/merge/pallas_call | solution.py:190
  3.6 3.0 %collective-permute-start.7 = (bf16[1040,128]{1,0:T(8,128)(2,1)S(1)}, bf16[1040,128]{1,0:T(8,128)(2,1)S(1)}, u32[]{:S(2)}, u32[]{:S(2)}) collective-permute-start(bf16[1040,128]{1,0:T(8,128)(2,1)S(1)} %get-tuple-element.28.refs_0_), channel_id=1, source_target_pairs={{0,8},{8,0},{16,24},{24,16},{1,9},{9,1},{17,25},{25,17},{2,10},{10... | collective-permute-start | bytes 798728 | tf_op jit(solution)/shard_map/exchange/ppermute | solution.py:214
  6.6 1.5 %collective-permute-start.8 = (bf16[1040,128]{1,0:T(8,128)(2,1)S(1)}, bf16[1040,128]{1,0:T(8,128)(2,1)S(1)}, u32[]{:S(2)}, u32[]{:S(2)}) collective-permute-start(bf16[1040,128]{1,0:T(8,128)(2,1)S(1)} %get-tuple-element.28.refs_0_), channel_id=1, source_target_pairs={{0,16},{8,24},{16,0},{24,8},{1,17},{9,25},{17,1},{25,9},{2,18},{10... | collective-permute-start | bytes 798728 | tf_op jit(solution)/shard_map/exchange/ppermute | solution.py:214
  8.1 1.6 %collective-permute-start.4 = (bf16[528,128]{1,0:T(8,128)(2,1)S(1)}, bf16[528,128]{1,0:T(8,128)(2,1)S(1)}, u32[]{:S(2)}, u32[]{:S(2)}) collective-permute-start(bf16[528,128]{1,0:T(8,128)(2,1)S(1)} %get-tuple-element.39.q_ref), channel_id=1, source_target_pairs={{0,2},{1,3},{2,0},{3,1},{4,6},{5,7},{6,4},{7,5},{8,10},{9,11},{10,... | collective-permute-start | bytes 405512 | tf_op jit(solution)/shard_map/exchange/ppermute | solution.py:221
  9.7 2.5 %collective-permute-start.6 = (bf16[528,128]{1,0:T(8,128)(2,1)S(1)}, bf16[528,128]{1,0:T(8,128)(2,1)S(1)}, u32[]{:S(2)}, u32[]{:S(2)}) collective-permute-start(bf16[528,128]{1,0:T(8,128)(2,1)S(1)} %get-tuple-element.39.q_ref), channel_id=1, source_target_pairs={{0,6},{1,7},{2,4},{3,5},{4,2},{5,3},{6,0},{7,1},{8,14},{9,15},{10,... | collective-permute-start | bytes 405512 | tf_op jit(solution)/shard_map/exchange/ppermute | solution.py:221
  12.1 1.0 %collective-permute-done.7.refs_1_ = bf16[1040,128]{1,0:T(8,128)(2,1)S(1)} collective-permute-done((bf16[1040,128]{1,0:T(8,128)(2,1)S(1)}, bf16[1040,128]{1,0:T(8,128)(2,1)S(1)}, u32[]{:S(2)}, u32[]{:S(2)}) %collective-permute-start.7) | collective-permute-done | bytes 266272 | tf_op jit(solution)/shard_map/exchange/ppermute | solution.py:214
  13.1 1.8 %collective-permute-start.9 = (bf16[528,128]{1,0:T(8,128)(2,1)S(1)}, bf16[528,128]{1,0:T(8,128)(2,1)S(1)}, u32[]{:S(2)}, u32[]{:S(2)}) collective-permute-start(bf16[528,128]{1,0:T(8,128)(2,1)S(1)} %slice.8), channel_id=1, source_target_pairs={{0,16},{8,24},{16,0},{24,8},{1,17},{9,25},{17,1},{25,9},{2,18},{10... | collective-permute-start | bytes 405512 | tf_op jit(solution)/shard_map/exchange/ppermute | solution.py:214
  15.0 0.0 collective-permute-done.8.refs_2_
  15.0 1.6 %collective-permute-start.10 = (bf16[512,128]{1,0:T(8,128)(2,1)S(1)}, bf16[512,128]{1,0:T(8,128)(2,1)S(1)}, u32[]{:S(2)}, u32[]{:S(2)}) collective-permute-start(bf16[512,128]{1,0:T(8,128)(2,1)S(1)} %slice.9), channel_id=1, source_target_pairs={{0,8},{8,0},{16,24},{24,16},{1,9},{9,1},{17,25},{25,17},{2,10},{10... | collective-permute-start | bytes 393224 | tf_op jit(solution)/shard_map/exchange/ppermute | solution.py:214
  16.6 0.0 collective-permute-done.4.q_ref
  16.6 2.6 %collective-permute-start.5 = (bf16[528,128]{1,0:T(8,128)(2,1)S(1)}, bf16[528,128]{1,0:T(8,128)(2,1)S(1)}, u32[]{:S(2)}, u32[]{:S(2)}) collective-permute-start(bf16[528,128]{1,0:T(8,128)(2,1)S(1)} %get-tuple-element.39.q_ref), channel_id=1, source_target_pairs={{0,4},{1,5},{2,6},{3,7},{4,0},{5,1},{6,2},{7,3},{8,12},{9,13},{10,... | collective-permute-start | bytes 405512 | tf_op jit(solution)/shard_map/exchange/ppermute | solution.py:221
  19.1 0.0 collective-permute-done.6.q_ref
  19.1 0.0 collective-permute-done.9.refs_3_
  19.2 0.8 %score.4 = (bf16[2,1024,256]{2,1,0:T(8,128)(2,1)S(1)}, f32[16,256]{1,0:T(8,128)S(1)}) custom-call(bf16[528,128]{1,0:T(8,128)(2,1)S(1)} %collective-permute-done.6.q_ref, bf16[1040,128]{1,0:T(8,128)(2,1)S(1)} %get-tuple-element.28.refs_0_, bf16[1040,128]{1,0:T(8,128)(2,1)S(1)} %collective-permute-done.7.refs_1_, ...), custom_call_target="tpu_custom_call" | custom-call | flops 134217728 | bytes 1048576 | tf_op jit(solution)/shard_map/score/score/pallas_call | solution.py:242
  19.9 0.1 collective-permute-done.10.refs_3_
  20.0 0.3 apply.4
  20.4 1.6 %collective-permute-start.11 = (bf16[544,128]{1,0:T(8,128)(2,1)S(1)}, bf16[544,128]{1,0:T(8,128)(2,1)S(1)}, u32[]{:S(2)}, u32[]{:S(2)}) collective-permute-start(bf16[544,128]{1,0:T(8,128)(2,1)S(1)} %apply.4), channel_id=1, source_target_pairs={{0,2},{1,3},{2,0},{3,1},{4,6},{5,7},{6,4},{7,5},{8,10},{9,11},{10,... | collective-permute-start | bytes 417800 | tf_op jit(solution)/shard_map/return/ppermute | solution.py:286
  22.0 0.7 %score.5 = (bf16[2,1024,256]{2,1,0:T(8,128)(2,1)S(1)}, f32[16,256]{1,0:T(8,128)S(1)}) custom-call(bf16[528,128]{1,0:T(8,128)(2,1)S(1)} %collective-permute-done.4.q_ref, bf16[1040,128]{1,0:T(8,128)(2,1)S(1)} %get-tuple-element.28.refs_0_, bf16[1040,128]{1,0:T(8,128)(2,1)S(1)} %collective-permute-done.7.refs_1_, ...), custom_call_target="tpu_custom_call" | custom-call | flops 134217728 | bytes 1048576 | tf_op jit(solution)/shard_map/score/score/pallas_call | solution.py:242
  22.8 0.3 apply.5
  23.1 0.5 %collective-permute-start.15 = (bf16[272,128]{1,0:T(8,128)(2,1)S(1)}, bf16[272,128]{1,0:T(8,128)(2,1)S(1)}, u32[]{:S(2)}, u32[]{:S(2)}) collective-permute-start(bf16[272,128]{1,0:T(8,128)(2,1)S(1)} %get-tuple-element.34), channel_id=1, source_target_pairs={{0,2},{1,3},{2,0},{3,1},{4,6},{5,7},{6,4},{7,5},{8,10},{9,11},{10,... | collective-permute-start | bytes 208904 | tf_op jit(solution)/shard_map/return/ppermute | solution.py:284
  23.6 0.9 %collective-permute-done.5.q_ref = bf16[528,128]{1,0:T(8,128)(2,1)S(1)} collective-permute-done((bf16[528,128]{1,0:T(8,128)(2,1)S(1)}, bf16[528,128]{1,0:T(8,128)(2,1)S(1)}, u32[]{:S(2)}, u32[]{:S(2)}) %collective-permute-start.5) | collective-permute-done | bytes 135200 | tf_op jit(solution)/shard_map/exchange/ppermute | solution.py:221
  24.5 0.8 %score.6 = (bf16[2,1024,256]{2,1,0:T(8,128)(2,1)S(1)}, f32[16,256]{1,0:T(8,128)S(1)}) custom-call(bf16[528,128]{1,0:T(8,128)(2,1)S(1)} %collective-permute-done.5.q_ref, bf16[1040,128]{1,0:T(8,128)(2,1)S(1)} %get-tuple-element.28.refs_0_, bf16[1040,128]{1,0:T(8,128)(2,1)S(1)} %collective-permute-done.7.refs_1_, ...), custom_call_target="tpu_custom_call" | custom-call | flops 134217728 | bytes 1048576 | tf_op jit(solution)/shard_map/score/score/pallas_call | solution.py:242
  25.3 0.3 apply.6.refs_0_
  25.6 1.1 %collective-permute-done.11.refs_1_ = bf16[544,128]{1,0:T(8,128)(2,1)S(1)} collective-permute-done((bf16[544,128]{1,0:T(8,128)(2,1)S(1)}, bf16[544,128]{1,0:T(8,128)(2,1)S(1)}, u32[]{:S(2)}, u32[]{:S(2)}) %collective-permute-start.11) | collective-permute-done | bytes 139296 | tf_op jit(solution)/shard_map/return/ppermute | solution.py:286
  26.7 0.1 add.1
  26.8 1.7 %collective-permute-start.13 = (bf16[272,128]{1,0:T(8,128)(2,1)S(1)}, bf16[272,128]{1,0:T(8,128)(2,1)S(1)}, u32[]{:S(2)}, u32[]{:S(2)}) collective-permute-start(bf16[272,128]{1,0:T(8,128)(2,1)S(1)} %get-tuple-element.38), channel_id=1, source_target_pairs={{0,4},{1,5},{2,6},{3,7},{4,0},{5,1},{6,2},{7,3},{8,12},{9,13},{10,... | collective-permute-start | bytes 208904 | tf_op jit(solution)/shard_map/return/ppermute | solution.py:284
  28.5 0.0 collective-permute-start.14
  28.5 0.8 %score.7 = (bf16[2,1024,256]{2,1,0:T(8,128)(2,1)S(1)}, f32[16,256]{1,0:T(8,128)S(1)}) custom-call(bf16[528,128]{1,0:T(8,128)(2,1)S(1)} %get-tuple-element.39.q_ref, bf16[1040,128]{1,0:T(8,128)(2,1)S(1)} %get-tuple-element.28.refs_0_, bf16[1040,128]{1,0:T(8,128)(2,1)S(1)} %collective-permute-done.7.refs_1_, ...), custom_call_target="tpu_custom_call" | custom-call | flops 134217728 | bytes 1048576 | tf_op jit(solution)/shard_map/score/score/pallas_call | solution.py:242
  29.3 0.3 apply.7
  29.6 2.3 %collective-permute-start.16 = (bf16[272,128]{1,0:T(8,128)(2,1)S(1)}, bf16[272,128]{1,0:T(8,128)(2,1)S(1)}, u32[]{:S(2)}, u32[]{:S(2)}) collective-permute-start(bf16[272,128]{1,0:T(8,128)(2,1)S(1)} %get-tuple-element.46), channel_id=1, source_target_pairs={{0,3},{1,2},{2,1},{3,0},{4,7},{5,6},{6,5},{7,4},{8,11},{9,10},{10,... | collective-permute-start | bytes 208904 | tf_op jit(solution)/shard_map/return/ppermute | solution.py:284
  31.9 0.3 collective-permute-start.12
  32.3 0.0 collective-permute-done.15.refs_4_
  32.3 3.6 %collective-permute-done.14.refs_3_ = bf16[272,128]{1,0:T(8,128)(2,1)S(1)} collective-permute-done((bf16[272,128]{1,0:T(8,128)(2,1)S(1)}, bf16[272,128]{1,0:T(8,128)(2,1)S(1)}, u32[]{:S(2)}, u32[]{:S(2)}) %collective-permute-start.14) | collective-permute-done | bytes 69664 | tf_op jit(solution)/shard_map/return/ppermute | solution.py:284
  35.9 0.0 collective-permute-done.13.refs_2_
  35.9 0.0 collective-permute-done.16.refs_5_
  35.9 0.0 collective-permute-done.12.refs_1_
  35.9 0.8 %combine.1 = bf16[128,512]{1,0:T(8,128)(2,1)} custom-call(bf16[272,128]{1,0:T(8,128)(2,1)S(1)} %get-tuple-element.42.refs_0_, bf16[272,128]{1,0:T(8,128)(2,1)S(1)} %collective-permute-done.12.refs_1_, bf16[272,128]{1,0:T(8,128)(2,1)S(1)} %collective-permute-done.13.refs_2_, bf16[272,128]{1,0:T(8,128)(2,1)S(1)} %collective-permute-done.14.refs_3_, ...), custom_call_target="tpu_custom_call" | custom-call | tf_op jit(solution)/shard_map/combine/combine/pallas_call | solution.py:309
  (2 shorter events, 0.0 us)
Async XLA Ops:
  0.0 2.7 %collective-permute-start.1 = (bf16[128,512]{1,0:T(8,128)(2,1)}, bf16[128,512]{1,0:T(8,128)(2,1)S(1)}, u32[]{:S(2)}, u32[]{:S(2)}) collective-permute-start(bf16[128,512]{1,0:T(8,128)(2,1)} %param.4), channel_id=1, source_target_pairs={{0,1},{1,0},{2,3},{3,2},{4,5},{5,4},{6,7},{7,6},{8,9},{9,8},{10,11... | collective-permute-start | bytes 393224 | tf_op jit(solution)/shard_map/swap/ppermute | solution.py:186
  0.5 2.3 %collective-permute-start.2 = (bf16[128,512]{1,0:T(8,128)(2,1)}, bf16[128,512]{1,0:T(8,128)(2,1)S(1)}, u32[]{:S(2)}, u32[]{:S(2)}) collective-permute-start(bf16[128,512]{1,0:T(8,128)(2,1)} %param.5), channel_id=1, source_target_pairs={{0,1},{1,0},{2,3},{3,2},{4,5},{5,4},{6,7},{7,6},{8,9},{9,8},{10,11... | collective-permute-start | bytes 393224 | tf_op jit(solution)/shard_map/swap/ppermute | solution.py:186
  0.5 2.3 %collective-permute-start.3 = (bf16[128,512]{1,0:T(8,128)(2,1)}, bf16[128,512]{1,0:T(8,128)(2,1)S(1)}, u32[]{:S(2)}, u32[]{:S(2)}) collective-permute-start(bf16[128,512]{1,0:T(8,128)(2,1)} %param.6), channel_id=1, source_target_pairs={{0,1},{1,0},{2,3},{3,2},{4,5},{5,4},{6,7},{7,6},{8,9},{9,8},{10,11... | collective-permute-start | bytes 393224 | tf_op jit(solution)/shard_map/swap/ppermute | solution.py:186
  1.0 1.8 %collective-permute-start = (s32[1]{0:T(128)}, s32[1]{0:T(128)}, u32[]{:S(2)}, u32[]{:S(2)}) collective-permute-start(s32[1]{0:T(128)} %param.7), channel_id=1, source_target_pairs={{0,1},{1,0},{2,3},{3,2},{4,5},{5,4},{6,7},{7,6},{8,9},{9,8},{10,11... | collective-permute-start | bytes 20 | tf_op jit(solution)/shard_map/swap/ppermute | solution.py:186
  3.6 9.6 %collective-permute-start.7 = (bf16[1040,128]{1,0:T(8,128)(2,1)S(1)}, bf16[1040,128]{1,0:T(8,128)(2,1)S(1)}, u32[]{:S(2)}, u32[]{:S(2)}) collective-permute-start(bf16[1040,128]{1,0:T(8,128)(2,1)S(1)} %get-tuple-element.28.refs_0_), channel_id=1, source_target_pairs={{0,8},{8,0},{16,24},{24,16},{1,9},{9,1},{17,25},{25,17},{2,10},{10... | collective-permute-start | bytes 798728 | tf_op jit(solution)/shard_map/exchange/ppermute | solution.py:214
  6.6 8.4 %collective-permute-start.8 = (bf16[1040,128]{1,0:T(8,128)(2,1)S(1)}, bf16[1040,128]{1,0:T(8,128)(2,1)S(1)}, u32[]{:S(2)}, u32[]{:S(2)}) collective-permute-start(bf16[1040,128]{1,0:T(8,128)(2,1)S(1)} %get-tuple-element.28.refs_0_), channel_id=1, source_target_pairs={{0,16},{8,24},{16,0},{24,8},{1,17},{9,25},{17,1},{25,9},{2,18},{10... | collective-permute-start | bytes 798728 | tf_op jit(solution)/shard_map/exchange/ppermute | solution.py:214
  8.1 8.5 %collective-permute-start.4 = (bf16[528,128]{1,0:T(8,128)(2,1)S(1)}, bf16[528,128]{1,0:T(8,128)(2,1)S(1)}, u32[]{:S(2)}, u32[]{:S(2)}) collective-permute-start(bf16[528,128]{1,0:T(8,128)(2,1)S(1)} %get-tuple-element.39.q_ref), channel_id=1, source_target_pairs={{0,2},{1,3},{2,0},{3,1},{4,6},{5,7},{6,4},{7,5},{8,10},{9,11},{10,... | collective-permute-start | bytes 405512 | tf_op jit(solution)/shard_map/exchange/ppermute | solution.py:221
  9.7 9.5 %collective-permute-start.6 = (bf16[528,128]{1,0:T(8,128)(2,1)S(1)}, bf16[528,128]{1,0:T(8,128)(2,1)S(1)}, u32[]{:S(2)}, u32[]{:S(2)}) collective-permute-start(bf16[528,128]{1,0:T(8,128)(2,1)S(1)} %get-tuple-element.39.q_ref), channel_id=1, source_target_pairs={{0,6},{1,7},{2,4},{3,5},{4,2},{5,3},{6,0},{7,1},{8,14},{9,15},{10,... | collective-permute-start | bytes 405512 | tf_op jit(solution)/shard_map/exchange/ppermute | solution.py:221
  13.1 6.0 %collective-permute-start.9 = (bf16[528,128]{1,0:T(8,128)(2,1)S(1)}, bf16[528,128]{1,0:T(8,128)(2,1)S(1)}, u32[]{:S(2)}, u32[]{:S(2)}) collective-permute-start(bf16[528,128]{1,0:T(8,128)(2,1)S(1)} %slice.8), channel_id=1, source_target_pairs={{0,16},{8,24},{16,0},{24,8},{1,17},{9,25},{17,1},{25,9},{2,18},{10... | collective-permute-start | bytes 405512 | tf_op jit(solution)/shard_map/exchange/ppermute | solution.py:214
  15.0 5.0 %collective-permute-start.10 = (bf16[512,128]{1,0:T(8,128)(2,1)S(1)}, bf16[512,128]{1,0:T(8,128)(2,1)S(1)}, u32[]{:S(2)}, u32[]{:S(2)}) collective-permute-start(bf16[512,128]{1,0:T(8,128)(2,1)S(1)} %slice.9), channel_id=1, source_target_pairs={{0,8},{8,0},{16,24},{24,16},{1,9},{9,1},{17,25},{25,17},{2,10},{10... | collective-permute-start | bytes 393224 | tf_op jit(solution)/shard_map/exchange/ppermute | solution.py:214
  16.6 8.0 %collective-permute-start.5 = (bf16[528,128]{1,0:T(8,128)(2,1)S(1)}, bf16[528,128]{1,0:T(8,128)(2,1)S(1)}, u32[]{:S(2)}, u32[]{:S(2)}) collective-permute-start(bf16[528,128]{1,0:T(8,128)(2,1)S(1)} %get-tuple-element.39.q_ref), channel_id=1, source_target_pairs={{0,4},{1,5},{2,6},{3,7},{4,0},{5,1},{6,2},{7,3},{8,12},{9,13},{10,... | collective-permute-start | bytes 405512 | tf_op jit(solution)/shard_map/exchange/ppermute | solution.py:221
  20.4 6.3 %collective-permute-start.11 = (bf16[544,128]{1,0:T(8,128)(2,1)S(1)}, bf16[544,128]{1,0:T(8,128)(2,1)S(1)}, u32[]{:S(2)}, u32[]{:S(2)}) collective-permute-start(bf16[544,128]{1,0:T(8,128)(2,1)S(1)} %apply.4), channel_id=1, source_target_pairs={{0,2},{1,3},{2,0},{3,1},{4,6},{5,7},{6,4},{7,5},{8,10},{9,11},{10,... | collective-permute-start | bytes 417800 | tf_op jit(solution)/shard_map/return/ppermute | solution.py:286
  23.1 9.1 %collective-permute-start.15 = (bf16[272,128]{1,0:T(8,128)(2,1)S(1)}, bf16[272,128]{1,0:T(8,128)(2,1)S(1)}, u32[]{:S(2)}, u32[]{:S(2)}) collective-permute-start(bf16[272,128]{1,0:T(8,128)(2,1)S(1)} %get-tuple-element.34), channel_id=1, source_target_pairs={{0,2},{1,3},{2,0},{3,1},{4,6},{5,7},{6,4},{7,5},{8,10},{9,11},{10,... | collective-permute-start | bytes 208904 | tf_op jit(solution)/shard_map/return/ppermute | solution.py:284
  26.8 9.1 %collective-permute-start.13 = (bf16[272,128]{1,0:T(8,128)(2,1)S(1)}, bf16[272,128]{1,0:T(8,128)(2,1)S(1)}, u32[]{:S(2)}, u32[]{:S(2)}) collective-permute-start(bf16[272,128]{1,0:T(8,128)(2,1)S(1)} %get-tuple-element.38), channel_id=1, source_target_pairs={{0,4},{1,5},{2,6},{3,7},{4,0},{5,1},{6,2},{7,3},{8,12},{9,13},{10,... | collective-permute-start | bytes 208904 | tf_op jit(solution)/shard_map/return/ppermute | solution.py:284
  28.5 7.4 %collective-permute-start.14 = (bf16[272,128]{1,0:T(8,128)(2,1)S(1)}, bf16[272,128]{1,0:T(8,128)(2,1)S(1)}, u32[]{:S(2)}, u32[]{:S(2)}) collective-permute-start(bf16[272,128]{1,0:T(8,128)(2,1)S(1)} %get-tuple-element.44), channel_id=1, source_target_pairs={{0,5},{1,4},{2,7},{3,6},{4,1},{5,0},{6,3},{7,2},{8,13},{9,12},{10,... | collective-permute-start | bytes 208904 | tf_op jit(solution)/shard_map/return/ppermute | solution.py:284
  29.6 6.3 %collective-permute-start.16 = (bf16[272,128]{1,0:T(8,128)(2,1)S(1)}, bf16[272,128]{1,0:T(8,128)(2,1)S(1)}, u32[]{:S(2)}, u32[]{:S(2)}) collective-permute-start(bf16[272,128]{1,0:T(8,128)(2,1)S(1)} %get-tuple-element.46), channel_id=1, source_target_pairs={{0,3},{1,2},{2,1},{3,0},{4,7},{5,6},{6,5},{7,4},{8,11},{9,10},{10,... | collective-permute-start | bytes 208904 | tf_op jit(solution)/shard_map/return/ppermute | solution.py:284
  31.9 3.9 %collective-permute-start.12 = (bf16[272,128]{1,0:T(8,128)(2,1)S(1)}, bf16[272,128]{1,0:T(8,128)(2,1)S(1)}, u32[]{:S(2)}, u32[]{:S(2)}) collective-permute-start(bf16[272,128]{1,0:T(8,128)(2,1)S(1)} %get-tuple-element.43), channel_id=1, source_target_pairs={{0,1},{1,0},{2,3},{3,2},{4,5},{5,4},{6,7},{7,6},{8,9},{9,8},{10,11... | collective-permute-start | bytes 208904 | tf_op jit(solution)/shard_map/return/ppermute | solution.py:307

commit v26 on v25

--- a/solution.py
+++ b/solution.py
@@ -30,7 +30,7 @@
         for j in range(PER):
             piece = ref[:, pl.ds(pl.multiple_of((core * PER + j) * size, size), size)]
             if turned:
-                piece = piece.astype(F32).T.astype(BF16)
+                piece = piece.T
             row = at + j * CORES * tok + b * tok
             out[row : row + tok, :] = piece
 
@@ -162,7 +162,7 @@
         for h in range(PER):
             _, total, numer = joined([part[h * size : (h + 1) * size, :] for part in mine], stats, h, rate)
             cols = pl.ds(pl.multiple_of((pair * PER + h) * size, size), size)
-            out_ref[:, cols] = (numer * (1.0 / total)).T.astype(BF16)
+            out_ref[:, cols] = (numer * (1.0 / total)).astype(BF16).T
 
 
 def vmem(n=1):

time: 36.9 us -> 36.8 us (level)
  no operation moved by 1% of the time
where the time goes in v26:
time: 36.8 us; the launch traced here: 36.7 us
  starting transfers between devices  22.1 us (60%)
  waiting for transfers between devices  6.72 us (18%)
  Pallas kernels  6.03 us (16%)
  other arithmetic  1.06 us (3%)
  between operations  0.79 us (2%)
    ppermute x4, starting transfers between devices, over(): return lax.ppermute(a, 'outer', [(o, o ^ r) for o in range(n_out)])  7.91 us
    ppermute x3, starting transfers between devices, shards(): q_by[r] = lax.ppermute(piece, 'inner', along_inner(r, 0))  6.64 us
    ppermute x4, starting transfers between devices, send(): lax.ppermute(parts[x], 'inner', along_inner(r, x))  4.54 us
    ppermute x4, waiting for transfers between devices, send(): lax.ppermute(parts[x], 'inner', along_inner(r, x))  3.62 us
    pallas_call x4, Pallas kernels, score(): pl.pallas_call(functools.partial(score_kernel, r == 0), out_shape=(jax.Sh...  3.02 us
    ppermute x1, starting transfers between devices, send(): lax.ppermute(parts[0], 'inner', along_inner(low(r), 0))  1.64 us
    pallas_call x4, Pallas kernels, apply(): pl.pallas_call(functools.partial(apply_kernel, wide, rows), out_shape=sha...  1.35 us
    ppermute x4, waiting for transfers between devices, over(): return lax.ppermute(a, 'outer', [(o, o ^ r) for o in range(n_out)])  1.11 us
  transfers between devices with their start and end apart: 17, of which 5 were waited for; matrix products, arithmetic and copies ran while one was open for 3% of the time, Pallas kernels for 12%

profile of v26, /device:TPU:0, one launch (start us, length us, event | category | flops | bytes accessed | tf_op | source)
XLA Modules:
  0.0 36.7 jit_solution(6624001499264699915)
XLA Ops:
  0.0 0.5 %collective-permute-start.1 = (bf16[128,512]{1,0:T(8,128)(2,1)}, bf16[128,512]{1,0:T(8,128)(2,1)S(1)}, u32[]{:S(2)}, u32[]{:S(2)}) collective-permute-start(bf16[128,512]{1,0:T(8,128)(2,1)} %param.4), channel_id=1, source_target_pairs={{0,1},{1,0},{2,3},{3,2},{4,5},{5,4},{6,7},{7,6},{8,9},{9,8},{10,11... | collective-permute-start | bytes 393224 | tf_op jit(solution)/shard_map/swap/ppermute | solution.py:186
  0.5 0.1 collective-permute-start.2
  0.5 0.5 %collective-permute-start.3 = (bf16[128,512]{1,0:T(8,128)(2,1)}, bf16[128,512]{1,0:T(8,128)(2,1)S(1)}, u32[]{:S(2)}, u32[]{:S(2)}) collective-permute-start(bf16[128,512]{1,0:T(8,128)(2,1)} %param.6), channel_id=1, source_target_pairs={{0,1},{1,0},{2,3},{3,2},{4,5},{5,4},{6,7},{7,6},{8,9},{9,8},{10,11... | collective-permute-start | bytes 393224 | tf_op jit(solution)/shard_map/swap/ppermute | solution.py:186
  1.0 0.1 collective-permute-start
  1.7 1.1 %pad_maximum_fusion.own = bf16[384,512]{1,0:T(8,128)(2,1)S(1)} fusion(bf16[128,512]{1,0:T(8,128)(2,1)} %param.6, bf16[128,512]{1,0:T(8,128)(2,1)} %param.5, bf16[128,512]{1,0:T(8,128)(2,1)} %param.4), kind=kLoop, calls=%fused_computation | loop fusion | flops 1179648 | bytes 786432 | tf_op jit(solution)/shard_map/swap/concatenate | solution.py:187
  2.7 0.0 collective-permute-done.p1
  2.7 0.0 collective-permute-done.1.q1
  2.8 0.0 collective-permute-done.2.k1
  2.8 0.0 collective-permute-done.3.v1
  2.8 0.8 %merge.1 = (bf16[528,128]{1,0:T(8,128)(2,1)S(1)}, bf16[1040,128]{1,0:T(8,128)(2,1)S(1)}) custom-call(s32[1]{0:T(128)S(6)} %copy.5.p0, s32[1]{0:T(128)} %collective-permute-done.p1, bf16[384,512]{1,0:T(8,128)(2,1)S(1)} %pad_maximum_fusion.own, bf16[128,512]{1,0:T(8,128)(2,1)S(1)} %collective-permute-done.1.q1, ...), custom_call_target="tpu_custom_call" | custom-call | tf_op jit(solution)/shard_map/merge/merge/pallas_call | solution.py:190
  3.5 3.0 %collective-permute-start.7 = (bf16[1040,128]{1,0:T(8,128)(2,1)S(1)}, bf16[1040,128]{1,0:T(8,128)(2,1)S(1)}, u32[]{:S(2)}, u32[]{:S(2)}) collective-permute-start(bf16[1040,128]{1,0:T(8,128)(2,1)S(1)} %get-tuple-element.28.refs_0_), channel_id=1, source_target_pairs={{0,8},{8,0},{16,24},{24,16},{1,9},{9,1},{17,25},{25,17},{2,10},{10... | collective-permute-start | bytes 798728 | tf_op jit(solution)/shard_map/exchange/ppermute | solution.py:214
  6.6 1.5 %collective-permute-start.8 = (bf16[1040,128]{1,0:T(8,128)(2,1)S(1)}, bf16[1040,128]{1,0:T(8,128)(2,1)S(1)}, u32[]{:S(2)}, u32[]{:S(2)}) collective-permute-start(bf16[1040,128]{1,0:T(8,128)(2,1)S(1)} %get-tuple-element.28.refs_0_), channel_id=1, source_target_pairs={{0,16},{8,24},{16,0},{24,8},{1,17},{9,25},{17,1},{25,9},{2,18},{10... | collective-permute-start | bytes 798728 | tf_op jit(solution)/shard_map/exchange/ppermute | solution.py:214
  8.1 1.6 %collective-permute-start.4 = (bf16[528,128]{1,0:T(8,128)(2,1)S(1)}, bf16[528,128]{1,0:T(8,128)(2,1)S(1)}, u32[]{:S(2)}, u32[]{:S(2)}) collective-permute-start(bf16[528,128]{1,0:T(8,128)(2,1)S(1)} %get-tuple-element.39.q_ref), channel_id=1, source_target_pairs={{0,2},{1,3},{2,0},{3,1},{4,6},{5,7},{6,4},{7,5},{8,10},{9,11},{10,... | collective-permute-start | bytes 405512 | tf_op jit(solution)/shard_map/exchange/ppermute | solution.py:221
  9.6 2.5 %collective-permute-start.6 = (bf16[528,128]{1,0:T(8,128)(2,1)S(1)}, bf16[528,128]{1,0:T(8,128)(2,1)S(1)}, u32[]{:S(2)}, u32[]{:S(2)}) collective-permute-start(bf16[528,128]{1,0:T(8,128)(2,1)S(1)} %get-tuple-element.39.q_ref), channel_id=1, source_target_pairs={{0,6},{1,7},{2,4},{3,5},{4,2},{5,3},{6,0},{7,1},{8,14},{9,15},{10,... | collective-permute-start | bytes 405512 | tf_op jit(solution)/shard_map/exchange/ppermute | solution.py:221
  12.1 1.0 %collective-permute-done.7.refs_1_ = bf16[1040,128]{1,0:T(8,128)(2,1)S(1)} collective-permute-done((bf16[1040,128]{1,0:T(8,128)(2,1)S(1)}, bf16[1040,128]{1,0:T(8,128)(2,1)S(1)}, u32[]{:S(2)}, u32[]{:S(2)}) %collective-permute-start.7) | collective-permute-done | bytes 266272 | tf_op jit(solution)/shard_map/exchange/ppermute | solution.py:214
  13.1 1.8 %collective-permute-start.9 = (bf16[528,128]{1,0:T(8,128)(2,1)S(1)}, bf16[528,128]{1,0:T(8,128)(2,1)S(1)}, u32[]{:S(2)}, u32[]{:S(2)}) collective-permute-start(bf16[528,128]{1,0:T(8,128)(2,1)S(1)} %slice.8), channel_id=1, source_target_pairs={{0,16},{8,24},{16,0},{24,8},{1,17},{9,25},{17,1},{25,9},{2,18},{10... | collective-permute-start | bytes 405512 | tf_op jit(solution)/shard_map/exchange/ppermute | solution.py:214
  15.0 0.0 collective-permute-done.8.refs_2_
  15.0 1.6 %collective-permute-start.10 = (bf16[512,128]{1,0:T(8,128)(2,1)S(1)}, bf16[512,128]{1,0:T(8,128)(2,1)S(1)}, u32[]{:S(2)}, u32[]{:S(2)}) collective-permute-start(bf16[512,128]{1,0:T(8,128)(2,1)S(1)} %slice.9), channel_id=1, source_target_pairs={{0,8},{8,0},{16,24},{24,16},{1,9},{9,1},{17,25},{25,17},{2,10},{10... | collective-permute-start | bytes 393224 | tf_op jit(solution)/shard_map/exchange/ppermute | solution.py:214
  16.5 0.0 collective-permute-done.4.q_ref
  16.5 2.6 %collective-permute-start.5 = (bf16[528,128]{1,0:T(8,128)(2,1)S(1)}, bf16[528,128]{1,0:T(8,128)(2,1)S(1)}, u32[]{:S(2)}, u32[]{:S(2)}) collective-permute-start(bf16[528,128]{1,0:T(8,128)(2,1)S(1)} %get-tuple-element.39.q_ref), channel_id=1, source_target_pairs={{0,4},{1,5},{2,6},{3,7},{4,0},{5,1},{6,2},{7,3},{8,12},{9,13},{10,... | collective-permute-start | bytes 405512 | tf_op jit(solution)/shard_map/exchange/ppermute | solution.py:221
  19.1 0.0 collective-permute-done.6.q_ref
  19.1 0.0 collective-permute-done.9.refs_3_
  19.1 0.8 %score.4 = (bf16[2,1024,256]{2,1,0:T(8,128)(2,1)S(1)}, f32[16,256]{1,0:T(8,128)S(1)}) custom-call(bf16[528,128]{1,0:T(8,128)(2,1)S(1)} %collective-permute-done.6.q_ref, bf16[1040,128]{1,0:T(8,128)(2,1)S(1)} %get-tuple-element.28.refs_0_, bf16[1040,128]{1,0:T(8,128)(2,1)S(1)} %collective-permute-done.7.refs_1_, ...), custom_call_target="tpu_custom_call" | custom-call | flops 134217728 | bytes 1048576 | tf_op jit(solution)/shard_map/score/score/pallas_call | solution.py:242
  19.9 0.1 collective-permute-done.10.refs_3_
  20.0 0.3 apply.4
  20.4 1.6 %collective-permute-start.11 = (bf16[544,128]{1,0:T(8,128)(2,1)S(1)}, bf16[544,128]{1,0:T(8,128)(2,1)S(1)}, u32[]{:S(2)}, u32[]{:S(2)}) collective-permute-start(bf16[544,128]{1,0:T(8,128)(2,1)S(1)} %apply.4), channel_id=1, source_target_pairs={{0,2},{1,3},{2,0},{3,1},{4,6},{5,7},{6,4},{7,5},{8,10},{9,11},{10,... | collective-permute-start | bytes 417800 | tf_op jit(solution)/shard_map/return/ppermute | solution.py:286
  22.0 0.8 %score.5 = (bf16[2,1024,256]{2,1,0:T(8,128)(2,1)S(1)}, f32[16,256]{1,0:T(8,128)S(1)}) custom-call(bf16[528,128]{1,0:T(8,128)(2,1)S(1)} %collective-permute-done.4.q_ref, bf16[1040,128]{1,0:T(8,128)(2,1)S(1)} %get-tuple-element.28.refs_0_, bf16[1040,128]{1,0:T(8,128)(2,1)S(1)} %collective-permute-done.7.refs_1_, ...), custom_call_target="tpu_custom_call" | custom-call | flops 134217728 | bytes 1048576 | tf_op jit(solution)/shard_map/score/score/pallas_call | solution.py:242
  22.8 0.3 apply.5
  23.1 0.5 %collective-permute-start.15 = (bf16[272,128]{1,0:T(8,128)(2,1)S(1)}, bf16[272,128]{1,0:T(8,128)(2,1)S(1)}, u32[]{:S(2)}, u32[]{:S(2)}) collective-permute-start(bf16[272,128]{1,0:T(8,128)(2,1)S(1)} %get-tuple-element.34), channel_id=1, source_target_pairs={{0,2},{1,3},{2,0},{3,1},{4,6},{5,7},{6,4},{7,5},{8,10},{9,11},{10,... | collective-permute-start | bytes 208904 | tf_op jit(solution)/shard_map/return/ppermute | solution.py:284
  23.6 0.9 %collective-permute-done.5.q_ref = bf16[528,128]{1,0:T(8,128)(2,1)S(1)} collective-permute-done((bf16[528,128]{1,0:T(8,128)(2,1)S(1)}, bf16[528,128]{1,0:T(8,128)(2,1)S(1)}, u32[]{:S(2)}, u32[]{:S(2)}) %collective-permute-start.5) | collective-permute-done | bytes 135200 | tf_op jit(solution)/shard_map/exchange/ppermute | solution.py:221
  24.5 0.8 %score.6 = (bf16[2,1024,256]{2,1,0:T(8,128)(2,1)S(1)}, f32[16,256]{1,0:T(8,128)S(1)}) custom-call(bf16[528,128]{1,0:T(8,128)(2,1)S(1)} %collective-permute-done.5.q_ref, bf16[1040,128]{1,0:T(8,128)(2,1)S(1)} %get-tuple-element.28.refs_0_, bf16[1040,128]{1,0:T(8,128)(2,1)S(1)} %collective-permute-done.7.refs_1_, ...), custom_call_target="tpu_custom_call" | custom-call | flops 134217728 | bytes 1048576 | tf_op jit(solution)/shard_map/score/score/pallas_call | solution.py:242
  25.3 0.3 apply.6.refs_0_
  25.6 1.1 %collective-permute-done.11.refs_1_ = bf16[544,128]{1,0:T(8,128)(2,1)S(1)} collective-permute-done((bf16[544,128]{1,0:T(8,128)(2,1)S(1)}, bf16[544,128]{1,0:T(8,128)(2,1)S(1)}, u32[]{:S(2)}, u32[]{:S(2)}) %collective-permute-start.11) | collective-permute-done | bytes 139296 | tf_op jit(solution)/shard_map/return/ppermute | solution.py:286
  26.7 0.1 add.1
  26.8 1.7 %collective-permute-start.13 = (bf16[272,128]{1,0:T(8,128)(2,1)S(1)}, bf16[272,128]{1,0:T(8,128)(2,1)S(1)}, u32[]{:S(2)}, u32[]{:S(2)}) collective-permute-start(bf16[272,128]{1,0:T(8,128)(2,1)S(1)} %get-tuple-element.38), channel_id=1, source_target_pairs={{0,4},{1,5},{2,6},{3,7},{4,0},{5,1},{6,2},{7,3},{8,12},{9,13},{10,... | collective-permute-start | bytes 208904 | tf_op jit(solution)/shard_map/return/ppermute | solution.py:284
  28.5 0.0 collective-permute-start.14
  28.5 0.8 %score.7 = (bf16[2,1024,256]{2,1,0:T(8,128)(2,1)S(1)}, f32[16,256]{1,0:T(8,128)S(1)}) custom-call(bf16[528,128]{1,0:T(8,128)(2,1)S(1)} %get-tuple-element.39.q_ref, bf16[1040,128]{1,0:T(8,128)(2,1)S(1)} %get-tuple-element.28.refs_0_, bf16[1040,128]{1,0:T(8,128)(2,1)S(1)} %collective-permute-done.7.refs_1_, ...), custom_call_target="tpu_custom_call" | custom-call | flops 134217728 | bytes 1048576 | tf_op jit(solution)/shard_map/score/score/pallas_call | solution.py:242
  29.2 0.3 apply.7
  29.6 2.3 %collective-permute-start.16 = (bf16[272,128]{1,0:T(8,128)(2,1)S(1)}, bf16[272,128]{1,0:T(8,128)(2,1)S(1)}, u32[]{:S(2)}, u32[]{:S(2)}) collective-permute-start(bf16[272,128]{1,0:T(8,128)(2,1)S(1)} %get-tuple-element.46), channel_id=1, source_target_pairs={{0,3},{1,2},{2,1},{3,0},{4,7},{5,6},{6,5},{7,4},{8,11},{9,10},{10,... | collective-permute-start | bytes 208904 | tf_op jit(solution)/shard_map/return/ppermute | solution.py:284
  31.9 0.3 collective-permute-start.12
  32.2 0.0 collective-permute-done.15.refs_4_
  32.2 3.6 %collective-permute-done.14.refs_3_ = bf16[272,128]{1,0:T(8,128)(2,1)S(1)} collective-permute-done((bf16[272,128]{1,0:T(8,128)(2,1)S(1)}, bf16[272,128]{1,0:T(8,128)(2,1)S(1)}, u32[]{:S(2)}, u32[]{:S(2)}) %collective-permute-start.14) | collective-permute-done | bytes 69664 | tf_op jit(solution)/shard_map/return/ppermute | solution.py:284
  35.9 0.0 collective-permute-done.13.refs_2_
  35.9 0.0 collective-permute-done.16.refs_5_
  35.9 0.0 collective-permute-done.12.refs_1_
  35.9 0.8 %combine.1 = bf16[128,512]{1,0:T(8,128)(2,1)} custom-call(bf16[272,128]{1,0:T(8,128)(2,1)S(1)} %get-tuple-element.42.refs_0_, bf16[272,128]{1,0:T(8,128)(2,1)S(1)} %collective-permute-done.12.refs_1_, bf16[272,128]{1,0:T(8,128)(2,1)S(1)} %collective-permute-done.13.refs_2_, bf16[272,128]{1,0:T(8,128)(2,1)S(1)} %collective-permute-done.14.refs_3_, ...), custom_call_target="tpu_custom_call" | custom-call | tf_op jit(solution)/shard_map/combine/combine/pallas_call | solution.py:309
  (2 shorter events, 0.0 us)
Async XLA Ops:
  0.0 2.7 %collective-permute-start.1 = (bf16[128,512]{1,0:T(8,128)(2,1)}, bf16[128,512]{1,0:T(8,128)(2,1)S(1)}, u32[]{:S(2)}, u32[]{:S(2)}) collective-permute-start(bf16[128,512]{1,0:T(8,128)(2,1)} %param.4), channel_id=1, source_target_pairs={{0,1},{1,0},{2,3},{3,2},{4,5},{5,4},{6,7},{7,6},{8,9},{9,8},{10,11... | collective-permute-start | bytes 393224 | tf_op jit(solution)/shard_map/swap/ppermute | solution.py:186
  0.5 2.3 %collective-permute-start.2 = (bf16[128,512]{1,0:T(8,128)(2,1)}, bf16[128,512]{1,0:T(8,128)(2,1)S(1)}, u32[]{:S(2)}, u32[]{:S(2)}) collective-permute-start(bf16[128,512]{1,0:T(8,128)(2,1)} %param.5), channel_id=1, source_target_pairs={{0,1},{1,0},{2,3},{3,2},{4,5},{5,4},{6,7},{7,6},{8,9},{9,8},{10,11... | collective-permute-start | bytes 393224 | tf_op jit(solution)/shard_map/swap/ppermute | solution.py:186
  0.5 2.3 %collective-permute-start.3 = (bf16[128,512]{1,0:T(8,128)(2,1)}, bf16[128,512]{1,0:T(8,128)(2,1)S(1)}, u32[]{:S(2)}, u32[]{:S(2)}) collective-permute-start(bf16[128,512]{1,0:T(8,128)(2,1)} %param.6), channel_id=1, source_target_pairs={{0,1},{1,0},{2,3},{3,2},{4,5},{5,4},{6,7},{7,6},{8,9},{9,8},{10,11... | collective-permute-start | bytes 393224 | tf_op jit(solution)/shard_map/swap/ppermute | solution.py:186
  1.0 1.8 %collective-permute-start = (s32[1]{0:T(128)}, s32[1]{0:T(128)}, u32[]{:S(2)}, u32[]{:S(2)}) collective-permute-start(s32[1]{0:T(128)} %param.7), channel_id=1, source_target_pairs={{0,1},{1,0},{2,3},{3,2},{4,5},{5,4},{6,7},{7,6},{8,9},{9,8},{10,11... | collective-permute-start | bytes 20 | tf_op jit(solution)/shard_map/swap/ppermute | solution.py:186
  3.5 9.6 %collective-permute-start.7 = (bf16[1040,128]{1,0:T(8,128)(2,1)S(1)}, bf16[1040,128]{1,0:T(8,128)(2,1)S(1)}, u32[]{:S(2)}, u32[]{:S(2)}) collective-permute-start(bf16[1040,128]{1,0:T(8,128)(2,1)S(1)} %get-tuple-element.28.refs_0_), channel_id=1, source_target_pairs={{0,8},{8,0},{16,24},{24,16},{1,9},{9,1},{17,25},{25,17},{2,10},{10... | collective-permute-start | bytes 798728 | tf_op jit(solution)/shard_map/exchange/ppermute | solution.py:214
  6.6 8.4 %collective-permute-start.8 = (bf16[1040,128]{1,0:T(8,128)(2,1)S(1)}, bf16[1040,128]{1,0:T(8,128)(2,1)S(1)}, u32[]{:S(2)}, u32[]{:S(2)}) collective-permute-start(bf16[1040,128]{1,0:T(8,128)(2,1)S(1)} %get-tuple-element.28.refs_0_), channel_id=1, source_target_pairs={{0,16},{8,24},{16,0},{24,8},{1,17},{9,25},{17,1},{25,9},{2,18},{10... | collective-permute-start | bytes 798728 | tf_op jit(solution)/shard_map/exchange/ppermute | solution.py:214
  8.1 8.5 %collective-permute-start.4 = (bf16[528,128]{1,0:T(8,128)(2,1)S(1)}, bf16[528,128]{1,0:T(8,128)(2,1)S(1)}, u32[]{:S(2)}, u32[]{:S(2)}) collective-permute-start(bf16[528,128]{1,0:T(8,128)(2,1)S(1)} %get-tuple-element.39.q_ref), channel_id=1, source_target_pairs={{0,2},{1,3},{2,0},{3,1},{4,6},{5,7},{6,4},{7,5},{8,10},{9,11},{10,... | collective-permute-start | bytes 405512 | tf_op jit(solution)/shard_map/exchange/ppermute | solution.py:221
  9.6 9.5 %collective-permute-start.6 = (bf16[528,128]{1,0:T(8,128)(2,1)S(1)}, bf16[528,128]{1,0:T(8,128)(2,1)S(1)}, u32[]{:S(2)}, u32[]{:S(2)}) collective-permute-start(bf16[528,128]{1,0:T(8,128)(2,1)S(1)} %get-tuple-element.39.q_ref), channel_id=1, source_target_pairs={{0,6},{1,7},{2,4},{3,5},{4,2},{5,3},{6,0},{7,1},{8,14},{9,15},{10,... | collective-permute-start | bytes 405512 | tf_op jit(solution)/shard_map/exchange/ppermute | solution.py:221
  13.1 6.0 %collective-permute-start.9 = (bf16[528,128]{1,0:T(8,128)(2,1)S(1)}, bf16[528,128]{1,0:T(8,128)(2,1)S(1)}, u32[]{:S(2)}, u32[]{:S(2)}) collective-permute-start(bf16[528,128]{1,0:T(8,128)(2,1)S(1)} %slice.8), channel_id=1, source_target_pairs={{0,16},{8,24},{16,0},{24,8},{1,17},{9,25},{17,1},{25,9},{2,18},{10... | collective-permute-start | bytes 405512 | tf_op jit(solution)/shard_map/exchange/ppermute | solution.py:214
  15.0 5.0 %collective-permute-start.10 = (bf16[512,128]{1,0:T(8,128)(2,1)S(1)}, bf16[512,128]{1,0:T(8,128)(2,1)S(1)}, u32[]{:S(2)}, u32[]{:S(2)}) collective-permute-start(bf16[512,128]{1,0:T(8,128)(2,1)S(1)} %slice.9), channel_id=1, source_target_pairs={{0,8},{8,0},{16,24},{24,16},{1,9},{9,1},{17,25},{25,17},{2,10},{10... | collective-permute-start | bytes 393224 | tf_op jit(solution)/shard_map/exchange/ppermute | solution.py:214
  16.5 8.0 %collective-permute-start.5 = (bf16[528,128]{1,0:T(8,128)(2,1)S(1)}, bf16[528,128]{1,0:T(8,128)(2,1)S(1)}, u32[]{:S(2)}, u32[]{:S(2)}) collective-permute-start(bf16[528,128]{1,0:T(8,128)(2,1)S(1)} %get-tuple-element.39.q_ref), channel_id=1, source_target_pairs={{0,4},{1,5},{2,6},{3,7},{4,0},{5,1},{6,2},{7,3},{8,12},{9,13},{10,... | collective-permute-start | bytes 405512 | tf_op jit(solution)/shard_map/exchange/ppermute | solution.py:221
  20.4 6.3 %collective-permute-start.11 = (bf16[544,128]{1,0:T(8,128)(2,1)S(1)}, bf16[544,128]{1,0:T(8,128)(2,1)S(1)}, u32[]{:S(2)}, u32[]{:S(2)}) collective-permute-start(bf16[544,128]{1,0:T(8,128)(2,1)S(1)} %apply.4), channel_id=1, source_target_pairs={{0,2},{1,3},{2,0},{3,1},{4,6},{5,7},{6,4},{7,5},{8,10},{9,11},{10,... | collective-permute-start | bytes 417800 | tf_op jit(solution)/shard_map/return/ppermute | solution.py:286
  23.1 9.1 %collective-permute-start.15 = (bf16[272,128]{1,0:T(8,128)(2,1)S(1)}, bf16[272,128]{1,0:T(8,128)(2,1)S(1)}, u32[]{:S(2)}, u32[]{:S(2)}) collective-permute-start(bf16[272,128]{1,0:T(8,128)(2,1)S(1)} %get-tuple-element.34), channel_id=1, source_target_pairs={{0,2},{1,3},{2,0},{3,1},{4,6},{5,7},{6,4},{7,5},{8,10},{9,11},{10,... | collective-permute-start | bytes 208904 | tf_op jit(solution)/shard_map/return/ppermute | solution.py:284
  26.8 9.1 %collective-permute-start.13 = (bf16[272,128]{1,0:T(8,128)(2,1)S(1)}, bf16[272,128]{1,0:T(8,128)(2,1)S(1)}, u32[]{:S(2)}, u32[]{:S(2)}) collective-permute-start(bf16[272,128]{1,0:T(8,128)(2,1)S(1)} %get-tuple-element.38), channel_id=1, source_target_pairs={{0,4},{1,5},{2,6},{3,7},{4,0},{5,1},{6,2},{7,3},{8,12},{9,13},{10,... | collective-permute-start | bytes 208904 | tf_op jit(solution)/shard_map/return/ppermute | solution.py:284
  28.5 7.4 %collective-permute-start.14 = (bf16[272,128]{1,0:T(8,128)(2,1)S(1)}, bf16[272,128]{1,0:T(8,128)(2,1)S(1)}, u32[]{:S(2)}, u32[]{:S(2)}) collective-permute-start(bf16[272,128]{1,0:T(8,128)(2,1)S(1)} %get-tuple-element.44), channel_id=1, source_target_pairs={{0,5},{1,4},{2,7},{3,6},{4,1},{5,0},{6,3},{7,2},{8,13},{9,12},{10,... | collective-permute-start | bytes 208904 | tf_op jit(solution)/shard_map/return/ppermute | solution.py:284
  29.6 6.3 %collective-permute-start.16 = (bf16[272,128]{1,0:T(8,128)(2,1)S(1)}, bf16[272,128]{1,0:T(8,128)(2,1)S(1)}, u32[]{:S(2)}, u32[]{:S(2)}) collective-permute-start(bf16[272,128]{1,0:T(8,128)(2,1)S(1)} %get-tuple-element.46), channel_id=1, source_target_pairs={{0,3},{1,2},{2,1},{3,0},{4,7},{5,6},{6,5},{7,4},{8,11},{9,10},{10,... | collective-permute-start | bytes 208904 | tf_op jit(solution)/shard_map/return/ppermute | solution.py:284
  31.9 3.9 %collective-permute-start.12 = (bf16[272,128]{1,0:T(8,128)(2,1)S(1)}, bf16[272,128]{1,0:T(8,128)(2,1)S(1)}, u32[]{:S(2)}, u32[]{:S(2)}) collective-permute-start(bf16[272,128]{1,0:T(8,128)(2,1)S(1)} %get-tuple-element.43), channel_id=1, source_target_pairs={{0,1},{1,0},{2,3},{3,2},{4,5},{5,4},{6,7},{7,6},{8,9},{9,8},{10,11... | collective-permute-start | bytes 208904 | tf_op jit(solution)/shard_map/return/ppermute | solution.py:307

commit v27 on v26

--- a/solution.py
+++ b/solution.py
@@ -49,6 +49,20 @@
     place(own.at[tok : 2 * tok, :], k1, kv_out, 0)
     kv_out[rows : rows + PAD, :] = pos
     place(own.at[2 * tok : 3 * tok, :], v1, kv_out, rows + PAD, turned=True)
+
+
+def pick_kernel(k0, v0, k1, v1, k_out, v_out):
+    core = lax.rem(lax.axis_index("inner"), CORES)
+
+    @pl.when(core == 0)
+    def _():
+        k_out[...] = k0[...]
+        v_out[...] = v0[...]
+
+    @pl.when(core != 0)
+    def _():
+        k_out[...] = k1[...]
+        v_out[...] = v1[...]
 
 
 def score_kernel(same, q_ref, *refs):
@@ -210,23 +224,39 @@
     def single(r):
         return r == low(r)
 
-    def over(a, r):
-        return lax.ppermute(a, "outer", [(o, o ^ r) for o in range(n_out)])
+    def over(a, flips):
+        pairs = [
+            (o * n_in + w * CORES + c, (o ^ flips[c]) * n_in + w * CORES + c)
+            for o in range(n_out)
+            for w in range(chips)
+            for c in range(CORES)
+        ]
+        return lax.ppermute(a, ("outer", "inner"), pairs)
+
+    def pick(first, second):
+        return pl.pallas_call(
+            pick_kernel,
+            out_shape=tuple(jax.ShapeDtypeStruct(a.shape, BF16) for a in first),
+            in_specs=vmem(4),
+            out_specs=tuple(vmem(2)),
+            compiler_params=params,
+            name="pick",
+        )(*first, *second)
 
     with jax.named_scope("exchange"):
-        whole = {r: over(kv_piece, r) if r else kv_piece for r in range(n_out) if single(r)}
+        whole = {r: over(kv_piece, (r, r)) if r else kv_piece for r in range(n_out) if single(r)}
         q_by = {0: q_piece}
         for r in sorted(range(1, chips), key=lambda r: (r != chips - 1, r)):
             piece = q_piece if r in (1, chips - 1) else after(q_piece, q_by[1])
             q_by[r] = lax.ppermute(piece, "inner", along_inner(r, 0))
         k_by = {r: a[:half, :] for r, a in whole.items() if r}
         v_by = {r: a[half:, :] for r, a in whole.items() if r}
-        for r in range(1, n_out):
-            if not single(r):
-                k_by[r] = over(k_by[r - high(r)], high(r))
         for r in sorted(range(1, n_out), key=lambda r: r.bit_count()):
             if not single(r):
-                v_by[r] = over(v_by[r - low(r)], low(r))
+                one, two = r - high(r), r - low(r)
+                k, v = pick((k_by[one], v_by[one]), (k_by[two], v_by[two]))
+                k_by[r] = over(k, (high(r), low(r)))
+                v_by[r] = over(after(v, q_by[1]) if chips > 1 else v, (high(r), low(r)))
         ks = [whole[r] if r in whole else k_by[r] for r in range(n_out)]
         vs = [whole[r] if r in whole else v_by[r] for r in range(n_out)]
         rows = tuple(half if r in whole else 0 for r in range(n_out))

time: 36.8 us -> 37.1 us (level)
  waiting for transfers between devices: 6.72 us -> 7.51 us
  starting transfers between devices: 22.1 us -> 21.4 us
    ppermute x4, waiting for transfers between devices: 1.11 us -> 3.48 us  [over(): return lax.ppermute(a, ('outer', 'inner'), pairs)]
    ppermute x4, starting transfers between devices: 7.91 us -> 6.61 us  [over(): return lax.ppermute(a, ('outer', 'inner'), pairs)]
    ppermute x3, waiting for transfers between devices: 0.9 us -> 0.01 us  [shards(): q_by[r] = lax.ppermute(piece, 'inner', along_inner(r, 0))]
    ppermute x4, starting transfers between devices: 4.54 us -> 5.16 us  [send(): lax.ppermute(parts[x], 'inner', along_inner(r, x))]
    ppermute x4, waiting for transfers between devices: 3.62 us -> 3.04 us  [send(): lax.ppermute(parts[x], 'inner', along_inner(r, x))]
  transfers between devices with their start and end apart: 17 -> 17, of which waited for: 5 -> 6; matrix products, arithmetic and copies ran while one was open for 3% -> 3% of each run, Pallas kernels for 12% -> 12%
where the time goes in v27:
time: 37.1 us; the launch traced here: 36.9 us
  starting transfers between devices  21.4 us (58%)
  waiting for transfers between devices  7.51 us (20%)
  Pallas kernels  6.12 us (16%)
  other arithmetic  1.06 us (3%)
  between operations  0.81 us (2%)
    ppermute x3, starting transfers between devices, shards(): q_by[r] = lax.ppermute(piece, 'inner', along_inner(r, 0))  6.64 us
    ppermute x4, starting transfers between devices, over(): return lax.ppermute(a, ('outer', 'inner'), pairs)  6.61 us
    ppermute x4, starting transfers between devices, send(): lax.ppermute(parts[x], 'inner', along_inner(r, x))  5.16 us
    ppermute x4, waiting for transfers between devices, over(): return lax.ppermute(a, ('outer', 'inner'), pairs)  3.48 us
    ppermute x4, waiting for transfers between devices, send(): lax.ppermute(parts[x], 'inner', along_inner(r, x))  3.04 us
    pallas_call x4, Pallas kernels, score(): pl.pallas_call(functools.partial(score_kernel, r == 0), out_shape=(jax.Sh...  3.01 us
    ppermute x1, starting transfers between devices, send(): lax.ppermute(parts[0], 'inner', along_inner(low(r), 0))  1.64 us
    pallas_call x4, Pallas kernels, apply(): pl.pallas_call(functools.partial(apply_kernel, wide, rows), out_shape=sha...  1.34 us
  transfers between devices with their start and end apart: 17, of which 6 were waited for; matrix products, arithmetic and copies ran while one was open for 3% of the time, Pallas kernels for 12%

profile of v27, /device:TPU:0, one launch (start us, length us, event | category | flops | bytes accessed | tf_op | source)
XLA Modules:
  0.0 36.9 jit_solution(3928439849245552513)
XLA Ops:
  0.0 0.5 %collective-permute-start.1 = (bf16[128,512]{1,0:T(8,128)(2,1)}, bf16[128,512]{1,0:T(8,128)(2,1)S(1)}, u32[]{:S(2)}, u32[]{:S(2)}) collective-permute-start(bf16[128,512]{1,0:T(8,128)(2,1)} %param.4), channel_id=1, source_target_pairs={{0,1},{1,0},{2,3},{3,2},{4,5},{5,4},{6,7},{7,6},{8,9},{9,8},{10,11... | collective-permute-start | bytes 393224 | tf_op jit(solution)/shard_map/swap/ppermute | solution.py:200
  0.5 0.1 collective-permute-start.2
  0.5 0.5 %collective-permute-start.3 = (bf16[128,512]{1,0:T(8,128)(2,1)}, bf16[128,512]{1,0:T(8,128)(2,1)S(1)}, u32[]{:S(2)}, u32[]{:S(2)}) collective-permute-start(bf16[128,512]{1,0:T(8,128)(2,1)} %param.6), channel_id=1, source_target_pairs={{0,1},{1,0},{2,3},{3,2},{4,5},{5,4},{6,7},{7,6},{8,9},{9,8},{10,11... | collective-permute-start | bytes 393224 | tf_op jit(solution)/shard_map/swap/ppermute | solution.py:200
  1.0 0.1 collective-permute-start
  1.7 1.1 %pad_maximum_fusion.own = bf16[384,512]{1,0:T(8,128)(2,1)S(1)} fusion(bf16[128,512]{1,0:T(8,128)(2,1)} %param.6, bf16[128,512]{1,0:T(8,128)(2,1)} %param.5, bf16[128,512]{1,0:T(8,128)(2,1)} %param.4), kind=kLoop, calls=%fused_computation | loop fusion | flops 1179648 | bytes 786432 | tf_op jit(solution)/shard_map/swap/concatenate | solution.py:201
  2.7 0.0 collective-permute-done.p1
  2.7 0.0 collective-permute-done.1.q1
  2.8 0.0 collective-permute-done.2.k1
  2.8 0.0 collective-permute-done.3.v1
  2.8 0.8 %merge.1 = (bf16[528,128]{1,0:T(8,128)(2,1)S(1)}, bf16[1040,128]{1,0:T(8,128)(2,1)S(1)}) custom-call(s32[1]{0:T(128)S(6)} %copy.5.p0, s32[1]{0:T(128)} %collective-permute-done.p1, bf16[384,512]{1,0:T(8,128)(2,1)S(1)} %pad_maximum_fusion.own, bf16[128,512]{1,0:T(8,128)(2,1)S(1)} %collective-permute-done.1.q1, ...), custom_call_target="tpu_custom_call" | custom-call | tf_op jit(solution)/shard_map/merge/merge/pallas_call | solution.py:204
  3.6 3.0 %collective-permute-start.8 = (bf16[1040,128]{1,0:T(8,128)(2,1)S(1)}, bf16[1040,128]{1,0:T(8,128)(2,1)S(1)}, u32[]{:S(2)}, u32[]{:S(2)}) collective-permute-start(bf16[1040,128]{1,0:T(8,128)(2,1)S(1)} %get-tuple-element.31.refs_0_), channel_id=1, source_target_pairs={{0,16},{1,17},{2,18},{3,19},{4,20},{5,21},{6,22},{7,23},{8,24},{9,... | collective-permute-start | bytes 798728 | tf_op jit(solution)/shard_map/exchange/ppermute | solution.py:234
  6.6 1.5 %collective-permute-start.7 = (bf16[1040,128]{1,0:T(8,128)(2,1)S(1)}, bf16[1040,128]{1,0:T(8,128)(2,1)S(1)}, u32[]{:S(2)}, u32[]{:S(2)}) collective-permute-start(bf16[1040,128]{1,0:T(8,128)(2,1)S(1)} %get-tuple-element.31.refs_0_), channel_id=1, source_target_pairs={{0,8},{1,9},{2,10},{3,11},{4,12},{5,13},{6,14},{7,15},{8,0},{9,1},... | collective-permute-start | bytes 798728 | tf_op jit(solution)/shard_map/exchange/ppermute | solution.py:234
  8.1 1.6 %collective-permute-start.4 = (bf16[528,128]{1,0:T(8,128)(2,1)S(1)}, bf16[528,128]{1,0:T(8,128)(2,1)S(1)}, u32[]{:S(2)}, u32[]{:S(2)}) collective-permute-start(bf16[528,128]{1,0:T(8,128)(2,1)S(1)} %get-tuple-element.45.q_ref), channel_id=1, source_target_pairs={{0,2},{1,3},{2,0},{3,1},{4,6},{5,7},{6,4},{7,5},{8,10},{9,11},{10,... | collective-permute-start | bytes 405512 | tf_op jit(solution)/shard_map/exchange/ppermute | solution.py:251
  9.7 2.5 %collective-permute-start.6 = (bf16[528,128]{1,0:T(8,128)(2,1)S(1)}, bf16[528,128]{1,0:T(8,128)(2,1)S(1)}, u32[]{:S(2)}, u32[]{:S(2)}) collective-permute-start(bf16[528,128]{1,0:T(8,128)(2,1)S(1)} %get-tuple-element.45.q_ref), channel_id=1, source_target_pairs={{0,6},{1,7},{2,4},{3,5},{4,2},{5,3},{6,0},{7,1},{8,14},{9,15},{10,... | collective-permute-start | bytes 405512 | tf_op jit(solution)/shard_map/exchange/ppermute | solution.py:251
  12.2 1.0 %collective-permute-done.8.refs_2_ = bf16[1040,128]{1,0:T(8,128)(2,1)S(1)} collective-permute-done((bf16[1040,128]{1,0:T(8,128)(2,1)S(1)}, bf16[1040,128]{1,0:T(8,128)(2,1)S(1)}, u32[]{:S(2)}, u32[]{:S(2)}) %collective-permute-start.8) | collective-permute-done | bytes 266272 | tf_op jit(solution)/shard_map/exchange/ppermute | solution.py:234
  13.2 1.4 %collective-permute-done.7.refs_1_ = bf16[1040,128]{1,0:T(8,128)(2,1)S(1)} collective-permute-done((bf16[1040,128]{1,0:T(8,128)(2,1)S(1)}, bf16[1040,128]{1,0:T(8,128)(2,1)S(1)}, u32[]{:S(2)}, u32[]{:S(2)}) %collective-permute-start.7) | collective-permute-done | bytes 266272 | tf_op jit(solution)/shard_map/exchange/ppermute | solution.py:234
  14.7 0.4 %collective-permute-start.9 = (bf16[528,128]{1,0:T(8,128)(2,1)S(1)}, bf16[528,128]{1,0:T(8,128)(2,1)S(1)}, u32[]{:S(2)}, u32[]{:S(2)}) collective-permute-start(bf16[528,128]{1,0:T(8,128)(2,1)S(1)} %get-tuple-element.32), channel_id=1, source_target_pairs={{0,16},{1,9},{2,18},{3,11},{4,20},{5,13},{6,22},{7,15},{8,24},{9,1... | collective-permute-start | bytes 405512 | tf_op jit(solution)/shard_map/exchange/ppermute | solution.py:234
  15.2 0.0 collective-permute-done.4.q_ref
  15.2 1.7 %collective-permute-start.10 = (bf16[512,128]{1,0:T(8,128)(2,1)S(1)}, bf16[512,128]{1,0:T(8,128)(2,1)S(1)}, u32[]{:S(2)}, u32[]{:S(2)}) collective-permute-start(bf16[512,128]{1,0:T(8,128)(2,1)S(1)} %get-tuple-element.36), channel_id=1, source_target_pairs={{0,16},{1,9},{2,18},{3,11},{4,20},{5,13},{6,22},{7,15},{8,24},{9,1... | collective-permute-start | bytes 393224 | tf_op jit(solution)/shard_map/exchange/ppermute | solution.py:234
  16.8 2.6 %collective-permute-start.5 = (bf16[528,128]{1,0:T(8,128)(2,1)S(1)}, bf16[528,128]{1,0:T(8,128)(2,1)S(1)}, u32[]{:S(2)}, u32[]{:S(2)}) collective-permute-start(bf16[528,128]{1,0:T(8,128)(2,1)S(1)} %get-tuple-element.45.q_ref), channel_id=1, source_target_pairs={{0,4},{1,5},{2,6},{3,7},{4,0},{5,1},{6,2},{7,3},{8,12},{9,13},{10,... | collective-permute-start | bytes 405512 | tf_op jit(solution)/shard_map/exchange/ppermute | solution.py:251
  19.4 0.0 collective-permute-done.6.q_ref
  19.4 0.4 %collective-permute-done.9.refs_3_ = bf16[528,128]{1,0:T(8,128)(2,1)S(1)} collective-permute-done((bf16[528,128]{1,0:T(8,128)(2,1)S(1)}, bf16[528,128]{1,0:T(8,128)(2,1)S(1)}, u32[]{:S(2)}, u32[]{:S(2)}) %collective-permute-start.9) | collective-permute-done | bytes 135200 | tf_op jit(solution)/shard_map/exchange/ppermute | solution.py:234
  19.8 0.8 %score.4 = (bf16[2,1024,256]{2,1,0:T(8,128)(2,1)S(1)}, f32[16,256]{1,0:T(8,128)S(1)}) custom-call(bf16[528,128]{1,0:T(8,128)(2,1)S(1)} %collective-permute-done.6.q_ref, bf16[1040,128]{1,0:T(8,128)(2,1)S(1)} %get-tuple-element.31.refs_0_, bf16[1040,128]{1,0:T(8,128)(2,1)S(1)} %collective-permute-done.7.refs_1_, ...), custom_call_target="tpu_custom_call" | custom-call | flops 134217728 | bytes 1048576 | tf_op jit(solution)/shard_map/score/score/pallas_call | solution.py:272
  20.6 0.6 %collective-permute-done.10.refs_3_ = bf16[512,128]{1,0:T(8,128)(2,1)S(1)} collective-permute-done((bf16[512,128]{1,0:T(8,128)(2,1)S(1)}, bf16[512,128]{1,0:T(8,128)(2,1)S(1)}, u32[]{:S(2)}, u32[]{:S(2)}) %collective-permute-start.10) | collective-permute-done | bytes 131104 | tf_op jit(solution)/shard_map/exchange/ppermute | solution.py:234
  21.2 0.3 apply.4
  21.6 1.6 %collective-permute-start.11 = (bf16[544,128]{1,0:T(8,128)(2,1)S(1)}, bf16[544,128]{1,0:T(8,128)(2,1)S(1)}, u32[]{:S(2)}, u32[]{:S(2)}) collective-permute-start(bf16[544,128]{1,0:T(8,128)(2,1)S(1)} %apply.4), channel_id=1, source_target_pairs={{0,2},{1,3},{2,0},{3,1},{4,6},{5,7},{6,4},{7,5},{8,10},{9,11},{10,... | collective-permute-start | bytes 417800 | tf_op jit(solution)/shard_map/return/ppermute | solution.py:316
  23.2 0.7 %score.5 = (bf16[2,1024,256]{2,1,0:T(8,128)(2,1)S(1)}, f32[16,256]{1,0:T(8,128)S(1)}) custom-call(bf16[528,128]{1,0:T(8,128)(2,1)S(1)} %collective-permute-done.4.q_ref, bf16[1040,128]{1,0:T(8,128)(2,1)S(1)} %get-tuple-element.31.refs_0_, bf16[1040,128]{1,0:T(8,128)(2,1)S(1)} %collective-permute-done.7.refs_1_, ...), custom_call_target="tpu_custom_call" | custom-call | flops 134217728 | bytes 1048576 | tf_op jit(solution)/shard_map/score/score/pallas_call | solution.py:272
  24.0 0.3 apply.5
  24.3 0.5 %collective-permute-start.15 = (bf16[272,128]{1,0:T(8,128)(2,1)S(1)}, bf16[272,128]{1,0:T(8,128)(2,1)S(1)}, u32[]{:S(2)}, u32[]{:S(2)}) collective-permute-start(bf16[272,128]{1,0:T(8,128)(2,1)S(1)} %get-tuple-element.40), channel_id=1, source_target_pairs={{0,2},{1,3},{2,0},{3,1},{4,6},{5,7},{6,4},{7,5},{8,10},{9,11},{10,... | collective-permute-start | bytes 208904 | tf_op jit(solution)/shard_map/return/ppermute | solution.py:314
  24.8 0.0 collective-permute-done.5.q_ref
  24.8 0.7 %score.6 = (bf16[2,1024,256]{2,1,0:T(8,128)(2,1)S(1)}, f32[16,256]{1,0:T(8,128)S(1)}) custom-call(bf16[528,128]{1,0:T(8,128)(2,1)S(1)} %collective-permute-done.5.q_ref, bf16[1040,128]{1,0:T(8,128)(2,1)S(1)} %get-tuple-element.31.refs_0_, bf16[1040,128]{1,0:T(8,128)(2,1)S(1)} %collective-permute-done.7.refs_1_, ...), custom_call_target="tpu_custom_call" | custom-call | flops 134217728 | bytes 1048576 | tf_op jit(solution)/shard_map/score/score/pallas_call | solution.py:272
  25.6 0.3 apply.6.refs_0_
  25.9 1.0 %collective-permute-done.11.refs_1_ = bf16[544,128]{1,0:T(8,128)(2,1)S(1)} collective-permute-done((bf16[544,128]{1,0:T(8,128)(2,1)S(1)}, bf16[544,128]{1,0:T(8,128)(2,1)S(1)}, u32[]{:S(2)}, u32[]{:S(2)}) %collective-permute-start.11) | collective-permute-done | bytes 139296 | tf_op jit(solution)/shard_map/return/ppermute | solution.py:316
  26.9 0.1 add.1
  27.0 2.7 %collective-permute-start.13 = (bf16[272,128]{1,0:T(8,128)(2,1)S(1)}, bf16[272,128]{1,0:T(8,128)(2,1)S(1)}, u32[]{:S(2)}, u32[]{:S(2)}) collective-permute-start(bf16[272,128]{1,0:T(8,128)(2,1)S(1)} %get-tuple-element.44), channel_id=1, source_target_pairs={{0,4},{1,5},{2,6},{3,7},{4,0},{5,1},{6,2},{7,3},{8,12},{9,13},{10,... | collective-permute-start | bytes 208904 | tf_op jit(solution)/shard_map/return/ppermute | solution.py:314
  29.6 0.0 collective-permute-start.14
  29.7 0.8 %score.7 = (bf16[2,1024,256]{2,1,0:T(8,128)(2,1)S(1)}, f32[16,256]{1,0:T(8,128)S(1)}) custom-call(bf16[528,128]{1,0:T(8,128)(2,1)S(1)} %get-tuple-element.45.q_ref, bf16[1040,128]{1,0:T(8,128)(2,1)S(1)} %get-tuple-element.31.refs_0_, bf16[1040,128]{1,0:T(8,128)(2,1)S(1)} %collective-permute-done.7.refs_1_, ...), custom_call_target="tpu_custom_call" | custom-call | flops 134217728 | bytes 1048576 | tf_op jit(solution)/shard_map/score/score/pallas_call | solution.py:272
  30.4 0.3 apply.7
  30.8 2.0 %collective-permute-start.16 = (bf16[272,128]{1,0:T(8,128)(2,1)S(1)}, bf16[272,128]{1,0:T(8,128)(2,1)S(1)}, u32[]{:S(2)}, u32[]{:S(2)}) collective-permute-start(bf16[272,128]{1,0:T(8,128)(2,1)S(1)} %get-tuple-element.52), channel_id=1, source_target_pairs={{0,3},{1,2},{2,1},{3,0},{4,7},{5,6},{6,5},{7,4},{8,11},{9,10},{10,... | collective-permute-start | bytes 208904 | tf_op jit(solution)/shard_map/return/ppermute | solution.py:314
  32.7 0.3 collective-permute-start.12
  33.1 0.0 collective-permute-done.15.refs_4_
  33.1 3.0 %collective-permute-done.14.refs_3_ = bf16[272,128]{1,0:T(8,128)(2,1)S(1)} collective-permute-done((bf16[272,128]{1,0:T(8,128)(2,1)S(1)}, bf16[272,128]{1,0:T(8,128)(2,1)S(1)}, u32[]{:S(2)}, u32[]{:S(2)}) %collective-permute-start.14) | collective-permute-done | bytes 69664 | tf_op jit(solution)/shard_map/return/ppermute | solution.py:314
  36.1 0.0 collective-permute-done.13.refs_2_
  36.1 0.0 collective-permute-done.16.refs_5_
  36.1 0.0 collective-permute-done.12.refs_1_
  36.1 0.8 %combine.1 = bf16[128,512]{1,0:T(8,128)(2,1)} custom-call(bf16[272,128]{1,0:T(8,128)(2,1)S(1)} %get-tuple-element.48.refs_0_, bf16[272,128]{1,0:T(8,128)(2,1)S(1)} %collective-permute-done.12.refs_1_, bf16[272,128]{1,0:T(8,128)(2,1)S(1)} %collective-permute-done.13.refs_2_, bf16[272,128]{1,0:T(8,128)(2,1)S(1)} %collective-permute-done.14.refs_3_, ...), custom_call_target="tpu_custom_call" | custom-call | tf_op jit(solution)/shard_map/combine/combine/pallas_call | solution.py:339
  (5 shorter events, 0.1 us)
Async XLA Ops:
  0.0 2.7 %collective-permute-start.1 = (bf16[128,512]{1,0:T(8,128)(2,1)}, bf16[128,512]{1,0:T(8,128)(2,1)S(1)}, u32[]{:S(2)}, u32[]{:S(2)}) collective-permute-start(bf16[128,512]{1,0:T(8,128)(2,1)} %param.4), channel_id=1, source_target_pairs={{0,1},{1,0},{2,3},{3,2},{4,5},{5,4},{6,7},{7,6},{8,9},{9,8},{10,11... | collective-permute-start | bytes 393224 | tf_op jit(solution)/shard_map/swap/ppermute | solution.py:200
  0.5 2.3 %collective-permute-start.2 = (bf16[128,512]{1,0:T(8,128)(2,1)}, bf16[128,512]{1,0:T(8,128)(2,1)S(1)}, u32[]{:S(2)}, u32[]{:S(2)}) collective-permute-start(bf16[128,512]{1,0:T(8,128)(2,1)} %param.5), channel_id=1, source_target_pairs={{0,1},{1,0},{2,3},{3,2},{4,5},{5,4},{6,7},{7,6},{8,9},{9,8},{10,11... | collective-permute-start | bytes 393224 | tf_op jit(solution)/shard_map/swap/ppermute | solution.py:200
  0.5 2.3 %collective-permute-start.3 = (bf16[128,512]{1,0:T(8,128)(2,1)}, bf16[128,512]{1,0:T(8,128)(2,1)S(1)}, u32[]{:S(2)}, u32[]{:S(2)}) collective-permute-start(bf16[128,512]{1,0:T(8,128)(2,1)} %param.6), channel_id=1, source_target_pairs={{0,1},{1,0},{2,3},{3,2},{4,5},{5,4},{6,7},{7,6},{8,9},{9,8},{10,11... | collective-permute-start | bytes 393224 | tf_op jit(solution)/shard_map/swap/ppermute | solution.py:200
  1.0 1.8 %collective-permute-start = (s32[1]{0:T(128)}, s32[1]{0:T(128)}, u32[]{:S(2)}, u32[]{:S(2)}) collective-permute-start(s32[1]{0:T(128)} %param.7), channel_id=1, source_target_pairs={{0,1},{1,0},{2,3},{3,2},{4,5},{5,4},{6,7},{7,6},{8,9},{9,8},{10,11... | collective-permute-start | bytes 20 | tf_op jit(solution)/shard_map/swap/ppermute | solution.py:200
  3.6 9.6 %collective-permute-start.8 = (bf16[1040,128]{1,0:T(8,128)(2,1)S(1)}, bf16[1040,128]{1,0:T(8,128)(2,1)S(1)}, u32[]{:S(2)}, u32[]{:S(2)}) collective-permute-start(bf16[1040,128]{1,0:T(8,128)(2,1)S(1)} %get-tuple-element.31.refs_0_), channel_id=1, source_target_pairs={{0,16},{1,17},{2,18},{3,19},{4,20},{5,21},{6,22},{7,23},{8,24},{9,... | collective-permute-start | bytes 798728 | tf_op jit(solution)/shard_map/exchange/ppermute | solution.py:234
  6.6 8.0 %collective-permute-start.7 = (bf16[1040,128]{1,0:T(8,128)(2,1)S(1)}, bf16[1040,128]{1,0:T(8,128)(2,1)S(1)}, u32[]{:S(2)}, u32[]{:S(2)}) collective-permute-start(bf16[1040,128]{1,0:T(8,128)(2,1)S(1)} %get-tuple-element.31.refs_0_), channel_id=1, source_target_pairs={{0,8},{1,9},{2,10},{3,11},{4,12},{5,13},{6,14},{7,15},{8,0},{9,1},... | collective-permute-start | bytes 798728 | tf_op jit(solution)/shard_map/exchange/ppermute | solution.py:234
  8.1 7.0 %collective-permute-start.4 = (bf16[528,128]{1,0:T(8,128)(2,1)S(1)}, bf16[528,128]{1,0:T(8,128)(2,1)S(1)}, u32[]{:S(2)}, u32[]{:S(2)}) collective-permute-start(bf16[528,128]{1,0:T(8,128)(2,1)S(1)} %get-tuple-element.45.q_ref), channel_id=1, source_target_pairs={{0,2},{1,3},{2,0},{3,1},{4,6},{5,7},{6,4},{7,5},{8,10},{9,11},{10,... | collective-permute-start | bytes 405512 | tf_op jit(solution)/shard_map/exchange/ppermute | solution.py:251
  9.7 9.7 %collective-permute-start.6 = (bf16[528,128]{1,0:T(8,128)(2,1)S(1)}, bf16[528,128]{1,0:T(8,128)(2,1)S(1)}, u32[]{:S(2)}, u32[]{:S(2)}) collective-permute-start(bf16[528,128]{1,0:T(8,128)(2,1)S(1)} %get-tuple-element.45.q_ref), channel_id=1, source_target_pairs={{0,6},{1,7},{2,4},{3,5},{4,2},{5,3},{6,0},{7,1},{8,14},{9,15},{10,... | collective-permute-start | bytes 405512 | tf_op jit(solution)/shard_map/exchange/ppermute | solution.py:251
  14.7 5.1 %collective-permute-start.9 = (bf16[528,128]{1,0:T(8,128)(2,1)S(1)}, bf16[528,128]{1,0:T(8,128)(2,1)S(1)}, u32[]{:S(2)}, u32[]{:S(2)}) collective-permute-start(bf16[528,128]{1,0:T(8,128)(2,1)S(1)} %get-tuple-element.32), channel_id=1, source_target_pairs={{0,16},{1,9},{2,18},{3,11},{4,20},{5,13},{6,22},{7,15},{8,24},{9,1... | collective-permute-start | bytes 405512 | tf_op jit(solution)/shard_map/exchange/ppermute | solution.py:234
  15.2 6.1 %collective-permute-start.10 = (bf16[512,128]{1,0:T(8,128)(2,1)S(1)}, bf16[512,128]{1,0:T(8,128)(2,1)S(1)}, u32[]{:S(2)}, u32[]{:S(2)}) collective-permute-start(bf16[512,128]{1,0:T(8,128)(2,1)S(1)} %get-tuple-element.36), channel_id=1, source_target_pairs={{0,16},{1,9},{2,18},{3,11},{4,20},{5,13},{6,22},{7,15},{8,24},{9,1... | collective-permute-start | bytes 393224 | tf_op jit(solution)/shard_map/exchange/ppermute | solution.py:234
  16.8 8.0 %collective-permute-start.5 = (bf16[528,128]{1,0:T(8,128)(2,1)S(1)}, bf16[528,128]{1,0:T(8,128)(2,1)S(1)}, u32[]{:S(2)}, u32[]{:S(2)}) collective-permute-start(bf16[528,128]{1,0:T(8,128)(2,1)S(1)} %get-tuple-element.45.q_ref), channel_id=1, source_target_pairs={{0,4},{1,5},{2,6},{3,7},{4,0},{5,1},{6,2},{7,3},{8,12},{9,13},{10,... | collective-permute-start | bytes 405512 | tf_op jit(solution)/shard_map/exchange/ppermute | solution.py:251
  21.6 5.3 %collective-permute-start.11 = (bf16[544,128]{1,0:T(8,128)(2,1)S(1)}, bf16[544,128]{1,0:T(8,128)(2,1)S(1)}, u32[]{:S(2)}, u32[]{:S(2)}) collective-permute-start(bf16[544,128]{1,0:T(8,128)(2,1)S(1)} %apply.4), channel_id=1, source_target_pairs={{0,2},{1,3},{2,0},{3,1},{4,6},{5,7},{6,4},{7,5},{8,10},{9,11},{10,... | collective-permute-start | bytes 417800 | tf_op jit(solution)/shard_map/return/ppermute | solution.py:316
  24.3 8.8 %collective-permute-start.15 = (bf16[272,128]{1,0:T(8,128)(2,1)S(1)}, bf16[272,128]{1,0:T(8,128)(2,1)S(1)}, u32[]{:S(2)}, u32[]{:S(2)}) collective-permute-start(bf16[272,128]{1,0:T(8,128)(2,1)S(1)} %get-tuple-element.40), channel_id=1, source_target_pairs={{0,2},{1,3},{2,0},{3,1},{4,6},{5,7},{6,4},{7,5},{8,10},{9,11},{10,... | collective-permute-start | bytes 208904 | tf_op jit(solution)/shard_map/return/ppermute | solution.py:314
  27.0 9.1 %collective-permute-start.13 = (bf16[272,128]{1,0:T(8,128)(2,1)S(1)}, bf16[272,128]{1,0:T(8,128)(2,1)S(1)}, u32[]{:S(2)}, u32[]{:S(2)}) collective-permute-start(bf16[272,128]{1,0:T(8,128)(2,1)S(1)} %get-tuple-element.44), channel_id=1, source_target_pairs={{0,4},{1,5},{2,6},{3,7},{4,0},{5,1},{6,2},{7,3},{8,12},{9,13},{10,... | collective-permute-start | bytes 208904 | tf_op jit(solution)/shard_map/return/ppermute | solution.py:314
  29.6 6.4 %collective-permute-start.14 = (bf16[272,128]{1,0:T(8,128)(2,1)S(1)}, bf16[272,128]{1,0:T(8,128)(2,1)S(1)}, u32[]{:S(2)}, u32[]{:S(2)}) collective-permute-start(bf16[272,128]{1,0:T(8,128)(2,1)S(1)} %get-tuple-element.50), channel_id=1, source_target_pairs={{0,5},{1,4},{2,7},{3,6},{4,1},{5,0},{6,3},{7,2},{8,13},{9,12},{10,... | collective-permute-start | bytes 208904 | tf_op jit(solution)/shard_map/return/ppermute | solution.py:314
  30.8 5.3 %collective-permute-start.16 = (bf16[272,128]{1,0:T(8,128)(2,1)S(1)}, bf16[272,128]{1,0:T(8,128)(2,1)S(1)}, u32[]{:S(2)}, u32[]{:S(2)}) collective-permute-start(bf16[272,128]{1,0:T(8,128)(2,1)S(1)} %get-tuple-element.52), channel_id=1, source_target_pairs={{0,3},{1,2},{2,1},{3,0},{4,7},{5,6},{6,5},{7,4},{8,11},{9,10},{10,... | collective-permute-start | bytes 208904 | tf_op jit(solution)/shard_map/return/ppermute | solution.py:314
  32.7 3.4 %collective-permute-start.12 = (bf16[272,128]{1,0:T(8,128)(2,1)S(1)}, bf16[272,128]{1,0:T(8,128)(2,1)S(1)}, u32[]{:S(2)}, u32[]{:S(2)}) collective-permute-start(bf16[272,128]{1,0:T(8,128)(2,1)S(1)} %get-tuple-element.49), channel_id=1, source_target_pairs={{0,1},{1,0},{2,3},{3,2},{4,5},{5,4},{6,7},{7,6},{8,9},{9,8},{10,11... | collective-permute-start | bytes 208904 | tf_op jit(solution)/shard_map/return/ppermute | solution.py:337

commit v28 on v26

--- a/solution.py
+++ b/solution.py
@@ -35,15 +35,15 @@
             out[row : row + tok, :] = piece
 
 
-def starts(p0, p1, size):
+def starts(p0, p1):
     half = PAD // CORES
-    return jnp.concatenate([jnp.full((half, size), p[0].astype(F32), F32) for p in (p0, p1)], axis=0).astype(BF16)
+    return jnp.concatenate([p[...].astype(F32)[0:half, :] for p in (p0, p1)], axis=0).astype(BF16)
 
 
 def merge_kernel(p0, p1, own, q1, k1, v1, q_out, kv_out):
     tok = q1.shape[0]
     rows = PER * CORES * tok
-    pos = starts(p0, p1, q_out.shape[1])
+    pos = starts(p0, p1)
     place(own.at[0:tok, :], q1, q_out, 0)
     q_out[rows:, :] = pos
     place(own.at[tok : 2 * tok, :], k1, kv_out, 0)
@@ -183,21 +183,21 @@
         return lax.optimization_barrier((a, b))[0]
 
     with jax.named_scope("swap"):
-        other = [lax.ppermute(a, "inner", along_inner(0, 1)) for a in (queries, keys, values, block_pos)]
+        here = jnp.broadcast_to(block_pos.astype(BF16)[:, None], (PAD, size))
+        other = [lax.ppermute(a, "inner", along_inner(0, 1)) for a in (queries, keys, values, here)]
         own = jnp.concatenate([queries, keys, values], axis=0)
     with jax.named_scope("merge"):
-        smem = [pl.BlockSpec(memory_space=pltpu.SMEM)]
         q_piece, kv_piece = pl.pallas_call(
             merge_kernel,
             out_shape=(
                 jax.ShapeDtypeStruct((PER * both + PAD, size), BF16),
                 jax.ShapeDtypeStruct((2 * PER * both + PAD, size), BF16),
             ),
-            in_specs=smem * 2 + vmem(4),
+            in_specs=vmem(6),
             out_specs=tuple(vmem(2)),
             compiler_params=params,
             name="merge",
-        )(block_pos, other[3], own, *other[:3])
+        )(here, other[3], own, *other[:3])
     half = PER * both + PAD
     block = PER * size + PAD
 

time: 36.8 us -> 36.5 us (level)
  Pallas kernels: 6.03 us -> 5.42 us
    pallas_call x1, Pallas kernels: 0.76 us -> 0.14 us  [shards(): pl.pallas_call(merge_kernel, out_shape=(jax.ShapeDtypeStruct((PER * both...]
where the time goes in v28:
time: 36.5 us; the launch traced here: 36.3 us
  starting transfers between devices  22.2 us (61%)
  waiting for transfers between devices  6.86 us (19%)
  Pallas kernels  5.42 us (15%)
  other arithmetic  1.06 us (3%)
  between operations  0.77 us (2%)
    ppermute x4, starting transfers between devices, over(): return lax.ppermute(a, 'outer', [(o, o ^ r) for o in range(n_out)])  7.89 us
    ppermute x3, starting transfers between devices, shards(): q_by[r] = lax.ppermute(piece, 'inner', along_inner(r, 0))  6.64 us
    ppermute x4, starting transfers between devices, send(): lax.ppermute(parts[x], 'inner', along_inner(r, x))  4.63 us
    ppermute x4, waiting for transfers between devices, send(): lax.ppermute(parts[x], 'inner', along_inner(r, x))  3.57 us
    pallas_call x4, Pallas kernels, score(): pl.pallas_call(functools.partial(score_kernel, r == 0), out_shape=(jax.Sh...  3.03 us
    ppermute x1, starting transfers between devices, send(): lax.ppermute(parts[0], 'inner', along_inner(low(r), 0))  1.64 us
    pallas_call x4, Pallas kernels, apply(): pl.pallas_call(functools.partial(apply_kernel, wide, rows), out_shape=sha...  1.35 us
    ppermute x4, waiting for transfers between devices, over(): return lax.ppermute(a, 'outer', [(o, o ^ r) for o in range(n_out)])  1.18 us
  transfers between devices with their start and end apart: 17, of which 5 were waited for; matrix products, arithmetic and copies ran while one was open for 3% of the time, Pallas kernels for 12%

profile of v28, /device:TPU:0, one launch (start us, length us, event | category | flops | bytes accessed | tf_op | source)
XLA Modules:
  0.0 36.3 jit_solution(6749197417030173780)
XLA Ops:
  0.0 0.5 %collective-permute-start.1 = (bf16[128,512]{1,0:T(8,128)(2,1)}, bf16[128,512]{1,0:T(8,128)(2,1)S(1)}, u32[]{:S(2)}, u32[]{:S(2)}) collective-permute-start(bf16[128,512]{1,0:T(8,128)(2,1)} %param.4), channel_id=1, source_target_pairs={{0,1},{1,0},{2,3},{3,2},{4,5},{5,4},{6,7},{7,6},{8,9},{9,8},{10,11... | collective-permute-start | bytes 393224 | tf_op jit(solution)/shard_map/swap/ppermute | solution.py:187
  0.5 0.1 collective-permute-start.2
  0.5 0.5 %collective-permute-start.3 = (bf16[128,512]{1,0:T(8,128)(2,1)}, bf16[128,512]{1,0:T(8,128)(2,1)S(1)}, u32[]{:S(2)}, u32[]{:S(2)}) collective-permute-start(bf16[128,512]{1,0:T(8,128)(2,1)} %param.6), channel_id=1, source_target_pairs={{0,1},{1,0},{2,3},{3,2},{4,5},{5,4},{6,7},{7,6},{8,9},{9,8},{10,11... | collective-permute-start | bytes 393224 | tf_op jit(solution)/shard_map/swap/ppermute | solution.py:187
  1.6 0.1 collective-permute-start
  1.8 1.1 %pad_maximum_fusion.own = bf16[384,512]{1,0:T(8,128)(2,1)S(1)} fusion(bf16[128,512]{1,0:T(8,128)(2,1)} %param.6, bf16[128,512]{1,0:T(8,128)(2,1)} %param.5, bf16[128,512]{1,0:T(8,128)(2,1)} %param.4), kind=kLoop, calls=%fused_computation | loop fusion | flops 1179648 | bytes 786432 | tf_op jit(solution)/shard_map/swap/concatenate | solution.py:188
  2.8 0.0 collective-permute-done.p1
  2.9 0.0 collective-permute-done.1.q1
  2.9 0.0 collective-permute-done.2.k1
  2.9 0.0 collective-permute-done.3.v1
  2.9 0.1 merge.1
  3.0 3.0 %collective-permute-start.7 = (bf16[1040,128]{1,0:T(8,128)(2,1)S(1)}, bf16[1040,128]{1,0:T(8,128)(2,1)S(1)}, u32[]{:S(2)}, u32[]{:S(2)}) collective-permute-start(bf16[1040,128]{1,0:T(8,128)(2,1)S(1)} %get-tuple-element.28.refs_0_), channel_id=1, source_target_pairs={{0,8},{8,0},{16,24},{24,16},{1,9},{9,1},{17,25},{25,17},{2,10},{10... | collective-permute-start | bytes 798728 | tf_op jit(solution)/shard_map/exchange/ppermute | solution.py:214
  6.0 1.5 %collective-permute-start.8 = (bf16[1040,128]{1,0:T(8,128)(2,1)S(1)}, bf16[1040,128]{1,0:T(8,128)(2,1)S(1)}, u32[]{:S(2)}, u32[]{:S(2)}) collective-permute-start(bf16[1040,128]{1,0:T(8,128)(2,1)S(1)} %get-tuple-element.28.refs_0_), channel_id=1, source_target_pairs={{0,16},{8,24},{16,0},{24,8},{1,17},{9,25},{17,1},{25,9},{2,18},{10... | collective-permute-start | bytes 798728 | tf_op jit(solution)/shard_map/exchange/ppermute | solution.py:214
  7.5 1.6 %collective-permute-start.4 = (bf16[528,128]{1,0:T(8,128)(2,1)S(1)}, bf16[528,128]{1,0:T(8,128)(2,1)S(1)}, u32[]{:S(2)}, u32[]{:S(2)}) collective-permute-start(bf16[528,128]{1,0:T(8,128)(2,1)S(1)} %get-tuple-element.39.q_ref), channel_id=1, source_target_pairs={{0,2},{1,3},{2,0},{3,1},{4,6},{5,7},{6,4},{7,5},{8,10},{9,11},{10,... | collective-permute-start | bytes 405512 | tf_op jit(solution)/shard_map/exchange/ppermute | solution.py:221
  9.1 2.5 %collective-permute-start.6 = (bf16[528,128]{1,0:T(8,128)(2,1)S(1)}, bf16[528,128]{1,0:T(8,128)(2,1)S(1)}, u32[]{:S(2)}, u32[]{:S(2)}) collective-permute-start(bf16[528,128]{1,0:T(8,128)(2,1)S(1)} %get-tuple-element.39.q_ref), channel_id=1, source_target_pairs={{0,6},{1,7},{2,4},{3,5},{4,2},{5,3},{6,0},{7,1},{8,14},{9,15},{10,... | collective-permute-start | bytes 405512 | tf_op jit(solution)/shard_map/exchange/ppermute | solution.py:221
  11.6 1.1 %collective-permute-done.7.refs_1_ = bf16[1040,128]{1,0:T(8,128)(2,1)S(1)} collective-permute-done((bf16[1040,128]{1,0:T(8,128)(2,1)S(1)}, bf16[1040,128]{1,0:T(8,128)(2,1)S(1)}, u32[]{:S(2)}, u32[]{:S(2)}) %collective-permute-start.7) | collective-permute-done | bytes 266272 | tf_op jit(solution)/shard_map/exchange/ppermute | solution.py:214
  12.7 1.8 %collective-permute-start.9 = (bf16[528,128]{1,0:T(8,128)(2,1)S(1)}, bf16[528,128]{1,0:T(8,128)(2,1)S(1)}, u32[]{:S(2)}, u32[]{:S(2)}) collective-permute-start(bf16[528,128]{1,0:T(8,128)(2,1)S(1)} %slice.8), channel_id=1, source_target_pairs={{0,16},{8,24},{16,0},{24,8},{1,17},{9,25},{17,1},{25,9},{2,18},{10... | collective-permute-start | bytes 405512 | tf_op jit(solution)/shard_map/exchange/ppermute | solution.py:214
  14.5 0.0 collective-permute-done.8.refs_2_
  14.5 1.6 %collective-permute-start.10 = (bf16[512,128]{1,0:T(8,128)(2,1)S(1)}, bf16[512,128]{1,0:T(8,128)(2,1)S(1)}, u32[]{:S(2)}, u32[]{:S(2)}) collective-permute-start(bf16[512,128]{1,0:T(8,128)(2,1)S(1)} %slice.9), channel_id=1, source_target_pairs={{0,8},{8,0},{16,24},{24,16},{1,9},{9,1},{17,25},{25,17},{2,10},{10... | collective-permute-start | bytes 393224 | tf_op jit(solution)/shard_map/exchange/ppermute | solution.py:214
  16.1 0.0 collective-permute-done.4.q_ref
  16.1 2.6 %collective-permute-start.5 = (bf16[528,128]{1,0:T(8,128)(2,1)S(1)}, bf16[528,128]{1,0:T(8,128)(2,1)S(1)}, u32[]{:S(2)}, u32[]{:S(2)}) collective-permute-start(bf16[528,128]{1,0:T(8,128)(2,1)S(1)} %get-tuple-element.39.q_ref), channel_id=1, source_target_pairs={{0,4},{1,5},{2,6},{3,7},{4,0},{5,1},{6,2},{7,3},{8,12},{9,13},{10,... | collective-permute-start | bytes 405512 | tf_op jit(solution)/shard_map/exchange/ppermute | solution.py:221
  18.7 0.0 collective-permute-done.6.q_ref
  18.7 0.0 collective-permute-done.9.refs_3_
  18.7 0.8 %score.4 = (bf16[2,1024,256]{2,1,0:T(8,128)(2,1)S(1)}, f32[16,256]{1,0:T(8,128)S(1)}) custom-call(bf16[528,128]{1,0:T(8,128)(2,1)S(1)} %collective-permute-done.6.q_ref, bf16[1040,128]{1,0:T(8,128)(2,1)S(1)} %get-tuple-element.28.refs_0_, bf16[1040,128]{1,0:T(8,128)(2,1)S(1)} %collective-permute-done.7.refs_1_, ...), custom_call_target="tpu_custom_call" | custom-call | flops 134217728 | bytes 1048576 | tf_op jit(solution)/shard_map/score/score/pallas_call | solution.py:242
  19.4 0.1 collective-permute-done.10.refs_3_
  19.5 0.3 apply.4
  19.9 1.6 %collective-permute-start.11 = (bf16[544,128]{1,0:T(8,128)(2,1)S(1)}, bf16[544,128]{1,0:T(8,128)(2,1)S(1)}, u32[]{:S(2)}, u32[]{:S(2)}) collective-permute-start(bf16[544,128]{1,0:T(8,128)(2,1)S(1)} %apply.4), channel_id=1, source_target_pairs={{0,2},{1,3},{2,0},{3,1},{4,6},{5,7},{6,4},{7,5},{8,10},{9,11},{10,... | collective-permute-start | bytes 417800 | tf_op jit(solution)/shard_map/return/ppermute | solution.py:286
  21.5 0.8 %score.5 = (bf16[2,1024,256]{2,1,0:T(8,128)(2,1)S(1)}, f32[16,256]{1,0:T(8,128)S(1)}) custom-call(bf16[528,128]{1,0:T(8,128)(2,1)S(1)} %collective-permute-done.4.q_ref, bf16[1040,128]{1,0:T(8,128)(2,1)S(1)} %get-tuple-element.28.refs_0_, bf16[1040,128]{1,0:T(8,128)(2,1)S(1)} %collective-permute-done.7.refs_1_, ...), custom_call_target="tpu_custom_call" | custom-call | flops 134217728 | bytes 1048576 | tf_op jit(solution)/shard_map/score/score/pallas_call | solution.py:242
  22.3 0.3 apply.5
  22.6 0.5 %collective-permute-start.15 = (bf16[272,128]{1,0:T(8,128)(2,1)S(1)}, bf16[272,128]{1,0:T(8,128)(2,1)S(1)}, u32[]{:S(2)}, u32[]{:S(2)}) collective-permute-start(bf16[272,128]{1,0:T(8,128)(2,1)S(1)} %get-tuple-element.34), channel_id=1, source_target_pairs={{0,2},{1,3},{2,0},{3,1},{4,6},{5,7},{6,4},{7,5},{8,10},{9,11},{10,... | collective-permute-start | bytes 208904 | tf_op jit(solution)/shard_map/return/ppermute | solution.py:284
  23.2 1.0 %collective-permute-done.5.q_ref = bf16[528,128]{1,0:T(8,128)(2,1)S(1)} collective-permute-done((bf16[528,128]{1,0:T(8,128)(2,1)S(1)}, bf16[528,128]{1,0:T(8,128)(2,1)S(1)}, u32[]{:S(2)}, u32[]{:S(2)}) %collective-permute-start.5) | collective-permute-done | bytes 135200 | tf_op jit(solution)/shard_map/exchange/ppermute | solution.py:221
  24.1 0.8 %score.6 = (bf16[2,1024,256]{2,1,0:T(8,128)(2,1)S(1)}, f32[16,256]{1,0:T(8,128)S(1)}) custom-call(bf16[528,128]{1,0:T(8,128)(2,1)S(1)} %collective-permute-done.5.q_ref, bf16[1040,128]{1,0:T(8,128)(2,1)S(1)} %get-tuple-element.28.refs_0_, bf16[1040,128]{1,0:T(8,128)(2,1)S(1)} %collective-permute-done.7.refs_1_, ...), custom_call_target="tpu_custom_call" | custom-call | flops 134217728 | bytes 1048576 | tf_op jit(solution)/shard_map/score/score/pallas_call | solution.py:242
  24.9 0.3 apply.6.refs_0_
  25.2 1.1 %collective-permute-done.11.refs_1_ = bf16[544,128]{1,0:T(8,128)(2,1)S(1)} collective-permute-done((bf16[544,128]{1,0:T(8,128)(2,1)S(1)}, bf16[544,128]{1,0:T(8,128)(2,1)S(1)}, u32[]{:S(2)}, u32[]{:S(2)}) %collective-permute-start.11) | collective-permute-done | bytes 139296 | tf_op jit(solution)/shard_map/return/ppermute | solution.py:286
  26.3 0.1 add.1
  26.4 1.8 %collective-permute-start.13 = (bf16[272,128]{1,0:T(8,128)(2,1)S(1)}, bf16[272,128]{1,0:T(8,128)(2,1)S(1)}, u32[]{:S(2)}, u32[]{:S(2)}) collective-permute-start(bf16[272,128]{1,0:T(8,128)(2,1)S(1)} %get-tuple-element.38), channel_id=1, source_target_pairs={{0,4},{1,5},{2,6},{3,7},{4,0},{5,1},{6,2},{7,3},{8,12},{9,13},{10,... | collective-permute-start | bytes 208904 | tf_op jit(solution)/shard_map/return/ppermute | solution.py:284
  28.2 0.0 collective-permute-start.14
  28.2 0.8 %score.7 = (bf16[2,1024,256]{2,1,0:T(8,128)(2,1)S(1)}, f32[16,256]{1,0:T(8,128)S(1)}) custom-call(bf16[528,128]{1,0:T(8,128)(2,1)S(1)} %get-tuple-element.39.q_ref, bf16[1040,128]{1,0:T(8,128)(2,1)S(1)} %get-tuple-element.28.refs_0_, bf16[1040,128]{1,0:T(8,128)(2,1)S(1)} %collective-permute-done.7.refs_1_, ...), custom_call_target="tpu_custom_call" | custom-call | flops 134217728 | bytes 1048576 | tf_op jit(solution)/shard_map/score/score/pallas_call | solution.py:242
  28.9 0.3 apply.7
  29.3 2.3 %collective-permute-start.16 = (bf16[272,128]{1,0:T(8,128)(2,1)S(1)}, bf16[272,128]{1,0:T(8,128)(2,1)S(1)}, u32[]{:S(2)}, u32[]{:S(2)}) collective-permute-start(bf16[272,128]{1,0:T(8,128)(2,1)S(1)} %get-tuple-element.46), channel_id=1, source_target_pairs={{0,3},{1,2},{2,1},{3,0},{4,7},{5,6},{6,5},{7,4},{8,11},{9,10},{10,... | collective-permute-start | bytes 208904 | tf_op jit(solution)/shard_map/return/ppermute | solution.py:284
  31.6 0.3 collective-permute-start.12
  31.9 0.0 collective-permute-done.15.refs_4_
  31.9 3.6 %collective-permute-done.14.refs_3_ = bf16[272,128]{1,0:T(8,128)(2,1)S(1)} collective-permute-done((bf16[272,128]{1,0:T(8,128)(2,1)S(1)}, bf16[272,128]{1,0:T(8,128)(2,1)S(1)}, u32[]{:S(2)}, u32[]{:S(2)}) %collective-permute-start.14) | collective-permute-done | bytes 69664 | tf_op jit(solution)/shard_map/return/ppermute | solution.py:284
  35.5 0.0 collective-permute-done.13.refs_2_
  35.5 0.0 collective-permute-done.16.refs_5_
  35.5 0.0 collective-permute-done.12.refs_1_
  35.5 0.8 %combine.1 = bf16[128,512]{1,0:T(8,128)(2,1)} custom-call(bf16[272,128]{1,0:T(8,128)(2,1)S(1)} %get-tuple-element.42.refs_0_, bf16[272,128]{1,0:T(8,128)(2,1)S(1)} %collective-permute-done.12.refs_1_, bf16[272,128]{1,0:T(8,128)(2,1)S(1)} %collective-permute-done.13.refs_2_, bf16[272,128]{1,0:T(8,128)(2,1)S(1)} %collective-permute-done.14.refs_3_, ...), custom_call_target="tpu_custom_call" | custom-call | tf_op jit(solution)/shard_map/combine/combine/pallas_call | solution.py:309
  (3 shorter events, 0.0 us)
Async XLA Ops:
  0.0 2.9 %collective-permute-start.1 = (bf16[128,512]{1,0:T(8,128)(2,1)}, bf16[128,512]{1,0:T(8,128)(2,1)S(1)}, u32[]{:S(2)}, u32[]{:S(2)}) collective-permute-start(bf16[128,512]{1,0:T(8,128)(2,1)} %param.4), channel_id=1, source_target_pairs={{0,1},{1,0},{2,3},{3,2},{4,5},{5,4},{6,7},{7,6},{8,9},{9,8},{10,11... | collective-permute-start | bytes 393224 | tf_op jit(solution)/shard_map/swap/ppermute | solution.py:187
  0.5 2.4 %collective-permute-start.2 = (bf16[128,512]{1,0:T(8,128)(2,1)}, bf16[128,512]{1,0:T(8,128)(2,1)S(1)}, u32[]{:S(2)}, u32[]{:S(2)}) collective-permute-start(bf16[128,512]{1,0:T(8,128)(2,1)} %param.5), channel_id=1, source_target_pairs={{0,1},{1,0},{2,3},{3,2},{4,5},{5,4},{6,7},{7,6},{8,9},{9,8},{10,11... | collective-permute-start | bytes 393224 | tf_op jit(solution)/shard_map/swap/ppermute | solution.py:187
  0.5 2.4 %collective-permute-start.3 = (bf16[128,512]{1,0:T(8,128)(2,1)}, bf16[128,512]{1,0:T(8,128)(2,1)S(1)}, u32[]{:S(2)}, u32[]{:S(2)}) collective-permute-start(bf16[128,512]{1,0:T(8,128)(2,1)} %param.6), channel_id=1, source_target_pairs={{0,1},{1,0},{2,3},{3,2},{4,5},{5,4},{6,7},{7,6},{8,9},{9,8},{10,11... | collective-permute-start | bytes 393224 | tf_op jit(solution)/shard_map/swap/ppermute | solution.py:187
  1.6 1.2 %collective-permute-start = (bf16[16,128]{1,0:T(8,128)(2,1)S(1)}, bf16[16,128]{1,0:T(8,128)(2,1)S(1)}, u32[]{:S(2)}, u32[]{:S(2)}) collective-permute-start(bf16[16,128]{1,0:T(8,128)(2,1)S(1)} %broadcast_in_dim.9.p0), channel_id=1, source_target_pairs={{0,1},{1,0},{2,3},{3,2},{4,5},{5,4},{6,7},{7,6},{8,9},{9,8},{10,11... | collective-permute-start | bytes 12296 | tf_op jit(solution)/shard_map/swap/ppermute | solution.py:187
  3.0 9.6 %collective-permute-start.7 = (bf16[1040,128]{1,0:T(8,128)(2,1)S(1)}, bf16[1040,128]{1,0:T(8,128)(2,1)S(1)}, u32[]{:S(2)}, u32[]{:S(2)}) collective-permute-start(bf16[1040,128]{1,0:T(8,128)(2,1)S(1)} %get-tuple-element.28.refs_0_), channel_id=1, source_target_pairs={{0,8},{8,0},{16,24},{24,16},{1,9},{9,1},{17,25},{25,17},{2,10},{10... | collective-permute-start | bytes 798728 | tf_op jit(solution)/shard_map/exchange/ppermute | solution.py:214
  6.0 8.5 %collective-permute-start.8 = (bf16[1040,128]{1,0:T(8,128)(2,1)S(1)}, bf16[1040,128]{1,0:T(8,128)(2,1)S(1)}, u32[]{:S(2)}, u32[]{:S(2)}) collective-permute-start(bf16[1040,128]{1,0:T(8,128)(2,1)S(1)} %get-tuple-element.28.refs_0_), channel_id=1, source_target_pairs={{0,16},{8,24},{16,0},{24,8},{1,17},{9,25},{17,1},{25,9},{2,18},{10... | collective-permute-start | bytes 798728 | tf_op jit(solution)/shard_map/exchange/ppermute | solution.py:214
  7.5 8.5 %collective-permute-start.4 = (bf16[528,128]{1,0:T(8,128)(2,1)S(1)}, bf16[528,128]{1,0:T(8,128)(2,1)S(1)}, u32[]{:S(2)}, u32[]{:S(2)}) collective-permute-start(bf16[528,128]{1,0:T(8,128)(2,1)S(1)} %get-tuple-element.39.q_ref), channel_id=1, source_target_pairs={{0,2},{1,3},{2,0},{3,1},{4,6},{5,7},{6,4},{7,5},{8,10},{9,11},{10,... | collective-permute-start | bytes 405512 | tf_op jit(solution)/shard_map/exchange/ppermute | solution.py:221
  9.1 9.6 %collective-permute-start.6 = (bf16[528,128]{1,0:T(8,128)(2,1)S(1)}, bf16[528,128]{1,0:T(8,128)(2,1)S(1)}, u32[]{:S(2)}, u32[]{:S(2)}) collective-permute-start(bf16[528,128]{1,0:T(8,128)(2,1)S(1)} %get-tuple-element.39.q_ref), channel_id=1, source_target_pairs={{0,6},{1,7},{2,4},{3,5},{4,2},{5,3},{6,0},{7,1},{8,14},{9,15},{10,... | collective-permute-start | bytes 405512 | tf_op jit(solution)/shard_map/exchange/ppermute | solution.py:221
  12.7 6.0 %collective-permute-start.9 = (bf16[528,128]{1,0:T(8,128)(2,1)S(1)}, bf16[528,128]{1,0:T(8,128)(2,1)S(1)}, u32[]{:S(2)}, u32[]{:S(2)}) collective-permute-start(bf16[528,128]{1,0:T(8,128)(2,1)S(1)} %slice.8), channel_id=1, source_target_pairs={{0,16},{8,24},{16,0},{24,8},{1,17},{9,25},{17,1},{25,9},{2,18},{10... | collective-permute-start | bytes 405512 | tf_op jit(solution)/shard_map/exchange/ppermute | solution.py:214
  14.5 5.0 %collective-permute-start.10 = (bf16[512,128]{1,0:T(8,128)(2,1)S(1)}, bf16[512,128]{1,0:T(8,128)(2,1)S(1)}, u32[]{:S(2)}, u32[]{:S(2)}) collective-permute-start(bf16[512,128]{1,0:T(8,128)(2,1)S(1)} %slice.9), channel_id=1, source_target_pairs={{0,8},{8,0},{16,24},{24,16},{1,9},{9,1},{17,25},{25,17},{2,10},{10... | collective-permute-start | bytes 393224 | tf_op jit(solution)/shard_map/exchange/ppermute | solution.py:214
  16.1 8.1 %collective-permute-start.5 = (bf16[528,128]{1,0:T(8,128)(2,1)S(1)}, bf16[528,128]{1,0:T(8,128)(2,1)S(1)}, u32[]{:S(2)}, u32[]{:S(2)}) collective-permute-start(bf16[528,128]{1,0:T(8,128)(2,1)S(1)} %get-tuple-element.39.q_ref), channel_id=1, source_target_pairs={{0,4},{1,5},{2,6},{3,7},{4,0},{5,1},{6,2},{7,3},{8,12},{9,13},{10,... | collective-permute-start | bytes 405512 | tf_op jit(solution)/shard_map/exchange/ppermute | solution.py:221
  19.9 6.4 %collective-permute-start.11 = (bf16[544,128]{1,0:T(8,128)(2,1)S(1)}, bf16[544,128]{1,0:T(8,128)(2,1)S(1)}, u32[]{:S(2)}, u32[]{:S(2)}) collective-permute-start(bf16[544,128]{1,0:T(8,128)(2,1)S(1)} %apply.4), channel_id=1, source_target_pairs={{0,2},{1,3},{2,0},{3,1},{4,6},{5,7},{6,4},{7,5},{8,10},{9,11},{10,... | collective-permute-start | bytes 417800 | tf_op jit(solution)/shard_map/return/ppermute | solution.py:286
  22.6 9.3 %collective-permute-start.15 = (bf16[272,128]{1,0:T(8,128)(2,1)S(1)}, bf16[272,128]{1,0:T(8,128)(2,1)S(1)}, u32[]{:S(2)}, u32[]{:S(2)}) collective-permute-start(bf16[272,128]{1,0:T(8,128)(2,1)S(1)} %get-tuple-element.34), channel_id=1, source_target_pairs={{0,2},{1,3},{2,0},{3,1},{4,6},{5,7},{6,4},{7,5},{8,10},{9,11},{10,... | collective-permute-start | bytes 208904 | tf_op jit(solution)/shard_map/return/ppermute | solution.py:284
  26.4 9.1 %collective-permute-start.13 = (bf16[272,128]{1,0:T(8,128)(2,1)S(1)}, bf16[272,128]{1,0:T(8,128)(2,1)S(1)}, u32[]{:S(2)}, u32[]{:S(2)}) collective-permute-start(bf16[272,128]{1,0:T(8,128)(2,1)S(1)} %get-tuple-element.38), channel_id=1, source_target_pairs={{0,4},{1,5},{2,6},{3,7},{4,0},{5,1},{6,2},{7,3},{8,12},{9,13},{10,... | collective-permute-start | bytes 208904 | tf_op jit(solution)/shard_map/return/ppermute | solution.py:284
  28.2 7.3 %collective-permute-start.14 = (bf16[272,128]{1,0:T(8,128)(2,1)S(1)}, bf16[272,128]{1,0:T(8,128)(2,1)S(1)}, u32[]{:S(2)}, u32[]{:S(2)}) collective-permute-start(bf16[272,128]{1,0:T(8,128)(2,1)S(1)} %get-tuple-element.44), channel_id=1, source_target_pairs={{0,5},{1,4},{2,7},{3,6},{4,1},{5,0},{6,3},{7,2},{8,13},{9,12},{10,... | collective-permute-start | bytes 208904 | tf_op jit(solution)/shard_map/return/ppermute | solution.py:284
  29.3 6.2 %collective-permute-start.16 = (bf16[272,128]{1,0:T(8,128)(2,1)S(1)}, bf16[272,128]{1,0:T(8,128)(2,1)S(1)}, u32[]{:S(2)}, u32[]{:S(2)}) collective-permute-start(bf16[272,128]{1,0:T(8,128)(2,1)S(1)} %get-tuple-element.46), channel_id=1, source_target_pairs={{0,3},{1,2},{2,1},{3,0},{4,7},{5,6},{6,5},{7,4},{8,11},{9,10},{10,... | collective-permute-start | bytes 208904 | tf_op jit(solution)/shard_map/return/ppermute | solution.py:284
  31.6 3.9 %collective-permute-start.12 = (bf16[272,128]{1,0:T(8,128)(2,1)S(1)}, bf16[272,128]{1,0:T(8,128)(2,1)S(1)}, u32[]{:S(2)}, u32[]{:S(2)}) collective-permute-start(bf16[272,128]{1,0:T(8,128)(2,1)S(1)} %get-tuple-element.43), channel_id=1, source_target_pairs={{0,1},{1,0},{2,3},{3,2},{4,5},{5,4},{6,7},{7,6},{8,9},{9,8},{10,11... | collective-permute-start | bytes 208904 | tf_op jit(solution)/shard_map/return/ppermute | solution.py:307

commit v29 on v28

--- a/solution.py
+++ b/solution.py
@@ -41,14 +41,14 @@
 
 
 def merge_kernel(p0, p1, own, q1, k1, v1, q_out, kv_out):
-    tok = q1.shape[0]
+    tok, width = q1.shape
     rows = PER * CORES * tok
     pos = starts(p0, p1)
-    place(own.at[0:tok, :], q1, q_out, 0)
+    place(own.at[:, 0:width], q1, q_out, 0)
     q_out[rows:, :] = pos
-    place(own.at[tok : 2 * tok, :], k1, kv_out, 0)
+    place(own.at[:, width : 2 * width], k1, kv_out, 0)
     kv_out[rows : rows + PAD, :] = pos
-    place(own.at[2 * tok : 3 * tok, :], v1, kv_out, rows + PAD, turned=True)
+    place(own.at[:, 2 * width : 3 * width], v1, kv_out, rows + PAD, turned=True)
 
 
 def score_kernel(same, q_ref, *refs):
@@ -185,7 +185,7 @@
     with jax.named_scope("swap"):
         here = jnp.broadcast_to(block_pos.astype(BF16)[:, None], (PAD, size))
         other = [lax.ppermute(a, "inner", along_inner(0, 1)) for a in (queries, keys, values, here)]
-        own = jnp.concatenate([queries, keys, values], axis=0)
+        own = jnp.concatenate([queries, keys, values], axis=1)
     with jax.named_scope("merge"):
         q_piece, kv_piece = pl.pallas_call(
             merge_kernel,

time: 36.5 us -> 37.1 us (1.016)
  waiting for transfers between devices: 6.86 us -> 7.46 us
  transfers between devices with their start and end apart: 17 -> 17, of which waited for: 5 -> 7; matrix products, arithmetic and copies ran while one was open for 3% -> 3% of each run, Pallas kernels for 12% -> 12%
where the time goes in v29:
time: 37.1 us; the launch traced here: 37 us
  starting transfers between devices  22.3 us (60%)
  waiting for transfers between devices  7.46 us (20%)
  Pallas kernels  5.4 us (15%)
  other arithmetic  1.06 us (3%)
  between operations  0.79 us (2%)
    ppermute x4, starting transfers between devices, over(): return lax.ppermute(a, 'outer', [(o, o ^ r) for o in range(n_out)])  7.65 us
    ppermute x3, starting transfers between devices, shards(): q_by[r] = lax.ppermute(piece, 'inner', along_inner(r, 0))  6.64 us
    ppermute x4, starting transfers between devices, send(): lax.ppermute(parts[x], 'inner', along_inner(r, x))  4.91 us
    ppermute x4, waiting for transfers between devices, send(): lax.ppermute(parts[x], 'inner', along_inner(r, x))  3.29 us
    pallas_call x4, Pallas kernels, score(): pl.pallas_call(functools.partial(score_kernel, r == 0), out_shape=(jax.Sh...  3.03 us
    ppermute x1, starting transfers between devices, send(): lax.ppermute(parts[0], 'inner', along_inner(low(r), 0))  1.64 us
    ppermute x4, waiting for transfers between devices, over(): return lax.ppermute(a, 'outer', [(o, o ^ r) for o in range(n_out)])  1.43 us
    pallas_call x4, Pallas kernels, apply(): pl.pallas_call(functools.partial(apply_kernel, wide, rows), out_shape=sha...  1.34 us
  transfers between devices with their start and end apart: 17, of which 7 were waited for; matrix products, arithmetic and copies ran while one was open for 3% of the time, Pallas kernels for 12%

profile of v29, /device:TPU:0, one launch (start us, length us, event | category | flops | bytes accessed | tf_op | source)
XLA Modules:
  0.0 37.0 jit_solution(4094587462336711210)
XLA Ops:
  0.7 0.5 %collective-permute-start = (bf16[16,128]{1,0:T(8,128)(2,1)S(1)}, bf16[16,128]{1,0:T(8,128)(2,1)S(1)}, u32[]{:S(2)}, u32[]{:S(2)}) collective-permute-start(bf16[16,128]{1,0:T(8,128)(2,1)S(1)} %broadcast_in_dim.9.p0), channel_id=1, source_target_pairs={{0,1},{1,0},{2,3},{3,2},{4,5},{5,4},{6,7},{7,6},{8,9},{9,8},{10,11... | collective-permute-start | bytes 12296 | tf_op jit(solution)/shard_map/swap/ppermute | solution.py:187
  1.2 0.1 collective-permute-start.1
  1.3 0.4 %collective-permute-start.2 = (bf16[128,512]{1,0:T(8,128)(2,1)}, bf16[128,512]{1,0:T(8,128)(2,1)S(1)}, u32[]{:S(2)}, u32[]{:S(2)}) collective-permute-start(bf16[128,512]{1,0:T(8,128)(2,1)} %param.5), channel_id=1, source_target_pairs={{0,1},{1,0},{2,3},{3,2},{4,5},{5,4},{6,7},{7,6},{8,9},{9,8},{10,11... | collective-permute-start | bytes 393224 | tf_op jit(solution)/shard_map/swap/ppermute | solution.py:187
  1.7 0.1 collective-permute-start.3
  1.8 1.1 %pad_maximum_fusion.own = bf16[128,1536]{1,0:T(8,128)(2,1)S(1)} fusion(bf16[128,512]{1,0:T(8,128)(2,1)} %param.6, bf16[128,512]{1,0:T(8,128)(2,1)} %param.5, bf16[128,512]{1,0:T(8,128)(2,1)} %param.4), kind=kLoop, calls=%fused_computation | loop fusion | flops 1179648 | bytes 786432 | tf_op jit(solution)/shard_map/swap/concatenate | solution.py:188
  2.8 0.0 collective-permute-done.p1
  2.8 0.0 collective-permute-done.1.q1
  2.9 0.1 collective-permute-done.2.k1
  2.9 0.3 collective-permute-done.3.v1
  3.3 0.1 merge.1
  3.4 2.7 %collective-permute-start.7 = (bf16[1040,128]{1,0:T(8,128)(2,1)S(1)}, bf16[1040,128]{1,0:T(8,128)(2,1)S(1)}, u32[]{:S(2)}, u32[]{:S(2)}) collective-permute-start(bf16[1040,128]{1,0:T(8,128)(2,1)S(1)} %get-tuple-element.28.refs_0_), channel_id=1, source_target_pairs={{0,8},{8,0},{16,24},{24,16},{1,9},{9,1},{17,25},{25,17},{2,10},{10... | collective-permute-start | bytes 798728 | tf_op jit(solution)/shard_map/exchange/ppermute | solution.py:214
  6.1 1.5 %collective-permute-start.8 = (bf16[1040,128]{1,0:T(8,128)(2,1)S(1)}, bf16[1040,128]{1,0:T(8,128)(2,1)S(1)}, u32[]{:S(2)}, u32[]{:S(2)}) collective-permute-start(bf16[1040,128]{1,0:T(8,128)(2,1)S(1)} %get-tuple-element.28.refs_0_), channel_id=1, source_target_pairs={{0,16},{8,24},{16,0},{24,8},{1,17},{9,25},{17,1},{25,9},{2,18},{10... | collective-permute-start | bytes 798728 | tf_op jit(solution)/shard_map/exchange/ppermute | solution.py:214
  7.7 1.6 %collective-permute-start.4 = (bf16[528,128]{1,0:T(8,128)(2,1)S(1)}, bf16[528,128]{1,0:T(8,128)(2,1)S(1)}, u32[]{:S(2)}, u32[]{:S(2)}) collective-permute-start(bf16[528,128]{1,0:T(8,128)(2,1)S(1)} %get-tuple-element.39.q_ref), channel_id=1, source_target_pairs={{0,2},{1,3},{2,0},{3,1},{4,6},{5,7},{6,4},{7,5},{8,10},{9,11},{10,... | collective-permute-start | bytes 405512 | tf_op jit(solution)/shard_map/exchange/ppermute | solution.py:221
  9.2 2.5 %collective-permute-start.6 = (bf16[528,128]{1,0:T(8,128)(2,1)S(1)}, bf16[528,128]{1,0:T(8,128)(2,1)S(1)}, u32[]{:S(2)}, u32[]{:S(2)}) collective-permute-start(bf16[528,128]{1,0:T(8,128)(2,1)S(1)} %get-tuple-element.39.q_ref), channel_id=1, source_target_pairs={{0,6},{1,7},{2,4},{3,5},{4,2},{5,3},{6,0},{7,1},{8,14},{9,15},{10,... | collective-permute-start | bytes 405512 | tf_op jit(solution)/shard_map/exchange/ppermute | solution.py:221
  11.7 1.3 %collective-permute-done.7.refs_1_ = bf16[1040,128]{1,0:T(8,128)(2,1)S(1)} collective-permute-done((bf16[1040,128]{1,0:T(8,128)(2,1)S(1)}, bf16[1040,128]{1,0:T(8,128)(2,1)S(1)}, u32[]{:S(2)}, u32[]{:S(2)}) %collective-permute-start.7) | collective-permute-done | bytes 266272 | tf_op jit(solution)/shard_map/exchange/ppermute | solution.py:214
  13.0 1.8 %collective-permute-start.9 = (bf16[528,128]{1,0:T(8,128)(2,1)S(1)}, bf16[528,128]{1,0:T(8,128)(2,1)S(1)}, u32[]{:S(2)}, u32[]{:S(2)}) collective-permute-start(bf16[528,128]{1,0:T(8,128)(2,1)S(1)} %slice.8), channel_id=1, source_target_pairs={{0,16},{8,24},{16,0},{24,8},{1,17},{9,25},{17,1},{25,9},{2,18},{10... | collective-permute-start | bytes 405512 | tf_op jit(solution)/shard_map/exchange/ppermute | solution.py:214
  14.9 0.0 collective-permute-done.8.refs_2_
  14.9 1.6 %collective-permute-start.10 = (bf16[512,128]{1,0:T(8,128)(2,1)S(1)}, bf16[512,128]{1,0:T(8,128)(2,1)S(1)}, u32[]{:S(2)}, u32[]{:S(2)}) collective-permute-start(bf16[512,128]{1,0:T(8,128)(2,1)S(1)} %slice.9), channel_id=1, source_target_pairs={{0,8},{8,0},{16,24},{24,16},{1,9},{9,1},{17,25},{25,17},{2,10},{10... | collective-permute-start | bytes 393224 | tf_op jit(solution)/shard_map/exchange/ppermute | solution.py:214
  16.4 0.0 collective-permute-done.4.q_ref
  16.4 2.6 %collective-permute-start.5 = (bf16[528,128]{1,0:T(8,128)(2,1)S(1)}, bf16[528,128]{1,0:T(8,128)(2,1)S(1)}, u32[]{:S(2)}, u32[]{:S(2)}) collective-permute-start(bf16[528,128]{1,0:T(8,128)(2,1)S(1)} %get-tuple-element.39.q_ref), channel_id=1, source_target_pairs={{0,4},{1,5},{2,6},{3,7},{4,0},{5,1},{6,2},{7,3},{8,12},{9,13},{10,... | collective-permute-start | bytes 405512 | tf_op jit(solution)/shard_map/exchange/ppermute | solution.py:221
  19.0 0.0 collective-permute-done.6.q_ref
  19.0 0.0 collective-permute-done.9.refs_3_
  19.0 0.8 %score.4 = (bf16[2,1024,256]{2,1,0:T(8,128)(2,1)S(1)}, f32[16,256]{1,0:T(8,128)S(1)}) custom-call(bf16[528,128]{1,0:T(8,128)(2,1)S(1)} %collective-permute-done.6.q_ref, bf16[1040,128]{1,0:T(8,128)(2,1)S(1)} %get-tuple-element.28.refs_0_, bf16[1040,128]{1,0:T(8,128)(2,1)S(1)} %collective-permute-done.7.refs_1_, ...), custom_call_target="tpu_custom_call" | custom-call | flops 134217728 | bytes 1048576 | tf_op jit(solution)/shard_map/score/score/pallas_call | solution.py:242
  19.8 0.1 collective-permute-done.10.refs_3_
  19.9 0.3 apply.4
  20.3 1.6 %collective-permute-start.11 = (bf16[544,128]{1,0:T(8,128)(2,1)S(1)}, bf16[544,128]{1,0:T(8,128)(2,1)S(1)}, u32[]{:S(2)}, u32[]{:S(2)}) collective-permute-start(bf16[544,128]{1,0:T(8,128)(2,1)S(1)} %apply.4), channel_id=1, source_target_pairs={{0,2},{1,3},{2,0},{3,1},{4,6},{5,7},{6,4},{7,5},{8,10},{9,11},{10,... | collective-permute-start | bytes 417800 | tf_op jit(solution)/shard_map/return/ppermute | solution.py:286
  21.9 0.8 %score.5 = (bf16[2,1024,256]{2,1,0:T(8,128)(2,1)S(1)}, f32[16,256]{1,0:T(8,128)S(1)}) custom-call(bf16[528,128]{1,0:T(8,128)(2,1)S(1)} %collective-permute-done.4.q_ref, bf16[1040,128]{1,0:T(8,128)(2,1)S(1)} %get-tuple-element.28.refs_0_, bf16[1040,128]{1,0:T(8,128)(2,1)S(1)} %collective-permute-done.7.refs_1_, ...), custom_call_target="tpu_custom_call" | custom-call | flops 134217728 | bytes 1048576 | tf_op jit(solution)/shard_map/score/score/pallas_call | solution.py:242
  22.7 0.3 apply.5
  23.0 0.5 %collective-permute-start.15 = (bf16[272,128]{1,0:T(8,128)(2,1)S(1)}, bf16[272,128]{1,0:T(8,128)(2,1)S(1)}, u32[]{:S(2)}, u32[]{:S(2)}) collective-permute-start(bf16[272,128]{1,0:T(8,128)(2,1)S(1)} %get-tuple-element.34), channel_id=1, source_target_pairs={{0,2},{1,3},{2,0},{3,1},{4,6},{5,7},{6,4},{7,5},{8,10},{9,11},{10,... | collective-permute-start | bytes 208904 | tf_op jit(solution)/shard_map/return/ppermute | solution.py:284
  23.5 1.3 %collective-permute-done.5.q_ref = bf16[528,128]{1,0:T(8,128)(2,1)S(1)} collective-permute-done((bf16[528,128]{1,0:T(8,128)(2,1)S(1)}, bf16[528,128]{1,0:T(8,128)(2,1)S(1)}, u32[]{:S(2)}, u32[]{:S(2)}) %collective-permute-start.5) | collective-permute-done | bytes 135200 | tf_op jit(solution)/shard_map/exchange/ppermute | solution.py:221
  24.8 0.8 %score.6 = (bf16[2,1024,256]{2,1,0:T(8,128)(2,1)S(1)}, f32[16,256]{1,0:T(8,128)S(1)}) custom-call(bf16[528,128]{1,0:T(8,128)(2,1)S(1)} %collective-permute-done.5.q_ref, bf16[1040,128]{1,0:T(8,128)(2,1)S(1)} %get-tuple-element.28.refs_0_, bf16[1040,128]{1,0:T(8,128)(2,1)S(1)} %collective-permute-done.7.refs_1_, ...), custom_call_target="tpu_custom_call" | custom-call | flops 134217728 | bytes 1048576 | tf_op jit(solution)/shard_map/score/score/pallas_call | solution.py:242
  25.5 0.3 apply.6.refs_0_
  25.9 1.1 %collective-permute-done.11.refs_1_ = bf16[544,128]{1,0:T(8,128)(2,1)S(1)} collective-permute-done((bf16[544,128]{1,0:T(8,128)(2,1)S(1)}, bf16[544,128]{1,0:T(8,128)(2,1)S(1)}, u32[]{:S(2)}, u32[]{:S(2)}) %collective-permute-start.11) | collective-permute-done | bytes 139296 | tf_op jit(solution)/shard_map/return/ppermute | solution.py:286
  27.0 0.1 add.1
  27.0 2.0 %collective-permute-start.13 = (bf16[272,128]{1,0:T(8,128)(2,1)S(1)}, bf16[272,128]{1,0:T(8,128)(2,1)S(1)}, u32[]{:S(2)}, u32[]{:S(2)}) collective-permute-start(bf16[272,128]{1,0:T(8,128)(2,1)S(1)} %get-tuple-element.38), channel_id=1, source_target_pairs={{0,4},{1,5},{2,6},{3,7},{4,0},{5,1},{6,2},{7,3},{8,12},{9,13},{10,... | collective-permute-start | bytes 208904 | tf_op jit(solution)/shard_map/return/ppermute | solution.py:284
  29.1 0.0 collective-permute-start.14
  29.1 0.8 %score.7 = (bf16[2,1024,256]{2,1,0:T(8,128)(2,1)S(1)}, f32[16,256]{1,0:T(8,128)S(1)}) custom-call(bf16[528,128]{1,0:T(8,128)(2,1)S(1)} %get-tuple-element.39.q_ref, bf16[1040,128]{1,0:T(8,128)(2,1)S(1)} %get-tuple-element.28.refs_0_, bf16[1040,128]{1,0:T(8,128)(2,1)S(1)} %collective-permute-done.7.refs_1_, ...), custom_call_target="tpu_custom_call" | custom-call | flops 134217728 | bytes 1048576 | tf_op jit(solution)/shard_map/score/score/pallas_call | solution.py:242
  29.9 0.3 apply.7
  30.2 2.3 %collective-permute-start.16 = (bf16[272,128]{1,0:T(8,128)(2,1)S(1)}, bf16[272,128]{1,0:T(8,128)(2,1)S(1)}, u32[]{:S(2)}, u32[]{:S(2)}) collective-permute-start(bf16[272,128]{1,0:T(8,128)(2,1)S(1)} %get-tuple-element.46), channel_id=1, source_target_pairs={{0,3},{1,2},{2,1},{3,0},{4,7},{5,6},{6,5},{7,4},{8,11},{9,10},{10,... | collective-permute-start | bytes 208904 | tf_op jit(solution)/shard_map/return/ppermute | solution.py:284
  32.6 0.3 collective-permute-start.12
  32.9 0.0 collective-permute-done.15.refs_4_
  32.9 3.3 %collective-permute-done.14.refs_3_ = bf16[272,128]{1,0:T(8,128)(2,1)S(1)} collective-permute-done((bf16[272,128]{1,0:T(8,128)(2,1)S(1)}, bf16[272,128]{1,0:T(8,128)(2,1)S(1)}, u32[]{:S(2)}, u32[]{:S(2)}) %collective-permute-start.14) | collective-permute-done | bytes 69664 | tf_op jit(solution)/shard_map/return/ppermute | solution.py:284
  36.2 0.0 collective-permute-done.13.refs_2_
  36.2 0.0 collective-permute-done.16.refs_5_
  36.2 0.0 collective-permute-done.12.refs_1_
  36.2 0.8 %combine.1 = bf16[128,512]{1,0:T(8,128)(2,1)} custom-call(bf16[272,128]{1,0:T(8,128)(2,1)S(1)} %get-tuple-element.42.refs_0_, bf16[272,128]{1,0:T(8,128)(2,1)S(1)} %collective-permute-done.12.refs_1_, bf16[272,128]{1,0:T(8,128)(2,1)S(1)} %collective-permute-done.13.refs_2_, bf16[272,128]{1,0:T(8,128)(2,1)S(1)} %collective-permute-done.14.refs_3_, ...), custom_call_target="tpu_custom_call" | custom-call | tf_op jit(solution)/shard_map/combine/combine/pallas_call | solution.py:309
  (3 shorter events, 0.0 us)
Async XLA Ops:
  0.7 2.2 %collective-permute-start = (bf16[16,128]{1,0:T(8,128)(2,1)S(1)}, bf16[16,128]{1,0:T(8,128)(2,1)S(1)}, u32[]{:S(2)}, u32[]{:S(2)}) collective-permute-start(bf16[16,128]{1,0:T(8,128)(2,1)S(1)} %broadcast_in_dim.9.p0), channel_id=1, source_target_pairs={{0,1},{1,0},{2,3},{3,2},{4,5},{5,4},{6,7},{7,6},{8,9},{9,8},{10,11... | collective-permute-start | bytes 12296 | tf_op jit(solution)/shard_map/swap/ppermute | solution.py:187
  1.2 1.7 %collective-permute-start.1 = (bf16[128,512]{1,0:T(8,128)(2,1)}, bf16[128,512]{1,0:T(8,128)(2,1)S(1)}, u32[]{:S(2)}, u32[]{:S(2)}) collective-permute-start(bf16[128,512]{1,0:T(8,128)(2,1)} %param.4), channel_id=1, source_target_pairs={{0,1},{1,0},{2,3},{3,2},{4,5},{5,4},{6,7},{7,6},{8,9},{9,8},{10,11... | collective-permute-start | bytes 393224 | tf_op jit(solution)/shard_map/swap/ppermute | solution.py:187
  1.3 1.7 %collective-permute-start.2 = (bf16[128,512]{1,0:T(8,128)(2,1)}, bf16[128,512]{1,0:T(8,128)(2,1)S(1)}, u32[]{:S(2)}, u32[]{:S(2)}) collective-permute-start(bf16[128,512]{1,0:T(8,128)(2,1)} %param.5), channel_id=1, source_target_pairs={{0,1},{1,0},{2,3},{3,2},{4,5},{5,4},{6,7},{7,6},{8,9},{9,8},{10,11... | collective-permute-start | bytes 393224 | tf_op jit(solution)/shard_map/swap/ppermute | solution.py:187
  1.7 1.6 %collective-permute-start.3 = (bf16[128,512]{1,0:T(8,128)(2,1)}, bf16[128,512]{1,0:T(8,128)(2,1)S(1)}, u32[]{:S(2)}, u32[]{:S(2)}) collective-permute-start(bf16[128,512]{1,0:T(8,128)(2,1)} %param.6), channel_id=1, source_target_pairs={{0,1},{1,0},{2,3},{3,2},{4,5},{5,4},{6,7},{7,6},{8,9},{9,8},{10,11... | collective-permute-start | bytes 393224 | tf_op jit(solution)/shard_map/swap/ppermute | solution.py:187
  3.4 9.6 %collective-permute-start.7 = (bf16[1040,128]{1,0:T(8,128)(2,1)S(1)}, bf16[1040,128]{1,0:T(8,128)(2,1)S(1)}, u32[]{:S(2)}, u32[]{:S(2)}) collective-permute-start(bf16[1040,128]{1,0:T(8,128)(2,1)S(1)} %get-tuple-element.28.refs_0_), channel_id=1, source_target_pairs={{0,8},{8,0},{16,24},{24,16},{1,9},{9,1},{17,25},{25,17},{2,10},{10... | collective-permute-start | bytes 798728 | tf_op jit(solution)/shard_map/exchange/ppermute | solution.py:214
  6.1 8.7 %collective-permute-start.8 = (bf16[1040,128]{1,0:T(8,128)(2,1)S(1)}, bf16[1040,128]{1,0:T(8,128)(2,1)S(1)}, u32[]{:S(2)}, u32[]{:S(2)}) collective-permute-start(bf16[1040,128]{1,0:T(8,128)(2,1)S(1)} %get-tuple-element.28.refs_0_), channel_id=1, source_target_pairs={{0,16},{8,24},{16,0},{24,8},{1,17},{9,25},{17,1},{25,9},{2,18},{10... | collective-permute-start | bytes 798728 | tf_op jit(solution)/shard_map/exchange/ppermute | solution.py:214
  7.7 8.8 %collective-permute-start.4 = (bf16[528,128]{1,0:T(8,128)(2,1)S(1)}, bf16[528,128]{1,0:T(8,128)(2,1)S(1)}, u32[]{:S(2)}, u32[]{:S(2)}) collective-permute-start(bf16[528,128]{1,0:T(8,128)(2,1)S(1)} %get-tuple-element.39.q_ref), channel_id=1, source_target_pairs={{0,2},{1,3},{2,0},{3,1},{4,6},{5,7},{6,4},{7,5},{8,10},{9,11},{10,... | collective-permute-start | bytes 405512 | tf_op jit(solution)/shard_map/exchange/ppermute | solution.py:221
  9.2 9.8 %collective-permute-start.6 = (bf16[528,128]{1,0:T(8,128)(2,1)S(1)}, bf16[528,128]{1,0:T(8,128)(2,1)S(1)}, u32[]{:S(2)}, u32[]{:S(2)}) collective-permute-start(bf16[528,128]{1,0:T(8,128)(2,1)S(1)} %get-tuple-element.39.q_ref), channel_id=1, source_target_pairs={{0,6},{1,7},{2,4},{3,5},{4,2},{5,3},{6,0},{7,1},{8,14},{9,15},{10,... | collective-permute-start | bytes 405512 | tf_op jit(solution)/shard_map/exchange/ppermute | solution.py:221
  13.0 6.0 %collective-permute-start.9 = (bf16[528,128]{1,0:T(8,128)(2,1)S(1)}, bf16[528,128]{1,0:T(8,128)(2,1)S(1)}, u32[]{:S(2)}, u32[]{:S(2)}) collective-permute-start(bf16[528,128]{1,0:T(8,128)(2,1)S(1)} %slice.8), channel_id=1, source_target_pairs={{0,16},{8,24},{16,0},{24,8},{1,17},{9,25},{17,1},{25,9},{2,18},{10... | collective-permute-start | bytes 405512 | tf_op jit(solution)/shard_map/exchange/ppermute | solution.py:214
  14.9 5.0 %collective-permute-start.10 = (bf16[512,128]{1,0:T(8,128)(2,1)S(1)}, bf16[512,128]{1,0:T(8,128)(2,1)S(1)}, u32[]{:S(2)}, u32[]{:S(2)}) collective-permute-start(bf16[512,128]{1,0:T(8,128)(2,1)S(1)} %slice.9), channel_id=1, source_target_pairs={{0,8},{8,0},{16,24},{24,16},{1,9},{9,1},{17,25},{25,17},{2,10},{10... | collective-permute-start | bytes 393224 | tf_op jit(solution)/shard_map/exchange/ppermute | solution.py:214
  16.4 8.3 %collective-permute-start.5 = (bf16[528,128]{1,0:T(8,128)(2,1)S(1)}, bf16[528,128]{1,0:T(8,128)(2,1)S(1)}, u32[]{:S(2)}, u32[]{:S(2)}) collective-permute-start(bf16[528,128]{1,0:T(8,128)(2,1)S(1)} %get-tuple-element.39.q_ref), channel_id=1, source_target_pairs={{0,4},{1,5},{2,6},{3,7},{4,0},{5,1},{6,2},{7,3},{8,12},{9,13},{10,... | collective-permute-start | bytes 405512 | tf_op jit(solution)/shard_map/exchange/ppermute | solution.py:221
  20.3 6.7 %collective-permute-start.11 = (bf16[544,128]{1,0:T(8,128)(2,1)S(1)}, bf16[544,128]{1,0:T(8,128)(2,1)S(1)}, u32[]{:S(2)}, u32[]{:S(2)}) collective-permute-start(bf16[544,128]{1,0:T(8,128)(2,1)S(1)} %apply.4), channel_id=1, source_target_pairs={{0,2},{1,3},{2,0},{3,1},{4,6},{5,7},{6,4},{7,5},{8,10},{9,11},{10,... | collective-permute-start | bytes 417800 | tf_op jit(solution)/shard_map/return/ppermute | solution.py:286
  23.0 9.9 %collective-permute-start.15 = (bf16[272,128]{1,0:T(8,128)(2,1)S(1)}, bf16[272,128]{1,0:T(8,128)(2,1)S(1)}, u32[]{:S(2)}, u32[]{:S(2)}) collective-permute-start(bf16[272,128]{1,0:T(8,128)(2,1)S(1)} %get-tuple-element.34), channel_id=1, source_target_pairs={{0,2},{1,3},{2,0},{3,1},{4,6},{5,7},{6,4},{7,5},{8,10},{9,11},{10,... | collective-permute-start | bytes 208904 | tf_op jit(solution)/shard_map/return/ppermute | solution.py:284
  27.0 9.1 %collective-permute-start.13 = (bf16[272,128]{1,0:T(8,128)(2,1)S(1)}, bf16[272,128]{1,0:T(8,128)(2,1)S(1)}, u32[]{:S(2)}, u32[]{:S(2)}) collective-permute-start(bf16[272,128]{1,0:T(8,128)(2,1)S(1)} %get-tuple-element.38), channel_id=1, source_target_pairs={{0,4},{1,5},{2,6},{3,7},{4,0},{5,1},{6,2},{7,3},{8,12},{9,13},{10,... | collective-permute-start | bytes 208904 | tf_op jit(solution)/shard_map/return/ppermute | solution.py:284
  29.1 7.1 %collective-permute-start.14 = (bf16[272,128]{1,0:T(8,128)(2,1)S(1)}, bf16[272,128]{1,0:T(8,128)(2,1)S(1)}, u32[]{:S(2)}, u32[]{:S(2)}) collective-permute-start(bf16[272,128]{1,0:T(8,128)(2,1)S(1)} %get-tuple-element.44), channel_id=1, source_target_pairs={{0,5},{1,4},{2,7},{3,6},{4,1},{5,0},{6,3},{7,2},{8,13},{9,12},{10,... | collective-permute-start | bytes 208904 | tf_op jit(solution)/shard_map/return/ppermute | solution.py:284
  30.2 6.0 %collective-permute-start.16 = (bf16[272,128]{1,0:T(8,128)(2,1)S(1)}, bf16[272,128]{1,0:T(8,128)(2,1)S(1)}, u32[]{:S(2)}, u32[]{:S(2)}) collective-permute-start(bf16[272,128]{1,0:T(8,128)(2,1)S(1)} %get-tuple-element.46), channel_id=1, source_target_pairs={{0,3},{1,2},{2,1},{3,0},{4,7},{5,6},{6,5},{7,4},{8,11},{9,10},{10,... | collective-permute-start | bytes 208904 | tf_op jit(solution)/shard_map/return/ppermute | solution.py:284
  32.6 3.6 %collective-permute-start.12 = (bf16[272,128]{1,0:T(8,128)(2,1)S(1)}, bf16[272,128]{1,0:T(8,128)(2,1)S(1)}, u32[]{:S(2)}, u32[]{:S(2)}) collective-permute-start(bf16[272,128]{1,0:T(8,128)(2,1)S(1)} %get-tuple-element.43), channel_id=1, source_target_pairs={{0,1},{1,0},{2,3},{3,2},{4,5},{5,4},{6,7},{7,6},{8,9},{9,8},{10,11... | collective-permute-start | bytes 208904 | tf_op jit(solution)/shard_map/return/ppermute | solution.py:307

commit v30 on v28

--- a/solution.py
+++ b/solution.py
@@ -280,7 +280,11 @@
 
     def send(r, parts):
         with jax.named_scope("return"):
-            if single(r):
+            if single(r) and r > 1:
+                both_blocks = lax.ppermute(parts[0], "inner", along_inner(r, 0))
+                ends.append(both_blocks[:block, :])
+                ends.append(lax.ppermute(both_blocks[block:, :], "inner", along_inner(0, 1)))
+            elif single(r):
                 ends.extend(lax.ppermute(parts[x], "inner", along_inner(r, x)) for x in range(CORES))
             else:
                 arrived[r - low(r)].append(lax.ppermute(parts[0], "inner", along_inner(low(r), 0)))
@@ -297,7 +301,7 @@
     for r in reversed(range(2, chips)):
         parts = partial[r]
         if arrived[r]:
-            parts = add([parts[0], *arrived[r]], not single(r))
+            parts = add([parts[0], *arrived[r]], True)
             done = parts[0]
         send(r, parts)
     done = both_kernels(0, done)

time: 36.5 us -> 35.8 us (0.981)
  starting transfers between devices: 22.2 us -> 21.8 us
    ppermute x4 -> x2, starting transfers between devices: 4.63 us -> 2.23 us  [send(): lax.ppermute(parts[x], 'inner', along_inner(r, x))]
    ppermute x4 -> x2, waiting for transfers between devices: 3.57 us -> 1.3 us  [send(): lax.ppermute(parts[x], 'inner', along_inner(r, x))]
    ppermute x0 -> x2, waiting for transfers between devices: none -> 2.21 us  [the longest x1 2.21 us: send(): both_blocks = lax.ppermute(parts[0], 'inner', along_inner(r, 0))]
    ppermute x0 -> x2, starting transfers between devices: none -> 2.17 us  [the longest x1 2.1 us: send(): both_blocks = lax.ppermute(parts[0], 'inner', along_inner(r, 0))]
    ppermute x1, waiting for transfers between devices: 1.07 us -> 0.32 us  [send(): lax.ppermute(parts[0], 'inner', along_inner(low(r), 0))]
    ppermute x3, waiting for transfers between devices: 0.99 us -> 1.5 us  [shards(): q_by[r] = lax.ppermute(piece, 'inner', along_inner(r, 0))]
  transfers between devices with their start and end apart: 17 -> 17, of which waited for: 5 -> 6; matrix products, arithmetic and copies ran while one was open for 3% -> 3% of each run, Pallas kernels for 12% -> 12%
where the time goes in v30:
time: 35.8 us; the launch traced here: 35.6 us
  starting transfers between devices  21.8 us (61%)
  waiting for transfers between devices  6.58 us (18%)
  Pallas kernels  5.42 us (15%)
  other arithmetic  1.06 us (3%)
  between operations  0.8 us (2%)
    ppermute x4, starting transfers between devices, over(): return lax.ppermute(a, 'outer', [(o, o ^ r) for o in range(n_out)])  7.89 us
    ppermute x3, starting transfers between devices, shards(): q_by[r] = lax.ppermute(piece, 'inner', along_inner(r, 0))  6.64 us
    pallas_call x4, Pallas kernels, score(): pl.pallas_call(functools.partial(score_kernel, r == 0), out_shape=(jax.Sh...  3.03 us
    ppermute x2, starting transfers between devices, send(): lax.ppermute(parts[x], 'inner', along_inner(r, x))  2.23 us
    ppermute x1, waiting for transfers between devices, send(): both_blocks = lax.ppermute(parts[0], 'inner', along_inner(r, 0))  2.21 us
    ppermute x1, starting transfers between devices, send(): both_blocks = lax.ppermute(parts[0], 'inner', along_inner(r, 0))  2.1 us
    ppermute x1, starting transfers between devices, send(): lax.ppermute(parts[0], 'inner', along_inner(low(r), 0))  1.64 us
    ppermute x3, waiting for transfers between devices, shards(): q_by[r] = lax.ppermute(piece, 'inner', along_inner(r, 0))  1.5 us
  transfers between devices with their start and end apart: 17, of which 6 were waited for; matrix products, arithmetic and copies ran while one was open for 3% of the time, Pallas kernels for 12%

profile of v30, /device:TPU:0, one launch (start us, length us, event | category | flops | bytes accessed | tf_op | source)
XLA Modules:
  0.0 35.6 jit_solution(8722517855798547041)
XLA Ops:
  0.0 0.5 %collective-permute-start.1 = (bf16[128,512]{1,0:T(8,128)(2,1)}, bf16[128,512]{1,0:T(8,128)(2,1)S(1)}, u32[]{:S(2)}, u32[]{:S(2)}) collective-permute-start(bf16[128,512]{1,0:T(8,128)(2,1)} %param.4), channel_id=1, source_target_pairs={{0,1},{1,0},{2,3},{3,2},{4,5},{5,4},{6,7},{7,6},{8,9},{9,8},{10,11... | collective-permute-start | bytes 393224 | tf_op jit(solution)/shard_map/swap/ppermute | solution.py:187
  0.5 0.1 collective-permute-start.2
  0.5 0.5 %collective-permute-start.3 = (bf16[128,512]{1,0:T(8,128)(2,1)}, bf16[128,512]{1,0:T(8,128)(2,1)S(1)}, u32[]{:S(2)}, u32[]{:S(2)}) collective-permute-start(bf16[128,512]{1,0:T(8,128)(2,1)} %param.6), channel_id=1, source_target_pairs={{0,1},{1,0},{2,3},{3,2},{4,5},{5,4},{6,7},{7,6},{8,9},{9,8},{10,11... | collective-permute-start | bytes 393224 | tf_op jit(solution)/shard_map/swap/ppermute | solution.py:187
  1.6 0.1 collective-permute-start
  1.8 1.1 %pad_maximum_fusion.own = bf16[384,512]{1,0:T(8,128)(2,1)S(1)} fusion(bf16[128,512]{1,0:T(8,128)(2,1)} %param.6, bf16[128,512]{1,0:T(8,128)(2,1)} %param.5, bf16[128,512]{1,0:T(8,128)(2,1)} %param.4), kind=kLoop, calls=%fused_computation | loop fusion | flops 1179648 | bytes 786432 | tf_op jit(solution)/shard_map/swap/concatenate | solution.py:188
  2.8 0.0 collective-permute-done.p1
  2.9 0.0 collective-permute-done.1.q1
  2.9 0.0 collective-permute-done.2.k1
  2.9 0.0 collective-permute-done.3.v1
  2.9 0.1 merge.1
  3.0 3.0 %collective-permute-start.7 = (bf16[1040,128]{1,0:T(8,128)(2,1)S(1)}, bf16[1040,128]{1,0:T(8,128)(2,1)S(1)}, u32[]{:S(2)}, u32[]{:S(2)}) collective-permute-start(bf16[1040,128]{1,0:T(8,128)(2,1)S(1)} %get-tuple-element.26.refs_0_), channel_id=1, source_target_pairs={{0,8},{8,0},{16,24},{24,16},{1,9},{9,1},{17,25},{25,17},{2,10},{10... | collective-permute-start | bytes 798728 | tf_op jit(solution)/shard_map/exchange/ppermute | solution.py:214
  6.0 1.5 %collective-permute-start.8 = (bf16[1040,128]{1,0:T(8,128)(2,1)S(1)}, bf16[1040,128]{1,0:T(8,128)(2,1)S(1)}, u32[]{:S(2)}, u32[]{:S(2)}) collective-permute-start(bf16[1040,128]{1,0:T(8,128)(2,1)S(1)} %get-tuple-element.26.refs_0_), channel_id=1, source_target_pairs={{0,16},{8,24},{16,0},{24,8},{1,17},{9,25},{17,1},{25,9},{2,18},{10... | collective-permute-start | bytes 798728 | tf_op jit(solution)/shard_map/exchange/ppermute | solution.py:214
  7.5 1.6 %collective-permute-start.4 = (bf16[528,128]{1,0:T(8,128)(2,1)S(1)}, bf16[528,128]{1,0:T(8,128)(2,1)S(1)}, u32[]{:S(2)}, u32[]{:S(2)}) collective-permute-start(bf16[528,128]{1,0:T(8,128)(2,1)S(1)} %get-tuple-element.36.q_ref), channel_id=1, source_target_pairs={{0,2},{1,3},{2,0},{3,1},{4,6},{5,7},{6,4},{7,5},{8,10},{9,11},{10,... | collective-permute-start | bytes 405512 | tf_op jit(solution)/shard_map/exchange/ppermute | solution.py:221
  9.1 2.5 %collective-permute-start.6 = (bf16[528,128]{1,0:T(8,128)(2,1)S(1)}, bf16[528,128]{1,0:T(8,128)(2,1)S(1)}, u32[]{:S(2)}, u32[]{:S(2)}) collective-permute-start(bf16[528,128]{1,0:T(8,128)(2,1)S(1)} %get-tuple-element.36.q_ref), channel_id=1, source_target_pairs={{0,6},{1,7},{2,4},{3,5},{4,2},{5,3},{6,0},{7,1},{8,14},{9,15},{10,... | collective-permute-start | bytes 405512 | tf_op jit(solution)/shard_map/exchange/ppermute | solution.py:221
  11.6 1.1 %collective-permute-done.7.refs_1_ = bf16[1040,128]{1,0:T(8,128)(2,1)S(1)} collective-permute-done((bf16[1040,128]{1,0:T(8,128)(2,1)S(1)}, bf16[1040,128]{1,0:T(8,128)(2,1)S(1)}, u32[]{:S(2)}, u32[]{:S(2)}) %collective-permute-start.7) | collective-permute-done | bytes 266272 | tf_op jit(solution)/shard_map/exchange/ppermute | solution.py:214
  12.7 1.8 %collective-permute-start.9 = (bf16[528,128]{1,0:T(8,128)(2,1)S(1)}, bf16[528,128]{1,0:T(8,128)(2,1)S(1)}, u32[]{:S(2)}, u32[]{:S(2)}) collective-permute-start(bf16[528,128]{1,0:T(8,128)(2,1)S(1)} %slice.16), channel_id=1, source_target_pairs={{0,16},{8,24},{16,0},{24,8},{1,17},{9,25},{17,1},{25,9},{2,18},{10... | collective-permute-start | bytes 405512 | tf_op jit(solution)/shard_map/exchange/ppermute | solution.py:214
  14.5 0.0 collective-permute-done.8.refs_2_
  14.5 1.6 %collective-permute-start.10 = (bf16[512,128]{1,0:T(8,128)(2,1)S(1)}, bf16[512,128]{1,0:T(8,128)(2,1)S(1)}, u32[]{:S(2)}, u32[]{:S(2)}) collective-permute-start(bf16[512,128]{1,0:T(8,128)(2,1)S(1)} %slice.17), channel_id=1, source_target_pairs={{0,8},{8,0},{16,24},{24,16},{1,9},{9,1},{17,25},{25,17},{2,10},{10... | collective-permute-start | bytes 393224 | tf_op jit(solution)/shard_map/exchange/ppermute | solution.py:214
  16.1 0.0 collective-permute-done.4.q_ref
  16.1 2.6 %collective-permute-start.5 = (bf16[528,128]{1,0:T(8,128)(2,1)S(1)}, bf16[528,128]{1,0:T(8,128)(2,1)S(1)}, u32[]{:S(2)}, u32[]{:S(2)}) collective-permute-start(bf16[528,128]{1,0:T(8,128)(2,1)S(1)} %get-tuple-element.36.q_ref), channel_id=1, source_target_pairs={{0,4},{1,5},{2,6},{3,7},{4,0},{5,1},{6,2},{7,3},{8,12},{9,13},{10,... | collective-permute-start | bytes 405512 | tf_op jit(solution)/shard_map/exchange/ppermute | solution.py:221
  18.7 0.0 collective-permute-done.6.q_ref
  18.7 0.0 collective-permute-done.9.refs_3_
  18.7 0.8 %score.4 = (bf16[2,1024,256]{2,1,0:T(8,128)(2,1)S(1)}, f32[16,256]{1,0:T(8,128)S(1)}) custom-call(bf16[528,128]{1,0:T(8,128)(2,1)S(1)} %collective-permute-done.6.q_ref, bf16[1040,128]{1,0:T(8,128)(2,1)S(1)} %get-tuple-element.26.refs_0_, bf16[1040,128]{1,0:T(8,128)(2,1)S(1)} %collective-permute-done.7.refs_1_, ...), custom_call_target="tpu_custom_call" | custom-call | flops 134217728 | bytes 1048576 | tf_op jit(solution)/shard_map/score/score/pallas_call | solution.py:242
  19.4 0.1 collective-permute-done.10.refs_3_
  19.5 0.3 apply.4
  19.9 1.6 %collective-permute-start.11 = (bf16[544,128]{1,0:T(8,128)(2,1)S(1)}, bf16[544,128]{1,0:T(8,128)(2,1)S(1)}, u32[]{:S(2)}, u32[]{:S(2)}) collective-permute-start(bf16[544,128]{1,0:T(8,128)(2,1)S(1)} %apply.4), channel_id=1, source_target_pairs={{0,2},{1,3},{2,0},{3,1},{4,6},{5,7},{6,4},{7,5},{8,10},{9,11},{10,... | collective-permute-start | bytes 417800 | tf_op jit(solution)/shard_map/return/ppermute | solution.py:290
  21.5 0.8 %score.5 = (bf16[2,1024,256]{2,1,0:T(8,128)(2,1)S(1)}, f32[16,256]{1,0:T(8,128)S(1)}) custom-call(bf16[528,128]{1,0:T(8,128)(2,1)S(1)} %collective-permute-done.4.q_ref, bf16[1040,128]{1,0:T(8,128)(2,1)S(1)} %get-tuple-element.26.refs_0_, bf16[1040,128]{1,0:T(8,128)(2,1)S(1)} %collective-permute-done.7.refs_1_, ...), custom_call_target="tpu_custom_call" | custom-call | flops 134217728 | bytes 1048576 | tf_op jit(solution)/shard_map/score/score/pallas_call | solution.py:242
  22.3 0.3 apply.5
  22.6 1.5 %collective-permute-done.5.q_ref = bf16[528,128]{1,0:T(8,128)(2,1)S(1)} collective-permute-done((bf16[528,128]{1,0:T(8,128)(2,1)S(1)}, bf16[528,128]{1,0:T(8,128)(2,1)S(1)}, u32[]{:S(2)}, u32[]{:S(2)}) %collective-permute-start.5) | collective-permute-done | bytes 135200 | tf_op jit(solution)/shard_map/exchange/ppermute | solution.py:221
  24.1 0.8 %score.6 = (bf16[2,1024,256]{2,1,0:T(8,128)(2,1)S(1)}, f32[16,256]{1,0:T(8,128)S(1)}) custom-call(bf16[528,128]{1,0:T(8,128)(2,1)S(1)} %collective-permute-done.5.q_ref, bf16[1040,128]{1,0:T(8,128)(2,1)S(1)} %get-tuple-element.26.refs_0_, bf16[1040,128]{1,0:T(8,128)(2,1)S(1)} %collective-permute-done.7.refs_1_, ...), custom_call_target="tpu_custom_call" | custom-call | flops 134217728 | bytes 1048576 | tf_op jit(solution)/shard_map/score/score/pallas_call | solution.py:242
  24.9 0.3 apply.6.refs_0_
  25.2 0.3 collective-permute-done.11.refs_1_
  25.6 0.1 add.1
  25.7 2.1 %collective-permute-start.13 = (bf16[544,128]{1,0:T(8,128)(2,1)S(1)}, bf16[544,128]{1,0:T(8,128)(2,1)S(1)}, u32[]{:S(2)}, u32[]{:S(2)}) collective-permute-start(bf16[544,128]{1,0:T(8,128)(2,1)S(1)} %add.1), channel_id=1, source_target_pairs={{0,4},{1,5},{2,6},{3,7},{4,0},{5,1},{6,2},{7,3},{8,12},{9,13},{10,... | collective-permute-start | bytes 417800 | tf_op jit(solution)/shard_map/return/ppermute | solution.py:284
  27.7 2.2 %collective-permute-start.15 = (bf16[272,128]{1,0:T(8,128)(2,1)S(1)}, bf16[272,128]{1,0:T(8,128)(2,1)S(1)}, u32[]{:S(2)}, u32[]{:S(2)}) collective-permute-start(bf16[272,128]{1,0:T(8,128)(2,1)S(1)} %get-tuple-element.32), channel_id=1, source_target_pairs={{0,2},{1,3},{2,0},{3,1},{4,6},{5,7},{6,4},{7,5},{8,10},{9,11},{10,... | collective-permute-start | bytes 208904 | tf_op jit(solution)/shard_map/return/ppermute | solution.py:288
  29.9 0.8 %score.7 = (bf16[2,1024,256]{2,1,0:T(8,128)(2,1)S(1)}, f32[16,256]{1,0:T(8,128)S(1)}) custom-call(bf16[528,128]{1,0:T(8,128)(2,1)S(1)} %get-tuple-element.36.q_ref, bf16[1040,128]{1,0:T(8,128)(2,1)S(1)} %get-tuple-element.26.refs_0_, bf16[1040,128]{1,0:T(8,128)(2,1)S(1)} %collective-permute-done.7.refs_1_, ...), custom_call_target="tpu_custom_call" | custom-call | flops 134217728 | bytes 1048576 | tf_op jit(solution)/shard_map/score/score/pallas_call | solution.py:242
  30.7 0.3 apply.7
  31.0 0.1 collective-permute-start.16
  31.1 0.1 collective-permute-start.12
  31.2 2.2 %collective-permute-done.13 = bf16[544,128]{1,0:T(8,128)(2,1)S(1)} collective-permute-done((bf16[544,128]{1,0:T(8,128)(2,1)S(1)}, bf16[544,128]{1,0:T(8,128)(2,1)S(1)}, u32[]{:S(2)}, u32[]{:S(2)}) %collective-permute-start.13) | collective-permute-done | bytes 139296 | tf_op jit(solution)/shard_map/return/ppermute | solution.py:284
  33.4 0.1 collective-permute-start.14
  33.5 0.0 collective-permute-done.15.refs_4_
  33.5 1.3 %collective-permute-done.16.refs_5_ = bf16[272,128]{1,0:T(8,128)(2,1)S(1)} collective-permute-done((bf16[272,128]{1,0:T(8,128)(2,1)S(1)}, bf16[272,128]{1,0:T(8,128)(2,1)S(1)}, u32[]{:S(2)}, u32[]{:S(2)}) %collective-permute-start.16) | collective-permute-done | bytes 69664 | tf_op jit(solution)/shard_map/return/ppermute | solution.py:288
  34.8 0.0 collective-permute-done.12.refs_1_
  34.8 0.0 collective-permute-done.14.refs_3_
  34.8 0.8 %combine.1 = bf16[128,512]{1,0:T(8,128)(2,1)} custom-call(bf16[272,128]{1,0:T(8,128)(2,1)S(1)} %get-tuple-element.39.refs_0_, bf16[272,128]{1,0:T(8,128)(2,1)S(1)} %collective-permute-done.12.refs_1_, bf16[272,128]{1,0:T(8,128)(2,1)S(1)} %get-tuple-element.44.refs_2_, bf16[272,128]{1,0:T(8,128)(2,1)S(1)} %collective-permute-done.14.refs_3_, ...), custom_call_target="tpu_custom_call" | custom-call | tf_op jit(solution)/shard_map/combine/combine/pallas_call | solution.py:313
  (4 shorter events, 0.0 us)
Async XLA Ops:
  0.0 2.9 %collective-permute-start.1 = (bf16[128,512]{1,0:T(8,128)(2,1)}, bf16[128,512]{1,0:T(8,128)(2,1)S(1)}, u32[]{:S(2)}, u32[]{:S(2)}) collective-permute-start(bf16[128,512]{1,0:T(8,128)(2,1)} %param.4), channel_id=1, source_target_pairs={{0,1},{1,0},{2,3},{3,2},{4,5},{5,4},{6,7},{7,6},{8,9},{9,8},{10,11... | collective-permute-start | bytes 393224 | tf_op jit(solution)/shard_map/swap/ppermute | solution.py:187
  0.5 2.4 %collective-permute-start.2 = (bf16[128,512]{1,0:T(8,128)(2,1)}, bf16[128,512]{1,0:T(8,128)(2,1)S(1)}, u32[]{:S(2)}, u32[]{:S(2)}) collective-permute-start(bf16[128,512]{1,0:T(8,128)(2,1)} %param.5), channel_id=1, source_target_pairs={{0,1},{1,0},{2,3},{3,2},{4,5},{5,4},{6,7},{7,6},{8,9},{9,8},{10,11... | collective-permute-start | bytes 393224 | tf_op jit(solution)/shard_map/swap/ppermute | solution.py:187
  0.5 2.4 %collective-permute-start.3 = (bf16[128,512]{1,0:T(8,128)(2,1)}, bf16[128,512]{1,0:T(8,128)(2,1)S(1)}, u32[]{:S(2)}, u32[]{:S(2)}) collective-permute-start(bf16[128,512]{1,0:T(8,128)(2,1)} %param.6), channel_id=1, source_target_pairs={{0,1},{1,0},{2,3},{3,2},{4,5},{5,4},{6,7},{7,6},{8,9},{9,8},{10,11... | collective-permute-start | bytes 393224 | tf_op jit(solution)/shard_map/swap/ppermute | solution.py:187
  1.6 1.2 %collective-permute-start = (bf16[16,128]{1,0:T(8,128)(2,1)S(1)}, bf16[16,128]{1,0:T(8,128)(2,1)S(1)}, u32[]{:S(2)}, u32[]{:S(2)}) collective-permute-start(bf16[16,128]{1,0:T(8,128)(2,1)S(1)} %broadcast_in_dim.9.p0), channel_id=1, source_target_pairs={{0,1},{1,0},{2,3},{3,2},{4,5},{5,4},{6,7},{7,6},{8,9},{9,8},{10,11... | collective-permute-start | bytes 12296 | tf_op jit(solution)/shard_map/swap/ppermute | solution.py:187
  3.0 9.6 %collective-permute-start.7 = (bf16[1040,128]{1,0:T(8,128)(2,1)S(1)}, bf16[1040,128]{1,0:T(8,128)(2,1)S(1)}, u32[]{:S(2)}, u32[]{:S(2)}) collective-permute-start(bf16[1040,128]{1,0:T(8,128)(2,1)S(1)} %get-tuple-element.26.refs_0_), channel_id=1, source_target_pairs={{0,8},{8,0},{16,24},{24,16},{1,9},{9,1},{17,25},{25,17},{2,10},{10... | collective-permute-start | bytes 798728 | tf_op jit(solution)/shard_map/exchange/ppermute | solution.py:214
  6.0 8.5 %collective-permute-start.8 = (bf16[1040,128]{1,0:T(8,128)(2,1)S(1)}, bf16[1040,128]{1,0:T(8,128)(2,1)S(1)}, u32[]{:S(2)}, u32[]{:S(2)}) collective-permute-start(bf16[1040,128]{1,0:T(8,128)(2,1)S(1)} %get-tuple-element.26.refs_0_), channel_id=1, source_target_pairs={{0,16},{8,24},{16,0},{24,8},{1,17},{9,25},{17,1},{25,9},{2,18},{10... | collective-permute-start | bytes 798728 | tf_op jit(solution)/shard_map/exchange/ppermute | solution.py:214
  7.5 8.5 %collective-permute-start.4 = (bf16[528,128]{1,0:T(8,128)(2,1)S(1)}, bf16[528,128]{1,0:T(8,128)(2,1)S(1)}, u32[]{:S(2)}, u32[]{:S(2)}) collective-permute-start(bf16[528,128]{1,0:T(8,128)(2,1)S(1)} %get-tuple-element.36.q_ref), channel_id=1, source_target_pairs={{0,2},{1,3},{2,0},{3,1},{4,6},{5,7},{6,4},{7,5},{8,10},{9,11},{10,... | collective-permute-start | bytes 405512 | tf_op jit(solution)/shard_map/exchange/ppermute | solution.py:221
  9.1 9.6 %collective-permute-start.6 = (bf16[528,128]{1,0:T(8,128)(2,1)S(1)}, bf16[528,128]{1,0:T(8,128)(2,1)S(1)}, u32[]{:S(2)}, u32[]{:S(2)}) collective-permute-start(bf16[528,128]{1,0:T(8,128)(2,1)S(1)} %get-tuple-element.36.q_ref), channel_id=1, source_target_pairs={{0,6},{1,7},{2,4},{3,5},{4,2},{5,3},{6,0},{7,1},{8,14},{9,15},{10,... | collective-permute-start | bytes 405512 | tf_op jit(solution)/shard_map/exchange/ppermute | solution.py:221
  12.7 6.0 %collective-permute-start.9 = (bf16[528,128]{1,0:T(8,128)(2,1)S(1)}, bf16[528,128]{1,0:T(8,128)(2,1)S(1)}, u32[]{:S(2)}, u32[]{:S(2)}) collective-permute-start(bf16[528,128]{1,0:T(8,128)(2,1)S(1)} %slice.16), channel_id=1, source_target_pairs={{0,16},{8,24},{16,0},{24,8},{1,17},{9,25},{17,1},{25,9},{2,18},{10... | collective-permute-start | bytes 405512 | tf_op jit(solution)/shard_map/exchange/ppermute | solution.py:214
  14.5 5.0 %collective-permute-start.10 = (bf16[512,128]{1,0:T(8,128)(2,1)S(1)}, bf16[512,128]{1,0:T(8,128)(2,1)S(1)}, u32[]{:S(2)}, u32[]{:S(2)}) collective-permute-start(bf16[512,128]{1,0:T(8,128)(2,1)S(1)} %slice.17), channel_id=1, source_target_pairs={{0,8},{8,0},{16,24},{24,16},{1,9},{9,1},{17,25},{25,17},{2,10},{10... | collective-permute-start | bytes 393224 | tf_op jit(solution)/shard_map/exchange/ppermute | solution.py:214
  16.1 8.1 %collective-permute-start.5 = (bf16[528,128]{1,0:T(8,128)(2,1)S(1)}, bf16[528,128]{1,0:T(8,128)(2,1)S(1)}, u32[]{:S(2)}, u32[]{:S(2)}) collective-permute-start(bf16[528,128]{1,0:T(8,128)(2,1)S(1)} %get-tuple-element.36.q_ref), channel_id=1, source_target_pairs={{0,4},{1,5},{2,6},{3,7},{4,0},{5,1},{6,2},{7,3},{8,12},{9,13},{10,... | collective-permute-start | bytes 405512 | tf_op jit(solution)/shard_map/exchange/ppermute | solution.py:221
  19.9 5.7 %collective-permute-start.11 = (bf16[544,128]{1,0:T(8,128)(2,1)S(1)}, bf16[544,128]{1,0:T(8,128)(2,1)S(1)}, u32[]{:S(2)}, u32[]{:S(2)}) collective-permute-start(bf16[544,128]{1,0:T(8,128)(2,1)S(1)} %apply.4), channel_id=1, source_target_pairs={{0,2},{1,3},{2,0},{3,1},{4,6},{5,7},{6,4},{7,5},{8,10},{9,11},{10,... | collective-permute-start | bytes 417800 | tf_op jit(solution)/shard_map/return/ppermute | solution.py:290
  25.7 7.8 %collective-permute-start.13 = (bf16[544,128]{1,0:T(8,128)(2,1)S(1)}, bf16[544,128]{1,0:T(8,128)(2,1)S(1)}, u32[]{:S(2)}, u32[]{:S(2)}) collective-permute-start(bf16[544,128]{1,0:T(8,128)(2,1)S(1)} %add.1), channel_id=1, source_target_pairs={{0,4},{1,5},{2,6},{3,7},{4,0},{5,1},{6,2},{7,3},{8,12},{9,13},{10,... | collective-permute-start | bytes 417800 | tf_op jit(solution)/shard_map/return/ppermute | solution.py:284
  27.7 5.8 %collective-permute-start.15 = (bf16[272,128]{1,0:T(8,128)(2,1)S(1)}, bf16[272,128]{1,0:T(8,128)(2,1)S(1)}, u32[]{:S(2)}, u32[]{:S(2)}) collective-permute-start(bf16[272,128]{1,0:T(8,128)(2,1)S(1)} %get-tuple-element.32), channel_id=1, source_target_pairs={{0,2},{1,3},{2,0},{3,1},{4,6},{5,7},{6,4},{7,5},{8,10},{9,11},{10,... | collective-permute-start | bytes 208904 | tf_op jit(solution)/shard_map/return/ppermute | solution.py:288
  31.0 3.8 %collective-permute-start.16 = (bf16[272,128]{1,0:T(8,128)(2,1)S(1)}, bf16[272,128]{1,0:T(8,128)(2,1)S(1)}, u32[]{:S(2)}, u32[]{:S(2)}) collective-permute-start(bf16[272,128]{1,0:T(8,128)(2,1)S(1)} %get-tuple-element.42), channel_id=1, source_target_pairs={{0,3},{1,2},{2,1},{3,0},{4,7},{5,6},{6,5},{7,4},{8,11},{9,10},{10,... | collective-permute-start | bytes 208904 | tf_op jit(solution)/shard_map/return/ppermute | solution.py:288
  31.1 3.7 %collective-permute-start.12 = (bf16[272,128]{1,0:T(8,128)(2,1)S(1)}, bf16[272,128]{1,0:T(8,128)(2,1)S(1)}, u32[]{:S(2)}, u32[]{:S(2)}) collective-permute-start(bf16[272,128]{1,0:T(8,128)(2,1)S(1)} %get-tuple-element.40), channel_id=1, source_target_pairs={{0,1},{1,0},{2,3},{3,2},{4,5},{5,4},{6,7},{7,6},{8,9},{9,8},{10,11... | collective-permute-start | bytes 208904 | tf_op jit(solution)/shard_map/return/ppermute | solution.py:311
  33.4 1.4 %collective-permute-start.14 = (bf16[272,128]{1,0:T(8,128)(2,1)S(1)}, bf16[272,128]{1,0:T(8,128)(2,1)S(1)}, u32[]{:S(2)}, u32[]{:S(2)}) collective-permute-start(bf16[272,128]{1,0:T(8,128)(2,1)S(1)} %get-tuple-element.43), channel_id=1, source_target_pairs={{0,1},{1,0},{2,3},{3,2},{4,5},{5,4},{6,7},{7,6},{8,9},{9,8},{10,11... | collective-permute-start | bytes 208904 | tf_op jit(solution)/shard_map/return/ppermute | solution.py:286

commit v31 on v30

--- a/solution.py
+++ b/solution.py
@@ -280,18 +280,16 @@
 
     def send(r, parts):
         with jax.named_scope("return"):
-            if single(r) and r > 1:
+            if single(r):
                 both_blocks = lax.ppermute(parts[0], "inner", along_inner(r, 0))
                 ends.append(both_blocks[:block, :])
                 ends.append(lax.ppermute(both_blocks[block:, :], "inner", along_inner(0, 1)))
-            elif single(r):
-                ends.extend(lax.ppermute(parts[x], "inner", along_inner(r, x)) for x in range(CORES))
             else:
                 arrived[r - low(r)].append(lax.ppermute(parts[0], "inner", along_inner(low(r), 0)))
 
     def both_kernels(r, done):
         weights_by[r] = score(r, done)
-        partial[r] = apply(r, r > 1)
+        partial[r] = apply(r, r > 0)
         return partial[r][0]
 
     done = None
@@ -306,7 +304,7 @@
         send(r, parts)
     done = both_kernels(0, done)
     if chips > 1:
-        send(1, [partial[1][0], after(partial[1][1], done)])
+        send(1, partial[1])
     with jax.named_scope("return"):
         ends = [partial[0][0], lax.ppermute(partial[0][1], "inner", along_inner(0, 1))] + ends
     with jax.named_scope("combine"):

time: 35.8 us -> 37 us (1.034)
  waiting for transfers between devices: 6.58 us -> 9.26 us
  starting transfers between devices: 21.8 us -> 20.2 us
    ppermute x2 -> x0, starting transfers between devices: 2.23 us -> none  [send(): lax.ppermute(parts[x], 'inner', along_inner(r, x))]
    ppermute x1 -> x2, waiting for transfers between devices: 2.21 us -> 3.99 us  [send(): both_blocks = lax.ppermute(parts[0], 'inner', along_inner(r, 0))]
    ppermute x1, waiting for transfers between devices: 0.32 us -> 1.82 us  [send(): lax.ppermute(parts[0], 'inner', along_inner(low(r), 0))]
    ppermute x2 -> x0, waiting for transfers between devices: 1.3 us -> none  [send(): lax.ppermute(parts[x], 'inner', along_inner(r, x))]
    ppermute x1 -> x2, waiting for transfers between devices: 0.01 us -> 1.23 us  [send(): lax.ppermute(both_blocks[block:, :], 'inner', along_inner(0, 1))]
    ppermute x3, waiting for transfers between devices: 1.5 us -> 0.99 us  [shards(): q_by[r] = lax.ppermute(piece, 'inner', along_inner(r, 0))]
    ppermute x1, starting transfers between devices: 0.1 us -> 0.56 us  [shards(): lax.ppermute(partial[0][1], 'inner', along_inner(0, 1))]
    ppermute x1 -> x2, starting transfers between devices: 2.1 us -> 2.27 us  [send(): both_blocks = lax.ppermute(parts[0], 'inner', along_inner(r, 0))]
  transfers between devices with their start and end apart: 17 -> 17, of which waited for: 6 -> 7; matrix products, arithmetic and copies ran while one was open for 3% -> 3% of each run, Pallas kernels for 12% -> 12%
where the time goes in v31:
time: 37 us; the launch traced here: 36.8 us
  starting transfers between devices  20.2 us (55%)
  waiting for transfers between devices  9.26 us (25%)
  Pallas kernels  5.42 us (15%)
  other arithmetic  1.06 us (3%)
  between operations  0.81 us (2%)
    ppermute x4, starting transfers between devices, over(): return lax.ppermute(a, 'outer', [(o, o ^ r) for o in range(n_out)])  7.89 us
    ppermute x3, starting transfers between devices, shards(): q_by[r] = lax.ppermute(piece, 'inner', along_inner(r, 0))  6.64 us
    ppermute x2, waiting for transfers between devices, send(): both_blocks = lax.ppermute(parts[0], 'inner', along_inner(r, 0))  3.99 us
    pallas_call x4, Pallas kernels, score(): pl.pallas_call(functools.partial(score_kernel, r == 0), out_shape=(jax.Sh...  3.03 us
    ppermute x2, starting transfers between devices, send(): both_blocks = lax.ppermute(parts[0], 'inner', along_inner(r, 0))  2.27 us
    ppermute x1, waiting for transfers between devices, send(): lax.ppermute(parts[0], 'inner', along_inner(low(r), 0))  1.82 us
    ppermute x1, starting transfers between devices, send(): lax.ppermute(parts[0], 'inner', along_inner(low(r), 0))  1.64 us
    pallas_call x4, Pallas kernels, apply(): pl.pallas_call(functools.partial(apply_kernel, wide, rows), out_shape=sha...  1.35 us
  transfers between devices with their start and end apart: 17, of which 7 were waited for; matrix products, arithmetic and copies ran while one was open for 3% of the time, Pallas kernels for 12%

profile of v31, /device:TPU:0, one launch (start us, length us, event | category | flops | bytes accessed | tf_op | source)
XLA Modules:
  0.0 36.8 jit_solution(10867765660854706335)
XLA Ops:
  0.0 0.5 %collective-permute-start.1 = (bf16[128,512]{1,0:T(8,128)(2,1)}, bf16[128,512]{1,0:T(8,128)(2,1)S(1)}, u32[]{:S(2)}, u32[]{:S(2)}) collective-permute-start(bf16[128,512]{1,0:T(8,128)(2,1)} %param.4), channel_id=1, source_target_pairs={{0,1},{1,0},{2,3},{3,2},{4,5},{5,4},{6,7},{7,6},{8,9},{9,8},{10,11... | collective-permute-start | bytes 393224 | tf_op jit(solution)/shard_map/swap/ppermute | solution.py:187
  0.5 0.1 collective-permute-start.2
  0.5 0.5 %collective-permute-start.3 = (bf16[128,512]{1,0:T(8,128)(2,1)}, bf16[128,512]{1,0:T(8,128)(2,1)S(1)}, u32[]{:S(2)}, u32[]{:S(2)}) collective-permute-start(bf16[128,512]{1,0:T(8,128)(2,1)} %param.6), channel_id=1, source_target_pairs={{0,1},{1,0},{2,3},{3,2},{4,5},{5,4},{6,7},{7,6},{8,9},{9,8},{10,11... | collective-permute-start | bytes 393224 | tf_op jit(solution)/shard_map/swap/ppermute | solution.py:187
  1.6 0.1 collective-permute-start
  1.8 1.1 %pad_maximum_fusion.own = bf16[384,512]{1,0:T(8,128)(2,1)S(1)} fusion(bf16[128,512]{1,0:T(8,128)(2,1)} %param.6, bf16[128,512]{1,0:T(8,128)(2,1)} %param.5, bf16[128,512]{1,0:T(8,128)(2,1)} %param.4), kind=kLoop, calls=%fused_computation | loop fusion | flops 1179648 | bytes 786432 | tf_op jit(solution)/shard_map/swap/concatenate | solution.py:188
  2.8 0.0 collective-permute-done.p1
  2.9 0.0 collective-permute-done.1.q1
  2.9 0.0 collective-permute-done.2.k1
  2.9 0.0 collective-permute-done.3.v1
  2.9 0.1 merge.1
  3.0 3.0 %collective-permute-start.7 = (bf16[1040,128]{1,0:T(8,128)(2,1)S(1)}, bf16[1040,128]{1,0:T(8,128)(2,1)S(1)}, u32[]{:S(2)}, u32[]{:S(2)}) collective-permute-start(bf16[1040,128]{1,0:T(8,128)(2,1)S(1)} %get-tuple-element.23.refs_0_), channel_id=1, source_target_pairs={{0,8},{8,0},{16,24},{24,16},{1,9},{9,1},{17,25},{25,17},{2,10},{10... | collective-permute-start | bytes 798728 | tf_op jit(solution)/shard_map/exchange/ppermute | solution.py:214
  6.0 1.5 %collective-permute-start.8 = (bf16[1040,128]{1,0:T(8,128)(2,1)S(1)}, bf16[1040,128]{1,0:T(8,128)(2,1)S(1)}, u32[]{:S(2)}, u32[]{:S(2)}) collective-permute-start(bf16[1040,128]{1,0:T(8,128)(2,1)S(1)} %get-tuple-element.23.refs_0_), channel_id=1, source_target_pairs={{0,16},{8,24},{16,0},{24,8},{1,17},{9,25},{17,1},{25,9},{2,18},{10... | collective-permute-start | bytes 798728 | tf_op jit(solution)/shard_map/exchange/ppermute | solution.py:214
  7.5 1.6 %collective-permute-start.4 = (bf16[528,128]{1,0:T(8,128)(2,1)S(1)}, bf16[528,128]{1,0:T(8,128)(2,1)S(1)}, u32[]{:S(2)}, u32[]{:S(2)}) collective-permute-start(bf16[528,128]{1,0:T(8,128)(2,1)S(1)} %get-tuple-element.32.q_ref), channel_id=1, source_target_pairs={{0,2},{1,3},{2,0},{3,1},{4,6},{5,7},{6,4},{7,5},{8,10},{9,11},{10,... | collective-permute-start | bytes 405512 | tf_op jit(solution)/shard_map/exchange/ppermute | solution.py:221
  9.1 2.5 %collective-permute-start.6 = (bf16[528,128]{1,0:T(8,128)(2,1)S(1)}, bf16[528,128]{1,0:T(8,128)(2,1)S(1)}, u32[]{:S(2)}, u32[]{:S(2)}) collective-permute-start(bf16[528,128]{1,0:T(8,128)(2,1)S(1)} %get-tuple-element.32.q_ref), channel_id=1, source_target_pairs={{0,6},{1,7},{2,4},{3,5},{4,2},{5,3},{6,0},{7,1},{8,14},{9,15},{10,... | collective-permute-start | bytes 405512 | tf_op jit(solution)/shard_map/exchange/ppermute | solution.py:221
  11.6 1.1 %collective-permute-done.7.refs_1_ = bf16[1040,128]{1,0:T(8,128)(2,1)S(1)} collective-permute-done((bf16[1040,128]{1,0:T(8,128)(2,1)S(1)}, bf16[1040,128]{1,0:T(8,128)(2,1)S(1)}, u32[]{:S(2)}, u32[]{:S(2)}) %collective-permute-start.7) | collective-permute-done | bytes 266272 | tf_op jit(solution)/shard_map/exchange/ppermute | solution.py:214
  12.7 1.8 %collective-permute-start.9 = (bf16[528,128]{1,0:T(8,128)(2,1)S(1)}, bf16[528,128]{1,0:T(8,128)(2,1)S(1)}, u32[]{:S(2)}, u32[]{:S(2)}) collective-permute-start(bf16[528,128]{1,0:T(8,128)(2,1)S(1)} %slice.24), channel_id=1, source_target_pairs={{0,16},{8,24},{16,0},{24,8},{1,17},{9,25},{17,1},{25,9},{2,18},{10... | collective-permute-start | bytes 405512 | tf_op jit(solution)/shard_map/exchange/ppermute | solution.py:214
  14.5 0.0 collective-permute-done.8.refs_2_
  14.5 1.6 %collective-permute-start.10 = (bf16[512,128]{1,0:T(8,128)(2,1)S(1)}, bf16[512,128]{1,0:T(8,128)(2,1)S(1)}, u32[]{:S(2)}, u32[]{:S(2)}) collective-permute-start(bf16[512,128]{1,0:T(8,128)(2,1)S(1)} %slice.25), channel_id=1, source_target_pairs={{0,8},{8,0},{16,24},{24,16},{1,9},{9,1},{17,25},{25,17},{2,10},{10... | collective-permute-start | bytes 393224 | tf_op jit(solution)/shard_map/exchange/ppermute | solution.py:214
  16.1 0.0 collective-permute-done.4.q_ref
  16.1 2.6 %collective-permute-start.5 = (bf16[528,128]{1,0:T(8,128)(2,1)S(1)}, bf16[528,128]{1,0:T(8,128)(2,1)S(1)}, u32[]{:S(2)}, u32[]{:S(2)}) collective-permute-start(bf16[528,128]{1,0:T(8,128)(2,1)S(1)} %get-tuple-element.32.q_ref), channel_id=1, source_target_pairs={{0,4},{1,5},{2,6},{3,7},{4,0},{5,1},{6,2},{7,3},{8,12},{9,13},{10,... | collective-permute-start | bytes 405512 | tf_op jit(solution)/shard_map/exchange/ppermute | solution.py:221
  18.7 0.0 collective-permute-done.6.q_ref
  18.7 0.0 collective-permute-done.9.refs_3_
  18.7 0.8 %score.4 = (bf16[2,1024,256]{2,1,0:T(8,128)(2,1)S(1)}, f32[16,256]{1,0:T(8,128)S(1)}) custom-call(bf16[528,128]{1,0:T(8,128)(2,1)S(1)} %collective-permute-done.6.q_ref, bf16[1040,128]{1,0:T(8,128)(2,1)S(1)} %get-tuple-element.23.refs_0_, bf16[1040,128]{1,0:T(8,128)(2,1)S(1)} %collective-permute-done.7.refs_1_, ...), custom_call_target="tpu_custom_call" | custom-call | flops 134217728 | bytes 1048576 | tf_op jit(solution)/shard_map/score/score/pallas_call | solution.py:242
  19.4 0.1 collective-permute-done.10.refs_3_
  19.5 0.3 apply.4
  19.9 1.6 %collective-permute-start.11 = (bf16[544,128]{1,0:T(8,128)(2,1)S(1)}, bf16[544,128]{1,0:T(8,128)(2,1)S(1)}, u32[]{:S(2)}, u32[]{:S(2)}) collective-permute-start(bf16[544,128]{1,0:T(8,128)(2,1)S(1)} %apply.4), channel_id=1, source_target_pairs={{0,2},{1,3},{2,0},{3,1},{4,6},{5,7},{6,4},{7,5},{8,10},{9,11},{10,... | collective-permute-start | bytes 417800 | tf_op jit(solution)/shard_map/return/ppermute | solution.py:288
  21.5 0.8 %score.5 = (bf16[2,1024,256]{2,1,0:T(8,128)(2,1)S(1)}, f32[16,256]{1,0:T(8,128)S(1)}) custom-call(bf16[528,128]{1,0:T(8,128)(2,1)S(1)} %collective-permute-done.4.q_ref, bf16[1040,128]{1,0:T(8,128)(2,1)S(1)} %get-tuple-element.23.refs_0_, bf16[1040,128]{1,0:T(8,128)(2,1)S(1)} %collective-permute-done.7.refs_1_, ...), custom_call_target="tpu_custom_call" | custom-call | flops 134217728 | bytes 1048576 | tf_op jit(solution)/shard_map/score/score/pallas_call | solution.py:242
  22.3 0.3 apply.5
  22.6 0.5 %collective-permute-start.15 = (bf16[544,128]{1,0:T(8,128)(2,1)S(1)}, bf16[544,128]{1,0:T(8,128)(2,1)S(1)}, u32[]{:S(2)}, u32[]{:S(2)}) collective-permute-start(bf16[544,128]{1,0:T(8,128)(2,1)S(1)} %apply.5), channel_id=1, source_target_pairs={{0,2},{1,3},{2,0},{3,1},{4,6},{5,7},{6,4},{7,5},{8,10},{9,11},{10,... | collective-permute-start | bytes 417800 | tf_op jit(solution)/shard_map/return/ppermute | solution.py:284
  23.2 1.0 %collective-permute-done.5.q_ref = bf16[528,128]{1,0:T(8,128)(2,1)S(1)} collective-permute-done((bf16[528,128]{1,0:T(8,128)(2,1)S(1)}, bf16[528,128]{1,0:T(8,128)(2,1)S(1)}, u32[]{:S(2)}, u32[]{:S(2)}) %collective-permute-start.5) | collective-permute-done | bytes 135200 | tf_op jit(solution)/shard_map/exchange/ppermute | solution.py:221
  24.1 0.8 %score.6 = (bf16[2,1024,256]{2,1,0:T(8,128)(2,1)S(1)}, f32[16,256]{1,0:T(8,128)S(1)}) custom-call(bf16[528,128]{1,0:T(8,128)(2,1)S(1)} %collective-permute-done.5.q_ref, bf16[1040,128]{1,0:T(8,128)(2,1)S(1)} %get-tuple-element.23.refs_0_, bf16[1040,128]{1,0:T(8,128)(2,1)S(1)} %collective-permute-done.7.refs_1_, ...), custom_call_target="tpu_custom_call" | custom-call | flops 134217728 | bytes 1048576 | tf_op jit(solution)/shard_map/score/score/pallas_call | solution.py:242
  24.9 0.3 apply.6.refs_0_
  25.2 1.8 %collective-permute-done.11.refs_1_ = bf16[544,128]{1,0:T(8,128)(2,1)S(1)} collective-permute-done((bf16[544,128]{1,0:T(8,128)(2,1)S(1)}, bf16[544,128]{1,0:T(8,128)(2,1)S(1)}, u32[]{:S(2)}, u32[]{:S(2)}) %collective-permute-start.11) | collective-permute-done | bytes 139296 | tf_op jit(solution)/shard_map/return/ppermute | solution.py:288
  27.1 0.1 add.1
  27.1 1.8 %collective-permute-start.13 = (bf16[544,128]{1,0:T(8,128)(2,1)S(1)}, bf16[544,128]{1,0:T(8,128)(2,1)S(1)}, u32[]{:S(2)}, u32[]{:S(2)}) collective-permute-start(bf16[544,128]{1,0:T(8,128)(2,1)S(1)} %add.1), channel_id=1, source_target_pairs={{0,4},{1,5},{2,6},{3,7},{4,0},{5,1},{6,2},{7,3},{8,12},{9,13},{10,... | collective-permute-start | bytes 417800 | tf_op jit(solution)/shard_map/return/ppermute | solution.py:284
  28.9 1.2 %collective-permute-done.15 = bf16[544,128]{1,0:T(8,128)(2,1)S(1)} collective-permute-done((bf16[544,128]{1,0:T(8,128)(2,1)S(1)}, bf16[544,128]{1,0:T(8,128)(2,1)S(1)}, u32[]{:S(2)}, u32[]{:S(2)}) %collective-permute-start.15) | collective-permute-done | bytes 139296 | tf_op jit(solution)/shard_map/return/ppermute | solution.py:284
  30.1 0.1 collective-permute-start.16
  30.1 0.8 %score.7 = (bf16[2,1024,256]{2,1,0:T(8,128)(2,1)S(1)}, f32[16,256]{1,0:T(8,128)S(1)}) custom-call(bf16[528,128]{1,0:T(8,128)(2,1)S(1)} %get-tuple-element.32.q_ref, bf16[1040,128]{1,0:T(8,128)(2,1)S(1)} %get-tuple-element.23.refs_0_, bf16[1040,128]{1,0:T(8,128)(2,1)S(1)} %collective-permute-done.7.refs_1_, ...), custom_call_target="tpu_custom_call" | custom-call | flops 134217728 | bytes 1048576 | tf_op jit(solution)/shard_map/score/score/pallas_call | solution.py:242
  30.9 0.3 apply.7
  31.3 0.6 %collective-permute-start.12 = (bf16[272,128]{1,0:T(8,128)(2,1)S(1)}, bf16[272,128]{1,0:T(8,128)(2,1)S(1)}, u32[]{:S(2)}, u32[]{:S(2)}) collective-permute-start(bf16[272,128]{1,0:T(8,128)(2,1)S(1)} %get-tuple-element.36), channel_id=1, source_target_pairs={{0,1},{1,0},{2,3},{3,2},{4,5},{5,4},{6,7},{7,6},{8,9},{9,8},{10,11... | collective-permute-start | bytes 208904 | tf_op jit(solution)/shard_map/return/ppermute | solution.py:309
  31.8 2.8 %collective-permute-done.13 = bf16[544,128]{1,0:T(8,128)(2,1)S(1)} collective-permute-done((bf16[544,128]{1,0:T(8,128)(2,1)S(1)}, bf16[544,128]{1,0:T(8,128)(2,1)S(1)}, u32[]{:S(2)}, u32[]{:S(2)}) %collective-permute-start.13) | collective-permute-done | bytes 139296 | tf_op jit(solution)/shard_map/return/ppermute | solution.py:284
  34.7 0.1 collective-permute-start.14
  34.7 0.0 collective-permute-done.16.refs_5_
  34.8 0.0 collective-permute-done.12.refs_1_
  34.8 1.2 %collective-permute-done.14.refs_3_ = bf16[272,128]{1,0:T(8,128)(2,1)S(1)} collective-permute-done((bf16[272,128]{1,0:T(8,128)(2,1)S(1)}, bf16[272,128]{1,0:T(8,128)(2,1)S(1)}, u32[]{:S(2)}, u32[]{:S(2)}) %collective-permute-start.14) | collective-permute-done | bytes 69664 | tf_op jit(solution)/shard_map/return/ppermute | solution.py:286
  36.0 0.8 %combine.1 = bf16[128,512]{1,0:T(8,128)(2,1)} custom-call(bf16[272,128]{1,0:T(8,128)(2,1)S(1)} %get-tuple-element.35.refs_0_, bf16[272,128]{1,0:T(8,128)(2,1)S(1)} %collective-permute-done.12.refs_1_, bf16[272,128]{1,0:T(8,128)(2,1)S(1)} %get-tuple-element.40.refs_2_, bf16[272,128]{1,0:T(8,128)(2,1)S(1)} %collective-permute-done.14.refs_3_, ...), custom_call_target="tpu_custom_call" | custom-call | tf_op jit(solution)/shard_map/combine/combine/pallas_call | solution.py:311
  (5 shorter events, 0.0 us)
Async XLA Ops:
  0.0 2.9 %collective-permute-start.1 = (bf16[128,512]{1,0:T(8,128)(2,1)}, bf16[128,512]{1,0:T(8,128)(2,1)S(1)}, u32[]{:S(2)}, u32[]{:S(2)}) collective-permute-start(bf16[128,512]{1,0:T(8,128)(2,1)} %param.4), channel_id=1, source_target_pairs={{0,1},{1,0},{2,3},{3,2},{4,5},{5,4},{6,7},{7,6},{8,9},{9,8},{10,11... | collective-permute-start | bytes 393224 | tf_op jit(solution)/shard_map/swap/ppermute | solution.py:187
  0.5 2.4 %collective-permute-start.2 = (bf16[128,512]{1,0:T(8,128)(2,1)}, bf16[128,512]{1,0:T(8,128)(2,1)S(1)}, u32[]{:S(2)}, u32[]{:S(2)}) collective-permute-start(bf16[128,512]{1,0:T(8,128)(2,1)} %param.5), channel_id=1, source_target_pairs={{0,1},{1,0},{2,3},{3,2},{4,5},{5,4},{6,7},{7,6},{8,9},{9,8},{10,11... | collective-permute-start | bytes 393224 | tf_op jit(solution)/shard_map/swap/ppermute | solution.py:187
  0.5 2.4 %collective-permute-start.3 = (bf16[128,512]{1,0:T(8,128)(2,1)}, bf16[128,512]{1,0:T(8,128)(2,1)S(1)}, u32[]{:S(2)}, u32[]{:S(2)}) collective-permute-start(bf16[128,512]{1,0:T(8,128)(2,1)} %param.6), channel_id=1, source_target_pairs={{0,1},{1,0},{2,3},{3,2},{4,5},{5,4},{6,7},{7,6},{8,9},{9,8},{10,11... | collective-permute-start | bytes 393224 | tf_op jit(solution)/shard_map/swap/ppermute | solution.py:187
  1.6 1.2 %collective-permute-start = (bf16[16,128]{1,0:T(8,128)(2,1)S(1)}, bf16[16,128]{1,0:T(8,128)(2,1)S(1)}, u32[]{:S(2)}, u32[]{:S(2)}) collective-permute-start(bf16[16,128]{1,0:T(8,128)(2,1)S(1)} %broadcast_in_dim.9.p0), channel_id=1, source_target_pairs={{0,1},{1,0},{2,3},{3,2},{4,5},{5,4},{6,7},{7,6},{8,9},{9,8},{10,11... | collective-permute-start | bytes 12296 | tf_op jit(solution)/shard_map/swap/ppermute | solution.py:187
  3.0 9.6 %collective-permute-start.7 = (bf16[1040,128]{1,0:T(8,128)(2,1)S(1)}, bf16[1040,128]{1,0:T(8,128)(2,1)S(1)}, u32[]{:S(2)}, u32[]{:S(2)}) collective-permute-start(bf16[1040,128]{1,0:T(8,128)(2,1)S(1)} %get-tuple-element.23.refs_0_), channel_id=1, source_target_pairs={{0,8},{8,0},{16,24},{24,16},{1,9},{9,1},{17,25},{25,17},{2,10},{10... | collective-permute-start | bytes 798728 | tf_op jit(solution)/shard_map/exchange/ppermute | solution.py:214
  6.0 8.5 %collective-permute-start.8 = (bf16[1040,128]{1,0:T(8,128)(2,1)S(1)}, bf16[1040,128]{1,0:T(8,128)(2,1)S(1)}, u32[]{:S(2)}, u32[]{:S(2)}) collective-permute-start(bf16[1040,128]{1,0:T(8,128)(2,1)S(1)} %get-tuple-element.23.refs_0_), channel_id=1, source_target_pairs={{0,16},{8,24},{16,0},{24,8},{1,17},{9,25},{17,1},{25,9},{2,18},{10... | collective-permute-start | bytes 798728 | tf_op jit(solution)/shard_map/exchange/ppermute | solution.py:214
  7.5 8.5 %collective-permute-start.4 = (bf16[528,128]{1,0:T(8,128)(2,1)S(1)}, bf16[528,128]{1,0:T(8,128)(2,1)S(1)}, u32[]{:S(2)}, u32[]{:S(2)}) collective-permute-start(bf16[528,128]{1,0:T(8,128)(2,1)S(1)} %get-tuple-element.32.q_ref), channel_id=1, source_target_pairs={{0,2},{1,3},{2,0},{3,1},{4,6},{5,7},{6,4},{7,5},{8,10},{9,11},{10,... | collective-permute-start | bytes 405512 | tf_op jit(solution)/shard_map/exchange/ppermute | solution.py:221
  9.1 9.6 %collective-permute-start.6 = (bf16[528,128]{1,0:T(8,128)(2,1)S(1)}, bf16[528,128]{1,0:T(8,128)(2,1)S(1)}, u32[]{:S(2)}, u32[]{:S(2)}) collective-permute-start(bf16[528,128]{1,0:T(8,128)(2,1)S(1)} %get-tuple-element.32.q_ref), channel_id=1, source_target_pairs={{0,6},{1,7},{2,4},{3,5},{4,2},{5,3},{6,0},{7,1},{8,14},{9,15},{10,... | collective-permute-start | bytes 405512 | tf_op jit(solution)/shard_map/exchange/ppermute | solution.py:221
  12.7 6.0 %collective-permute-start.9 = (bf16[528,128]{1,0:T(8,128)(2,1)S(1)}, bf16[528,128]{1,0:T(8,128)(2,1)S(1)}, u32[]{:S(2)}, u32[]{:S(2)}) collective-permute-start(bf16[528,128]{1,0:T(8,128)(2,1)S(1)} %slice.24), channel_id=1, source_target_pairs={{0,16},{8,24},{16,0},{24,8},{1,17},{9,25},{17,1},{25,9},{2,18},{10... | collective-permute-start | bytes 405512 | tf_op jit(solution)/shard_map/exchange/ppermute | solution.py:214
  14.5 5.0 %collective-permute-start.10 = (bf16[512,128]{1,0:T(8,128)(2,1)S(1)}, bf16[512,128]{1,0:T(8,128)(2,1)S(1)}, u32[]{:S(2)}, u32[]{:S(2)}) collective-permute-start(bf16[512,128]{1,0:T(8,128)(2,1)S(1)} %slice.25), channel_id=1, source_target_pairs={{0,8},{8,0},{16,24},{24,16},{1,9},{9,1},{17,25},{25,17},{2,10},{10... | collective-permute-start | bytes 393224 | tf_op jit(solution)/shard_map/exchange/ppermute | solution.py:214
  16.1 8.1 %collective-permute-start.5 = (bf16[528,128]{1,0:T(8,128)(2,1)S(1)}, bf16[528,128]{1,0:T(8,128)(2,1)S(1)}, u32[]{:S(2)}, u32[]{:S(2)}) collective-permute-start(bf16[528,128]{1,0:T(8,128)(2,1)S(1)} %get-tuple-element.32.q_ref), channel_id=1, source_target_pairs={{0,4},{1,5},{2,6},{3,7},{4,0},{5,1},{6,2},{7,3},{8,12},{9,13},{10,... | collective-permute-start | bytes 405512 | tf_op jit(solution)/shard_map/exchange/ppermute | solution.py:221
  19.9 7.2 %collective-permute-start.11 = (bf16[544,128]{1,0:T(8,128)(2,1)S(1)}, bf16[544,128]{1,0:T(8,128)(2,1)S(1)}, u32[]{:S(2)}, u32[]{:S(2)}) collective-permute-start(bf16[544,128]{1,0:T(8,128)(2,1)S(1)} %apply.4), channel_id=1, source_target_pairs={{0,2},{1,3},{2,0},{3,1},{4,6},{5,7},{6,4},{7,5},{8,10},{9,11},{10,... | collective-permute-start | bytes 417800 | tf_op jit(solution)/shard_map/return/ppermute | solution.py:288
  22.6 7.4 %collective-permute-start.15 = (bf16[544,128]{1,0:T(8,128)(2,1)S(1)}, bf16[544,128]{1,0:T(8,128)(2,1)S(1)}, u32[]{:S(2)}, u32[]{:S(2)}) collective-permute-start(bf16[544,128]{1,0:T(8,128)(2,1)S(1)} %apply.5), channel_id=1, source_target_pairs={{0,2},{1,3},{2,0},{3,1},{4,6},{5,7},{6,4},{7,5},{8,10},{9,11},{10,... | collective-permute-start | bytes 417800 | tf_op jit(solution)/shard_map/return/ppermute | solution.py:284
  27.1 7.5 %collective-permute-start.13 = (bf16[544,128]{1,0:T(8,128)(2,1)S(1)}, bf16[544,128]{1,0:T(8,128)(2,1)S(1)}, u32[]{:S(2)}, u32[]{:S(2)}) collective-permute-start(bf16[544,128]{1,0:T(8,128)(2,1)S(1)} %add.1), channel_id=1, source_target_pairs={{0,4},{1,5},{2,6},{3,7},{4,0},{5,1},{6,2},{7,3},{8,12},{9,13},{10,... | collective-permute-start | bytes 417800 | tf_op jit(solution)/shard_map/return/ppermute | solution.py:284
  30.1 4.7 %collective-permute-start.16 = (bf16[272,128]{1,0:T(8,128)(2,1)S(1)}, bf16[272,128]{1,0:T(8,128)(2,1)S(1)}, u32[]{:S(2)}, u32[]{:S(2)}) collective-permute-start(bf16[272,128]{1,0:T(8,128)(2,1)S(1)} %get-tuple-element.37), channel_id=1, source_target_pairs={{0,1},{1,0},{2,3},{3,2},{4,5},{5,4},{6,7},{7,6},{8,9},{9,8},{10,11... | collective-permute-start | bytes 208904 | tf_op jit(solution)/shard_map/return/ppermute | solution.py:286
  31.3 3.5 %collective-permute-start.12 = (bf16[272,128]{1,0:T(8,128)(2,1)S(1)}, bf16[272,128]{1,0:T(8,128)(2,1)S(1)}, u32[]{:S(2)}, u32[]{:S(2)}) collective-permute-start(bf16[272,128]{1,0:T(8,128)(2,1)S(1)} %get-tuple-element.36), channel_id=1, source_target_pairs={{0,1},{1,0},{2,3},{3,2},{4,5},{5,4},{6,7},{7,6},{8,9},{9,8},{10,11... | collective-permute-start | bytes 208904 | tf_op jit(solution)/shard_map/return/ppermute | solution.py:309
  34.7 1.3 %collective-permute-start.14 = (bf16[272,128]{1,0:T(8,128)(2,1)S(1)}, bf16[272,128]{1,0:T(8,128)(2,1)S(1)}, u32[]{:S(2)}, u32[]{:S(2)}) collective-permute-start(bf16[272,128]{1,0:T(8,128)(2,1)S(1)} %get-tuple-element.39), channel_id=1, source_target_pairs={{0,1},{1,0},{2,3},{3,2},{4,5},{5,4},{6,7},{7,6},{8,9},{9,8},{10,11... | collective-permute-start | bytes 208904 | tf_op jit(solution)/shard_map/return/ppermute | solution.py:286
